TPU v7x, 32 devices: a whole 2x2x4 slice. The times are simulated.
32 devices in a mesh: groups: 2 (over y), dp: 4 (over z), tensor: 4 (over x, core).
Axes of the slice: x: 2, y: 2, z: 4, core: 2. Of those that a mesh axis runs over, the one named last changes fastest.
Arguments:
- activations: bfloat16 [64, 256, 4096], P(('groups', 'dp'), None, 'tensor'), parts along dimension 0, may hold values from -6 to 6
- out_grads: bfloat16 [64, 256, 14336], P(('groups', 'dp'), None, 'tensor'), parts along dimension 0, may hold values from -6 to 6
- proj_in: bfloat16 [4096, 64], P('tensor'), may hold values from -0.09375 to 0.09375
- proj_out: bfloat16 [14336, 64], P('tensor'), may hold values from -0.046875 to 0.046875
- lengths: int32 [64], P(('groups', 'dp')), parts along dimension 0, may hold values from 1 to 256, 6144 in all
- test_grads: bfloat16 [1024, 4096], P(('groups', 'dp')), parts along dimension 0, may hold values from -0.09375 to 0.09375
Outputs:
- scores: float32 [64, 512], P(('groups', 'dp')), parts along dimension 0
There are 2 independent parts, one for each index of `groups`. A program takes and returns all parts, laid end to end along the dimension named above; an argument that names none is the same for every part. Nothing has to cross between parts.
All inputs are finite; a program needn't handle non-finite values. No bound on the sum of `lengths` on one device may be relied on, other than what follows from the above.
Results may differ from a plain program's by a relative error of at most 0.0029.
Values may be sent and summed in bfloat16 or wider, within the bound.
No kernel may reach another device: no remote copies, remote signals or barrier semaphores. Data moves between devices by JAX's collectives and lax.ppermute only.
A program may use at most 128 MiB of HBM per device.

v0:
```python
import jax
import jax.numpy as jnp
from jax import lax
from jax.sharding import PartitionSpec as P


def shards(activations, out_grads, proj_in, proj_out, lengths, test_grads):
    seq_count, seq_slots, feat_width = activations.shape
    hidden_width = out_grads.shape[2]
    rank_size = proj_in.shape[1]
    part_in = jnp.dot(
        activations.reshape(seq_count * seq_slots, feat_width),
        proj_in,
        preferred_element_type=jnp.float32,
    )
    part_out = jnp.dot(
        out_grads.reshape(seq_count * seq_slots, hidden_width),
        proj_out,
        preferred_element_type=jnp.float32,
    )
    part_in = part_in.reshape(seq_count, seq_slots, rank_size)
    part_out = part_out.reshape(seq_count, seq_slots, rank_size)
    full_in, full_out = lax.psum((part_in, part_out), "tensor")
    position = jnp.arange(seq_slots, dtype=jnp.int32)
    keep = (position[None, :] < lengths[:, None]).astype(jnp.float32)
    masked = full_in * keep[:, :, None]
    example_grads = jnp.einsum("nti,ntj->nij", masked, full_out, precision=lax.Precision.HIGHEST)
    example_grads = example_grads / lengths.astype(jnp.float32)[:, None, None]
    flat = example_grads.reshape(seq_count, rank_size * rank_size)
    scale = jnp.sqrt(jnp.mean(flat * flat, axis=1, keepdims=True) + 1e-06)
    unit = (flat / scale).astype(jnp.bfloat16)
    return lax.dot_general(
        unit,
        lax.all_gather(test_grads, "dp", axis=0, tiled=True),
        (((1,), (1,)), ((), ())),
        preferred_element_type=jnp.float32,
    )


def solution(mesh):
    placed = (
        P(("groups", "dp"), None, "tensor"),
        P(("groups", "dp"), None, "tensor"),
        P("tensor", None),
        P("tensor", None),
        P(("groups", "dp")),
        P(("groups", "dp"), None),
    )
    return jax.shard_map(
        shards, mesh=mesh, in_specs=placed, out_specs=P(("groups", "dp"), None), check_vma=False
    )
```

profile of v0, /device:TPU:0, one launch (start us, length us, event | category | flops | bytes accessed | tf_op | source)
XLA Modules:
  0.0 118.1 jit_solution(15807567187676826569)
XLA Ops:
  7.4 0.0 copy-start
  7.4 0.0 copy-start.2
  7.4 0.0 all-reduce.3.cloned.1.call-start
  7.4 1.0 copy-done
  8.4 0.0 copy-start.1
  8.4 10.6 %fusion.1 = f32[8,256,64]{1,2,0:T(8,128)} fusion(bf16[8,256,3584]{2,1,0:T(8,128)(2,1)} %param.7, bf16[3584,64]{0,1:T(8,128)(2,1)S(1)} %copy-done), kind=kOutput, calls=%fused_computation.2 | convolution fusion | flops 939524096 | bytes 15663104 | tf_op jit(solution)/shard_map/dot_general | solution.py:16
  19.0 0.0 copy-done.2
  19.0 0.0 copy-done.1
  19.0 0.0 copy-start.3
  19.0 2.2 %fusion.4 = f32[8,256,64]{1,2,0:T(8,128)} fusion(bf16[8,256,1024]{2,1,0:T(8,128)(2,1)S(1)} %copy-done.1, bf16[1024,64]{0,1:T(8,128)(2,1)S(1)} %copy-done.2), kind=kOutput, calls=%fused_computation.6 | convolution fusion | flops 268435456 | bytes 4849664 | tf_op jit(solution)/shard_map/dot_general | solution.py:11
  21.2 0.0 all-reduce.3.cloned.1.call-update
  21.3 0.0 all-gather.2.cloned.1.call-start
  21.3 0.5 all-gather.2.cloned.1.call-update
  21.8 0.0 copy-done.3
  21.9 0.1 fusion.8
  21.9 38.7 %all-reduce.3.cloned.1.call-done = (f32[8,256,64]{1,2,0:T(8,128)}, f32[8,256,64]{1,2,0:T(8,128)}) async-done(((f32[8,256,64]{1,2,0:T(8,128)}, f32[8,256,64]{1,2,0:T(8,128)}), (f32[8,256,64]{1,2,0:T(8,128)}, f32[8,256,64]{1,2,0:T(8,128)})) %all-reduce.3.cloned.1.call-update) | async-done | bytes 1048592 | tf_op jit(solution)/shard_map/psum | solution.py:23
  60.6 1.9 %multiply_reduce_fusion = (f32[8]{0:T(128)S(1)}, f32[8,64,64]{2,1,0:T(8,128)S(1)}) fusion(f32[8]{0:T(128)S(1)} %convert_element_type.14, f32[8,256,64]{1,2,0:T(8,128)} %get-tuple-element.5, f32[8,256,64]{1,2,0:T(8,128)} %get-tuple-element.6, f32[8,256]{1,0:T(8,128)S(1)} %fusion.8), kind=kOutput, calls=%fused_computation.4 | convolution fusion | flops 100892664 | bytes 1187904 | tf_op jit(solution)/shard_map/nti,ntj->nij/dot_general | solution.py:27
  62.5 0.1 reshape.42
  62.7 44.0 %all-gather.2.cloned.1.call-done = bf16[512,4096]{1,0:T(8,128)(2,1)} async-done(((bf16[128,4096]{1,0:T(8,128)(2,1)}), bf16[512,4096]{1,0:T(8,128)(2,1)}) %all-gather.2.cloned.1.call-update) | async-done | bytes 4194320 | tf_op jit(solution)/shard_map/all_gather | solution.py:34
  106.6 4.0 %fusion.6 = f32[8,512]{1,0:T(8,128)} fusion(bf16[512,4096]{1,0:T(8,128)(2,1)} %all-gather.2.cloned.1.call-done, f32[8,4096]{1,0:T(8,128)S(1)} %reshape.42, f32[8]{0:T(128)S(1)} %add_sqrt_fusion), kind=kOutput, calls=%fused_computation.9 | convolution fusion | flops 33619968 | bytes 4341792 | tf_op jit(solution)/shard_map/dot_general | solution.py:32
  (2 shorter events, 0.0 us)
Async XLA Ops:
  7.4 1.0 copy-start
  7.4 11.7 %copy-start.2 = (bf16[1024,64]{0,1:T(8,128)(2,1)S(1)}, bf16[1024,64]{0,1:T(8,128)(2,1)}, u32[]{:S(2)}) copy-start(bf16[1024,64]{0,1:T(8,128)(2,1)} %param.8) | copy-start | bytes 393220
  7.4 53.2 %all-reduce.3.cloned.1.call-start = ((), (), s32[]{:S(2)}) async-start(), calls=%async_computation.1 | async-start | bytes 2097152 | tf_op jit(solution)/shard_map/psum | solution.py:23
  8.4 10.6 %copy-start.1 = (bf16[8,256,1024]{2,1,0:T(8,128)(2,1)S(1)}, bf16[8,256,1024]{2,1,0:T(8,128)(2,1)}, u32[]{:S(2)}) copy-start(bf16[8,256,1024]{2,1,0:T(8,128)(2,1)} %param.6) | copy-start | bytes 12582916
  19.0 2.8 %copy-start.3 = (s32[8]{0:T(128)S(1)}, s32[8]{0:T(128)}, u32[]{:S(2)}) copy-start(s32[8]{0:T(128)} %param.10) | copy-start | bytes 100
  21.3 85.4 %all-gather.2.cloned.1.call-start = ((), (), s32[]{:S(2)}) async-start(), calls=%async_computation | async-start | bytes 5242880 | tf_op jit(solution)/shard_map/all_gather | solution.py:34
Sparse Core Ops, SparseCore 0:
  21.4 39.1 all-reduce.2
Sparse Core Ops, SparseCore 1:
  23.3 83.3 all-gather.1
where the time goes:
time: 118 us
  waiting for transfers between devices  83.2 us (71%)
  matrix products  18.7 us (16%)
  between operations  14.9 us (13%)
    all_gather x1, waiting for transfers between devices, shards(): lax.all_gather(test_grads, 'dp', axis=0, tiled=True)  44 us
    psum x1, waiting for transfers between devices, shards(): full_in, full_out = lax.psum((part_in, part_out), 'tensor')  38.7 us
    dot_general x1, matrix products, shards(): jnp.dot(out_grads.reshape(seq_count * seq_slots, hidden_width), proj_out,...  10.6 us
    dot_general x1, matrix products, shards(): lax.dot_general(unit, lax.all_gather(test_grads, 'dp', axis=0, tiled=True...  3.99 us
  transfers between devices with their start and end apart: 2, of which 2 were waited for; matrix products, arithmetic and copies ran while one was open for 2% of the time, Pallas kernels for 0%

commit v1 on v0

v1 whole, which is shorter than its diff:
```python
import functools

import jax
import jax.numpy as jnp
from jax import lax
from jax.experimental import pallas as pl
from jax.experimental.pallas import tpu as pltpu
from jax.sharding import PartitionSpec as P

CORES = 2
NT = (((1,), (1,)), ((), ()))
TN = (((0,), (0,)), ((), ()))


def xor_permute(value, axis, size, step):
    return lax.ppermute(value, axis, [(i, i ^ step) for i in range(size)])


def project_kernel(steps, share, act, og, wi, wo, out, abuf, obuf, asem, osem):
    me = lax.axis_index("tensor")
    copies = []
    for at, step in enumerate(steps):
        for k in range(share):
            slot = at * share + k
            seq = (me ^ step) * share + k
            copies.append(
                (
                    pltpu.make_async_copy(act.at[seq], abuf.at[slot], asem.at[slot]),
                    pltpu.make_async_copy(og.at[seq], obuf.at[slot], osem.at[slot]),
                )
            )
    for a_copy, o_copy in copies:
        a_copy.start()
        o_copy.start()
    wide_in = jnp.concatenate([wi[...], jnp.zeros_like(wi)], axis=0)
    wide_out = jnp.concatenate([jnp.zeros_like(wo), wo[...]], axis=0)
    for slot, (a_copy, o_copy) in enumerate(copies):
        a_copy.wait()
        part = lax.dot_general(abuf[slot], wide_in, NT, preferred_element_type=jnp.float32)
        o_copy.wait()
        out[slot] = part + lax.dot_general(obuf[slot], wide_out, NT, preferred_element_type=jnp.float32)


def project(act, og, wi, wo, steps, share):
    count = len(steps) * share
    slots, feat, hidden = act.shape[1], act.shape[2], og.shape[2]
    rank = wi.shape[0]
    return pl.pallas_call(
        functools.partial(project_kernel, steps, share),
        out_shape=jax.ShapeDtypeStruct((count, slots, 2 * rank), jnp.float32),
        in_specs=[pl.BlockSpec(memory_space=pl.ANY)] * 2 + [pl.BlockSpec(memory_space=pltpu.VMEM)] * 2,
        out_specs=pl.BlockSpec(memory_space=pltpu.VMEM),
        scratch_shapes=[
            pltpu.VMEM((count, slots, feat), act.dtype),
            pltpu.VMEM((count, slots, hidden), og.dtype),
            pltpu.SemaphoreType.DMA((count,)),
            pltpu.SemaphoreType.DMA((count,)),
        ],
        compiler_params=pltpu.CompilerParams(vmem_limit_bytes=40 << 20),
        cost_estimate=pl.CostEstimate(
            flops=2 * count * slots * (feat + hidden) * 256,
            bytes_accessed=2 * count * slots * (feat + hidden),
            transcendentals=0,
        ),
    )(act, og, wi, wo)


def unit_kernel(share, rank, size, lens, *refs):
    parts, outs, pair, held = refs[: -2 - size], refs[-2 - size : -2], refs[-2], refs[-1]
    me = lax.axis_index("tensor")
    slots = parts[0].shape[1]
    rows = rank * rank // 128
    span = rows // size
    lane = lax.broadcasted_iota(jnp.int32, (rows, 2 * rank), 1)
    row = lax.broadcasted_iota(jnp.int32, (slots, 2 * rank), 0)
    for k in range(share):
        full = parts[0][k]
        for part in parts[1:]:
            full = full + part[k]
        length = lens[me * share + k]
        masked = jnp.where(row < length, full, 0.0)
        both = lax.dot_general(
            masked, full, TN, precision=lax.Precision.HIGHEST, preferred_element_type=jnp.float32
        )
        pair[...] = both[:rank] / length.astype(jnp.float32)
        even = pltpu.roll(pair[pl.ds(0, rows, stride=2), :], rank, 1)
        odd = pair[pl.ds(1, rows, stride=2), :]
        flat = jnp.where(lane < rank, even, odd)
        scale = jnp.sqrt(jnp.sum(flat * flat) / (rank * rank) + 1e-06)
        unit = flat / scale
        for at in range(size):
            held[at] = unit[at * span : (at + 1) * span]
        for step in range(size):
            outs[step][k] = held[me ^ step]


def units(lens, parts, share, rank, size):
    rows = rank * rank // 128
    span = rows // size
    return pl.pallas_call(
        functools.partial(unit_kernel, share, rank, size),
        out_shape=[jax.ShapeDtypeStruct((share, span, 128), jnp.float32)] * size,
        in_specs=[pl.BlockSpec(memory_space=pltpu.SMEM)] + [pl.BlockSpec(memory_space=pltpu.VMEM)] * len(parts),
        out_specs=[pl.BlockSpec(memory_space=pltpu.VMEM)] * size,
        scratch_shapes=[
            pltpu.VMEM((rank, 2 * rank), jnp.float32),
            pltpu.VMEM((size, span, 128), jnp.float32),
        ],
    )(lens, *parts)


def score_kernel(share, size, groups, *refs):
    unit_refs, test_refs, out, held = refs[:size], refs[size : size + groups], refs[-2], refs[-1]
    me, dp = lax.axis_index("tensor"), lax.axis_index("dp")
    span = unit_refs[0].shape[1]
    for step in range(size):
        for k in range(share):
            held[(me ^ step) * share + k] = unit_refs[step][k]
    unit = jnp.concatenate([held[:, c, :] for c in range(span)], axis=1).astype(jnp.bfloat16)
    tests = test_refs[0].shape[0]
    for step in range(groups):
        part = lax.dot_general(unit, test_refs[step][...], NT, preferred_element_type=jnp.float32)
        out[:, pl.ds(pl.multiple_of((dp ^ step) * tests, 128), tests)] = part


def score(unit_parts, test_parts, share):
    size, groups = len(unit_parts), len(test_parts)
    tests, width = test_parts[0].shape
    return pl.pallas_call(
        functools.partial(score_kernel, share, size, groups),
        out_shape=jax.ShapeDtypeStruct((share * size, tests * groups), jnp.float32),
        in_specs=[pl.BlockSpec(memory_space=pltpu.VMEM)] * (size + groups),
        out_specs=pl.BlockSpec(memory_space=pltpu.VMEM),
        scratch_shapes=[pltpu.VMEM((share * size, width // 128, 128), jnp.float32)],
        compiler_params=pltpu.CompilerParams(vmem_limit_bytes=40 << 20),
    )(*unit_parts, *test_parts)


def shards(size, groups, activations, out_grads, proj_in, proj_out, lengths, test_grads):
    rank = proj_in.shape[1]
    share = activations.shape[0] // size
    me = lax.axis_index("tensor")
    width = test_grads.shape[1] // size
    own_tests = lax.dynamic_slice_in_dim(test_grads, me * width, width, 1)
    test_parts = [own_tests] + [xor_permute(own_tests, "dp", groups, step) for step in range(1, groups)]

    wi, wo = proj_in.T, proj_out.T
    chips = size // CORES
    far = [CORES * x for x in range(1, chips)]
    other = project(activations, out_grads, wi, wo, [step ^ 1 for step in far] + [1], share)
    arrived = xor_permute(other, "tensor", size, 1)
    far_part = project(activations, out_grads, wi, wo, far, share)
    cut = len(far) * share
    send = far_part + arrived[:cut]
    sums = [xor_permute(send[i * share : (i + 1) * share], "tensor", size, step) for i, step in enumerate(far)]
    near_part = project(activations, out_grads, wi, wo, [0], share)
    unit_outs = units(lengths, [near_part, arrived[cut:]] + sums, share, rank, size)
    unit_parts = [unit_outs[0]] + [xor_permute(unit_outs[step], "tensor", size, step) for step in range(1, size)]
    part = score(unit_parts, test_parts, share)
    step = 1
    parts = [part] + [xor_permute(part, "tensor", size, step) for step in range(1, size)]
    while len(parts) > 1:
        parts = [parts[i] + parts[i + 1] for i in range(0, len(parts), 2)]
    return parts[0]


def solution(mesh):
    placed = (
        P(("groups", "dp"), None, "tensor"),
        P(("groups", "dp"), None, "tensor"),
        P("tensor", None),
        P("tensor", None),
        P(("groups", "dp")),
        P(("groups", "dp"), None),
    )
    return jax.shard_map(
        functools.partial(shards, mesh.shape["tensor"], mesh.shape["dp"]),
        mesh=mesh,
        in_specs=placed,
        out_specs=P(("groups", "dp"), None),
        check_vma=False,
    )
```

time: 118 us -> 53.3 us (0.45)
  the two profiles are of different devices: /device:TPU:0 before, /device:TPU:10 now
where the time goes in v1:
time: 53.3 us; the launch traced here: 53 us
  Pallas kernels  18.7 us (35%)
  waiting for transfers between devices  16.2 us (30%)
  local copies, waits for them, and re-layouts  8.49 us (16%)
  starting transfers between devices  8.17 us (15%)
  other arithmetic  1.36 us (3%)
    ppermute x11, waiting for transfers between devices, xor_permute(): return lax.ppermute(value, axis, [(i, i ^ step) for i in range(size)])  16.2 us
    pallas_call x3, Pallas kernels, project(): pl.pallas_call(functools.partial(project_kernel, steps, share), out_shape...  15.9 us
    unnamed x20, local copies, waits for them, and re-layouts  8.47 us
    ppermute x11, starting transfers between devices, xor_permute(): return lax.ppermute(value, axis, [(i, i ^ step) for i in range(size)])  8.17 us
    pallas_call x1, Pallas kernels, units(): pl.pallas_call(functools.partial(unit_kernel, share, rank, size), out_sha...  2.4 us
  transfers between devices with their start and end apart: 11, of which 4 were waited for; matrix products, arithmetic and copies ran while one was open for 0% of the time, Pallas kernels for 21%

profile of v1, /device:TPU:10, one launch (start us, length us, event | category | flops | bytes accessed | tf_op | source)
XLA Modules:
  0.0 53.0 jit_solution(17363532049321468739)
XLA Ops:
  0.0 2.3 %copy-done.1 = bf16[8,256,1024]{2,1,0:T(8,128)(2,1)S(1)} copy-done((bf16[8,256,1024]{2,1,0:T(8,128)(2,1)S(1)}, bf16[8,256,1024]{2,1,0:T(8,128)(2,1)}, u32[]{:S(2)}) %copy-start.1) | copy-done | bytes 4194328
  2.3 1.0 %copy-done.3 = bf16[3584,64]{0,1:T(8,128)(2,1)S(1)} copy-done((bf16[3584,64]{0,1:T(8,128)(2,1)S(1)}, bf16[3584,64]{0,1:T(8,128)(2,1)}, u32[]{:S(2)}) %copy-start.3) | copy-done | bytes 458776
  3.3 0.9 %copy-done.5 = bf16[1024,64]{0,1:T(8,128)(2,1)S(1)} copy-done((bf16[1024,64]{0,1:T(8,128)(2,1)S(1)}, bf16[1024,64]{0,1:T(8,128)(2,1)}, u32[]{:S(2)}) %copy-start.5) | copy-done | bytes 131096
  4.2 7.2 %shard_map.65 = f32[4,256,128]{2,1,0:T(8,128)S(1)} custom-call(bf16[8,256,1024]{2,1,0:T(8,128)(2,1)S(1)} %copy-done.1, bf16[8,256,3584]{2,1,0:T(8,128)(2,1)} %og.5, bf16[64,1024]{1,0:T(8,128)(2,1)S(1)} %bitcast.5, bf16[64,3584]{1,0:T(8,128)(2,1)S(1)} %bitcast.2), custom_call_target="tpu_custom_call" | custom-call | flops 2415919104 | bytes 9437184 | tf_op jit(solution)/shard_map/pallas_call | solution.py:48
  11.4 0.1 collective-permute-start
  11.6 0.0 copy-start.2
  11.6 2.2 %copy-done.2 = bf16[8,256,1024]{2,1,0:T(8,128)(2,1)S(1)} copy-done((bf16[8,256,1024]{2,1,0:T(8,128)(2,1)S(1)}, bf16[8,256,1024]{2,1,0:T(8,128)(2,1)}, u32[]{:S(2)}) %copy-start.2) | copy-done | bytes 4194328
  13.7 4.3 %shard_map.66 = f32[2,256,128]{2,1,0:T(8,128)S(1)} custom-call(bf16[8,256,1024]{2,1,0:T(8,128)(2,1)S(1)} %copy-done.2, bf16[8,256,3584]{2,1,0:T(8,128)(2,1)} %og.5, bf16[64,1024]{1,0:T(8,128)(2,1)S(1)} %bitcast.6, bf16[64,3584]{1,0:T(8,128)(2,1)S(1)} %bitcast.3), custom_call_target="tpu_custom_call" | custom-call | flops 1207959552 | bytes 4718592 | tf_op jit(solution)/shard_map/pallas_call | solution.py:48
  18.1 0.7 %slice_add_fusion = (f32[2,256,128]{2,1,0:T(8,128)S(1)}, f32[2,256,128]{2,1,0:T(8,128)}) fusion(f32[2,256,128]{2,1,0:T(8,128)S(1)} %shard_map.66, f32[4,256,128]{2,1,0:T(8,128)S(1)} %collective-permute-done), kind=kLoop, calls=%fused_computation | loop fusion | flops 65536 | bytes 1310720 | tf_op jit(solution)/shard_map/add | solution.py:154
  18.9 0.5 %collective-permute-start.1 = (f32[2,256,128]{2,1,0:T(8,128)S(1)}, f32[2,256,128]{2,1,0:T(8,128)S(1)}, u32[]{:S(2)}, u32[]{:S(2)}) collective-permute-start(f32[2,256,128]{2,1,0:T(8,128)S(1)} %get-tuple-element.13), channel_id=1, source_target_pairs={{0,2},{1,3},{2,0},{3,1},{4,6},{5,7},{6,4},{7,5},{8,10},{9,11},{10,... | collective-permute-start | bytes 786440 | tf_op jit(solution)/shard_map/ppermute | solution.py:16
  19.4 0.1 collective-permute-start.5
  19.5 3.0 %collective-permute-start.6 = (bf16[128,1024]{1,0:T(8,128)(2,1)S(1)}, bf16[128,1024]{1,0:T(8,128)(2,1)S(1)}, u32[]{:S(2)}, u32[]{:S(2)}) collective-permute-start(bf16[128,1024]{1,0:T(8,128)(2,1)S(1)} %constant_dynamic-slice_fusion.refs_4_), channel_id=1, source_target_pairs={{0,8},{4,12},{8,0},{12,4},{1,9},{5,13},{9,1},{13,5},{2,10},{6,14},... | collective-permute-start | bytes 786440 | tf_op jit(solution)/shard_map/ppermute | solution.py:16
  22.5 0.4 collective-permute-start.7
  23.0 4.3 %shard_map.64.refs_0_ = f32[2,256,128]{2,1,0:T(8,128)S(1)} custom-call(bf16[8,256,1024]{2,1,0:T(8,128)(2,1)S(1)} %copy-done.2, bf16[8,256,3584]{2,1,0:T(8,128)(2,1)} %og.5, bf16[64,1024]{1,0:T(8,128)(2,1)S(1)} %bitcast.7, bf16[64,3584]{1,0:T(8,128)(2,1)S(1)} %bitcast.4), custom_call_target="tpu_custom_call" | custom-call | flops 1207959552 | bytes 4718592 | tf_op jit(solution)/shard_map/pallas_call | solution.py:48
  27.3 0.7 %copy-done.7 = f32[2,256,128]{2,1,0:T(8,128)} copy-done((f32[2,256,128]{2,1,0:T(8,128)}, f32[2,256,128]{2,1,0:T(8,128)S(1)}, u32[]{:S(2)}) %copy-start.7) | copy-done | bytes 262168
  28.0 0.7 %copy-done.9 = f32[2,256,128]{2,1,0:T(8,128)} copy-done((f32[2,256,128]{2,1,0:T(8,128)}, f32[2,256,128]{2,1,0:T(8,128)S(1)}, u32[]{:S(2)}) %copy-start.9) | copy-done | bytes 262168
  28.7 2.4 %shard_map.67 = (f32[2,8,128]{2,1,0:T(8,128)}, f32[2,8,128]{2,1,0:T(8,128)}, f32[2,8,128]{2,1,0:T(8,128)}, f32[2,8,128]{2,1,0:T(8,128)}) custom-call(s32[8]{0:T(128)} %lens.1, f32[2,256,128]{2,1,0:T(8,128)} %copy-done.7, f32[2,256,128]{2,1,0:T(8,128)} %get-tuple-element.14.refs_1_, f32[2,256,128]{2,1,0:T(8,128)} %copy-done.9), custom_call_target="tpu_custom_call" | custom-call | tf_op jit(solution)/shard_map/pallas_call | solution.py:100
  31.1 0.0 collective-permute-start.2
  31.1 1.6 %collective-permute-start.3 = (f32[2,8,128]{2,1,0:T(8,128)}, f32[2,8,128]{2,1,0:T(8,128)S(1)}, u32[]{:S(2)}, u32[]{:S(2)}) collective-permute-start(f32[2,8,128]{2,1,0:T(8,128)} %get-tuple-element.11), channel_id=1, source_target_pairs={{0,2},{1,3},{2,0},{3,1},{4,6},{5,7},{6,4},{7,5},{8,10},{9,11},{10,... | collective-permute-start | bytes 24584 | tf_op jit(solution)/shard_map/ppermute | solution.py:16
  32.7 0.3 collective-permute-start.4
  33.0 7.5 %collective-permute-done.6.refs_6_ = bf16[128,1024]{1,0:T(8,128)(2,1)S(1)} collective-permute-done((bf16[128,1024]{1,0:T(8,128)(2,1)S(1)}, bf16[128,1024]{1,0:T(8,128)(2,1)S(1)}, u32[]{:S(2)}, u32[]{:S(2)}) %collective-permute-start.6) | collective-permute-done | bytes 262176 | tf_op jit(solution)/shard_map/ppermute | solution.py:16
  40.5 5.5 %collective-permute-done.7.refs_7_ = bf16[128,1024]{1,0:T(8,128)(2,1)S(1)} collective-permute-done((bf16[128,1024]{1,0:T(8,128)(2,1)S(1)}, bf16[128,1024]{1,0:T(8,128)(2,1)S(1)}, u32[]{:S(2)}, u32[]{:S(2)}) %collective-permute-start.7) | collective-permute-done | bytes 262176 | tf_op jit(solution)/shard_map/ppermute | solution.py:16
  46.0 0.0 collective-permute-done.2.refs_1_
  46.0 0.0 copy-start.8
  46.0 0.7 %copy-done.8 = f32[2,8,128]{2,1,0:T(8,128)S(1)} copy-done((f32[2,8,128]{2,1,0:T(8,128)S(1)}, f32[2,8,128]{2,1,0:T(8,128)}, u32[]{:S(2)}) %copy-start.8) | copy-done | bytes 8216
  46.7 0.4 shard_map.68
  47.1 0.2 collective-permute-start.10
  47.3 1.4 %collective-permute-start.8 = (f32[8,512]{1,0:T(8,128)S(1)}, f32[8,512]{1,0:T(8,128)S(1)}, u32[]{:S(2)}, u32[]{:S(2)}) collective-permute-start(f32[8,512]{1,0:T(8,128)S(1)} %shard_map.68), channel_id=1, source_target_pairs={{0,1},{1,0},{2,3},{3,2},{4,5},{5,4},{6,7},{7,6},{8,9},{9,8},{10,11... | collective-permute-start | bytes 49160 | tf_op jit(solution)/shard_map/ppermute | solution.py:16
  48.7 0.5 %collective-permute-start.9 = (f32[8,512]{1,0:T(8,128)S(1)}, f32[8,512]{1,0:T(8,128)S(1)}, u32[]{:S(2)}, u32[]{:S(2)}) collective-permute-start(f32[8,512]{1,0:T(8,128)S(1)} %shard_map.68), channel_id=1, source_target_pairs={{0,2},{1,3},{2,0},{3,1},{4,6},{5,7},{6,4},{7,5},{8,10},{9,11},{10,... | collective-permute-start | bytes 49160 | tf_op jit(solution)/shard_map/ppermute | solution.py:16
  49.2 1.1 %collective-permute-done.10 = f32[8,512]{1,0:T(8,128)S(1)} collective-permute-done((f32[8,512]{1,0:T(8,128)S(1)}, f32[8,512]{1,0:T(8,128)S(1)}, u32[]{:S(2)}, u32[]{:S(2)}) %collective-permute-start.10) | collective-permute-done | bytes 16416 | tf_op jit(solution)/shard_map/ppermute | solution.py:16
  50.4 2.1 %collective-permute-done.9 = f32[8,512]{1,0:T(8,128)S(1)} collective-permute-done((f32[8,512]{1,0:T(8,128)S(1)}, f32[8,512]{1,0:T(8,128)S(1)}, u32[]{:S(2)}, u32[]{:S(2)}) %collective-permute-start.9) | collective-permute-done | bytes 16416 | tf_op jit(solution)/shard_map/ppermute | solution.py:16
  52.4 0.6 %add_add_fusion = f32[8,512]{1,0:T(8,128)} fusion(f32[8,512]{1,0:T(8,128)S(1)} %collective-permute-done.9, f32[8,512]{1,0:T(8,128)S(1)} %collective-permute-done.10, f32[8,512]{1,0:T(8,128)S(1)} %shard_map.68, f32[8,512]{1,0:T(8,128)S(1)} %collective-permute-done.8), kind=kLoop, calls=%fused_computation.1 | loop fusion | flops 12288 | bytes 81920 | tf_op jit(solution)/shard_map/add | solution.py:163
  (18 shorter events, 0.1 us)
Async XLA Ops:
  0.0 19.4 %copy-start = (bf16[128,4096]{1,0:T(8,128)(2,1)S(1)}, bf16[128,4096]{1,0:T(8,128)(2,1)}, u32[]{:S(2)}) copy-start(bf16[128,4096]{1,0:T(8,128)(2,1)} %param.11) | copy-start | bytes 3145732
  0.0 2.3 %copy-start.1 = (bf16[8,256,1024]{2,1,0:T(8,128)(2,1)S(1)}, bf16[8,256,1024]{2,1,0:T(8,128)(2,1)}, u32[]{:S(2)}) copy-start(bf16[8,256,1024]{2,1,0:T(8,128)(2,1)} %act.5) | copy-start | bytes 12582916
  2.3 1.0 %copy-start.3 = (bf16[3584,64]{0,1:T(8,128)(2,1)S(1)}, bf16[3584,64]{0,1:T(8,128)(2,1)}, u32[]{:S(2)}) copy-start(bf16[3584,64]{0,1:T(8,128)(2,1)} %param.9) | copy-start | bytes 1376260
  3.3 0.9 %copy-start.5 = (bf16[1024,64]{0,1:T(8,128)(2,1)S(1)}, bf16[1024,64]{0,1:T(8,128)(2,1)}, u32[]{:S(2)}) copy-start(bf16[1024,64]{0,1:T(8,128)(2,1)} %param.8) | copy-start | bytes 393220
  4.2 7.3 %copy-start.4 = (bf16[3584,64]{0,1:T(8,128)(2,1)S(1)}, bf16[3584,64]{0,1:T(8,128)(2,1)}, u32[]{:S(2)}) copy-start(bf16[3584,64]{0,1:T(8,128)(2,1)} %param.9) | copy-start | bytes 1376260
  4.2 7.3 %copy-start.6 = (bf16[1024,64]{0,1:T(8,128)(2,1)S(1)}, bf16[1024,64]{0,1:T(8,128)(2,1)}, u32[]{:S(2)}) copy-start(bf16[1024,64]{0,1:T(8,128)(2,1)} %param.8) | copy-start | bytes 393220
  11.4 6.7 %collective-permute-start = (f32[4,256,128]{2,1,0:T(8,128)S(1)}, f32[4,256,128]{2,1,0:T(8,128)S(1)}, u32[]{:S(2)}, u32[]{:S(2)}) collective-permute-start(f32[4,256,128]{2,1,0:T(8,128)S(1)} %shard_map.65), channel_id=1, source_target_pairs={{0,1},{1,0},{2,3},{3,2},{4,5},{5,4},{6,7},{7,6},{8,9},{9,8},{10,11... | collective-permute-start | bytes 1572872 | tf_op jit(solution)/shard_map/ppermute | solution.py:16
  11.6 2.2 %copy-start.2 = (bf16[8,256,1024]{2,1,0:T(8,128)(2,1)S(1)}, bf16[8,256,1024]{2,1,0:T(8,128)(2,1)}, u32[]{:S(2)}) copy-start(bf16[8,256,1024]{2,1,0:T(8,128)(2,1)} %act.5) | copy-start | bytes 12582916
  18.9 9.2 %collective-permute-start.1 = (f32[2,256,128]{2,1,0:T(8,128)S(1)}, f32[2,256,128]{2,1,0:T(8,128)S(1)}, u32[]{:S(2)}, u32[]{:S(2)}) collective-permute-start(f32[2,256,128]{2,1,0:T(8,128)S(1)} %get-tuple-element.13), channel_id=1, source_target_pairs={{0,2},{1,3},{2,0},{3,1},{4,6},{5,7},{6,4},{7,5},{8,10},{9,11},{10,... | collective-permute-start | bytes 786440 | tf_op jit(solution)/shard_map/ppermute | solution.py:16
  19.4 13.3 %collective-permute-start.5 = (bf16[128,1024]{1,0:T(8,128)(2,1)S(1)}, bf16[128,1024]{1,0:T(8,128)(2,1)S(1)}, u32[]{:S(2)}, u32[]{:S(2)}) collective-permute-start(bf16[128,1024]{1,0:T(8,128)(2,1)S(1)} %constant_dynamic-slice_fusion.refs_4_), channel_id=1, source_target_pairs={{0,4},{4,0},{8,12},{12,8},{1,5},{5,1},{9,13},{13,9},{2,6},{6,2},{1... | collective-permute-start | bytes 786440 | tf_op jit(solution)/shard_map/ppermute | solution.py:16
  19.5 21.0 %collective-permute-start.6 = (bf16[128,1024]{1,0:T(8,128)(2,1)S(1)}, bf16[128,1024]{1,0:T(8,128)(2,1)S(1)}, u32[]{:S(2)}, u32[]{:S(2)}) collective-permute-start(bf16[128,1024]{1,0:T(8,128)(2,1)S(1)} %constant_dynamic-slice_fusion.refs_4_), channel_id=1, source_target_pairs={{0,8},{4,12},{8,0},{12,4},{1,9},{5,13},{9,1},{13,5},{2,10},{6,14},... | collective-permute-start | bytes 786440 | tf_op jit(solution)/shard_map/ppermute | solution.py:16
  22.5 23.4 %collective-permute-start.7 = (bf16[128,1024]{1,0:T(8,128)(2,1)S(1)}, bf16[128,1024]{1,0:T(8,128)(2,1)S(1)}, u32[]{:S(2)}, u32[]{:S(2)}) collective-permute-start(bf16[128,1024]{1,0:T(8,128)(2,1)S(1)} %constant_dynamic-slice_fusion.refs_4_), channel_id=1, source_target_pairs={{0,12},{4,8},{8,4},{12,0},{1,13},{5,9},{9,5},{13,1},{2,14},{6,10},... | collective-permute-start | bytes 786440 | tf_op jit(solution)/shard_map/ppermute | solution.py:16
  27.3 0.7 %copy-start.7 = (f32[2,256,128]{2,1,0:T(8,128)}, f32[2,256,128]{2,1,0:T(8,128)S(1)}, u32[]{:S(2)}) copy-start(f32[2,256,128]{2,1,0:T(8,128)S(1)} %shard_map.64.refs_0_) | copy-start | bytes 786436
  28.0 0.7 %copy-start.9 = (f32[2,256,128]{2,1,0:T(8,128)}, f32[2,256,128]{2,1,0:T(8,128)S(1)}, u32[]{:S(2)}) copy-start(f32[2,256,128]{2,1,0:T(8,128)S(1)} %collective-permute-done.1.refs_2_) | copy-start | bytes 786436
  31.1 14.8 %collective-permute-start.2 = (f32[2,8,128]{2,1,0:T(8,128)}, f32[2,8,128]{2,1,0:T(8,128)S(1)}, u32[]{:S(2)}, u32[]{:S(2)}) collective-permute-start(f32[2,8,128]{2,1,0:T(8,128)} %get-tuple-element.10), channel_id=1, source_target_pairs={{0,1},{1,0},{2,3},{3,2},{4,5},{5,4},{6,7},{7,6},{8,9},{9,8},{10,11... | collective-permute-start | bytes 24584 | tf_op jit(solution)/shard_map/ppermute | solution.py:16
  31.1 14.8 %collective-permute-start.3 = (f32[2,8,128]{2,1,0:T(8,128)}, f32[2,8,128]{2,1,0:T(8,128)S(1)}, u32[]{:S(2)}, u32[]{:S(2)}) collective-permute-start(f32[2,8,128]{2,1,0:T(8,128)} %get-tuple-element.11), channel_id=1, source_target_pairs={{0,2},{1,3},{2,0},{3,1},{4,6},{5,7},{6,4},{7,5},{8,10},{9,11},{10,... | collective-permute-start | bytes 24584 | tf_op jit(solution)/shard_map/ppermute | solution.py:16
  32.7 13.3 %collective-permute-start.4 = (f32[2,8,128]{2,1,0:T(8,128)}, f32[2,8,128]{2,1,0:T(8,128)S(1)}, u32[]{:S(2)}, u32[]{:S(2)}) collective-permute-start(f32[2,8,128]{2,1,0:T(8,128)} %get-tuple-element.12), channel_id=1, source_target_pairs={{0,3},{1,2},{2,1},{3,0},{4,7},{5,6},{6,5},{7,4},{8,11},{9,10},{10,... | collective-permute-start | bytes 24584 | tf_op jit(solution)/shard_map/ppermute | solution.py:16
  46.0 0.7 %copy-start.8 = (f32[2,8,128]{2,1,0:T(8,128)S(1)}, f32[2,8,128]{2,1,0:T(8,128)}, u32[]{:S(2)}) copy-start(f32[2,8,128]{2,1,0:T(8,128)} %get-tuple-element.9.refs_0_) | copy-start | bytes 24580
  47.1 3.3 %collective-permute-start.10 = (f32[8,512]{1,0:T(8,128)S(1)}, f32[8,512]{1,0:T(8,128)S(1)}, u32[]{:S(2)}, u32[]{:S(2)}) collective-permute-start(f32[8,512]{1,0:T(8,128)S(1)} %shard_map.68), channel_id=1, source_target_pairs={{0,3},{1,2},{2,1},{3,0},{4,7},{5,6},{6,5},{7,4},{8,11},{9,10},{10,... | collective-permute-start | bytes 49160 | tf_op jit(solution)/shard_map/ppermute | solution.py:16
  47.3 3.1 %collective-permute-start.8 = (f32[8,512]{1,0:T(8,128)S(1)}, f32[8,512]{1,0:T(8,128)S(1)}, u32[]{:S(2)}, u32[]{:S(2)}) collective-permute-start(f32[8,512]{1,0:T(8,128)S(1)} %shard_map.68), channel_id=1, source_target_pairs={{0,1},{1,0},{2,3},{3,2},{4,5},{5,4},{6,7},{7,6},{8,9},{9,8},{10,11... | collective-permute-start | bytes 49160 | tf_op jit(solution)/shard_map/ppermute | solution.py:16
  48.7 3.7 %collective-permute-start.9 = (f32[8,512]{1,0:T(8,128)S(1)}, f32[8,512]{1,0:T(8,128)S(1)}, u32[]{:S(2)}, u32[]{:S(2)}) collective-permute-start(f32[8,512]{1,0:T(8,128)S(1)} %shard_map.68), channel_id=1, source_target_pairs={{0,2},{1,3},{2,0},{3,1},{4,6},{5,7},{6,4},{7,5},{8,10},{9,11},{10,... | collective-permute-start | bytes 49160 | tf_op jit(solution)/shard_map/ppermute | solution.py:16

commit v2 on v0

v2 whole, which is shorter than its diff:
```python
import functools

import jax
import jax.numpy as jnp
from jax import lax
from jax.experimental import pallas as pl
from jax.experimental.pallas import tpu as pltpu
from jax.sharding import PartitionSpec as P

CORES = 2
AHEAD = 2
NT = (((1,), (1,)), ((), ()))
NN = (((1,), (0,)), ((), ()))
TN = (((0,), (0,)), ((), ()))
VMEM_BYTES = 60 << 20


def xor_permute(value, axis, size, step):
    return lax.ppermute(value, axis, [(i, i ^ step) for i in range(size)])


def project_kernel(steps, share, after, act, og, wi, wo, lens, *refs):
    refs = refs[after:]
    outs, (abuf, obuf, wibuf, wobuf, wide_in, wide_out, lenbuf, asem, osem, wsem) = refs[:-10], refs[-10:]
    me = lax.axis_index("tensor")
    rank, feat = wibuf.shape
    hidden = wobuf.shape[1]
    slots = abuf.shape[1]
    count = len(steps) * share
    seqs = [(me ^ step) * share + k for step in steps for k in range(share)]
    small = [
        pltpu.make_async_copy(lens, lenbuf, wsem.at[0]),
        pltpu.make_async_copy(wi, wibuf, wsem.at[1]),
        pltpu.make_async_copy(wo, wobuf, wsem.at[2]),
    ]
    copies = [
        (
            pltpu.make_async_copy(act.at[seq], abuf.at[slot], asem.at[slot]),
            pltpu.make_async_copy(og.at[seq], obuf.at[slot], osem.at[slot]),
        )
        for slot, seq in enumerate(seqs)
    ]
    for copy in small:
        copy.start()
    for slot in range(min(AHEAD, count)):
        copies[slot][0].start()
        copies[slot][1].start()
    for copy in small:
        copy.wait()
    wide_in[...] = jnp.concatenate([wibuf[...], jnp.zeros_like(wibuf)], axis=0).T
    wide_out[...] = jnp.concatenate([jnp.zeros_like(wobuf), wobuf[...]], axis=0).T
    row = lax.broadcasted_iota(jnp.int32, (slots, 2 * rank), 0)
    lane = lax.broadcasted_iota(jnp.int32, (slots, 2 * rank), 1)
    per = count // len(outs)
    for slot in range(count):
        copies[slot][0].wait()
        part = lax.dot_general(abuf[slot], wide_in[...], NN, preferred_element_type=jnp.float32)
        copies[slot][1].wait()
        if slot + AHEAD < count:
            copies[slot + AHEAD][0].start()
            copies[slot + AHEAD][1].start()
        part = part + lax.dot_general(obuf[slot], wide_out[...], NN, preferred_element_type=jnp.float32)
        length = lenbuf[seqs[slot]]
        scale = jnp.where(lane < rank, 1.0 / length.astype(jnp.float32), 1.0)
        outs[slot // per][slot % per] = jnp.where(row < length, part * scale, 0.0)


def project(act, og, wi, wo, lens, groups, share, after=()):
    steps = [step for group in groups for step in group]
    count = len(steps) * share
    slots, feat, hidden = act.shape[1], act.shape[2], og.shape[2]
    rank = wi.shape[0]
    return pl.pallas_call(
        functools.partial(project_kernel, steps, share, len(after)),
        out_shape=[jax.ShapeDtypeStruct((len(group) * share, slots, 2 * rank), jnp.float32) for group in groups],
        in_specs=[pl.BlockSpec(memory_space=pl.ANY)] * (5 + len(after)),
        out_specs=[pl.BlockSpec(memory_space=pltpu.VMEM)] * len(groups),
        scratch_shapes=[
            pltpu.VMEM((count, slots, feat), act.dtype),
            pltpu.VMEM((count, slots, hidden), og.dtype),
            pltpu.VMEM((rank, feat), wi.dtype),
            pltpu.VMEM((rank, hidden), wo.dtype),
            pltpu.VMEM((feat, 2 * rank), wi.dtype),
            pltpu.VMEM((hidden, 2 * rank), wo.dtype),
            pltpu.SMEM(lens.shape, lens.dtype),
            pltpu.SemaphoreType.DMA((count,)),
            pltpu.SemaphoreType.DMA((count,)),
            pltpu.SemaphoreType.DMA((3,)),
        ],
        compiler_params=pltpu.CompilerParams(vmem_limit_bytes=VMEM_BYTES),
        cost_estimate=pl.CostEstimate(
            flops=2 * count * slots * (feat + hidden) * 256,
            bytes_accessed=2 * count * slots * (feat + hidden),
            transcendentals=0,
        ),
    )(act, og, wi, wo, lens, *after)


def unit_kernel(share, rank, size, groups, *refs):
    parts, out, pairs = refs[:-2], refs[-2], refs[-1]
    rows = rank * rank // 128
    span = rows // size
    lane = lax.broadcasted_iota(jnp.int32, (rows, 2 * rank), 1)
    for k in range(share):
        full = parts[0][k]
        for part in parts[1:]:
            full = full + part[k]
        high = full.astype(jnp.bfloat16)
        low = (full - high.astype(jnp.float32)).astype(jnp.bfloat16)
        dot = functools.partial(lax.dot_general, dimension_numbers=TN, preferred_element_type=jnp.float32)
        both = dot(high, high) + (dot(high, low) + dot(low, high))
        pairs[k] = both[:rank]
    for k in range(share):
        even = pltpu.roll(pairs[k, pl.ds(0, rows, stride=2), :], rank, 1)
        odd = pairs[k, pl.ds(1, rows, stride=2), :]
        flat = jnp.where(lane < rank, even, odd)
        scale = jnp.sqrt(jnp.sum(flat * flat) / (rank * rank) + 1e-06)
        unit = (flat / scale).astype(jnp.bfloat16)
        for to in range(groups * size):
            at = to % size * span
            out[to, k] = unit[at : at + span]


def units(parts, share, rank, size, groups):
    span = rank * rank // 128 // size
    return pl.pallas_call(
        functools.partial(unit_kernel, share, rank, size, groups),
        out_shape=jax.ShapeDtypeStruct((groups * size, share, span, 128), jnp.bfloat16),
        in_specs=[pl.BlockSpec(memory_space=pltpu.VMEM)] * len(parts),
        out_specs=pl.BlockSpec(memory_space=pltpu.VMEM),
        scratch_shapes=[pltpu.VMEM((share, rank, 2 * rank), jnp.float32)],
    )(*parts)


def score_kernel(size, unit_ref, test_ref, out):
    span = unit_ref.shape[1]
    whole = unit_ref[...].astype(jnp.float32)
    unit = jnp.concatenate([whole[:, c, :] for c in range(span)], axis=1).astype(jnp.bfloat16)
    part = lax.dot_general(unit, test_ref[...], NT, preferred_element_type=jnp.float32)
    rows = out.shape[1]
    for to in range(out.shape[0]):
        at = to // size * rows
        out[to] = part[at : at + rows]


def score(unit_all, own_tests, size, groups):
    seqs, tests = unit_all.shape[0], own_tests.shape[0]
    return pl.pallas_call(
        functools.partial(score_kernel, size),
        out_shape=jax.ShapeDtypeStruct((groups * size, seqs // groups, tests), jnp.float32),
        in_specs=[pl.BlockSpec(memory_space=pltpu.VMEM)] * 2,
        out_specs=pl.BlockSpec(memory_space=pltpu.VMEM),
    )(unit_all, own_tests)


def finish_kernel(size, parts, out):
    tests = parts.shape[2]
    for group in range(parts.shape[0] // size):
        total = parts[group * size]
        for i in range(1, size):
            total = total + parts[group * size + i]
        out[:, group * tests : (group + 1) * tests] = total


def finish(parts, size):
    count, rows, tests = parts.shape
    return pl.pallas_call(
        functools.partial(finish_kernel, size),
        out_shape=jax.ShapeDtypeStruct((rows, count // size * tests), jnp.float32),
        in_specs=[pl.BlockSpec(memory_space=pltpu.VMEM)],
        out_specs=pl.BlockSpec(memory_space=pltpu.VMEM),
    )(parts)


def shards(size, groups, activations, out_grads, proj_in, proj_out, lengths, test_grads):
    rank = proj_in.shape[1]
    share = activations.shape[0] // size
    me = lax.axis_index("tensor")
    width = test_grads.shape[1] // size
    own_tests = lax.dynamic_slice_in_dim(test_grads, me * width, width, 1)

    far = [CORES * x for x in range(1, size // CORES)]
    arrays = (activations, out_grads, proj_in.T, proj_out.T, lengths)
    far_other, far_own = project(*arrays, [[step ^ 1 for step in far], far], share)
    far_sum = far_own + xor_permute(far_other, "tensor", size, 1)
    sums = [xor_permute(far_sum[i * share : (i + 1) * share], "tensor", size, step) for i, step in enumerate(far)]
    near_other, near_own = project(*arrays, [[1], [0]], share, [far_sum])
    arrived = xor_permute(near_other, "tensor", size, 1)
    unit_cut = units([near_own, arrived] + sums, share, rank, size, groups)
    unit_all = lax.all_to_all(unit_cut, ("dp", "tensor"), 0, 0, tiled=True)
    part = score(unit_all.reshape(-1, *unit_all.shape[2:]), own_tests, size, groups)
    parts = lax.all_to_all(part, ("dp", "tensor"), 0, 0, tiled=True)
    return finish(parts, size)


def solution(mesh):
    placed = (
        P(("groups", "dp"), None, "tensor"),
        P(("groups", "dp"), None, "tensor"),
        P("tensor", None),
        P("tensor", None),
        P(("groups", "dp")),
        P(("groups", "dp"), None),
    )
    return jax.shard_map(
        functools.partial(shards, mesh.shape["tensor"], mesh.shape["dp"]),
        mesh=mesh,
        in_specs=placed,
        out_specs=P(("groups", "dp"), None),
        check_vma=False,
    )
```

time: 118 us -> 57.2 us (0.48)
  waiting for transfers between devices: 83.2 us -> 14.3 us
  matrix products: 18.7 us -> 0 us
  Pallas kernels: 0 us -> 17.9 us
  between operations: 14.9 us -> 0.05 us
  blocking collectives: 0 us -> 11 us
  starting transfers between devices: 0.05 us -> 9.76 us
  other arithmetic: 0.08 us -> 1.69 us
    all_gather x1 -> x0, waiting for transfers between devices: 44 us -> none  [shards(): lax.all_gather(test_grads, 'dp', axis=0, tiled=True)]
    psum x1 -> x0, waiting for transfers between devices: 38.7 us -> none  [shards(): full_in, full_out = lax.psum((part_in, part_out), 'tensor')]
    dot_general x4 -> x0, matrix products: 18.7 us -> none  [the longest x1 10.6 us: shards(): jnp.dot(out_grads.reshape(seq_count * seq_slots, hidden_width), proj_out,...]
    pallas_call x0 -> x5, Pallas kernels: none -> 17.9 us  [the longest x2 12.4 us: project(): pl.pallas_call(functools.partial(project_kernel, steps, share, len(after)...]
    all_to_all x0 -> x1, blocking collectives: none -> 11 us  [shards(): parts = lax.all_to_all(part, ('dp', 'tensor'), 0, 0, tiled=True)]
    ppermute x0 -> x3, waiting for transfers between devices: none -> 8.19 us  [xor_permute(): return lax.ppermute(value, axis, [(i, i ^ step) for i in range(size)])]
    all_to_all x0 -> x1, starting transfers between devices: none -> 6.17 us  [shards(): unit_all = lax.all_to_all(unit_cut, ('dp', 'tensor'), 0, 0, tiled=True)]
    all_to_all x0 -> x1, waiting for transfers between devices: none -> 6.15 us  [shards(): unit_all = lax.all_to_all(unit_cut, ('dp', 'tensor'), 0, 0, tiled=True)]
  transfers between devices with their start and end apart: 2 -> 4, of which waited for: 2 -> 3; matrix products, arithmetic and copies ran while one was open for 2% -> 1% of each run, Pallas kernels for 0% -> 0%
where the time goes in v2:
time: 57.2 us; the launch traced here: 56.8 us
  Pallas kernels  17.9 us (31%)
  waiting for transfers between devices  14.3 us (25%)
  blocking collectives  11 us (19%)
  starting transfers between devices  9.76 us (17%)
  local copies, waits for them, and re-layouts  2.06 us (4%)
  other arithmetic  1.69 us (3%)
    pallas_call x2, Pallas kernels, project(): pl.pallas_call(functools.partial(project_kernel, steps, share, len(after)...  12.4 us
    all_to_all x1, blocking collectives, shards(): parts = lax.all_to_all(part, ('dp', 'tensor'), 0, 0, tiled=True)  11 us
    ppermute x3, waiting for transfers between devices, xor_permute(): return lax.ppermute(value, axis, [(i, i ^ step) for i in range(size)])  8.19 us
    all_to_all x1, starting transfers between devices, shards(): unit_all = lax.all_to_all(unit_cut, ('dp', 'tensor'), 0, 0, tiled=True)  6.17 us
    all_to_all x1, waiting for transfers between devices, shards(): unit_all = lax.all_to_all(unit_cut, ('dp', 'tensor'), 0, 0, tiled=True)  6.15 us
    ppermute x3, starting transfers between devices, xor_permute(): return lax.ppermute(value, axis, [(i, i ^ step) for i in range(size)])  3.59 us
    pallas_call x1, Pallas kernels, units(): pl.pallas_call(functools.partial(unit_kernel, share, rank, size, groups),...  2.29 us
    pallas_call x1, Pallas kernels, score(): pl.pallas_call(functools.partial(score_kernel, size), out_shape=jax.Shape...  1.81 us
  transfers between devices with their start and end apart: 4, of which 3 were waited for; matrix products, arithmetic and copies ran while one was open for 1% of the time, Pallas kernels for 0%

profile of v2, /device:TPU:0, one launch (start us, length us, event | category | flops | bytes accessed | tf_op | source)
XLA Modules:
  0.0 56.8 jit_solution(10541779549048729739)
XLA Ops:
  0.0 0.0 copy-start
  0.0 6.2 %shard_map.64 = (f32[2,256,128]{2,1,0:T(8,128)}, f32[2,256,128]{2,1,0:T(8,128)}) custom-call(bf16[8,256,1024]{2,1,0:T(8,128)(2,1)} %act.3, bf16[8,256,3584]{2,1,0:T(8,128)(2,1)} %og.3, bf16[64,1024]{1,0:T(8,128)(2,1)} %bitcast.5, bf16[64,3584]{1,0:T(8,128)(2,1)} %bitcast.3, s32[8]{0:T(128)} %lens.3), custom_call_target="tpu_custom_call" | custom-call | flops 2415919104 | bytes 9437184 | tf_op jit(solution)/shard_map/pallas_call | solution.py:73
  6.2 0.5 collective-permute-start
  6.7 1.4 %collective-permute-done = f32[2,256,128]{2,1,0:T(8,128)S(1)} collective-permute-done((f32[2,256,128]{2,1,0:T(8,128)}, f32[2,256,128]{2,1,0:T(8,128)S(1)}, u32[]{:S(2)}, u32[]{:S(2)}) %collective-permute-start) | collective-permute-done | bytes 262176 | tf_op jit(solution)/shard_map/ppermute | solution.py:19
  8.1 1.7 %add.6.refs_0_ = f32[2,256,128]{2,1,0:T(8,128)} add(f32[2,256,128]{2,1,0:T(8,128)} %get-tuple-element.9, f32[2,256,128]{2,1,0:T(8,128)S(1)} %collective-permute-done) | non-fusion elementwise | flops 65536 | bytes 786432 | tf_op jit(solution)/shard_map/add | solution.py:185
  9.8 0.0 copy-start.1
  9.8 6.2 %shard_map.65 = (f32[2,256,128]{2,1,0:T(8,128)}, f32[2,256,128]{2,1,0:T(8,128)}) custom-call(bf16[8,256,1024]{2,1,0:T(8,128)(2,1)} %act.3, bf16[8,256,3584]{2,1,0:T(8,128)(2,1)} %og.3, bf16[64,1024]{1,0:T(8,128)(2,1)} %bitcast.6, bf16[64,3584]{1,0:T(8,128)(2,1)} %bitcast.4, s32[8]{0:T(128)} %lens.3, f32[2,256,128]{2,1,0:T(8,128)} %add.6.refs_0_), custom_call_target="tpu_custom_call" | custom-call | flops 2415919104 | bytes 9437184 | tf_op jit(solution)/shard_map/pallas_call | solution.py:73
  16.0 0.4 collective-permute-start.1
  16.4 0.0 copy-done.1
  16.4 2.6 %collective-permute-start.2 = (f32[2,256,128]{2,1,0:T(8,128)S(1)}, f32[2,256,128]{2,1,0:T(8,128)S(1)}, u32[]{:S(2)}, u32[]{:S(2)}) collective-permute-start(f32[2,256,128]{2,1,0:T(8,128)S(1)} %copy-done.1), channel_id=1, source_target_pairs={{0,2},{1,3},{2,0},{3,1},{4,6},{5,7},{6,4},{7,5},{8,10},{9,11},{10,... | collective-permute-start | bytes 786440 | tf_op jit(solution)/shard_map/ppermute | solution.py:19
  19.1 0.0 collective-permute-done.1.refs_1_
  19.1 0.0 copy-start.2
  19.1 6.8 %collective-permute-done.2.refs_2_ = f32[2,256,128]{2,1,0:T(8,128)S(1)} collective-permute-done((f32[2,256,128]{2,1,0:T(8,128)S(1)}, f32[2,256,128]{2,1,0:T(8,128)S(1)}, u32[]{:S(2)}, u32[]{:S(2)}) %collective-permute-start.2) | collective-permute-done | bytes 262176 | tf_op jit(solution)/shard_map/ppermute | solution.py:19
  25.9 0.0 copy-start.3
  25.9 0.0 copy-done.2
  25.9 0.7 %copy-done.3 = f32[2,256,128]{2,1,0:T(8,128)} copy-done((f32[2,256,128]{2,1,0:T(8,128)}, f32[2,256,128]{2,1,0:T(8,128)S(1)}, u32[]{:S(2)}) %copy-start.3) | copy-done | bytes 262168
  26.6 2.3 %shard_map.66 = bf16[16,2,8,128]{3,2,1,0:T(8,128)(2,1)} custom-call(f32[2,256,128]{2,1,0:T(8,128)} %get-tuple-element.11.refs_0_, f32[2,256,128]{2,1,0:T(8,128)} %copy-done.2, f32[2,256,128]{2,1,0:T(8,128)} %copy-done.3), custom_call_target="tpu_custom_call" | custom-call | tf_op jit(solution)/shard_map/pallas_call | solution.py:126
  28.9 6.2 %all-to-all-start = ((bf16[16,2,8,128]{3,2,1,0:T(8,128)(2,1)}), bf16[16,2,8,128]{3,2,1,0:T(8,128)(2,1)S(1)}, u32[]{:S(2)}, u32[]{:S(2)}) async-start(bf16[16,2,8,128]{3,2,1,0:T(8,128)(2,1)} %shard_map.66), calls=%async_computation | async-start | bytes 131072 | tf_op jit(solution)/shard_map/all_to_all | solution.py:190
  35.0 0.0 copy-done
  35.1 0.7 %constant_dynamic-slice_fusion.test_ref = bf16[128,1024]{1,0:T(8,128)(2,1)} fusion(bf16[128,4096]{1,0:T(8,128)(2,1)S(1)} %copy-done, s32[]{:T(128)S(6)} %select_n.3), kind=kLoop, calls=%fused_computation | loop fusion | bytes 524292 | tf_op jit(solution)/shard_map/dynamic_slice | solution.py:180
  35.8 6.1 %all-to-all-done = bf16[16,2,8,128]{3,2,1,0:T(8,128)(2,1)S(1)} async-done(((bf16[16,2,8,128]{3,2,1,0:T(8,128)(2,1)}), bf16[16,2,8,128]{3,2,1,0:T(8,128)(2,1)S(1)}, u32[]{:S(2)}, u32[]{:S(2)}) %all-to-all-start) | async-done | bytes 65568 | tf_op jit(solution)/shard_map/all_to_all | solution.py:190
  41.9 0.0 copy-start.4
  41.9 0.6 %copy-done.4 = bf16[16,2,8,128]{3,2,1,0:T(8,128)(2,1)} copy-done((bf16[16,2,8,128]{3,2,1,0:T(8,128)(2,1)}, bf16[16,2,8,128]{3,2,1,0:T(8,128)(2,1)S(1)}, u32[]{:S(2)}) %copy-start.4) | copy-done | bytes 65560
  42.6 1.8 %shard_map.67 = f32[16,8,128]{2,1,0:T(8,128)} custom-call(bf16[32,8,128]{2,1,0:T(8,128)(2,1)} %bitcast.7, bf16[128,1024]{1,0:T(8,128)(2,1)} %constant_dynamic-slice_fusion.test_ref), custom_call_target="tpu_custom_call" | custom-call | tf_op jit(solution)/shard_map/pallas_call | solution.py:148
  44.4 11.0 %all_to_all.10.parts = f32[16,8,128]{2,1,0:T(8,128)} all-to-all(f32[16,8,128]{2,1,0:T(8,128)} %shard_map.67), channel_id=1, replica_groups=mesh['groups'=2,'dp'=4,'tensor'=4] {'dp','tensor'}, dimensions={0} | all-to-all | bytes 131072 | tf_op jit(solution)/shard_map/all_to_all | solution.py:192
  55.4 1.4 %shard_map.68 = f32[8,512]{1,0:T(8,128)} custom-call(f32[16,8,128]{2,1,0:T(8,128)} %all_to_all.10.parts), custom_call_target="tpu_custom_call" | custom-call | tf_op jit(solution)/shard_map/pallas_call | solution.py:167
Async XLA Ops:
  0.0 35.1 %copy-start = (bf16[128,4096]{1,0:T(8,128)(2,1)S(1)}, bf16[128,4096]{1,0:T(8,128)(2,1)}, u32[]{:S(2)}) copy-start(bf16[128,4096]{1,0:T(8,128)(2,1)} %param.11) | copy-start | bytes 3145732
  6.2 1.9 %collective-permute-start = (f32[2,256,128]{2,1,0:T(8,128)}, f32[2,256,128]{2,1,0:T(8,128)S(1)}, u32[]{:S(2)}, u32[]{:S(2)}) collective-permute-start(f32[2,256,128]{2,1,0:T(8,128)} %get-tuple-element.10), channel_id=1, source_target_pairs={{0,1},{1,0},{2,3},{3,2},{4,5},{5,4},{6,7},{7,6},{8,9},{9,8},{10,11... | collective-permute-start | bytes 786440 | tf_op jit(solution)/shard_map/ppermute | solution.py:19
  9.8 6.6 %copy-start.1 = (f32[2,256,128]{2,1,0:T(8,128)S(1)}, f32[2,256,128]{2,1,0:T(8,128)}, u32[]{:S(2)}) copy-start(f32[2,256,128]{2,1,0:T(8,128)} %add.6.refs_0_) | copy-start | bytes 786436
  16.0 3.1 %collective-permute-start.1 = (f32[2,256,128]{2,1,0:T(8,128)}, f32[2,256,128]{2,1,0:T(8,128)S(1)}, u32[]{:S(2)}, u32[]{:S(2)}) collective-permute-start(f32[2,256,128]{2,1,0:T(8,128)} %get-tuple-element.12), channel_id=1, source_target_pairs={{0,1},{1,0},{2,3},{3,2},{4,5},{5,4},{6,7},{7,6},{8,9},{9,8},{10,11... | collective-permute-start | bytes 786440 | tf_op jit(solution)/shard_map/ppermute | solution.py:19
  16.4 9.5 %collective-permute-start.2 = (f32[2,256,128]{2,1,0:T(8,128)S(1)}, f32[2,256,128]{2,1,0:T(8,128)S(1)}, u32[]{:S(2)}, u32[]{:S(2)}) collective-permute-start(f32[2,256,128]{2,1,0:T(8,128)S(1)} %copy-done.1), channel_id=1, source_target_pairs={{0,2},{1,3},{2,0},{3,1},{4,6},{5,7},{6,4},{7,5},{8,10},{9,11},{10,... | collective-permute-start | bytes 786440 | tf_op jit(solution)/shard_map/ppermute | solution.py:19
  19.1 6.8 %copy-start.2 = (f32[2,256,128]{2,1,0:T(8,128)}, f32[2,256,128]{2,1,0:T(8,128)S(1)}, u32[]{:S(2)}) copy-start(f32[2,256,128]{2,1,0:T(8,128)S(1)} %collective-permute-done.1.refs_1_) | copy-start | bytes 786436
  25.9 0.7 %copy-start.3 = (f32[2,256,128]{2,1,0:T(8,128)}, f32[2,256,128]{2,1,0:T(8,128)S(1)}, u32[]{:S(2)}) copy-start(f32[2,256,128]{2,1,0:T(8,128)S(1)} %collective-permute-done.2.refs_2_) | copy-start | bytes 786436
  28.9 13.1 %all-to-all-start = ((bf16[16,2,8,128]{3,2,1,0:T(8,128)(2,1)}), bf16[16,2,8,128]{3,2,1,0:T(8,128)(2,1)S(1)}, u32[]{:S(2)}, u32[]{:S(2)}) async-start(bf16[16,2,8,128]{3,2,1,0:T(8,128)(2,1)} %shard_map.66), calls=%async_computation | async-start | bytes 131072 | tf_op jit(solution)/shard_map/all_to_all | solution.py:190
  41.9 0.6 %copy-start.4 = (bf16[16,2,8,128]{3,2,1,0:T(8,128)(2,1)}, bf16[16,2,8,128]{3,2,1,0:T(8,128)(2,1)S(1)}, u32[]{:S(2)}) copy-start(bf16[16,2,8,128]{3,2,1,0:T(8,128)(2,1)S(1)} %all-to-all-done) | copy-start | bytes 196612

commit v3 on v2

--- a/solution.py
+++ b/solution.py
@@ -8,6 +8,7 @@
 from jax.sharding import PartitionSpec as P
 
 CORES = 2
+PIECE = 512
 AHEAD = 2
 NT = (((1,), (1,)), ((), ()))
 NN = (((1,), (0,)), ((), ()))
@@ -54,12 +55,18 @@
     per = count // len(outs)
     for slot in range(count):
         copies[slot][0].wait()
-        part = lax.dot_general(abuf[slot], wide_in[...], NN, preferred_element_type=jnp.float32)
         copies[slot][1].wait()
         if slot + AHEAD < count:
             copies[slot + AHEAD][0].start()
             copies[slot + AHEAD][1].start()
-        part = part + lax.dot_general(obuf[slot], wide_out[...], NN, preferred_element_type=jnp.float32)
+        pieces = [
+            lax.dot_general(
+                buf[slot, :, at : at + PIECE], wide[at : at + PIECE], NN, preferred_element_type=jnp.float32
+            )
+            for buf, wide in ((abuf, wide_in), (obuf, wide_out))
+            for at in range(0, wide.shape[0], PIECE)
+        ]
+        part = sum(pieces[2::2], pieces[0]) + sum(pieces[3::2], pieces[1])
         length = lenbuf[seqs[slot]]
         scale = jnp.where(lane < rank, 1.0 / length.astype(jnp.float32), 1.0)
         outs[slot // per][slot % per] = jnp.where(row < length, part * scale, 0.0)
@@ -73,7 +80,7 @@
     return pl.pallas_call(
         functools.partial(project_kernel, steps, share, len(after)),
         out_shape=[jax.ShapeDtypeStruct((len(group) * share, slots, 2 * rank), jnp.float32) for group in groups],
-        in_specs=[pl.BlockSpec(memory_space=pl.ANY)] * (5 + len(after)),
+        in_specs=[pl.BlockSpec(memory_space=pl.ANY)] * 5 + [pl.BlockSpec(memory_space=pltpu.VMEM)] * len(after),
         out_specs=[pl.BlockSpec(memory_space=pltpu.VMEM)] * len(groups),
         scratch_shapes=[
             pltpu.VMEM((count, slots, feat), act.dtype),
@@ -96,18 +103,18 @@
     )(act, og, wi, wo, lens, *after)
 
 
-def unit_kernel(share, rank, size, groups, *refs):
+def unit_kernel(share, rank, size, *refs):
     parts, out, pairs = refs[:-2], refs[-2], refs[-1]
     rows = rank * rank // 128
     span = rows // size
     lane = lax.broadcasted_iota(jnp.int32, (rows, 2 * rank), 1)
+    dot = functools.partial(lax.dot_general, dimension_numbers=TN, preferred_element_type=jnp.float32)
     for k in range(share):
         full = parts[0][k]
         for part in parts[1:]:
             full = full + part[k]
         high = full.astype(jnp.bfloat16)
         low = (full - high.astype(jnp.float32)).astype(jnp.bfloat16)
-        dot = functools.partial(lax.dot_general, dimension_numbers=TN, preferred_element_type=jnp.float32)
         both = dot(high, high) + (dot(high, low) + dot(low, high))
         pairs[k] = both[:rank]
     for k in range(share):
@@ -115,61 +122,50 @@
         odd = pairs[k, pl.ds(1, rows, stride=2), :]
         flat = jnp.where(lane < rank, even, odd)
         scale = jnp.sqrt(jnp.sum(flat * flat) / (rank * rank) + 1e-06)
-        unit = (flat / scale).astype(jnp.bfloat16)
-        for to in range(groups * size):
-            at = to % size * span
-            out[to, k] = unit[at : at + span]
-
-
-def units(parts, share, rank, size, groups):
+        unit = flat / scale
+        for to in range(size):
+            out[to, k] = unit[to * span : (to + 1) * span]
+
+
+def units(parts, share, rank, size):
     span = rank * rank // 128 // size
     return pl.pallas_call(
-        functools.partial(unit_kernel, share, rank, size, groups),
-        out_shape=jax.ShapeDtypeStruct((groups * size, share, span, 128), jnp.bfloat16),
+        functools.partial(unit_kernel, share, rank, size),
+        out_shape=jax.ShapeDtypeStruct((size, share, span, 128), jnp.float32),
         in_specs=[pl.BlockSpec(memory_space=pltpu.VMEM)] * len(parts),
         out_specs=pl.BlockSpec(memory_space=pltpu.VMEM),
         scratch_shapes=[pltpu.VMEM((share, rank, 2 * rank), jnp.float32)],
     )(*parts)
 
 
-def score_kernel(size, unit_ref, test_ref, out):
+def score_kernel(unit_ref, *refs):
+    test_refs, out = refs[:-1], refs[-1]
+    dp = lax.axis_index("dp")
     span = unit_ref.shape[1]
-    whole = unit_ref[...].astype(jnp.float32)
-    unit = jnp.concatenate([whole[:, c, :] for c in range(span)], axis=1).astype(jnp.bfloat16)
-    part = lax.dot_general(unit, test_ref[...], NT, preferred_element_type=jnp.float32)
-    rows = out.shape[1]
-    for to in range(out.shape[0]):
-        at = to // size * rows
-        out[to] = part[at : at + rows]
-
-
-def score(unit_all, own_tests, size, groups):
-    seqs, tests = unit_all.shape[0], own_tests.shape[0]
+    unit = jnp.concatenate([unit_ref[:, c, :] for c in range(span)], axis=1).astype(jnp.bfloat16)
+    tests = test_refs[0].shape[0]
+    for step, test_ref in enumerate(test_refs):
+        part = lax.dot_general(unit, test_ref[...], NT, preferred_element_type=jnp.float32)
+        for to in range(out.shape[0]):
+            out[to, :, pl.ds(pl.multiple_of((dp ^ step) * tests, 128), tests)] = part
+
+
+def score(unit_all, test_parts, size):
+    seqs, tests = unit_all.shape[0], test_parts[0].shape[0]
     return pl.pallas_call(
-        functools.partial(score_kernel, size),
-        out_shape=jax.ShapeDtypeStruct((groups * size, seqs // groups, tests), jnp.float32),
-        in_specs=[pl.BlockSpec(memory_space=pltpu.VMEM)] * 2,
+        score_kernel,
+        out_shape=jax.ShapeDtypeStruct((size, seqs, tests * len(test_parts)), jnp.float32),
+        in_specs=[pl.BlockSpec(memory_space=pltpu.VMEM)] * (1 + len(test_parts)),
         out_specs=pl.BlockSpec(memory_space=pltpu.VMEM),
-    )(unit_all, own_tests)
-
-
-def finish_kernel(size, parts, out):
-    tests = parts.shape[2]
-    for group in range(parts.shape[0] // size):
-        total = parts[group * size]
-        for i in range(1, size):
-            total = total + parts[group * size + i]
-        out[:, group * tests : (group + 1) * tests] = total
-
-
-def finish(parts, size):
-    count, rows, tests = parts.shape
-    return pl.pallas_call(
-        functools.partial(finish_kernel, size),
-        out_shape=jax.ShapeDtypeStruct((rows, count // size * tests), jnp.float32),
-        in_specs=[pl.BlockSpec(memory_space=pltpu.VMEM)],
-        out_specs=pl.BlockSpec(memory_space=pltpu.VMEM),
-    )(parts)
+    )(unit_all, *test_parts)
+
+
+def gather_tests(own, groups):
+    if groups == 4:
+        across = xor_permute(own, "dp", groups, 3)
+        beside = xor_permute(own, "dp", groups, 1)
+        return [own, beside, xor_permute(across, "dp", groups, 1), across]
+    return [own] + [xor_permute(own, "dp", groups, step) for step in range(1, groups)]
 
 
 def shards(size, groups, activations, out_grads, proj_in, proj_out, lengths, test_grads):
@@ -178,19 +174,20 @@
     me = lax.axis_index("tensor")
     width = test_grads.shape[1] // size
     own_tests = lax.dynamic_slice_in_dim(test_grads, me * width, width, 1)
+    test_parts = gather_tests(own_tests, groups)
 
     far = [CORES * x for x in range(1, size // CORES)]
-    arrays = (activations, out_grads, proj_in.T, proj_out.T, lengths)
-    far_other, far_own = project(*arrays, [[step ^ 1 for step in far], far], share)
+    arrays = (activations, out_grads, proj_in.T, proj_out.T)
+    far_other, far_own = project(*arrays, lengths, [[step ^ 1 for step in far], far], share, [own_tests])
     far_sum = far_own + xor_permute(far_other, "tensor", size, 1)
     sums = [xor_permute(far_sum[i * share : (i + 1) * share], "tensor", size, step) for i, step in enumerate(far)]
-    near_other, near_own = project(*arrays, [[1], [0]], share, [far_sum])
+    near_other, near_own = project(*arrays, lengths, [[1], [0]], share, [far_sum])
     arrived = xor_permute(near_other, "tensor", size, 1)
-    unit_cut = units([near_own, arrived] + sums, share, rank, size, groups)
-    unit_all = lax.all_to_all(unit_cut, ("dp", "tensor"), 0, 0, tiled=True)
-    part = score(unit_all.reshape(-1, *unit_all.shape[2:]), own_tests, size, groups)
-    parts = lax.all_to_all(part, ("dp", "tensor"), 0, 0, tiled=True)
-    return finish(parts, size)
+    unit_cut = units([near_own, arrived] + sums, share, rank, size)
+    unit_all = lax.all_to_all(unit_cut, "tensor", 0, 0, tiled=True)
+    part = score(unit_all.reshape(-1, *unit_all.shape[2:]), test_parts, size)
+    parts = lax.all_to_all(part, "tensor", 0, 0, tiled=True)
+    return functools.reduce(jnp.add, [parts[i] for i in range(size)])
 
 
 def solution(mesh):

time: 57.2 us -> 53.1 us (0.928)
  waiting for transfers between devices: 14.3 us -> 8.93 us
  blocking collectives: 11 us -> 7.37 us
  starting transfers between devices: 9.76 us -> 12.2 us
  local copies, waits for them, and re-layouts: 2.06 us -> 3.28 us
  other arithmetic: 1.69 us -> 2.3 us
  Pallas kernels: 17.9 us -> 18.5 us
    ppermute x3 -> x6, starting transfers between devices: 3.59 us -> 8.94 us  [xor_permute(): return lax.ppermute(value, axis, [(i, i ^ step) for i in range(size)])]
    all_to_all x1, blocking collectives: 11 us -> 7.37 us  [shards(): parts = lax.all_to_all(part, 'tensor', 0, 0, tiled=True)]
    all_to_all x1, starting transfers between devices: 6.17 us -> 3.26 us  [shards(): unit_all = lax.all_to_all(unit_cut, 'tensor', 0, 0, tiled=True)]
    all_to_all x1, waiting for transfers between devices: 6.15 us -> 3.31 us  [shards(): unit_all = lax.all_to_all(unit_cut, 'tensor', 0, 0, tiled=True)]
    ppermute x3 -> x6, waiting for transfers between devices: 8.19 us -> 5.62 us  [xor_permute(): return lax.ppermute(value, axis, [(i, i ^ step) for i in range(size)])]
    pallas_call x2, Pallas kernels: 12.4 us -> 14 us  [project(): pl.pallas_call(functools.partial(project_kernel, steps, share, len(after)...]
    unnamed x10 -> x18, local copies, waits for them, and re-layouts: 1.33 us -> 2.55 us
    pallas_call x3 -> x2, Pallas kernels: 5.55 us -> 4.48 us  [the longest x1 2.25 us: units(): pl.pallas_call(functools.partial(unit_kernel, share, rank, size), out_sha...]
  transfers between devices with their start and end apart: 4 -> 7, of which waited for: 3 -> 3; matrix products, arithmetic and copies ran while one was open for 1% -> 3% of each run, Pallas kernels for 0% -> 18%
where the time goes in v3:
time: 53.1 us; the launch traced here: 52.6 us
  Pallas kernels  18.5 us (35%)
  starting transfers between devices  12.2 us (23%)
  waiting for transfers between devices  8.93 us (17%)
  blocking collectives  7.37 us (14%)
  local copies, waits for them, and re-layouts  3.28 us (6%)
  other arithmetic  2.3 us (4%)
    pallas_call x2, Pallas kernels, project(): pl.pallas_call(functools.partial(project_kernel, steps, share, len(after)...  14 us
    ppermute x6, starting transfers between devices, xor_permute(): return lax.ppermute(value, axis, [(i, i ^ step) for i in range(size)])  8.94 us
    all_to_all x1, blocking collectives, shards(): parts = lax.all_to_all(part, 'tensor', 0, 0, tiled=True)  7.37 us
    ppermute x6, waiting for transfers between devices, xor_permute(): return lax.ppermute(value, axis, [(i, i ^ step) for i in range(size)])  5.62 us
    all_to_all x1, waiting for transfers between devices, shards(): unit_all = lax.all_to_all(unit_cut, 'tensor', 0, 0, tiled=True)  3.31 us
    all_to_all x1, starting transfers between devices, shards(): unit_all = lax.all_to_all(unit_cut, 'tensor', 0, 0, tiled=True)  3.26 us
    unnamed x18, local copies, waits for them, and re-layouts  2.55 us
    pallas_call x1, Pallas kernels, units(): pl.pallas_call(functools.partial(unit_kernel, share, rank, size), out_sha...  2.25 us
  transfers between devices with their start and end apart: 7, of which 3 were waited for; matrix products, arithmetic and copies ran while one was open for 3% of the time, Pallas kernels for 18%

profile of v3, /device:TPU:0, one launch (start us, length us, event | category | flops | bytes accessed | tf_op | source)
XLA Modules:
  0.0 52.6 jit_solution(17181247964615584306)
XLA Ops:
  0.0 0.0 copy-start
  0.0 1.2 %copy-done = bf16[128,4096]{1,0:T(8,128)(2,1)S(1)} copy-done((bf16[128,4096]{1,0:T(8,128)(2,1)S(1)}, bf16[128,4096]{1,0:T(8,128)(2,1)}, u32[]{:S(2)}) %copy-start) | copy-done | bytes 1048600
  1.2 0.7 %constant_dynamic-slice_fusion.refs_0_ = bf16[128,1024]{1,0:T(8,128)(2,1)} fusion(bf16[128,4096]{1,0:T(8,128)(2,1)S(1)} %copy-done, s32[]{:T(128)S(6)} %select_n.3), kind=kLoop, calls=%fused_computation.4 | loop fusion | bytes 524292 | tf_op jit(solution)/shard_map/dynamic_slice | solution.py:176
  2.0 7.0 %shard_map.64 = (f32[2,256,128]{2,1,0:T(8,128)}, f32[2,256,128]{2,1,0:T(8,128)}) custom-call(bf16[8,256,1024]{2,1,0:T(8,128)(2,1)} %act.3, bf16[8,256,3584]{2,1,0:T(8,128)(2,1)} %og.3, bf16[64,1024]{1,0:T(8,128)(2,1)} %bitcast.7, bf16[64,3584]{1,0:T(8,128)(2,1)} %bitcast.5, s32[8]{0:T(128)} %lens.3, bf16[128,1024]{1,0:T(8,128)(2,1)} %constant_dynamic-slice_fusion.refs_0_), custom_call_target="tpu_custom_call" | custom-call | flops 2415919104 | bytes 9437184 | tf_op jit(solution)/shard_map/pallas_call | solution.py:80
  9.0 0.5 collective-permute-start
  9.5 0.0 copy-done.1
  9.5 4.7 %collective-permute-start.4 = (bf16[128,1024]{1,0:T(8,128)(2,1)S(1)}, bf16[128,1024]{1,0:T(8,128)(2,1)S(1)}, u32[]{:S(2)}, u32[]{:S(2)}) collective-permute-start(bf16[128,1024]{1,0:T(8,128)(2,1)S(1)} %copy-done.1), channel_id=1, source_target_pairs={{0,12},{4,8},{8,4},{12,0},{1,13},{5,9},{9,5},{13,1},{2,14},{6,10},... | collective-permute-start | bytes 786440 | tf_op jit(solution)/shard_map/ppermute | solution.py:20
  14.2 0.0 collective-permute-done
  14.2 1.7 %add.21.refs_0_ = f32[2,256,128]{2,1,0:T(8,128)} add(f32[2,256,128]{2,1,0:T(8,128)} %get-tuple-element.9, f32[2,256,128]{2,1,0:T(8,128)S(1)} %collective-permute-done) | non-fusion elementwise | flops 65536 | bytes 786432 | tf_op jit(solution)/shard_map/add | solution.py:182
  15.9 7.0 %shard_map.65 = (f32[2,256,128]{2,1,0:T(8,128)}, f32[2,256,128]{2,1,0:T(8,128)}) custom-call(bf16[8,256,1024]{2,1,0:T(8,128)(2,1)} %act.3, bf16[8,256,3584]{2,1,0:T(8,128)(2,1)} %og.3, bf16[64,1024]{1,0:T(8,128)(2,1)} %bitcast.8, bf16[64,3584]{1,0:T(8,128)(2,1)} %bitcast.6, s32[8]{0:T(128)} %lens.3, f32[2,256,128]{2,1,0:T(8,128)} %add.21.refs_0_), custom_call_target="tpu_custom_call" | custom-call | flops 2415919104 | bytes 9437184 | tf_op jit(solution)/shard_map/pallas_call | solution.py:80
  22.9 0.2 collective-permute-start.1
  23.1 0.0 copy-done.2
  23.1 1.5 %collective-permute-start.2 = (f32[2,256,128]{2,1,0:T(8,128)S(1)}, f32[2,256,128]{2,1,0:T(8,128)S(1)}, u32[]{:S(2)}, u32[]{:S(2)}) collective-permute-start(f32[2,256,128]{2,1,0:T(8,128)S(1)} %copy-done.2), channel_id=1, source_target_pairs={{0,2},{1,3},{2,0},{3,1},{4,6},{5,7},{6,4},{7,5},{8,10},{9,11},{10,... | collective-permute-start | bytes 786440 | tf_op jit(solution)/shard_map/ppermute | solution.py:20
  24.6 0.0 collective-permute-start.3
  24.6 0.0 collective-permute-done.4.refs_3_
  24.6 2.0 %collective-permute-start.5 = (bf16[128,1024]{1,0:T(8,128)(2,1)S(1)}, bf16[128,1024]{1,0:T(8,128)(2,1)S(1)}, u32[]{:S(2)}, u32[]{:S(2)}) collective-permute-start(bf16[128,1024]{1,0:T(8,128)(2,1)S(1)} %collective-permute-done.4.refs_3_), channel_id=1, source_target_pairs={{0,4},{4,0},{8,12},{12,8},{1,5},{5,1},{9,13},{13,9},{2,6},{6,2},{1... | collective-permute-start | bytes 786440 | tf_op jit(solution)/shard_map/ppermute | solution.py:20
  26.6 0.0 collective-permute-done.1.refs_1_
  26.6 5.0 %collective-permute-done.2.refs_2_ = f32[2,256,128]{2,1,0:T(8,128)S(1)} collective-permute-done((f32[2,256,128]{2,1,0:T(8,128)S(1)}, f32[2,256,128]{2,1,0:T(8,128)S(1)}, u32[]{:S(2)}, u32[]{:S(2)}) %collective-permute-start.2) | collective-permute-done | bytes 262176 | tf_op jit(solution)/shard_map/ppermute | solution.py:20
  31.6 0.0 copy-done.3
  31.7 0.7 %copy-done.4 = f32[2,256,128]{2,1,0:T(8,128)} copy-done((f32[2,256,128]{2,1,0:T(8,128)}, f32[2,256,128]{2,1,0:T(8,128)S(1)}, u32[]{:S(2)}) %copy-start.4) | copy-done | bytes 262168
  32.4 2.3 %shard_map.66 = f32[4,2,8,128]{3,2,1,0:T(8,128)} custom-call(f32[2,256,128]{2,1,0:T(8,128)} %get-tuple-element.11.refs_0_, f32[2,256,128]{2,1,0:T(8,128)} %copy-done.3, f32[2,256,128]{2,1,0:T(8,128)} %copy-done.4), custom_call_target="tpu_custom_call" | custom-call | tf_op jit(solution)/shard_map/pallas_call | solution.py:132
  34.6 3.3 %all-to-all-start = ((f32[4,2,8,128]{3,2,1,0:T(8,128)}), f32[4,2,8,128]{3,2,1,0:T(8,128)S(1)}, u32[]{:S(2)}, u32[]{:S(2)}) async-start(f32[4,2,8,128]{3,2,1,0:T(8,128)} %shard_map.66), calls=%async_computation | async-start | bytes 65536 | tf_op jit(solution)/shard_map/all_to_all | solution.py:187
  37.9 0.0 collective-permute-done.3.refs_1_
  37.9 0.0 copy-start.6
  37.9 0.6 %collective-permute-done.5.refs_2_ = bf16[128,1024]{1,0:T(8,128)(2,1)S(1)} collective-permute-done((bf16[128,1024]{1,0:T(8,128)(2,1)S(1)}, bf16[128,1024]{1,0:T(8,128)(2,1)S(1)}, u32[]{:S(2)}, u32[]{:S(2)}) %collective-permute-start.5) | collective-permute-done | bytes 262176 | tf_op jit(solution)/shard_map/ppermute | solution.py:20
  38.5 3.3 %all-to-all-done = f32[4,2,8,128]{3,2,1,0:T(8,128)S(1)} async-done(((f32[4,2,8,128]{3,2,1,0:T(8,128)}), f32[4,2,8,128]{3,2,1,0:T(8,128)S(1)}, u32[]{:S(2)}, u32[]{:S(2)}) %all-to-all-start) | async-done | bytes 32800 | tf_op jit(solution)/shard_map/all_to_all | solution.py:187
  41.8 0.0 copy-done.5
  41.8 0.0 copy-done.7
  41.8 0.6 %copy-done.8 = f32[4,2,8,128]{3,2,1,0:T(8,128)} copy-done((f32[4,2,8,128]{3,2,1,0:T(8,128)}, f32[4,2,8,128]{3,2,1,0:T(8,128)S(1)}, u32[]{:S(2)}) %copy-start.8) | copy-done | bytes 32792
  42.4 2.2 %shard_map.67 = f32[4,8,512]{2,1,0:T(8,128)} custom-call(f32[8,8,128]{2,1,0:T(8,128)} %bitcast.9, bf16[128,1024]{1,0:T(8,128)(2,1)} %constant_dynamic-slice_fusion.refs_0_, bf16[128,1024]{1,0:T(8,128)(2,1)} %copy-done.6, bf16[128,1024]{1,0:T(8,128)(2,1)} %copy-done.7, bf16[128,1024]{1,0:T(8,128)(2,1)} %copy-done.5), custom_call_target="tpu_custom_call" | custom-call | tf_op jit(solution)/shard_map/pallas_call | solution.py:155
  44.6 7.4 %all_to_all.10 = f32[4,8,512]{2,1,0:T(8,128)S(1)} all-to-all(f32[4,8,512]{2,1,0:T(8,128)} %shard_map.67), channel_id=1, replica_groups=mesh['groups'=2,'dp'=4,'tensor'=4] {'tensor'}, dimensions={0} | all-to-all | bytes 131072 | tf_op jit(solution)/shard_map/all_to_all | solution.py:189
  52.0 0.6 %fusion = f32[8,512]{1,0:T(8,128)} fusion(f32[4,8,512]{2,1,0:T(8,128)S(1)} %all_to_all.10), kind=kLoop, calls=%fused_computation.1 | loop fusion | flops 12288 | bytes 81920 | tf_op jit(solution)/shard_map/add | solution.py:190
  (8 shorter events, 0.0 us)
Async XLA Ops:
  0.0 1.2 %copy-start = (bf16[128,4096]{1,0:T(8,128)(2,1)S(1)}, bf16[128,4096]{1,0:T(8,128)(2,1)}, u32[]{:S(2)}) copy-start(bf16[128,4096]{1,0:T(8,128)(2,1)} %param.11) | copy-start | bytes 3145732
  2.0 7.5 %copy-start.1 = (bf16[128,1024]{1,0:T(8,128)(2,1)S(1)}, bf16[128,1024]{1,0:T(8,128)(2,1)}, u32[]{:S(2)}) copy-start(bf16[128,1024]{1,0:T(8,128)(2,1)} %constant_dynamic-slice_fusion.refs_0_) | copy-start | bytes 786436
  9.0 5.2 %collective-permute-start = (f32[2,256,128]{2,1,0:T(8,128)}, f32[2,256,128]{2,1,0:T(8,128)S(1)}, u32[]{:S(2)}, u32[]{:S(2)}) collective-permute-start(f32[2,256,128]{2,1,0:T(8,128)} %get-tuple-element.10), channel_id=1, source_target_pairs={{0,1},{1,0},{2,3},{3,2},{4,5},{5,4},{6,7},{7,6},{8,9},{9,8},{10,11... | collective-permute-start | bytes 786440 | tf_op jit(solution)/shard_map/ppermute | solution.py:20
  9.5 15.1 %collective-permute-start.4 = (bf16[128,1024]{1,0:T(8,128)(2,1)S(1)}, bf16[128,1024]{1,0:T(8,128)(2,1)S(1)}, u32[]{:S(2)}, u32[]{:S(2)}) collective-permute-start(bf16[128,1024]{1,0:T(8,128)(2,1)S(1)} %copy-done.1), channel_id=1, source_target_pairs={{0,12},{4,8},{8,4},{12,0},{1,13},{5,9},{9,5},{13,1},{2,14},{6,10},... | collective-permute-start | bytes 786440 | tf_op jit(solution)/shard_map/ppermute | solution.py:20
  15.9 7.2 %copy-start.2 = (f32[2,256,128]{2,1,0:T(8,128)S(1)}, f32[2,256,128]{2,1,0:T(8,128)}, u32[]{:S(2)}) copy-start(f32[2,256,128]{2,1,0:T(8,128)} %add.21.refs_0_) | copy-start | bytes 786436
  22.9 3.8 %collective-permute-start.1 = (f32[2,256,128]{2,1,0:T(8,128)}, f32[2,256,128]{2,1,0:T(8,128)S(1)}, u32[]{:S(2)}, u32[]{:S(2)}) collective-permute-start(f32[2,256,128]{2,1,0:T(8,128)} %get-tuple-element.12), channel_id=1, source_target_pairs={{0,1},{1,0},{2,3},{3,2},{4,5},{5,4},{6,7},{7,6},{8,9},{9,8},{10,11... | collective-permute-start | bytes 786440 | tf_op jit(solution)/shard_map/ppermute | solution.py:20
  23.1 8.6 %collective-permute-start.2 = (f32[2,256,128]{2,1,0:T(8,128)S(1)}, f32[2,256,128]{2,1,0:T(8,128)S(1)}, u32[]{:S(2)}, u32[]{:S(2)}) collective-permute-start(f32[2,256,128]{2,1,0:T(8,128)S(1)} %copy-done.2), channel_id=1, source_target_pairs={{0,2},{1,3},{2,0},{3,1},{4,6},{5,7},{6,4},{7,5},{8,10},{9,11},{10,... | collective-permute-start | bytes 786440 | tf_op jit(solution)/shard_map/ppermute | solution.py:20
  24.6 13.3 %collective-permute-start.3 = (bf16[128,1024]{1,0:T(8,128)(2,1)S(1)}, bf16[128,1024]{1,0:T(8,128)(2,1)S(1)}, u32[]{:S(2)}, u32[]{:S(2)}) collective-permute-start(bf16[128,1024]{1,0:T(8,128)(2,1)S(1)} %copy-done.1), channel_id=1, source_target_pairs={{0,4},{4,0},{8,12},{12,8},{1,5},{5,1},{9,13},{13,9},{2,6},{6,2},{1... | collective-permute-start | bytes 786440 | tf_op jit(solution)/shard_map/ppermute | solution.py:20
  24.6 17.2 %copy-start.5 = (bf16[128,1024]{1,0:T(8,128)(2,1)}, bf16[128,1024]{1,0:T(8,128)(2,1)S(1)}, u32[]{:S(2)}) copy-start(bf16[128,1024]{1,0:T(8,128)(2,1)S(1)} %collective-permute-done.4.refs_3_) | copy-start | bytes 786436
  24.6 13.9 %collective-permute-start.5 = (bf16[128,1024]{1,0:T(8,128)(2,1)S(1)}, bf16[128,1024]{1,0:T(8,128)(2,1)S(1)}, u32[]{:S(2)}, u32[]{:S(2)}) collective-permute-start(bf16[128,1024]{1,0:T(8,128)(2,1)S(1)} %collective-permute-done.4.refs_3_), channel_id=1, source_target_pairs={{0,4},{4,0},{8,12},{12,8},{1,5},{5,1},{9,13},{13,9},{2,6},{6,2},{1... | collective-permute-start | bytes 786440 | tf_op jit(solution)/shard_map/ppermute | solution.py:20
  26.6 5.0 %copy-start.3 = (f32[2,256,128]{2,1,0:T(8,128)}, f32[2,256,128]{2,1,0:T(8,128)S(1)}, u32[]{:S(2)}) copy-start(f32[2,256,128]{2,1,0:T(8,128)S(1)} %collective-permute-done.1.refs_1_) | copy-start | bytes 786436
  31.6 0.7 %copy-start.4 = (f32[2,256,128]{2,1,0:T(8,128)}, f32[2,256,128]{2,1,0:T(8,128)S(1)}, u32[]{:S(2)}) copy-start(f32[2,256,128]{2,1,0:T(8,128)S(1)} %collective-permute-done.2.refs_2_) | copy-start | bytes 786436
  34.6 7.2 %all-to-all-start = ((f32[4,2,8,128]{3,2,1,0:T(8,128)}), f32[4,2,8,128]{3,2,1,0:T(8,128)S(1)}, u32[]{:S(2)}, u32[]{:S(2)}) async-start(f32[4,2,8,128]{3,2,1,0:T(8,128)} %shard_map.66), calls=%async_computation | async-start | bytes 65536 | tf_op jit(solution)/shard_map/all_to_all | solution.py:187
  37.9 3.9 %copy-start.6 = (bf16[128,1024]{1,0:T(8,128)(2,1)}, bf16[128,1024]{1,0:T(8,128)(2,1)S(1)}, u32[]{:S(2)}) copy-start(bf16[128,1024]{1,0:T(8,128)(2,1)S(1)} %collective-permute-done.3.refs_1_) | copy-start | bytes 786436
  38.5 3.3 %copy-start.7 = (bf16[128,1024]{1,0:T(8,128)(2,1)}, bf16[128,1024]{1,0:T(8,128)(2,1)S(1)}, u32[]{:S(2)}) copy-start(bf16[128,1024]{1,0:T(8,128)(2,1)S(1)} %collective-permute-done.5.refs_2_) | copy-start | bytes 786436
  41.8 0.6 %copy-start.8 = (f32[4,2,8,128]{3,2,1,0:T(8,128)}, f32[4,2,8,128]{3,2,1,0:T(8,128)S(1)}, u32[]{:S(2)}) copy-start(f32[4,2,8,128]{3,2,1,0:T(8,128)S(1)} %all-to-all-done) | copy-start | bytes 98308

commit v4 on v3

v4 whole, which is shorter than its diff:
```python
import functools

import jax
import jax.numpy as jnp
from jax import lax
from jax.experimental import pallas as pl
from jax.experimental.pallas import tpu as pltpu
from jax.sharding import PartitionSpec as P

CORES = 2
AHEAD = 2
NT = (((1,), (1,)), ((), ()))
HBM = pl.BlockSpec(memory_space=pltpu.HBM)
in_hbm = functools.partial(pltpu.with_memory_space_constraint, memory_space=pltpu.HBM)
VMEM = pl.BlockSpec(memory_space=pltpu.VMEM)


def xor_permute(value, axis, size, step):
    return lax.ppermute(value, axis, [(i, i ^ step) for i in range(size)])


def cut_kernel(tests, out, sem):
    width = out.shape[1]
    start = pl.multiple_of(lax.axis_index("tensor") * width, 128)
    copy = pltpu.make_async_copy(tests.at[:, pl.ds(start, width)], out, sem)
    copy.start()
    copy.wait()


def cut_tests(tests, size):
    rows, width = tests.shape
    return pl.pallas_call(
        cut_kernel,
        out_shape=jax.ShapeDtypeStruct((rows, width // size), tests.dtype),
        in_specs=[HBM],
        out_specs=VMEM,
        scratch_shapes=[pltpu.SemaphoreType.DMA],
    )(in_hbm(tests))


def project_kernel(steps, share, block, after, act, og, wi, wo, lens, *refs):
    refs = refs[after:]
    outs, (abuf, obuf, wibuf, wobuf, lenbuf, asem, osem, wsem) = refs[:-8], refs[-8:]
    me = lax.axis_index("tensor")
    rank, feat = wibuf.shape
    hidden = wobuf.shape[1]
    slots = abuf.shape[1]
    count = len(steps) * share
    seqs = [(me ^ step) * share + k for step in steps for k in range(share)]
    small = [
        pltpu.make_async_copy(wi, wibuf, wsem.at[0]),
        pltpu.make_async_copy(wo, wobuf, wsem.at[1]),
        pltpu.make_async_copy(lens, lenbuf, wsem.at[2]),
    ]
    copies = [
        (
            pltpu.make_async_copy(act.at[seq], abuf.at[slot], asem.at[slot]),
            pltpu.make_async_copy(og.at[seq], obuf.at[slot], osem.at[slot]),
        )
        for slot, seq in enumerate(seqs)
    ]
    for copy in small:
        copy.start()
    for slot in range(min(AHEAD * block, count)):
        copies[slot][0].start()
        copies[slot][1].start()
    for copy in small:
        copy.wait()
    col = lax.broadcasted_iota(jnp.int32, (rank, slots), 1)
    per = count // len(outs)
    for first in range(0, count, block):
        here = range(first, first + block)
        for slot in here:
            copies[slot][0].wait()
        tokens = abuf[first : first + block].reshape(block * slots, feat)
        part_in = lax.dot_general(wibuf[...], tokens, NT, preferred_element_type=jnp.float32)
        for slot in here:
            copies[slot][1].wait()
        for slot in here:
            if slot + AHEAD * block < count:
                copies[slot + AHEAD * block][0].start()
                copies[slot + AHEAD * block][1].start()
        tokens = obuf[first : first + block].reshape(block * slots, hidden)
        part_out = lax.dot_general(wobuf[...], tokens, NT, preferred_element_type=jnp.float32)
        for at, slot in enumerate(here):
            length = lenbuf[seqs[slot]]
            out = outs[slot // per]
            one = part_in[:, at * slots : (at + 1) * slots] * (1.0 / length.astype(jnp.float32))
            out[slot % per, :rank] = jnp.where(col < length, one, 0.0)
            out[slot % per, rank:] = part_out[:, at * slots : (at + 1) * slots]


def project(act, og, wi, wo, lens, groups, share, block, after=()):
    steps = [step for group in groups for step in group]
    count = len(steps) * share
    slots, feat, hidden = act.shape[1], act.shape[2], og.shape[2]
    rank = wi.shape[0]
    return pl.pallas_call(
        functools.partial(project_kernel, steps, share, block, len(after)),
        out_shape=[jax.ShapeDtypeStruct((len(group) * share, 2 * rank, slots), jnp.float32) for group in groups],
        in_specs=[HBM] * 5 + [VMEM] * len(after),
        out_specs=[VMEM] * len(groups),
        scratch_shapes=[
            pltpu.VMEM((count, slots, feat), act.dtype),
            pltpu.VMEM((count, slots, hidden), og.dtype),
            pltpu.VMEM((rank, feat), wi.dtype),
            pltpu.VMEM((rank, hidden), wo.dtype),
            pltpu.SMEM(lens.shape, lens.dtype),
            pltpu.SemaphoreType.DMA((count,)),
            pltpu.SemaphoreType.DMA((count,)),
            pltpu.SemaphoreType.DMA((3,)),
        ],
        compiler_params=pltpu.CompilerParams(vmem_limit_bytes=24 << 20),
        cost_estimate=pl.CostEstimate(
            flops=2 * count * slots * (feat + hidden) * 256,
            bytes_accessed=2 * count * slots * (feat + hidden),
            transcendentals=0,
        ),
    )(*map(in_hbm, (act, og, wi, wo, lens)), *after)


def unit_kernel(share, rank, size, *refs):
    singles, parts, outs = refs[:share], refs[share : -2 - size], refs[-2 - size : -2]
    pairs, held = refs[-2:]
    me = lax.axis_index("tensor")
    rows = rank * rank // 128
    span = rows // size
    dot = functools.partial(lax.dot_general, dimension_numbers=NT, preferred_element_type=jnp.float32)
    for k in range(share):
        full = singles[k][0]
        for part in parts:
            full = full + part[k]
        high = full.astype(jnp.bfloat16)
        low = (full - high.astype(jnp.float32)).astype(jnp.bfloat16)
        left, right = slice(None, rank), slice(rank, None)
        pairs[k] = dot(high[left], high[right]) + (dot(high[left], low[right]) + dot(low[left], high[right]))
    for k in range(share):
        even = pairs[k, pl.ds(0, rows, stride=2), :]
        odd = pairs[k, pl.ds(1, rows, stride=2), :]
        flat = jnp.concatenate([even, odd], axis=1)
        scale = jnp.sqrt(jnp.sum(flat * flat) / (rank * rank) + 1e-06)
        unit = flat / scale
        for to in range(size):
            held[to] = unit[to * span : (to + 1) * span]
        for step in range(size):
            outs[step][k] = held[me ^ step]


def units(parts, singles, share, rank, size):
    span = rank * rank // 128 // size
    return pl.pallas_call(
        functools.partial(unit_kernel, share, rank, size),
        out_shape=[jax.ShapeDtypeStruct((share, span, 128), jnp.float32)] * size,
        in_specs=[VMEM] * (share + len(parts)),
        out_specs=[VMEM] * size,
        scratch_shapes=[pltpu.VMEM((share, rank, rank), jnp.float32), pltpu.VMEM((size, span, 128), jnp.float32)],
    )(*singles, *parts)


def score_kernel(share, size, *refs):
    unit_refs, test_refs, out, held = refs[:size], refs[size:-2], refs[-2], refs[-1]
    me, dp = lax.axis_index("tensor"), lax.axis_index("dp")
    for step in range(size):
        for k in range(share):
            held[(me ^ step) * share + k] = unit_refs[step][k]
    unit = jnp.concatenate([held[:, c, :] for c in range(held.shape[1])], axis=1).astype(jnp.bfloat16)
    tests = test_refs[0].shape[0]
    for step, test_ref in enumerate(test_refs):
        part = lax.dot_general(unit, test_ref[...], NT, preferred_element_type=jnp.float32)
        out[:, pl.ds(pl.multiple_of((dp ^ step) * tests, 128), tests)] = part


def score(unit_parts, test_parts, share):
    size, groups = len(unit_parts), len(test_parts)
    tests, width = test_parts[0].shape
    return pl.pallas_call(
        functools.partial(score_kernel, share, size),
        out_shape=jax.ShapeDtypeStruct((share * size, tests * groups), jnp.float32),
        in_specs=[VMEM] * (size + groups),
        out_specs=VMEM,
        scratch_shapes=[pltpu.VMEM((share * size, width // 128, 128), jnp.float32)],
    )(*unit_parts, *test_parts)


def gather_tests(own, groups):
    if groups == 4:
        across = xor_permute(own, "dp", groups, 3)
        beside = xor_permute(own, "dp", groups, 1)
        return [own, beside, xor_permute(across, "dp", groups, 1), across]
    return [own] + [xor_permute(own, "dp", groups, step) for step in range(1, groups)]


def shards(size, groups, activations, out_grads, proj_in, proj_out, lengths, test_grads):
    rank = proj_in.shape[1]
    share = activations.shape[0] // size
    own_tests = cut_tests(test_grads, size)
    test_parts = gather_tests(own_tests, groups)

    far = [CORES * x for x in range(1, size // CORES)]
    arrays = (activations, out_grads, proj_in.T, proj_out.T, lengths)
    far_other, far_own = project(*arrays, [[step ^ 1 for step in far], far], share, 1, [own_tests])
    far_sum = far_own + xor_permute(far_other, "tensor", size, 1)
    sums = [xor_permute(far_sum[i * share : (i + 1) * share], "tensor", size, step) for i, step in enumerate(far)]
    near_other, near_own = project(*arrays, [[1], [0]], share, share, [far_sum])
    arrived = [xor_permute(near_other[k : k + 1], "tensor", size, 1) for k in range(share)]
    unit_outs = units([near_own] + sums, arrived, share, rank, size)
    unit_parts = [unit_outs[0]] + [xor_permute(unit_outs[step], "tensor", size, step) for step in range(1, size)]
    part = score(unit_parts, test_parts, share)
    parts = [part] + [xor_permute(part, "tensor", size, step) for step in range(1, size)]
    while len(parts) > 1:
        parts = [parts[i] + parts[i + 1] for i in range(0, len(parts), 2)]
    return parts[0]


def solution(mesh):
    placed = (
        P(("groups", "dp"), None, "tensor"),
        P(("groups", "dp"), None, "tensor"),
        P("tensor", None),
        P("tensor", None),
        P(("groups", "dp")),
        P(("groups", "dp"), None),
    )
    return jax.shard_map(
        functools.partial(shards, mesh.shape["tensor"], mesh.shape["dp"]),
        mesh=mesh,
        in_specs=placed,
        out_specs=P(("groups", "dp"), None),
        check_vma=False,
    )
```

time: 53.1 us -> 46.3 us (0.87)
  blocking collectives: 7.37 us -> 0 us
  starting transfers between devices: 12.2 us -> 15.9 us
  waiting for transfers between devices: 8.93 us -> 6.64 us
  Pallas kernels: 18.5 us -> 20.6 us
  local copies, waits for them, and re-layouts: 3.28 us -> 1.35 us
  other arithmetic: 2.3 us -> 1.37 us
    all_to_all x1 -> x0, blocking collectives: 7.37 us -> none  [shards(): parts = lax.all_to_all(part, 'tensor', 0, 0, tiled=True)]
    ppermute x6 -> x13, starting transfers between devices: 8.94 us -> 15.9 us  [xor_permute(): return lax.ppermute(value, axis, [(i, i ^ step) for i in range(size)])]
    all_to_all x1 -> x0, waiting for transfers between devices: 3.31 us -> none  [shards(): unit_all = lax.all_to_all(unit_cut, 'tensor', 0, 0, tiled=True)]
    all_to_all x1 -> x0, starting transfers between devices: 3.26 us -> none  [shards(): unit_all = lax.all_to_all(unit_cut, 'tensor', 0, 0, tiled=True)]
    pallas_call x3 -> x4, Pallas kernels: 16.2 us -> 18.3 us  [the longest x2 14.4 us: project(): pl.pallas_call(functools.partial(project_kernel, steps, share, block, len...]
    add x1, other arithmetic: 1.68 us -> 0.04 us  [shards(): far_sum = far_own + xor_permute(far_other, 'tensor', size, 1)]
    unnamed x18 -> x20, local copies, waits for them, and re-layouts: 2.55 us -> 1.33 us
    ppermute x6 -> x13, waiting for transfers between devices: 5.62 us -> 6.64 us  [xor_permute(): return lax.ppermute(value, axis, [(i, i ^ step) for i in range(size)])]
  transfers between devices with their start and end apart: 7 -> 13, of which waited for: 3 -> 5; matrix products, arithmetic and copies ran while one was open for 3% -> 0% of each run, Pallas kernels for 18% -> 18%
where the time goes in v4:
time: 46.3 us; the launch traced here: 46 us
  Pallas kernels  20.6 us (44%)
  starting transfers between devices  15.9 us (34%)
  waiting for transfers between devices  6.64 us (14%)
  other arithmetic  1.37 us (3%)
  local copies, waits for them, and re-layouts  1.35 us (3%)
    ppermute x13, starting transfers between devices, xor_permute(): return lax.ppermute(value, axis, [(i, i ^ step) for i in range(size)])  15.9 us
    pallas_call x2, Pallas kernels, project(): pl.pallas_call(functools.partial(project_kernel, steps, share, block, len...  14.4 us
    ppermute x13, waiting for transfers between devices, xor_permute(): return lax.ppermute(value, axis, [(i, i ^ step) for i in range(size)])  6.64 us
    pallas_call x1, Pallas kernels, units(): pl.pallas_call(functools.partial(unit_kernel, share, rank, size), out_sha...  2.28 us
    pallas_call x1, Pallas kernels, score(): pl.pallas_call(functools.partial(score_kernel, share, size), out_shape=ja...  2.25 us
    pallas_call x1, Pallas kernels, cut_tests(): pl.pallas_call(cut_kernel, out_shape=jax.ShapeDtypeStruct((rows, width //...  1.66 us
    unnamed x20, local copies, waits for them, and re-layouts  1.33 us
    add x1, other arithmetic, shards(): parts = [parts[i] + parts[i + 1] for i in range(0, len(parts), 2)]  1.33 us
  transfers between devices with their start and end apart: 13, of which 5 were waited for; matrix products, arithmetic and copies ran while one was open for 0% of the time, Pallas kernels for 18%

profile of v4, /device:TPU:0, one launch (start us, length us, event | category | flops | bytes accessed | tf_op | source)
XLA Modules:
  0.0 46.0 jit_solution(12960610601862298669)
XLA Ops:
  0.0 1.7 %shard_map.64.refs_0_.refs_4_ = bf16[128,1024]{1,0:T(8,128)(2,1)} custom-call(bf16[128,4096]{1,0:T(8,128)(2,1)} %tests.1), custom_call_target="tpu_custom_call" | custom-call | tf_op jit(solution)/shard_map/pallas_call | solution.py:32
  1.7 8.5 %shard_map.65 = (f32[2,128,256]{2,1,0:T(8,128)S(1)}, f32[2,128,256]{2,1,0:T(8,128)S(1)}) custom-call(bf16[8,256,1024]{2,1,0:T(8,128)(2,1)} %act.3, bf16[8,256,3584]{2,1,0:T(8,128)(2,1)} %og.3, bf16[64,1024]{1,0:T(8,128)(2,1)} %bitcast.4, bf16[64,3584]{1,0:T(8,128)(2,1)} %bitcast.2, s32[8]{0:T(128)} %lens.3, bf16[128,1024]{1,0:T(8,128)(2,1)} %shard_map.64.refs_0_.refs_4_), custom_call_target="tpu_custom_call" | custom-call | flops 2415919104 | bytes 9437184 | tf_op jit(solution)/shard_map/pallas_call | solution.py:98
  10.2 0.5 %collective-permute-start = (f32[2,128,256]{2,1,0:T(8,128)S(1)}, f32[2,128,256]{2,1,0:T(8,128)S(1)}, u32[]{:S(2)}, u32[]{:S(2)}) collective-permute-start(f32[2,128,256]{2,1,0:T(8,128)S(1)} %get-tuple-element.14), channel_id=1, source_target_pairs={{0,1},{1,0},{2,3},{3,2},{4,5},{5,4},{6,7},{7,6},{8,9},{9,8},{10,11... | collective-permute-start | bytes 786440 | tf_op jit(solution)/shard_map/ppermute | solution.py:19
  10.7 4.7 %collective-permute-start.8 = (bf16[128,1024]{1,0:T(8,128)(2,1)}, bf16[128,1024]{1,0:T(8,128)(2,1)S(1)}, u32[]{:S(2)}, u32[]{:S(2)}) collective-permute-start(bf16[128,1024]{1,0:T(8,128)(2,1)} %shard_map.64.refs_0_.refs_4_), channel_id=1, source_target_pairs={{0,12},{4,8},{8,4},{12,0},{1,13},{5,9},{9,5},{13,1},{2,14},{6,10},... | collective-permute-start | bytes 786440 | tf_op jit(solution)/shard_map/ppermute | solution.py:19
  15.4 0.0 collective-permute-done
  15.4 1.6 %collective-permute-start.3 = (f32[2,128,256]{2,1,0:T(8,128)S(1)}, f32[2,128,256]{2,1,0:T(8,128)S(1)}, u32[]{:S(2)}, u32[]{:S(2)}) collective-permute-start(f32[2,128,256]{2,1,0:T(8,128)S(1)} %add.12.refs_0_), channel_id=1, source_target_pairs={{0,2},{1,3},{2,0},{3,1},{4,6},{5,7},{6,4},{7,5},{8,10},{9,11},{10,... | collective-permute-start | bytes 786440 | tf_op jit(solution)/shard_map/ppermute | solution.py:19
  17.0 6.0 %shard_map.66 = (f32[2,128,256]{2,1,0:T(8,128)S(1)}, f32[2,128,256]{2,1,0:T(8,128)S(1)}) custom-call(bf16[8,256,1024]{2,1,0:T(8,128)(2,1)} %act.3, bf16[8,256,3584]{2,1,0:T(8,128)(2,1)} %og.3, bf16[64,1024]{1,0:T(8,128)(2,1)} %bitcast.5, bf16[64,3584]{1,0:T(8,128)(2,1)} %bitcast.3, s32[8]{0:T(128)} %lens.3, f32[2,128,256]{2,1,0:T(8,128)S(1)} %add.12.refs_0_), custom_call_target="tpu_custom_call" | custom-call | flops 2415919104 | bytes 9437184 | tf_op jit(solution)/shard_map/pallas_call | solution.py:98
  23.0 4.9 %collective-permute-start.9 = (bf16[128,1024]{1,0:T(8,128)(2,1)S(1)}, bf16[128,1024]{1,0:T(8,128)(2,1)S(1)}, u32[]{:S(2)}, u32[]{:S(2)}) collective-permute-start(bf16[128,1024]{1,0:T(8,128)(2,1)S(1)} %collective-permute-done.8.refs_7_), channel_id=1, source_target_pairs={{0,4},{4,0},{8,12},{12,8},{1,5},{5,1},{9,13},{13,9},{2,6},{6,2},{1... | collective-permute-start | bytes 786440 | tf_op jit(solution)/shard_map/ppermute | solution.py:19
  27.8 0.1 collective-permute-start.1
  27.9 0.5 %collective-permute-start.2 = (f32[1,128,256]{2,1,0:T(8,128)S(1)}, f32[1,128,256]{2,1,0:T(8,128)S(1)}, u32[]{:S(2)}, u32[]{:S(2)}) collective-permute-start(f32[1,128,256]{2,1,0:T(8,128)S(1)} %get-tuple-element.21), channel_id=1, source_target_pairs={{0,1},{1,0},{2,3},{3,2},{4,5},{5,4},{6,7},{7,6},{8,9},{9,8},{10,11... | collective-permute-start | bytes 393224 | tf_op jit(solution)/shard_map/ppermute | solution.py:19
  28.4 0.8 %collective-permute-done.1.refs_0_ = f32[1,128,256]{2,1,0:T(8,128)S(1)} collective-permute-done((f32[1,128,256]{2,1,0:T(8,128)S(1)}, f32[1,128,256]{2,1,0:T(8,128)S(1)}, u32[]{:S(2)}, u32[]{:S(2)}) %collective-permute-start.1) | collective-permute-done | bytes 131104 | tf_op jit(solution)/shard_map/ppermute | solution.py:19
  29.2 0.2 collective-permute-done.2.refs_1_
  29.5 0.4 copy-done.5
  29.9 0.2 copy-done.6
  30.1 0.1 copy-done.1
  30.2 2.3 %shard_map.67 = (f32[2,8,128]{2,1,0:T(8,128)}, f32[2,8,128]{2,1,0:T(8,128)}, f32[2,8,128]{2,1,0:T(8,128)}, f32[2,8,128]{2,1,0:T(8,128)}) custom-call(f32[1,128,256]{2,1,0:T(8,128)} %copy-done.5, f32[1,128,256]{2,1,0:T(8,128)} %copy-done.6, f32[2,128,256]{2,1,0:T(8,128)} %copy-done, f32[2,128,256]{2,1,0:T(8,128)} %copy-done.1), custom_call_target="tpu_custom_call" | custom-call | tf_op jit(solution)/shard_map/pallas_call | solution.py:151
  32.5 0.3 collective-permute-start.4
  32.8 1.5 %collective-permute-start.5 = (f32[2,8,128]{2,1,0:T(8,128)}, f32[2,8,128]{2,1,0:T(8,128)S(1)}, u32[]{:S(2)}, u32[]{:S(2)}) collective-permute-start(f32[2,8,128]{2,1,0:T(8,128)} %get-tuple-element.19), channel_id=1, source_target_pairs={{0,2},{1,3},{2,0},{3,1},{4,6},{5,7},{6,4},{7,5},{8,10},{9,11},{10,... | collective-permute-start | bytes 24584 | tf_op jit(solution)/shard_map/ppermute | solution.py:19
  34.3 0.0 collective-permute-start.6
  34.3 0.0 collective-permute-done.9.refs_6_
  34.4 0.0 collective-permute-done.4.refs_1_
  34.4 2.3 %collective-permute-done.5.refs_2_ = f32[2,8,128]{2,1,0:T(8,128)S(1)} collective-permute-done((f32[2,8,128]{2,1,0:T(8,128)}, f32[2,8,128]{2,1,0:T(8,128)S(1)}, u32[]{:S(2)}, u32[]{:S(2)}) %collective-permute-start.5) | collective-permute-done | bytes 8224 | tf_op jit(solution)/shard_map/ppermute | solution.py:19
  36.7 0.9 %collective-permute-done.6.refs_3_ = f32[2,8,128]{2,1,0:T(8,128)S(1)} collective-permute-done((f32[2,8,128]{2,1,0:T(8,128)}, f32[2,8,128]{2,1,0:T(8,128)S(1)}, u32[]{:S(2)}, u32[]{:S(2)}) %collective-permute-start.6) | collective-permute-done | bytes 8224 | tf_op jit(solution)/shard_map/ppermute | solution.py:19
  37.6 0.6 %copy-done.9 = f32[2,8,128]{2,1,0:T(8,128)} copy-done((f32[2,8,128]{2,1,0:T(8,128)}, f32[2,8,128]{2,1,0:T(8,128)S(1)}, u32[]{:S(2)}) %copy-start.9) | copy-done | bytes 8216
  38.2 2.2 %shard_map.68 = f32[8,512]{1,0:T(8,128)} custom-call(f32[2,8,128]{2,1,0:T(8,128)} %get-tuple-element.17.refs_0_, f32[2,8,128]{2,1,0:T(8,128)} %copy-done.7, f32[2,8,128]{2,1,0:T(8,128)} %copy-done.8, f32[2,8,128]{2,1,0:T(8,128)} %copy-done.9, bf16[128,1024]{1,0:T(8,128)(2,1)} %shard_map.64.refs_0_.refs_4_, bf16[128,1024]{1,0:T(8,128)(2,1)} %copy-done.3, ...), custom_call_target="tpu_custom_call" | custom-call | tf_op jit(solution)/shard_map/pallas_call | solution.py:176
  40.4 0.1 collective-permute-start.10
  40.5 0.6 %collective-permute-start.11 = (f32[8,512]{1,0:T(8,128)}, f32[8,512]{1,0:T(8,128)S(1)}, u32[]{:S(2)}, u32[]{:S(2)}) collective-permute-start(f32[8,512]{1,0:T(8,128)} %shard_map.68), channel_id=1, source_target_pairs={{0,2},{1,3},{2,0},{3,1},{4,6},{5,7},{6,4},{7,5},{8,10},{9,11},{10,... | collective-permute-start | bytes 49160 | tf_op jit(solution)/shard_map/ppermute | solution.py:19
  41.2 1.1 %collective-permute-start.12 = (f32[8,512]{1,0:T(8,128)}, f32[8,512]{1,0:T(8,128)S(1)}, u32[]{:S(2)}, u32[]{:S(2)}) collective-permute-start(f32[8,512]{1,0:T(8,128)} %shard_map.68), channel_id=1, source_target_pairs={{0,3},{1,2},{2,1},{3,0},{4,7},{5,6},{6,5},{7,4},{8,11},{9,10},{10,... | collective-permute-start | bytes 49160 | tf_op jit(solution)/shard_map/ppermute | solution.py:19
  42.3 0.0 collective-permute-done.10
  42.3 2.4 %collective-permute-done.11 = f32[8,512]{1,0:T(8,128)S(1)} collective-permute-done((f32[8,512]{1,0:T(8,128)}, f32[8,512]{1,0:T(8,128)S(1)}, u32[]{:S(2)}, u32[]{:S(2)}) %collective-permute-start.11) | collective-permute-done | bytes 16416 | tf_op jit(solution)/shard_map/ppermute | solution.py:19
  44.7 0.0 collective-permute-done.12
  44.7 1.3 %add_add_fusion = f32[8,512]{1,0:T(8,128)} fusion(f32[8,512]{1,0:T(8,128)S(1)} %collective-permute-done.11, f32[8,512]{1,0:T(8,128)S(1)} %collective-permute-done.12, f32[8,512]{1,0:T(8,128)} %shard_map.68, f32[8,512]{1,0:T(8,128)S(1)} %collective-permute-done.10), kind=kLoop, calls=%fused_computation | loop fusion | flops 12288 | bytes 81920 | tf_op jit(solution)/shard_map/add | solution.py:211
  (22 shorter events, 0.1 us)
Async XLA Ops:
  10.2 5.2 %collective-permute-start = (f32[2,128,256]{2,1,0:T(8,128)S(1)}, f32[2,128,256]{2,1,0:T(8,128)S(1)}, u32[]{:S(2)}, u32[]{:S(2)}) collective-permute-start(f32[2,128,256]{2,1,0:T(8,128)S(1)} %get-tuple-element.14), channel_id=1, source_target_pairs={{0,1},{1,0},{2,3},{3,2},{4,5},{5,4},{6,7},{7,6},{8,9},{9,8},{10,11... | collective-permute-start | bytes 786440 | tf_op jit(solution)/shard_map/ppermute | solution.py:19
  10.7 12.3 %collective-permute-start.8 = (bf16[128,1024]{1,0:T(8,128)(2,1)}, bf16[128,1024]{1,0:T(8,128)(2,1)S(1)}, u32[]{:S(2)}, u32[]{:S(2)}) collective-permute-start(bf16[128,1024]{1,0:T(8,128)(2,1)} %shard_map.64.refs_0_.refs_4_), channel_id=1, source_target_pairs={{0,12},{4,8},{8,4},{12,0},{1,13},{5,9},{9,5},{13,1},{2,14},{6,10},... | collective-permute-start | bytes 786440 | tf_op jit(solution)/shard_map/ppermute | solution.py:19
  15.3 19.0 %collective-permute-start.7 = (bf16[128,1024]{1,0:T(8,128)(2,1)}, bf16[128,1024]{1,0:T(8,128)(2,1)S(1)}, u32[]{:S(2)}, u32[]{:S(2)}) collective-permute-start(bf16[128,1024]{1,0:T(8,128)(2,1)} %shard_map.64.refs_0_.refs_4_), channel_id=1, source_target_pairs={{0,4},{4,0},{8,12},{12,8},{1,5},{5,1},{9,13},{13,9},{2,6},{6,2},{1... | collective-permute-start | bytes 786440 | tf_op jit(solution)/shard_map/ppermute | solution.py:19
  15.4 14.0 %collective-permute-start.3 = (f32[2,128,256]{2,1,0:T(8,128)S(1)}, f32[2,128,256]{2,1,0:T(8,128)S(1)}, u32[]{:S(2)}, u32[]{:S(2)}) collective-permute-start(f32[2,128,256]{2,1,0:T(8,128)S(1)} %add.12.refs_0_), channel_id=1, source_target_pairs={{0,2},{1,3},{2,0},{3,1},{4,6},{5,7},{6,4},{7,5},{8,10},{9,11},{10,... | collective-permute-start | bytes 786440 | tf_op jit(solution)/shard_map/ppermute | solution.py:19
  22.9 6.5 %copy-start = (f32[2,128,256]{2,1,0:T(8,128)}, f32[2,128,256]{2,1,0:T(8,128)S(1)}, u32[]{:S(2)}) copy-start(f32[2,128,256]{2,1,0:T(8,128)S(1)} %get-tuple-element.16.refs_2_) | copy-start | bytes 786436
  22.9 14.6 %copy-start.2 = (bf16[128,1024]{1,0:T(8,128)(2,1)}, bf16[128,1024]{1,0:T(8,128)(2,1)S(1)}, u32[]{:S(2)}) copy-start(bf16[128,1024]{1,0:T(8,128)(2,1)S(1)} %collective-permute-done.8.refs_7_) | copy-start | bytes 786436
  23.0 11.4 %collective-permute-start.9 = (bf16[128,1024]{1,0:T(8,128)(2,1)S(1)}, bf16[128,1024]{1,0:T(8,128)(2,1)S(1)}, u32[]{:S(2)}, u32[]{:S(2)}) collective-permute-start(bf16[128,1024]{1,0:T(8,128)(2,1)S(1)} %collective-permute-done.8.refs_7_), channel_id=1, source_target_pairs={{0,4},{4,0},{8,12},{12,8},{1,5},{5,1},{9,13},{13,9},{2,6},{6,2},{1... | collective-permute-start | bytes 786440 | tf_op jit(solution)/shard_map/ppermute | solution.py:19
  27.8 1.4 %collective-permute-start.1 = (f32[1,128,256]{2,1,0:T(8,128)S(1)}, f32[1,128,256]{2,1,0:T(8,128)S(1)}, u32[]{:S(2)}, u32[]{:S(2)}) collective-permute-start(f32[1,128,256]{2,1,0:T(8,128)S(1)} %get-tuple-element.22), channel_id=1, source_target_pairs={{0,1},{1,0},{2,3},{3,2},{4,5},{5,4},{6,7},{7,6},{8,9},{9,8},{10,11... | collective-permute-start | bytes 393224 | tf_op jit(solution)/shard_map/ppermute | solution.py:19
  27.9 1.5 %collective-permute-start.2 = (f32[1,128,256]{2,1,0:T(8,128)S(1)}, f32[1,128,256]{2,1,0:T(8,128)S(1)}, u32[]{:S(2)}, u32[]{:S(2)}) collective-permute-start(f32[1,128,256]{2,1,0:T(8,128)S(1)} %get-tuple-element.21), channel_id=1, source_target_pairs={{0,1},{1,0},{2,3},{3,2},{4,5},{5,4},{6,7},{7,6},{8,9},{9,8},{10,11... | collective-permute-start | bytes 393224 | tf_op jit(solution)/shard_map/ppermute | solution.py:19
  29.2 0.6 %copy-start.5 = (f32[1,128,256]{2,1,0:T(8,128)}, f32[1,128,256]{2,1,0:T(8,128)S(1)}, u32[]{:S(2)}) copy-start(f32[1,128,256]{2,1,0:T(8,128)S(1)} %collective-permute-done.1.refs_0_) | copy-start | bytes 393220
  29.4 0.7 %copy-start.6 = (f32[1,128,256]{2,1,0:T(8,128)}, f32[1,128,256]{2,1,0:T(8,128)S(1)}, u32[]{:S(2)}) copy-start(f32[1,128,256]{2,1,0:T(8,128)S(1)} %collective-permute-done.2.refs_1_) | copy-start | bytes 393220
  29.4 0.8 %copy-start.1 = (f32[2,128,256]{2,1,0:T(8,128)}, f32[2,128,256]{2,1,0:T(8,128)S(1)}, u32[]{:S(2)}) copy-start(f32[2,128,256]{2,1,0:T(8,128)S(1)} %collective-permute-done.3.refs_3_) | copy-start | bytes 786436
  32.5 1.9 %collective-permute-start.4 = (f32[2,8,128]{2,1,0:T(8,128)}, f32[2,8,128]{2,1,0:T(8,128)S(1)}, u32[]{:S(2)}, u32[]{:S(2)}) collective-permute-start(f32[2,8,128]{2,1,0:T(8,128)} %get-tuple-element.18), channel_id=1, source_target_pairs={{0,1},{1,0},{2,3},{3,2},{4,5},{5,4},{6,7},{7,6},{8,9},{9,8},{10,11... | collective-permute-start | bytes 24584 | tf_op jit(solution)/shard_map/ppermute | solution.py:19
  32.8 3.9 %collective-permute-start.5 = (f32[2,8,128]{2,1,0:T(8,128)}, f32[2,8,128]{2,1,0:T(8,128)S(1)}, u32[]{:S(2)}, u32[]{:S(2)}) collective-permute-start(f32[2,8,128]{2,1,0:T(8,128)} %get-tuple-element.19), channel_id=1, source_target_pairs={{0,2},{1,3},{2,0},{3,1},{4,6},{5,7},{6,4},{7,5},{8,10},{9,11},{10,... | collective-permute-start | bytes 24584 | tf_op jit(solution)/shard_map/ppermute | solution.py:19
  34.3 3.3 %collective-permute-start.6 = (f32[2,8,128]{2,1,0:T(8,128)}, f32[2,8,128]{2,1,0:T(8,128)S(1)}, u32[]{:S(2)}, u32[]{:S(2)}) collective-permute-start(f32[2,8,128]{2,1,0:T(8,128)} %get-tuple-element.20), channel_id=1, source_target_pairs={{0,3},{1,2},{2,1},{3,0},{4,7},{5,6},{6,5},{7,4},{8,11},{9,10},{10,... | collective-permute-start | bytes 24584 | tf_op jit(solution)/shard_map/ppermute | solution.py:19
  34.3 3.2 %copy-start.3 = (bf16[128,1024]{1,0:T(8,128)(2,1)}, bf16[128,1024]{1,0:T(8,128)(2,1)S(1)}, u32[]{:S(2)}) copy-start(bf16[128,1024]{1,0:T(8,128)(2,1)S(1)} %collective-permute-done.7.refs_5_) | copy-start | bytes 786436
  34.4 3.2 %copy-start.4 = (bf16[128,1024]{1,0:T(8,128)(2,1)}, bf16[128,1024]{1,0:T(8,128)(2,1)S(1)}, u32[]{:S(2)}) copy-start(bf16[128,1024]{1,0:T(8,128)(2,1)S(1)} %collective-permute-done.9.refs_6_) | copy-start | bytes 786436
  34.4 3.2 %copy-start.7 = (f32[2,8,128]{2,1,0:T(8,128)}, f32[2,8,128]{2,1,0:T(8,128)S(1)}, u32[]{:S(2)}) copy-start(f32[2,8,128]{2,1,0:T(8,128)S(1)} %collective-permute-done.4.refs_1_) | copy-start | bytes 24580
  36.7 0.9 %copy-start.8 = (f32[2,8,128]{2,1,0:T(8,128)}, f32[2,8,128]{2,1,0:T(8,128)S(1)}, u32[]{:S(2)}) copy-start(f32[2,8,128]{2,1,0:T(8,128)S(1)} %collective-permute-done.5.refs_2_) | copy-start | bytes 24580
  37.6 0.6 %copy-start.9 = (f32[2,8,128]{2,1,0:T(8,128)}, f32[2,8,128]{2,1,0:T(8,128)S(1)}, u32[]{:S(2)}) copy-start(f32[2,8,128]{2,1,0:T(8,128)S(1)} %collective-permute-done.6.refs_3_) | copy-start | bytes 24580
  40.4 1.9 %collective-permute-start.10 = (f32[8,512]{1,0:T(8,128)}, f32[8,512]{1,0:T(8,128)S(1)}, u32[]{:S(2)}, u32[]{:S(2)}) collective-permute-start(f32[8,512]{1,0:T(8,128)} %shard_map.68), channel_id=1, source_target_pairs={{0,1},{1,0},{2,3},{3,2},{4,5},{5,4},{6,7},{7,6},{8,9},{9,8},{10,11... | collective-permute-start | bytes 49160 | tf_op jit(solution)/shard_map/ppermute | solution.py:19
  40.5 4.1 %collective-permute-start.11 = (f32[8,512]{1,0:T(8,128)}, f32[8,512]{1,0:T(8,128)S(1)}, u32[]{:S(2)}, u32[]{:S(2)}) collective-permute-start(f32[8,512]{1,0:T(8,128)} %shard_map.68), channel_id=1, source_target_pairs={{0,2},{1,3},{2,0},{3,1},{4,6},{5,7},{6,4},{7,5},{8,10},{9,11},{10,... | collective-permute-start | bytes 49160 | tf_op jit(solution)/shard_map/ppermute | solution.py:19
  41.2 3.5 %collective-permute-start.12 = (f32[8,512]{1,0:T(8,128)}, f32[8,512]{1,0:T(8,128)S(1)}, u32[]{:S(2)}, u32[]{:S(2)}) collective-permute-start(f32[8,512]{1,0:T(8,128)} %shard_map.68), channel_id=1, source_target_pairs={{0,3},{1,2},{2,1},{3,0},{4,7},{5,6},{6,5},{7,4},{8,11},{9,10},{10,... | collective-permute-start | bytes 49160 | tf_op jit(solution)/shard_map/ppermute | solution.py:19

commit v5 on v4

v5 whole, which is shorter than its diff:
```python
import functools

import jax
import jax.numpy as jnp
from jax import lax
from jax.experimental import pallas as pl
from jax.experimental.pallas import tpu as pltpu
from jax.sharding import PartitionSpec as P

CORES = 2
PIECE = 512
AHEAD = 4
SMALL = pltpu.CompilerParams(vmem_limit_bytes=8 << 20)
NT = (((1,), (1,)), ((), ()))
HBM = pl.BlockSpec(memory_space=pltpu.HBM)
in_hbm = functools.partial(pltpu.with_memory_space_constraint, memory_space=pltpu.HBM)
VMEM = pl.BlockSpec(memory_space=pltpu.VMEM)


def xor_permute(value, axis, size, step):
    return lax.ppermute(value, axis, [(i, i ^ step) for i in range(size)])


def cut_kernel(tests, out, sem):
    width = out.shape[1]
    start = pl.multiple_of(lax.axis_index("tensor") * width, 128)
    copy = pltpu.make_async_copy(tests.at[:, pl.ds(start, width)], out, sem)
    copy.start()
    copy.wait()


def cut_tests(tests, size):
    rows, width = tests.shape
    return pl.pallas_call(
        cut_kernel,
        out_shape=jax.ShapeDtypeStruct((rows, width // size), tests.dtype),
        in_specs=[HBM],
        out_specs=VMEM,
        scratch_shapes=[pltpu.SemaphoreType.DMA],
        compiler_params=SMALL,
    )(in_hbm(tests))


COST = 1 << 32


def project_kernel(steps, share, rows_first, after, act, og, wi, wo, lens, *refs):
    refs = refs[after:]
    outs, (buf, wibuf, wobuf, lenbuf, sem, wsem) = refs[:-6], refs[-6:]
    me = lax.axis_index("tensor")
    rank = wibuf.shape[0]
    slots = buf.shape[2]
    count = len(steps) * share
    tokens = count * slots
    small = [
        pltpu.make_async_copy(wi, wibuf, wsem.at[0]),
        pltpu.make_async_copy(wo, wobuf, wsem.at[1]),
        pltpu.make_async_copy(lens, lenbuf, wsem.at[2]),
    ]
    pieces = [(side, at) for side, ref in enumerate((act, og)) for at in range(0, ref.shape[2], PIECE)]
    copies = []
    for slot, (side, at) in enumerate(pieces):
        width = min(PIECE, (act, og)[side].shape[2] - at)
        copies.append(
            [
                pltpu.make_async_copy(
                    (act, og)[side].at[pl.ds((me ^ step) * share, share), :, pl.ds(at, width)],
                    buf.at[slot, pl.ds(i * share, share), :, pl.ds(0, width)],
                    sem.at[slot, i],
                )
                for i, step in enumerate(steps)
            ]
        )
    small[0].start()
    for slot, group in enumerate(copies):
        if slot == 1:
            small[1].start()
            small[2].start()
        if slot < AHEAD:
            for copy in group:
                copy.start()
    sums = [None, None]
    for slot, (side, at) in enumerate(pieces):
        if at == 0:
            small[side].wait()
        for copy in copies[slot]:
            copy.wait()
        if slot + AHEAD < len(pieces):
            for copy in copies[slot + AHEAD]:
                copy.start()
        weight = (wibuf, wobuf)[side][:, at : at + PIECE]
        token = buf[slot].reshape(tokens, PIECE)[:, : weight.shape[1]]
        pair = (token, weight) if rows_first else (weight, token)
        part = lax.dot_general(*pair, NT, preferred_element_type=jnp.float32)
        sums[side] = part if sums[side] is None else sums[side] + part
    if rows_first:
        sums = [one.T for one in sums]
    small[2].wait()
    col = lax.broadcasted_iota(jnp.int32, (rank, slots), 1)
    per = count // len(outs)
    for slot in range(count):
        length = lenbuf[(me ^ steps[slot // share]) * share + slot % share]
        out = outs[slot // per]
        one = sums[0][:, slot * slots : (slot + 1) * slots] * (1.0 / length.astype(jnp.float32))
        out[slot % per, :rank] = jnp.where(col < length, one, 0.0)
        out[slot % per, rank:] = sums[1][:, slot * slots : (slot + 1) * slots]


def project(act, og, wi, wo, lens, groups, share, rows_first, cost, after=()):
    steps = [step for group in groups for step in group]
    count = len(steps) * share
    slots, feat, hidden = act.shape[1], act.shape[2], og.shape[2]
    rank = wi.shape[0]
    pieces = -(-feat // PIECE) - (-hidden // PIECE)
    return pl.pallas_call(
        functools.partial(project_kernel, steps, share, rows_first, len(after)),
        out_shape=[jax.ShapeDtypeStruct((len(group) * share, 2 * rank, slots), jnp.float32) for group in groups],
        in_specs=[HBM] * 5 + [VMEM] * len(after),
        out_specs=[VMEM] * len(groups),
        scratch_shapes=[
            pltpu.VMEM((pieces, count, slots, PIECE), act.dtype),
            pltpu.VMEM((rank, feat), wi.dtype),
            pltpu.VMEM((rank, hidden), wo.dtype),
            pltpu.SMEM(lens.shape, lens.dtype),
            pltpu.SemaphoreType.DMA((pieces, len(steps))),
            pltpu.SemaphoreType.DMA((3,)),
        ],
        compiler_params=pltpu.CompilerParams(vmem_limit_bytes=32 << 20),
        cost_estimate=pl.CostEstimate(flops=cost, bytes_accessed=cost // 256, transcendentals=0),
    )(*map(in_hbm, (act, og, wi, wo, lens)), *after)


def unit_kernel(share, rank, size, *refs):
    singles, parts, outs = refs[:share], refs[share : -2 - size], refs[-2 - size : -2]
    pairs, held = refs[-2:]
    me = lax.axis_index("tensor")
    rows = rank * rank // 128
    span = rows // size
    dot = functools.partial(lax.dot_general, dimension_numbers=NT, preferred_element_type=jnp.float32)
    for k in range(share):
        full = singles[k][0]
        for part in parts:
            full = full + part[k]
        high = full.astype(jnp.bfloat16)
        low = (full - high.astype(jnp.float32)).astype(jnp.bfloat16)
        left, right = slice(None, rank), slice(rank, None)
        pairs[k] = dot(high[left], high[right]) + (dot(high[left], low[right]) + dot(low[left], high[right]))
    for k in range(share):
        even = pairs[k, pl.ds(0, rows, stride=2), :]
        odd = pairs[k, pl.ds(1, rows, stride=2), :]
        flat = jnp.concatenate([even, odd], axis=1)
        scale = jnp.sqrt(jnp.sum(flat * flat) / (rank * rank) + 1e-06)
        unit = flat / scale
        for to in range(size):
            held[to] = unit[to * span : (to + 1) * span]
        for step in range(size):
            outs[step][k] = held[me ^ step]


def units(parts, singles, share, rank, size):
    span = rank * rank // 128 // size
    return pl.pallas_call(
        functools.partial(unit_kernel, share, rank, size),
        out_shape=[jax.ShapeDtypeStruct((share, span, 128), jnp.float32)] * size,
        in_specs=[VMEM] * (share + len(parts)),
        out_specs=[VMEM] * size,
        scratch_shapes=[pltpu.VMEM((share, rank, rank), jnp.float32), pltpu.VMEM((size, span, 128), jnp.float32)],
        compiler_params=SMALL,
    )(*singles, *parts)


def score_kernel(share, size, shifts, *refs):
    unit_refs, test_refs, out, held = refs[:size], refs[size:-2], refs[-2], refs[-1]
    me, dp = lax.axis_index("tensor"), lax.axis_index("dp")
    for step in range(size):
        for k in range(share):
            held[(me ^ step) * share + k] = unit_refs[step][k]
    unit = jnp.concatenate([held[:, c, :] for c in range(held.shape[1])], axis=1).astype(jnp.bfloat16)
    tests = test_refs[0].shape[0]
    for step, test_ref in zip(shifts, test_refs):
        part = lax.dot_general(unit, test_ref[...], NT, preferred_element_type=jnp.float32)
        at = lax.rem(dp - step + len(shifts), len(shifts)) * tests
        out[:, pl.ds(pl.multiple_of(at, 128), tests)] = part


def score(unit_parts, test_parts, share):
    size, groups = len(unit_parts), len(test_parts)
    tests, width = test_parts[0].shape
    shifts = tuple(test_parts)
    return pl.pallas_call(
        functools.partial(score_kernel, share, size, shifts),
        out_shape=jax.ShapeDtypeStruct((share * size, tests * groups), jnp.float32),
        in_specs=[VMEM] * (size + groups),
        out_specs=VMEM,
        scratch_shapes=[pltpu.VMEM((share * size, width // 128, 128), jnp.float32)],
        compiler_params=SMALL,
    )(*unit_parts, *test_parts.values())


def shift(value, axis, size, step):
    return lax.ppermute(value, axis, [(i, (i + step) % size) for i in range(size)])


def shards(size, groups, activations, out_grads, proj_in, proj_out, lengths, test_grads):
    rank = proj_in.shape[1]
    share = activations.shape[0] // size
    own_tests = cut_tests(test_grads, size)
    tests = {0: own_tests, 1: shift(own_tests, "dp", groups, 1)}
    if groups == 4:
        tests[3] = shift(own_tests, "dp", groups, 3)
        tests[2] = shift(tests[1], "dp", groups, 1)
    else:
        tests.update({step: shift(own_tests, "dp", groups, step) for step in range(2, groups)})

    far = [CORES * x for x in range(1, size // CORES)]
    arrays = (activations, out_grads, proj_in.T, proj_out.T, lengths)
    far_other, far_own = project(*arrays, [[step ^ 1 for step in far], far], share, False, COST, [own_tests])
    far_sum = far_own + xor_permute(far_other, "tensor", size, 1)
    sums = [xor_permute(far_sum[i * share : (i + 1) * share], "tensor", size, step) for i, step in enumerate(far)]
    near_other, near_own = project(*arrays, [[1], [0]], share, True, COST, [far_sum])
    arrived = [xor_permute(near_other[k : k + 1], "tensor", size, 1) for k in range(share)]
    unit_outs = units([near_own] + sums, arrived, share, rank, size)
    unit_parts = [unit_outs[0]] + [xor_permute(unit_outs[step], "tensor", size, step) for step in range(1, size)]
    part = score(unit_parts, tests, share)
    parts = [part] + [xor_permute(part, "tensor", size, step) for step in range(1, size)]
    while len(parts) > 1:
        parts = [parts[i] + parts[i + 1] for i in range(0, len(parts), 2)]
    return parts[0]


def solution(mesh):
    placed = (
        P(("groups", "dp"), None, "tensor"),
        P(("groups", "dp"), None, "tensor"),
        P("tensor", None),
        P("tensor", None),
        P(("groups", "dp")),
        P(("groups", "dp"), None),
    )
    return jax.shard_map(
        functools.partial(shards, mesh.shape["tensor"], mesh.shape["dp"]),
        mesh=mesh,
        in_specs=placed,
        out_specs=P(("groups", "dp"), None),
        check_vma=False,
    )
```

time: 46.3 us -> 35.7 us (0.77)
  Pallas kernels: 20.6 us -> 14.4 us
  starting transfers between devices: 15.9 us -> 11.4 us
  waiting for transfers between devices: 6.64 us -> 8.98 us
  local copies, waits for them, and re-layouts: 1.35 us -> 0.02 us
  other arithmetic: 1.37 us -> 0.65 us
    ppermute x13 -> x10, starting transfers between devices: 15.9 us -> 6.58 us  [xor_permute(): return lax.ppermute(value, axis, [(i, i ^ step) for i in range(size)])]
    ppermute x0 -> x3, waiting for transfers between devices: none -> 5.58 us  [shift(): lax.ppermute(value, axis, [(i, (i + step) % size) for i in range(size)])]
    ppermute x0 -> x3, starting transfers between devices: none -> 4.81 us  [shift(): lax.ppermute(value, axis, [(i, (i + step) % size) for i in range(size)])]
    pallas_call x3, Pallas kernels: 16.7 us -> 12.9 us  [the longest x2 12.6 us: project(): pl.pallas_call(functools.partial(project_kernel, steps, share, rows_first...]
    ppermute x13 -> x10, waiting for transfers between devices: 6.64 us -> 3.4 us  [xor_permute(): return lax.ppermute(value, axis, [(i, i ^ step) for i in range(size)])]
    pallas_call x1, Pallas kernels: 2.28 us -> 0.51 us  [units(): pl.pallas_call(functools.partial(unit_kernel, share, rank, size), out_sha...]
    unnamed x20 -> x0, local copies, waits for them, and re-layouts: 1.33 us -> none
    add x1, other arithmetic: 1.33 us -> 0.61 us  [shards(): parts = [parts[i] + parts[i + 1] for i in range(0, len(parts), 2)]]
  transfers between devices with their start and end apart: 13 -> 13, of which waited for: 5 -> 5; matrix products, arithmetic and copies ran while one was open for 0% -> 0% of each run, Pallas kernels for 18% -> 22%
where the time goes in v5:
time: 35.7 us; the launch traced here: 35.5 us
  Pallas kernels  14.4 us (40%)
  starting transfers between devices  11.4 us (32%)
  waiting for transfers between devices  8.98 us (25%)
  other arithmetic  0.65 us (2%)
    pallas_call x2, Pallas kernels, project(): pl.pallas_call(functools.partial(project_kernel, steps, share, rows_first...  12.6 us
    ppermute x10, starting transfers between devices, xor_permute(): return lax.ppermute(value, axis, [(i, i ^ step) for i in range(size)])  6.58 us
    ppermute x3, waiting for transfers between devices, shift(): lax.ppermute(value, axis, [(i, (i + step) % size) for i in range(size)])  5.58 us
    ppermute x3, starting transfers between devices, shift(): lax.ppermute(value, axis, [(i, (i + step) % size) for i in range(size)])  4.81 us
    ppermute x10, waiting for transfers between devices, xor_permute(): return lax.ppermute(value, axis, [(i, i ^ step) for i in range(size)])  3.4 us
    pallas_call x1, Pallas kernels, cut_tests(): pl.pallas_call(cut_kernel, out_shape=jax.ShapeDtypeStruct((rows, width //...  0.96 us
  transfers between devices with their start and end apart: 13, of which 5 were waited for; matrix products, arithmetic and copies ran while one was open for 0% of the time, Pallas kernels for 22%

profile of v5, /device:TPU:0, one launch (start us, length us, event | category | flops | bytes accessed | tf_op | source)
XLA Modules:
  0.0 35.5 jit_solution(694653079691704135)
XLA Ops:
  0.0 1.0 %shard_map.64.refs_0_.refs_4_ = bf16[128,1024]{1,0:T(8,128)(2,1)S(1)} custom-call(bf16[128,4096]{1,0:T(8,128)(2,1)} %tests.1), custom_call_target="tpu_custom_call" | custom-call | tf_op jit(solution)/shard_map/pallas_call | solution.py:34
  1.0 5.3 %shard_map.65 = (f32[2,128,256]{2,1,0:T(8,128)S(1)}, f32[2,128,256]{2,1,0:T(8,128)S(1)}) custom-call(bf16[8,256,1024]{2,1,0:T(8,128)(2,1)} %act.3, bf16[8,256,3584]{2,1,0:T(8,128)(2,1)} %og.3, bf16[64,1024]{1,0:T(8,128)(2,1)} %bitcast.4, bf16[64,3584]{1,0:T(8,128)(2,1)} %bitcast.2, s32[8]{0:T(128)} %lens.3, bf16[128,1024]{1,0:T(8,128)(2,1)S(1)} %shard_map.64.refs_0_.refs_4_), custom_call_target="tpu_custom_call" | custom-call | flops 4294967296 | bytes 16777216 | tf_op jit(solution)/shard_map/pallas_call | solution.py:115
  6.3 0.5 %collective-permute-start = (f32[2,128,256]{2,1,0:T(8,128)S(1)}, f32[2,128,256]{2,1,0:T(8,128)S(1)}, u32[]{:S(2)}, u32[]{:S(2)}) collective-permute-start(f32[2,128,256]{2,1,0:T(8,128)S(1)} %get-tuple-element.14), channel_id=1, source_target_pairs={{0,1},{1,0},{2,3},{3,2},{4,5},{5,4},{6,7},{7,6},{8,9},{9,8},{10,11... | collective-permute-start | bytes 786440 | tf_op jit(solution)/shard_map/ppermute | solution.py:21
  6.8 2.6 %collective-permute-start.7 = (bf16[128,1024]{1,0:T(8,128)(2,1)S(1)}, bf16[128,1024]{1,0:T(8,128)(2,1)S(1)}, u32[]{:S(2)}, u32[]{:S(2)}) collective-permute-start(bf16[128,1024]{1,0:T(8,128)(2,1)S(1)} %shard_map.64.refs_0_.refs_4_), channel_id=1, source_target_pairs={{0,4},{4,8},{8,12},{12,0},{1,5},{5,9},{9,13},{13,1},{2,6},{6,10},{... | collective-permute-start | bytes 786440 | tf_op jit(solution)/shard_map/ppermute | solution.py:201
  9.5 2.1 %collective-permute-start.8 = (bf16[128,1024]{1,0:T(8,128)(2,1)S(1)}, bf16[128,1024]{1,0:T(8,128)(2,1)S(1)}, u32[]{:S(2)}, u32[]{:S(2)}) collective-permute-start(bf16[128,1024]{1,0:T(8,128)(2,1)S(1)} %shard_map.64.refs_0_.refs_4_), channel_id=1, source_target_pairs={{0,12},{4,0},{8,4},{12,8},{1,13},{5,1},{9,5},{13,9},{2,14},{6,2},{... | collective-permute-start | bytes 786440 | tf_op jit(solution)/shard_map/ppermute | solution.py:201
  11.6 0.0 collective-permute-done
  11.6 1.7 %collective-permute-start.3 = (f32[2,128,256]{2,1,0:T(8,128)S(1)}, f32[2,128,256]{2,1,0:T(8,128)S(1)}, u32[]{:S(2)}, u32[]{:S(2)}) collective-permute-start(f32[2,128,256]{2,1,0:T(8,128)S(1)} %add.12.refs_0_), channel_id=1, source_target_pairs={{0,2},{1,3},{2,0},{3,1},{4,6},{5,7},{6,4},{7,5},{8,10},{9,11},{10,... | collective-permute-start | bytes 786440 | tf_op jit(solution)/shard_map/ppermute | solution.py:21
  13.3 7.2 %shard_map.66 = (f32[2,128,256]{2,1,0:T(8,128)S(1)}, f32[2,128,256]{2,1,0:T(8,128)S(1)}) custom-call(bf16[8,256,1024]{2,1,0:T(8,128)(2,1)} %act.3, bf16[8,256,3584]{2,1,0:T(8,128)(2,1)} %og.3, bf16[64,1024]{1,0:T(8,128)(2,1)} %bitcast.5, bf16[64,3584]{1,0:T(8,128)(2,1)} %bitcast.3, s32[8]{0:T(128)} %lens.3, f32[2,128,256]{2,1,0:T(8,128)S(1)} %add.12.refs_0_), custom_call_target="tpu_custom_call" | custom-call | flops 4294967296 | bytes 16777216 | tf_op jit(solution)/shard_map/pallas_call | solution.py:115
  20.5 0.0 collective-permute-done.7.refs_5_
  20.6 0.1 collective-permute-start.9
  20.6 0.1 collective-permute-start.1
  20.7 0.5 %collective-permute-start.2 = (f32[1,128,256]{2,1,0:T(8,128)S(1)}, f32[1,128,256]{2,1,0:T(8,128)S(1)}, u32[]{:S(2)}, u32[]{:S(2)}) collective-permute-start(f32[1,128,256]{2,1,0:T(8,128)S(1)} %get-tuple-element.21), channel_id=1, source_target_pairs={{0,1},{1,0},{2,3},{3,2},{4,5},{5,4},{6,7},{7,6},{8,9},{9,8},{10,11... | collective-permute-start | bytes 393224 | tf_op jit(solution)/shard_map/ppermute | solution.py:21
  21.2 0.8 %collective-permute-done.1.refs_0_ = f32[1,128,256]{2,1,0:T(8,128)S(1)} collective-permute-done((f32[1,128,256]{2,1,0:T(8,128)S(1)}, f32[1,128,256]{2,1,0:T(8,128)S(1)}, u32[]{:S(2)}, u32[]{:S(2)}) %collective-permute-start.1) | collective-permute-done | bytes 131104 | tf_op jit(solution)/shard_map/ppermute | solution.py:21
  22.1 0.2 collective-permute-done.2.refs_1_
  22.2 0.0 collective-permute-done.3.refs_3_
  22.3 0.5 %shard_map.67 = (f32[2,8,128]{2,1,0:T(8,128)S(1)}, f32[2,8,128]{2,1,0:T(8,128)S(1)}, f32[2,8,128]{2,1,0:T(8,128)S(1)}, f32[2,8,128]{2,1,0:T(8,128)S(1)}) custom-call(f32[1,128,256]{2,1,0:T(8,128)S(1)} %collective-permute-done.1.refs_0_, f32[1,128,256]{2,1,0:T(8,128)S(1)} %collective-permute-done.2.refs_1_, f32[2,128,256]{2,1,0:T(8,128)S(1)} %get-tuple-element.16.refs_2_, ...), custom_call_target="tpu_custom_call" | custom-call | tf_op jit(solution)/shard_map/pallas_call | solution.py:162
  22.8 0.4 %collective-permute-start.4 = (f32[2,8,128]{2,1,0:T(8,128)S(1)}, f32[2,8,128]{2,1,0:T(8,128)S(1)}, u32[]{:S(2)}, u32[]{:S(2)}) collective-permute-start(f32[2,8,128]{2,1,0:T(8,128)S(1)} %get-tuple-element.18), channel_id=1, source_target_pairs={{0,1},{1,0},{2,3},{3,2},{4,5},{5,4},{6,7},{7,6},{8,9},{9,8},{10,11... | collective-permute-start | bytes 24584 | tf_op jit(solution)/shard_map/ppermute | solution.py:21
  23.2 0.4 %collective-permute-start.5 = (f32[2,8,128]{2,1,0:T(8,128)S(1)}, f32[2,8,128]{2,1,0:T(8,128)S(1)}, u32[]{:S(2)}, u32[]{:S(2)}) collective-permute-start(f32[2,8,128]{2,1,0:T(8,128)S(1)} %get-tuple-element.19), channel_id=1, source_target_pairs={{0,2},{1,3},{2,0},{3,1},{4,6},{5,7},{6,4},{7,5},{8,10},{9,11},{10,... | collective-permute-start | bytes 24584 | tf_op jit(solution)/shard_map/ppermute | solution.py:21
  23.6 1.1 %collective-permute-start.6 = (f32[2,8,128]{2,1,0:T(8,128)S(1)}, f32[2,8,128]{2,1,0:T(8,128)S(1)}, u32[]{:S(2)}, u32[]{:S(2)}) collective-permute-start(f32[2,8,128]{2,1,0:T(8,128)S(1)} %get-tuple-element.20), channel_id=1, source_target_pairs={{0,3},{1,2},{2,1},{3,0},{4,7},{5,6},{6,5},{7,4},{8,11},{9,10},{10,... | collective-permute-start | bytes 24584 | tf_op jit(solution)/shard_map/ppermute | solution.py:21
  24.7 0.0 collective-permute-done.8.refs_6_
  24.7 5.6 %collective-permute-done.9.refs_7_ = bf16[128,1024]{1,0:T(8,128)(2,1)S(1)} collective-permute-done((bf16[128,1024]{1,0:T(8,128)(2,1)S(1)}, bf16[128,1024]{1,0:T(8,128)(2,1)S(1)}, u32[]{:S(2)}, u32[]{:S(2)}) %collective-permute-start.9) | collective-permute-done | bytes 262176 | tf_op jit(solution)/shard_map/ppermute | solution.py:201
  30.3 0.0 collective-permute-done.4.refs_1_
  30.3 0.0 collective-permute-done.5.refs_2_
  30.3 0.0 collective-permute-done.6.refs_3_
  30.3 0.4 %shard_map.68 = f32[8,512]{1,0:T(8,128)S(1)} custom-call(f32[2,8,128]{2,1,0:T(8,128)S(1)} %get-tuple-element.17.refs_0_, f32[2,8,128]{2,1,0:T(8,128)S(1)} %collective-permute-done.4.refs_1_, f32[2,8,128]{2,1,0:T(8,128)S(1)} %collective-permute-done.5.refs_2_, f32[2,8,128]{2,1,0:T(8,128)S(1)} %collective-permute-done.6.refs_3_, ...), custom_call_target="tpu_custom_call" | custom-call | tf_op jit(solution)/shard_map/pallas_call | solution.py:190
  30.7 0.0 collective-permute-start.10
  30.7 1.1 %collective-permute-start.11 = (f32[8,512]{1,0:T(8,128)S(1)}, f32[8,512]{1,0:T(8,128)S(1)}, u32[]{:S(2)}, u32[]{:S(2)}) collective-permute-start(f32[8,512]{1,0:T(8,128)S(1)} %shard_map.68), channel_id=1, source_target_pairs={{0,2},{1,3},{2,0},{3,1},{4,6},{5,7},{6,4},{7,5},{8,10},{9,11},{10,... | collective-permute-start | bytes 49160 | tf_op jit(solution)/shard_map/ppermute | solution.py:21
  31.7 0.8 %collective-permute-start.12 = (f32[8,512]{1,0:T(8,128)S(1)}, f32[8,512]{1,0:T(8,128)S(1)}, u32[]{:S(2)}, u32[]{:S(2)}) collective-permute-start(f32[8,512]{1,0:T(8,128)S(1)} %shard_map.68), channel_id=1, source_target_pairs={{0,3},{1,2},{2,1},{3,0},{4,7},{5,6},{6,5},{7,4},{8,11},{9,10},{10,... | collective-permute-start | bytes 49160 | tf_op jit(solution)/shard_map/ppermute | solution.py:21
  32.5 0.0 collective-permute-done.10
  32.5 1.9 %collective-permute-done.11 = f32[8,512]{1,0:T(8,128)S(1)} collective-permute-done((f32[8,512]{1,0:T(8,128)S(1)}, f32[8,512]{1,0:T(8,128)S(1)}, u32[]{:S(2)}, u32[]{:S(2)}) %collective-permute-start.11) | collective-permute-done | bytes 16416 | tf_op jit(solution)/shard_map/ppermute | solution.py:21
  34.4 0.5 %collective-permute-done.12 = f32[8,512]{1,0:T(8,128)S(1)} collective-permute-done((f32[8,512]{1,0:T(8,128)S(1)}, f32[8,512]{1,0:T(8,128)S(1)}, u32[]{:S(2)}, u32[]{:S(2)}) %collective-permute-start.12) | collective-permute-done | bytes 16416 | tf_op jit(solution)/shard_map/ppermute | solution.py:21
  34.9 0.6 %add_add_fusion = f32[8,512]{1,0:T(8,128)} fusion(f32[8,512]{1,0:T(8,128)S(1)} %collective-permute-done.11, f32[8,512]{1,0:T(8,128)S(1)} %collective-permute-done.12, f32[8,512]{1,0:T(8,128)S(1)} %shard_map.68, f32[8,512]{1,0:T(8,128)S(1)} %collective-permute-done.10), kind=kLoop, calls=%fused_computation | loop fusion | flops 12288 | bytes 81920 | tf_op jit(solution)/shard_map/add | solution.py:227
  (2 shorter events, 0.1 us)
Async XLA Ops:
  6.3 5.3 %collective-permute-start = (f32[2,128,256]{2,1,0:T(8,128)S(1)}, f32[2,128,256]{2,1,0:T(8,128)S(1)}, u32[]{:S(2)}, u32[]{:S(2)}) collective-permute-start(f32[2,128,256]{2,1,0:T(8,128)S(1)} %get-tuple-element.14), channel_id=1, source_target_pairs={{0,1},{1,0},{2,3},{3,2},{4,5},{5,4},{6,7},{7,6},{8,9},{9,8},{10,11... | collective-permute-start | bytes 786440 | tf_op jit(solution)/shard_map/ppermute | solution.py:21
  6.8 13.7 %collective-permute-start.7 = (bf16[128,1024]{1,0:T(8,128)(2,1)S(1)}, bf16[128,1024]{1,0:T(8,128)(2,1)S(1)}, u32[]{:S(2)}, u32[]{:S(2)}) collective-permute-start(bf16[128,1024]{1,0:T(8,128)(2,1)S(1)} %shard_map.64.refs_0_.refs_4_), channel_id=1, source_target_pairs={{0,4},{4,8},{8,12},{12,0},{1,5},{5,9},{9,13},{13,1},{2,6},{6,10},{... | collective-permute-start | bytes 786440 | tf_op jit(solution)/shard_map/ppermute | solution.py:201
  9.5 15.2 %collective-permute-start.8 = (bf16[128,1024]{1,0:T(8,128)(2,1)S(1)}, bf16[128,1024]{1,0:T(8,128)(2,1)S(1)}, u32[]{:S(2)}, u32[]{:S(2)}) collective-permute-start(bf16[128,1024]{1,0:T(8,128)(2,1)S(1)} %shard_map.64.refs_0_.refs_4_), channel_id=1, source_target_pairs={{0,12},{4,0},{8,4},{12,8},{1,13},{5,1},{9,5},{13,9},{2,14},{6,2},{... | collective-permute-start | bytes 786440 | tf_op jit(solution)/shard_map/ppermute | solution.py:201
  11.6 10.6 %collective-permute-start.3 = (f32[2,128,256]{2,1,0:T(8,128)S(1)}, f32[2,128,256]{2,1,0:T(8,128)S(1)}, u32[]{:S(2)}, u32[]{:S(2)}) collective-permute-start(f32[2,128,256]{2,1,0:T(8,128)S(1)} %add.12.refs_0_), channel_id=1, source_target_pairs={{0,2},{1,3},{2,0},{3,1},{4,6},{5,7},{6,4},{7,5},{8,10},{9,11},{10,... | collective-permute-start | bytes 786440 | tf_op jit(solution)/shard_map/ppermute | solution.py:21
  20.6 9.7 %collective-permute-start.9 = (bf16[128,1024]{1,0:T(8,128)(2,1)S(1)}, bf16[128,1024]{1,0:T(8,128)(2,1)S(1)}, u32[]{:S(2)}, u32[]{:S(2)}) collective-permute-start(bf16[128,1024]{1,0:T(8,128)(2,1)S(1)} %collective-permute-done.7.refs_5_), channel_id=1, source_target_pairs={{0,4},{4,8},{8,12},{12,0},{1,5},{5,9},{9,13},{13,1},{2,6},{6,10},{... | collective-permute-start | bytes 786440 | tf_op jit(solution)/shard_map/ppermute | solution.py:201
  20.6 1.4 %collective-permute-start.1 = (f32[1,128,256]{2,1,0:T(8,128)S(1)}, f32[1,128,256]{2,1,0:T(8,128)S(1)}, u32[]{:S(2)}, u32[]{:S(2)}) collective-permute-start(f32[1,128,256]{2,1,0:T(8,128)S(1)} %get-tuple-element.22), channel_id=1, source_target_pairs={{0,1},{1,0},{2,3},{3,2},{4,5},{5,4},{6,7},{7,6},{8,9},{9,8},{10,11... | collective-permute-start | bytes 393224 | tf_op jit(solution)/shard_map/ppermute | solution.py:21
  20.7 1.5 %collective-permute-start.2 = (f32[1,128,256]{2,1,0:T(8,128)S(1)}, f32[1,128,256]{2,1,0:T(8,128)S(1)}, u32[]{:S(2)}, u32[]{:S(2)}) collective-permute-start(f32[1,128,256]{2,1,0:T(8,128)S(1)} %get-tuple-element.21), channel_id=1, source_target_pairs={{0,1},{1,0},{2,3},{3,2},{4,5},{5,4},{6,7},{7,6},{8,9},{9,8},{10,11... | collective-permute-start | bytes 393224 | tf_op jit(solution)/shard_map/ppermute | solution.py:21
  22.8 7.5 %collective-permute-start.4 = (f32[2,8,128]{2,1,0:T(8,128)S(1)}, f32[2,8,128]{2,1,0:T(8,128)S(1)}, u32[]{:S(2)}, u32[]{:S(2)}) collective-permute-start(f32[2,8,128]{2,1,0:T(8,128)S(1)} %get-tuple-element.18), channel_id=1, source_target_pairs={{0,1},{1,0},{2,3},{3,2},{4,5},{5,4},{6,7},{7,6},{8,9},{9,8},{10,11... | collective-permute-start | bytes 24584 | tf_op jit(solution)/shard_map/ppermute | solution.py:21
  23.2 7.1 %collective-permute-start.5 = (f32[2,8,128]{2,1,0:T(8,128)S(1)}, f32[2,8,128]{2,1,0:T(8,128)S(1)}, u32[]{:S(2)}, u32[]{:S(2)}) collective-permute-start(f32[2,8,128]{2,1,0:T(8,128)S(1)} %get-tuple-element.19), channel_id=1, source_target_pairs={{0,2},{1,3},{2,0},{3,1},{4,6},{5,7},{6,4},{7,5},{8,10},{9,11},{10,... | collective-permute-start | bytes 24584 | tf_op jit(solution)/shard_map/ppermute | solution.py:21
  23.6 6.7 %collective-permute-start.6 = (f32[2,8,128]{2,1,0:T(8,128)S(1)}, f32[2,8,128]{2,1,0:T(8,128)S(1)}, u32[]{:S(2)}, u32[]{:S(2)}) collective-permute-start(f32[2,8,128]{2,1,0:T(8,128)S(1)} %get-tuple-element.20), channel_id=1, source_target_pairs={{0,3},{1,2},{2,1},{3,0},{4,7},{5,6},{6,5},{7,4},{8,11},{9,10},{10,... | collective-permute-start | bytes 24584 | tf_op jit(solution)/shard_map/ppermute | solution.py:21
  30.7 1.9 %collective-permute-start.10 = (f32[8,512]{1,0:T(8,128)S(1)}, f32[8,512]{1,0:T(8,128)S(1)}, u32[]{:S(2)}, u32[]{:S(2)}) collective-permute-start(f32[8,512]{1,0:T(8,128)S(1)} %shard_map.68), channel_id=1, source_target_pairs={{0,1},{1,0},{2,3},{3,2},{4,5},{5,4},{6,7},{7,6},{8,9},{9,8},{10,11... | collective-permute-start | bytes 49160 | tf_op jit(solution)/shard_map/ppermute | solution.py:21
  30.7 3.8 %collective-permute-start.11 = (f32[8,512]{1,0:T(8,128)S(1)}, f32[8,512]{1,0:T(8,128)S(1)}, u32[]{:S(2)}, u32[]{:S(2)}) collective-permute-start(f32[8,512]{1,0:T(8,128)S(1)} %shard_map.68), channel_id=1, source_target_pairs={{0,2},{1,3},{2,0},{3,1},{4,6},{5,7},{6,4},{7,5},{8,10},{9,11},{10,... | collective-permute-start | bytes 49160 | tf_op jit(solution)/shard_map/ppermute | solution.py:21
  31.7 3.2 %collective-permute-start.12 = (f32[8,512]{1,0:T(8,128)S(1)}, f32[8,512]{1,0:T(8,128)S(1)}, u32[]{:S(2)}, u32[]{:S(2)}) collective-permute-start(f32[8,512]{1,0:T(8,128)S(1)} %shard_map.68), channel_id=1, source_target_pairs={{0,3},{1,2},{2,1},{3,0},{4,7},{5,6},{6,5},{7,4},{8,11},{9,10},{10,... | collective-permute-start | bytes 49160 | tf_op jit(solution)/shard_map/ppermute | solution.py:21

commit v6 on v5

--- a/solution.py
+++ b/solution.py
@@ -12,6 +12,7 @@
 AHEAD = 4
 SMALL = pltpu.CompilerParams(vmem_limit_bytes=8 << 20)
 NT = (((1,), (1,)), ((), ()))
+NN = (((1,), (0,)), ((), ()))
 HBM = pl.BlockSpec(memory_space=pltpu.HBM)
 in_hbm = functools.partial(pltpu.with_memory_space_constraint, memory_space=pltpu.HBM)
 VMEM = pl.BlockSpec(memory_space=pltpu.VMEM)
@@ -44,7 +45,7 @@
 COST = 1 << 32
 
 
-def project_kernel(steps, share, rows_first, after, act, og, wi, wo, lens, *refs):
+def project_kernel(steps, share, rows_first, ahead, after, act, og, wi, wo, lens, *refs):
     refs = refs[after:]
     outs, (buf, wibuf, wobuf, lenbuf, sem, wsem) = refs[:-6], refs[-6:]
     me = lax.axis_index("tensor")
@@ -76,7 +77,7 @@
         if slot == 1:
             small[1].start()
             small[2].start()
-        if slot < AHEAD:
+        if slot < ahead:
             for copy in group:
                 copy.start()
     sums = [None, None]
@@ -85,16 +86,26 @@
             small[side].wait()
         for copy in copies[slot]:
             copy.wait()
-        if slot + AHEAD < len(pieces):
-            for copy in copies[slot + AHEAD]:
+        if slot + ahead < len(pieces):
+            for copy in copies[slot + ahead]:
                 copy.start()
         weight = (wibuf, wobuf)[side][:, at : at + PIECE]
         token = buf[slot].reshape(tokens, PIECE)[:, : weight.shape[1]]
-        pair = (token, weight) if rows_first else (weight, token)
-        part = lax.dot_general(*pair, NT, preferred_element_type=jnp.float32)
-        sums[side] = part if sums[side] is None else sums[side] + part
+        if rows_first:
+            none = jnp.zeros_like(weight)
+            wide = jnp.concatenate([none, weight] if side else [weight, none], axis=0).T
+            half = tokens // 2
+            part = [
+                lax.dot_general(token[i * half : (i + 1) * half], wide, NN, preferred_element_type=jnp.float32)
+                for i in range(2)
+            ]
+            sums = part if slot == 0 else [sums[0] + part[0], sums[1] + part[1]]
+        else:
+            part = lax.dot_general(weight, token, NT, preferred_element_type=jnp.float32)
+            sums[side] = part if sums[side] is None else sums[side] + part
     if rows_first:
-        sums = [one.T for one in sums]
+        whole = jnp.concatenate([one.T for one in sums], axis=1)
+        sums = [whole[:rank], whole[rank:]]
     small[2].wait()
     col = lax.broadcasted_iota(jnp.int32, (rank, slots), 1)
     per = count // len(outs)
@@ -106,14 +117,14 @@
         out[slot % per, rank:] = sums[1][:, slot * slots : (slot + 1) * slots]
 
 
-def project(act, og, wi, wo, lens, groups, share, rows_first, cost, after=()):
+def project(act, og, wi, wo, lens, groups, share, rows_first, ahead, after=()):
     steps = [step for group in groups for step in group]
     count = len(steps) * share
     slots, feat, hidden = act.shape[1], act.shape[2], og.shape[2]
     rank = wi.shape[0]
     pieces = -(-feat // PIECE) - (-hidden // PIECE)
     return pl.pallas_call(
-        functools.partial(project_kernel, steps, share, rows_first, len(after)),
+        functools.partial(project_kernel, steps, share, rows_first, ahead, len(after)),
         out_shape=[jax.ShapeDtypeStruct((len(group) * share, 2 * rank, slots), jnp.float32) for group in groups],
         in_specs=[HBM] * 5 + [VMEM] * len(after),
         out_specs=[VMEM] * len(groups),
@@ -126,7 +137,7 @@
             pltpu.SemaphoreType.DMA((3,)),
         ],
         compiler_params=pltpu.CompilerParams(vmem_limit_bytes=32 << 20),
-        cost_estimate=pl.CostEstimate(flops=cost, bytes_accessed=cost // 256, transcendentals=0),
+        cost_estimate=pl.CostEstimate(flops=COST, bytes_accessed=COST // 256, transcendentals=0),
     )(*map(in_hbm, (act, og, wi, wo, lens)), *after)
 
 
@@ -214,10 +225,11 @@
 
     far = [CORES * x for x in range(1, size // CORES)]
     arrays = (activations, out_grads, proj_in.T, proj_out.T, lengths)
-    far_other, far_own = project(*arrays, [[step ^ 1 for step in far], far], share, False, COST, [own_tests])
+    far_other, far_own = project(*arrays, [[step ^ 1 for step in far], far], share, False, 9, [own_tests])
+    far_other = far_other + 0.0 * tests[1][0, 0].astype(jnp.float32)
     far_sum = far_own + xor_permute(far_other, "tensor", size, 1)
     sums = [xor_permute(far_sum[i * share : (i + 1) * share], "tensor", size, step) for i, step in enumerate(far)]
-    near_other, near_own = project(*arrays, [[1], [0]], share, True, COST, [far_sum])
+    near_other, near_own = project(*arrays, [[1], [0]], share, True, 4, [far_sum, tests[1]])
     arrived = [xor_permute(near_other[k : k + 1], "tensor", size, 1) for k in range(share)]
     unit_outs = units([near_own] + sums, arrived, share, rank, size)
     unit_parts = [unit_outs[0]] + [xor_permute(unit_outs[step], "tensor", size, step) for step in range(1, size)]

time: 35.7 us -> 34.7 us (0.972)
  waiting for transfers between devices: 8.98 us -> 7.53 us
  between operations: 0.08 us -> 0.73 us
  local copies, waits for them, and re-layouts: 0.02 us -> 0.53 us
  Pallas kernels: 14.4 us -> 13.9 us
    ppermute x3, waiting for transfers between devices: 5.58 us -> 3.35 us  [shift(): lax.ppermute(value, axis, [(i, (i + step) % size) for i in range(size)])]
    ppermute x10, waiting for transfers between devices: 3.4 us -> 4.18 us  [xor_permute(): return lax.ppermute(value, axis, [(i, i ^ step) for i in range(size)])]
    ppermute x10, starting transfers between devices: 6.58 us -> 6 us  [xor_permute(): return lax.ppermute(value, axis, [(i, i ^ step) for i in range(size)])]
    slice x0 -> x1, local copies, waits for them, and re-layouts: none -> 0.51 us  [shards(): far_other = far_other + 0.0 * tests[1][0, 0].astype(jnp.float32)]
    pallas_call x2, Pallas kernels: 12.6 us -> 12.1 us  [project(): pl.pallas_call(functools.partial(project_kernel, steps, share, rows_first...]
  transfers between devices with their start and end apart: 13 -> 13, of which waited for: 5 -> 8; matrix products, arithmetic and copies ran while one was open for 0% -> 0% of each run, Pallas kernels for 22% -> 37%
where the time goes in v6:
time: 34.7 us; the launch traced here: 34.5 us
  Pallas kernels  13.9 us (40%)
  starting transfers between devices  11.2 us (32%)
  waiting for transfers between devices  7.53 us (22%)
  between operations  0.73 us (2%)
  other arithmetic  0.67 us (2%)
  local copies, waits for them, and re-layouts  0.53 us (2%)
    pallas_call x2, Pallas kernels, project(): pl.pallas_call(functools.partial(project_kernel, steps, share, rows_first...  12.1 us
    ppermute x10, starting transfers between devices, xor_permute(): return lax.ppermute(value, axis, [(i, i ^ step) for i in range(size)])  6 us
    ppermute x3, starting transfers between devices, shift(): lax.ppermute(value, axis, [(i, (i + step) % size) for i in range(size)])  5.15 us
    ppermute x10, waiting for transfers between devices, xor_permute(): return lax.ppermute(value, axis, [(i, i ^ step) for i in range(size)])  4.18 us
    ppermute x3, waiting for transfers between devices, shift(): lax.ppermute(value, axis, [(i, (i + step) % size) for i in range(size)])  3.35 us
    pallas_call x1, Pallas kernels, cut_tests(): pl.pallas_call(cut_kernel, out_shape=jax.ShapeDtypeStruct((rows, width //...  0.96 us
  transfers between devices with their start and end apart: 13, of which 8 were waited for; matrix products, arithmetic and copies ran while one was open for 0% of the time, Pallas kernels for 37%

profile of v6, /device:TPU:0, one launch (start us, length us, event | category | flops | bytes accessed | tf_op | source)
XLA Modules:
  0.0 34.5 jit_solution(7017984013778997799)
XLA Ops:
  0.0 1.0 %shard_map.64.refs_0_.refs_4_ = bf16[128,1024]{1,0:T(8,128)(2,1)S(1)} custom-call(bf16[128,4096]{1,0:T(8,128)(2,1)} %tests.1), custom_call_target="tpu_custom_call" | custom-call | tf_op jit(solution)/shard_map/pallas_call | solution.py:35
  1.0 3.1 %collective-permute-start = (bf16[128,1024]{1,0:T(8,128)(2,1)S(1)}, bf16[128,1024]{1,0:T(8,128)(2,1)S(1)}, u32[]{:S(2)}, u32[]{:S(2)}) collective-permute-start(bf16[128,1024]{1,0:T(8,128)(2,1)S(1)} %shard_map.64.refs_0_.refs_4_), channel_id=1, source_target_pairs={{0,4},{4,8},{8,12},{12,0},{1,5},{5,9},{9,13},{13,1},{2,6},{6,10},{... | collective-permute-start | bytes 786440 | tf_op jit(solution)/shard_map/ppermute | solution.py:212
  4.0 6.8 %shard_map.65 = (f32[2,128,256]{2,1,0:T(8,128)S(1)}, f32[2,128,256]{2,1,0:T(8,128)S(1)}) custom-call(bf16[8,256,1024]{2,1,0:T(8,128)(2,1)} %act.3, bf16[8,256,3584]{2,1,0:T(8,128)(2,1)} %og.3, bf16[64,1024]{1,0:T(8,128)(2,1)} %bitcast.5, bf16[64,3584]{1,0:T(8,128)(2,1)} %bitcast.3, s32[8]{0:T(128)} %lens.3, bf16[128,1024]{1,0:T(8,128)(2,1)S(1)} %shard_map.64.refs_0_.refs_4_), custom_call_target="tpu_custom_call" | custom-call | flops 4294967296 | bytes 16777216 | tf_op jit(solution)/shard_map/pallas_call | solution.py:126
  10.9 1.5 %collective-permute-done.refs_1_.refs_5_ = bf16[128,1024]{1,0:T(8,128)(2,1)S(1)} collective-permute-done((bf16[128,1024]{1,0:T(8,128)(2,1)S(1)}, bf16[128,1024]{1,0:T(8,128)(2,1)S(1)}, u32[]{:S(2)}, u32[]{:S(2)}) %collective-permute-start) | collective-permute-done | bytes 262176 | tf_op jit(solution)/shard_map/ppermute | solution.py:212
  12.4 0.5 %slice.12 = bf16[1,1]{1,0:T(2,128)(2,1)} slice(bf16[128,1024]{1,0:T(8,128)(2,1)S(1)} %collective-permute-done.refs_1_.refs_5_), slice={[0:1], [0:1]} | slice | bytes 4 | tf_op jit(solution)/shard_map/slice | solution.py:229
  13.6 0.1 collective-permute-start.1
  13.6 1.8 %collective-permute-start.8 = (bf16[128,1024]{1,0:T(8,128)(2,1)S(1)}, bf16[128,1024]{1,0:T(8,128)(2,1)S(1)}, u32[]{:S(2)}, u32[]{:S(2)}) collective-permute-start(bf16[128,1024]{1,0:T(8,128)(2,1)S(1)} %shard_map.64.refs_0_.refs_4_), channel_id=1, source_target_pairs={{0,12},{4,0},{8,4},{12,8},{1,13},{5,1},{9,5},{13,9},{2,14},{6,2},{... | collective-permute-start | bytes 786440 | tf_op jit(solution)/shard_map/ppermute | solution.py:212
  15.4 0.3 collective-permute-start.9
  15.7 0.0 collective-permute-done.1
  15.8 1.6 %collective-permute-start.4 = (f32[2,128,256]{2,1,0:T(8,128)S(1)}, f32[2,128,256]{2,1,0:T(8,128)S(1)}, u32[]{:S(2)}, u32[]{:S(2)}) collective-permute-start(f32[2,128,256]{2,1,0:T(8,128)S(1)} %add.20.refs_0_), channel_id=1, source_target_pairs={{0,2},{1,3},{2,0},{3,1},{4,6},{5,7},{6,4},{7,5},{8,10},{9,11},{10,... | collective-permute-start | bytes 786440 | tf_op jit(solution)/shard_map/ppermute | solution.py:22
  17.3 5.3 %shard_map.66 = (f32[2,128,256]{2,1,0:T(8,128)S(1)}, f32[2,128,256]{2,1,0:T(8,128)S(1)}) custom-call(bf16[8,256,1024]{2,1,0:T(8,128)(2,1)} %act.3, bf16[8,256,3584]{2,1,0:T(8,128)(2,1)} %og.3, bf16[64,1024]{1,0:T(8,128)(2,1)} %bitcast.6, bf16[64,3584]{1,0:T(8,128)(2,1)} %bitcast.4, s32[8]{0:T(128)} %lens.3, f32[2,128,256]{2,1,0:T(8,128)S(1)} %add.20.refs_0_, ...), custom_call_target="tpu_custom_call" | custom-call | flops 4294967296 | bytes 16777216 | tf_op jit(solution)/shard_map/pallas_call | solution.py:126
  22.6 0.1 collective-permute-start.2
  22.7 0.5 %collective-permute-start.3 = (f32[1,128,256]{2,1,0:T(8,128)S(1)}, f32[1,128,256]{2,1,0:T(8,128)S(1)}, u32[]{:S(2)}, u32[]{:S(2)}) collective-permute-start(f32[1,128,256]{2,1,0:T(8,128)S(1)} %get-tuple-element.21), channel_id=1, source_target_pairs={{0,1},{1,0},{2,3},{3,2},{4,5},{5,4},{6,7},{7,6},{8,9},{9,8},{10,11... | collective-permute-start | bytes 393224 | tf_op jit(solution)/shard_map/ppermute | solution.py:22
  23.2 0.8 %collective-permute-done.2.refs_0_ = f32[1,128,256]{2,1,0:T(8,128)S(1)} collective-permute-done((f32[1,128,256]{2,1,0:T(8,128)S(1)}, f32[1,128,256]{2,1,0:T(8,128)S(1)}, u32[]{:S(2)}, u32[]{:S(2)}) %collective-permute-start.2) | collective-permute-done | bytes 131104 | tf_op jit(solution)/shard_map/ppermute | solution.py:22
  24.0 0.2 collective-permute-done.3.refs_1_
  24.2 0.5 %shard_map.67 = (f32[2,8,128]{2,1,0:T(8,128)S(1)}, f32[2,8,128]{2,1,0:T(8,128)S(1)}, f32[2,8,128]{2,1,0:T(8,128)S(1)}, f32[2,8,128]{2,1,0:T(8,128)S(1)}) custom-call(f32[1,128,256]{2,1,0:T(8,128)S(1)} %collective-permute-done.2.refs_0_, f32[1,128,256]{2,1,0:T(8,128)S(1)} %collective-permute-done.3.refs_1_, f32[2,128,256]{2,1,0:T(8,128)S(1)} %get-tuple-element.16.refs_2_, ...), custom_call_target="tpu_custom_call" | custom-call | tf_op jit(solution)/shard_map/pallas_call | solution.py:173
  24.7 0.4 %collective-permute-start.5 = (f32[2,8,128]{2,1,0:T(8,128)S(1)}, f32[2,8,128]{2,1,0:T(8,128)S(1)}, u32[]{:S(2)}, u32[]{:S(2)}) collective-permute-start(f32[2,8,128]{2,1,0:T(8,128)S(1)} %get-tuple-element.18), channel_id=1, source_target_pairs={{0,1},{1,0},{2,3},{3,2},{4,5},{5,4},{6,7},{7,6},{8,9},{9,8},{10,11... | collective-permute-start | bytes 24584 | tf_op jit(solution)/shard_map/ppermute | solution.py:22
  25.1 1.0 %collective-permute-start.6 = (f32[2,8,128]{2,1,0:T(8,128)S(1)}, f32[2,8,128]{2,1,0:T(8,128)S(1)}, u32[]{:S(2)}, u32[]{:S(2)}) collective-permute-start(f32[2,8,128]{2,1,0:T(8,128)S(1)} %get-tuple-element.19), channel_id=1, source_target_pairs={{0,2},{1,3},{2,0},{3,1},{4,6},{5,7},{6,4},{7,5},{8,10},{9,11},{10,... | collective-permute-start | bytes 24584 | tf_op jit(solution)/shard_map/ppermute | solution.py:22
  26.1 0.6 %collective-permute-start.7 = (f32[2,8,128]{2,1,0:T(8,128)S(1)}, f32[2,8,128]{2,1,0:T(8,128)S(1)}, u32[]{:S(2)}, u32[]{:S(2)}) collective-permute-start(f32[2,8,128]{2,1,0:T(8,128)S(1)} %get-tuple-element.20), channel_id=1, source_target_pairs={{0,3},{1,2},{2,1},{3,0},{4,7},{5,6},{6,5},{7,4},{8,11},{9,10},{10,... | collective-permute-start | bytes 24584 | tf_op jit(solution)/shard_map/ppermute | solution.py:22
  26.7 0.0 collective-permute-done.8.refs_6_
  26.7 1.9 %collective-permute-done.9.refs_7_ = bf16[128,1024]{1,0:T(8,128)(2,1)S(1)} collective-permute-done((bf16[128,1024]{1,0:T(8,128)(2,1)S(1)}, bf16[128,1024]{1,0:T(8,128)(2,1)S(1)}, u32[]{:S(2)}, u32[]{:S(2)}) %collective-permute-start.9) | collective-permute-done | bytes 262176 | tf_op jit(solution)/shard_map/ppermute | solution.py:212
  28.5 0.0 collective-permute-done.5.refs_1_
  28.5 0.2 collective-permute-done.6.refs_2_
  28.8 0.4 %collective-permute-done.7.refs_3_ = f32[2,8,128]{2,1,0:T(8,128)S(1)} collective-permute-done((f32[2,8,128]{2,1,0:T(8,128)S(1)}, f32[2,8,128]{2,1,0:T(8,128)S(1)}, u32[]{:S(2)}, u32[]{:S(2)}) %collective-permute-start.7) | collective-permute-done | bytes 8224 | tf_op jit(solution)/shard_map/ppermute | solution.py:22
  29.2 0.4 %shard_map.68 = f32[8,512]{1,0:T(8,128)S(1)} custom-call(f32[2,8,128]{2,1,0:T(8,128)S(1)} %get-tuple-element.17.refs_0_, f32[2,8,128]{2,1,0:T(8,128)S(1)} %collective-permute-done.5.refs_1_, f32[2,8,128]{2,1,0:T(8,128)S(1)} %collective-permute-done.6.refs_2_, f32[2,8,128]{2,1,0:T(8,128)S(1)} %collective-permute-done.7.refs_3_, ...), custom_call_target="tpu_custom_call" | custom-call | tf_op jit(solution)/shard_map/pallas_call | solution.py:201
  29.5 0.2 collective-permute-start.10
  29.7 1.1 %collective-permute-start.11 = (f32[8,512]{1,0:T(8,128)S(1)}, f32[8,512]{1,0:T(8,128)S(1)}, u32[]{:S(2)}, u32[]{:S(2)}) collective-permute-start(f32[8,512]{1,0:T(8,128)S(1)} %shard_map.68), channel_id=1, source_target_pairs={{0,2},{1,3},{2,0},{3,1},{4,6},{5,7},{6,4},{7,5},{8,10},{9,11},{10,... | collective-permute-start | bytes 49160 | tf_op jit(solution)/shard_map/ppermute | solution.py:22
  30.8 0.6 %collective-permute-start.12 = (f32[8,512]{1,0:T(8,128)S(1)}, f32[8,512]{1,0:T(8,128)S(1)}, u32[]{:S(2)}, u32[]{:S(2)}) collective-permute-start(f32[8,512]{1,0:T(8,128)S(1)} %shard_map.68), channel_id=1, source_target_pairs={{0,3},{1,2},{2,1},{3,0},{4,7},{5,6},{6,5},{7,4},{8,11},{9,10},{10,... | collective-permute-start | bytes 49160 | tf_op jit(solution)/shard_map/ppermute | solution.py:22
  31.4 0.0 collective-permute-done.10
  31.4 2.0 %collective-permute-done.11 = f32[8,512]{1,0:T(8,128)S(1)} collective-permute-done((f32[8,512]{1,0:T(8,128)S(1)}, f32[8,512]{1,0:T(8,128)S(1)}, u32[]{:S(2)}, u32[]{:S(2)}) %collective-permute-start.11) | collective-permute-done | bytes 16416 | tf_op jit(solution)/shard_map/ppermute | solution.py:22
  33.5 0.5 %collective-permute-done.12 = f32[8,512]{1,0:T(8,128)S(1)} collective-permute-done((f32[8,512]{1,0:T(8,128)S(1)}, f32[8,512]{1,0:T(8,128)S(1)}, u32[]{:S(2)}, u32[]{:S(2)}) %collective-permute-start.12) | collective-permute-done | bytes 16416 | tf_op jit(solution)/shard_map/ppermute | solution.py:22
  33.9 0.6 %add_add_fusion = f32[8,512]{1,0:T(8,128)} fusion(f32[8,512]{1,0:T(8,128)S(1)} %collective-permute-done.11, f32[8,512]{1,0:T(8,128)S(1)} %collective-permute-done.12, f32[8,512]{1,0:T(8,128)S(1)} %shard_map.68, f32[8,512]{1,0:T(8,128)S(1)} %collective-permute-done.10), kind=kLoop, calls=%fused_computation.1 | loop fusion | flops 12288 | bytes 81920 | tf_op jit(solution)/shard_map/add | solution.py:239
  (4 shorter events, 0.1 us)
Async XLA Ops:
  1.0 11.4 %collective-permute-start = (bf16[128,1024]{1,0:T(8,128)(2,1)S(1)}, bf16[128,1024]{1,0:T(8,128)(2,1)S(1)}, u32[]{:S(2)}, u32[]{:S(2)}) collective-permute-start(bf16[128,1024]{1,0:T(8,128)(2,1)S(1)} %shard_map.64.refs_0_.refs_4_), channel_id=1, source_target_pairs={{0,4},{4,8},{8,12},{12,0},{1,5},{5,9},{9,13},{13,1},{2,6},{6,10},{... | collective-permute-start | bytes 786440 | tf_op jit(solution)/shard_map/ppermute | solution.py:212
  13.6 2.2 %collective-permute-start.1 = (f32[2,128,256]{2,1,0:T(8,128)S(1)}, f32[2,128,256]{2,1,0:T(8,128)S(1)}, u32[]{:S(2)}, u32[]{:S(2)}) collective-permute-start(f32[2,128,256]{2,1,0:T(8,128)S(1)} %broadcast_add_fusion), channel_id=1, source_target_pairs={{0,1},{1,0},{2,3},{3,2},{4,5},{5,4},{6,7},{7,6},{8,9},{9,8},{10,11... | collective-permute-start | bytes 786440 | tf_op jit(solution)/shard_map/ppermute | solution.py:22
  13.6 13.0 %collective-permute-start.8 = (bf16[128,1024]{1,0:T(8,128)(2,1)S(1)}, bf16[128,1024]{1,0:T(8,128)(2,1)S(1)}, u32[]{:S(2)}, u32[]{:S(2)}) collective-permute-start(bf16[128,1024]{1,0:T(8,128)(2,1)S(1)} %shard_map.64.refs_0_.refs_4_), channel_id=1, source_target_pairs={{0,12},{4,0},{8,4},{12,8},{1,13},{5,1},{9,5},{13,9},{2,14},{6,2},{... | collective-permute-start | bytes 786440 | tf_op jit(solution)/shard_map/ppermute | solution.py:212
  15.4 13.1 %collective-permute-start.9 = (bf16[128,1024]{1,0:T(8,128)(2,1)S(1)}, bf16[128,1024]{1,0:T(8,128)(2,1)S(1)}, u32[]{:S(2)}, u32[]{:S(2)}) collective-permute-start(bf16[128,1024]{1,0:T(8,128)(2,1)S(1)} %collective-permute-done.refs_1_.refs_5_), channel_id=1, source_target_pairs={{0,4},{4,8},{8,12},{12,0},{1,5},{5,9},{9,13},{13,1},{2,6},{6,10},{... | collective-permute-start | bytes 786440 | tf_op jit(solution)/shard_map/ppermute | solution.py:212
  15.8 8.4 %collective-permute-start.4 = (f32[2,128,256]{2,1,0:T(8,128)S(1)}, f32[2,128,256]{2,1,0:T(8,128)S(1)}, u32[]{:S(2)}, u32[]{:S(2)}) collective-permute-start(f32[2,128,256]{2,1,0:T(8,128)S(1)} %add.20.refs_0_), channel_id=1, source_target_pairs={{0,2},{1,3},{2,0},{3,1},{4,6},{5,7},{6,4},{7,5},{8,10},{9,11},{10,... | collective-permute-start | bytes 786440 | tf_op jit(solution)/shard_map/ppermute | solution.py:22
  22.6 1.4 %collective-permute-start.2 = (f32[1,128,256]{2,1,0:T(8,128)S(1)}, f32[1,128,256]{2,1,0:T(8,128)S(1)}, u32[]{:S(2)}, u32[]{:S(2)}) collective-permute-start(f32[1,128,256]{2,1,0:T(8,128)S(1)} %get-tuple-element.22), channel_id=1, source_target_pairs={{0,1},{1,0},{2,3},{3,2},{4,5},{5,4},{6,7},{7,6},{8,9},{9,8},{10,11... | collective-permute-start | bytes 393224 | tf_op jit(solution)/shard_map/ppermute | solution.py:22
  22.7 1.5 %collective-permute-start.3 = (f32[1,128,256]{2,1,0:T(8,128)S(1)}, f32[1,128,256]{2,1,0:T(8,128)S(1)}, u32[]{:S(2)}, u32[]{:S(2)}) collective-permute-start(f32[1,128,256]{2,1,0:T(8,128)S(1)} %get-tuple-element.21), channel_id=1, source_target_pairs={{0,1},{1,0},{2,3},{3,2},{4,5},{5,4},{6,7},{7,6},{8,9},{9,8},{10,11... | collective-permute-start | bytes 393224 | tf_op jit(solution)/shard_map/ppermute | solution.py:22
  24.7 3.8 %collective-permute-start.5 = (f32[2,8,128]{2,1,0:T(8,128)S(1)}, f32[2,8,128]{2,1,0:T(8,128)S(1)}, u32[]{:S(2)}, u32[]{:S(2)}) collective-permute-start(f32[2,8,128]{2,1,0:T(8,128)S(1)} %get-tuple-element.18), channel_id=1, source_target_pairs={{0,1},{1,0},{2,3},{3,2},{4,5},{5,4},{6,7},{7,6},{8,9},{9,8},{10,11... | collective-permute-start | bytes 24584 | tf_op jit(solution)/shard_map/ppermute | solution.py:22
  25.1 3.7 %collective-permute-start.6 = (f32[2,8,128]{2,1,0:T(8,128)S(1)}, f32[2,8,128]{2,1,0:T(8,128)S(1)}, u32[]{:S(2)}, u32[]{:S(2)}) collective-permute-start(f32[2,8,128]{2,1,0:T(8,128)S(1)} %get-tuple-element.19), channel_id=1, source_target_pairs={{0,2},{1,3},{2,0},{3,1},{4,6},{5,7},{6,4},{7,5},{8,10},{9,11},{10,... | collective-permute-start | bytes 24584 | tf_op jit(solution)/shard_map/ppermute | solution.py:22
  26.1 3.1 %collective-permute-start.7 = (f32[2,8,128]{2,1,0:T(8,128)S(1)}, f32[2,8,128]{2,1,0:T(8,128)S(1)}, u32[]{:S(2)}, u32[]{:S(2)}) collective-permute-start(f32[2,8,128]{2,1,0:T(8,128)S(1)} %get-tuple-element.20), channel_id=1, source_target_pairs={{0,3},{1,2},{2,1},{3,0},{4,7},{5,6},{6,5},{7,4},{8,11},{9,10},{10,... | collective-permute-start | bytes 24584 | tf_op jit(solution)/shard_map/ppermute | solution.py:22
  29.5 1.9 %collective-permute-start.10 = (f32[8,512]{1,0:T(8,128)S(1)}, f32[8,512]{1,0:T(8,128)S(1)}, u32[]{:S(2)}, u32[]{:S(2)}) collective-permute-start(f32[8,512]{1,0:T(8,128)S(1)} %shard_map.68), channel_id=1, source_target_pairs={{0,1},{1,0},{2,3},{3,2},{4,5},{5,4},{6,7},{7,6},{8,9},{9,8},{10,11... | collective-permute-start | bytes 49160 | tf_op jit(solution)/shard_map/ppermute | solution.py:22
  29.7 3.7 %collective-permute-start.11 = (f32[8,512]{1,0:T(8,128)S(1)}, f32[8,512]{1,0:T(8,128)S(1)}, u32[]{:S(2)}, u32[]{:S(2)}) collective-permute-start(f32[8,512]{1,0:T(8,128)S(1)} %shard_map.68), channel_id=1, source_target_pairs={{0,2},{1,3},{2,0},{3,1},{4,6},{5,7},{6,4},{7,5},{8,10},{9,11},{10,... | collective-permute-start | bytes 49160 | tf_op jit(solution)/shard_map/ppermute | solution.py:22
  30.8 3.2 %collective-permute-start.12 = (f32[8,512]{1,0:T(8,128)S(1)}, f32[8,512]{1,0:T(8,128)S(1)}, u32[]{:S(2)}, u32[]{:S(2)}) collective-permute-start(f32[8,512]{1,0:T(8,128)S(1)} %shard_map.68), channel_id=1, source_target_pairs={{0,3},{1,2},{2,1},{3,0},{4,7},{5,6},{6,5},{7,4},{8,11},{9,10},{10,... | collective-permute-start | bytes 49160 | tf_op jit(solution)/shard_map/ppermute | solution.py:22

commit v7 on v6

--- a/solution.py
+++ b/solution.py
@@ -8,8 +8,6 @@
 from jax.sharding import PartitionSpec as P
 
 CORES = 2
-PIECE = 512
-AHEAD = 4
 SMALL = pltpu.CompilerParams(vmem_limit_bytes=8 << 20)
 NT = (((1,), (1,)), ((), ()))
 NN = (((1,), (0,)), ((), ()))
@@ -45,7 +43,7 @@
 COST = 1 << 32
 
 
-def project_kernel(steps, share, rows_first, ahead, after, act, og, wi, wo, lens, *refs):
+def project_kernel(steps, share, rows_first, ahead, piece, after, act, og, wi, wo, lens, *refs):
     refs = refs[after:]
     outs, (buf, wibuf, wobuf, lenbuf, sem, wsem) = refs[:-6], refs[-6:]
     me = lax.axis_index("tensor")
@@ -58,10 +56,10 @@
         pltpu.make_async_copy(wo, wobuf, wsem.at[1]),
         pltpu.make_async_copy(lens, lenbuf, wsem.at[2]),
     ]
-    pieces = [(side, at) for side, ref in enumerate((act, og)) for at in range(0, ref.shape[2], PIECE)]
+    pieces = [(side, at) for side, ref in enumerate((act, og)) for at in range(0, ref.shape[2], piece)]
     copies = []
     for slot, (side, at) in enumerate(pieces):
-        width = min(PIECE, (act, og)[side].shape[2] - at)
+        width = min(piece, (act, og)[side].shape[2] - at)
         copies.append(
             [
                 pltpu.make_async_copy(
@@ -89,8 +87,8 @@
         if slot + ahead < len(pieces):
             for copy in copies[slot + ahead]:
                 copy.start()
-        weight = (wibuf, wobuf)[side][:, at : at + PIECE]
-        token = buf[slot].reshape(tokens, PIECE)[:, : weight.shape[1]]
+        weight = (wibuf, wobuf)[side][:, at : at + piece]
+        token = buf[slot].reshape(tokens, piece)[:, : weight.shape[1]]
         if rows_first:
             none = jnp.zeros_like(weight)
             wide = jnp.concatenate([none, weight] if side else [weight, none], axis=0).T
@@ -117,19 +115,19 @@
         out[slot % per, rank:] = sums[1][:, slot * slots : (slot + 1) * slots]
 
 
-def project(act, og, wi, wo, lens, groups, share, rows_first, ahead, after=()):
+def project(act, og, wi, wo, lens, groups, share, rows_first, ahead, piece, after=()):
     steps = [step for group in groups for step in group]
     count = len(steps) * share
     slots, feat, hidden = act.shape[1], act.shape[2], og.shape[2]
     rank = wi.shape[0]
-    pieces = -(-feat // PIECE) - (-hidden // PIECE)
-    return pl.pallas_call(
-        functools.partial(project_kernel, steps, share, rows_first, ahead, len(after)),
+    pieces = -(-feat // piece) - (-hidden // piece)
+    return pl.pallas_call(
+        functools.partial(project_kernel, steps, share, rows_first, ahead, piece, len(after)),
         out_shape=[jax.ShapeDtypeStruct((len(group) * share, 2 * rank, slots), jnp.float32) for group in groups],
         in_specs=[HBM] * 5 + [VMEM] * len(after),
         out_specs=[VMEM] * len(groups),
         scratch_shapes=[
-            pltpu.VMEM((pieces, count, slots, PIECE), act.dtype),
+            pltpu.VMEM((pieces, count, slots, piece), act.dtype),
             pltpu.VMEM((rank, feat), wi.dtype),
             pltpu.VMEM((rank, hidden), wo.dtype),
             pltpu.SMEM(lens.shape, lens.dtype),
@@ -142,15 +140,14 @@
 
 
 def unit_kernel(share, rank, size, *refs):
-    singles, parts, outs = refs[:share], refs[share : -2 - size], refs[-2 - size : -2]
-    pairs, held = refs[-2:]
+    parts, outs, pairs, held = refs[:-4], refs[-4:-2], refs[-2], refs[-1]
     me = lax.axis_index("tensor")
     rows = rank * rank // 128
     span = rows // size
     dot = functools.partial(lax.dot_general, dimension_numbers=NT, preferred_element_type=jnp.float32)
     for k in range(share):
-        full = singles[k][0]
-        for part in parts:
+        full = parts[0][k]
+        for part in parts[1:]:
             full = full + part[k]
         high = full.astype(jnp.bfloat16)
         low = (full - high.astype(jnp.float32)).astype(jnp.bfloat16)
@@ -163,29 +160,32 @@
         scale = jnp.sqrt(jnp.sum(flat * flat) / (rank * rank) + 1e-06)
         unit = flat / scale
         for to in range(size):
-            held[to] = unit[to * span : (to + 1) * span]
-        for step in range(size):
-            outs[step][k] = held[me ^ step]
-
-
-def units(parts, singles, share, rank, size):
+            held[to, k] = unit[to * span : (to + 1) * span]
+    for j in range(size // CORES):
+        for core in range(CORES):
+            outs[core][j] = held[me ^ core ^ (CORES * j)]
+
+
+def units(parts, share, rank, size):
     span = rank * rank // 128 // size
     return pl.pallas_call(
         functools.partial(unit_kernel, share, rank, size),
-        out_shape=[jax.ShapeDtypeStruct((share, span, 128), jnp.float32)] * size,
-        in_specs=[VMEM] * (share + len(parts)),
-        out_specs=[VMEM] * size,
-        scratch_shapes=[pltpu.VMEM((share, rank, rank), jnp.float32), pltpu.VMEM((size, span, 128), jnp.float32)],
+        out_shape=[jax.ShapeDtypeStruct((size // CORES, share, span, 128), jnp.float32)] * CORES,
+        in_specs=[VMEM] * len(parts),
+        out_specs=[VMEM] * CORES,
+        scratch_shapes=[pltpu.VMEM((share, rank, rank), jnp.float32), pltpu.VMEM((size, share, span, 128), jnp.float32)],
         compiler_params=SMALL,
-    )(*singles, *parts)
-
-
-def score_kernel(share, size, shifts, *refs):
-    unit_refs, test_refs, out, held = refs[:size], refs[size:-2], refs[-2], refs[-1]
+    )(*parts)
+
+
+def score_kernel(share, far, shifts, own_ref, core_ref, *refs):
+    far_refs, test_refs, out, held = refs[: len(far)], refs[len(far) : -2], refs[-2], refs[-1]
     me, dp = lax.axis_index("tensor"), lax.axis_index("dp")
-    for step in range(size):
+    blocks = [(me, own_ref.at[0]), (me ^ 1, core_ref.at[0])]
+    blocks += [(me ^ step ^ core, ref.at[core]) for step, ref in zip(far, far_refs) for core in range(CORES)]
+    for owner, ref in blocks:
         for k in range(share):
-            held[(me ^ step) * share + k] = unit_refs[step][k]
+            held[owner * share + k] = ref[k]
     unit = jnp.concatenate([held[:, c, :] for c in range(held.shape[1])], axis=1).astype(jnp.bfloat16)
     tests = test_refs[0].shape[0]
     for step, test_ref in zip(shifts, test_refs):
@@ -194,18 +194,16 @@
         out[:, pl.ds(pl.multiple_of(at, 128), tests)] = part
 
 
-def score(unit_parts, test_parts, share):
-    size, groups = len(unit_parts), len(test_parts)
+def score(own, core, far_units, test_parts, share, size):
     tests, width = test_parts[0].shape
-    shifts = tuple(test_parts)
-    return pl.pallas_call(
-        functools.partial(score_kernel, share, size, shifts),
-        out_shape=jax.ShapeDtypeStruct((share * size, tests * groups), jnp.float32),
-        in_specs=[VMEM] * (size + groups),
+    return pl.pallas_call(
+        functools.partial(score_kernel, share, tuple(far_units), tuple(test_parts)),
+        out_shape=jax.ShapeDtypeStruct((share * size, tests * len(test_parts)), jnp.float32),
+        in_specs=[VMEM] * (2 + len(far_units) + len(test_parts)),
         out_specs=VMEM,
         scratch_shapes=[pltpu.VMEM((share * size, width // 128, 128), jnp.float32)],
         compiler_params=SMALL,
-    )(*unit_parts, *test_parts.values())
+    )(own, core, *far_units.values(), *test_parts.values())
 
 
 def shift(value, axis, size, step):
@@ -218,23 +216,30 @@
     own_tests = cut_tests(test_grads, size)
     tests = {0: own_tests, 1: shift(own_tests, "dp", groups, 1)}
     if groups == 4:
+        tests[2] = shift(tests[1], "dp", groups, 1)
         tests[3] = shift(own_tests, "dp", groups, 3)
-        tests[2] = shift(tests[1], "dp", groups, 1)
     else:
         tests.update({step: shift(own_tests, "dp", groups, step) for step in range(2, groups)})
 
     far = [CORES * x for x in range(1, size // CORES)]
     arrays = (activations, out_grads, proj_in.T, proj_out.T, lengths)
-    far_other, far_own = project(*arrays, [[step ^ 1 for step in far], far], share, False, 9, [own_tests])
-    far_other = far_other + 0.0 * tests[1][0, 0].astype(jnp.float32)
+    far_other, far_own = project(*arrays, [[step ^ 1 for step in far], far], share, False, 4, 512, [own_tests])
+    slots = far_other.shape[2]
+    far_other = far_other + 0.0 * tests[1][:1, :slots].astype(jnp.float32)
     far_sum = far_own + xor_permute(far_other, "tensor", size, 1)
     sums = [xor_permute(far_sum[i * share : (i + 1) * share], "tensor", size, step) for i, step in enumerate(far)]
-    near_other, near_own = project(*arrays, [[1], [0]], share, True, 4, [far_sum, tests[1]])
-    arrived = [xor_permute(near_other[k : k + 1], "tensor", size, 1) for k in range(share)]
-    unit_outs = units([near_own] + sums, arrived, share, rank, size)
-    unit_parts = [unit_outs[0]] + [xor_permute(unit_outs[step], "tensor", size, step) for step in range(1, size)]
-    part = score(unit_parts, tests, share)
-    parts = [part] + [xor_permute(part, "tensor", size, step) for step in range(1, size)]
+    near_other = project(*arrays, [[1]], share, False, 4, 1024, [far_sum, tests[1]])[0]
+    arrived = xor_permute(near_other, "tensor", size, 1)
+    near_own = project(*arrays, [[0]], share, False, 4, 1024, [near_other])[0]
+
+    own, core = units([near_own, arrived] + sums, share, rank, size)
+    core = xor_permute(core, "tensor", size, 1)
+    far_units = {
+        step: xor_permute(jnp.stack([own[j + 1], core[j + 1]]), "tensor", size, step) for j, step in enumerate(far)
+    }
+    part = score(own, core, far_units, tests, share, size)
+    part = part + xor_permute(part, "tensor", size, 1)
+    parts = [part] + [xor_permute(part, "tensor", size, step) for step in far]
     while len(parts) > 1:
         parts = [parts[i] + parts[i + 1] for i in range(0, len(parts), 2)]
     return parts[0]

time: 34.7 us -> 35 us (level)
  waiting for transfers between devices: 7.53 us -> 10.8 us
  starting transfers between devices: 11.2 us -> 9.19 us
  between operations: 0.73 us -> 0.09 us
  local copies, waits for them, and re-layouts: 0.53 us -> 0.01 us
    ppermute x10 -> x7, waiting for transfers between devices: 4.18 us -> 6.8 us  [xor_permute(): return lax.ppermute(value, axis, [(i, i ^ step) for i in range(size)])]
    ppermute x10 -> x7, starting transfers between devices: 6 us -> 4.03 us  [xor_permute(): return lax.ppermute(value, axis, [(i, i ^ step) for i in range(size)])]
    ppermute x3, waiting for transfers between devices: 3.35 us -> 3.95 us  [shift(): lax.ppermute(value, axis, [(i, (i + step) % size) for i in range(size)])]
    slice x2, local copies, waits for them, and re-layouts: 0.53 us -> 0.01 us  [the longest x1 0.01 us: shards(): own[j + 1]]
    pallas_call x2 -> x3, Pallas kernels: 12.1 us -> 12.3 us  [project(): pl.pallas_call(functools.partial(project_kernel, steps, share, rows_first...]
  transfers between devices with their start and end apart: 13 -> 10, of which waited for: 8 -> 6; matrix products, arithmetic and copies ran while one was open for 0% -> 0% of each run, Pallas kernels for 37% -> 37%
where the time goes in v7:
time: 35 us; the launch traced here: 34.8 us
  Pallas kernels  14.1 us (40%)
  waiting for transfers between devices  10.8 us (31%)
  starting transfers between devices  9.19 us (26%)
  other arithmetic  0.68 us (2%)
    pallas_call x3, Pallas kernels, project(): pl.pallas_call(functools.partial(project_kernel, steps, share, rows_first...  12.3 us
    ppermute x7, waiting for transfers between devices, xor_permute(): return lax.ppermute(value, axis, [(i, i ^ step) for i in range(size)])  6.8 us
    ppermute x3, starting transfers between devices, shift(): lax.ppermute(value, axis, [(i, (i + step) % size) for i in range(size)])  5.15 us
    ppermute x7, starting transfers between devices, xor_permute(): return lax.ppermute(value, axis, [(i, i ^ step) for i in range(size)])  4.03 us
    ppermute x3, waiting for transfers between devices, shift(): lax.ppermute(value, axis, [(i, (i + step) % size) for i in range(size)])  3.95 us
    pallas_call x1, Pallas kernels, cut_tests(): pl.pallas_call(cut_kernel, out_shape=jax.ShapeDtypeStruct((rows, width //...  0.96 us
  transfers between devices with their start and end apart: 10, of which 6 were waited for; matrix products, arithmetic and copies ran while one was open for 0% of the time, Pallas kernels for 37%

profile of v7, /device:TPU:0, one launch (start us, length us, event | category | flops | bytes accessed | tf_op | source)
XLA Modules:
  0.0 34.8 jit_solution(7114710082348054488)
XLA Ops:
  0.0 1.0 %shard_map.64.refs_0_.refs_1_ = bf16[128,1024]{1,0:T(8,128)(2,1)S(1)} custom-call(bf16[128,4096]{1,0:T(8,128)(2,1)} %tests.1), custom_call_target="tpu_custom_call" | custom-call | tf_op jit(solution)/shard_map/pallas_call | solution.py:33
  1.0 3.1 %collective-permute-start = (bf16[128,1024]{1,0:T(8,128)(2,1)S(1)}, bf16[128,1024]{1,0:T(8,128)(2,1)S(1)}, u32[]{:S(2)}, u32[]{:S(2)}) collective-permute-start(bf16[128,1024]{1,0:T(8,128)(2,1)S(1)} %shard_map.64.refs_0_.refs_1_), channel_id=1, source_target_pairs={{0,4},{4,8},{8,12},{12,0},{1,5},{5,9},{9,13},{13,1},{2,6},{6,10},{... | collective-permute-start | bytes 786440 | tf_op jit(solution)/shard_map/ppermute | solution.py:210
  4.0 5.3 %shard_map.65 = (f32[2,128,256]{2,1,0:T(8,128)S(1)}, f32[2,128,256]{2,1,0:T(8,128)S(1)}) custom-call(bf16[8,256,1024]{2,1,0:T(8,128)(2,1)} %act.5, bf16[8,256,3584]{2,1,0:T(8,128)(2,1)} %og.5, bf16[64,1024]{1,0:T(8,128)(2,1)} %bitcast.6, bf16[64,3584]{1,0:T(8,128)(2,1)} %bitcast.3, s32[8]{0:T(128)} %lens.5, bf16[128,1024]{1,0:T(8,128)(2,1)S(1)} %shard_map.64.refs_0_.refs_1_), custom_call_target="tpu_custom_call" | custom-call | flops 4294967296 | bytes 16777216 | tf_op jit(solution)/shard_map/pallas_call | solution.py:124
  9.4 3.0 %collective-permute-done.refs_1_.refs_2_ = bf16[128,1024]{1,0:T(8,128)(2,1)S(1)} collective-permute-done((bf16[128,1024]{1,0:T(8,128)(2,1)S(1)}, bf16[128,1024]{1,0:T(8,128)(2,1)S(1)}, u32[]{:S(2)}, u32[]{:S(2)}) %collective-permute-start) | collective-permute-done | bytes 262176 | tf_op jit(solution)/shard_map/ppermute | solution.py:210
  12.4 0.1 collective-permute-start.1
  12.5 1.8 %collective-permute-start.7 = (bf16[128,1024]{1,0:T(8,128)(2,1)S(1)}, bf16[128,1024]{1,0:T(8,128)(2,1)S(1)}, u32[]{:S(2)}, u32[]{:S(2)}) collective-permute-start(bf16[128,1024]{1,0:T(8,128)(2,1)S(1)} %shard_map.64.refs_0_.refs_1_), channel_id=1, source_target_pairs={{0,12},{4,0},{8,4},{12,8},{1,13},{5,1},{9,5},{13,9},{2,14},{6,2},{... | collective-permute-start | bytes 786440 | tf_op jit(solution)/shard_map/ppermute | solution.py:210
  14.3 0.3 collective-permute-start.6
  14.6 0.0 collective-permute-done.1
  14.6 1.6 %collective-permute-start.3 = (f32[2,128,256]{2,1,0:T(8,128)S(1)}, f32[2,128,256]{2,1,0:T(8,128)S(1)}, u32[]{:S(2)}, u32[]{:S(2)}) collective-permute-start(f32[2,128,256]{2,1,0:T(8,128)S(1)} %add.22.refs_0_), channel_id=1, source_target_pairs={{0,2},{1,3},{2,0},{3,1},{4,6},{5,7},{6,4},{7,5},{8,10},{9,11},{10,... | collective-permute-start | bytes 786440 | tf_op jit(solution)/shard_map/ppermute | solution.py:20
  16.2 3.5 %shard_map.66.refs_0_ = f32[2,128,256]{2,1,0:T(8,128)S(1)} custom-call(bf16[8,256,1024]{2,1,0:T(8,128)(2,1)} %act.5, bf16[8,256,3584]{2,1,0:T(8,128)(2,1)} %og.5, bf16[64,1024]{1,0:T(8,128)(2,1)} %bitcast.7, bf16[64,3584]{1,0:T(8,128)(2,1)} %bitcast.4, s32[8]{0:T(128)} %lens.5, f32[2,128,256]{2,1,0:T(8,128)S(1)} %add.22.refs_0_, ...), custom_call_target="tpu_custom_call" | custom-call | flops 4294967296 | bytes 16777216 | tf_op jit(solution)/shard_map/pallas_call | solution.py:124
  19.6 0.1 collective-permute-start.2
  19.7 3.5 %shard_map.67.refs_0_ = f32[2,128,256]{2,1,0:T(8,128)S(1)} custom-call(bf16[8,256,1024]{2,1,0:T(8,128)(2,1)} %act.5, bf16[8,256,3584]{2,1,0:T(8,128)(2,1)} %og.5, bf16[64,1024]{1,0:T(8,128)(2,1)} %bitcast.8, bf16[64,3584]{1,0:T(8,128)(2,1)} %bitcast.5, s32[8]{0:T(128)} %lens.5, f32[2,128,256]{2,1,0:T(8,128)S(1)} %shard_map.66.refs_0_), custom_call_target="tpu_custom_call" | custom-call | flops 4294967296 | bytes 16777216 | tf_op jit(solution)/shard_map/pallas_call | solution.py:124
  23.2 0.0 collective-permute-done.2.refs_1_
  23.2 0.0 collective-permute-done.3.refs_2_
  23.2 0.5 %shard_map.68 = (f32[2,2,8,128]{3,2,1,0:T(8,128)S(1)}, f32[2,2,8,128]{3,2,1,0:T(8,128)S(1)}) custom-call(f32[2,128,256]{2,1,0:T(8,128)S(1)} %shard_map.67.refs_0_, f32[2,128,256]{2,1,0:T(8,128)S(1)} %collective-permute-done.2.refs_1_, f32[2,128,256]{2,1,0:T(8,128)S(1)} %collective-permute-done.3.refs_2_), custom_call_target="tpu_custom_call" | custom-call | tf_op jit(solution)/shard_map/pallas_call | solution.py:171
  23.7 0.6 %collective-permute-start.4 = (f32[2,2,8,128]{3,2,1,0:T(8,128)S(1)}, f32[2,2,8,128]{3,2,1,0:T(8,128)S(1)}, u32[]{:S(2)}, u32[]{:S(2)}) collective-permute-start(f32[2,2,8,128]{3,2,1,0:T(8,128)S(1)} %get-tuple-element.12), channel_id=1, source_target_pairs={{0,1},{1,0},{2,3},{3,2},{4,5},{5,4},{6,7},{7,6},{8,9},{9,8},{10,11... | collective-permute-start | bytes 49160 | tf_op jit(solution)/shard_map/ppermute | solution.py:20
  24.3 0.8 %collective-permute-done.4.core_ref = f32[2,2,8,128]{3,2,1,0:T(8,128)S(1)} collective-permute-done((f32[2,2,8,128]{3,2,1,0:T(8,128)S(1)}, f32[2,2,8,128]{3,2,1,0:T(8,128)S(1)}, u32[]{:S(2)}, u32[]{:S(2)}) %collective-permute-start.4) | collective-permute-done | bytes 16416 | tf_op jit(solution)/shard_map/ppermute | solution.py:20
  25.1 0.9 %collective-permute-start.5 = (f32[2,2,8,128]{3,2,1,0:T(8,128)S(1)}, f32[2,2,8,128]{3,2,1,0:T(8,128)S(1)}, u32[]{:S(2)}, u32[]{:S(2)}) collective-permute-start(f32[2,2,8,128]{3,2,1,0:T(8,128)S(1)} %pad_maximum_fusion), channel_id=1, source_target_pairs={{0,2},{1,3},{2,0},{3,1},{4,6},{5,7},{6,4},{7,5},{8,10},{9,11},{10,... | collective-permute-start | bytes 49160 | tf_op jit(solution)/shard_map/ppermute | solution.py:20
  26.0 0.0 collective-permute-done.7.refs_4_
  26.0 0.9 %collective-permute-done.6.refs_3_ = bf16[128,1024]{1,0:T(8,128)(2,1)S(1)} collective-permute-done((bf16[128,1024]{1,0:T(8,128)(2,1)S(1)}, bf16[128,1024]{1,0:T(8,128)(2,1)S(1)}, u32[]{:S(2)}, u32[]{:S(2)}) %collective-permute-start.6) | collective-permute-done | bytes 262176 | tf_op jit(solution)/shard_map/ppermute | solution.py:210
  27.0 1.9 %collective-permute-done.5.refs_0_ = f32[2,2,8,128]{3,2,1,0:T(8,128)S(1)} collective-permute-done((f32[2,2,8,128]{3,2,1,0:T(8,128)S(1)}, f32[2,2,8,128]{3,2,1,0:T(8,128)S(1)}, u32[]{:S(2)}, u32[]{:S(2)}) %collective-permute-start.5) | collective-permute-done | bytes 16416 | tf_op jit(solution)/shard_map/ppermute | solution.py:20
  28.9 0.4 %shard_map.69 = f32[8,512]{1,0:T(8,128)S(1)} custom-call(f32[2,2,8,128]{3,2,1,0:T(8,128)S(1)} %get-tuple-element.11.own_ref, f32[2,2,8,128]{3,2,1,0:T(8,128)S(1)} %collective-permute-done.4.core_ref, f32[2,2,8,128]{3,2,1,0:T(8,128)S(1)} %collective-permute-done.5.refs_0_, bf16[128,1024]{1,0:T(8,128)(2,1)S(1)} %shard_map.64.refs_0_.refs_1_, ...), custom_call_target="tpu_custom_call" | custom-call | tf_op jit(solution)/shard_map/pallas_call | solution.py:199
  29.3 0.0 collective-permute-start.8
  29.3 1.2 %collective-permute-done.8 = f32[8,512]{1,0:T(8,128)S(1)} collective-permute-done((f32[8,512]{1,0:T(8,128)S(1)}, f32[8,512]{1,0:T(8,128)S(1)}, u32[]{:S(2)}, u32[]{:S(2)}) %collective-permute-start.8) | collective-permute-done | bytes 16416 | tf_op jit(solution)/shard_map/ppermute | solution.py:20
  30.5 0.9 %collective-permute-start.9 = (f32[8,512]{1,0:T(8,128)S(1)}, f32[8,512]{1,0:T(8,128)S(1)}, u32[]{:S(2)}, u32[]{:S(2)}) collective-permute-start(f32[8,512]{1,0:T(8,128)S(1)} %add.23), channel_id=1, source_target_pairs={{0,2},{1,3},{2,0},{3,1},{4,6},{5,7},{6,4},{7,5},{8,10},{9,11},{10,... | collective-permute-start | bytes 49160 | tf_op jit(solution)/shard_map/ppermute | solution.py:20
  31.3 2.9 %collective-permute-done.9 = f32[8,512]{1,0:T(8,128)S(1)} collective-permute-done((f32[8,512]{1,0:T(8,128)S(1)}, f32[8,512]{1,0:T(8,128)S(1)}, u32[]{:S(2)}, u32[]{:S(2)}) %collective-permute-start.9) | collective-permute-done | bytes 16416 | tf_op jit(solution)/shard_map/ppermute | solution.py:20
  34.2 0.6 %add.24 = f32[8,512]{1,0:T(8,128)} add(f32[8,512]{1,0:T(8,128)S(1)} %add.23, f32[8,512]{1,0:T(8,128)S(1)} %collective-permute-done.9) | non-fusion elementwise | flops 4096 | bytes 49152 | tf_op jit(solution)/shard_map/add | solution.py:244
  (7 shorter events, 0.1 us)
Async XLA Ops:
  1.0 11.4 %collective-permute-start = (bf16[128,1024]{1,0:T(8,128)(2,1)S(1)}, bf16[128,1024]{1,0:T(8,128)(2,1)S(1)}, u32[]{:S(2)}, u32[]{:S(2)}) collective-permute-start(bf16[128,1024]{1,0:T(8,128)(2,1)S(1)} %shard_map.64.refs_0_.refs_1_), channel_id=1, source_target_pairs={{0,4},{4,8},{8,12},{12,0},{1,5},{5,9},{9,13},{13,1},{2,6},{6,10},{... | collective-permute-start | bytes 786440 | tf_op jit(solution)/shard_map/ppermute | solution.py:210
  12.4 2.2 %collective-permute-start.1 = (f32[2,128,256]{2,1,0:T(8,128)S(1)}, f32[2,128,256]{2,1,0:T(8,128)S(1)}, u32[]{:S(2)}, u32[]{:S(2)}) collective-permute-start(f32[2,128,256]{2,1,0:T(8,128)S(1)} %broadcast_add_fusion), channel_id=1, source_target_pairs={{0,1},{1,0},{2,3},{3,2},{4,5},{5,4},{6,7},{7,6},{8,9},{9,8},{10,11... | collective-permute-start | bytes 786440 | tf_op jit(solution)/shard_map/ppermute | solution.py:20
  12.5 13.5 %collective-permute-start.7 = (bf16[128,1024]{1,0:T(8,128)(2,1)S(1)}, bf16[128,1024]{1,0:T(8,128)(2,1)S(1)}, u32[]{:S(2)}, u32[]{:S(2)}) collective-permute-start(bf16[128,1024]{1,0:T(8,128)(2,1)S(1)} %shard_map.64.refs_0_.refs_1_), channel_id=1, source_target_pairs={{0,12},{4,0},{8,4},{12,8},{1,13},{5,1},{9,5},{13,9},{2,14},{6,2},{... | collective-permute-start | bytes 786440 | tf_op jit(solution)/shard_map/ppermute | solution.py:210
  14.3 12.7 %collective-permute-start.6 = (bf16[128,1024]{1,0:T(8,128)(2,1)S(1)}, bf16[128,1024]{1,0:T(8,128)(2,1)S(1)}, u32[]{:S(2)}, u32[]{:S(2)}) collective-permute-start(bf16[128,1024]{1,0:T(8,128)(2,1)S(1)} %collective-permute-done.refs_1_.refs_2_), channel_id=1, source_target_pairs={{0,4},{4,8},{8,12},{12,0},{1,5},{5,9},{9,13},{13,1},{2,6},{6,10},{... | collective-permute-start | bytes 786440 | tf_op jit(solution)/shard_map/ppermute | solution.py:210
  14.6 8.6 %collective-permute-start.3 = (f32[2,128,256]{2,1,0:T(8,128)S(1)}, f32[2,128,256]{2,1,0:T(8,128)S(1)}, u32[]{:S(2)}, u32[]{:S(2)}) collective-permute-start(f32[2,128,256]{2,1,0:T(8,128)S(1)} %add.22.refs_0_), channel_id=1, source_target_pairs={{0,2},{1,3},{2,0},{3,1},{4,6},{5,7},{6,4},{7,5},{8,10},{9,11},{10,... | collective-permute-start | bytes 786440 | tf_op jit(solution)/shard_map/ppermute | solution.py:20
  19.6 3.6 %collective-permute-start.2 = (f32[2,128,256]{2,1,0:T(8,128)S(1)}, f32[2,128,256]{2,1,0:T(8,128)S(1)}, u32[]{:S(2)}, u32[]{:S(2)}) collective-permute-start(f32[2,128,256]{2,1,0:T(8,128)S(1)} %shard_map.66.refs_0_), channel_id=1, source_target_pairs={{0,1},{1,0},{2,3},{3,2},{4,5},{5,4},{6,7},{7,6},{8,9},{9,8},{10,11... | collective-permute-start | bytes 786440 | tf_op jit(solution)/shard_map/ppermute | solution.py:20
  23.7 1.4 %collective-permute-start.4 = (f32[2,2,8,128]{3,2,1,0:T(8,128)S(1)}, f32[2,2,8,128]{3,2,1,0:T(8,128)S(1)}, u32[]{:S(2)}, u32[]{:S(2)}) collective-permute-start(f32[2,2,8,128]{3,2,1,0:T(8,128)S(1)} %get-tuple-element.12), channel_id=1, source_target_pairs={{0,1},{1,0},{2,3},{3,2},{4,5},{5,4},{6,7},{7,6},{8,9},{9,8},{10,11... | collective-permute-start | bytes 49160 | tf_op jit(solution)/shard_map/ppermute | solution.py:20
  25.1 3.7 %collective-permute-start.5 = (f32[2,2,8,128]{3,2,1,0:T(8,128)S(1)}, f32[2,2,8,128]{3,2,1,0:T(8,128)S(1)}, u32[]{:S(2)}, u32[]{:S(2)}) collective-permute-start(f32[2,2,8,128]{3,2,1,0:T(8,128)S(1)} %pad_maximum_fusion), channel_id=1, source_target_pairs={{0,2},{1,3},{2,0},{3,1},{4,6},{5,7},{6,4},{7,5},{8,10},{9,11},{10,... | collective-permute-start | bytes 49160 | tf_op jit(solution)/shard_map/ppermute | solution.py:20
  29.3 1.2 %collective-permute-start.8 = (f32[8,512]{1,0:T(8,128)S(1)}, f32[8,512]{1,0:T(8,128)S(1)}, u32[]{:S(2)}, u32[]{:S(2)}) collective-permute-start(f32[8,512]{1,0:T(8,128)S(1)} %shard_map.69), channel_id=1, source_target_pairs={{0,1},{1,0},{2,3},{3,2},{4,5},{5,4},{6,7},{7,6},{8,9},{9,8},{10,11... | collective-permute-start | bytes 49160 | tf_op jit(solution)/shard_map/ppermute | solution.py:20
  30.5 3.7 %collective-permute-start.9 = (f32[8,512]{1,0:T(8,128)S(1)}, f32[8,512]{1,0:T(8,128)S(1)}, u32[]{:S(2)}, u32[]{:S(2)}) collective-permute-start(f32[8,512]{1,0:T(8,128)S(1)} %add.23), channel_id=1, source_target_pairs={{0,2},{1,3},{2,0},{3,1},{4,6},{5,7},{6,4},{7,5},{8,10},{9,11},{10,... | collective-permute-start | bytes 49160 | tf_op jit(solution)/shard_map/ppermute | solution.py:20

commit v8 on v7

--- a/solution.py
+++ b/solution.py
@@ -10,7 +10,6 @@
 CORES = 2
 SMALL = pltpu.CompilerParams(vmem_limit_bytes=8 << 20)
 NT = (((1,), (1,)), ((), ()))
-NN = (((1,), (0,)), ((), ()))
 HBM = pl.BlockSpec(memory_space=pltpu.HBM)
 in_hbm = functools.partial(pltpu.with_memory_space_constraint, memory_space=pltpu.HBM)
 VMEM = pl.BlockSpec(memory_space=pltpu.VMEM)
@@ -43,7 +42,7 @@
 COST = 1 << 32
 
 
-def project_kernel(steps, share, rows_first, ahead, piece, after, act, og, wi, wo, lens, *refs):
+def project_kernel(steps, share, ahead, piece, after, act, og, wi, wo, lens, *refs):
     refs = refs[after:]
     outs, (buf, wibuf, wobuf, lenbuf, sem, wsem) = refs[:-6], refs[-6:]
     me = lax.axis_index("tensor")
@@ -89,40 +88,26 @@
                 copy.start()
         weight = (wibuf, wobuf)[side][:, at : at + piece]
         token = buf[slot].reshape(tokens, piece)[:, : weight.shape[1]]
-        if rows_first:
-            none = jnp.zeros_like(weight)
-            wide = jnp.concatenate([none, weight] if side else [weight, none], axis=0).T
-            half = tokens // 2
-            part = [
-                lax.dot_general(token[i * half : (i + 1) * half], wide, NN, preferred_element_type=jnp.float32)
-                for i in range(2)
-            ]
-            sums = part if slot == 0 else [sums[0] + part[0], sums[1] + part[1]]
-        else:
-            part = lax.dot_general(weight, token, NT, preferred_element_type=jnp.float32)
-            sums[side] = part if sums[side] is None else sums[side] + part
-    if rows_first:
-        whole = jnp.concatenate([one.T for one in sums], axis=1)
-        sums = [whole[:rank], whole[rank:]]
+        part = lax.dot_general(weight, token, NT, preferred_element_type=jnp.float32)
+        sums[side] = part if sums[side] is None else sums[side] + part
     small[2].wait()
     col = lax.broadcasted_iota(jnp.int32, (rank, slots), 1)
-    per = count // len(outs)
-    for slot in range(count):
+    places = [out.at[i] for out in outs for i in range(out.shape[0])]
+    for slot, out in enumerate(places):
         length = lenbuf[(me ^ steps[slot // share]) * share + slot % share]
-        out = outs[slot // per]
         one = sums[0][:, slot * slots : (slot + 1) * slots] * (1.0 / length.astype(jnp.float32))
-        out[slot % per, :rank] = jnp.where(col < length, one, 0.0)
-        out[slot % per, rank:] = sums[1][:, slot * slots : (slot + 1) * slots]
-
-
-def project(act, og, wi, wo, lens, groups, share, rows_first, ahead, piece, after=()):
+        out[:rank] = jnp.where(col < length, one, 0.0)
+        out[rank:] = sums[1][:, slot * slots : (slot + 1) * slots]
+
+
+def project(act, og, wi, wo, lens, groups, share, ahead, piece, after=()):
     steps = [step for group in groups for step in group]
     count = len(steps) * share
     slots, feat, hidden = act.shape[1], act.shape[2], og.shape[2]
     rank = wi.shape[0]
     pieces = -(-feat // piece) - (-hidden // piece)
     return pl.pallas_call(
-        functools.partial(project_kernel, steps, share, rows_first, ahead, piece, len(after)),
+        functools.partial(project_kernel, steps, share, ahead, piece, len(after)),
         out_shape=[jax.ShapeDtypeStruct((len(group) * share, 2 * rank, slots), jnp.float32) for group in groups],
         in_specs=[HBM] * 5 + [VMEM] * len(after),
         out_specs=[VMEM] * len(groups),
@@ -223,16 +208,16 @@
 
     far = [CORES * x for x in range(1, size // CORES)]
     arrays = (activations, out_grads, proj_in.T, proj_out.T, lengths)
-    far_other, far_own = project(*arrays, [[step ^ 1 for step in far], far], share, False, 4, 512, [own_tests])
-    slots = far_other.shape[2]
-    far_other = far_other + 0.0 * tests[1][:1, :slots].astype(jnp.float32)
-    far_sum = far_own + xor_permute(far_other, "tensor", size, 1)
+    sends = [[step ^ 1 for step in far] + [1], far]
+    other, far_own = project(*arrays, sends, share, 3, 512, [own_tests])
+    other = other + 0.0 * tests[1][:1, : other.shape[2]].astype(jnp.float32)
+    arrived = xor_permute(other, "tensor", size, 1)
+    cut = len(far) * share
+    far_sum = far_own + arrived[:cut]
     sums = [xor_permute(far_sum[i * share : (i + 1) * share], "tensor", size, step) for i, step in enumerate(far)]
-    near_other = project(*arrays, [[1]], share, False, 4, 1024, [far_sum, tests[1]])[0]
-    arrived = xor_permute(near_other, "tensor", size, 1)
-    near_own = project(*arrays, [[0]], share, False, 4, 1024, [near_other])[0]
-
-    own, core = units([near_own, arrived] + sums, share, rank, size)
+    near_own = project(*arrays, [[0]], share, 4, 1024, [far_sum])[0]
+
+    own, core = units([near_own, arrived[cut:]] + sums, share, rank, size)
     core = xor_permute(core, "tensor", size, 1)
     far_units = {
         step: xor_permute(jnp.stack([own[j + 1], core[j + 1]]), "tensor", size, step) for j, step in enumerate(far)

time: 35 us -> 34.5 us (0.986)
  Pallas kernels: 14.1 us -> 12.6 us
  starting transfers between devices: 9.19 us -> 9.84 us
    ppermute x7 -> x6, waiting for transfers between devices: 6.8 us -> 8.3 us  [xor_permute(): return lax.ppermute(value, axis, [(i, i ^ step) for i in range(size)])]
    pallas_call x3 -> x2, Pallas kernels: 12.3 us -> 10.8 us  [project(): pl.pallas_call(functools.partial(project_kernel, steps, share, ahead, pie...]
    ppermute x3, waiting for transfers between devices: 3.95 us -> 2.74 us  [shift(): lax.ppermute(value, axis, [(i, (i + step) % size) for i in range(size)])]
    ppermute x7 -> x6, starting transfers between devices: 4.03 us -> 4.68 us  [xor_permute(): return lax.ppermute(value, axis, [(i, i ^ step) for i in range(size)])]
  transfers between devices with their start and end apart: 10 -> 9, of which waited for: 6 -> 7; matrix products, arithmetic and copies ran while one was open for 0% -> 0% of each run, Pallas kernels for 37% -> 33%
where the time goes in v8:
time: 34.5 us; the launch traced here: 34.3 us
  Pallas kernels  12.6 us (37%)
  waiting for transfers between devices  11 us (32%)
  starting transfers between devices  9.84 us (29%)
  other arithmetic  0.72 us (2%)
    pallas_call x2, Pallas kernels, project(): pl.pallas_call(functools.partial(project_kernel, steps, share, ahead, pie...  10.8 us
    ppermute x6, waiting for transfers between devices, xor_permute(): return lax.ppermute(value, axis, [(i, i ^ step) for i in range(size)])  8.3 us
    ppermute x3, starting transfers between devices, shift(): lax.ppermute(value, axis, [(i, (i + step) % size) for i in range(size)])  5.15 us
    ppermute x6, starting transfers between devices, xor_permute(): return lax.ppermute(value, axis, [(i, i ^ step) for i in range(size)])  4.68 us
    ppermute x3, waiting for transfers between devices, shift(): lax.ppermute(value, axis, [(i, (i + step) % size) for i in range(size)])  2.74 us
    pallas_call x1, Pallas kernels, cut_tests(): pl.pallas_call(cut_kernel, out_shape=jax.ShapeDtypeStruct((rows, width //...  0.96 us
  transfers between devices with their start and end apart: 9, of which 7 were waited for; matrix products, arithmetic and copies ran while one was open for 0% of the time, Pallas kernels for 33%

profile of v8, /device:TPU:0, one launch (start us, length us, event | category | flops | bytes accessed | tf_op | source)
XLA Modules:
  0.0 34.3 jit_solution(6106789960077398228)
XLA Ops:
  0.0 1.0 %shard_map.64.refs_0_.refs_1_ = bf16[128,1024]{1,0:T(8,128)(2,1)S(1)} custom-call(bf16[128,4096]{1,0:T(8,128)(2,1)} %tests.1), custom_call_target="tpu_custom_call" | custom-call | tf_op jit(solution)/shard_map/pallas_call | solution.py:32
  1.0 3.1 %collective-permute-start = (bf16[128,1024]{1,0:T(8,128)(2,1)S(1)}, bf16[128,1024]{1,0:T(8,128)(2,1)S(1)}, u32[]{:S(2)}, u32[]{:S(2)}) collective-permute-start(bf16[128,1024]{1,0:T(8,128)(2,1)S(1)} %shard_map.64.refs_0_.refs_1_), channel_id=1, source_target_pairs={{0,4},{4,8},{8,12},{12,0},{1,5},{5,9},{9,13},{13,1},{2,6},{6,10},{... | collective-permute-start | bytes 786440 | tf_op jit(solution)/shard_map/ppermute | solution.py:195
  4.0 7.3 %shard_map.65 = (f32[4,128,256]{2,1,0:T(8,128)S(1)}, f32[2,128,256]{2,1,0:T(8,128)S(1)}) custom-call(bf16[8,256,1024]{2,1,0:T(8,128)(2,1)} %act.3, bf16[8,256,3584]{2,1,0:T(8,128)(2,1)} %og.3, bf16[64,1024]{1,0:T(8,128)(2,1)} %bitcast.5, bf16[64,3584]{1,0:T(8,128)(2,1)} %bitcast.3, s32[8]{0:T(128)} %lens.3, bf16[128,1024]{1,0:T(8,128)(2,1)S(1)} %shard_map.64.refs_0_.refs_1_), custom_call_target="tpu_custom_call" | custom-call | flops 4294967296 | bytes 16777216 | tf_op jit(solution)/shard_map/pallas_call | solution.py:109
  11.4 1.0 %collective-permute-done.refs_2_ = bf16[128,1024]{1,0:T(8,128)(2,1)S(1)} collective-permute-done((bf16[128,1024]{1,0:T(8,128)(2,1)S(1)}, bf16[128,1024]{1,0:T(8,128)(2,1)S(1)}, u32[]{:S(2)}, u32[]{:S(2)}) %collective-permute-start) | collective-permute-done | bytes 262176 | tf_op jit(solution)/shard_map/ppermute | solution.py:195
  12.4 0.1 collective-permute-start.1
  12.5 1.8 %collective-permute-start.6 = (bf16[128,1024]{1,0:T(8,128)(2,1)S(1)}, bf16[128,1024]{1,0:T(8,128)(2,1)S(1)}, u32[]{:S(2)}, u32[]{:S(2)}) collective-permute-start(bf16[128,1024]{1,0:T(8,128)(2,1)S(1)} %shard_map.64.refs_0_.refs_1_), channel_id=1, source_target_pairs={{0,12},{4,0},{8,4},{12,8},{1,13},{5,1},{9,5},{13,9},{2,14},{6,2},{... | collective-permute-start | bytes 786440 | tf_op jit(solution)/shard_map/ppermute | solution.py:195
  14.3 0.3 collective-permute-start.5
  14.6 0.0 collective-permute-done.1
  14.6 0.1 fusion.1
  14.6 1.6 %collective-permute-start.2 = (f32[2,128,256]{2,1,0:T(8,128)S(1)}, f32[2,128,256]{2,1,0:T(8,128)S(1)}, u32[]{:S(2)}, u32[]{:S(2)}) collective-permute-start(f32[2,128,256]{2,1,0:T(8,128)S(1)} %get-tuple-element.14.refs_0_), channel_id=1, source_target_pairs={{0,2},{1,3},{2,0},{3,1},{4,6},{5,7},{6,4},{7,5},{8,10},{9,11},{10,... | collective-permute-start | bytes 786440 | tf_op jit(solution)/shard_map/ppermute | solution.py:19
  16.2 3.5 %shard_map.66.refs_0_ = f32[2,128,256]{2,1,0:T(8,128)S(1)} custom-call(bf16[8,256,1024]{2,1,0:T(8,128)(2,1)} %act.3, bf16[8,256,3584]{2,1,0:T(8,128)(2,1)} %og.3, bf16[64,1024]{1,0:T(8,128)(2,1)} %bitcast.6, bf16[64,3584]{1,0:T(8,128)(2,1)} %bitcast.4, s32[8]{0:T(128)} %lens.3, f32[2,128,256]{2,1,0:T(8,128)S(1)} %get-tuple-element.14.refs_0_), custom_call_target="tpu_custom_call" | custom-call | flops 4294967296 | bytes 16777216 | tf_op jit(solution)/shard_map/pallas_call | solution.py:109
  19.7 3.2 %collective-permute-done.2.refs_2_ = f32[2,128,256]{2,1,0:T(8,128)S(1)} collective-permute-done((f32[2,128,256]{2,1,0:T(8,128)S(1)}, f32[2,128,256]{2,1,0:T(8,128)S(1)}, u32[]{:S(2)}, u32[]{:S(2)}) %collective-permute-start.2) | collective-permute-done | bytes 262176 | tf_op jit(solution)/shard_map/ppermute | solution.py:19
  22.9 0.5 %shard_map.67 = (f32[2,2,8,128]{3,2,1,0:T(8,128)S(1)}, f32[2,2,8,128]{3,2,1,0:T(8,128)S(1)}) custom-call(f32[2,128,256]{2,1,0:T(8,128)S(1)} %shard_map.66.refs_0_, f32[2,128,256]{2,1,0:T(8,128)S(1)} %get-tuple-element.13.refs_1_, f32[2,128,256]{2,1,0:T(8,128)S(1)} %collective-permute-done.2.refs_2_), custom_call_target="tpu_custom_call" | custom-call | tf_op jit(solution)/shard_map/pallas_call | solution.py:156
  23.4 0.1 collective-permute-start.3
  23.5 1.2 %collective-permute-done.3.core_ref = f32[2,2,8,128]{3,2,1,0:T(8,128)S(1)} collective-permute-done((f32[2,2,8,128]{3,2,1,0:T(8,128)S(1)}, f32[2,2,8,128]{3,2,1,0:T(8,128)S(1)}, u32[]{:S(2)}, u32[]{:S(2)}) %collective-permute-start.3) | collective-permute-done | bytes 16416 | tf_op jit(solution)/shard_map/ppermute | solution.py:19
  24.6 1.5 %collective-permute-start.4 = (f32[2,2,8,128]{3,2,1,0:T(8,128)S(1)}, f32[2,2,8,128]{3,2,1,0:T(8,128)S(1)}, u32[]{:S(2)}, u32[]{:S(2)}) collective-permute-start(f32[2,2,8,128]{3,2,1,0:T(8,128)S(1)} %pad_maximum_fusion), channel_id=1, source_target_pairs={{0,2},{1,3},{2,0},{3,1},{4,6},{5,7},{6,4},{7,5},{8,10},{9,11},{10,... | collective-permute-start | bytes 49160 | tf_op jit(solution)/shard_map/ppermute | solution.py:19
  26.1 0.0 collective-permute-done.6.refs_4_
  26.1 1.7 %collective-permute-done.5.refs_3_ = bf16[128,1024]{1,0:T(8,128)(2,1)S(1)} collective-permute-done((bf16[128,1024]{1,0:T(8,128)(2,1)S(1)}, bf16[128,1024]{1,0:T(8,128)(2,1)S(1)}, u32[]{:S(2)}, u32[]{:S(2)}) %collective-permute-start.5) | collective-permute-done | bytes 262176 | tf_op jit(solution)/shard_map/ppermute | solution.py:195
  27.9 0.5 %collective-permute-done.4.refs_0_ = f32[2,2,8,128]{3,2,1,0:T(8,128)S(1)} collective-permute-done((f32[2,2,8,128]{3,2,1,0:T(8,128)S(1)}, f32[2,2,8,128]{3,2,1,0:T(8,128)S(1)}, u32[]{:S(2)}, u32[]{:S(2)}) %collective-permute-start.4) | collective-permute-done | bytes 16416 | tf_op jit(solution)/shard_map/ppermute | solution.py:19
  28.4 0.4 %shard_map.68 = f32[8,512]{1,0:T(8,128)S(1)} custom-call(f32[2,2,8,128]{3,2,1,0:T(8,128)S(1)} %get-tuple-element.11.own_ref, f32[2,2,8,128]{3,2,1,0:T(8,128)S(1)} %collective-permute-done.3.core_ref, f32[2,2,8,128]{3,2,1,0:T(8,128)S(1)} %collective-permute-done.4.refs_0_, bf16[128,1024]{1,0:T(8,128)(2,1)S(1)} %shard_map.64.refs_0_.refs_1_, ...), custom_call_target="tpu_custom_call" | custom-call | tf_op jit(solution)/shard_map/pallas_call | solution.py:184
  28.8 0.0 collective-permute-start.7
  28.8 1.2 %collective-permute-done.7 = f32[8,512]{1,0:T(8,128)S(1)} collective-permute-done((f32[8,512]{1,0:T(8,128)S(1)}, f32[8,512]{1,0:T(8,128)S(1)}, u32[]{:S(2)}, u32[]{:S(2)}) %collective-permute-start.7) | collective-permute-done | bytes 16416 | tf_op jit(solution)/shard_map/ppermute | solution.py:19
  30.0 1.5 %collective-permute-start.8 = (f32[8,512]{1,0:T(8,128)S(1)}, f32[8,512]{1,0:T(8,128)S(1)}, u32[]{:S(2)}, u32[]{:S(2)}) collective-permute-start(f32[8,512]{1,0:T(8,128)S(1)} %add.23), channel_id=1, source_target_pairs={{0,2},{1,3},{2,0},{3,1},{4,6},{5,7},{6,4},{7,5},{8,10},{9,11},{10,... | collective-permute-start | bytes 49160 | tf_op jit(solution)/shard_map/ppermute | solution.py:19
  31.5 2.2 %collective-permute-done.8 = f32[8,512]{1,0:T(8,128)S(1)} collective-permute-done((f32[8,512]{1,0:T(8,128)S(1)}, f32[8,512]{1,0:T(8,128)S(1)}, u32[]{:S(2)}, u32[]{:S(2)}) %collective-permute-start.8) | collective-permute-done | bytes 16416 | tf_op jit(solution)/shard_map/ppermute | solution.py:19
  33.7 0.6 %add.24 = f32[8,512]{1,0:T(8,128)} add(f32[8,512]{1,0:T(8,128)S(1)} %add.23, f32[8,512]{1,0:T(8,128)S(1)} %collective-permute-done.8) | non-fusion elementwise | flops 4096 | bytes 49152 | tf_op jit(solution)/shard_map/add | solution.py:229
  (6 shorter events, 0.1 us)
Async XLA Ops:
  1.0 11.4 %collective-permute-start = (bf16[128,1024]{1,0:T(8,128)(2,1)S(1)}, bf16[128,1024]{1,0:T(8,128)(2,1)S(1)}, u32[]{:S(2)}, u32[]{:S(2)}) collective-permute-start(bf16[128,1024]{1,0:T(8,128)(2,1)S(1)} %shard_map.64.refs_0_.refs_1_), channel_id=1, source_target_pairs={{0,4},{4,8},{8,12},{12,0},{1,5},{5,9},{9,13},{13,1},{2,6},{6,10},{... | collective-permute-start | bytes 786440 | tf_op jit(solution)/shard_map/ppermute | solution.py:195
  12.4 2.2 %collective-permute-start.1 = (f32[4,128,256]{2,1,0:T(8,128)S(1)}, f32[4,128,256]{2,1,0:T(8,128)S(1)}, u32[]{:S(2)}, u32[]{:S(2)}) collective-permute-start(f32[4,128,256]{2,1,0:T(8,128)S(1)} %broadcast_add_fusion), channel_id=1, source_target_pairs={{0,1},{1,0},{2,3},{3,2},{4,5},{5,4},{6,7},{7,6},{8,9},{9,8},{10,11... | collective-permute-start | bytes 1572872 | tf_op jit(solution)/shard_map/ppermute | solution.py:19
  12.5 13.6 %collective-permute-start.6 = (bf16[128,1024]{1,0:T(8,128)(2,1)S(1)}, bf16[128,1024]{1,0:T(8,128)(2,1)S(1)}, u32[]{:S(2)}, u32[]{:S(2)}) collective-permute-start(bf16[128,1024]{1,0:T(8,128)(2,1)S(1)} %shard_map.64.refs_0_.refs_1_), channel_id=1, source_target_pairs={{0,12},{4,0},{8,4},{12,8},{1,13},{5,1},{9,5},{13,9},{2,14},{6,2},{... | collective-permute-start | bytes 786440 | tf_op jit(solution)/shard_map/ppermute | solution.py:195
  14.3 13.6 %collective-permute-start.5 = (bf16[128,1024]{1,0:T(8,128)(2,1)S(1)}, bf16[128,1024]{1,0:T(8,128)(2,1)S(1)}, u32[]{:S(2)}, u32[]{:S(2)}) collective-permute-start(bf16[128,1024]{1,0:T(8,128)(2,1)S(1)} %collective-permute-done.refs_2_), channel_id=1, source_target_pairs={{0,4},{4,8},{8,12},{12,0},{1,5},{5,9},{9,13},{13,1},{2,6},{6,10},{... | collective-permute-start | bytes 786440 | tf_op jit(solution)/shard_map/ppermute | solution.py:195
  14.6 8.2 %collective-permute-start.2 = (f32[2,128,256]{2,1,0:T(8,128)S(1)}, f32[2,128,256]{2,1,0:T(8,128)S(1)}, u32[]{:S(2)}, u32[]{:S(2)}) collective-permute-start(f32[2,128,256]{2,1,0:T(8,128)S(1)} %get-tuple-element.14.refs_0_), channel_id=1, source_target_pairs={{0,2},{1,3},{2,0},{3,1},{4,6},{5,7},{6,4},{7,5},{8,10},{9,11},{10,... | collective-permute-start | bytes 786440 | tf_op jit(solution)/shard_map/ppermute | solution.py:19
  23.4 1.2 %collective-permute-start.3 = (f32[2,2,8,128]{3,2,1,0:T(8,128)S(1)}, f32[2,2,8,128]{3,2,1,0:T(8,128)S(1)}, u32[]{:S(2)}, u32[]{:S(2)}) collective-permute-start(f32[2,2,8,128]{3,2,1,0:T(8,128)S(1)} %get-tuple-element.12), channel_id=1, source_target_pairs={{0,1},{1,0},{2,3},{3,2},{4,5},{5,4},{6,7},{7,6},{8,9},{9,8},{10,11... | collective-permute-start | bytes 49160 | tf_op jit(solution)/shard_map/ppermute | solution.py:19
  24.6 3.7 %collective-permute-start.4 = (f32[2,2,8,128]{3,2,1,0:T(8,128)S(1)}, f32[2,2,8,128]{3,2,1,0:T(8,128)S(1)}, u32[]{:S(2)}, u32[]{:S(2)}) collective-permute-start(f32[2,2,8,128]{3,2,1,0:T(8,128)S(1)} %pad_maximum_fusion), channel_id=1, source_target_pairs={{0,2},{1,3},{2,0},{3,1},{4,6},{5,7},{6,4},{7,5},{8,10},{9,11},{10,... | collective-permute-start | bytes 49160 | tf_op jit(solution)/shard_map/ppermute | solution.py:19
  28.8 1.2 %collective-permute-start.7 = (f32[8,512]{1,0:T(8,128)S(1)}, f32[8,512]{1,0:T(8,128)S(1)}, u32[]{:S(2)}, u32[]{:S(2)}) collective-permute-start(f32[8,512]{1,0:T(8,128)S(1)} %shard_map.68), channel_id=1, source_target_pairs={{0,1},{1,0},{2,3},{3,2},{4,5},{5,4},{6,7},{7,6},{8,9},{9,8},{10,11... | collective-permute-start | bytes 49160 | tf_op jit(solution)/shard_map/ppermute | solution.py:19
  30.0 3.7 %collective-permute-start.8 = (f32[8,512]{1,0:T(8,128)S(1)}, f32[8,512]{1,0:T(8,128)S(1)}, u32[]{:S(2)}, u32[]{:S(2)}) collective-permute-start(f32[8,512]{1,0:T(8,128)S(1)} %add.23), channel_id=1, source_target_pairs={{0,2},{1,3},{2,0},{3,1},{4,6},{5,7},{6,4},{7,5},{8,10},{9,11},{10,... | collective-permute-start | bytes 49160 | tf_op jit(solution)/shard_map/ppermute | solution.py:19

commit v9 on v5

--- a/solution.py
+++ b/solution.py
@@ -8,8 +8,6 @@
 from jax.sharding import PartitionSpec as P
 
 CORES = 2
-PIECE = 512
-AHEAD = 4
 SMALL = pltpu.CompilerParams(vmem_limit_bytes=8 << 20)
 NT = (((1,), (1,)), ((), ()))
 HBM = pl.BlockSpec(memory_space=pltpu.HBM)
@@ -44,89 +42,85 @@
 COST = 1 << 32
 
 
-def project_kernel(steps, share, rows_first, after, act, og, wi, wo, lens, *refs):
+def cut(total, piece, last):
+    ends = list(range(piece, total - last + 1, piece))
+    ends += [total - last] if total - last > 0 and (not ends or ends[-1] < total - last) else []
+    ends += [total]
+    return [slice(start, end) for start, end in zip([0] + ends[:-1], ends)]
+
+
+def project_kernel(seqs, share, ahead, pieces, after, act, og, wi, wo, lens, *refs):
     refs = refs[after:]
     outs, (buf, wibuf, wobuf, lenbuf, sem, wsem) = refs[:-6], refs[-6:]
     me = lax.axis_index("tensor")
     rank = wibuf.shape[0]
-    slots = buf.shape[2]
-    count = len(steps) * share
-    tokens = count * slots
+    count, slots = buf.shape[1:3]
+    places = [(me ^ step) * share + k for step, k in seqs]
     small = [
         pltpu.make_async_copy(wi, wibuf, wsem.at[0]),
         pltpu.make_async_copy(wo, wobuf, wsem.at[1]),
         pltpu.make_async_copy(lens, lenbuf, wsem.at[2]),
     ]
-    pieces = [(side, at) for side, ref in enumerate((act, og)) for at in range(0, ref.shape[2], PIECE)]
-    copies = []
-    for slot, (side, at) in enumerate(pieces):
-        width = min(PIECE, (act, og)[side].shape[2] - at)
-        copies.append(
-            [
-                pltpu.make_async_copy(
-                    (act, og)[side].at[pl.ds((me ^ step) * share, share), :, pl.ds(at, width)],
-                    buf.at[slot, pl.ds(i * share, share), :, pl.ds(0, width)],
-                    sem.at[slot, i],
-                )
-                for i, step in enumerate(steps)
-            ]
-        )
+    copies = [
+        [
+            pltpu.make_async_copy(
+                (act, og)[side].at[place, :, pl.ds(span.start, span.stop - span.start)],
+                buf.at[slot, i, :, pl.ds(0, span.stop - span.start)],
+                sem.at[slot, i],
+            )
+            for i, place in enumerate(places)
+        ]
+        for slot, (side, span) in enumerate(pieces)
+    ]
     small[0].start()
-    for slot, group in enumerate(copies):
-        if slot == 1:
+    for slot, group in enumerate(copies[:ahead]):
+        for copy in group:
+            copy.start()
+        if slot == 0:
             small[1].start()
             small[2].start()
-        if slot < AHEAD:
-            for copy in group:
-                copy.start()
     sums = [None, None]
-    for slot, (side, at) in enumerate(pieces):
-        if at == 0:
+    for slot, (side, span) in enumerate(pieces):
+        if span.start == 0:
             small[side].wait()
         for copy in copies[slot]:
             copy.wait()
-        if slot + AHEAD < len(pieces):
-            for copy in copies[slot + AHEAD]:
-                copy.start()
-        weight = (wibuf, wobuf)[side][:, at : at + PIECE]
-        token = buf[slot].reshape(tokens, PIECE)[:, : weight.shape[1]]
-        pair = (token, weight) if rows_first else (weight, token)
-        part = lax.dot_general(*pair, NT, preferred_element_type=jnp.float32)
+        for copy in copies[slot + ahead] if slot + ahead < len(copies) else ():
+            copy.start()
+        token = buf[slot].reshape(count * slots, buf.shape[3])[:, : span.stop - span.start]
+        part = lax.dot_general((wibuf, wobuf)[side][:, span], token, NT, preferred_element_type=jnp.float32)
         sums[side] = part if sums[side] is None else sums[side] + part
-    if rows_first:
-        sums = [one.T for one in sums]
     small[2].wait()
     col = lax.broadcasted_iota(jnp.int32, (rank, slots), 1)
-    per = count // len(outs)
-    for slot in range(count):
-        length = lenbuf[(me ^ steps[slot // share]) * share + slot % share]
-        out = outs[slot // per]
+    rows = [out.at[i] for out in outs for i in range(out.shape[0])]
+    for slot, (row, place) in enumerate(zip(rows, places)):
+        length = lenbuf[place]
         one = sums[0][:, slot * slots : (slot + 1) * slots] * (1.0 / length.astype(jnp.float32))
-        out[slot % per, :rank] = jnp.where(col < length, one, 0.0)
-        out[slot % per, rank:] = sums[1][:, slot * slots : (slot + 1) * slots]
-
-
-def project(act, og, wi, wo, lens, groups, share, rows_first, cost, after=()):
-    steps = [step for group in groups for step in group]
-    count = len(steps) * share
+        row[:rank] = jnp.where(col < length, one, 0.0)
+        row[rank:] = sums[1][:, slot * slots : (slot + 1) * slots]
+
+
+def project(act, og, wi, wo, lens, groups, share, ahead, piece, after=()):
+    seqs = [seq for group in groups for seq in group]
+    count = len(seqs)
     slots, feat, hidden = act.shape[1], act.shape[2], og.shape[2]
     rank = wi.shape[0]
-    pieces = -(-feat // PIECE) - (-hidden // PIECE)
-    return pl.pallas_call(
-        functools.partial(project_kernel, steps, share, rows_first, len(after)),
-        out_shape=[jax.ShapeDtypeStruct((len(group) * share, 2 * rank, slots), jnp.float32) for group in groups],
+    pieces = [(0, span) for span in cut(feat, 512, 512)] + [(1, span) for span in cut(hidden, piece, 256)]
+    return pl.pallas_call(
+        functools.partial(project_kernel, seqs, share, ahead, pieces, len(after)),
+        out_shape=[jax.ShapeDtypeStruct((len(group), 2 * rank, slots), jnp.float32) for group in groups],
         in_specs=[HBM] * 5 + [VMEM] * len(after),
         out_specs=[VMEM] * len(groups),
         scratch_shapes=[
-            pltpu.VMEM((pieces, count, slots, PIECE), act.dtype),
+            pltpu.VMEM((len(pieces), count, slots, max(piece, 512)), act.dtype),
             pltpu.VMEM((rank, feat), wi.dtype),
             pltpu.VMEM((rank, hidden), wo.dtype),
             pltpu.SMEM(lens.shape, lens.dtype),
-            pltpu.SemaphoreType.DMA((pieces, len(steps))),
+            pltpu.SemaphoreType.DMA((len(pieces), count)),
             pltpu.SemaphoreType.DMA((3,)),
         ],
         compiler_params=pltpu.CompilerParams(vmem_limit_bytes=32 << 20),
-        cost_estimate=pl.CostEstimate(flops=cost, bytes_accessed=cost // 256, transcendentals=0),
+        cost_estimate=pl.CostEstimate(flops=COST, bytes_accessed=COST // 256, transcendentals=0),
     )(*map(in_hbm, (act, og, wi, wo, lens)), *after)
 
 
@@ -205,21 +199,29 @@
     rank = proj_in.shape[1]
     share = activations.shape[0] // size
     own_tests = cut_tests(test_grads, size)
-    tests = {0: own_tests, 1: shift(own_tests, "dp", groups, 1)}
+    tests = {0: own_tests, -1: shift(own_tests, "dp", groups, -1)}
     if groups == 4:
-        tests[3] = shift(own_tests, "dp", groups, 3)
-        tests[2] = shift(tests[1], "dp", groups, 1)
+        tests[-2] = shift(tests[-1], "dp", groups, -1)
+        tests[1] = shift(own_tests, "dp", groups, 1)
     else:
-        tests.update({step: shift(own_tests, "dp", groups, step) for step in range(2, groups)})
+        tests.update({-step: shift(own_tests, "dp", groups, -step) for step in range(2, groups)})
 
     far = [CORES * x for x in range(1, size // CORES)]
     arrays = (activations, out_grads, proj_in.T, proj_out.T, lengths)
-    far_other, far_own = project(*arrays, [[step ^ 1 for step in far], far], share, False, COST, [own_tests])
-    far_sum = far_own + xor_permute(far_other, "tensor", size, 1)
+    here = range(share)
+    early, late = here[: share // 2], here[share // 2 :]
+    sends = [[(step ^ 1, k) for step in far for k in here] + [(1, k) for k in early], [(step, k) for step in far for k in here]]
+    other, far_own = project(*arrays, sends, share, 3, 896, [own_tests])
+    other = other + 0.0 * tests[-1][:1, : other.shape[2]].astype(jnp.float32)
+    arrived = xor_permute(other, "tensor", size, 1)
+    split = len(far) * share
+    far_sum = far_own + arrived[:split]
     sums = [xor_permute(far_sum[i * share : (i + 1) * share], "tensor", size, step) for i, step in enumerate(far)]
-    near_other, near_own = project(*arrays, [[1], [0]], share, True, COST, [far_sum])
-    arrived = [xor_permute(near_other[k : k + 1], "tensor", size, 1) for k in range(share)]
-    unit_outs = units([near_own] + sums, arrived, share, rank, size)
+    near_other, near_own = project(*arrays, [[(1, k) for k in late], [(0, k) for k in here]], share, 3, 896, [far_sum])
+    last = xor_permute(near_other, "tensor", size, 1)
+    singles = [arrived[split + k : split + k + 1] for k in early] + [last[k : k + 1] for k in range(len(late))]
+
+    unit_outs = units([near_own] + sums, singles, share, rank, size)
     unit_parts = [unit_outs[0]] + [xor_permute(unit_outs[step], "tensor", size, step) for step in range(1, size)]
     part = score(unit_parts, tests, share)
     parts = [part] + [xor_permute(part, "tensor", size, step) for step in range(1, size)]

time: 35.7 us -> 36.1 us (1.011)
  starting transfers between devices: 11.4 us -> 14.8 us
  waiting for transfers between devices: 8.98 us -> 5.92 us
    ppermute x3, waiting for transfers between devices: 5.58 us -> 0.01 us  [shift(): lax.ppermute(value, axis, [(i, (i + step) % size) for i in range(size)])]
    ppermute x3, starting transfers between devices: 4.81 us -> 8.97 us  [shift(): lax.ppermute(value, axis, [(i, (i + step) % size) for i in range(size)])]
    ppermute x10 -> x9, waiting for transfers between devices: 3.4 us -> 5.91 us  [xor_permute(): return lax.ppermute(value, axis, [(i, i ^ step) for i in range(size)])]
    ppermute x10 -> x9, starting transfers between devices: 6.58 us -> 5.78 us  [xor_permute(): return lax.ppermute(value, axis, [(i, i ^ step) for i in range(size)])]
  transfers between devices with their start and end apart: 13 -> 12, of which waited for: 5 -> 5; matrix products, arithmetic and copies ran while one was open for 0% -> 0% of each run, Pallas kernels for 22% -> 37%
where the time goes in v9:
time: 36.1 us; the launch traced here: 36 us
  starting transfers between devices  14.8 us (41%)
  Pallas kernels  14.5 us (40%)
  waiting for transfers between devices  5.92 us (16%)
  other arithmetic  0.68 us (2%)
    pallas_call x2, Pallas kernels, project(): pl.pallas_call(functools.partial(project_kernel, seqs, share, ahead, piec...  12.6 us
    ppermute x3, starting transfers between devices, shift(): lax.ppermute(value, axis, [(i, (i + step) % size) for i in range(size)])  8.97 us
    ppermute x9, waiting for transfers between devices, xor_permute(): return lax.ppermute(value, axis, [(i, i ^ step) for i in range(size)])  5.91 us
    ppermute x9, starting transfers between devices, xor_permute(): return lax.ppermute(value, axis, [(i, i ^ step) for i in range(size)])  5.78 us
    pallas_call x1, Pallas kernels, cut_tests(): pl.pallas_call(cut_kernel, out_shape=jax.ShapeDtypeStruct((rows, width //...  0.96 us
  transfers between devices with their start and end apart: 12, of which 5 were waited for; matrix products, arithmetic and copies ran while one was open for 0% of the time, Pallas kernels for 37%

profile of v9, /device:TPU:0, one launch (start us, length us, event | category | flops | bytes accessed | tf_op | source)
XLA Modules:
  0.0 36.0 jit_solution(12175656735861525547)
XLA Ops:
  0.0 1.0 %shard_map.64.refs_0_.refs_4_ = bf16[128,1024]{1,0:T(8,128)(2,1)S(1)} custom-call(bf16[128,4096]{1,0:T(8,128)(2,1)} %tests.1), custom_call_target="tpu_custom_call" | custom-call | tf_op jit(solution)/shard_map/pallas_call | solution.py:32
  1.0 5.1 %collective-permute-start = (bf16[128,1024]{1,0:T(8,128)(2,1)S(1)}, bf16[128,1024]{1,0:T(8,128)(2,1)S(1)}, u32[]{:S(2)}, u32[]{:S(2)}) collective-permute-start(bf16[128,1024]{1,0:T(8,128)(2,1)S(1)} %shard_map.64.refs_0_.refs_4_), channel_id=1, source_target_pairs={{0,12},{4,0},{8,4},{12,8},{1,13},{5,1},{9,5},{13,9},{2,14},{6,2},{... | collective-permute-start | bytes 786440 | tf_op jit(solution)/shard_map/ppermute | solution.py:195
  6.1 7.4 %shard_map.65 = (f32[3,128,256]{2,1,0:T(8,128)S(1)}, f32[2,128,256]{2,1,0:T(8,128)S(1)}) custom-call(bf16[8,256,1024]{2,1,0:T(8,128)(2,1)} %act.3, bf16[8,256,3584]{2,1,0:T(8,128)(2,1)} %og.3, bf16[64,1024]{1,0:T(8,128)(2,1)} %bitcast.5, bf16[64,3584]{1,0:T(8,128)(2,1)} %bitcast.3, s32[8]{0:T(128)} %lens.3, bf16[128,1024]{1,0:T(8,128)(2,1)S(1)} %shard_map.64.refs_0_.refs_4_), custom_call_target="tpu_custom_call" | custom-call | flops 4294967296 | bytes 16777216 | tf_op jit(solution)/shard_map/pallas_call | solution.py:109
  13.5 0.0 collective-permute-done.refs_5_
  13.5 0.1 collective-permute-start.1
  13.6 0.1 collective-permute-start.8
  13.7 3.8 %collective-permute-start.7 = (bf16[128,1024]{1,0:T(8,128)(2,1)S(1)}, bf16[128,1024]{1,0:T(8,128)(2,1)S(1)}, u32[]{:S(2)}, u32[]{:S(2)}) collective-permute-start(bf16[128,1024]{1,0:T(8,128)(2,1)S(1)} %collective-permute-done.refs_5_), channel_id=1, source_target_pairs={{0,12},{4,0},{8,4},{12,8},{1,13},{5,1},{9,5},{13,9},{2,14},{6,2},{... | collective-permute-start | bytes 786440 | tf_op jit(solution)/shard_map/ppermute | solution.py:195
  17.5 0.0 collective-permute-done.1
  17.5 1.6 %collective-permute-start.3 = (f32[2,128,256]{2,1,0:T(8,128)S(1)}, f32[2,128,256]{2,1,0:T(8,128)S(1)}, u32[]{:S(2)}, u32[]{:S(2)}) collective-permute-start(f32[2,128,256]{2,1,0:T(8,128)S(1)} %slice_add_fusion.refs_0_), channel_id=1, source_target_pairs={{0,2},{1,3},{2,0},{3,1},{4,6},{5,7},{6,4},{7,5},{8,10},{9,11},{10,... | collective-permute-start | bytes 786440 | tf_op jit(solution)/shard_map/ppermute | solution.py:19
  19.1 5.2 %shard_map.66 = (f32[1,128,256]{2,1,0:T(8,128)S(1)}, f32[2,128,256]{2,1,0:T(8,128)S(1)}) custom-call(bf16[8,256,1024]{2,1,0:T(8,128)(2,1)} %act.3, bf16[8,256,3584]{2,1,0:T(8,128)(2,1)} %og.3, bf16[64,1024]{1,0:T(8,128)(2,1)} %bitcast.6, bf16[64,3584]{1,0:T(8,128)(2,1)} %bitcast.4, s32[8]{0:T(128)} %lens.3, f32[2,128,256]{2,1,0:T(8,128)S(1)} %slice_add_fusion.refs_0_), custom_call_target="tpu_custom_call" | custom-call | flops 4294967296 | bytes 16777216 | tf_op jit(solution)/shard_map/pallas_call | solution.py:109
  24.3 0.1 collective-permute-start.2
  24.4 1.3 %collective-permute-done.2.refs_1_ = f32[1,128,256]{2,1,0:T(8,128)S(1)} collective-permute-done((f32[1,128,256]{2,1,0:T(8,128)S(1)}, f32[1,128,256]{2,1,0:T(8,128)S(1)}, u32[]{:S(2)}, u32[]{:S(2)}) %collective-permute-start.2) | collective-permute-done | bytes 131104 | tf_op jit(solution)/shard_map/ppermute | solution.py:19
  25.8 0.0 collective-permute-done.3.refs_3_
  25.8 0.5 %shard_map.67 = (f32[2,8,128]{2,1,0:T(8,128)S(1)}, f32[2,8,128]{2,1,0:T(8,128)S(1)}, f32[2,8,128]{2,1,0:T(8,128)S(1)}, f32[2,8,128]{2,1,0:T(8,128)S(1)}) custom-call(f32[1,128,256]{2,1,0:T(8,128)S(1)} %slice.13.refs_0_, f32[1,128,256]{2,1,0:T(8,128)S(1)} %collective-permute-done.2.refs_1_, f32[2,128,256]{2,1,0:T(8,128)S(1)} %get-tuple-element.16.refs_2_, ...), custom_call_target="tpu_custom_call" | custom-call | tf_op jit(solution)/shard_map/pallas_call | solution.py:156
  26.3 0.2 collective-permute-start.4
  26.5 1.4 %collective-permute-start.5 = (f32[2,8,128]{2,1,0:T(8,128)S(1)}, f32[2,8,128]{2,1,0:T(8,128)S(1)}, u32[]{:S(2)}, u32[]{:S(2)}) collective-permute-start(f32[2,8,128]{2,1,0:T(8,128)S(1)} %get-tuple-element.19), channel_id=1, source_target_pairs={{0,2},{1,3},{2,0},{3,1},{4,6},{5,7},{6,4},{7,5},{8,10},{9,11},{10,... | collective-permute-start | bytes 24584 | tf_op jit(solution)/shard_map/ppermute | solution.py:19
  27.9 0.3 collective-permute-start.6
  28.2 0.0 collective-permute-done.8.refs_7_
  28.2 0.0 collective-permute-done.7.refs_6_
  28.2 0.0 collective-permute-done.4.refs_1_
  28.2 1.9 %collective-permute-done.5.refs_2_ = f32[2,8,128]{2,1,0:T(8,128)S(1)} collective-permute-done((f32[2,8,128]{2,1,0:T(8,128)S(1)}, f32[2,8,128]{2,1,0:T(8,128)S(1)}, u32[]{:S(2)}, u32[]{:S(2)}) %collective-permute-start.5) | collective-permute-done | bytes 8224 | tf_op jit(solution)/shard_map/ppermute | solution.py:19
  30.2 0.8 %collective-permute-done.6.refs_3_ = f32[2,8,128]{2,1,0:T(8,128)S(1)} collective-permute-done((f32[2,8,128]{2,1,0:T(8,128)S(1)}, f32[2,8,128]{2,1,0:T(8,128)S(1)}, u32[]{:S(2)}, u32[]{:S(2)}) %collective-permute-start.6) | collective-permute-done | bytes 8224 | tf_op jit(solution)/shard_map/ppermute | solution.py:19
  30.9 0.4 %shard_map.68 = f32[8,512]{1,0:T(8,128)S(1)} custom-call(f32[2,8,128]{2,1,0:T(8,128)S(1)} %get-tuple-element.17.refs_0_, f32[2,8,128]{2,1,0:T(8,128)S(1)} %collective-permute-done.4.refs_1_, f32[2,8,128]{2,1,0:T(8,128)S(1)} %collective-permute-done.5.refs_2_, f32[2,8,128]{2,1,0:T(8,128)S(1)} %collective-permute-done.6.refs_3_, ...), custom_call_target="tpu_custom_call" | custom-call | tf_op jit(solution)/shard_map/pallas_call | solution.py:184
  31.3 0.7 %collective-permute-start.10 = (f32[8,512]{1,0:T(8,128)S(1)}, f32[8,512]{1,0:T(8,128)S(1)}, u32[]{:S(2)}, u32[]{:S(2)}) collective-permute-start(f32[8,512]{1,0:T(8,128)S(1)} %shard_map.68), channel_id=1, source_target_pairs={{0,2},{1,3},{2,0},{3,1},{4,6},{5,7},{6,4},{7,5},{8,10},{9,11},{10,... | collective-permute-start | bytes 49160 | tf_op jit(solution)/shard_map/ppermute | solution.py:19
  32.0 0.8 %collective-permute-start.11 = (f32[8,512]{1,0:T(8,128)S(1)}, f32[8,512]{1,0:T(8,128)S(1)}, u32[]{:S(2)}, u32[]{:S(2)}) collective-permute-start(f32[8,512]{1,0:T(8,128)S(1)} %shard_map.68), channel_id=1, source_target_pairs={{0,3},{1,2},{2,1},{3,0},{4,7},{5,6},{6,5},{7,4},{8,11},{9,10},{10,... | collective-permute-start | bytes 49160 | tf_op jit(solution)/shard_map/ppermute | solution.py:19
  32.8 0.6 %collective-permute-start.9 = (f32[8,512]{1,0:T(8,128)S(1)}, f32[8,512]{1,0:T(8,128)S(1)}, u32[]{:S(2)}, u32[]{:S(2)}) collective-permute-start(f32[8,512]{1,0:T(8,128)S(1)} %shard_map.68), channel_id=1, source_target_pairs={{0,1},{1,0},{2,3},{3,2},{4,5},{5,4},{6,7},{7,6},{8,9},{9,8},{10,11... | collective-permute-start | bytes 49160 | tf_op jit(solution)/shard_map/ppermute | solution.py:19
  33.5 1.7 %collective-permute-done.10 = f32[8,512]{1,0:T(8,128)S(1)} collective-permute-done((f32[8,512]{1,0:T(8,128)S(1)}, f32[8,512]{1,0:T(8,128)S(1)}, u32[]{:S(2)}, u32[]{:S(2)}) %collective-permute-start.10) | collective-permute-done | bytes 16416 | tf_op jit(solution)/shard_map/ppermute | solution.py:19
  35.1 0.2 collective-permute-done.11
  35.3 0.0 collective-permute-done.9
  35.3 0.6 %add_add_fusion = f32[8,512]{1,0:T(8,128)} fusion(f32[8,512]{1,0:T(8,128)S(1)} %collective-permute-done.10, f32[8,512]{1,0:T(8,128)S(1)} %collective-permute-done.11, f32[8,512]{1,0:T(8,128)S(1)} %shard_map.68, f32[8,512]{1,0:T(8,128)S(1)} %collective-permute-done.9), kind=kLoop, calls=%fused_computation.2 | loop fusion | flops 12288 | bytes 81920 | tf_op jit(solution)/shard_map/add | solution.py:229
  (4 shorter events, 0.1 us)
Async XLA Ops:
  1.0 12.5 %collective-permute-start = (bf16[128,1024]{1,0:T(8,128)(2,1)S(1)}, bf16[128,1024]{1,0:T(8,128)(2,1)S(1)}, u32[]{:S(2)}, u32[]{:S(2)}) collective-permute-start(bf16[128,1024]{1,0:T(8,128)(2,1)S(1)} %shard_map.64.refs_0_.refs_4_), channel_id=1, source_target_pairs={{0,12},{4,0},{8,4},{12,8},{1,13},{5,1},{9,5},{13,9},{2,14},{6,2},{... | collective-permute-start | bytes 786440 | tf_op jit(solution)/shard_map/ppermute | solution.py:195
  13.5 4.0 %collective-permute-start.1 = (f32[3,128,256]{2,1,0:T(8,128)S(1)}, f32[3,128,256]{2,1,0:T(8,128)S(1)}, u32[]{:S(2)}, u32[]{:S(2)}) collective-permute-start(f32[3,128,256]{2,1,0:T(8,128)S(1)} %broadcast_add_fusion), channel_id=1, source_target_pairs={{0,1},{1,0},{2,3},{3,2},{4,5},{5,4},{6,7},{7,6},{8,9},{9,8},{10,11... | collective-permute-start | bytes 1179656 | tf_op jit(solution)/shard_map/ppermute | solution.py:19
  13.6 14.6 %collective-permute-start.8 = (bf16[128,1024]{1,0:T(8,128)(2,1)S(1)}, bf16[128,1024]{1,0:T(8,128)(2,1)S(1)}, u32[]{:S(2)}, u32[]{:S(2)}) collective-permute-start(bf16[128,1024]{1,0:T(8,128)(2,1)S(1)} %shard_map.64.refs_0_.refs_4_), channel_id=1, source_target_pairs={{0,4},{4,8},{8,12},{12,0},{1,5},{5,9},{9,13},{13,1},{2,6},{6,10},{... | collective-permute-start | bytes 786440 | tf_op jit(solution)/shard_map/ppermute | solution.py:195
  13.7 14.5 %collective-permute-start.7 = (bf16[128,1024]{1,0:T(8,128)(2,1)S(1)}, bf16[128,1024]{1,0:T(8,128)(2,1)S(1)}, u32[]{:S(2)}, u32[]{:S(2)}) collective-permute-start(bf16[128,1024]{1,0:T(8,128)(2,1)S(1)} %collective-permute-done.refs_5_), channel_id=1, source_target_pairs={{0,12},{4,0},{8,4},{12,8},{1,13},{5,1},{9,5},{13,9},{2,14},{6,2},{... | collective-permute-start | bytes 786440 | tf_op jit(solution)/shard_map/ppermute | solution.py:195
  17.5 8.2 %collective-permute-start.3 = (f32[2,128,256]{2,1,0:T(8,128)S(1)}, f32[2,128,256]{2,1,0:T(8,128)S(1)}, u32[]{:S(2)}, u32[]{:S(2)}) collective-permute-start(f32[2,128,256]{2,1,0:T(8,128)S(1)} %slice_add_fusion.refs_0_), channel_id=1, source_target_pairs={{0,2},{1,3},{2,0},{3,1},{4,6},{5,7},{6,4},{7,5},{8,10},{9,11},{10,... | collective-permute-start | bytes 786440 | tf_op jit(solution)/shard_map/ppermute | solution.py:19
  24.3 1.4 %collective-permute-start.2 = (f32[1,128,256]{2,1,0:T(8,128)S(1)}, f32[1,128,256]{2,1,0:T(8,128)S(1)}, u32[]{:S(2)}, u32[]{:S(2)}) collective-permute-start(f32[1,128,256]{2,1,0:T(8,128)S(1)} %get-tuple-element.15), channel_id=1, source_target_pairs={{0,1},{1,0},{2,3},{3,2},{4,5},{5,4},{6,7},{7,6},{8,9},{9,8},{10,11... | collective-permute-start | bytes 393224 | tf_op jit(solution)/shard_map/ppermute | solution.py:19
  26.3 1.9 %collective-permute-start.4 = (f32[2,8,128]{2,1,0:T(8,128)S(1)}, f32[2,8,128]{2,1,0:T(8,128)S(1)}, u32[]{:S(2)}, u32[]{:S(2)}) collective-permute-start(f32[2,8,128]{2,1,0:T(8,128)S(1)} %get-tuple-element.18), channel_id=1, source_target_pairs={{0,1},{1,0},{2,3},{3,2},{4,5},{5,4},{6,7},{7,6},{8,9},{9,8},{10,11... | collective-permute-start | bytes 24584 | tf_op jit(solution)/shard_map/ppermute | solution.py:19
  26.5 3.7 %collective-permute-start.5 = (f32[2,8,128]{2,1,0:T(8,128)S(1)}, f32[2,8,128]{2,1,0:T(8,128)S(1)}, u32[]{:S(2)}, u32[]{:S(2)}) collective-permute-start(f32[2,8,128]{2,1,0:T(8,128)S(1)} %get-tuple-element.19), channel_id=1, source_target_pairs={{0,2},{1,3},{2,0},{3,1},{4,6},{5,7},{6,4},{7,5},{8,10},{9,11},{10,... | collective-permute-start | bytes 24584 | tf_op jit(solution)/shard_map/ppermute | solution.py:19
  27.9 3.1 %collective-permute-start.6 = (f32[2,8,128]{2,1,0:T(8,128)S(1)}, f32[2,8,128]{2,1,0:T(8,128)S(1)}, u32[]{:S(2)}, u32[]{:S(2)}) collective-permute-start(f32[2,8,128]{2,1,0:T(8,128)S(1)} %get-tuple-element.20), channel_id=1, source_target_pairs={{0,3},{1,2},{2,1},{3,0},{4,7},{5,6},{6,5},{7,4},{8,11},{9,10},{10,... | collective-permute-start | bytes 24584 | tf_op jit(solution)/shard_map/ppermute | solution.py:19
  31.3 3.8 %collective-permute-start.10 = (f32[8,512]{1,0:T(8,128)S(1)}, f32[8,512]{1,0:T(8,128)S(1)}, u32[]{:S(2)}, u32[]{:S(2)}) collective-permute-start(f32[8,512]{1,0:T(8,128)S(1)} %shard_map.68), channel_id=1, source_target_pairs={{0,2},{1,3},{2,0},{3,1},{4,6},{5,7},{6,4},{7,5},{8,10},{9,11},{10,... | collective-permute-start | bytes 49160 | tf_op jit(solution)/shard_map/ppermute | solution.py:19
  32.0 3.3 %collective-permute-start.11 = (f32[8,512]{1,0:T(8,128)S(1)}, f32[8,512]{1,0:T(8,128)S(1)}, u32[]{:S(2)}, u32[]{:S(2)}) collective-permute-start(f32[8,512]{1,0:T(8,128)S(1)} %shard_map.68), channel_id=1, source_target_pairs={{0,3},{1,2},{2,1},{3,0},{4,7},{5,6},{6,5},{7,4},{8,11},{9,10},{10,... | collective-permute-start | bytes 49160 | tf_op jit(solution)/shard_map/ppermute | solution.py:19
  32.8 2.5 %collective-permute-start.9 = (f32[8,512]{1,0:T(8,128)S(1)}, f32[8,512]{1,0:T(8,128)S(1)}, u32[]{:S(2)}, u32[]{:S(2)}) collective-permute-start(f32[8,512]{1,0:T(8,128)S(1)} %shard_map.68), channel_id=1, source_target_pairs={{0,1},{1,0},{2,3},{3,2},{4,5},{5,4},{6,7},{7,6},{8,9},{9,8},{10,11... | collective-permute-start | bytes 49160 | tf_op jit(solution)/shard_map/ppermute | solution.py:19

commit v10 on v9

--- a/solution.py
+++ b/solution.py
@@ -49,13 +49,14 @@
     return [slice(start, end) for start, end in zip([0] + ends[:-1], ends)]
 
 
-def project_kernel(seqs, share, ahead, pieces, after, act, og, wi, wo, lens, *refs):
+def project_kernel(steps, share, ahead, pieces, after, act, og, wi, wo, lens, *refs):
     refs = refs[after:]
     outs, (buf, wibuf, wobuf, lenbuf, sem, wsem) = refs[:-6], refs[-6:]
     me = lax.axis_index("tensor")
     rank = wibuf.shape[0]
-    count, slots = buf.shape[1:3]
-    places = [(me ^ step) * share + k for step, k in seqs]
+    slots = buf.shape[2]
+    count = len(steps) * share
+    tokens = count * slots
     small = [
         pltpu.make_async_copy(wi, wibuf, wsem.at[0]),
         pltpu.make_async_copy(wo, wobuf, wsem.at[1]),
@@ -64,11 +65,11 @@
     copies = [
         [
             pltpu.make_async_copy(
-                (act, og)[side].at[place, :, pl.ds(span.start, span.stop - span.start)],
-                buf.at[slot, i, :, pl.ds(0, span.stop - span.start)],
+                (act, og)[side].at[pl.ds((me ^ step) * share, share), :, pl.ds(span.start, span.stop - span.start)],
+                buf.at[slot, pl.ds(i * share, share), :, pl.ds(0, span.stop - span.start)],
                 sem.at[slot, i],
             )
-            for i, place in enumerate(places)
+            for i, step in enumerate(steps)
         ]
         for slot, (side, span) in enumerate(pieces)
     ]
@@ -87,36 +88,36 @@
             copy.wait()
         for copy in copies[slot + ahead] if slot + ahead < len(copies) else ():
             copy.start()
-        token = buf[slot].reshape(count * slots, buf.shape[3])[:, : span.stop - span.start]
+        token = buf[slot].reshape(tokens, buf.shape[3])[:, : span.stop - span.start]
         part = lax.dot_general((wibuf, wobuf)[side][:, span], token, NT, preferred_element_type=jnp.float32)
         sums[side] = part if sums[side] is None else sums[side] + part
     small[2].wait()
     col = lax.broadcasted_iota(jnp.int32, (rank, slots), 1)
-    rows = [out.at[i] for out in outs for i in range(out.shape[0])]
-    for slot, (row, place) in enumerate(zip(rows, places)):
-        length = lenbuf[place]
+    places = [out.at[i] for out in outs for i in range(out.shape[0])]
+    for slot, out in enumerate(places):
+        length = lenbuf[(me ^ steps[slot // share]) * share + slot % share]
         one = sums[0][:, slot * slots : (slot + 1) * slots] * (1.0 / length.astype(jnp.float32))
-        row[:rank] = jnp.where(col < length, one, 0.0)
-        row[rank:] = sums[1][:, slot * slots : (slot + 1) * slots]
+        out[:rank] = jnp.where(col < length, one, 0.0)
+        out[rank:] = sums[1][:, slot * slots : (slot + 1) * slots]
 
 
 def project(act, og, wi, wo, lens, groups, share, ahead, piece, after=()):
-    seqs = [seq for group in groups for seq in group]
-    count = len(seqs)
+    steps = [step for group in groups for step in group]
+    count = len(steps) * share
     slots, feat, hidden = act.shape[1], act.shape[2], og.shape[2]
     rank = wi.shape[0]
-    pieces = [(0, span) for span in cut(feat, 512, 512)] + [(1, span) for span in cut(hidden, piece, 256)]
-    return pl.pallas_call(
-        functools.partial(project_kernel, seqs, share, ahead, pieces, len(after)),
-        out_shape=[jax.ShapeDtypeStruct((len(group), 2 * rank, slots), jnp.float32) for group in groups],
+    pieces = [(0, span) for span in cut(feat, piece, piece)] + [(1, span) for span in cut(hidden, piece, 256)]
+    return pl.pallas_call(
+        functools.partial(project_kernel, steps, share, ahead, pieces, len(after)),
+        out_shape=[jax.ShapeDtypeStruct((len(group) * share, 2 * rank, slots), jnp.float32) for group in groups],
         in_specs=[HBM] * 5 + [VMEM] * len(after),
         out_specs=[VMEM] * len(groups),
         scratch_shapes=[
-            pltpu.VMEM((len(pieces), count, slots, max(piece, 512)), act.dtype),
+            pltpu.VMEM((len(pieces), count, slots, piece), act.dtype),
             pltpu.VMEM((rank, feat), wi.dtype),
             pltpu.VMEM((rank, hidden), wo.dtype),
             pltpu.SMEM(lens.shape, lens.dtype),
-            pltpu.SemaphoreType.DMA((len(pieces), count)),
+            pltpu.SemaphoreType.DMA((len(pieces), len(steps))),
             pltpu.SemaphoreType.DMA((3,)),
         ],
         compiler_params=pltpu.CompilerParams(vmem_limit_bytes=32 << 20),
@@ -125,15 +126,15 @@
 
 
 def unit_kernel(share, rank, size, *refs):
-    singles, parts, outs = refs[:share], refs[share : -2 - size], refs[-2 - size : -2]
+    parts, outs = refs[: -2 - size], refs[-2 - size : -2]
     pairs, held = refs[-2:]
     me = lax.axis_index("tensor")
     rows = rank * rank // 128
     span = rows // size
     dot = functools.partial(lax.dot_general, dimension_numbers=NT, preferred_element_type=jnp.float32)
     for k in range(share):
-        full = singles[k][0]
-        for part in parts:
+        full = parts[0][k]
+        for part in parts[1:]:
             full = full + part[k]
         high = full.astype(jnp.bfloat16)
         low = (full - high.astype(jnp.float32)).astype(jnp.bfloat16)
@@ -151,16 +152,16 @@
             outs[step][k] = held[me ^ step]
 
 
-def units(parts, singles, share, rank, size):
+def units(parts, share, rank, size):
     span = rank * rank // 128 // size
     return pl.pallas_call(
         functools.partial(unit_kernel, share, rank, size),
         out_shape=[jax.ShapeDtypeStruct((share, span, 128), jnp.float32)] * size,
-        in_specs=[VMEM] * (share + len(parts)),
+        in_specs=[VMEM] * len(parts),
         out_specs=[VMEM] * size,
         scratch_shapes=[pltpu.VMEM((share, rank, rank), jnp.float32), pltpu.VMEM((size, span, 128), jnp.float32)],
         compiler_params=SMALL,
-    )(*singles, *parts)
+    )(*parts)
 
 
 def score_kernel(share, size, shifts, *refs):
@@ -199,29 +200,25 @@
     rank = proj_in.shape[1]
     share = activations.shape[0] // size
     own_tests = cut_tests(test_grads, size)
-    tests = {0: own_tests, -1: shift(own_tests, "dp", groups, -1)}
+    tests = {0: own_tests, 1: shift(own_tests, "dp", groups, 1)}
     if groups == 4:
-        tests[-2] = shift(tests[-1], "dp", groups, -1)
-        tests[1] = shift(own_tests, "dp", groups, 1)
+        tests[2] = shift(tests[1], "dp", groups, 1)
+        tests[3] = shift(own_tests, "dp", groups, 3)
     else:
-        tests.update({-step: shift(own_tests, "dp", groups, -step) for step in range(2, groups)})
+        tests.update({step: shift(own_tests, "dp", groups, step) for step in range(2, groups)})
 
     far = [CORES * x for x in range(1, size // CORES)]
     arrays = (activations, out_grads, proj_in.T, proj_out.T, lengths)
-    here = range(share)
-    early, late = here[: share // 2], here[share // 2 :]
-    sends = [[(step ^ 1, k) for step in far for k in here] + [(1, k) for k in early], [(step, k) for step in far for k in here]]
-    other, far_own = project(*arrays, sends, share, 3, 896, [own_tests])
-    other = other + 0.0 * tests[-1][:1, : other.shape[2]].astype(jnp.float32)
+    sends = [[step ^ 1 for step in far] + [1], far]
+    other, far_own = project(*arrays, sends, share, 2, 512, [own_tests])
+    other = other + 0.0 * tests[1][:1, : other.shape[2]].astype(jnp.float32)
     arrived = xor_permute(other, "tensor", size, 1)
-    split = len(far) * share
-    far_sum = far_own + arrived[:split]
+    cut_at = len(far) * share
+    far_sum = far_own + arrived[:cut_at]
     sums = [xor_permute(far_sum[i * share : (i + 1) * share], "tensor", size, step) for i, step in enumerate(far)]
-    near_other, near_own = project(*arrays, [[(1, k) for k in late], [(0, k) for k in here]], share, 3, 896, [far_sum])
-    last = xor_permute(near_other, "tensor", size, 1)
-    singles = [arrived[split + k : split + k + 1] for k in early] + [last[k : k + 1] for k in range(len(late))]
-
-    unit_outs = units([near_own] + sums, singles, share, rank, size)
+    near_own = project(*arrays, [[0]], share, 4, 512, [far_sum])[0]
+
+    unit_outs = units([near_own, arrived[cut_at:]] + sums, share, rank, size)
     unit_parts = [unit_outs[0]] + [xor_permute(unit_outs[step], "tensor", size, step) for step in range(1, size)]
     part = score(unit_parts, tests, share)
     parts = [part] + [xor_permute(part, "tensor", size, step) for step in range(1, size)]

time: 36.1 us -> 35.7 us (0.989)
  starting transfers between devices: 14.8 us -> 11.1 us
  waiting for transfers between devices: 5.92 us -> 9.27 us
    ppermute x3, starting transfers between devices: 8.97 us -> 5.18 us  [shift(): lax.ppermute(value, axis, [(i, (i + step) % size) for i in range(size)])]
    ppermute x3, waiting for transfers between devices: 0.01 us -> 3.29 us  [shift(): lax.ppermute(value, axis, [(i, (i + step) % size) for i in range(size)])]
    ppermute x9 -> x8, starting transfers between devices: 5.78 us -> 5.92 us  [xor_permute(): return lax.ppermute(value, axis, [(i, i ^ step) for i in range(size)])]
    ppermute x9 -> x8, waiting for transfers between devices: 5.91 us -> 5.98 us  [xor_permute(): return lax.ppermute(value, axis, [(i, i ^ step) for i in range(size)])]
  transfers between devices with their start and end apart: 12 -> 11, of which waited for: 5 -> 4; matrix products, arithmetic and copies ran while one was open for 0% -> 0% of each run, Pallas kernels for 37% -> 36%
where the time goes in v10:
time: 35.7 us; the launch traced here: 35.4 us
  Pallas kernels  14.2 us (40%)
  starting transfers between devices  11.1 us (31%)
  waiting for transfers between devices  9.27 us (26%)
  other arithmetic  0.71 us (2%)
    pallas_call x2, Pallas kernels, project(): pl.pallas_call(functools.partial(project_kernel, steps, share, ahead, pie...  12.4 us
    ppermute x8, waiting for transfers between devices, xor_permute(): return lax.ppermute(value, axis, [(i, i ^ step) for i in range(size)])  5.98 us
    ppermute x8, starting transfers between devices, xor_permute(): return lax.ppermute(value, axis, [(i, i ^ step) for i in range(size)])  5.92 us
    ppermute x3, starting transfers between devices, shift(): lax.ppermute(value, axis, [(i, (i + step) % size) for i in range(size)])  5.18 us
    ppermute x3, waiting for transfers between devices, shift(): lax.ppermute(value, axis, [(i, (i + step) % size) for i in range(size)])  3.29 us
    pallas_call x1, Pallas kernels, cut_tests(): pl.pallas_call(cut_kernel, out_shape=jax.ShapeDtypeStruct((rows, width //...  0.96 us
  transfers between devices with their start and end apart: 11, of which 4 were waited for; matrix products, arithmetic and copies ran while one was open for 0% of the time, Pallas kernels for 36%

profile of v10, /device:TPU:0, one launch (start us, length us, event | category | flops | bytes accessed | tf_op | source)
XLA Modules:
  0.0 35.4 jit_solution(17621291233849814141)
XLA Ops:
  0.0 1.0 %shard_map.64.refs_0_.refs_4_ = bf16[128,1024]{1,0:T(8,128)(2,1)S(1)} custom-call(bf16[128,4096]{1,0:T(8,128)(2,1)} %tests.1), custom_call_target="tpu_custom_call" | custom-call | tf_op jit(solution)/shard_map/pallas_call | solution.py:32
  1.0 3.1 %collective-permute-start = (bf16[128,1024]{1,0:T(8,128)(2,1)S(1)}, bf16[128,1024]{1,0:T(8,128)(2,1)S(1)}, u32[]{:S(2)}, u32[]{:S(2)}) collective-permute-start(bf16[128,1024]{1,0:T(8,128)(2,1)S(1)} %shard_map.64.refs_0_.refs_4_), channel_id=1, source_target_pairs={{0,4},{4,8},{8,12},{12,0},{1,5},{5,9},{9,13},{13,1},{2,6},{6,10},{... | collective-permute-start | bytes 786440 | tf_op jit(solution)/shard_map/ppermute | solution.py:196
  4.0 8.5 %shard_map.65 = (f32[4,128,256]{2,1,0:T(8,128)S(1)}, f32[2,128,256]{2,1,0:T(8,128)S(1)}) custom-call(bf16[8,256,1024]{2,1,0:T(8,128)(2,1)} %act.3, bf16[8,256,3584]{2,1,0:T(8,128)(2,1)} %og.3, bf16[64,1024]{1,0:T(8,128)(2,1)} %bitcast.5, bf16[64,3584]{1,0:T(8,128)(2,1)} %bitcast.3, s32[8]{0:T(128)} %lens.3, bf16[128,1024]{1,0:T(8,128)(2,1)S(1)} %shard_map.64.refs_0_.refs_4_), custom_call_target="tpu_custom_call" | custom-call | flops 4294967296 | bytes 16777216 | tf_op jit(solution)/shard_map/pallas_call | solution.py:110
  12.5 0.0 collective-permute-done.refs_5_
  12.6 0.1 collective-permute-start.1
  12.7 2.1 %collective-permute-start.7 = (bf16[128,1024]{1,0:T(8,128)(2,1)S(1)}, bf16[128,1024]{1,0:T(8,128)(2,1)S(1)}, u32[]{:S(2)}, u32[]{:S(2)}) collective-permute-start(bf16[128,1024]{1,0:T(8,128)(2,1)S(1)} %shard_map.64.refs_0_.refs_4_), channel_id=1, source_target_pairs={{0,12},{4,0},{8,4},{12,8},{1,13},{5,1},{9,5},{13,9},{2,14},{6,2},{... | collective-permute-start | bytes 786440 | tf_op jit(solution)/shard_map/ppermute | solution.py:196
  14.8 0.0 collective-permute-start.6
  14.8 0.0 collective-permute-done.1
  14.8 0.1 fusion.1
  14.8 1.8 %collective-permute-start.2 = (f32[2,128,256]{2,1,0:T(8,128)S(1)}, f32[2,128,256]{2,1,0:T(8,128)S(1)}, u32[]{:S(2)}, u32[]{:S(2)}) collective-permute-start(f32[2,128,256]{2,1,0:T(8,128)S(1)} %get-tuple-element.18.refs_0_), channel_id=1, source_target_pairs={{0,2},{1,3},{2,0},{3,1},{4,6},{5,7},{6,4},{7,5},{8,10},{9,11},{10,... | collective-permute-start | bytes 786440 | tf_op jit(solution)/shard_map/ppermute | solution.py:19
  16.6 3.9 %shard_map.66.refs_0_ = f32[2,128,256]{2,1,0:T(8,128)S(1)} custom-call(bf16[8,256,1024]{2,1,0:T(8,128)(2,1)} %act.3, bf16[8,256,3584]{2,1,0:T(8,128)(2,1)} %og.3, bf16[64,1024]{1,0:T(8,128)(2,1)} %bitcast.6, bf16[64,3584]{1,0:T(8,128)(2,1)} %bitcast.4, s32[8]{0:T(128)} %lens.3, f32[2,128,256]{2,1,0:T(8,128)S(1)} %get-tuple-element.18.refs_0_), custom_call_target="tpu_custom_call" | custom-call | flops 4294967296 | bytes 16777216 | tf_op jit(solution)/shard_map/pallas_call | solution.py:110
  20.5 2.8 %collective-permute-done.2.refs_2_ = f32[2,128,256]{2,1,0:T(8,128)S(1)} collective-permute-done((f32[2,128,256]{2,1,0:T(8,128)S(1)}, f32[2,128,256]{2,1,0:T(8,128)S(1)}, u32[]{:S(2)}, u32[]{:S(2)}) %collective-permute-start.2) | collective-permute-done | bytes 262176 | tf_op jit(solution)/shard_map/ppermute | solution.py:19
  23.3 0.5 %shard_map.67 = (f32[2,8,128]{2,1,0:T(8,128)S(1)}, f32[2,8,128]{2,1,0:T(8,128)S(1)}, f32[2,8,128]{2,1,0:T(8,128)S(1)}, f32[2,8,128]{2,1,0:T(8,128)S(1)}) custom-call(f32[2,128,256]{2,1,0:T(8,128)S(1)} %shard_map.66.refs_0_, f32[2,128,256]{2,1,0:T(8,128)S(1)} %get-tuple-element.17.refs_1_, f32[2,128,256]{2,1,0:T(8,128)S(1)} %collective-permute-done.2.refs_2_), custom_call_target="tpu_custom_call" | custom-call | tf_op jit(solution)/shard_map/pallas_call | solution.py:157
  23.8 0.1 collective-permute-start.3
  23.9 1.8 %collective-permute-start.4 = (f32[2,8,128]{2,1,0:T(8,128)S(1)}, f32[2,8,128]{2,1,0:T(8,128)S(1)}, u32[]{:S(2)}, u32[]{:S(2)}) collective-permute-start(f32[2,8,128]{2,1,0:T(8,128)S(1)} %get-tuple-element.15), channel_id=1, source_target_pairs={{0,2},{1,3},{2,0},{3,1},{4,6},{5,7},{6,4},{7,5},{8,10},{9,11},{10,... | collective-permute-start | bytes 24584 | tf_op jit(solution)/shard_map/ppermute | solution.py:19
  25.6 0.1 collective-permute-start.5
  25.7 0.0 collective-permute-done.7.refs_7_
  25.7 3.3 %collective-permute-done.6.refs_6_ = bf16[128,1024]{1,0:T(8,128)(2,1)S(1)} collective-permute-done((bf16[128,1024]{1,0:T(8,128)(2,1)S(1)}, bf16[128,1024]{1,0:T(8,128)(2,1)S(1)}, u32[]{:S(2)}, u32[]{:S(2)}) %collective-permute-start.6) | collective-permute-done | bytes 262176 | tf_op jit(solution)/shard_map/ppermute | solution.py:196
  29.0 0.0 collective-permute-done.3.refs_1_
  29.0 0.0 collective-permute-done.4.refs_2_
  29.0 0.0 collective-permute-done.5.refs_3_
  29.0 0.4 %shard_map.68 = f32[8,512]{1,0:T(8,128)S(1)} custom-call(f32[2,8,128]{2,1,0:T(8,128)S(1)} %get-tuple-element.13.refs_0_, f32[2,8,128]{2,1,0:T(8,128)S(1)} %collective-permute-done.3.refs_1_, f32[2,8,128]{2,1,0:T(8,128)S(1)} %collective-permute-done.4.refs_2_, f32[2,8,128]{2,1,0:T(8,128)S(1)} %collective-permute-done.5.refs_3_, ...), custom_call_target="tpu_custom_call" | custom-call | tf_op jit(solution)/shard_map/pallas_call | solution.py:185
  29.4 0.8 %collective-permute-start.10 = (f32[8,512]{1,0:T(8,128)S(1)}, f32[8,512]{1,0:T(8,128)S(1)}, u32[]{:S(2)}, u32[]{:S(2)}) collective-permute-start(f32[8,512]{1,0:T(8,128)S(1)} %shard_map.68), channel_id=1, source_target_pairs={{0,3},{1,2},{2,1},{3,0},{4,7},{5,6},{6,5},{7,4},{8,11},{9,10},{10,... | collective-permute-start | bytes 49160 | tf_op jit(solution)/shard_map/ppermute | solution.py:19
  30.2 0.9 %collective-permute-start.8 = (f32[8,512]{1,0:T(8,128)S(1)}, f32[8,512]{1,0:T(8,128)S(1)}, u32[]{:S(2)}, u32[]{:S(2)}) collective-permute-start(f32[8,512]{1,0:T(8,128)S(1)} %shard_map.68), channel_id=1, source_target_pairs={{0,1},{1,0},{2,3},{3,2},{4,5},{5,4},{6,7},{7,6},{8,9},{9,8},{10,11... | collective-permute-start | bytes 49160 | tf_op jit(solution)/shard_map/ppermute | solution.py:19
  31.0 0.5 %collective-permute-start.9 = (f32[8,512]{1,0:T(8,128)S(1)}, f32[8,512]{1,0:T(8,128)S(1)}, u32[]{:S(2)}, u32[]{:S(2)}) collective-permute-start(f32[8,512]{1,0:T(8,128)S(1)} %shard_map.68), channel_id=1, source_target_pairs={{0,2},{1,3},{2,0},{3,1},{4,6},{5,7},{6,4},{7,5},{8,10},{9,11},{10,... | collective-permute-start | bytes 49160 | tf_op jit(solution)/shard_map/ppermute | solution.py:19
  31.6 1.0 %collective-permute-done.10 = f32[8,512]{1,0:T(8,128)S(1)} collective-permute-done((f32[8,512]{1,0:T(8,128)S(1)}, f32[8,512]{1,0:T(8,128)S(1)}, u32[]{:S(2)}, u32[]{:S(2)}) %collective-permute-start.10) | collective-permute-done | bytes 16416 | tf_op jit(solution)/shard_map/ppermute | solution.py:19
  32.6 0.0 collective-permute-done.8
  32.6 2.2 %collective-permute-done.9 = f32[8,512]{1,0:T(8,128)S(1)} collective-permute-done((f32[8,512]{1,0:T(8,128)S(1)}, f32[8,512]{1,0:T(8,128)S(1)}, u32[]{:S(2)}, u32[]{:S(2)}) %collective-permute-start.9) | collective-permute-done | bytes 16416 | tf_op jit(solution)/shard_map/ppermute | solution.py:19
  34.8 0.6 %add_add_fusion = f32[8,512]{1,0:T(8,128)} fusion(f32[8,512]{1,0:T(8,128)S(1)} %collective-permute-done.9, f32[8,512]{1,0:T(8,128)S(1)} %collective-permute-done.10, f32[8,512]{1,0:T(8,128)S(1)} %shard_map.68, f32[8,512]{1,0:T(8,128)S(1)} %collective-permute-done.8), kind=kLoop, calls=%fused_computation.2 | loop fusion | flops 12288 | bytes 81920 | tf_op jit(solution)/shard_map/add | solution.py:226
  (2 shorter events, 0.0 us)
Async XLA Ops:
  1.0 11.6 %collective-permute-start = (bf16[128,1024]{1,0:T(8,128)(2,1)S(1)}, bf16[128,1024]{1,0:T(8,128)(2,1)S(1)}, u32[]{:S(2)}, u32[]{:S(2)}) collective-permute-start(bf16[128,1024]{1,0:T(8,128)(2,1)S(1)} %shard_map.64.refs_0_.refs_4_), channel_id=1, source_target_pairs={{0,4},{4,8},{8,12},{12,0},{1,5},{5,9},{9,13},{13,1},{2,6},{6,10},{... | collective-permute-start | bytes 786440 | tf_op jit(solution)/shard_map/ppermute | solution.py:196
  12.6 2.2 %collective-permute-start.1 = (f32[4,128,256]{2,1,0:T(8,128)S(1)}, f32[4,128,256]{2,1,0:T(8,128)S(1)}, u32[]{:S(2)}, u32[]{:S(2)}) collective-permute-start(f32[4,128,256]{2,1,0:T(8,128)S(1)} %broadcast_add_fusion), channel_id=1, source_target_pairs={{0,1},{1,0},{2,3},{3,2},{4,5},{5,4},{6,7},{7,6},{8,9},{9,8},{10,11... | collective-permute-start | bytes 1572872 | tf_op jit(solution)/shard_map/ppermute | solution.py:19
  12.7 13.1 %collective-permute-start.7 = (bf16[128,1024]{1,0:T(8,128)(2,1)S(1)}, bf16[128,1024]{1,0:T(8,128)(2,1)S(1)}, u32[]{:S(2)}, u32[]{:S(2)}) collective-permute-start(bf16[128,1024]{1,0:T(8,128)(2,1)S(1)} %shard_map.64.refs_0_.refs_4_), channel_id=1, source_target_pairs={{0,12},{4,0},{8,4},{12,8},{1,13},{5,1},{9,5},{13,9},{2,14},{6,2},{... | collective-permute-start | bytes 786440 | tf_op jit(solution)/shard_map/ppermute | solution.py:196
  14.8 14.2 %collective-permute-start.6 = (bf16[128,1024]{1,0:T(8,128)(2,1)S(1)}, bf16[128,1024]{1,0:T(8,128)(2,1)S(1)}, u32[]{:S(2)}, u32[]{:S(2)}) collective-permute-start(bf16[128,1024]{1,0:T(8,128)(2,1)S(1)} %collective-permute-done.refs_5_), channel_id=1, source_target_pairs={{0,4},{4,8},{8,12},{12,0},{1,5},{5,9},{9,13},{13,1},{2,6},{6,10},{... | collective-permute-start | bytes 786440 | tf_op jit(solution)/shard_map/ppermute | solution.py:196
  14.8 8.4 %collective-permute-start.2 = (f32[2,128,256]{2,1,0:T(8,128)S(1)}, f32[2,128,256]{2,1,0:T(8,128)S(1)}, u32[]{:S(2)}, u32[]{:S(2)}) collective-permute-start(f32[2,128,256]{2,1,0:T(8,128)S(1)} %get-tuple-element.18.refs_0_), channel_id=1, source_target_pairs={{0,2},{1,3},{2,0},{3,1},{4,6},{5,7},{6,4},{7,5},{8,10},{9,11},{10,... | collective-permute-start | bytes 786440 | tf_op jit(solution)/shard_map/ppermute | solution.py:19
  23.8 5.2 %collective-permute-start.3 = (f32[2,8,128]{2,1,0:T(8,128)S(1)}, f32[2,8,128]{2,1,0:T(8,128)S(1)}, u32[]{:S(2)}, u32[]{:S(2)}) collective-permute-start(f32[2,8,128]{2,1,0:T(8,128)S(1)} %get-tuple-element.14), channel_id=1, source_target_pairs={{0,1},{1,0},{2,3},{3,2},{4,5},{5,4},{6,7},{7,6},{8,9},{9,8},{10,11... | collective-permute-start | bytes 24584 | tf_op jit(solution)/shard_map/ppermute | solution.py:19
  23.9 5.2 %collective-permute-start.4 = (f32[2,8,128]{2,1,0:T(8,128)S(1)}, f32[2,8,128]{2,1,0:T(8,128)S(1)}, u32[]{:S(2)}, u32[]{:S(2)}) collective-permute-start(f32[2,8,128]{2,1,0:T(8,128)S(1)} %get-tuple-element.15), channel_id=1, source_target_pairs={{0,2},{1,3},{2,0},{3,1},{4,6},{5,7},{6,4},{7,5},{8,10},{9,11},{10,... | collective-permute-start | bytes 24584 | tf_op jit(solution)/shard_map/ppermute | solution.py:19
  25.6 3.4 %collective-permute-start.5 = (f32[2,8,128]{2,1,0:T(8,128)S(1)}, f32[2,8,128]{2,1,0:T(8,128)S(1)}, u32[]{:S(2)}, u32[]{:S(2)}) collective-permute-start(f32[2,8,128]{2,1,0:T(8,128)S(1)} %get-tuple-element.16), channel_id=1, source_target_pairs={{0,3},{1,2},{2,1},{3,0},{4,7},{5,6},{6,5},{7,4},{8,11},{9,10},{10,... | collective-permute-start | bytes 24584 | tf_op jit(solution)/shard_map/ppermute | solution.py:19
  29.4 3.2 %collective-permute-start.10 = (f32[8,512]{1,0:T(8,128)S(1)}, f32[8,512]{1,0:T(8,128)S(1)}, u32[]{:S(2)}, u32[]{:S(2)}) collective-permute-start(f32[8,512]{1,0:T(8,128)S(1)} %shard_map.68), channel_id=1, source_target_pairs={{0,3},{1,2},{2,1},{3,0},{4,7},{5,6},{6,5},{7,4},{8,11},{9,10},{10,... | collective-permute-start | bytes 49160 | tf_op jit(solution)/shard_map/ppermute | solution.py:19
  30.2 2.4 %collective-permute-start.8 = (f32[8,512]{1,0:T(8,128)S(1)}, f32[8,512]{1,0:T(8,128)S(1)}, u32[]{:S(2)}, u32[]{:S(2)}) collective-permute-start(f32[8,512]{1,0:T(8,128)S(1)} %shard_map.68), channel_id=1, source_target_pairs={{0,1},{1,0},{2,3},{3,2},{4,5},{5,4},{6,7},{7,6},{8,9},{9,8},{10,11... | collective-permute-start | bytes 49160 | tf_op jit(solution)/shard_map/ppermute | solution.py:19
  31.0 3.7 %collective-permute-start.9 = (f32[8,512]{1,0:T(8,128)S(1)}, f32[8,512]{1,0:T(8,128)S(1)}, u32[]{:S(2)}, u32[]{:S(2)}) collective-permute-start(f32[8,512]{1,0:T(8,128)S(1)} %shard_map.68), channel_id=1, source_target_pairs={{0,2},{1,3},{2,0},{3,1},{4,6},{5,7},{6,4},{7,5},{8,10},{9,11},{10,... | collective-permute-start | bytes 49160 | tf_op jit(solution)/shard_map/ppermute | solution.py:19

commit v11 on v10

--- a/solution.py
+++ b/solution.py
@@ -42,11 +42,12 @@
 COST = 1 << 32
 
 
-def cut(total, piece, last):
-    ends = list(range(piece, total - last + 1, piece))
-    ends += [total - last] if total - last > 0 and (not ends or ends[-1] < total - last) else []
-    ends += [total]
-    return [slice(start, end) for start, end in zip([0] + ends[:-1], ends)]
+def cut(total, widths):
+    slices = []
+    while not slices or slices[-1].stop < total:
+        start = slices[-1].stop if slices else 0
+        slices.append(slice(start, min(start + widths[min(len(slices), len(widths) - 1)], total)))
+    return slices
 
 
 def project_kernel(steps, share, ahead, pieces, after, act, og, wi, wo, lens, *refs):
@@ -101,12 +102,13 @@
         out[rank:] = sums[1][:, slot * slots : (slot + 1) * slots]
 
 
-def project(act, og, wi, wo, lens, groups, share, ahead, piece, after=()):
+def project(act, og, wi, wo, lens, groups, share, ahead, widths, after=()):
     steps = [step for group in groups for step in group]
     count = len(steps) * share
     slots, feat, hidden = act.shape[1], act.shape[2], og.shape[2]
     rank = wi.shape[0]
-    pieces = [(0, span) for span in cut(feat, piece, piece)] + [(1, span) for span in cut(hidden, piece, 256)]
+    pieces = [(0, span) for span in cut(feat, widths)] + [(1, span) for span in cut(hidden, [512])]
+    piece = max(span.stop - span.start for _, span in pieces)
     return pl.pallas_call(
         functools.partial(project_kernel, steps, share, ahead, pieces, len(after)),
         out_shape=[jax.ShapeDtypeStruct((len(group) * share, 2 * rank, slots), jnp.float32) for group in groups],
@@ -164,7 +166,7 @@
     )(*parts)
 
 
-def score_kernel(share, size, shifts, *refs):
+def score_kernel(share, size, groups, origins, *refs):
     unit_refs, test_refs, out, held = refs[:size], refs[size:-2], refs[-2], refs[-1]
     me, dp = lax.axis_index("tensor"), lax.axis_index("dp")
     for step in range(size):
@@ -172,55 +174,62 @@
             held[(me ^ step) * share + k] = unit_refs[step][k]
     unit = jnp.concatenate([held[:, c, :] for c in range(held.shape[1])], axis=1).astype(jnp.bfloat16)
     tests = test_refs[0].shape[0]
-    for step, test_ref in zip(shifts, test_refs):
+    out[...] = jnp.zeros_like(out)
+    for (factor, offset), test_ref in zip(origins, test_refs):
         part = lax.dot_general(unit, test_ref[...], NT, preferred_element_type=jnp.float32)
-        at = lax.rem(dp - step + len(shifts), len(shifts)) * tests
-        out[:, pl.ds(pl.multiple_of(at, 128), tests)] = part
-
-
-def score(unit_parts, test_parts, share):
-    size, groups = len(unit_parts), len(test_parts)
-    tests, width = test_parts[0].shape
-    shifts = tuple(test_parts)
-    return pl.pallas_call(
-        functools.partial(score_kernel, share, size, shifts),
+        at = lax.rem(factor * dp + offset + groups, groups) * tests
+        out[:, pl.ds(pl.multiple_of(at, 128), tests)] += part
+
+
+def score(unit_parts, test_parts, share, groups):
+    size = len(unit_parts)
+    tests, width = test_parts[0][0].shape
+    origins = [origin for _, *origin in test_parts]
+    return pl.pallas_call(
+        functools.partial(score_kernel, share, size, groups, origins),
         out_shape=jax.ShapeDtypeStruct((share * size, tests * groups), jnp.float32),
-        in_specs=[VMEM] * (size + groups),
+        in_specs=[VMEM] * (size + len(test_parts)),
         out_specs=VMEM,
         scratch_shapes=[pltpu.VMEM((share * size, width // 128, 128), jnp.float32)],
         compiler_params=SMALL,
-    )(*unit_parts, *test_parts.values())
-
-
-def shift(value, axis, size, step):
-    return lax.ppermute(value, axis, [(i, (i + step) % size) for i in range(size)])
+    )(*unit_parts, *(shard for shard, *_ in test_parts))
+
+
+def gather_tests(own, groups):
+    if groups != 4:
+        shards = [lax.ppermute(own, "dp", [(i, (i + step) % groups) for i in range(groups)]) for step in range(1, groups)]
+        return [(own, 1, 0)] + [(shard, 1, -step) for step, shard in enumerate(shards, 1)], shards[:1]
+    below = lax.ppermute(own, "dp", [(0, 1), (1, 2), (2, 3)])
+    above = lax.ppermute(own, "dp", [(1, 0), (2, 1), (3, 2)])
+    lower = lax.axis_index("dp") == 1
+    outer, inner = jnp.where(lower, below, above), jnp.where(lower, above, below)
+    ends = lax.ppermute(inner, "dp", [(1, 0), (2, 3)])
+    middle = lax.ppermute(outer, "dp", [(1, 2), (2, 1)])
+    across = lax.ppermute(outer, "dp", [(1, 3), (2, 0)])
+    return [(own, 1, 0), (below, 1, -1), (above, 1, 1), (ends, 1, 2), (middle, 1, 2), (across, -1, 3)], [below, above]
 
 
 def shards(size, groups, activations, out_grads, proj_in, proj_out, lengths, test_grads):
     rank = proj_in.shape[1]
     share = activations.shape[0] // size
     own_tests = cut_tests(test_grads, size)
-    tests = {0: own_tests, 1: shift(own_tests, "dp", groups, 1)}
-    if groups == 4:
-        tests[2] = shift(tests[1], "dp", groups, 1)
-        tests[3] = shift(own_tests, "dp", groups, 3)
-    else:
-        tests.update({step: shift(own_tests, "dp", groups, step) for step in range(2, groups)})
+    tests, first = gather_tests(own_tests, groups)
 
     far = [CORES * x for x in range(1, size // CORES)]
     arrays = (activations, out_grads, proj_in.T, proj_out.T, lengths)
     sends = [[step ^ 1 for step in far] + [1], far]
-    other, far_own = project(*arrays, sends, share, 2, 512, [own_tests])
-    other = other + 0.0 * tests[1][:1, : other.shape[2]].astype(jnp.float32)
+    other, far_own = project(*arrays, sends, share, 3, [128, 256, 640], [own_tests])
+    for shard in first:
+        other = other + 0.0 * shard[:1, : other.shape[2]].astype(jnp.float32)
     arrived = xor_permute(other, "tensor", size, 1)
     cut_at = len(far) * share
     far_sum = far_own + arrived[:cut_at]
     sums = [xor_permute(far_sum[i * share : (i + 1) * share], "tensor", size, step) for i, step in enumerate(far)]
-    near_own = project(*arrays, [[0]], share, 4, 512, [far_sum])[0]
+    near_own = project(*arrays, [[0]], share, 7, [128, 256, 256, 384], [far_sum])[0]
 
     unit_outs = units([near_own, arrived[cut_at:]] + sums, share, rank, size)
     unit_parts = [unit_outs[0]] + [xor_permute(unit_outs[step], "tensor", size, step) for step in range(1, size)]
-    part = score(unit_parts, tests, share)
+    part = score(unit_parts, tests, share, groups)
     parts = [part] + [xor_permute(part, "tensor", size, step) for step in range(1, size)]
     while len(parts) > 1:
         parts = [parts[i] + parts[i + 1] for i in range(0, len(parts), 2)]

time: 35.7 us -> 42.4 us (1.19)
  waiting for transfers between devices: 9.27 us -> 13.5 us
  starting transfers between devices: 11.1 us -> 14.9 us
  Pallas kernels: 14.2 us -> 12.8 us
    ppermute x3 -> x5, starting transfers between devices: 5.18 us -> 9.5 us  [the longest x1 4.94 us: gather_tests(): below = lax.ppermute(own, 'dp', [(0, 1), (1, 2), (2, 3)])]
    ppermute x3 -> x5, waiting for transfers between devices: 3.29 us -> 6.86 us  [the longest x1 3.02 us: gather_tests(): ends = lax.ppermute(inner, 'dp', [(1, 0), (2, 3)])]
    pallas_call x2, Pallas kernels: 12.4 us -> 10.8 us  [project(): pl.pallas_call(functools.partial(project_kernel, steps, share, ahead, pie...]
    ppermute x8, waiting for transfers between devices: 5.98 us -> 6.63 us  [xor_permute(): return lax.ppermute(value, axis, [(i, i ^ step) for i in range(size)])]
    ppermute x8, starting transfers between devices: 5.92 us -> 5.44 us  [xor_permute(): return lax.ppermute(value, axis, [(i, i ^ step) for i in range(size)])]
  transfers between devices with their start and end apart: 11 -> 13, of which waited for: 4 -> 6; matrix products, arithmetic and copies ran while one was open for 0% -> 0% of each run, Pallas kernels for 36% -> 27%
where the time goes in v11:
time: 42.4 us; the launch traced here: 42.1 us
  starting transfers between devices  14.9 us (35%)
  waiting for transfers between devices  13.5 us (32%)
  Pallas kernels  12.8 us (30%)
  other arithmetic  0.77 us (2%)
    pallas_call x2, Pallas kernels, project(): pl.pallas_call(functools.partial(project_kernel, steps, share, ahead, pie...  10.8 us
    ppermute x8, waiting for transfers between devices, xor_permute(): return lax.ppermute(value, axis, [(i, i ^ step) for i in range(size)])  6.63 us
    ppermute x8, starting transfers between devices, xor_permute(): return lax.ppermute(value, axis, [(i, i ^ step) for i in range(size)])  5.44 us
    ppermute x1, starting transfers between devices, gather_tests(): below = lax.ppermute(own, 'dp', [(0, 1), (1, 2), (2, 3)])  4.94 us
    ppermute x1, waiting for transfers between devices, gather_tests(): ends = lax.ppermute(inner, 'dp', [(1, 0), (2, 3)])  3.02 us
    ppermute x1, waiting for transfers between devices, gather_tests(): across = lax.ppermute(outer, 'dp', [(1, 3), (2, 0)])  2.86 us
    ppermute x1, starting transfers between devices, gather_tests(): across = lax.ppermute(outer, 'dp', [(1, 3), (2, 0)])  1.29 us
    ppermute x1, starting transfers between devices, gather_tests(): ends = lax.ppermute(inner, 'dp', [(1, 0), (2, 3)])  1.29 us
  transfers between devices with their start and end apart: 13, of which 6 were waited for; matrix products, arithmetic and copies ran while one was open for 0% of the time, Pallas kernels for 27%

profile of v11, /device:TPU:0, one launch (start us, length us, event | category | flops | bytes accessed | tf_op | source)
XLA Modules:
  0.0 42.1 jit_solution(6919319873508547239)
XLA Ops:
  0.0 1.0 %shard_map.64.refs_0_.refs_4_ = bf16[128,1024]{1,0:T(8,128)(2,1)S(1)} custom-call(bf16[128,4096]{1,0:T(8,128)(2,1)} %tests.1), custom_call_target="tpu_custom_call" | custom-call | tf_op jit(solution)/shard_map/pallas_call | solution.py:32
  1.0 4.9 %collective-permute-start = (bf16[128,1024]{1,0:T(8,128)(2,1)S(1)}, bf16[128,1024]{1,0:T(8,128)(2,1)S(1)}, u32[]{:S(2)}, u32[]{:S(2)}) collective-permute-start(bf16[128,1024]{1,0:T(8,128)(2,1)S(1)} %shard_map.64.refs_0_.refs_4_), channel_id=1, source_target_pairs={{0,4},{4,8},{8,12},{1,5},{5,9},{9,13},{2,6},{6,10},{10,14},{3,7},{... | collective-permute-start | bytes 786440 | tf_op jit(solution)/shard_map/ppermute | solution.py:202
  5.9 1.3 %collective-permute-start.1 = (bf16[128,1024]{1,0:T(8,128)(2,1)S(1)}, bf16[128,1024]{1,0:T(8,128)(2,1)S(1)}, u32[]{:S(2)}, u32[]{:S(2)}) collective-permute-start(bf16[128,1024]{1,0:T(8,128)(2,1)S(1)} %shard_map.64.refs_0_.refs_4_), channel_id=1, source_target_pairs={{4,0},{8,4},{12,8},{5,1},{9,5},{13,9},{6,2},{10,6},{14,10},{7,3},{... | collective-permute-start | bytes 786440 | tf_op jit(solution)/shard_map/ppermute | solution.py:203
  7.2 7.3 %shard_map.65 = (f32[4,128,256]{2,1,0:T(8,128)S(1)}, f32[2,128,256]{2,1,0:T(8,128)S(1)}) custom-call(bf16[8,256,1024]{2,1,0:T(8,128)(2,1)} %act.3, bf16[8,256,3584]{2,1,0:T(8,128)(2,1)} %og.3, bf16[64,1024]{1,0:T(8,128)(2,1)} %bitcast.6, bf16[64,3584]{1,0:T(8,128)(2,1)} %bitcast.4, s32[8]{0:T(128)} %lens.3, bf16[128,1024]{1,0:T(8,128)(2,1)S(1)} %shard_map.64.refs_0_.refs_4_), custom_call_target="tpu_custom_call" | custom-call | flops 4294967296 | bytes 16777216 | tf_op jit(solution)/shard_map/pallas_call | solution.py:112
  14.6 0.0 collective-permute-done.refs_5_
  14.6 1.0 %collective-permute-done.1.refs_6_ = bf16[128,1024]{1,0:T(8,128)(2,1)S(1)} collective-permute-done((bf16[128,1024]{1,0:T(8,128)(2,1)S(1)}, bf16[128,1024]{1,0:T(8,128)(2,1)S(1)}, u32[]{:S(2)}, u32[]{:S(2)}) %collective-permute-start.1) | collective-permute-done | bytes 262176 | tf_op jit(solution)/shard_map/ppermute | solution.py:203
  15.6 0.1 add_add_fusion
  15.6 0.1 collective-permute-start.2
  15.8 0.7 %collective-permute-start.8 = (bf16[128,1024]{1,0:T(8,128)(2,1)S(1)}, bf16[128,1024]{1,0:T(8,128)(2,1)S(1)}, u32[]{:S(2)}, u32[]{:S(2)}) collective-permute-start(bf16[128,1024]{1,0:T(8,128)(2,1)S(1)} %get-tuple-element.17), channel_id=1, source_target_pairs={{4,8},{8,4},{5,9},{9,5},{6,10},{10,6},{7,11},{11,7},{20,24},{24,20... | collective-permute-start | bytes 786440 | tf_op jit(solution)/shard_map/ppermute | solution.py:207
  16.5 1.3 %collective-permute-start.9 = (bf16[128,1024]{1,0:T(8,128)(2,1)S(1)}, bf16[128,1024]{1,0:T(8,128)(2,1)S(1)}, u32[]{:S(2)}, u32[]{:S(2)}) collective-permute-start(bf16[128,1024]{1,0:T(8,128)(2,1)S(1)} %get-tuple-element.17), channel_id=1, source_target_pairs={{4,12},{8,0},{5,13},{9,1},{6,14},{10,2},{7,15},{11,3},{20,28},{24,... | collective-permute-start | bytes 786440 | tf_op jit(solution)/shard_map/ppermute | solution.py:208
  17.8 1.3 %collective-permute-start.7 = (bf16[128,1024]{1,0:T(8,128)(2,1)S(1)}, bf16[128,1024]{1,0:T(8,128)(2,1)S(1)}, u32[]{:S(2)}, u32[]{:S(2)}) collective-permute-start(bf16[128,1024]{1,0:T(8,128)(2,1)S(1)} %get-tuple-element.18), channel_id=1, source_target_pairs={{4,0},{8,12},{5,1},{9,13},{6,2},{10,14},{7,3},{11,15},{20,16},{24,... | collective-permute-start | bytes 786440 | tf_op jit(solution)/shard_map/ppermute | solution.py:206
  19.1 0.0 collective-permute-done.2
  19.1 0.1 fusion.2
  19.1 1.6 %collective-permute-start.3 = (f32[2,128,256]{2,1,0:T(8,128)S(1)}, f32[2,128,256]{2,1,0:T(8,128)S(1)}, u32[]{:S(2)}, u32[]{:S(2)}) collective-permute-start(f32[2,128,256]{2,1,0:T(8,128)S(1)} %get-tuple-element.20.refs_0_), channel_id=1, source_target_pairs={{0,2},{1,3},{2,0},{3,1},{4,6},{5,7},{6,4},{7,5},{8,10},{9,11},{10,... | collective-permute-start | bytes 786440 | tf_op jit(solution)/shard_map/ppermute | solution.py:19
  20.7 3.4 %shard_map.66.refs_0_ = f32[2,128,256]{2,1,0:T(8,128)S(1)} custom-call(bf16[8,256,1024]{2,1,0:T(8,128)(2,1)} %act.3, bf16[8,256,3584]{2,1,0:T(8,128)(2,1)} %og.3, bf16[64,1024]{1,0:T(8,128)(2,1)} %bitcast.7, bf16[64,3584]{1,0:T(8,128)(2,1)} %bitcast.5, s32[8]{0:T(128)} %lens.3, f32[2,128,256]{2,1,0:T(8,128)S(1)} %get-tuple-element.20.refs_0_), custom_call_target="tpu_custom_call" | custom-call | flops 4294967296 | bytes 16777216 | tf_op jit(solution)/shard_map/pallas_call | solution.py:112
  24.1 3.8 %collective-permute-done.3.refs_2_ = f32[2,128,256]{2,1,0:T(8,128)S(1)} collective-permute-done((f32[2,128,256]{2,1,0:T(8,128)S(1)}, f32[2,128,256]{2,1,0:T(8,128)S(1)}, u32[]{:S(2)}, u32[]{:S(2)}) %collective-permute-start.3) | collective-permute-done | bytes 262176 | tf_op jit(solution)/shard_map/ppermute | solution.py:19
  27.9 0.5 %shard_map.67 = (f32[2,8,128]{2,1,0:T(8,128)S(1)}, f32[2,8,128]{2,1,0:T(8,128)S(1)}, f32[2,8,128]{2,1,0:T(8,128)S(1)}, f32[2,8,128]{2,1,0:T(8,128)S(1)}) custom-call(f32[2,128,256]{2,1,0:T(8,128)S(1)} %shard_map.66.refs_0_, f32[2,128,256]{2,1,0:T(8,128)S(1)} %get-tuple-element.19.refs_1_, f32[2,128,256]{2,1,0:T(8,128)S(1)} %collective-permute-done.3.refs_2_), custom_call_target="tpu_custom_call" | custom-call | tf_op jit(solution)/shard_map/pallas_call | solution.py:159
  28.4 0.1 collective-permute-start.4
  28.5 1.6 %collective-permute-start.5 = (f32[2,8,128]{2,1,0:T(8,128)S(1)}, f32[2,8,128]{2,1,0:T(8,128)S(1)}, u32[]{:S(2)}, u32[]{:S(2)}) collective-permute-start(f32[2,8,128]{2,1,0:T(8,128)S(1)} %get-tuple-element.15), channel_id=1, source_target_pairs={{0,2},{1,3},{2,0},{3,1},{4,6},{5,7},{6,4},{7,5},{8,10},{9,11},{10,... | collective-permute-start | bytes 24584 | tf_op jit(solution)/shard_map/ppermute | solution.py:19
  30.0 0.0 collective-permute-done.8.refs_8_
  30.0 0.3 collective-permute-start.6
  30.3 2.9 %collective-permute-done.9.refs_9_ = bf16[128,1024]{1,0:T(8,128)(2,1)S(1)} collective-permute-done((bf16[128,1024]{1,0:T(8,128)(2,1)S(1)}, bf16[128,1024]{1,0:T(8,128)(2,1)S(1)}, u32[]{:S(2)}, u32[]{:S(2)}) %collective-permute-start.9) | collective-permute-done | bytes 262176 | tf_op jit(solution)/shard_map/ppermute | solution.py:208
  33.2 3.0 %collective-permute-done.7.refs_7_ = bf16[128,1024]{1,0:T(8,128)(2,1)S(1)} collective-permute-done((bf16[128,1024]{1,0:T(8,128)(2,1)S(1)}, bf16[128,1024]{1,0:T(8,128)(2,1)S(1)}, u32[]{:S(2)}, u32[]{:S(2)}) %collective-permute-start.7) | collective-permute-done | bytes 262176 | tf_op jit(solution)/shard_map/ppermute | solution.py:206
  36.2 0.0 collective-permute-done.6.refs_3_
  36.2 0.5 %shard_map.68 = f32[8,512]{1,0:T(8,128)S(1)} custom-call(f32[2,8,128]{2,1,0:T(8,128)S(1)} %get-tuple-element.13.refs_0_, f32[2,8,128]{2,1,0:T(8,128)S(1)} %collective-permute-done.4.refs_1_, f32[2,8,128]{2,1,0:T(8,128)S(1)} %collective-permute-done.5.refs_2_, f32[2,8,128]{2,1,0:T(8,128)S(1)} %collective-permute-done.6.refs_3_, ...), custom_call_target="tpu_custom_call" | custom-call | tf_op jit(solution)/shard_map/pallas_call | solution.py:188
  36.7 0.0 collective-permute-start.10
  36.8 1.6 %collective-permute-start.11 = (f32[8,512]{1,0:T(8,128)S(1)}, f32[8,512]{1,0:T(8,128)S(1)}, u32[]{:S(2)}, u32[]{:S(2)}) collective-permute-start(f32[8,512]{1,0:T(8,128)S(1)} %shard_map.68), channel_id=1, source_target_pairs={{0,2},{1,3},{2,0},{3,1},{4,6},{5,7},{6,4},{7,5},{8,10},{9,11},{10,... | collective-permute-start | bytes 49160 | tf_op jit(solution)/shard_map/ppermute | solution.py:19
  38.3 0.3 collective-permute-start.12
  38.6 0.0 collective-permute-done.10
  38.6 1.9 %collective-permute-done.11 = f32[8,512]{1,0:T(8,128)S(1)} collective-permute-done((f32[8,512]{1,0:T(8,128)S(1)}, f32[8,512]{1,0:T(8,128)S(1)}, u32[]{:S(2)}, u32[]{:S(2)}) %collective-permute-start.11) | collective-permute-done | bytes 16416 | tf_op jit(solution)/shard_map/ppermute | solution.py:19
  40.6 0.9 %collective-permute-done.12 = f32[8,512]{1,0:T(8,128)S(1)} collective-permute-done((f32[8,512]{1,0:T(8,128)S(1)}, f32[8,512]{1,0:T(8,128)S(1)}, u32[]{:S(2)}, u32[]{:S(2)}) %collective-permute-start.12) | collective-permute-done | bytes 16416 | tf_op jit(solution)/shard_map/ppermute | solution.py:19
  41.5 0.6 %add_add_fusion.1 = f32[8,512]{1,0:T(8,128)} fusion(f32[8,512]{1,0:T(8,128)S(1)} %collective-permute-done.11, f32[8,512]{1,0:T(8,128)S(1)} %collective-permute-done.12, f32[8,512]{1,0:T(8,128)S(1)} %shard_map.68, f32[8,512]{1,0:T(8,128)S(1)} %collective-permute-done.10), kind=kLoop, calls=%fused_computation.4 | loop fusion | flops 12288 | bytes 81920 | tf_op jit(solution)/shard_map/add | solution.py:235
  (5 shorter events, 0.1 us)
Async XLA Ops:
  1.0 13.6 %collective-permute-start = (bf16[128,1024]{1,0:T(8,128)(2,1)S(1)}, bf16[128,1024]{1,0:T(8,128)(2,1)S(1)}, u32[]{:S(2)}, u32[]{:S(2)}) collective-permute-start(bf16[128,1024]{1,0:T(8,128)(2,1)S(1)} %shard_map.64.refs_0_.refs_4_), channel_id=1, source_target_pairs={{0,4},{4,8},{8,12},{1,5},{5,9},{9,13},{2,6},{6,10},{10,14},{3,7},{... | collective-permute-start | bytes 786440 | tf_op jit(solution)/shard_map/ppermute | solution.py:202
  5.9 9.7 %collective-permute-start.1 = (bf16[128,1024]{1,0:T(8,128)(2,1)S(1)}, bf16[128,1024]{1,0:T(8,128)(2,1)S(1)}, u32[]{:S(2)}, u32[]{:S(2)}) collective-permute-start(bf16[128,1024]{1,0:T(8,128)(2,1)S(1)} %shard_map.64.refs_0_.refs_4_), channel_id=1, source_target_pairs={{4,0},{8,4},{12,8},{5,1},{9,5},{13,9},{6,2},{10,6},{14,10},{7,3},{... | collective-permute-start | bytes 786440 | tf_op jit(solution)/shard_map/ppermute | solution.py:203
  15.6 3.4 %collective-permute-start.2 = (f32[4,128,256]{2,1,0:T(8,128)S(1)}, f32[4,128,256]{2,1,0:T(8,128)S(1)}, u32[]{:S(2)}, u32[]{:S(2)}) collective-permute-start(f32[4,128,256]{2,1,0:T(8,128)S(1)} %add_add_fusion), channel_id=1, source_target_pairs={{0,1},{1,0},{2,3},{3,2},{4,5},{5,4},{6,7},{7,6},{8,9},{9,8},{10,11... | collective-permute-start | bytes 1572872 | tf_op jit(solution)/shard_map/ppermute | solution.py:19
  15.8 14.3 %collective-permute-start.8 = (bf16[128,1024]{1,0:T(8,128)(2,1)S(1)}, bf16[128,1024]{1,0:T(8,128)(2,1)S(1)}, u32[]{:S(2)}, u32[]{:S(2)}) collective-permute-start(bf16[128,1024]{1,0:T(8,128)(2,1)S(1)} %get-tuple-element.17), channel_id=1, source_target_pairs={{4,8},{8,4},{5,9},{9,5},{6,10},{10,6},{7,11},{11,7},{20,24},{24,20... | collective-permute-start | bytes 786440 | tf_op jit(solution)/shard_map/ppermute | solution.py:207
  16.5 16.7 %collective-permute-start.9 = (bf16[128,1024]{1,0:T(8,128)(2,1)S(1)}, bf16[128,1024]{1,0:T(8,128)(2,1)S(1)}, u32[]{:S(2)}, u32[]{:S(2)}) collective-permute-start(bf16[128,1024]{1,0:T(8,128)(2,1)S(1)} %get-tuple-element.17), channel_id=1, source_target_pairs={{4,12},{8,0},{5,13},{9,1},{6,14},{10,2},{7,15},{11,3},{20,28},{24,... | collective-permute-start | bytes 786440 | tf_op jit(solution)/shard_map/ppermute | solution.py:208
  17.8 18.5 %collective-permute-start.7 = (bf16[128,1024]{1,0:T(8,128)(2,1)S(1)}, bf16[128,1024]{1,0:T(8,128)(2,1)S(1)}, u32[]{:S(2)}, u32[]{:S(2)}) collective-permute-start(bf16[128,1024]{1,0:T(8,128)(2,1)S(1)} %get-tuple-element.18), channel_id=1, source_target_pairs={{4,0},{8,12},{5,1},{9,13},{6,2},{10,14},{7,3},{11,15},{20,16},{24,... | collective-permute-start | bytes 786440 | tf_op jit(solution)/shard_map/ppermute | solution.py:206
  19.1 8.8 %collective-permute-start.3 = (f32[2,128,256]{2,1,0:T(8,128)S(1)}, f32[2,128,256]{2,1,0:T(8,128)S(1)}, u32[]{:S(2)}, u32[]{:S(2)}) collective-permute-start(f32[2,128,256]{2,1,0:T(8,128)S(1)} %get-tuple-element.20.refs_0_), channel_id=1, source_target_pairs={{0,2},{1,3},{2,0},{3,1},{4,6},{5,7},{6,4},{7,5},{8,10},{9,11},{10,... | collective-permute-start | bytes 786440 | tf_op jit(solution)/shard_map/ppermute | solution.py:19
  28.4 7.8 %collective-permute-start.4 = (f32[2,8,128]{2,1,0:T(8,128)S(1)}, f32[2,8,128]{2,1,0:T(8,128)S(1)}, u32[]{:S(2)}, u32[]{:S(2)}) collective-permute-start(f32[2,8,128]{2,1,0:T(8,128)S(1)} %get-tuple-element.14), channel_id=1, source_target_pairs={{0,1},{1,0},{2,3},{3,2},{4,5},{5,4},{6,7},{7,6},{8,9},{9,8},{10,11... | collective-permute-start | bytes 24584 | tf_op jit(solution)/shard_map/ppermute | solution.py:19
  28.5 7.7 %collective-permute-start.5 = (f32[2,8,128]{2,1,0:T(8,128)S(1)}, f32[2,8,128]{2,1,0:T(8,128)S(1)}, u32[]{:S(2)}, u32[]{:S(2)}) collective-permute-start(f32[2,8,128]{2,1,0:T(8,128)S(1)} %get-tuple-element.15), channel_id=1, source_target_pairs={{0,2},{1,3},{2,0},{3,1},{4,6},{5,7},{6,4},{7,5},{8,10},{9,11},{10,... | collective-permute-start | bytes 24584 | tf_op jit(solution)/shard_map/ppermute | solution.py:19
  30.0 6.2 %collective-permute-start.6 = (f32[2,8,128]{2,1,0:T(8,128)S(1)}, f32[2,8,128]{2,1,0:T(8,128)S(1)}, u32[]{:S(2)}, u32[]{:S(2)}) collective-permute-start(f32[2,8,128]{2,1,0:T(8,128)S(1)} %get-tuple-element.16), channel_id=1, source_target_pairs={{0,3},{1,2},{2,1},{3,0},{4,7},{5,6},{6,5},{7,4},{8,11},{9,10},{10,... | collective-permute-start | bytes 24584 | tf_op jit(solution)/shard_map/ppermute | solution.py:19
  36.7 1.9 %collective-permute-start.10 = (f32[8,512]{1,0:T(8,128)S(1)}, f32[8,512]{1,0:T(8,128)S(1)}, u32[]{:S(2)}, u32[]{:S(2)}) collective-permute-start(f32[8,512]{1,0:T(8,128)S(1)} %shard_map.68), channel_id=1, source_target_pairs={{0,1},{1,0},{2,3},{3,2},{4,5},{5,4},{6,7},{7,6},{8,9},{9,8},{10,11... | collective-permute-start | bytes 49160 | tf_op jit(solution)/shard_map/ppermute | solution.py:19
  36.8 3.8 %collective-permute-start.11 = (f32[8,512]{1,0:T(8,128)S(1)}, f32[8,512]{1,0:T(8,128)S(1)}, u32[]{:S(2)}, u32[]{:S(2)}) collective-permute-start(f32[8,512]{1,0:T(8,128)S(1)} %shard_map.68), channel_id=1, source_target_pairs={{0,2},{1,3},{2,0},{3,1},{4,6},{5,7},{6,4},{7,5},{8,10},{9,11},{10,... | collective-permute-start | bytes 49160 | tf_op jit(solution)/shard_map/ppermute | solution.py:19
  38.3 3.2 %collective-permute-start.12 = (f32[8,512]{1,0:T(8,128)S(1)}, f32[8,512]{1,0:T(8,128)S(1)}, u32[]{:S(2)}, u32[]{:S(2)}) collective-permute-start(f32[8,512]{1,0:T(8,128)S(1)} %shard_map.68), channel_id=1, source_target_pairs={{0,3},{1,2},{2,1},{3,0},{4,7},{5,6},{6,5},{7,4},{8,11},{9,10},{10,... | collective-permute-start | bytes 49160 | tf_op jit(solution)/shard_map/ppermute | solution.py:19

commit v12 on v10

--- a/solution.py
+++ b/solution.py
@@ -40,23 +40,15 @@
 
 
 COST = 1 << 32
-
-
-def cut(total, piece, last):
-    ends = list(range(piece, total - last + 1, piece))
-    ends += [total - last] if total - last > 0 and (not ends or ends[-1] < total - last) else []
-    ends += [total]
-    return [slice(start, end) for start, end in zip([0] + ends[:-1], ends)]
+PIECE = 512
 
 
 def project_kernel(steps, share, ahead, pieces, after, act, og, wi, wo, lens, *refs):
     refs = refs[after:]
-    outs, (buf, wibuf, wobuf, lenbuf, sem, wsem) = refs[:-6], refs[-6:]
+    outs, (buf, wibuf, wobuf, wide, lenbuf, sem, wsem) = refs[:-7], refs[-7:]
     me = lax.axis_index("tensor")
-    rank = wibuf.shape[0]
-    slots = buf.shape[2]
-    count = len(steps) * share
-    tokens = count * slots
+    rank, feat = wibuf.shape
+    slots, piece = buf.shape[2:]
     small = [
         pltpu.make_async_copy(wi, wibuf, wsem.at[0]),
         pltpu.make_async_copy(wo, wobuf, wsem.at[1]),
@@ -65,57 +57,65 @@
     copies = [
         [
             pltpu.make_async_copy(
-                (act, og)[side].at[pl.ds((me ^ step) * share, share), :, pl.ds(span.start, span.stop - span.start)],
-                buf.at[slot, pl.ds(i * share, share), :, pl.ds(0, span.stop - span.start)],
+                (act, og)[side].at[pl.ds((me ^ step) * share, share), :, pl.ds(at, width)],
+                buf.at[slot, pl.ds(i * share, share), :, pl.ds(0, width)],
                 sem.at[slot, i],
             )
             for i, step in enumerate(steps)
         ]
-        for slot, (side, span) in enumerate(pieces)
+        for slot, (side, at, width) in enumerate(pieces)
     ]
-    small[0].start()
-    for slot, group in enumerate(copies[:ahead]):
+    for copy in small:
+        copy.start()
+    for group in copies[:ahead]:
         for copy in group:
             copy.start()
-        if slot == 0:
-            small[1].start()
-            small[2].start()
-    sums = [None, None]
-    for slot, (side, span) in enumerate(pieces):
-        if span.start == 0:
-            small[side].wait()
+    for copy in small:
+        copy.wait()
+    for side, at, width in pieces:
+        weight = (wibuf, wobuf)[side][:, at : at + width]
+        none = jnp.zeros_like(weight)
+        both = jnp.concatenate([none, weight] if side else [weight, none], axis=0)
+        wide[side * feat + at : side * feat + at + width] = both.T
+    sums = [None] * len(steps)
+    for slot, (side, at, width) in enumerate(pieces):
         for copy in copies[slot]:
             copy.wait()
         for copy in copies[slot + ahead] if slot + ahead < len(copies) else ():
             copy.start()
-        token = buf[slot].reshape(tokens, buf.shape[3])[:, : span.stop - span.start]
-        part = lax.dot_general((wibuf, wobuf)[side][:, span], token, NT, preferred_element_type=jnp.float32)
-        sums[side] = part if sums[side] is None else sums[side] + part
-    small[2].wait()
-    col = lax.broadcasted_iota(jnp.int32, (rank, slots), 1)
+        weight = wide[side * feat + at : side * feat + at + width]
+        for i in range(len(steps)):
+            token = buf[slot, i * share : (i + 1) * share].reshape(share * slots, piece)[:, :width]
+            part = jnp.dot(token, weight, preferred_element_type=jnp.float32)
+            sums[i] = part if sums[i] is None else sums[i] + part
+    row = lax.broadcasted_iota(jnp.int32, (slots, 2 * rank), 0)
+    lane = lax.broadcasted_iota(jnp.int32, (slots, 2 * rank), 1)
     places = [out.at[i] for out in outs for i in range(out.shape[0])]
     for slot, out in enumerate(places):
-        length = lenbuf[(me ^ steps[slot // share]) * share + slot % share]
-        one = sums[0][:, slot * slots : (slot + 1) * slots] * (1.0 / length.astype(jnp.float32))
-        out[:rank] = jnp.where(col < length, one, 0.0)
-        out[rank:] = sums[1][:, slot * slots : (slot + 1) * slots]
-
-
-def project(act, og, wi, wo, lens, groups, share, ahead, piece, after=()):
+        i, k = divmod(slot, share)
+        length = lenbuf[(me ^ steps[i]) * share + k]
+        scale = jnp.where(lane < rank, 1.0 / length.astype(jnp.float32), 1.0)
+        out[...] = jnp.where(row < length, sums[i][k * slots : (k + 1) * slots] * scale, 0.0)
+
+
+def project(act, og, wi, wo, lens, groups, share, ahead, after=()):
     steps = [step for group in groups for step in group]
     count = len(steps) * share
     slots, feat, hidden = act.shape[1], act.shape[2], og.shape[2]
     rank = wi.shape[0]
-    pieces = [(0, span) for span in cut(feat, piece, piece)] + [(1, span) for span in cut(hidden, piece, 256)]
+    pieces = [
+        (side, at, min(PIECE, total - at)) for side, total in enumerate((feat, hidden)) for at in range(0, total, PIECE)
+    ]
     return pl.pallas_call(
         functools.partial(project_kernel, steps, share, ahead, pieces, len(after)),
-        out_shape=[jax.ShapeDtypeStruct((len(group) * share, 2 * rank, slots), jnp.float32) for group in groups],
+        out_shape=[jax.ShapeDtypeStruct((len(group) * share, slots, 2 * rank), jnp.float32) for group in groups],
         in_specs=[HBM] * 5 + [VMEM] * len(after),
         out_specs=[VMEM] * len(groups),
         scratch_shapes=[
-            pltpu.VMEM((len(pieces), count, slots, piece), act.dtype),
+            pltpu.VMEM((len(pieces), count, slots, PIECE), act.dtype),
             pltpu.VMEM((rank, feat), wi.dtype),
             pltpu.VMEM((rank, hidden), wo.dtype),
+            pltpu.VMEM((feat + hidden, 2 * rank), wo.dtype),
             pltpu.SMEM(lens.shape, lens.dtype),
             pltpu.SemaphoreType.DMA((len(pieces), len(steps))),
             pltpu.SemaphoreType.DMA((3,)),
@@ -136,6 +136,7 @@
         full = parts[0][k]
         for part in parts[1:]:
             full = full + part[k]
+        full = full.T
         high = full.astype(jnp.bfloat16)
         low = (full - high.astype(jnp.float32)).astype(jnp.bfloat16)
         left, right = slice(None, rank), slice(rank, None)
@@ -210,13 +211,13 @@
     far = [CORES * x for x in range(1, size // CORES)]
     arrays = (activations, out_grads, proj_in.T, proj_out.T, lengths)
     sends = [[step ^ 1 for step in far] + [1], far]
-    other, far_own = project(*arrays, sends, share, 2, 512, [own_tests])
+    other, far_own = project(*arrays, sends, share, 3, [own_tests])
     other = other + 0.0 * tests[1][:1, : other.shape[2]].astype(jnp.float32)
     arrived = xor_permute(other, "tensor", size, 1)
     cut_at = len(far) * share
     far_sum = far_own + arrived[:cut_at]
     sums = [xor_permute(far_sum[i * share : (i + 1) * share], "tensor", size, step) for i, step in enumerate(far)]
-    near_own = project(*arrays, [[0]], share, 4, 512, [far_sum])[0]
+    near_own = project(*arrays, [[0]], share, 6, [far_sum])[0]
 
     unit_outs = units([near_own, arrived[cut_at:]] + sums, share, rank, size)
     unit_parts = [unit_outs[0]] + [xor_permute(unit_outs[step], "tensor", size, step) for step in range(1, size)]

time: 35.7 us -> 35.8 us (level)
  Pallas kernels: 14.2 us -> 15.7 us
  waiting for transfers between devices: 9.27 us -> 8.09 us
    pallas_call x2, Pallas kernels: 12.4 us -> 13.8 us  [project(): pl.pallas_call(functools.partial(project_kernel, steps, share, ahead, pie...]
    ppermute x8, waiting for transfers between devices: 5.98 us -> 4.86 us  [xor_permute(): return lax.ppermute(value, axis, [(i, i ^ step) for i in range(size)])]
  transfers between devices with their start and end apart: 11 -> 11, of which waited for: 4 -> 4; matrix products, arithmetic and copies ran while one was open for 0% -> 0% of each run, Pallas kernels for 36% -> 40%
where the time goes in v12:
time: 35.8 us; the launch traced here: 35.7 us
  Pallas kernels  15.7 us (44%)
  starting transfers between devices  11.1 us (31%)
  waiting for transfers between devices  8.09 us (23%)
  other arithmetic  0.71 us (2%)
    pallas_call x2, Pallas kernels, project(): pl.pallas_call(functools.partial(project_kernel, steps, share, ahead, pie...  13.8 us
    ppermute x8, starting transfers between devices, xor_permute(): return lax.ppermute(value, axis, [(i, i ^ step) for i in range(size)])  5.91 us
    ppermute x3, starting transfers between devices, shift(): lax.ppermute(value, axis, [(i, (i + step) % size) for i in range(size)])  5.18 us
    ppermute x8, waiting for transfers between devices, xor_permute(): return lax.ppermute(value, axis, [(i, i ^ step) for i in range(size)])  4.86 us
    ppermute x3, waiting for transfers between devices, shift(): lax.ppermute(value, axis, [(i, (i + step) % size) for i in range(size)])  3.23 us
    pallas_call x1, Pallas kernels, cut_tests(): pl.pallas_call(cut_kernel, out_shape=jax.ShapeDtypeStruct((rows, width //...  0.96 us
  transfers between devices with their start and end apart: 11, of which 4 were waited for; matrix products, arithmetic and copies ran while one was open for 0% of the time, Pallas kernels for 40%

profile of v12, /device:TPU:0, one launch (start us, length us, event | category | flops | bytes accessed | tf_op | source)
XLA Modules:
  0.0 35.7 jit_solution(5058758072405786460)
XLA Ops:
  0.0 1.0 %shard_map.64.refs_0_.refs_4_ = bf16[128,1024]{1,0:T(8,128)(2,1)S(1)} custom-call(bf16[128,4096]{1,0:T(8,128)(2,1)} %tests.1), custom_call_target="tpu_custom_call" | custom-call | tf_op jit(solution)/shard_map/pallas_call | solution.py:32
  1.0 3.1 %collective-permute-start = (bf16[128,1024]{1,0:T(8,128)(2,1)S(1)}, bf16[128,1024]{1,0:T(8,128)(2,1)S(1)}, u32[]{:S(2)}, u32[]{:S(2)}) collective-permute-start(bf16[128,1024]{1,0:T(8,128)(2,1)S(1)} %shard_map.64.refs_0_.refs_4_), channel_id=1, source_target_pairs={{0,4},{4,8},{8,12},{12,0},{1,5},{5,9},{9,13},{13,1},{2,6},{6,10},{... | collective-permute-start | bytes 786440 | tf_op jit(solution)/shard_map/ppermute | solution.py:197
  4.0 8.8 %shard_map.65 = (f32[4,256,128]{2,1,0:T(8,128)S(1)}, f32[2,256,128]{2,1,0:T(8,128)S(1)}) custom-call(bf16[8,256,1024]{2,1,0:T(8,128)(2,1)} %act.3, bf16[8,256,3584]{2,1,0:T(8,128)(2,1)} %og.3, bf16[64,1024]{1,0:T(8,128)(2,1)} %bitcast.6, bf16[64,3584]{1,0:T(8,128)(2,1)} %bitcast.4, s32[8]{0:T(128)} %lens.3, bf16[128,1024]{1,0:T(8,128)(2,1)S(1)} %shard_map.64.refs_0_.refs_4_), custom_call_target="tpu_custom_call" | custom-call | flops 4294967296 | bytes 16777216 | tf_op jit(solution)/shard_map/pallas_call | solution.py:109
  12.8 0.0 collective-permute-done.refs_5_
  12.9 0.1 collective-permute-start.1
  13.0 2.1 %collective-permute-start.7 = (bf16[128,1024]{1,0:T(8,128)(2,1)S(1)}, bf16[128,1024]{1,0:T(8,128)(2,1)S(1)}, u32[]{:S(2)}, u32[]{:S(2)}) collective-permute-start(bf16[128,1024]{1,0:T(8,128)(2,1)S(1)} %shard_map.64.refs_0_.refs_4_), channel_id=1, source_target_pairs={{0,12},{4,0},{8,4},{12,8},{1,13},{5,1},{9,5},{13,9},{2,14},{6,2},{... | collective-permute-start | bytes 786440 | tf_op jit(solution)/shard_map/ppermute | solution.py:197
  15.1 0.0 collective-permute-start.6
  15.1 0.0 collective-permute-done.1
  15.1 0.1 fusion.2
  15.1 1.8 %collective-permute-start.2 = (f32[2,256,128]{2,1,0:T(8,128)S(1)}, f32[2,256,128]{2,1,0:T(8,128)S(1)}, u32[]{:S(2)}, u32[]{:S(2)}) collective-permute-start(f32[2,256,128]{2,1,0:T(8,128)S(1)} %get-tuple-element.18.refs_0_), channel_id=1, source_target_pairs={{0,2},{1,3},{2,0},{3,1},{4,6},{5,7},{6,4},{7,5},{8,10},{9,11},{10,... | collective-permute-start | bytes 786440 | tf_op jit(solution)/shard_map/ppermute | solution.py:19
  16.9 5.0 %shard_map.66.refs_0_ = f32[2,256,128]{2,1,0:T(8,128)S(1)} custom-call(bf16[8,256,1024]{2,1,0:T(8,128)(2,1)} %act.3, bf16[8,256,3584]{2,1,0:T(8,128)(2,1)} %og.3, bf16[64,1024]{1,0:T(8,128)(2,1)} %bitcast.7, bf16[64,3584]{1,0:T(8,128)(2,1)} %bitcast.5, s32[8]{0:T(128)} %lens.3, f32[2,256,128]{2,1,0:T(8,128)S(1)} %get-tuple-element.18.refs_0_), custom_call_target="tpu_custom_call" | custom-call | flops 4294967296 | bytes 16777216 | tf_op jit(solution)/shard_map/pallas_call | solution.py:109
  21.9 1.6 %collective-permute-done.2.refs_2_ = f32[2,256,128]{2,1,0:T(8,128)S(1)} collective-permute-done((f32[2,256,128]{2,1,0:T(8,128)S(1)}, f32[2,256,128]{2,1,0:T(8,128)S(1)}, u32[]{:S(2)}, u32[]{:S(2)}) %collective-permute-start.2) | collective-permute-done | bytes 262176 | tf_op jit(solution)/shard_map/ppermute | solution.py:19
  23.6 0.6 %shard_map.67 = (f32[2,8,128]{2,1,0:T(8,128)S(1)}, f32[2,8,128]{2,1,0:T(8,128)S(1)}, f32[2,8,128]{2,1,0:T(8,128)S(1)}, f32[2,8,128]{2,1,0:T(8,128)S(1)}) custom-call(f32[2,256,128]{2,1,0:T(8,128)S(1)} %shard_map.66.refs_0_, f32[2,256,128]{2,1,0:T(8,128)S(1)} %get-tuple-element.17.refs_1_, f32[2,256,128]{2,1,0:T(8,128)S(1)} %collective-permute-done.2.refs_2_), custom_call_target="tpu_custom_call" | custom-call | tf_op jit(solution)/shard_map/pallas_call | solution.py:158
  24.2 0.1 collective-permute-start.3
  24.2 1.8 %collective-permute-start.4 = (f32[2,8,128]{2,1,0:T(8,128)S(1)}, f32[2,8,128]{2,1,0:T(8,128)S(1)}, u32[]{:S(2)}, u32[]{:S(2)}) collective-permute-start(f32[2,8,128]{2,1,0:T(8,128)S(1)} %get-tuple-element.15), channel_id=1, source_target_pairs={{0,2},{1,3},{2,0},{3,1},{4,6},{5,7},{6,4},{7,5},{8,10},{9,11},{10,... | collective-permute-start | bytes 24584 | tf_op jit(solution)/shard_map/ppermute | solution.py:19
  26.0 0.1 collective-permute-start.5
  26.1 0.0 collective-permute-done.7.refs_7_
  26.1 3.2 %collective-permute-done.6.refs_6_ = bf16[128,1024]{1,0:T(8,128)(2,1)S(1)} collective-permute-done((bf16[128,1024]{1,0:T(8,128)(2,1)S(1)}, bf16[128,1024]{1,0:T(8,128)(2,1)S(1)}, u32[]{:S(2)}, u32[]{:S(2)}) %collective-permute-start.6) | collective-permute-done | bytes 262176 | tf_op jit(solution)/shard_map/ppermute | solution.py:197
  29.3 0.0 collective-permute-done.3.refs_1_
  29.3 0.0 collective-permute-done.4.refs_2_
  29.3 0.0 collective-permute-done.5.refs_3_
  29.3 0.4 %shard_map.68 = f32[8,512]{1,0:T(8,128)S(1)} custom-call(f32[2,8,128]{2,1,0:T(8,128)S(1)} %get-tuple-element.13.refs_0_, f32[2,8,128]{2,1,0:T(8,128)S(1)} %collective-permute-done.3.refs_1_, f32[2,8,128]{2,1,0:T(8,128)S(1)} %collective-permute-done.4.refs_2_, f32[2,8,128]{2,1,0:T(8,128)S(1)} %collective-permute-done.5.refs_3_, ...), custom_call_target="tpu_custom_call" | custom-call | tf_op jit(solution)/shard_map/pallas_call | solution.py:186
  29.7 0.8 %collective-permute-start.10 = (f32[8,512]{1,0:T(8,128)S(1)}, f32[8,512]{1,0:T(8,128)S(1)}, u32[]{:S(2)}, u32[]{:S(2)}) collective-permute-start(f32[8,512]{1,0:T(8,128)S(1)} %shard_map.68), channel_id=1, source_target_pairs={{0,3},{1,2},{2,1},{3,0},{4,7},{5,6},{6,5},{7,4},{8,11},{9,10},{10,... | collective-permute-start | bytes 49160 | tf_op jit(solution)/shard_map/ppermute | solution.py:19
  30.5 0.9 %collective-permute-start.8 = (f32[8,512]{1,0:T(8,128)S(1)}, f32[8,512]{1,0:T(8,128)S(1)}, u32[]{:S(2)}, u32[]{:S(2)}) collective-permute-start(f32[8,512]{1,0:T(8,128)S(1)} %shard_map.68), channel_id=1, source_target_pairs={{0,1},{1,0},{2,3},{3,2},{4,5},{5,4},{6,7},{7,6},{8,9},{9,8},{10,11... | collective-permute-start | bytes 49160 | tf_op jit(solution)/shard_map/ppermute | solution.py:19
  31.3 0.5 %collective-permute-start.9 = (f32[8,512]{1,0:T(8,128)S(1)}, f32[8,512]{1,0:T(8,128)S(1)}, u32[]{:S(2)}, u32[]{:S(2)}) collective-permute-start(f32[8,512]{1,0:T(8,128)S(1)} %shard_map.68), channel_id=1, source_target_pairs={{0,2},{1,3},{2,0},{3,1},{4,6},{5,7},{6,4},{7,5},{8,10},{9,11},{10,... | collective-permute-start | bytes 49160 | tf_op jit(solution)/shard_map/ppermute | solution.py:19
  31.9 1.0 %collective-permute-done.10 = f32[8,512]{1,0:T(8,128)S(1)} collective-permute-done((f32[8,512]{1,0:T(8,128)S(1)}, f32[8,512]{1,0:T(8,128)S(1)}, u32[]{:S(2)}, u32[]{:S(2)}) %collective-permute-start.10) | collective-permute-done | bytes 16416 | tf_op jit(solution)/shard_map/ppermute | solution.py:19
  32.9 0.0 collective-permute-done.8
  32.9 2.2 %collective-permute-done.9 = f32[8,512]{1,0:T(8,128)S(1)} collective-permute-done((f32[8,512]{1,0:T(8,128)S(1)}, f32[8,512]{1,0:T(8,128)S(1)}, u32[]{:S(2)}, u32[]{:S(2)}) %collective-permute-start.9) | collective-permute-done | bytes 16416 | tf_op jit(solution)/shard_map/ppermute | solution.py:19
  35.1 0.6 %add_add_fusion = f32[8,512]{1,0:T(8,128)} fusion(f32[8,512]{1,0:T(8,128)S(1)} %collective-permute-done.9, f32[8,512]{1,0:T(8,128)S(1)} %collective-permute-done.10, f32[8,512]{1,0:T(8,128)S(1)} %shard_map.68, f32[8,512]{1,0:T(8,128)S(1)} %collective-permute-done.8), kind=kLoop, calls=%fused_computation.2 | loop fusion | flops 12288 | bytes 81920 | tf_op jit(solution)/shard_map/add | solution.py:227
  (2 shorter events, 0.0 us)
Async XLA Ops:
  1.0 11.9 %collective-permute-start = (bf16[128,1024]{1,0:T(8,128)(2,1)S(1)}, bf16[128,1024]{1,0:T(8,128)(2,1)S(1)}, u32[]{:S(2)}, u32[]{:S(2)}) collective-permute-start(bf16[128,1024]{1,0:T(8,128)(2,1)S(1)} %shard_map.64.refs_0_.refs_4_), channel_id=1, source_target_pairs={{0,4},{4,8},{8,12},{12,0},{1,5},{5,9},{9,13},{13,1},{2,6},{6,10},{... | collective-permute-start | bytes 786440 | tf_op jit(solution)/shard_map/ppermute | solution.py:197
  12.9 2.2 %collective-permute-start.1 = (f32[4,256,128]{2,1,0:T(8,128)S(1)}, f32[4,256,128]{2,1,0:T(8,128)S(1)}, u32[]{:S(2)}, u32[]{:S(2)}) collective-permute-start(f32[4,256,128]{2,1,0:T(8,128)S(1)} %broadcast_add_fusion), channel_id=1, source_target_pairs={{0,1},{1,0},{2,3},{3,2},{4,5},{5,4},{6,7},{7,6},{8,9},{9,8},{10,11... | collective-permute-start | bytes 1572872 | tf_op jit(solution)/shard_map/ppermute | solution.py:19
  13.0 13.1 %collective-permute-start.7 = (bf16[128,1024]{1,0:T(8,128)(2,1)S(1)}, bf16[128,1024]{1,0:T(8,128)(2,1)S(1)}, u32[]{:S(2)}, u32[]{:S(2)}) collective-permute-start(bf16[128,1024]{1,0:T(8,128)(2,1)S(1)} %shard_map.64.refs_0_.refs_4_), channel_id=1, source_target_pairs={{0,12},{4,0},{8,4},{12,8},{1,13},{5,1},{9,5},{13,9},{2,14},{6,2},{... | collective-permute-start | bytes 786440 | tf_op jit(solution)/shard_map/ppermute | solution.py:197
  15.1 14.2 %collective-permute-start.6 = (bf16[128,1024]{1,0:T(8,128)(2,1)S(1)}, bf16[128,1024]{1,0:T(8,128)(2,1)S(1)}, u32[]{:S(2)}, u32[]{:S(2)}) collective-permute-start(bf16[128,1024]{1,0:T(8,128)(2,1)S(1)} %collective-permute-done.refs_5_), channel_id=1, source_target_pairs={{0,4},{4,8},{8,12},{12,0},{1,5},{5,9},{9,13},{13,1},{2,6},{6,10},{... | collective-permute-start | bytes 786440 | tf_op jit(solution)/shard_map/ppermute | solution.py:197
  15.1 8.4 %collective-permute-start.2 = (f32[2,256,128]{2,1,0:T(8,128)S(1)}, f32[2,256,128]{2,1,0:T(8,128)S(1)}, u32[]{:S(2)}, u32[]{:S(2)}) collective-permute-start(f32[2,256,128]{2,1,0:T(8,128)S(1)} %get-tuple-element.18.refs_0_), channel_id=1, source_target_pairs={{0,2},{1,3},{2,0},{3,1},{4,6},{5,7},{6,4},{7,5},{8,10},{9,11},{10,... | collective-permute-start | bytes 786440 | tf_op jit(solution)/shard_map/ppermute | solution.py:19
  24.2 5.2 %collective-permute-start.3 = (f32[2,8,128]{2,1,0:T(8,128)S(1)}, f32[2,8,128]{2,1,0:T(8,128)S(1)}, u32[]{:S(2)}, u32[]{:S(2)}) collective-permute-start(f32[2,8,128]{2,1,0:T(8,128)S(1)} %get-tuple-element.14), channel_id=1, source_target_pairs={{0,1},{1,0},{2,3},{3,2},{4,5},{5,4},{6,7},{7,6},{8,9},{9,8},{10,11... | collective-permute-start | bytes 24584 | tf_op jit(solution)/shard_map/ppermute | solution.py:19
  24.2 5.1 %collective-permute-start.4 = (f32[2,8,128]{2,1,0:T(8,128)S(1)}, f32[2,8,128]{2,1,0:T(8,128)S(1)}, u32[]{:S(2)}, u32[]{:S(2)}) collective-permute-start(f32[2,8,128]{2,1,0:T(8,128)S(1)} %get-tuple-element.15), channel_id=1, source_target_pairs={{0,2},{1,3},{2,0},{3,1},{4,6},{5,7},{6,4},{7,5},{8,10},{9,11},{10,... | collective-permute-start | bytes 24584 | tf_op jit(solution)/shard_map/ppermute | solution.py:19
  26.0 3.4 %collective-permute-start.5 = (f32[2,8,128]{2,1,0:T(8,128)S(1)}, f32[2,8,128]{2,1,0:T(8,128)S(1)}, u32[]{:S(2)}, u32[]{:S(2)}) collective-permute-start(f32[2,8,128]{2,1,0:T(8,128)S(1)} %get-tuple-element.16), channel_id=1, source_target_pairs={{0,3},{1,2},{2,1},{3,0},{4,7},{5,6},{6,5},{7,4},{8,11},{9,10},{10,... | collective-permute-start | bytes 24584 | tf_op jit(solution)/shard_map/ppermute | solution.py:19
  29.7 3.2 %collective-permute-start.10 = (f32[8,512]{1,0:T(8,128)S(1)}, f32[8,512]{1,0:T(8,128)S(1)}, u32[]{:S(2)}, u32[]{:S(2)}) collective-permute-start(f32[8,512]{1,0:T(8,128)S(1)} %shard_map.68), channel_id=1, source_target_pairs={{0,3},{1,2},{2,1},{3,0},{4,7},{5,6},{6,5},{7,4},{8,11},{9,10},{10,... | collective-permute-start | bytes 49160 | tf_op jit(solution)/shard_map/ppermute | solution.py:19
  30.5 2.4 %collective-permute-start.8 = (f32[8,512]{1,0:T(8,128)S(1)}, f32[8,512]{1,0:T(8,128)S(1)}, u32[]{:S(2)}, u32[]{:S(2)}) collective-permute-start(f32[8,512]{1,0:T(8,128)S(1)} %shard_map.68), channel_id=1, source_target_pairs={{0,1},{1,0},{2,3},{3,2},{4,5},{5,4},{6,7},{7,6},{8,9},{9,8},{10,11... | collective-permute-start | bytes 49160 | tf_op jit(solution)/shard_map/ppermute | solution.py:19
  31.3 3.7 %collective-permute-start.9 = (f32[8,512]{1,0:T(8,128)S(1)}, f32[8,512]{1,0:T(8,128)S(1)}, u32[]{:S(2)}, u32[]{:S(2)}) collective-permute-start(f32[8,512]{1,0:T(8,128)S(1)} %shard_map.68), channel_id=1, source_target_pairs={{0,2},{1,3},{2,0},{3,1},{4,6},{5,7},{6,4},{7,5},{8,10},{9,11},{10,... | collective-permute-start | bytes 49160 | tf_op jit(solution)/shard_map/ppermute | solution.py:19

commit v13 on v8

--- a/solution.py
+++ b/solution.py
@@ -125,7 +125,8 @@
 
 
 def unit_kernel(share, rank, size, *refs):
-    parts, outs, pairs, held = refs[:-4], refs[-4:-2], refs[-2], refs[-1]
+    parts, outs = refs[: -2 - size], refs[-2 - size : -2]
+    pairs, held = refs[-2:]
     me = lax.axis_index("tensor")
     rows = rank * rank // 128
     span = rows // size
@@ -145,32 +146,29 @@
         scale = jnp.sqrt(jnp.sum(flat * flat) / (rank * rank) + 1e-06)
         unit = flat / scale
         for to in range(size):
-            held[to, k] = unit[to * span : (to + 1) * span]
-    for j in range(size // CORES):
-        for core in range(CORES):
-            outs[core][j] = held[me ^ core ^ (CORES * j)]
+            held[to] = unit[to * span : (to + 1) * span]
+        for step in range(size):
+            outs[step][k] = held[me ^ step]
 
 
 def units(parts, share, rank, size):
     span = rank * rank // 128 // size
     return pl.pallas_call(
         functools.partial(unit_kernel, share, rank, size),
-        out_shape=[jax.ShapeDtypeStruct((size // CORES, share, span, 128), jnp.float32)] * CORES,
+        out_shape=[jax.ShapeDtypeStruct((share, span, 128), jnp.float32)] * size,
         in_specs=[VMEM] * len(parts),
-        out_specs=[VMEM] * CORES,
-        scratch_shapes=[pltpu.VMEM((share, rank, rank), jnp.float32), pltpu.VMEM((size, share, span, 128), jnp.float32)],
+        out_specs=[VMEM] * size,
+        scratch_shapes=[pltpu.VMEM((share, rank, rank), jnp.float32), pltpu.VMEM((size, span, 128), jnp.float32)],
         compiler_params=SMALL,
     )(*parts)
 
 
-def score_kernel(share, far, shifts, own_ref, core_ref, *refs):
-    far_refs, test_refs, out, held = refs[: len(far)], refs[len(far) : -2], refs[-2], refs[-1]
+def score_kernel(share, size, shifts, *refs):
+    unit_refs, test_refs, out, held = refs[:size], refs[size:-2], refs[-2], refs[-1]
     me, dp = lax.axis_index("tensor"), lax.axis_index("dp")
-    blocks = [(me, own_ref.at[0]), (me ^ 1, core_ref.at[0])]
-    blocks += [(me ^ step ^ core, ref.at[core]) for step, ref in zip(far, far_refs) for core in range(CORES)]
-    for owner, ref in blocks:
+    for step in range(size):
         for k in range(share):
-            held[owner * share + k] = ref[k]
+            held[(me ^ step) * share + k] = unit_refs[step][k]
     unit = jnp.concatenate([held[:, c, :] for c in range(held.shape[1])], axis=1).astype(jnp.bfloat16)
     tests = test_refs[0].shape[0]
     for step, test_ref in zip(shifts, test_refs):
@@ -179,16 +177,18 @@
         out[:, pl.ds(pl.multiple_of(at, 128), tests)] = part
 
 
-def score(own, core, far_units, test_parts, share, size):
+def score(unit_parts, test_parts, share):
+    size, groups = len(unit_parts), len(test_parts)
     tests, width = test_parts[0].shape
-    return pl.pallas_call(
-        functools.partial(score_kernel, share, tuple(far_units), tuple(test_parts)),
-        out_shape=jax.ShapeDtypeStruct((share * size, tests * len(test_parts)), jnp.float32),
-        in_specs=[VMEM] * (2 + len(far_units) + len(test_parts)),
+    shifts = tuple(test_parts)
+    return pl.pallas_call(
+        functools.partial(score_kernel, share, size, shifts),
+        out_shape=jax.ShapeDtypeStruct((share * size, tests * groups), jnp.float32),
+        in_specs=[VMEM] * (size + groups),
         out_specs=VMEM,
         scratch_shapes=[pltpu.VMEM((share * size, width // 128, 128), jnp.float32)],
         compiler_params=SMALL,
-    )(own, core, *far_units.values(), *test_parts.values())
+    )(*unit_parts, *test_parts.values())
 
 
 def shift(value, axis, size, step):
@@ -208,23 +208,17 @@
 
     far = [CORES * x for x in range(1, size // CORES)]
     arrays = (activations, out_grads, proj_in.T, proj_out.T, lengths)
-    sends = [[step ^ 1 for step in far] + [1], far]
-    other, far_own = project(*arrays, sends, share, 3, 512, [own_tests])
-    other = other + 0.0 * tests[1][:1, : other.shape[2]].astype(jnp.float32)
-    arrived = xor_permute(other, "tensor", size, 1)
-    cut = len(far) * share
-    far_sum = far_own + arrived[:cut]
+    far_other, far_own = project(*arrays, [[step ^ 1 for step in far], far], share, 4, 512, [own_tests])
+    far_sum = far_own + xor_permute(far_other, "tensor", size, 1)
     sums = [xor_permute(far_sum[i * share : (i + 1) * share], "tensor", size, step) for i, step in enumerate(far)]
-    near_own = project(*arrays, [[0]], share, 4, 1024, [far_sum])[0]
-
-    own, core = units([near_own, arrived[cut:]] + sums, share, rank, size)
-    core = xor_permute(core, "tensor", size, 1)
-    far_units = {
-        step: xor_permute(jnp.stack([own[j + 1], core[j + 1]]), "tensor", size, step) for j, step in enumerate(far)
-    }
-    part = score(own, core, far_units, tests, share, size)
-    part = part + xor_permute(part, "tensor", size, 1)
-    parts = [part] + [xor_permute(part, "tensor", size, step) for step in far]
+    here = xor_permute(tests[1][:16, :128], "tensor", size, 1)
+    near_other, near_own = project(*arrays, [[1], [0]], share, 4, 512, [far_sum, here])
+    arrived = jnp.concatenate([xor_permute(near_other[k : k + 1], "tensor", size, 1) for k in range(share)])
+
+    unit_outs = units([near_own, arrived] + sums, share, rank, size)
+    unit_parts = [unit_outs[0]] + [xor_permute(unit_outs[step], "tensor", size, step) for step in range(1, size)]
+    part = score(unit_parts, tests, share)
+    parts = [part] + [xor_permute(part, "tensor", size, step) for step in range(1, size)]
     while len(parts) > 1:
         parts = [parts[i] + parts[i + 1] for i in range(0, len(parts), 2)]
     return parts[0]

time: 34.5 us -> 33.5 us (0.971)
  waiting for transfers between devices: 11 us -> 8.97 us
  starting transfers between devices: 9.84 us -> 11.1 us
    ppermute x6 -> x11, waiting for transfers between devices: 8.3 us -> 4.6 us  [xor_permute(): return lax.ppermute(value, axis, [(i, i ^ step) for i in range(size)])]
    ppermute x3, waiting for transfers between devices: 2.74 us -> 4.37 us  [shift(): lax.ppermute(value, axis, [(i, (i + step) % size) for i in range(size)])]
    ppermute x6 -> x11, starting transfers between devices: 4.68 us -> 6 us  [xor_permute(): return lax.ppermute(value, axis, [(i, i ^ step) for i in range(size)])]
  transfers between devices with their start and end apart: 9 -> 14, of which waited for: 7 -> 8; matrix products, arithmetic and copies ran while one was open for 0% -> 0% of each run, Pallas kernels for 33% -> 33%
where the time goes in v13:
time: 33.5 us; the launch traced here: 33.3 us
  Pallas kernels  12.5 us (37%)
  starting transfers between devices  11.1 us (33%)
  waiting for transfers between devices  8.97 us (27%)
  other arithmetic  0.67 us (2%)
    pallas_call x2, Pallas kernels, project(): pl.pallas_call(functools.partial(project_kernel, steps, share, ahead, pie...  10.6 us
    ppermute x11, starting transfers between devices, xor_permute(): return lax.ppermute(value, axis, [(i, i ^ step) for i in range(size)])  6 us
    ppermute x3, starting transfers between devices, shift(): lax.ppermute(value, axis, [(i, (i + step) % size) for i in range(size)])  5.1 us
    ppermute x11, waiting for transfers between devices, xor_permute(): return lax.ppermute(value, axis, [(i, i ^ step) for i in range(size)])  4.6 us
    ppermute x3, waiting for transfers between devices, shift(): lax.ppermute(value, axis, [(i, (i + step) % size) for i in range(size)])  4.37 us
    pallas_call x1, Pallas kernels, cut_tests(): pl.pallas_call(cut_kernel, out_shape=jax.ShapeDtypeStruct((rows, width //...  0.96 us
  transfers between devices with their start and end apart: 14, of which 8 were waited for; matrix products, arithmetic and copies ran while one was open for 0% of the time, Pallas kernels for 33%

profile of v13, /device:TPU:0, one launch (start us, length us, event | category | flops | bytes accessed | tf_op | source)
XLA Modules:
  0.0 33.3 jit_solution(1141601130124354338)
XLA Ops:
  0.0 1.0 %shard_map.64.refs_0_.refs_4_ = bf16[128,1024]{1,0:T(8,128)(2,1)S(1)} custom-call(bf16[128,4096]{1,0:T(8,128)(2,1)} %tests.1), custom_call_target="tpu_custom_call" | custom-call | tf_op jit(solution)/shard_map/pallas_call | solution.py:32
  1.0 3.1 %collective-permute-start.1 = (bf16[128,1024]{1,0:T(8,128)(2,1)S(1)}, bf16[128,1024]{1,0:T(8,128)(2,1)S(1)}, u32[]{:S(2)}, u32[]{:S(2)}) collective-permute-start(bf16[128,1024]{1,0:T(8,128)(2,1)S(1)} %shard_map.64.refs_0_.refs_4_), channel_id=1, source_target_pairs={{0,4},{4,8},{8,12},{12,0},{1,5},{5,9},{9,13},{13,1},{2,6},{6,10},{... | collective-permute-start | bytes 786440 | tf_op jit(solution)/shard_map/ppermute | solution.py:195
  4.0 5.3 %shard_map.65 = (f32[2,128,256]{2,1,0:T(8,128)S(1)}, f32[2,128,256]{2,1,0:T(8,128)S(1)}) custom-call(bf16[8,256,1024]{2,1,0:T(8,128)(2,1)} %act.3, bf16[8,256,3584]{2,1,0:T(8,128)(2,1)} %og.3, bf16[64,1024]{1,0:T(8,128)(2,1)} %bitcast.4, bf16[64,3584]{1,0:T(8,128)(2,1)} %bitcast.2, s32[8]{0:T(128)} %lens.3, bf16[128,1024]{1,0:T(8,128)(2,1)S(1)} %shard_map.64.refs_0_.refs_4_), custom_call_target="tpu_custom_call" | custom-call | flops 4294967296 | bytes 16777216 | tf_op jit(solution)/shard_map/pallas_call | solution.py:109
  9.4 0.1 collective-permute-start
  9.4 2.9 %collective-permute-done.1.refs_5_ = bf16[128,1024]{1,0:T(8,128)(2,1)S(1)} collective-permute-done((bf16[128,1024]{1,0:T(8,128)(2,1)S(1)}, bf16[128,1024]{1,0:T(8,128)(2,1)S(1)}, u32[]{:S(2)}, u32[]{:S(2)}) %collective-permute-start.1) | collective-permute-done | bytes 262176 | tf_op jit(solution)/shard_map/ppermute | solution.py:195
  12.4 0.0 collective-permute-start.2
  12.4 1.7 %collective-permute-start.10 = (bf16[128,1024]{1,0:T(8,128)(2,1)S(1)}, bf16[128,1024]{1,0:T(8,128)(2,1)S(1)}, u32[]{:S(2)}, u32[]{:S(2)}) collective-permute-start(bf16[128,1024]{1,0:T(8,128)(2,1)S(1)} %shard_map.64.refs_0_.refs_4_), channel_id=1, source_target_pairs={{0,12},{4,0},{8,4},{12,8},{1,13},{5,1},{9,5},{13,9},{2,14},{6,2},{... | collective-permute-start | bytes 786440 | tf_op jit(solution)/shard_map/ppermute | solution.py:195
  14.1 0.0 collective-permute-done
  14.2 1.6 %collective-permute-start.5 = (f32[2,128,256]{2,1,0:T(8,128)S(1)}, f32[2,128,256]{2,1,0:T(8,128)S(1)}, u32[]{:S(2)}, u32[]{:S(2)}) collective-permute-start(f32[2,128,256]{2,1,0:T(8,128)S(1)} %add.12.refs_0_), channel_id=1, source_target_pairs={{0,2},{1,3},{2,0},{3,1},{4,6},{5,7},{6,4},{7,5},{8,10},{9,11},{10,... | collective-permute-start | bytes 786440 | tf_op jit(solution)/shard_map/ppermute | solution.py:19
  15.7 0.3 collective-permute-start.9
  16.0 5.3 %shard_map.66 = (f32[2,128,256]{2,1,0:T(8,128)S(1)}, f32[2,128,256]{2,1,0:T(8,128)S(1)}) custom-call(bf16[8,256,1024]{2,1,0:T(8,128)(2,1)} %act.3, bf16[8,256,3584]{2,1,0:T(8,128)(2,1)} %og.3, bf16[64,1024]{1,0:T(8,128)(2,1)} %bitcast.5, bf16[64,3584]{1,0:T(8,128)(2,1)} %bitcast.3, s32[8]{0:T(128)} %lens.3, f32[2,128,256]{2,1,0:T(8,128)S(1)} %add.12.refs_0_, ...), custom_call_target="tpu_custom_call" | custom-call | flops 4294967296 | bytes 16777216 | tf_op jit(solution)/shard_map/pallas_call | solution.py:109
  21.4 0.1 collective-permute-start.3
  21.4 0.5 %collective-permute-start.4 = (f32[1,128,256]{2,1,0:T(8,128)S(1)}, f32[1,128,256]{2,1,0:T(8,128)S(1)}, u32[]{:S(2)}, u32[]{:S(2)}) collective-permute-start(f32[1,128,256]{2,1,0:T(8,128)S(1)} %get-tuple-element.22), channel_id=1, source_target_pairs={{0,1},{1,0},{2,3},{3,2},{4,5},{5,4},{6,7},{7,6},{8,9},{9,8},{10,11... | collective-permute-start | bytes 393224 | tf_op jit(solution)/shard_map/ppermute | solution.py:19
  21.9 0.8 %collective-permute-done.3 = f32[1,128,256]{2,1,0:T(8,128)S(1)} collective-permute-done((f32[1,128,256]{2,1,0:T(8,128)S(1)}, f32[1,128,256]{2,1,0:T(8,128)S(1)}, u32[]{:S(2)}, u32[]{:S(2)}) %collective-permute-start.3) | collective-permute-done | bytes 131104 | tf_op jit(solution)/shard_map/ppermute | solution.py:19
  22.8 0.2 collective-permute-done.4
  23.0 0.0 collective-permute-done.5.refs_2_
  23.0 0.5 %shard_map.67 = (f32[2,8,128]{2,1,0:T(8,128)S(1)}, f32[2,8,128]{2,1,0:T(8,128)S(1)}, f32[2,8,128]{2,1,0:T(8,128)S(1)}, f32[2,8,128]{2,1,0:T(8,128)S(1)}) custom-call(f32[2,128,256]{2,1,0:T(8,128)S(1)} %get-tuple-element.15.refs_0_, f32[2,128,256]{2,1,0:T(8,128)S(1)} %pad_maximum_fusion.refs_1_, f32[2,128,256]{2,1,0:T(8,128)S(1)} %collective-permute-done.5.refs_2_), custom_call_target="tpu_custom_call" | custom-call | tf_op jit(solution)/shard_map/pallas_call | solution.py:156
  23.5 0.4 %collective-permute-start.6 = (f32[2,8,128]{2,1,0:T(8,128)S(1)}, f32[2,8,128]{2,1,0:T(8,128)S(1)}, u32[]{:S(2)}, u32[]{:S(2)}) collective-permute-start(f32[2,8,128]{2,1,0:T(8,128)S(1)} %get-tuple-element.18), channel_id=1, source_target_pairs={{0,1},{1,0},{2,3},{3,2},{4,5},{5,4},{6,7},{7,6},{8,9},{9,8},{10,11... | collective-permute-start | bytes 24584 | tf_op jit(solution)/shard_map/ppermute | solution.py:19
  23.9 0.9 %collective-permute-start.7 = (f32[2,8,128]{2,1,0:T(8,128)S(1)}, f32[2,8,128]{2,1,0:T(8,128)S(1)}, u32[]{:S(2)}, u32[]{:S(2)}) collective-permute-start(f32[2,8,128]{2,1,0:T(8,128)S(1)} %get-tuple-element.19), channel_id=1, source_target_pairs={{0,2},{1,3},{2,0},{3,1},{4,6},{5,7},{6,4},{7,5},{8,10},{9,11},{10,... | collective-permute-start | bytes 24584 | tf_op jit(solution)/shard_map/ppermute | solution.py:19
  24.8 0.6 %collective-permute-start.8 = (f32[2,8,128]{2,1,0:T(8,128)S(1)}, f32[2,8,128]{2,1,0:T(8,128)S(1)}, u32[]{:S(2)}, u32[]{:S(2)}) collective-permute-start(f32[2,8,128]{2,1,0:T(8,128)S(1)} %get-tuple-element.20), channel_id=1, source_target_pairs={{0,3},{1,2},{2,1},{3,0},{4,7},{5,6},{6,5},{7,4},{8,11},{9,10},{10,... | collective-permute-start | bytes 24584 | tf_op jit(solution)/shard_map/ppermute | solution.py:19
  25.4 0.0 collective-permute-done.10.refs_7_
  25.4 1.4 %collective-permute-done.9.refs_6_ = bf16[128,1024]{1,0:T(8,128)(2,1)S(1)} collective-permute-done((bf16[128,1024]{1,0:T(8,128)(2,1)S(1)}, bf16[128,1024]{1,0:T(8,128)(2,1)S(1)}, u32[]{:S(2)}, u32[]{:S(2)}) %collective-permute-start.9) | collective-permute-done | bytes 262176 | tf_op jit(solution)/shard_map/ppermute | solution.py:195
  26.9 0.0 collective-permute-done.6.refs_1_
  26.9 0.7 %collective-permute-done.7.refs_2_ = f32[2,8,128]{2,1,0:T(8,128)S(1)} collective-permute-done((f32[2,8,128]{2,1,0:T(8,128)S(1)}, f32[2,8,128]{2,1,0:T(8,128)S(1)}, u32[]{:S(2)}, u32[]{:S(2)}) %collective-permute-start.7) | collective-permute-done | bytes 8224 | tf_op jit(solution)/shard_map/ppermute | solution.py:19
  27.5 0.3 %collective-permute-done.8.refs_3_ = f32[2,8,128]{2,1,0:T(8,128)S(1)} collective-permute-done((f32[2,8,128]{2,1,0:T(8,128)S(1)}, f32[2,8,128]{2,1,0:T(8,128)S(1)}, u32[]{:S(2)}, u32[]{:S(2)}) %collective-permute-start.8) | collective-permute-done | bytes 8224 | tf_op jit(solution)/shard_map/ppermute | solution.py:19
  27.9 0.4 %shard_map.68 = f32[8,512]{1,0:T(8,128)S(1)} custom-call(f32[2,8,128]{2,1,0:T(8,128)S(1)} %get-tuple-element.17.refs_0_, f32[2,8,128]{2,1,0:T(8,128)S(1)} %collective-permute-done.6.refs_1_, f32[2,8,128]{2,1,0:T(8,128)S(1)} %collective-permute-done.7.refs_2_, f32[2,8,128]{2,1,0:T(8,128)S(1)} %collective-permute-done.8.refs_3_, ...), custom_call_target="tpu_custom_call" | custom-call | tf_op jit(solution)/shard_map/pallas_call | solution.py:184
  28.3 0.2 collective-permute-start.11
  28.5 1.1 %collective-permute-start.12 = (f32[8,512]{1,0:T(8,128)S(1)}, f32[8,512]{1,0:T(8,128)S(1)}, u32[]{:S(2)}, u32[]{:S(2)}) collective-permute-start(f32[8,512]{1,0:T(8,128)S(1)} %shard_map.68), channel_id=1, source_target_pairs={{0,2},{1,3},{2,0},{3,1},{4,6},{5,7},{6,4},{7,5},{8,10},{9,11},{10,... | collective-permute-start | bytes 49160 | tf_op jit(solution)/shard_map/ppermute | solution.py:19
  29.5 0.6 %collective-permute-start.13 = (f32[8,512]{1,0:T(8,128)S(1)}, f32[8,512]{1,0:T(8,128)S(1)}, u32[]{:S(2)}, u32[]{:S(2)}) collective-permute-start(f32[8,512]{1,0:T(8,128)S(1)} %shard_map.68), channel_id=1, source_target_pairs={{0,3},{1,2},{2,1},{3,0},{4,7},{5,6},{6,5},{7,4},{8,11},{9,10},{10,... | collective-permute-start | bytes 49160 | tf_op jit(solution)/shard_map/ppermute | solution.py:19
  30.2 2.0 %collective-permute-done.12 = f32[8,512]{1,0:T(8,128)S(1)} collective-permute-done((f32[8,512]{1,0:T(8,128)S(1)}, f32[8,512]{1,0:T(8,128)S(1)}, u32[]{:S(2)}, u32[]{:S(2)}) %collective-permute-start.12) | collective-permute-done | bytes 16416 | tf_op jit(solution)/shard_map/ppermute | solution.py:19
  32.2 0.5 %collective-permute-done.13 = f32[8,512]{1,0:T(8,128)S(1)} collective-permute-done((f32[8,512]{1,0:T(8,128)S(1)}, f32[8,512]{1,0:T(8,128)S(1)}, u32[]{:S(2)}, u32[]{:S(2)}) %collective-permute-start.13) | collective-permute-done | bytes 16416 | tf_op jit(solution)/shard_map/ppermute | solution.py:19
  32.7 0.6 %add_add_fusion = f32[8,512]{1,0:T(8,128)} fusion(f32[8,512]{1,0:T(8,128)S(1)} %collective-permute-done.12, f32[8,512]{1,0:T(8,128)S(1)} %collective-permute-done.13, f32[8,512]{1,0:T(8,128)S(1)} %shard_map.68, f32[8,512]{1,0:T(8,128)S(1)} %collective-permute-done.11), kind=kLoop, calls=%fused_computation.1 | loop fusion | flops 12288 | bytes 81920 | tf_op jit(solution)/shard_map/add | solution.py:223
  (6 shorter events, 0.1 us)
Async XLA Ops:
  1.0 11.4 %collective-permute-start.1 = (bf16[128,1024]{1,0:T(8,128)(2,1)S(1)}, bf16[128,1024]{1,0:T(8,128)(2,1)S(1)}, u32[]{:S(2)}, u32[]{:S(2)}) collective-permute-start(bf16[128,1024]{1,0:T(8,128)(2,1)S(1)} %shard_map.64.refs_0_.refs_4_), channel_id=1, source_target_pairs={{0,4},{4,8},{8,12},{12,0},{1,5},{5,9},{9,13},{13,1},{2,6},{6,10},{... | collective-permute-start | bytes 786440 | tf_op jit(solution)/shard_map/ppermute | solution.py:195
  9.4 4.8 %collective-permute-start = (f32[2,128,256]{2,1,0:T(8,128)S(1)}, f32[2,128,256]{2,1,0:T(8,128)S(1)}, u32[]{:S(2)}, u32[]{:S(2)}) collective-permute-start(f32[2,128,256]{2,1,0:T(8,128)S(1)} %get-tuple-element.14), channel_id=1, source_target_pairs={{0,1},{1,0},{2,3},{3,2},{4,5},{5,4},{6,7},{7,6},{8,9},{9,8},{10,11... | collective-permute-start | bytes 786440 | tf_op jit(solution)/shard_map/ppermute | solution.py:19
  12.4 3.6 %collective-permute-start.2 = (bf16[16,128]{1,0:T(8,128)(2,1)S(1)}, bf16[16,128]{1,0:T(8,128)(2,1)S(1)}, u32[]{:S(2)}, u32[]{:S(2)}) collective-permute-start(bf16[16,128]{1,0:T(8,128)(2,1)S(1)} %slice.12), channel_id=1, source_target_pairs={{0,1},{1,0},{2,3},{3,2},{4,5},{5,4},{6,7},{7,6},{8,9},{9,8},{10,11... | collective-permute-start | bytes 12296 | tf_op jit(solution)/shard_map/ppermute | solution.py:19
  12.4 13.1 %collective-permute-start.10 = (bf16[128,1024]{1,0:T(8,128)(2,1)S(1)}, bf16[128,1024]{1,0:T(8,128)(2,1)S(1)}, u32[]{:S(2)}, u32[]{:S(2)}) collective-permute-start(bf16[128,1024]{1,0:T(8,128)(2,1)S(1)} %shard_map.64.refs_0_.refs_4_), channel_id=1, source_target_pairs={{0,12},{4,0},{8,4},{12,8},{1,13},{5,1},{9,5},{13,9},{2,14},{6,2},{... | collective-permute-start | bytes 786440 | tf_op jit(solution)/shard_map/ppermute | solution.py:195
  14.2 8.8 %collective-permute-start.5 = (f32[2,128,256]{2,1,0:T(8,128)S(1)}, f32[2,128,256]{2,1,0:T(8,128)S(1)}, u32[]{:S(2)}, u32[]{:S(2)}) collective-permute-start(f32[2,128,256]{2,1,0:T(8,128)S(1)} %add.12.refs_0_), channel_id=1, source_target_pairs={{0,2},{1,3},{2,0},{3,1},{4,6},{5,7},{6,4},{7,5},{8,10},{9,11},{10,... | collective-permute-start | bytes 786440 | tf_op jit(solution)/shard_map/ppermute | solution.py:19
  15.7 11.2 %collective-permute-start.9 = (bf16[128,1024]{1,0:T(8,128)(2,1)S(1)}, bf16[128,1024]{1,0:T(8,128)(2,1)S(1)}, u32[]{:S(2)}, u32[]{:S(2)}) collective-permute-start(bf16[128,1024]{1,0:T(8,128)(2,1)S(1)} %collective-permute-done.1.refs_5_), channel_id=1, source_target_pairs={{0,4},{4,8},{8,12},{12,0},{1,5},{5,9},{9,13},{13,1},{2,6},{6,10},{... | collective-permute-start | bytes 786440 | tf_op jit(solution)/shard_map/ppermute | solution.py:195
  21.4 1.4 %collective-permute-start.3 = (f32[1,128,256]{2,1,0:T(8,128)S(1)}, f32[1,128,256]{2,1,0:T(8,128)S(1)}, u32[]{:S(2)}, u32[]{:S(2)}) collective-permute-start(f32[1,128,256]{2,1,0:T(8,128)S(1)} %get-tuple-element.21), channel_id=1, source_target_pairs={{0,1},{1,0},{2,3},{3,2},{4,5},{5,4},{6,7},{7,6},{8,9},{9,8},{10,11... | collective-permute-start | bytes 393224 | tf_op jit(solution)/shard_map/ppermute | solution.py:19
  21.4 1.5 %collective-permute-start.4 = (f32[1,128,256]{2,1,0:T(8,128)S(1)}, f32[1,128,256]{2,1,0:T(8,128)S(1)}, u32[]{:S(2)}, u32[]{:S(2)}) collective-permute-start(f32[1,128,256]{2,1,0:T(8,128)S(1)} %get-tuple-element.22), channel_id=1, source_target_pairs={{0,1},{1,0},{2,3},{3,2},{4,5},{5,4},{6,7},{7,6},{8,9},{9,8},{10,11... | collective-permute-start | bytes 393224 | tf_op jit(solution)/shard_map/ppermute | solution.py:19
  23.5 3.4 %collective-permute-start.6 = (f32[2,8,128]{2,1,0:T(8,128)S(1)}, f32[2,8,128]{2,1,0:T(8,128)S(1)}, u32[]{:S(2)}, u32[]{:S(2)}) collective-permute-start(f32[2,8,128]{2,1,0:T(8,128)S(1)} %get-tuple-element.18), channel_id=1, source_target_pairs={{0,1},{1,0},{2,3},{3,2},{4,5},{5,4},{6,7},{7,6},{8,9},{9,8},{10,11... | collective-permute-start | bytes 24584 | tf_op jit(solution)/shard_map/ppermute | solution.py:19
  23.9 3.7 %collective-permute-start.7 = (f32[2,8,128]{2,1,0:T(8,128)S(1)}, f32[2,8,128]{2,1,0:T(8,128)S(1)}, u32[]{:S(2)}, u32[]{:S(2)}) collective-permute-start(f32[2,8,128]{2,1,0:T(8,128)S(1)} %get-tuple-element.19), channel_id=1, source_target_pairs={{0,2},{1,3},{2,0},{3,1},{4,6},{5,7},{6,4},{7,5},{8,10},{9,11},{10,... | collective-permute-start | bytes 24584 | tf_op jit(solution)/shard_map/ppermute | solution.py:19
  24.8 3.1 %collective-permute-start.8 = (f32[2,8,128]{2,1,0:T(8,128)S(1)}, f32[2,8,128]{2,1,0:T(8,128)S(1)}, u32[]{:S(2)}, u32[]{:S(2)}) collective-permute-start(f32[2,8,128]{2,1,0:T(8,128)S(1)} %get-tuple-element.20), channel_id=1, source_target_pairs={{0,3},{1,2},{2,1},{3,0},{4,7},{5,6},{6,5},{7,4},{8,11},{9,10},{10,... | collective-permute-start | bytes 24584 | tf_op jit(solution)/shard_map/ppermute | solution.py:19
  28.3 1.9 %collective-permute-start.11 = (f32[8,512]{1,0:T(8,128)S(1)}, f32[8,512]{1,0:T(8,128)S(1)}, u32[]{:S(2)}, u32[]{:S(2)}) collective-permute-start(f32[8,512]{1,0:T(8,128)S(1)} %shard_map.68), channel_id=1, source_target_pairs={{0,1},{1,0},{2,3},{3,2},{4,5},{5,4},{6,7},{7,6},{8,9},{9,8},{10,11... | collective-permute-start | bytes 49160 | tf_op jit(solution)/shard_map/ppermute | solution.py:19
  28.5 3.7 %collective-permute-start.12 = (f32[8,512]{1,0:T(8,128)S(1)}, f32[8,512]{1,0:T(8,128)S(1)}, u32[]{:S(2)}, u32[]{:S(2)}) collective-permute-start(f32[8,512]{1,0:T(8,128)S(1)} %shard_map.68), channel_id=1, source_target_pairs={{0,2},{1,3},{2,0},{3,1},{4,6},{5,7},{6,4},{7,5},{8,10},{9,11},{10,... | collective-permute-start | bytes 49160 | tf_op jit(solution)/shard_map/ppermute | solution.py:19
  29.5 3.2 %collective-permute-start.13 = (f32[8,512]{1,0:T(8,128)S(1)}, f32[8,512]{1,0:T(8,128)S(1)}, u32[]{:S(2)}, u32[]{:S(2)}) collective-permute-start(f32[8,512]{1,0:T(8,128)S(1)} %shard_map.68), channel_id=1, source_target_pairs={{0,3},{1,2},{2,1},{3,0},{4,7},{5,6},{6,5},{7,4},{8,11},{9,10},{10,... | collective-permute-start | bytes 49160 | tf_op jit(solution)/shard_map/ppermute | solution.py:19

commit v14 on v13

--- a/solution.py
+++ b/solution.py
@@ -163,7 +163,7 @@
     )(*parts)
 
 
-def score_kernel(share, size, shifts, *refs):
+def score_kernel(share, size, origins, *refs):
     unit_refs, test_refs, out, held = refs[:size], refs[size:-2], refs[-2], refs[-1]
     me, dp = lax.axis_index("tensor"), lax.axis_index("dp")
     for step in range(size):
@@ -171,47 +171,50 @@
             held[(me ^ step) * share + k] = unit_refs[step][k]
     unit = jnp.concatenate([held[:, c, :] for c in range(held.shape[1])], axis=1).astype(jnp.bfloat16)
     tests = test_refs[0].shape[0]
-    for step, test_ref in zip(shifts, test_refs):
+    for (factor, offset, modulus), test_ref in zip(origins, test_refs):
         part = lax.dot_general(unit, test_ref[...], NT, preferred_element_type=jnp.float32)
-        at = lax.rem(dp - step + len(shifts), len(shifts)) * tests
+        at = lax.rem(factor * dp + offset, modulus) * tests
         out[:, pl.ds(pl.multiple_of(at, 128), tests)] = part
 
 
 def score(unit_parts, test_parts, share):
     size, groups = len(unit_parts), len(test_parts)
-    tests, width = test_parts[0].shape
-    shifts = tuple(test_parts)
-    return pl.pallas_call(
-        functools.partial(score_kernel, share, size, shifts),
+    tests, width = test_parts[0][0].shape
+    origins = [origin for _, *origin in test_parts]
+    return pl.pallas_call(
+        functools.partial(score_kernel, share, size, origins),
         out_shape=jax.ShapeDtypeStruct((share * size, tests * groups), jnp.float32),
         in_specs=[VMEM] * (size + groups),
         out_specs=VMEM,
         scratch_shapes=[pltpu.VMEM((share * size, width // 128, 128), jnp.float32)],
         compiler_params=SMALL,
-    )(*unit_parts, *test_parts.values())
-
-
-def shift(value, axis, size, step):
-    return lax.ppermute(value, axis, [(i, (i + step) % size) for i in range(size)])
+    )(*unit_parts, *(shard for shard, *_ in test_parts))
+
+
+def gather_tests(own, groups):
+    ring = [0, 1, 3, 2] if groups == 4 else list(range(groups))
+
+    def shift(value, step):
+        return lax.ppermute(value, "dp", [(ring[i], ring[(i + step) % groups]) for i in range(groups)])
+
+    if groups == 4:
+        first = shift(own, 1)
+        return [(own, 1, 0, 4), (first, -2, 12, 5), (shift(own, -1), 2, 1, 5), (shift(first, 1), -1, 3, 4)]
+    return [(own, 1, 0, groups)] + [(shift(own, step), 1, groups - step, groups) for step in range(1, groups)]
 
 
 def shards(size, groups, activations, out_grads, proj_in, proj_out, lengths, test_grads):
     rank = proj_in.shape[1]
     share = activations.shape[0] // size
     own_tests = cut_tests(test_grads, size)
-    tests = {0: own_tests, 1: shift(own_tests, "dp", groups, 1)}
-    if groups == 4:
-        tests[2] = shift(tests[1], "dp", groups, 1)
-        tests[3] = shift(own_tests, "dp", groups, 3)
-    else:
-        tests.update({step: shift(own_tests, "dp", groups, step) for step in range(2, groups)})
+    tests = gather_tests(own_tests, groups)
 
     far = [CORES * x for x in range(1, size // CORES)]
     arrays = (activations, out_grads, proj_in.T, proj_out.T, lengths)
     far_other, far_own = project(*arrays, [[step ^ 1 for step in far], far], share, 4, 512, [own_tests])
     far_sum = far_own + xor_permute(far_other, "tensor", size, 1)
     sums = [xor_permute(far_sum[i * share : (i + 1) * share], "tensor", size, step) for i, step in enumerate(far)]
-    here = xor_permute(tests[1][:16, :128], "tensor", size, 1)
+    here = xor_permute(tests[1][0][:16, :128], "tensor", size, 1)
     near_other, near_own = project(*arrays, [[1], [0]], share, 4, 512, [far_sum, here])
     arrived = jnp.concatenate([xor_permute(near_other[k : k + 1], "tensor", size, 1) for k in range(share)])
 

time: 33.5 us -> 33.5 us (level)
    ppermute x11, waiting for transfers between devices: 4.6 us -> 3.86 us  [xor_permute(): return lax.ppermute(value, axis, [(i, i ^ step) for i in range(size)])]
    ppermute x3, waiting for transfers between devices: 4.37 us -> 4.95 us  [shift(): lax.ppermute(value, 'dp', [(ring[i], ring[(i + step) % groups]) for i in...]
  transfers between devices with their start and end apart: 14 -> 14, of which waited for: 8 -> 6; matrix products, arithmetic and copies ran while one was open for 0% -> 0% of each run, Pallas kernels for 33% -> 33%
where the time goes in v14:
time: 33.5 us; the launch traced here: 33.3 us
  Pallas kernels  12.5 us (37%)
  starting transfers between devices  11.3 us (34%)
  waiting for transfers between devices  8.81 us (26%)
  other arithmetic  0.67 us (2%)
    pallas_call x2, Pallas kernels, project(): pl.pallas_call(functools.partial(project_kernel, steps, share, ahead, pie...  10.6 us
    ppermute x11, starting transfers between devices, xor_permute(): return lax.ppermute(value, axis, [(i, i ^ step) for i in range(size)])  6 us
    ppermute x3, starting transfers between devices, shift(): lax.ppermute(value, 'dp', [(ring[i], ring[(i + step) % groups]) for i in...  5.26 us
    ppermute x3, waiting for transfers between devices, shift(): lax.ppermute(value, 'dp', [(ring[i], ring[(i + step) % groups]) for i in...  4.95 us
    ppermute x11, waiting for transfers between devices, xor_permute(): return lax.ppermute(value, axis, [(i, i ^ step) for i in range(size)])  3.86 us
    pallas_call x1, Pallas kernels, cut_tests(): pl.pallas_call(cut_kernel, out_shape=jax.ShapeDtypeStruct((rows, width //...  0.96 us
  transfers between devices with their start and end apart: 14, of which 6 were waited for; matrix products, arithmetic and copies ran while one was open for 0% of the time, Pallas kernels for 33%

profile of v14, /device:TPU:0, one launch (start us, length us, event | category | flops | bytes accessed | tf_op | source)
XLA Modules:
  0.0 33.3 jit_solution(7830263836574807301)
XLA Ops:
  0.0 1.0 %shard_map.64.refs_0_.refs_4_ = bf16[128,1024]{1,0:T(8,128)(2,1)S(1)} custom-call(bf16[128,4096]{1,0:T(8,128)(2,1)} %tests.1), custom_call_target="tpu_custom_call" | custom-call | tf_op jit(solution)/shard_map/pallas_call | solution.py:32
  1.0 3.1 %collective-permute-start.1 = (bf16[128,1024]{1,0:T(8,128)(2,1)S(1)}, bf16[128,1024]{1,0:T(8,128)(2,1)S(1)}, u32[]{:S(2)}, u32[]{:S(2)}) collective-permute-start(bf16[128,1024]{1,0:T(8,128)(2,1)S(1)} %shard_map.64.refs_0_.refs_4_), channel_id=1, source_target_pairs={{0,4},{4,12},{12,8},{8,0},{1,5},{5,13},{13,9},{9,1},{2,6},{6,14},{... | collective-permute-start | bytes 786440 | tf_op jit(solution)/shard_map/ppermute | solution.py:198
  4.0 5.3 %shard_map.65 = (f32[2,128,256]{2,1,0:T(8,128)S(1)}, f32[2,128,256]{2,1,0:T(8,128)S(1)}) custom-call(bf16[8,256,1024]{2,1,0:T(8,128)(2,1)} %act.3, bf16[8,256,3584]{2,1,0:T(8,128)(2,1)} %og.3, bf16[64,1024]{1,0:T(8,128)(2,1)} %bitcast.4, bf16[64,3584]{1,0:T(8,128)(2,1)} %bitcast.2, s32[8]{0:T(128)} %lens.3, bf16[128,1024]{1,0:T(8,128)(2,1)S(1)} %shard_map.64.refs_0_.refs_4_), custom_call_target="tpu_custom_call" | custom-call | flops 4294967296 | bytes 16777216 | tf_op jit(solution)/shard_map/pallas_call | solution.py:109
  9.4 0.1 collective-permute-start
  9.4 1.9 %collective-permute-done.1.refs_5_ = bf16[128,1024]{1,0:T(8,128)(2,1)S(1)} collective-permute-done((bf16[128,1024]{1,0:T(8,128)(2,1)S(1)}, bf16[128,1024]{1,0:T(8,128)(2,1)S(1)}, u32[]{:S(2)}, u32[]{:S(2)}) %collective-permute-start.1) | collective-permute-done | bytes 262176 | tf_op jit(solution)/shard_map/ppermute | solution.py:198
  11.4 0.0 collective-permute-start.2
  11.4 1.7 %collective-permute-start.9 = (bf16[128,1024]{1,0:T(8,128)(2,1)S(1)}, bf16[128,1024]{1,0:T(8,128)(2,1)S(1)}, u32[]{:S(2)}, u32[]{:S(2)}) collective-permute-start(bf16[128,1024]{1,0:T(8,128)(2,1)S(1)} %shard_map.64.refs_0_.refs_4_), channel_id=1, source_target_pairs={{0,8},{4,0},{12,4},{8,12},{1,9},{5,1},{13,5},{9,13},{2,10},{6,2},{... | collective-permute-start | bytes 786440 | tf_op jit(solution)/shard_map/ppermute | solution.py:198
  13.1 0.0 collective-permute-done
  13.2 1.6 %collective-permute-start.5 = (f32[2,128,256]{2,1,0:T(8,128)S(1)}, f32[2,128,256]{2,1,0:T(8,128)S(1)}, u32[]{:S(2)}, u32[]{:S(2)}) collective-permute-start(f32[2,128,256]{2,1,0:T(8,128)S(1)} %add.12.refs_0_), channel_id=1, source_target_pairs={{0,2},{1,3},{2,0},{3,1},{4,6},{5,7},{6,4},{7,5},{8,10},{9,11},{10,... | collective-permute-start | bytes 786440 | tf_op jit(solution)/shard_map/ppermute | solution.py:19
  14.7 0.4 %collective-permute-start.10 = (bf16[128,1024]{1,0:T(8,128)(2,1)S(1)}, bf16[128,1024]{1,0:T(8,128)(2,1)S(1)}, u32[]{:S(2)}, u32[]{:S(2)}) collective-permute-start(bf16[128,1024]{1,0:T(8,128)(2,1)S(1)} %collective-permute-done.1.refs_5_), channel_id=1, source_target_pairs={{0,4},{4,12},{12,8},{8,0},{1,5},{5,13},{13,9},{9,1},{2,6},{6,14},{... | collective-permute-start | bytes 786440 | tf_op jit(solution)/shard_map/ppermute | solution.py:198
  15.2 0.0 collective-permute-done.2.refs_1_
  15.2 5.3 %shard_map.66 = (f32[2,128,256]{2,1,0:T(8,128)S(1)}, f32[2,128,256]{2,1,0:T(8,128)S(1)}) custom-call(bf16[8,256,1024]{2,1,0:T(8,128)(2,1)} %act.3, bf16[8,256,3584]{2,1,0:T(8,128)(2,1)} %og.3, bf16[64,1024]{1,0:T(8,128)(2,1)} %bitcast.5, bf16[64,3584]{1,0:T(8,128)(2,1)} %bitcast.3, s32[8]{0:T(128)} %lens.3, f32[2,128,256]{2,1,0:T(8,128)S(1)} %add.12.refs_0_, ...), custom_call_target="tpu_custom_call" | custom-call | flops 4294967296 | bytes 16777216 | tf_op jit(solution)/shard_map/pallas_call | solution.py:109
  20.5 0.1 collective-permute-start.3
  20.6 0.5 %collective-permute-start.4 = (f32[1,128,256]{2,1,0:T(8,128)S(1)}, f32[1,128,256]{2,1,0:T(8,128)S(1)}, u32[]{:S(2)}, u32[]{:S(2)}) collective-permute-start(f32[1,128,256]{2,1,0:T(8,128)S(1)} %get-tuple-element.22), channel_id=1, source_target_pairs={{0,1},{1,0},{2,3},{3,2},{4,5},{5,4},{6,7},{7,6},{8,9},{9,8},{10,11... | collective-permute-start | bytes 393224 | tf_op jit(solution)/shard_map/ppermute | solution.py:19
  21.1 0.8 %collective-permute-done.3 = f32[1,128,256]{2,1,0:T(8,128)S(1)} collective-permute-done((f32[1,128,256]{2,1,0:T(8,128)S(1)}, f32[1,128,256]{2,1,0:T(8,128)S(1)}, u32[]{:S(2)}, u32[]{:S(2)}) %collective-permute-start.3) | collective-permute-done | bytes 131104 | tf_op jit(solution)/shard_map/ppermute | solution.py:19
  21.9 0.2 collective-permute-done.4
  22.1 0.0 collective-permute-done.5.refs_2_
  22.1 0.5 %shard_map.67 = (f32[2,8,128]{2,1,0:T(8,128)S(1)}, f32[2,8,128]{2,1,0:T(8,128)S(1)}, f32[2,8,128]{2,1,0:T(8,128)S(1)}, f32[2,8,128]{2,1,0:T(8,128)S(1)}) custom-call(f32[2,128,256]{2,1,0:T(8,128)S(1)} %get-tuple-element.15.refs_0_, f32[2,128,256]{2,1,0:T(8,128)S(1)} %pad_maximum_fusion.refs_1_, f32[2,128,256]{2,1,0:T(8,128)S(1)} %collective-permute-done.5.refs_2_), custom_call_target="tpu_custom_call" | custom-call | tf_op jit(solution)/shard_map/pallas_call | solution.py:156
  22.6 0.4 %collective-permute-start.6 = (f32[2,8,128]{2,1,0:T(8,128)S(1)}, f32[2,8,128]{2,1,0:T(8,128)S(1)}, u32[]{:S(2)}, u32[]{:S(2)}) collective-permute-start(f32[2,8,128]{2,1,0:T(8,128)S(1)} %get-tuple-element.18), channel_id=1, source_target_pairs={{0,1},{1,0},{2,3},{3,2},{4,5},{5,4},{6,7},{7,6},{8,9},{9,8},{10,11... | collective-permute-start | bytes 24584 | tf_op jit(solution)/shard_map/ppermute | solution.py:19
  23.0 0.8 %collective-permute-start.7 = (f32[2,8,128]{2,1,0:T(8,128)S(1)}, f32[2,8,128]{2,1,0:T(8,128)S(1)}, u32[]{:S(2)}, u32[]{:S(2)}) collective-permute-start(f32[2,8,128]{2,1,0:T(8,128)S(1)} %get-tuple-element.19), channel_id=1, source_target_pairs={{0,2},{1,3},{2,0},{3,1},{4,6},{5,7},{6,4},{7,5},{8,10},{9,11},{10,... | collective-permute-start | bytes 24584 | tf_op jit(solution)/shard_map/ppermute | solution.py:19
  23.8 0.8 %collective-permute-start.8 = (f32[2,8,128]{2,1,0:T(8,128)S(1)}, f32[2,8,128]{2,1,0:T(8,128)S(1)}, u32[]{:S(2)}, u32[]{:S(2)}) collective-permute-start(f32[2,8,128]{2,1,0:T(8,128)S(1)} %get-tuple-element.20), channel_id=1, source_target_pairs={{0,3},{1,2},{2,1},{3,0},{4,7},{5,6},{6,5},{7,4},{8,11},{9,10},{10,... | collective-permute-start | bytes 24584 | tf_op jit(solution)/shard_map/ppermute | solution.py:19
  24.6 0.0 collective-permute-done.9.refs_6_
  24.6 3.0 %collective-permute-done.10.refs_7_ = bf16[128,1024]{1,0:T(8,128)(2,1)S(1)} collective-permute-done((bf16[128,1024]{1,0:T(8,128)(2,1)S(1)}, bf16[128,1024]{1,0:T(8,128)(2,1)S(1)}, u32[]{:S(2)}, u32[]{:S(2)}) %collective-permute-start.10) | collective-permute-done | bytes 262176 | tf_op jit(solution)/shard_map/ppermute | solution.py:198
  27.6 0.0 collective-permute-done.6.refs_1_
  27.6 0.4 %shard_map.68 = f32[8,512]{1,0:T(8,128)S(1)} custom-call(f32[2,8,128]{2,1,0:T(8,128)S(1)} %get-tuple-element.17.refs_0_, f32[2,8,128]{2,1,0:T(8,128)S(1)} %collective-permute-done.6.refs_1_, f32[2,8,128]{2,1,0:T(8,128)S(1)} %collective-permute-done.7.refs_2_, f32[2,8,128]{2,1,0:T(8,128)S(1)} %collective-permute-done.8.refs_3_, ...), custom_call_target="tpu_custom_call" | custom-call | tf_op jit(solution)/shard_map/pallas_call | solution.py:184
  28.0 0.0 collective-permute-start.11
  28.0 1.5 %collective-permute-start.12 = (f32[8,512]{1,0:T(8,128)S(1)}, f32[8,512]{1,0:T(8,128)S(1)}, u32[]{:S(2)}, u32[]{:S(2)}) collective-permute-start(f32[8,512]{1,0:T(8,128)S(1)} %shard_map.68), channel_id=1, source_target_pairs={{0,2},{1,3},{2,0},{3,1},{4,6},{5,7},{6,4},{7,5},{8,10},{9,11},{10,... | collective-permute-start | bytes 49160 | tf_op jit(solution)/shard_map/ppermute | solution.py:19
  29.5 0.3 %collective-permute-start.13 = (f32[8,512]{1,0:T(8,128)S(1)}, f32[8,512]{1,0:T(8,128)S(1)}, u32[]{:S(2)}, u32[]{:S(2)}) collective-permute-start(f32[8,512]{1,0:T(8,128)S(1)} %shard_map.68), channel_id=1, source_target_pairs={{0,3},{1,2},{2,1},{3,0},{4,7},{5,6},{6,5},{7,4},{8,11},{9,10},{10,... | collective-permute-start | bytes 49160 | tf_op jit(solution)/shard_map/ppermute | solution.py:19
  29.9 0.0 collective-permute-done.11
  29.9 1.9 %collective-permute-done.12 = f32[8,512]{1,0:T(8,128)S(1)} collective-permute-done((f32[8,512]{1,0:T(8,128)S(1)}, f32[8,512]{1,0:T(8,128)S(1)}, u32[]{:S(2)}, u32[]{:S(2)}) %collective-permute-start.12) | collective-permute-done | bytes 16416 | tf_op jit(solution)/shard_map/ppermute | solution.py:19
  31.8 0.9 %collective-permute-done.13 = f32[8,512]{1,0:T(8,128)S(1)} collective-permute-done((f32[8,512]{1,0:T(8,128)S(1)}, f32[8,512]{1,0:T(8,128)S(1)}, u32[]{:S(2)}, u32[]{:S(2)}) %collective-permute-start.13) | collective-permute-done | bytes 16416 | tf_op jit(solution)/shard_map/ppermute | solution.py:19
  32.7 0.6 %add_add_fusion = f32[8,512]{1,0:T(8,128)} fusion(f32[8,512]{1,0:T(8,128)S(1)} %collective-permute-done.12, f32[8,512]{1,0:T(8,128)S(1)} %collective-permute-done.13, f32[8,512]{1,0:T(8,128)S(1)} %shard_map.68, f32[8,512]{1,0:T(8,128)S(1)} %collective-permute-done.11), kind=kLoop, calls=%fused_computation.1 | loop fusion | flops 12288 | bytes 81920 | tf_op jit(solution)/shard_map/add | solution.py:226
  (6 shorter events, 0.1 us)
Async XLA Ops:
  1.0 10.4 %collective-permute-start.1 = (bf16[128,1024]{1,0:T(8,128)(2,1)S(1)}, bf16[128,1024]{1,0:T(8,128)(2,1)S(1)}, u32[]{:S(2)}, u32[]{:S(2)}) collective-permute-start(bf16[128,1024]{1,0:T(8,128)(2,1)S(1)} %shard_map.64.refs_0_.refs_4_), channel_id=1, source_target_pairs={{0,4},{4,12},{12,8},{8,0},{1,5},{5,13},{13,9},{9,1},{2,6},{6,14},{... | collective-permute-start | bytes 786440 | tf_op jit(solution)/shard_map/ppermute | solution.py:198
  9.4 3.7 %collective-permute-start = (f32[2,128,256]{2,1,0:T(8,128)S(1)}, f32[2,128,256]{2,1,0:T(8,128)S(1)}, u32[]{:S(2)}, u32[]{:S(2)}) collective-permute-start(f32[2,128,256]{2,1,0:T(8,128)S(1)} %get-tuple-element.14), channel_id=1, source_target_pairs={{0,1},{1,0},{2,3},{3,2},{4,5},{5,4},{6,7},{7,6},{8,9},{9,8},{10,11... | collective-permute-start | bytes 786440 | tf_op jit(solution)/shard_map/ppermute | solution.py:19
  11.4 3.8 %collective-permute-start.2 = (bf16[16,128]{1,0:T(8,128)(2,1)S(1)}, bf16[16,128]{1,0:T(8,128)(2,1)S(1)}, u32[]{:S(2)}, u32[]{:S(2)}) collective-permute-start(bf16[16,128]{1,0:T(8,128)(2,1)S(1)} %slice.12), channel_id=1, source_target_pairs={{0,1},{1,0},{2,3},{3,2},{4,5},{5,4},{6,7},{7,6},{8,9},{9,8},{10,11... | collective-permute-start | bytes 12296 | tf_op jit(solution)/shard_map/ppermute | solution.py:19
  11.4 13.2 %collective-permute-start.9 = (bf16[128,1024]{1,0:T(8,128)(2,1)S(1)}, bf16[128,1024]{1,0:T(8,128)(2,1)S(1)}, u32[]{:S(2)}, u32[]{:S(2)}) collective-permute-start(bf16[128,1024]{1,0:T(8,128)(2,1)S(1)} %shard_map.64.refs_0_.refs_4_), channel_id=1, source_target_pairs={{0,8},{4,0},{12,4},{8,12},{1,9},{5,1},{13,5},{9,13},{2,10},{6,2},{... | collective-permute-start | bytes 786440 | tf_op jit(solution)/shard_map/ppermute | solution.py:198
  13.2 9.0 %collective-permute-start.5 = (f32[2,128,256]{2,1,0:T(8,128)S(1)}, f32[2,128,256]{2,1,0:T(8,128)S(1)}, u32[]{:S(2)}, u32[]{:S(2)}) collective-permute-start(f32[2,128,256]{2,1,0:T(8,128)S(1)} %add.12.refs_0_), channel_id=1, source_target_pairs={{0,2},{1,3},{2,0},{3,1},{4,6},{5,7},{6,4},{7,5},{8,10},{9,11},{10,... | collective-permute-start | bytes 786440 | tf_op jit(solution)/shard_map/ppermute | solution.py:19
  14.7 12.9 %collective-permute-start.10 = (bf16[128,1024]{1,0:T(8,128)(2,1)S(1)}, bf16[128,1024]{1,0:T(8,128)(2,1)S(1)}, u32[]{:S(2)}, u32[]{:S(2)}) collective-permute-start(bf16[128,1024]{1,0:T(8,128)(2,1)S(1)} %collective-permute-done.1.refs_5_), channel_id=1, source_target_pairs={{0,4},{4,12},{12,8},{8,0},{1,5},{5,13},{13,9},{9,1},{2,6},{6,14},{... | collective-permute-start | bytes 786440 | tf_op jit(solution)/shard_map/ppermute | solution.py:198
  20.5 1.4 %collective-permute-start.3 = (f32[1,128,256]{2,1,0:T(8,128)S(1)}, f32[1,128,256]{2,1,0:T(8,128)S(1)}, u32[]{:S(2)}, u32[]{:S(2)}) collective-permute-start(f32[1,128,256]{2,1,0:T(8,128)S(1)} %get-tuple-element.21), channel_id=1, source_target_pairs={{0,1},{1,0},{2,3},{3,2},{4,5},{5,4},{6,7},{7,6},{8,9},{9,8},{10,11... | collective-permute-start | bytes 393224 | tf_op jit(solution)/shard_map/ppermute | solution.py:19
  20.6 1.5 %collective-permute-start.4 = (f32[1,128,256]{2,1,0:T(8,128)S(1)}, f32[1,128,256]{2,1,0:T(8,128)S(1)}, u32[]{:S(2)}, u32[]{:S(2)}) collective-permute-start(f32[1,128,256]{2,1,0:T(8,128)S(1)} %get-tuple-element.22), channel_id=1, source_target_pairs={{0,1},{1,0},{2,3},{3,2},{4,5},{5,4},{6,7},{7,6},{8,9},{9,8},{10,11... | collective-permute-start | bytes 393224 | tf_op jit(solution)/shard_map/ppermute | solution.py:19
  22.6 5.0 %collective-permute-start.6 = (f32[2,8,128]{2,1,0:T(8,128)S(1)}, f32[2,8,128]{2,1,0:T(8,128)S(1)}, u32[]{:S(2)}, u32[]{:S(2)}) collective-permute-start(f32[2,8,128]{2,1,0:T(8,128)S(1)} %get-tuple-element.18), channel_id=1, source_target_pairs={{0,1},{1,0},{2,3},{3,2},{4,5},{5,4},{6,7},{7,6},{8,9},{9,8},{10,11... | collective-permute-start | bytes 24584 | tf_op jit(solution)/shard_map/ppermute | solution.py:19
  23.0 4.6 %collective-permute-start.7 = (f32[2,8,128]{2,1,0:T(8,128)S(1)}, f32[2,8,128]{2,1,0:T(8,128)S(1)}, u32[]{:S(2)}, u32[]{:S(2)}) collective-permute-start(f32[2,8,128]{2,1,0:T(8,128)S(1)} %get-tuple-element.19), channel_id=1, source_target_pairs={{0,2},{1,3},{2,0},{3,1},{4,6},{5,7},{6,4},{7,5},{8,10},{9,11},{10,... | collective-permute-start | bytes 24584 | tf_op jit(solution)/shard_map/ppermute | solution.py:19
  23.8 3.8 %collective-permute-start.8 = (f32[2,8,128]{2,1,0:T(8,128)S(1)}, f32[2,8,128]{2,1,0:T(8,128)S(1)}, u32[]{:S(2)}, u32[]{:S(2)}) collective-permute-start(f32[2,8,128]{2,1,0:T(8,128)S(1)} %get-tuple-element.20), channel_id=1, source_target_pairs={{0,3},{1,2},{2,1},{3,0},{4,7},{5,6},{6,5},{7,4},{8,11},{9,10},{10,... | collective-permute-start | bytes 24584 | tf_op jit(solution)/shard_map/ppermute | solution.py:19
  28.0 1.9 %collective-permute-start.11 = (f32[8,512]{1,0:T(8,128)S(1)}, f32[8,512]{1,0:T(8,128)S(1)}, u32[]{:S(2)}, u32[]{:S(2)}) collective-permute-start(f32[8,512]{1,0:T(8,128)S(1)} %shard_map.68), channel_id=1, source_target_pairs={{0,1},{1,0},{2,3},{3,2},{4,5},{5,4},{6,7},{7,6},{8,9},{9,8},{10,11... | collective-permute-start | bytes 49160 | tf_op jit(solution)/shard_map/ppermute | solution.py:19
  28.0 3.7 %collective-permute-start.12 = (f32[8,512]{1,0:T(8,128)S(1)}, f32[8,512]{1,0:T(8,128)S(1)}, u32[]{:S(2)}, u32[]{:S(2)}) collective-permute-start(f32[8,512]{1,0:T(8,128)S(1)} %shard_map.68), channel_id=1, source_target_pairs={{0,2},{1,3},{2,0},{3,1},{4,6},{5,7},{6,4},{7,5},{8,10},{9,11},{10,... | collective-permute-start | bytes 49160 | tf_op jit(solution)/shard_map/ppermute | solution.py:19
  29.5 3.2 %collective-permute-start.13 = (f32[8,512]{1,0:T(8,128)S(1)}, f32[8,512]{1,0:T(8,128)S(1)}, u32[]{:S(2)}, u32[]{:S(2)}) collective-permute-start(f32[8,512]{1,0:T(8,128)S(1)} %shard_map.68), channel_id=1, source_target_pairs={{0,3},{1,2},{2,1},{3,0},{4,7},{5,6},{6,5},{7,4},{8,11},{9,10},{10,... | collective-permute-start | bytes 49160 | tf_op jit(solution)/shard_map/ppermute | solution.py:19

commit v15 on v14

--- a/solution.py
+++ b/solution.py
@@ -40,6 +40,7 @@
 
 
 COST = 1 << 32
+LATER = 1<<10
 
 
 def project_kernel(steps, share, ahead, piece, after, act, og, wi, wo, lens, *refs):
@@ -100,7 +101,7 @@
         out[rank:] = sums[1][:, slot * slots : (slot + 1) * slots]
 
 
-def project(act, og, wi, wo, lens, groups, share, ahead, piece, after=()):
+def project(act, og, wi, wo, lens, groups, share, ahead, piece, cost, after=()):
     steps = [step for group in groups for step in group]
     count = len(steps) * share
     slots, feat, hidden = act.shape[1], act.shape[2], og.shape[2]
@@ -120,7 +121,7 @@
             pltpu.SemaphoreType.DMA((3,)),
         ],
         compiler_params=pltpu.CompilerParams(vmem_limit_bytes=32 << 20),
-        cost_estimate=pl.CostEstimate(flops=COST, bytes_accessed=COST // 256, transcendentals=0),
+        cost_estimate=pl.CostEstimate(flops=cost, bytes_accessed=cost // 256, transcendentals=0),
     )(*map(in_hbm, (act, og, wi, wo, lens)), *after)
 
 
@@ -211,12 +212,15 @@
 
     far = [CORES * x for x in range(1, size // CORES)]
     arrays = (activations, out_grads, proj_in.T, proj_out.T, lengths)
-    far_other, far_own = project(*arrays, [[step ^ 1 for step in far], far], share, 4, 512, [own_tests])
+    far_other, far_own = project(*arrays, [[step ^ 1 for step in far], far], share, 4, 512, COST, [own_tests])
     far_sum = far_own + xor_permute(far_other, "tensor", size, 1)
     sums = [xor_permute(far_sum[i * share : (i + 1) * share], "tensor", size, step) for i, step in enumerate(far)]
     here = xor_permute(tests[1][0][:16, :128], "tensor", size, 1)
-    near_other, near_own = project(*arrays, [[1], [0]], share, 4, 512, [far_sum, here])
-    arrived = jnp.concatenate([xor_permute(near_other[k : k + 1], "tensor", size, 1) for k in range(share)])
+    near_other, near_own = project(*arrays, [[1], [0]], share, 4, 512, LATER, [far_sum, here])
+    late = tests[2][0][: near_other.shape[1], : near_other.shape[2]].astype(jnp.float32)
+    pieces = [near_other[k : k + 1] for k in range(share)]
+    pieces[0] = pieces[0] + 0.0 * late[None]
+    arrived = jnp.concatenate([xor_permute(one, "tensor", size, 1) for one in pieces])
 
     unit_outs = units([near_own, arrived] + sums, share, rank, size)
     unit_parts = [unit_outs[0]] + [xor_permute(unit_outs[step], "tensor", size, step) for step in range(1, size)]

time: 33.5 us -> 32.7 us (0.976)
  waiting for transfers between devices: 8.81 us -> 6.84 us
  starting transfers between devices: 11.3 us -> 12.4 us
    ppermute x3, waiting for transfers between devices: 4.95 us -> 2.93 us  [shift(): lax.ppermute(value, 'dp', [(ring[i], ring[(i + step) % groups]) for i in...]
    ppermute x3, starting transfers between devices: 5.26 us -> 6.3 us  [shift(): lax.ppermute(value, 'dp', [(ring[i], ring[(i + step) % groups]) for i in...]
  transfers between devices with their start and end apart: 14 -> 14, of which waited for: 6 -> 7; matrix products, arithmetic and copies ran while one was open for 0% -> 0% of each run, Pallas kernels for 33% -> 34%
where the time goes in v15:
time: 32.7 us; the launch traced here: 32.5 us
  Pallas kernels  12.5 us (38%)
  starting transfers between devices  12.4 us (38%)
  waiting for transfers between devices  6.84 us (21%)
  other arithmetic  0.7 us (2%)
    pallas_call x2, Pallas kernels, project(): pl.pallas_call(functools.partial(project_kernel, steps, share, ahead, pie...  10.6 us
    ppermute x3, starting transfers between devices, shift(): lax.ppermute(value, 'dp', [(ring[i], ring[(i + step) % groups]) for i in...  6.3 us
    ppermute x11, starting transfers between devices, xor_permute(): return lax.ppermute(value, axis, [(i, i ^ step) for i in range(size)])  6.08 us
    ppermute x11, waiting for transfers between devices, xor_permute(): return lax.ppermute(value, axis, [(i, i ^ step) for i in range(size)])  3.91 us
    ppermute x3, waiting for transfers between devices, shift(): lax.ppermute(value, 'dp', [(ring[i], ring[(i + step) % groups]) for i in...  2.93 us
    pallas_call x1, Pallas kernels, cut_tests(): pl.pallas_call(cut_kernel, out_shape=jax.ShapeDtypeStruct((rows, width //...  0.96 us
  transfers between devices with their start and end apart: 14, of which 7 were waited for; matrix products, arithmetic and copies ran while one was open for 0% of the time, Pallas kernels for 34%

profile of v15, /device:TPU:0, one launch (start us, length us, event | category | flops | bytes accessed | tf_op | source)
XLA Modules:
  0.0 32.5 jit_solution(6212040575722348233)
XLA Ops:
  0.0 1.0 %shard_map.64.refs_0_.refs_4_ = bf16[128,1024]{1,0:T(8,128)(2,1)S(1)} custom-call(bf16[128,4096]{1,0:T(8,128)(2,1)} %tests.1), custom_call_target="tpu_custom_call" | custom-call | tf_op jit(solution)/shard_map/pallas_call | solution.py:32
  1.0 3.1 %collective-permute-start.1 = (bf16[128,1024]{1,0:T(8,128)(2,1)S(1)}, bf16[128,1024]{1,0:T(8,128)(2,1)S(1)}, u32[]{:S(2)}, u32[]{:S(2)}) collective-permute-start(bf16[128,1024]{1,0:T(8,128)(2,1)S(1)} %shard_map.64.refs_0_.refs_4_), channel_id=1, source_target_pairs={{0,4},{4,12},{12,8},{8,0},{1,5},{5,13},{13,9},{9,1},{2,6},{6,14},{... | collective-permute-start | bytes 786440 | tf_op jit(solution)/shard_map/ppermute | solution.py:199
  4.0 5.3 %shard_map.65 = (f32[2,128,256]{2,1,0:T(8,128)S(1)}, f32[2,128,256]{2,1,0:T(8,128)S(1)}) custom-call(bf16[8,256,1024]{2,1,0:T(8,128)(2,1)} %act.3, bf16[8,256,3584]{2,1,0:T(8,128)(2,1)} %og.3, bf16[64,1024]{1,0:T(8,128)(2,1)} %bitcast.6, bf16[64,3584]{1,0:T(8,128)(2,1)} %bitcast.4, s32[8]{0:T(128)} %lens.3, bf16[128,1024]{1,0:T(8,128)(2,1)S(1)} %shard_map.64.refs_0_.refs_4_), custom_call_target="tpu_custom_call" | custom-call | flops 4294967296 | bytes 16777216 | tf_op jit(solution)/shard_map/pallas_call | solution.py:110
  9.4 0.1 collective-permute-start
  9.4 1.1 %collective-permute-start.3 = (bf16[128,1024]{1,0:T(8,128)(2,1)S(1)}, bf16[128,1024]{1,0:T(8,128)(2,1)S(1)}, u32[]{:S(2)}, u32[]{:S(2)}) collective-permute-start(bf16[128,1024]{1,0:T(8,128)(2,1)S(1)} %shard_map.64.refs_0_.refs_4_), channel_id=1, source_target_pairs={{0,8},{4,0},{12,4},{8,12},{1,9},{5,1},{13,5},{9,13},{2,10},{6,2},{... | collective-permute-start | bytes 786440 | tf_op jit(solution)/shard_map/ppermute | solution.py:199
  10.5 0.8 %collective-permute-done.1.refs_5_ = bf16[128,1024]{1,0:T(8,128)(2,1)S(1)} collective-permute-done((bf16[128,1024]{1,0:T(8,128)(2,1)S(1)}, bf16[128,1024]{1,0:T(8,128)(2,1)S(1)}, u32[]{:S(2)}, u32[]{:S(2)}) %collective-permute-start.1) | collective-permute-done | bytes 262176 | tf_op jit(solution)/shard_map/ppermute | solution.py:199
  11.4 0.0 collective-permute-start.2
  11.4 0.0 collective-permute-done
  11.4 1.6 %collective-permute-start.6 = (f32[2,128,256]{2,1,0:T(8,128)S(1)}, f32[2,128,256]{2,1,0:T(8,128)S(1)}, u32[]{:S(2)}, u32[]{:S(2)}) collective-permute-start(f32[2,128,256]{2,1,0:T(8,128)S(1)} %add.15.refs_0_), channel_id=1, source_target_pairs={{0,2},{1,3},{2,0},{3,1},{4,6},{5,7},{6,4},{7,5},{8,10},{9,11},{10,... | collective-permute-start | bytes 786440 | tf_op jit(solution)/shard_map/ppermute | solution.py:19
  13.0 2.1 %collective-permute-start.10 = (bf16[128,1024]{1,0:T(8,128)(2,1)S(1)}, bf16[128,1024]{1,0:T(8,128)(2,1)S(1)}, u32[]{:S(2)}, u32[]{:S(2)}) collective-permute-start(bf16[128,1024]{1,0:T(8,128)(2,1)S(1)} %collective-permute-done.1.refs_5_), channel_id=1, source_target_pairs={{0,4},{4,12},{12,8},{8,0},{1,5},{5,13},{13,9},{9,1},{2,6},{6,14},{... | collective-permute-start | bytes 786440 | tf_op jit(solution)/shard_map/ppermute | solution.py:199
  15.2 0.0 collective-permute-done.2.refs_1_
  15.2 5.3 %shard_map.66 = (f32[2,128,256]{2,1,0:T(8,128)S(1)}, f32[2,128,256]{2,1,0:T(8,128)S(1)}) custom-call(bf16[8,256,1024]{2,1,0:T(8,128)(2,1)} %act.3, bf16[8,256,3584]{2,1,0:T(8,128)(2,1)} %og.3, bf16[64,1024]{1,0:T(8,128)(2,1)} %bitcast.7, bf16[64,3584]{1,0:T(8,128)(2,1)} %bitcast.5, s32[8]{0:T(128)} %lens.3, f32[2,128,256]{2,1,0:T(8,128)S(1)} %add.15.refs_0_, ...), custom_call_target="tpu_custom_call" | custom-call | flops 1024 | bytes 4 | tf_op jit(solution)/shard_map/pallas_call | solution.py:110
  20.5 0.0 collective-permute-done.3.refs_6_
  20.5 0.1 collective-permute-start.4
  20.6 0.5 %collective-permute-start.5 = (f32[1,128,256]{2,1,0:T(8,128)S(1)}, f32[1,128,256]{2,1,0:T(8,128)S(1)}, u32[]{:S(2)}, u32[]{:S(2)}) collective-permute-start(f32[1,128,256]{2,1,0:T(8,128)S(1)} %get-tuple-element.22), channel_id=1, source_target_pairs={{0,1},{1,0},{2,3},{3,2},{4,5},{5,4},{6,7},{7,6},{8,9},{9,8},{10,11... | collective-permute-start | bytes 393224 | tf_op jit(solution)/shard_map/ppermute | solution.py:19
  21.1 0.8 %collective-permute-done.4 = f32[1,128,256]{2,1,0:T(8,128)S(1)} collective-permute-done((f32[1,128,256]{2,1,0:T(8,128)S(1)}, f32[1,128,256]{2,1,0:T(8,128)S(1)}, u32[]{:S(2)}, u32[]{:S(2)}) %collective-permute-start.4) | collective-permute-done | bytes 131104 | tf_op jit(solution)/shard_map/ppermute | solution.py:19
  21.9 0.2 collective-permute-done.5
  22.2 0.5 %shard_map.67 = (f32[2,8,128]{2,1,0:T(8,128)S(1)}, f32[2,8,128]{2,1,0:T(8,128)S(1)}, f32[2,8,128]{2,1,0:T(8,128)S(1)}, f32[2,8,128]{2,1,0:T(8,128)S(1)}) custom-call(f32[2,128,256]{2,1,0:T(8,128)S(1)} %get-tuple-element.15.refs_0_, f32[2,128,256]{2,1,0:T(8,128)S(1)} %pad_maximum_fusion.refs_1_, f32[2,128,256]{2,1,0:T(8,128)S(1)} %collective-permute-done.6.refs_2_), custom_call_target="tpu_custom_call" | custom-call | tf_op jit(solution)/shard_map/pallas_call | solution.py:157
  22.7 0.4 %collective-permute-start.7 = (f32[2,8,128]{2,1,0:T(8,128)S(1)}, f32[2,8,128]{2,1,0:T(8,128)S(1)}, u32[]{:S(2)}, u32[]{:S(2)}) collective-permute-start(f32[2,8,128]{2,1,0:T(8,128)S(1)} %get-tuple-element.18), channel_id=1, source_target_pairs={{0,1},{1,0},{2,3},{3,2},{4,5},{5,4},{6,7},{7,6},{8,9},{9,8},{10,11... | collective-permute-start | bytes 24584 | tf_op jit(solution)/shard_map/ppermute | solution.py:19
  23.1 0.5 %collective-permute-start.8 = (f32[2,8,128]{2,1,0:T(8,128)S(1)}, f32[2,8,128]{2,1,0:T(8,128)S(1)}, u32[]{:S(2)}, u32[]{:S(2)}) collective-permute-start(f32[2,8,128]{2,1,0:T(8,128)S(1)} %get-tuple-element.19), channel_id=1, source_target_pairs={{0,2},{1,3},{2,0},{3,1},{4,6},{5,7},{6,4},{7,5},{8,10},{9,11},{10,... | collective-permute-start | bytes 24584 | tf_op jit(solution)/shard_map/ppermute | solution.py:19
  23.6 1.0 %collective-permute-start.9 = (f32[2,8,128]{2,1,0:T(8,128)S(1)}, f32[2,8,128]{2,1,0:T(8,128)S(1)}, u32[]{:S(2)}, u32[]{:S(2)}) collective-permute-start(f32[2,8,128]{2,1,0:T(8,128)S(1)} %get-tuple-element.20), channel_id=1, source_target_pairs={{0,3},{1,2},{2,1},{3,0},{4,7},{5,6},{6,5},{7,4},{8,11},{9,10},{10,... | collective-permute-start | bytes 24584 | tf_op jit(solution)/shard_map/ppermute | solution.py:19
  24.6 2.1 %collective-permute-done.10.refs_7_ = bf16[128,1024]{1,0:T(8,128)(2,1)S(1)} collective-permute-done((bf16[128,1024]{1,0:T(8,128)(2,1)S(1)}, bf16[128,1024]{1,0:T(8,128)(2,1)S(1)}, u32[]{:S(2)}, u32[]{:S(2)}) %collective-permute-start.10) | collective-permute-done | bytes 262176 | tf_op jit(solution)/shard_map/ppermute | solution.py:199
  26.7 0.0 collective-permute-done.7.refs_1_
  26.7 0.1 collective-permute-done.8.refs_2_
  26.8 0.0 collective-permute-done.9.refs_3_
  26.8 0.4 %shard_map.68 = f32[8,512]{1,0:T(8,128)S(1)} custom-call(f32[2,8,128]{2,1,0:T(8,128)S(1)} %get-tuple-element.17.refs_0_, f32[2,8,128]{2,1,0:T(8,128)S(1)} %collective-permute-done.7.refs_1_, f32[2,8,128]{2,1,0:T(8,128)S(1)} %collective-permute-done.8.refs_2_, f32[2,8,128]{2,1,0:T(8,128)S(1)} %collective-permute-done.9.refs_3_, ...), custom_call_target="tpu_custom_call" | custom-call | tf_op jit(solution)/shard_map/pallas_call | solution.py:185
  27.1 0.1 collective-permute-start.11
  27.3 1.4 %collective-permute-start.12 = (f32[8,512]{1,0:T(8,128)S(1)}, f32[8,512]{1,0:T(8,128)S(1)}, u32[]{:S(2)}, u32[]{:S(2)}) collective-permute-start(f32[8,512]{1,0:T(8,128)S(1)} %shard_map.68), channel_id=1, source_target_pairs={{0,2},{1,3},{2,0},{3,1},{4,6},{5,7},{6,4},{7,5},{8,10},{9,11},{10,... | collective-permute-start | bytes 49160 | tf_op jit(solution)/shard_map/ppermute | solution.py:19
  28.7 0.4 %collective-permute-start.13 = (f32[8,512]{1,0:T(8,128)S(1)}, f32[8,512]{1,0:T(8,128)S(1)}, u32[]{:S(2)}, u32[]{:S(2)}) collective-permute-start(f32[8,512]{1,0:T(8,128)S(1)} %shard_map.68), channel_id=1, source_target_pairs={{0,3},{1,2},{2,1},{3,0},{4,7},{5,6},{6,5},{7,4},{8,11},{9,10},{10,... | collective-permute-start | bytes 49160 | tf_op jit(solution)/shard_map/ppermute | solution.py:19
  29.1 2.0 %collective-permute-done.12 = f32[8,512]{1,0:T(8,128)S(1)} collective-permute-done((f32[8,512]{1,0:T(8,128)S(1)}, f32[8,512]{1,0:T(8,128)S(1)}, u32[]{:S(2)}, u32[]{:S(2)}) %collective-permute-start.12) | collective-permute-done | bytes 16416 | tf_op jit(solution)/shard_map/ppermute | solution.py:19
  31.0 0.9 %collective-permute-done.13 = f32[8,512]{1,0:T(8,128)S(1)} collective-permute-done((f32[8,512]{1,0:T(8,128)S(1)}, f32[8,512]{1,0:T(8,128)S(1)}, u32[]{:S(2)}, u32[]{:S(2)}) %collective-permute-start.13) | collective-permute-done | bytes 16416 | tf_op jit(solution)/shard_map/ppermute | solution.py:19
  31.9 0.6 %add_add_fusion = f32[8,512]{1,0:T(8,128)} fusion(f32[8,512]{1,0:T(8,128)S(1)} %collective-permute-done.12, f32[8,512]{1,0:T(8,128)S(1)} %collective-permute-done.13, f32[8,512]{1,0:T(8,128)S(1)} %shard_map.68, f32[8,512]{1,0:T(8,128)S(1)} %collective-permute-done.11), kind=kLoop, calls=%fused_computation.2 | loop fusion | flops 12288 | bytes 81920 | tf_op jit(solution)/shard_map/add | solution.py:230
  (6 shorter events, 0.1 us)
Async XLA Ops:
  1.0 10.4 %collective-permute-start.1 = (bf16[128,1024]{1,0:T(8,128)(2,1)S(1)}, bf16[128,1024]{1,0:T(8,128)(2,1)S(1)}, u32[]{:S(2)}, u32[]{:S(2)}) collective-permute-start(bf16[128,1024]{1,0:T(8,128)(2,1)S(1)} %shard_map.64.refs_0_.refs_4_), channel_id=1, source_target_pairs={{0,4},{4,12},{12,8},{8,0},{1,5},{5,13},{13,9},{9,1},{2,6},{6,14},{... | collective-permute-start | bytes 786440 | tf_op jit(solution)/shard_map/ppermute | solution.py:199
  9.4 2.0 %collective-permute-start = (f32[2,128,256]{2,1,0:T(8,128)S(1)}, f32[2,128,256]{2,1,0:T(8,128)S(1)}, u32[]{:S(2)}, u32[]{:S(2)}) collective-permute-start(f32[2,128,256]{2,1,0:T(8,128)S(1)} %get-tuple-element.14), channel_id=1, source_target_pairs={{0,1},{1,0},{2,3},{3,2},{4,5},{5,4},{6,7},{7,6},{8,9},{9,8},{10,11... | collective-permute-start | bytes 786440 | tf_op jit(solution)/shard_map/ppermute | solution.py:19
  9.4 11.0 %collective-permute-start.3 = (bf16[128,1024]{1,0:T(8,128)(2,1)S(1)}, bf16[128,1024]{1,0:T(8,128)(2,1)S(1)}, u32[]{:S(2)}, u32[]{:S(2)}) collective-permute-start(bf16[128,1024]{1,0:T(8,128)(2,1)S(1)} %shard_map.64.refs_0_.refs_4_), channel_id=1, source_target_pairs={{0,8},{4,0},{12,4},{8,12},{1,9},{5,1},{13,5},{9,13},{2,10},{6,2},{... | collective-permute-start | bytes 786440 | tf_op jit(solution)/shard_map/ppermute | solution.py:199
  11.4 3.8 %collective-permute-start.2 = (bf16[16,128]{1,0:T(8,128)(2,1)S(1)}, bf16[16,128]{1,0:T(8,128)(2,1)S(1)}, u32[]{:S(2)}, u32[]{:S(2)}) collective-permute-start(bf16[16,128]{1,0:T(8,128)(2,1)S(1)} %slice.16), channel_id=1, source_target_pairs={{0,1},{1,0},{2,3},{3,2},{4,5},{5,4},{6,7},{7,6},{8,9},{9,8},{10,11... | collective-permute-start | bytes 12296 | tf_op jit(solution)/shard_map/ppermute | solution.py:19
  11.4 10.7 %collective-permute-start.6 = (f32[2,128,256]{2,1,0:T(8,128)S(1)}, f32[2,128,256]{2,1,0:T(8,128)S(1)}, u32[]{:S(2)}, u32[]{:S(2)}) collective-permute-start(f32[2,128,256]{2,1,0:T(8,128)S(1)} %add.15.refs_0_), channel_id=1, source_target_pairs={{0,2},{1,3},{2,0},{3,1},{4,6},{5,7},{6,4},{7,5},{8,10},{9,11},{10,... | collective-permute-start | bytes 786440 | tf_op jit(solution)/shard_map/ppermute | solution.py:19
  13.0 13.7 %collective-permute-start.10 = (bf16[128,1024]{1,0:T(8,128)(2,1)S(1)}, bf16[128,1024]{1,0:T(8,128)(2,1)S(1)}, u32[]{:S(2)}, u32[]{:S(2)}) collective-permute-start(bf16[128,1024]{1,0:T(8,128)(2,1)S(1)} %collective-permute-done.1.refs_5_), channel_id=1, source_target_pairs={{0,4},{4,12},{12,8},{8,0},{1,5},{5,13},{13,9},{9,1},{2,6},{6,14},{... | collective-permute-start | bytes 786440 | tf_op jit(solution)/shard_map/ppermute | solution.py:199
  20.5 1.4 %collective-permute-start.4 = (f32[1,128,256]{2,1,0:T(8,128)S(1)}, f32[1,128,256]{2,1,0:T(8,128)S(1)}, u32[]{:S(2)}, u32[]{:S(2)}) collective-permute-start(f32[1,128,256]{2,1,0:T(8,128)S(1)} %get-tuple-element.21), channel_id=1, source_target_pairs={{0,1},{1,0},{2,3},{3,2},{4,5},{5,4},{6,7},{7,6},{8,9},{9,8},{10,11... | collective-permute-start | bytes 393224 | tf_op jit(solution)/shard_map/ppermute | solution.py:19
  20.6 1.5 %collective-permute-start.5 = (f32[1,128,256]{2,1,0:T(8,128)S(1)}, f32[1,128,256]{2,1,0:T(8,128)S(1)}, u32[]{:S(2)}, u32[]{:S(2)}) collective-permute-start(f32[1,128,256]{2,1,0:T(8,128)S(1)} %get-tuple-element.22), channel_id=1, source_target_pairs={{0,1},{1,0},{2,3},{3,2},{4,5},{5,4},{6,7},{7,6},{8,9},{9,8},{10,11... | collective-permute-start | bytes 393224 | tf_op jit(solution)/shard_map/ppermute | solution.py:19
  22.7 4.0 %collective-permute-start.7 = (f32[2,8,128]{2,1,0:T(8,128)S(1)}, f32[2,8,128]{2,1,0:T(8,128)S(1)}, u32[]{:S(2)}, u32[]{:S(2)}) collective-permute-start(f32[2,8,128]{2,1,0:T(8,128)S(1)} %get-tuple-element.18), channel_id=1, source_target_pairs={{0,1},{1,0},{2,3},{3,2},{4,5},{5,4},{6,7},{7,6},{8,9},{9,8},{10,11... | collective-permute-start | bytes 24584 | tf_op jit(solution)/shard_map/ppermute | solution.py:19
  23.1 3.7 %collective-permute-start.8 = (f32[2,8,128]{2,1,0:T(8,128)S(1)}, f32[2,8,128]{2,1,0:T(8,128)S(1)}, u32[]{:S(2)}, u32[]{:S(2)}) collective-permute-start(f32[2,8,128]{2,1,0:T(8,128)S(1)} %get-tuple-element.19), channel_id=1, source_target_pairs={{0,2},{1,3},{2,0},{3,1},{4,6},{5,7},{6,4},{7,5},{8,10},{9,11},{10,... | collective-permute-start | bytes 24584 | tf_op jit(solution)/shard_map/ppermute | solution.py:19
  23.6 3.2 %collective-permute-start.9 = (f32[2,8,128]{2,1,0:T(8,128)S(1)}, f32[2,8,128]{2,1,0:T(8,128)S(1)}, u32[]{:S(2)}, u32[]{:S(2)}) collective-permute-start(f32[2,8,128]{2,1,0:T(8,128)S(1)} %get-tuple-element.20), channel_id=1, source_target_pairs={{0,3},{1,2},{2,1},{3,0},{4,7},{5,6},{6,5},{7,4},{8,11},{9,10},{10,... | collective-permute-start | bytes 24584 | tf_op jit(solution)/shard_map/ppermute | solution.py:19
  27.1 1.9 %collective-permute-start.11 = (f32[8,512]{1,0:T(8,128)S(1)}, f32[8,512]{1,0:T(8,128)S(1)}, u32[]{:S(2)}, u32[]{:S(2)}) collective-permute-start(f32[8,512]{1,0:T(8,128)S(1)} %shard_map.68), channel_id=1, source_target_pairs={{0,1},{1,0},{2,3},{3,2},{4,5},{5,4},{6,7},{7,6},{8,9},{9,8},{10,11... | collective-permute-start | bytes 49160 | tf_op jit(solution)/shard_map/ppermute | solution.py:19
  27.3 3.7 %collective-permute-start.12 = (f32[8,512]{1,0:T(8,128)S(1)}, f32[8,512]{1,0:T(8,128)S(1)}, u32[]{:S(2)}, u32[]{:S(2)}) collective-permute-start(f32[8,512]{1,0:T(8,128)S(1)} %shard_map.68), channel_id=1, source_target_pairs={{0,2},{1,3},{2,0},{3,1},{4,6},{5,7},{6,4},{7,5},{8,10},{9,11},{10,... | collective-permute-start | bytes 49160 | tf_op jit(solution)/shard_map/ppermute | solution.py:19
  28.7 3.2 %collective-permute-start.13 = (f32[8,512]{1,0:T(8,128)S(1)}, f32[8,512]{1,0:T(8,128)S(1)}, u32[]{:S(2)}, u32[]{:S(2)}) collective-permute-start(f32[8,512]{1,0:T(8,128)S(1)} %shard_map.68), channel_id=1, source_target_pairs={{0,3},{1,2},{2,1},{3,0},{4,7},{5,6},{6,5},{7,4},{8,11},{9,10},{10,... | collective-permute-start | bytes 49160 | tf_op jit(solution)/shard_map/ppermute | solution.py:19

commit v16 on v15

--- a/solution.py
+++ b/solution.py
@@ -43,14 +43,15 @@
 LATER = 1<<10
 
 
-def project_kernel(steps, share, ahead, piece, after, act, og, wi, wo, lens, *refs):
+def project_kernel(blocks, share, ahead, piece, after, act, og, wi, wo, lens, *refs):
     refs = refs[after:]
     outs, (buf, wibuf, wobuf, lenbuf, sem, wsem) = refs[:-6], refs[-6:]
     me = lax.axis_index("tensor")
     rank = wibuf.shape[0]
-    slots = buf.shape[2]
-    count = len(steps) * share
+    count, slots = buf.shape[1:3]
     tokens = count * slots
+    starts = [(me ^ step) * share + first for step, first, _ in blocks]
+    ends = [sum(size for *_, size in blocks[: i + 1]) for i in range(len(blocks))]
     small = [
         pltpu.make_async_copy(wi, wibuf, wsem.at[0]),
         pltpu.make_async_copy(wo, wobuf, wsem.at[1]),
@@ -63,11 +64,11 @@
         copies.append(
             [
                 pltpu.make_async_copy(
-                    (act, og)[side].at[pl.ds((me ^ step) * share, share), :, pl.ds(at, width)],
-                    buf.at[slot, pl.ds(i * share, share), :, pl.ds(0, width)],
+                    (act, og)[side].at[pl.ds(start, size), :, pl.ds(at, width)],
+                    buf.at[slot, pl.ds(end - size, size), :, pl.ds(0, width)],
                     sem.at[slot, i],
                 )
-                for i, step in enumerate(steps)
+                for i, (start, end, (*_, size)) in enumerate(zip(starts, ends, blocks))
             ]
         )
     small[0].start()
@@ -94,22 +95,24 @@
     small[2].wait()
     col = lax.broadcasted_iota(jnp.int32, (rank, slots), 1)
     places = [out.at[i] for out in outs for i in range(out.shape[0])]
-    for slot, out in enumerate(places):
-        length = lenbuf[(me ^ steps[slot // share]) * share + slot % share]
+    seqs = [start + k for start, (*_, size) in zip(starts, blocks) for k in range(size)]
+    for slot, (out, seq) in enumerate(zip(places, seqs)):
+        length = lenbuf[seq]
         one = sums[0][:, slot * slots : (slot + 1) * slots] * (1.0 / length.astype(jnp.float32))
         out[:rank] = jnp.where(col < length, one, 0.0)
         out[rank:] = sums[1][:, slot * slots : (slot + 1) * slots]
 
 
 def project(act, og, wi, wo, lens, groups, share, ahead, piece, cost, after=()):
-    steps = [step for group in groups for step in group]
-    count = len(steps) * share
+    blocks = [block for group in groups for block in group]
+    counts = [sum(size for *_, size in group) for group in groups]
+    count = sum(counts)
     slots, feat, hidden = act.shape[1], act.shape[2], og.shape[2]
     rank = wi.shape[0]
     pieces = -(-feat // piece) - (-hidden // piece)
     return pl.pallas_call(
-        functools.partial(project_kernel, steps, share, ahead, piece, len(after)),
-        out_shape=[jax.ShapeDtypeStruct((len(group) * share, 2 * rank, slots), jnp.float32) for group in groups],
+        functools.partial(project_kernel, blocks, share, ahead, piece, len(after)),
+        out_shape=[jax.ShapeDtypeStruct((size, 2 * rank, slots), jnp.float32) for size in counts],
         in_specs=[HBM] * 5 + [VMEM] * len(after),
         out_specs=[VMEM] * len(groups),
         scratch_shapes=[
@@ -117,7 +120,7 @@
             pltpu.VMEM((rank, feat), wi.dtype),
             pltpu.VMEM((rank, hidden), wo.dtype),
             pltpu.SMEM(lens.shape, lens.dtype),
-            pltpu.SemaphoreType.DMA((pieces, len(steps))),
+            pltpu.SemaphoreType.DMA((pieces, len(blocks))),
             pltpu.SemaphoreType.DMA((3,)),
         ],
         compiler_params=pltpu.CompilerParams(vmem_limit_bytes=32 << 20),
@@ -212,15 +215,20 @@
 
     far = [CORES * x for x in range(1, size // CORES)]
     arrays = (activations, out_grads, proj_in.T, proj_out.T, lengths)
-    far_other, far_own = project(*arrays, [[step ^ 1 for step in far], far], share, 4, 512, COST, [own_tests])
+    early = share // 2
+    sends = [[(step ^ 1, 0, share) for step in far], [(step, 0, share) for step in far]]
+    far_other, far_own, *near_first = project(
+        *arrays, sends + [[(1, 0, early)]] * bool(early), share, 4, 512, COST, [own_tests]
+    )
     far_sum = far_own + xor_permute(far_other, "tensor", size, 1)
     sums = [xor_permute(far_sum[i * share : (i + 1) * share], "tensor", size, step) for i, step in enumerate(far)]
     here = xor_permute(tests[1][0][:16, :128], "tensor", size, 1)
-    near_other, near_own = project(*arrays, [[1], [0]], share, 4, 512, LATER, [far_sum, here])
+    groups_left = [[(1, early, share - early)], [(0, 0, share)]]
+    near_other, near_own = project(*arrays, groups_left, share, 5, 512, LATER, [far_sum, here])
     late = tests[2][0][: near_other.shape[1], : near_other.shape[2]].astype(jnp.float32)
-    pieces = [near_other[k : k + 1] for k in range(share)]
+    pieces = [near_other[k : k + 1] for k in range(share - early)]
     pieces[0] = pieces[0] + 0.0 * late[None]
-    arrived = jnp.concatenate([xor_permute(one, "tensor", size, 1) for one in pieces])
+    arrived = jnp.concatenate([xor_permute(one, "tensor", size, 1) for one in near_first + pieces])
 
     unit_outs = units([near_own, arrived] + sums, share, rank, size)
     unit_parts = [unit_outs[0]] + [xor_permute(unit_outs[step], "tensor", size, step) for step in range(1, size)]

time: 32.7 us -> 34.3 us (1.049)
  Pallas kernels: 12.5 us -> 14.4 us
  waiting for transfers between devices: 6.84 us -> 6.35 us
    pallas_call x2, Pallas kernels: 10.6 us -> 12.5 us  [project(): pl.pallas_call(functools.partial(project_kernel, blocks, share, ahead, pi...]
    ppermute x3, waiting for transfers between devices: 2.93 us -> 2.43 us  [shift(): lax.ppermute(value, 'dp', [(ring[i], ring[(i + step) % groups]) for i in...]
  transfers between devices with their start and end apart: 14 -> 14, of which waited for: 7 -> 4; matrix products, arithmetic and copies ran while one was open for 0% -> 0% of each run, Pallas kernels for 34% -> 38%
where the time goes in v16:
time: 34.3 us; the launch traced here: 34.1 us
  Pallas kernels  14.4 us (42%)
  starting transfers between devices  12.6 us (37%)
  waiting for transfers between devices  6.35 us (19%)
  other arithmetic  0.69 us (2%)
    pallas_call x2, Pallas kernels, project(): pl.pallas_call(functools.partial(project_kernel, blocks, share, ahead, pi...  12.5 us
    ppermute x3, starting transfers between devices, shift(): lax.ppermute(value, 'dp', [(ring[i], ring[(i + step) % groups]) for i in...  6.35 us
    ppermute x11, starting transfers between devices, xor_permute(): return lax.ppermute(value, axis, [(i, i ^ step) for i in range(size)])  6.26 us
    ppermute x11, waiting for transfers between devices, xor_permute(): return lax.ppermute(value, axis, [(i, i ^ step) for i in range(size)])  3.91 us
    ppermute x3, waiting for transfers between devices, shift(): lax.ppermute(value, 'dp', [(ring[i], ring[(i + step) % groups]) for i in...  2.43 us
    pallas_call x1, Pallas kernels, cut_tests(): pl.pallas_call(cut_kernel, out_shape=jax.ShapeDtypeStruct((rows, width //...  0.96 us
  transfers between devices with their start and end apart: 14, of which 4 were waited for; matrix products, arithmetic and copies ran while one was open for 0% of the time, Pallas kernels for 38%

profile of v16, /device:TPU:0, one launch (start us, length us, event | category | flops | bytes accessed | tf_op | source)
XLA Modules:
  0.0 34.1 jit_solution(4793955288177709216)
XLA Ops:
  0.0 1.0 %shard_map.64.refs_0_.refs_4_ = bf16[128,1024]{1,0:T(8,128)(2,1)S(1)} custom-call(bf16[128,4096]{1,0:T(8,128)(2,1)} %tests.1), custom_call_target="tpu_custom_call" | custom-call | tf_op jit(solution)/shard_map/pallas_call | solution.py:32
  1.0 3.1 %collective-permute-start.1 = (bf16[128,1024]{1,0:T(8,128)(2,1)S(1)}, bf16[128,1024]{1,0:T(8,128)(2,1)S(1)}, u32[]{:S(2)}, u32[]{:S(2)}) collective-permute-start(bf16[128,1024]{1,0:T(8,128)(2,1)S(1)} %shard_map.64.refs_0_.refs_4_), channel_id=1, source_target_pairs={{0,4},{4,12},{12,8},{8,0},{1,5},{5,13},{13,9},{9,1},{2,6},{6,14},{... | collective-permute-start | bytes 786440 | tf_op jit(solution)/shard_map/ppermute | solution.py:202
  4.0 7.3 %shard_map.65 = (f32[2,128,256]{2,1,0:T(8,128)S(1)}, f32[2,128,256]{2,1,0:T(8,128)S(1)}, f32[1,128,256]{2,1,0:T(8,128)S(1)}) custom-call(bf16[8,256,1024]{2,1,0:T(8,128)(2,1)} %act.3, bf16[8,256,3584]{2,1,0:T(8,128)(2,1)} %og.3, bf16[64,1024]{1,0:T(8,128)(2,1)} %bitcast.6, bf16[64,3584]{1,0:T(8,128)(2,1)} %bitcast.4, s32[8]{0:T(128)} %lens.3, ...), custom_call_target="tpu_custom_call" | custom-call | flops 4294967296 | bytes 16777216 | tf_op jit(solution)/shard_map/pallas_call | solution.py:113
  11.3 0.1 collective-permute-start
  11.4 1.1 %collective-permute-start.4 = (bf16[128,1024]{1,0:T(8,128)(2,1)S(1)}, bf16[128,1024]{1,0:T(8,128)(2,1)S(1)}, u32[]{:S(2)}, u32[]{:S(2)}) collective-permute-start(bf16[128,1024]{1,0:T(8,128)(2,1)S(1)} %shard_map.64.refs_0_.refs_4_), channel_id=1, source_target_pairs={{0,8},{4,0},{12,4},{8,12},{1,9},{5,1},{13,5},{9,13},{2,10},{6,2},{... | collective-permute-start | bytes 786440 | tf_op jit(solution)/shard_map/ppermute | solution.py:202
  12.5 0.0 collective-permute-done.1.refs_5_
  12.5 0.2 collective-permute-start.2
  12.7 0.3 %collective-permute-start.3 = (f32[1,128,256]{2,1,0:T(8,128)S(1)}, f32[1,128,256]{2,1,0:T(8,128)S(1)}, u32[]{:S(2)}, u32[]{:S(2)}) collective-permute-start(f32[1,128,256]{2,1,0:T(8,128)S(1)} %get-tuple-element.17), channel_id=1, source_target_pairs={{0,1},{1,0},{2,3},{3,2},{4,5},{5,4},{6,7},{7,6},{8,9},{9,8},{10,11... | collective-permute-start | bytes 393224 | tf_op jit(solution)/shard_map/ppermute | solution.py:19
  13.0 0.0 collective-permute-done
  13.1 1.8 %collective-permute-start.6 = (f32[2,128,256]{2,1,0:T(8,128)S(1)}, f32[2,128,256]{2,1,0:T(8,128)S(1)}, u32[]{:S(2)}, u32[]{:S(2)}) collective-permute-start(f32[2,128,256]{2,1,0:T(8,128)S(1)} %add.15.refs_0_), channel_id=1, source_target_pairs={{0,2},{1,3},{2,0},{3,1},{4,6},{5,7},{6,4},{7,5},{8,10},{9,11},{10,... | collective-permute-start | bytes 786440 | tf_op jit(solution)/shard_map/ppermute | solution.py:19
  14.9 2.2 %collective-permute-start.10 = (bf16[128,1024]{1,0:T(8,128)(2,1)S(1)}, bf16[128,1024]{1,0:T(8,128)(2,1)S(1)}, u32[]{:S(2)}, u32[]{:S(2)}) collective-permute-start(bf16[128,1024]{1,0:T(8,128)(2,1)S(1)} %collective-permute-done.1.refs_5_), channel_id=1, source_target_pairs={{0,4},{4,12},{12,8},{8,0},{1,5},{5,13},{13,9},{9,1},{2,6},{6,14},{... | collective-permute-start | bytes 786440 | tf_op jit(solution)/shard_map/ppermute | solution.py:202
  17.1 0.0 collective-permute-done.2.refs_1_
  17.1 5.2 %shard_map.66 = (f32[1,128,256]{2,1,0:T(8,128)S(1)}, f32[2,128,256]{2,1,0:T(8,128)S(1)}) custom-call(bf16[8,256,1024]{2,1,0:T(8,128)(2,1)} %act.3, bf16[8,256,3584]{2,1,0:T(8,128)(2,1)} %og.3, bf16[64,1024]{1,0:T(8,128)(2,1)} %bitcast.7, bf16[64,3584]{1,0:T(8,128)(2,1)} %bitcast.5, s32[8]{0:T(128)} %lens.3, f32[2,128,256]{2,1,0:T(8,128)S(1)} %add.15.refs_0_, ...), custom_call_target="tpu_custom_call" | custom-call | flops 1024 | bytes 4 | tf_op jit(solution)/shard_map/pallas_call | solution.py:113
  22.3 0.0 collective-permute-done.4.refs_6_
  22.3 0.1 collective-permute-start.5
  22.4 1.3 %collective-permute-done.5 = f32[1,128,256]{2,1,0:T(8,128)S(1)} collective-permute-done((f32[1,128,256]{2,1,0:T(8,128)S(1)}, f32[1,128,256]{2,1,0:T(8,128)S(1)}, u32[]{:S(2)}, u32[]{:S(2)}) %collective-permute-start.5) | collective-permute-done | bytes 131104 | tf_op jit(solution)/shard_map/ppermute | solution.py:19
  23.8 0.5 %shard_map.67 = (f32[2,8,128]{2,1,0:T(8,128)S(1)}, f32[2,8,128]{2,1,0:T(8,128)S(1)}, f32[2,8,128]{2,1,0:T(8,128)S(1)}, f32[2,8,128]{2,1,0:T(8,128)S(1)}) custom-call(f32[2,128,256]{2,1,0:T(8,128)S(1)} %get-tuple-element.16.refs_0_, f32[2,128,256]{2,1,0:T(8,128)S(1)} %pad_maximum_fusion.refs_1_, f32[2,128,256]{2,1,0:T(8,128)S(1)} %collective-permute-done.6.refs_2_), custom_call_target="tpu_custom_call" | custom-call | tf_op jit(solution)/shard_map/pallas_call | solution.py:160
  24.3 0.2 collective-permute-start.7
  24.5 0.6 %collective-permute-start.8 = (f32[2,8,128]{2,1,0:T(8,128)S(1)}, f32[2,8,128]{2,1,0:T(8,128)S(1)}, u32[]{:S(2)}, u32[]{:S(2)}) collective-permute-start(f32[2,8,128]{2,1,0:T(8,128)S(1)} %get-tuple-element.21), channel_id=1, source_target_pairs={{0,2},{1,3},{2,0},{3,1},{4,6},{5,7},{6,4},{7,5},{8,10},{9,11},{10,... | collective-permute-start | bytes 24584 | tf_op jit(solution)/shard_map/ppermute | solution.py:19
  25.1 1.2 %collective-permute-start.9 = (f32[2,8,128]{2,1,0:T(8,128)S(1)}, f32[2,8,128]{2,1,0:T(8,128)S(1)}, u32[]{:S(2)}, u32[]{:S(2)}) collective-permute-start(f32[2,8,128]{2,1,0:T(8,128)S(1)} %get-tuple-element.22), channel_id=1, source_target_pairs={{0,3},{1,2},{2,1},{3,0},{4,7},{5,6},{6,5},{7,4},{8,11},{9,10},{10,... | collective-permute-start | bytes 24584 | tf_op jit(solution)/shard_map/ppermute | solution.py:19
  26.2 2.4 %collective-permute-done.10.refs_7_ = bf16[128,1024]{1,0:T(8,128)(2,1)S(1)} collective-permute-done((bf16[128,1024]{1,0:T(8,128)(2,1)S(1)}, bf16[128,1024]{1,0:T(8,128)(2,1)S(1)}, u32[]{:S(2)}, u32[]{:S(2)}) %collective-permute-start.10) | collective-permute-done | bytes 262176 | tf_op jit(solution)/shard_map/ppermute | solution.py:202
  28.7 0.0 collective-permute-done.7.refs_1_
  28.7 0.0 collective-permute-done.8.refs_2_
  28.7 0.0 collective-permute-done.9.refs_3_
  28.7 0.4 %shard_map.68 = f32[8,512]{1,0:T(8,128)S(1)} custom-call(f32[2,8,128]{2,1,0:T(8,128)S(1)} %get-tuple-element.19.refs_0_, f32[2,8,128]{2,1,0:T(8,128)S(1)} %collective-permute-done.7.refs_1_, f32[2,8,128]{2,1,0:T(8,128)S(1)} %collective-permute-done.8.refs_2_, f32[2,8,128]{2,1,0:T(8,128)S(1)} %collective-permute-done.9.refs_3_, ...), custom_call_target="tpu_custom_call" | custom-call | tf_op jit(solution)/shard_map/pallas_call | solution.py:188
  29.0 0.0 collective-permute-start.11
  29.1 1.3 %collective-permute-start.12 = (f32[8,512]{1,0:T(8,128)S(1)}, f32[8,512]{1,0:T(8,128)S(1)}, u32[]{:S(2)}, u32[]{:S(2)}) collective-permute-start(f32[8,512]{1,0:T(8,128)S(1)} %shard_map.68), channel_id=1, source_target_pairs={{0,2},{1,3},{2,0},{3,1},{4,6},{5,7},{6,4},{7,5},{8,10},{9,11},{10,... | collective-permute-start | bytes 49160 | tf_op jit(solution)/shard_map/ppermute | solution.py:19
  30.3 0.6 %collective-permute-start.13 = (f32[8,512]{1,0:T(8,128)S(1)}, f32[8,512]{1,0:T(8,128)S(1)}, u32[]{:S(2)}, u32[]{:S(2)}) collective-permute-start(f32[8,512]{1,0:T(8,128)S(1)} %shard_map.68), channel_id=1, source_target_pairs={{0,3},{1,2},{2,1},{3,0},{4,7},{5,6},{6,5},{7,4},{8,11},{9,10},{10,... | collective-permute-start | bytes 49160 | tf_op jit(solution)/shard_map/ppermute | solution.py:19
  30.9 0.0 collective-permute-done.11
  30.9 1.9 %collective-permute-done.12 = f32[8,512]{1,0:T(8,128)S(1)} collective-permute-done((f32[8,512]{1,0:T(8,128)S(1)}, f32[8,512]{1,0:T(8,128)S(1)}, u32[]{:S(2)}, u32[]{:S(2)}) %collective-permute-start.12) | collective-permute-done | bytes 16416 | tf_op jit(solution)/shard_map/ppermute | solution.py:19
  32.8 0.7 %collective-permute-done.13 = f32[8,512]{1,0:T(8,128)S(1)} collective-permute-done((f32[8,512]{1,0:T(8,128)S(1)}, f32[8,512]{1,0:T(8,128)S(1)}, u32[]{:S(2)}, u32[]{:S(2)}) %collective-permute-start.13) | collective-permute-done | bytes 16416 | tf_op jit(solution)/shard_map/ppermute | solution.py:19
  33.5 0.6 %add_add_fusion = f32[8,512]{1,0:T(8,128)} fusion(f32[8,512]{1,0:T(8,128)S(1)} %collective-permute-done.12, f32[8,512]{1,0:T(8,128)S(1)} %collective-permute-done.13, f32[8,512]{1,0:T(8,128)S(1)} %shard_map.68, f32[8,512]{1,0:T(8,128)S(1)} %collective-permute-done.11), kind=kLoop, calls=%fused_computation.2 | loop fusion | flops 12288 | bytes 81920 | tf_op jit(solution)/shard_map/add | solution.py:238
  (6 shorter events, 0.1 us)
Async XLA Ops:
  1.0 11.5 %collective-permute-start.1 = (bf16[128,1024]{1,0:T(8,128)(2,1)S(1)}, bf16[128,1024]{1,0:T(8,128)(2,1)S(1)}, u32[]{:S(2)}, u32[]{:S(2)}) collective-permute-start(bf16[128,1024]{1,0:T(8,128)(2,1)S(1)} %shard_map.64.refs_0_.refs_4_), channel_id=1, source_target_pairs={{0,4},{4,12},{12,8},{8,0},{1,5},{5,13},{13,9},{9,1},{2,6},{6,14},{... | collective-permute-start | bytes 786440 | tf_op jit(solution)/shard_map/ppermute | solution.py:202
  11.3 1.7 %collective-permute-start = (f32[2,128,256]{2,1,0:T(8,128)S(1)}, f32[2,128,256]{2,1,0:T(8,128)S(1)}, u32[]{:S(2)}, u32[]{:S(2)}) collective-permute-start(f32[2,128,256]{2,1,0:T(8,128)S(1)} %get-tuple-element.15), channel_id=1, source_target_pairs={{0,1},{1,0},{2,3},{3,2},{4,5},{5,4},{6,7},{7,6},{8,9},{9,8},{10,11... | collective-permute-start | bytes 786440 | tf_op jit(solution)/shard_map/ppermute | solution.py:19
  11.4 10.9 %collective-permute-start.4 = (bf16[128,1024]{1,0:T(8,128)(2,1)S(1)}, bf16[128,1024]{1,0:T(8,128)(2,1)S(1)}, u32[]{:S(2)}, u32[]{:S(2)}) collective-permute-start(bf16[128,1024]{1,0:T(8,128)(2,1)S(1)} %shard_map.64.refs_0_.refs_4_), channel_id=1, source_target_pairs={{0,8},{4,0},{12,4},{8,12},{1,9},{5,1},{13,5},{9,13},{2,10},{6,2},{... | collective-permute-start | bytes 786440 | tf_op jit(solution)/shard_map/ppermute | solution.py:202
  12.5 4.5 %collective-permute-start.2 = (bf16[16,128]{1,0:T(8,128)(2,1)S(1)}, bf16[16,128]{1,0:T(8,128)(2,1)S(1)}, u32[]{:S(2)}, u32[]{:S(2)}) collective-permute-start(bf16[16,128]{1,0:T(8,128)(2,1)S(1)} %slice.8), channel_id=1, source_target_pairs={{0,1},{1,0},{2,3},{3,2},{4,5},{5,4},{6,7},{7,6},{8,9},{9,8},{10,11... | collective-permute-start | bytes 12296 | tf_op jit(solution)/shard_map/ppermute | solution.py:19
  12.7 9.7 %collective-permute-start.3 = (f32[1,128,256]{2,1,0:T(8,128)S(1)}, f32[1,128,256]{2,1,0:T(8,128)S(1)}, u32[]{:S(2)}, u32[]{:S(2)}) collective-permute-start(f32[1,128,256]{2,1,0:T(8,128)S(1)} %get-tuple-element.17), channel_id=1, source_target_pairs={{0,1},{1,0},{2,3},{3,2},{4,5},{5,4},{6,7},{7,6},{8,9},{9,8},{10,11... | collective-permute-start | bytes 393224 | tf_op jit(solution)/shard_map/ppermute | solution.py:19
  13.1 10.7 %collective-permute-start.6 = (f32[2,128,256]{2,1,0:T(8,128)S(1)}, f32[2,128,256]{2,1,0:T(8,128)S(1)}, u32[]{:S(2)}, u32[]{:S(2)}) collective-permute-start(f32[2,128,256]{2,1,0:T(8,128)S(1)} %add.15.refs_0_), channel_id=1, source_target_pairs={{0,2},{1,3},{2,0},{3,1},{4,6},{5,7},{6,4},{7,5},{8,10},{9,11},{10,... | collective-permute-start | bytes 786440 | tf_op jit(solution)/shard_map/ppermute | solution.py:19
  14.9 13.8 %collective-permute-start.10 = (bf16[128,1024]{1,0:T(8,128)(2,1)S(1)}, bf16[128,1024]{1,0:T(8,128)(2,1)S(1)}, u32[]{:S(2)}, u32[]{:S(2)}) collective-permute-start(bf16[128,1024]{1,0:T(8,128)(2,1)S(1)} %collective-permute-done.1.refs_5_), channel_id=1, source_target_pairs={{0,4},{4,12},{12,8},{8,0},{1,5},{5,13},{13,9},{9,1},{2,6},{6,14},{... | collective-permute-start | bytes 786440 | tf_op jit(solution)/shard_map/ppermute | solution.py:202
  22.3 1.4 %collective-permute-start.5 = (f32[1,128,256]{2,1,0:T(8,128)S(1)}, f32[1,128,256]{2,1,0:T(8,128)S(1)}, u32[]{:S(2)}, u32[]{:S(2)}) collective-permute-start(f32[1,128,256]{2,1,0:T(8,128)S(1)} %bitcast_add_fusion), channel_id=1, source_target_pairs={{0,1},{1,0},{2,3},{3,2},{4,5},{5,4},{6,7},{7,6},{8,9},{9,8},{10,11... | collective-permute-start | bytes 393224 | tf_op jit(solution)/shard_map/ppermute | solution.py:19
  24.3 4.4 %collective-permute-start.7 = (f32[2,8,128]{2,1,0:T(8,128)S(1)}, f32[2,8,128]{2,1,0:T(8,128)S(1)}, u32[]{:S(2)}, u32[]{:S(2)}) collective-permute-start(f32[2,8,128]{2,1,0:T(8,128)S(1)} %get-tuple-element.20), channel_id=1, source_target_pairs={{0,1},{1,0},{2,3},{3,2},{4,5},{5,4},{6,7},{7,6},{8,9},{9,8},{10,11... | collective-permute-start | bytes 24584 | tf_op jit(solution)/shard_map/ppermute | solution.py:19
  24.5 4.1 %collective-permute-start.8 = (f32[2,8,128]{2,1,0:T(8,128)S(1)}, f32[2,8,128]{2,1,0:T(8,128)S(1)}, u32[]{:S(2)}, u32[]{:S(2)}) collective-permute-start(f32[2,8,128]{2,1,0:T(8,128)S(1)} %get-tuple-element.21), channel_id=1, source_target_pairs={{0,2},{1,3},{2,0},{3,1},{4,6},{5,7},{6,4},{7,5},{8,10},{9,11},{10,... | collective-permute-start | bytes 24584 | tf_op jit(solution)/shard_map/ppermute | solution.py:19
  25.1 3.6 %collective-permute-start.9 = (f32[2,8,128]{2,1,0:T(8,128)S(1)}, f32[2,8,128]{2,1,0:T(8,128)S(1)}, u32[]{:S(2)}, u32[]{:S(2)}) collective-permute-start(f32[2,8,128]{2,1,0:T(8,128)S(1)} %get-tuple-element.22), channel_id=1, source_target_pairs={{0,3},{1,2},{2,1},{3,0},{4,7},{5,6},{6,5},{7,4},{8,11},{9,10},{10,... | collective-permute-start | bytes 24584 | tf_op jit(solution)/shard_map/ppermute | solution.py:19
  29.0 1.9 %collective-permute-start.11 = (f32[8,512]{1,0:T(8,128)S(1)}, f32[8,512]{1,0:T(8,128)S(1)}, u32[]{:S(2)}, u32[]{:S(2)}) collective-permute-start(f32[8,512]{1,0:T(8,128)S(1)} %shard_map.68), channel_id=1, source_target_pairs={{0,1},{1,0},{2,3},{3,2},{4,5},{5,4},{6,7},{7,6},{8,9},{9,8},{10,11... | collective-permute-start | bytes 49160 | tf_op jit(solution)/shard_map/ppermute | solution.py:19
  29.1 3.7 %collective-permute-start.12 = (f32[8,512]{1,0:T(8,128)S(1)}, f32[8,512]{1,0:T(8,128)S(1)}, u32[]{:S(2)}, u32[]{:S(2)}) collective-permute-start(f32[8,512]{1,0:T(8,128)S(1)} %shard_map.68), channel_id=1, source_target_pairs={{0,2},{1,3},{2,0},{3,1},{4,6},{5,7},{6,4},{7,5},{8,10},{9,11},{10,... | collective-permute-start | bytes 49160 | tf_op jit(solution)/shard_map/ppermute | solution.py:19
  30.3 3.2 %collective-permute-start.13 = (f32[8,512]{1,0:T(8,128)S(1)}, f32[8,512]{1,0:T(8,128)S(1)}, u32[]{:S(2)}, u32[]{:S(2)}) collective-permute-start(f32[8,512]{1,0:T(8,128)S(1)} %shard_map.68), channel_id=1, source_target_pairs={{0,3},{1,2},{2,1},{3,0},{4,7},{5,6},{6,5},{7,4},{8,11},{9,10},{10,... | collective-permute-start | bytes 49160 | tf_op jit(solution)/shard_map/ppermute | solution.py:19

commit v17 on v15

--- a/solution.py
+++ b/solution.py
@@ -19,110 +19,113 @@
     return lax.ppermute(value, axis, [(i, i ^ step) for i in range(size)])
 
 
-def cut_kernel(tests, out, sem):
-    width = out.shape[1]
+def first_kernel(tests, wi, wo, own, wide, wibuf, wobuf, sem):
+    width = own.shape[1]
     start = pl.multiple_of(lax.axis_index("tensor") * width, 128)
-    copy = pltpu.make_async_copy(tests.at[:, pl.ds(start, width)], out, sem)
-    copy.start()
-    copy.wait()
-
-
-def cut_tests(tests, size):
+    copies = [
+        pltpu.make_async_copy(wi, wibuf, sem.at[0]),
+        pltpu.make_async_copy(wo, wobuf, sem.at[1]),
+        pltpu.make_async_copy(tests.at[:, pl.ds(start, width)], own, sem.at[2]),
+    ]
+    for copy in copies:
+        copy.start()
+    feat = wibuf.shape[1]
+    for side, buf in enumerate((wibuf, wobuf)):
+        copies[side].wait()
+        for at in range(0, buf.shape[1], 256):
+            weight = buf[:, at : at + 256]
+            none = jnp.zeros_like(weight)
+            both = jnp.concatenate([none, weight] if side else [weight, none], axis=0)
+            wide[side * feat + at : side * feat + at + weight.shape[1]] = both.T
+    copies[2].wait()
+
+
+def first(tests, wi, wo, size):
     rows, width = tests.shape
-    return pl.pallas_call(
-        cut_kernel,
-        out_shape=jax.ShapeDtypeStruct((rows, width // size), tests.dtype),
-        in_specs=[HBM],
-        out_specs=VMEM,
-        scratch_shapes=[pltpu.SemaphoreType.DMA],
+    rank, feat = wi.shape
+    return pl.pallas_call(
+        first_kernel,
+        out_shape=[
+            jax.ShapeDtypeStruct((rows, width // size), tests.dtype),
+            jax.ShapeDtypeStruct((feat + wo.shape[1], 2 * rank), wi.dtype),
+        ],
+        in_specs=[HBM] * 3,
+        out_specs=[VMEM] * 2,
+        scratch_shapes=[pltpu.VMEM(wi.shape, wi.dtype), pltpu.VMEM(wo.shape, wo.dtype), pltpu.SemaphoreType.DMA((3,))],
         compiler_params=SMALL,
-    )(in_hbm(tests))
+    )(in_hbm(tests), in_hbm(wi), in_hbm(wo))
 
 
 COST = 1 << 32
 LATER = 1<<10
 
 
-def project_kernel(steps, share, ahead, piece, after, act, og, wi, wo, lens, *refs):
+def project_kernel(steps, share, ahead, piece, after, act, og, lens, wide, *refs):
     refs = refs[after:]
-    outs, (buf, wibuf, wobuf, lenbuf, sem, wsem) = refs[:-6], refs[-6:]
+    outs, (buf, lenbuf, sem, lensem) = refs[:-4], refs[-4:]
     me = lax.axis_index("tensor")
-    rank = wibuf.shape[0]
-    slots = buf.shape[2]
-    count = len(steps) * share
-    tokens = count * slots
-    small = [
-        pltpu.make_async_copy(wi, wibuf, wsem.at[0]),
-        pltpu.make_async_copy(wo, wobuf, wsem.at[1]),
-        pltpu.make_async_copy(lens, lenbuf, wsem.at[2]),
+    rank = wide.shape[1] // 2
+    slots, feat = act.shape[1:]
+    lencopy = pltpu.make_async_copy(lens, lenbuf, lensem)
+    pieces = [
+        (side, at, min(piece, ref.shape[2] - at)) for side, ref in enumerate((act, og)) for at in range(0, ref.shape[2], piece)
     ]
-    pieces = [(side, at) for side, ref in enumerate((act, og)) for at in range(0, ref.shape[2], piece)]
-    copies = []
-    for slot, (side, at) in enumerate(pieces):
-        width = min(piece, (act, og)[side].shape[2] - at)
-        copies.append(
-            [
-                pltpu.make_async_copy(
-                    (act, og)[side].at[pl.ds((me ^ step) * share, share), :, pl.ds(at, width)],
-                    buf.at[slot, pl.ds(i * share, share), :, pl.ds(0, width)],
-                    sem.at[slot, i],
-                )
-                for i, step in enumerate(steps)
-            ]
-        )
-    small[0].start()
-    for slot, group in enumerate(copies):
-        if slot == 1:
-            small[1].start()
-            small[2].start()
-        if slot < ahead:
-            for copy in group:
-                copy.start()
-    sums = [None, None]
-    for slot, (side, at) in enumerate(pieces):
-        if at == 0:
-            small[side].wait()
+    copies = [
+        [
+            pltpu.make_async_copy(
+                (act, og)[side].at[pl.ds((me ^ step) * share, share), :, pl.ds(at, width)],
+                buf.at[slot, pl.ds(i * share, share), :, pl.ds(0, width)],
+                sem.at[slot, i],
+            )
+            for i, step in enumerate(steps)
+        ]
+        for slot, (side, at, width) in enumerate(pieces)
+    ]
+    for group in copies[:ahead]:
+        for copy in group:
+            copy.start()
+    lencopy.start()
+    sums = [None] * len(steps)
+    for slot, (side, at, width) in enumerate(pieces):
         for copy in copies[slot]:
             copy.wait()
-        if slot + ahead < len(pieces):
-            for copy in copies[slot + ahead]:
-                copy.start()
-        weight = (wibuf, wobuf)[side][:, at : at + piece]
-        token = buf[slot].reshape(tokens, piece)[:, : weight.shape[1]]
-        part = lax.dot_general(weight, token, NT, preferred_element_type=jnp.float32)
-        sums[side] = part if sums[side] is None else sums[side] + part
-    small[2].wait()
+        for copy in copies[slot + ahead] if slot + ahead < len(copies) else ():
+            copy.start()
+        weight = wide[side * feat + at : side * feat + at + width]
+        for i in range(len(steps)):
+            token = buf[slot, i * share : (i + 1) * share].reshape(share * slots, piece)[:, :width]
+            part = jnp.dot(token, weight, preferred_element_type=jnp.float32)
+            sums[i] = part if sums[i] is None else sums[i] + part
+    lencopy.wait()
     col = lax.broadcasted_iota(jnp.int32, (rank, slots), 1)
     places = [out.at[i] for out in outs for i in range(out.shape[0])]
     for slot, out in enumerate(places):
-        length = lenbuf[(me ^ steps[slot // share]) * share + slot % share]
-        one = sums[0][:, slot * slots : (slot + 1) * slots] * (1.0 / length.astype(jnp.float32))
-        out[:rank] = jnp.where(col < length, one, 0.0)
-        out[rank:] = sums[1][:, slot * slots : (slot + 1) * slots]
-
-
-def project(act, og, wi, wo, lens, groups, share, ahead, piece, cost, after=()):
+        i, k = divmod(slot, share)
+        length = lenbuf[(me ^ steps[i]) * share + k]
+        both = sums[i][k * slots : (k + 1) * slots].T
+        out[:rank] = jnp.where(col < length, both[:rank] * (1.0 / length.astype(jnp.float32)), 0.0)
+        out[rank:] = both[rank:]
+
+
+def project(act, og, lens, wide, groups, share, ahead, piece, cost, after=()):
     steps = [step for group in groups for step in group]
     count = len(steps) * share
     slots, feat, hidden = act.shape[1], act.shape[2], og.shape[2]
-    rank = wi.shape[0]
     pieces = -(-feat // piece) - (-hidden // piece)
     return pl.pallas_call(
         functools.partial(project_kernel, steps, share, ahead, piece, len(after)),
-        out_shape=[jax.ShapeDtypeStruct((len(group) * share, 2 * rank, slots), jnp.float32) for group in groups],
-        in_specs=[HBM] * 5 + [VMEM] * len(after),
+        out_shape=[jax.ShapeDtypeStruct((len(group) * share, wide.shape[1], slots), jnp.float32) for group in groups],
+        in_specs=[HBM] * 3 + [VMEM] * (1 + len(after)),
         out_specs=[VMEM] * len(groups),
         scratch_shapes=[
             pltpu.VMEM((pieces, count, slots, piece), act.dtype),
-            pltpu.VMEM((rank, feat), wi.dtype),
-            pltpu.VMEM((rank, hidden), wo.dtype),
             pltpu.SMEM(lens.shape, lens.dtype),
             pltpu.SemaphoreType.DMA((pieces, len(steps))),
-            pltpu.SemaphoreType.DMA((3,)),
+            pltpu.SemaphoreType.DMA,
         ],
         compiler_params=pltpu.CompilerParams(vmem_limit_bytes=32 << 20),
         cost_estimate=pl.CostEstimate(flops=cost, bytes_accessed=cost // 256, transcendentals=0),
-    )(*map(in_hbm, (act, og, wi, wo, lens)), *after)
+    )(*map(in_hbm, (act, og, lens)), wide, *after)
 
 
 def unit_kernel(share, rank, size, *refs):
@@ -207,11 +210,11 @@
 def shards(size, groups, activations, out_grads, proj_in, proj_out, lengths, test_grads):
     rank = proj_in.shape[1]
     share = activations.shape[0] // size
-    own_tests = cut_tests(test_grads, size)
+    own_tests, wide = first(test_grads, proj_in.T, proj_out.T, size)
     tests = gather_tests(own_tests, groups)
 
     far = [CORES * x for x in range(1, size // CORES)]
-    arrays = (activations, out_grads, proj_in.T, proj_out.T, lengths)
+    arrays = (activations, out_grads, lengths, wide)
     far_other, far_own = project(*arrays, [[step ^ 1 for step in far], far], share, 4, 512, COST, [own_tests])
     far_sum = far_own + xor_permute(far_other, "tensor", size, 1)
     sums = [xor_permute(far_sum[i * share : (i + 1) * share], "tensor", size, step) for i, step in enumerate(far)]

time: 32.7 us -> 32.7 us (level)
  waiting for transfers between devices: 6.84 us -> 7.5 us
  starting transfers between devices: 12.4 us -> 12 us
    pallas_call x2, Pallas kernels: 10.6 us -> 9.93 us  [project(): pl.pallas_call(functools.partial(project_kernel, steps, share, ahead, pie...]
    ppermute x3, waiting for transfers between devices: 2.93 us -> 3.62 us  [shift(): lax.ppermute(value, 'dp', [(ring[i], ring[(i + step) % groups]) for i in...]
    pallas_call x1, Pallas kernels: 0.96 us -> 1.4 us  [first(): pl.pallas_call(first_kernel, out_shape=[jax.ShapeDtypeStruct((rows, width...]
    ppermute x3, starting transfers between devices: 6.3 us -> 5.94 us  [shift(): lax.ppermute(value, 'dp', [(ring[i], ring[(i + step) % groups]) for i in...]
  transfers between devices with their start and end apart: 14 -> 14, of which waited for: 7 -> 6; matrix products, arithmetic and copies ran while one was open for 0% -> 0% of each run, Pallas kernels for 34% -> 32%
where the time goes in v17:
time: 32.7 us; the launch traced here: 32.5 us
  Pallas kernels  12.2 us (37%)
  starting transfers between devices  12 us (37%)
  waiting for transfers between devices  7.5 us (23%)
  other arithmetic  0.69 us (2%)
    pallas_call x2, Pallas kernels, project(): pl.pallas_call(functools.partial(project_kernel, steps, share, ahead, pie...  9.93 us
    ppermute x11, starting transfers between devices, xor_permute(): return lax.ppermute(value, axis, [(i, i ^ step) for i in range(size)])  6.05 us
    ppermute x3, starting transfers between devices, shift(): lax.ppermute(value, 'dp', [(ring[i], ring[(i + step) % groups]) for i in...  5.94 us
    ppermute x11, waiting for transfers between devices, xor_permute(): return lax.ppermute(value, axis, [(i, i ^ step) for i in range(size)])  3.88 us
    ppermute x3, waiting for transfers between devices, shift(): lax.ppermute(value, 'dp', [(ring[i], ring[(i + step) % groups]) for i in...  3.62 us
    pallas_call x1, Pallas kernels, first(): pl.pallas_call(first_kernel, out_shape=[jax.ShapeDtypeStruct((rows, width...  1.4 us
  transfers between devices with their start and end apart: 14, of which 6 were waited for; matrix products, arithmetic and copies ran while one was open for 0% of the time, Pallas kernels for 32%

profile of v17, /device:TPU:0, one launch (start us, length us, event | category | flops | bytes accessed | tf_op | source)
XLA Modules:
  0.0 32.5 jit_solution(17379112708678054991)
XLA Ops:
  0.0 1.4 %shard_map.64 = (bf16[128,1024]{1,0:T(8,128)(2,1)S(1)}, bf16[4608,128]{1,0:T(8,128)(2,1)S(1)}) custom-call(bf16[128,4096]{1,0:T(8,128)(2,1)} %tests.1, bf16[64,1024]{1,0:T(8,128)(2,1)} %bitcast.5, bf16[64,3584]{1,0:T(8,128)(2,1)} %bitcast.4), custom_call_target="tpu_custom_call" | custom-call | tf_op jit(solution)/shard_map/pallas_call | solution.py:46
  1.4 3.1 %collective-permute-start.1 = (bf16[128,1024]{1,0:T(8,128)(2,1)S(1)}, bf16[128,1024]{1,0:T(8,128)(2,1)S(1)}, u32[]{:S(2)}, u32[]{:S(2)}) collective-permute-start(bf16[128,1024]{1,0:T(8,128)(2,1)S(1)} %get-tuple-element.16.refs_0_.refs_4_), channel_id=1, source_target_pairs={{0,4},{4,12},{12,8},{8,0},{1,5},{5,13},{13,9},{9,1},{2,6},{6,14},{... | collective-permute-start | bytes 786440 | tf_op jit(solution)/shard_map/ppermute | solution.py:202
  4.5 5.0 %shard_map.65 = (f32[2,128,256]{2,1,0:T(8,128)S(1)}, f32[2,128,256]{2,1,0:T(8,128)S(1)}) custom-call(bf16[8,256,1024]{2,1,0:T(8,128)(2,1)} %act.3, bf16[8,256,3584]{2,1,0:T(8,128)(2,1)} %og.3, s32[8]{0:T(128)} %lens.3, bf16[4608,128]{1,0:T(8,128)(2,1)S(1)} %get-tuple-element.15.wide, bf16[128,1024]{1,0:T(8,128)(2,1)S(1)} %get-tuple-element.16.refs_0_.refs_4_), custom_call_target="tpu_custom_call" | custom-call | flops 4294967296 | bytes 16777216 | tf_op jit(solution)/shard_map/pallas_call | solution.py:115
  9.5 0.1 collective-permute-start
  9.5 1.1 %collective-permute-start.3 = (bf16[128,1024]{1,0:T(8,128)(2,1)S(1)}, bf16[128,1024]{1,0:T(8,128)(2,1)S(1)}, u32[]{:S(2)}, u32[]{:S(2)}) collective-permute-start(bf16[128,1024]{1,0:T(8,128)(2,1)S(1)} %get-tuple-element.16.refs_0_.refs_4_), channel_id=1, source_target_pairs={{0,8},{4,0},{12,4},{8,12},{1,9},{5,1},{13,5},{9,13},{2,10},{6,2},{... | collective-permute-start | bytes 786440 | tf_op jit(solution)/shard_map/ppermute | solution.py:202
  10.6 1.2 %collective-permute-done.1.refs_5_ = bf16[128,1024]{1,0:T(8,128)(2,1)S(1)} collective-permute-done((bf16[128,1024]{1,0:T(8,128)(2,1)S(1)}, bf16[128,1024]{1,0:T(8,128)(2,1)S(1)}, u32[]{:S(2)}, u32[]{:S(2)}) %collective-permute-start.1) | collective-permute-done | bytes 262176 | tf_op jit(solution)/shard_map/ppermute | solution.py:202
  11.8 0.0 collective-permute-start.2
  11.8 0.0 collective-permute-done
  11.9 1.6 %collective-permute-start.6 = (f32[2,128,256]{2,1,0:T(8,128)S(1)}, f32[2,128,256]{2,1,0:T(8,128)S(1)}, u32[]{:S(2)}, u32[]{:S(2)}) collective-permute-start(f32[2,128,256]{2,1,0:T(8,128)S(1)} %add.15.refs_0_), channel_id=1, source_target_pairs={{0,2},{1,3},{2,0},{3,1},{4,6},{5,7},{6,4},{7,5},{8,10},{9,11},{10,... | collective-permute-start | bytes 786440 | tf_op jit(solution)/shard_map/ppermute | solution.py:19
  13.5 1.8 %collective-permute-start.10 = (bf16[128,1024]{1,0:T(8,128)(2,1)S(1)}, bf16[128,1024]{1,0:T(8,128)(2,1)S(1)}, u32[]{:S(2)}, u32[]{:S(2)}) collective-permute-start(bf16[128,1024]{1,0:T(8,128)(2,1)S(1)} %collective-permute-done.1.refs_5_), channel_id=1, source_target_pairs={{0,4},{4,12},{12,8},{8,0},{1,5},{5,13},{13,9},{9,1},{2,6},{6,14},{... | collective-permute-start | bytes 786440 | tf_op jit(solution)/shard_map/ppermute | solution.py:202
  15.2 0.0 collective-permute-done.2.refs_1_
  15.3 5.0 %shard_map.66 = (f32[2,128,256]{2,1,0:T(8,128)S(1)}, f32[2,128,256]{2,1,0:T(8,128)S(1)}) custom-call(bf16[8,256,1024]{2,1,0:T(8,128)(2,1)} %act.3, bf16[8,256,3584]{2,1,0:T(8,128)(2,1)} %og.3, s32[8]{0:T(128)} %lens.3, bf16[4608,128]{1,0:T(8,128)(2,1)S(1)} %get-tuple-element.15.wide, f32[2,128,256]{2,1,0:T(8,128)S(1)} %add.15.refs_0_, ...), custom_call_target="tpu_custom_call" | custom-call | flops 1024 | bytes 4 | tf_op jit(solution)/shard_map/pallas_call | solution.py:115
  20.3 0.1 collective-permute-start.4
  20.4 0.5 %collective-permute-start.5 = (f32[1,128,256]{2,1,0:T(8,128)S(1)}, f32[1,128,256]{2,1,0:T(8,128)S(1)}, u32[]{:S(2)}, u32[]{:S(2)}) collective-permute-start(f32[1,128,256]{2,1,0:T(8,128)S(1)} %get-tuple-element.26), channel_id=1, source_target_pairs={{0,1},{1,0},{2,3},{3,2},{4,5},{5,4},{6,7},{7,6},{8,9},{9,8},{10,11... | collective-permute-start | bytes 393224 | tf_op jit(solution)/shard_map/ppermute | solution.py:19
  20.9 0.8 %collective-permute-done.4 = f32[1,128,256]{2,1,0:T(8,128)S(1)} collective-permute-done((f32[1,128,256]{2,1,0:T(8,128)S(1)}, f32[1,128,256]{2,1,0:T(8,128)S(1)}, u32[]{:S(2)}, u32[]{:S(2)}) %collective-permute-start.4) | collective-permute-done | bytes 131104 | tf_op jit(solution)/shard_map/ppermute | solution.py:19
  21.7 0.2 collective-permute-done.5
  21.9 0.0 collective-permute-done.6.refs_2_
  21.9 0.5 %shard_map.67 = (f32[2,8,128]{2,1,0:T(8,128)S(1)}, f32[2,8,128]{2,1,0:T(8,128)S(1)}, f32[2,8,128]{2,1,0:T(8,128)S(1)}, f32[2,8,128]{2,1,0:T(8,128)S(1)}) custom-call(f32[2,128,256]{2,1,0:T(8,128)S(1)} %get-tuple-element.19.refs_0_, f32[2,128,256]{2,1,0:T(8,128)S(1)} %pad_maximum_fusion.refs_1_, f32[2,128,256]{2,1,0:T(8,128)S(1)} %collective-permute-done.6.refs_2_), custom_call_target="tpu_custom_call" | custom-call | tf_op jit(solution)/shard_map/pallas_call | solution.py:160
  22.4 0.4 %collective-permute-start.7 = (f32[2,8,128]{2,1,0:T(8,128)S(1)}, f32[2,8,128]{2,1,0:T(8,128)S(1)}, u32[]{:S(2)}, u32[]{:S(2)}) collective-permute-start(f32[2,8,128]{2,1,0:T(8,128)S(1)} %get-tuple-element.22), channel_id=1, source_target_pairs={{0,1},{1,0},{2,3},{3,2},{4,5},{5,4},{6,7},{7,6},{8,9},{9,8},{10,11... | collective-permute-start | bytes 24584 | tf_op jit(solution)/shard_map/ppermute | solution.py:19
  22.8 0.5 %collective-permute-start.8 = (f32[2,8,128]{2,1,0:T(8,128)S(1)}, f32[2,8,128]{2,1,0:T(8,128)S(1)}, u32[]{:S(2)}, u32[]{:S(2)}) collective-permute-start(f32[2,8,128]{2,1,0:T(8,128)S(1)} %get-tuple-element.23), channel_id=1, source_target_pairs={{0,2},{1,3},{2,0},{3,1},{4,6},{5,7},{6,4},{7,5},{8,10},{9,11},{10,... | collective-permute-start | bytes 24584 | tf_op jit(solution)/shard_map/ppermute | solution.py:19
  23.3 1.0 %collective-permute-start.9 = (f32[2,8,128]{2,1,0:T(8,128)S(1)}, f32[2,8,128]{2,1,0:T(8,128)S(1)}, u32[]{:S(2)}, u32[]{:S(2)}) collective-permute-start(f32[2,8,128]{2,1,0:T(8,128)S(1)} %get-tuple-element.24), channel_id=1, source_target_pairs={{0,3},{1,2},{2,1},{3,0},{4,7},{5,6},{6,5},{7,4},{8,11},{9,10},{10,... | collective-permute-start | bytes 24584 | tf_op jit(solution)/shard_map/ppermute | solution.py:19
  24.4 2.4 %collective-permute-done.10.refs_7_ = bf16[128,1024]{1,0:T(8,128)(2,1)S(1)} collective-permute-done((bf16[128,1024]{1,0:T(8,128)(2,1)S(1)}, bf16[128,1024]{1,0:T(8,128)(2,1)S(1)}, u32[]{:S(2)}, u32[]{:S(2)}) %collective-permute-start.10) | collective-permute-done | bytes 262176 | tf_op jit(solution)/shard_map/ppermute | solution.py:202
  26.8 0.0 collective-permute-done.7.refs_1_
  26.8 0.0 collective-permute-done.8.refs_2_
  26.8 0.0 collective-permute-done.9.refs_3_
  26.8 0.4 %shard_map.68 = f32[8,512]{1,0:T(8,128)S(1)} custom-call(f32[2,8,128]{2,1,0:T(8,128)S(1)} %get-tuple-element.21.refs_0_, f32[2,8,128]{2,1,0:T(8,128)S(1)} %collective-permute-done.7.refs_1_, f32[2,8,128]{2,1,0:T(8,128)S(1)} %collective-permute-done.8.refs_2_, f32[2,8,128]{2,1,0:T(8,128)S(1)} %collective-permute-done.9.refs_3_, ...), custom_call_target="tpu_custom_call" | custom-call | tf_op jit(solution)/shard_map/pallas_call | solution.py:188
  27.2 0.1 collective-permute-start.11
  27.2 1.5 %collective-permute-start.12 = (f32[8,512]{1,0:T(8,128)S(1)}, f32[8,512]{1,0:T(8,128)S(1)}, u32[]{:S(2)}, u32[]{:S(2)}) collective-permute-start(f32[8,512]{1,0:T(8,128)S(1)} %shard_map.68), channel_id=1, source_target_pairs={{0,2},{1,3},{2,0},{3,1},{4,6},{5,7},{6,4},{7,5},{8,10},{9,11},{10,... | collective-permute-start | bytes 49160 | tf_op jit(solution)/shard_map/ppermute | solution.py:19
  28.7 0.3 collective-permute-start.13
  29.1 1.9 %collective-permute-done.12 = f32[8,512]{1,0:T(8,128)S(1)} collective-permute-done((f32[8,512]{1,0:T(8,128)S(1)}, f32[8,512]{1,0:T(8,128)S(1)}, u32[]{:S(2)}, u32[]{:S(2)}) %collective-permute-start.12) | collective-permute-done | bytes 16416 | tf_op jit(solution)/shard_map/ppermute | solution.py:19
  31.0 0.9 %collective-permute-done.13 = f32[8,512]{1,0:T(8,128)S(1)} collective-permute-done((f32[8,512]{1,0:T(8,128)S(1)}, f32[8,512]{1,0:T(8,128)S(1)}, u32[]{:S(2)}, u32[]{:S(2)}) %collective-permute-start.13) | collective-permute-done | bytes 16416 | tf_op jit(solution)/shard_map/ppermute | solution.py:19
  31.9 0.6 %add_add_fusion = f32[8,512]{1,0:T(8,128)} fusion(f32[8,512]{1,0:T(8,128)S(1)} %collective-permute-done.12, f32[8,512]{1,0:T(8,128)S(1)} %collective-permute-done.13, f32[8,512]{1,0:T(8,128)S(1)} %shard_map.68, f32[8,512]{1,0:T(8,128)S(1)} %collective-permute-done.11), kind=kLoop, calls=%fused_computation.2 | loop fusion | flops 12288 | bytes 81920 | tf_op jit(solution)/shard_map/add | solution.py:233
  (6 shorter events, 0.1 us)
Async XLA Ops:
  1.4 10.4 %collective-permute-start.1 = (bf16[128,1024]{1,0:T(8,128)(2,1)S(1)}, bf16[128,1024]{1,0:T(8,128)(2,1)S(1)}, u32[]{:S(2)}, u32[]{:S(2)}) collective-permute-start(bf16[128,1024]{1,0:T(8,128)(2,1)S(1)} %get-tuple-element.16.refs_0_.refs_4_), channel_id=1, source_target_pairs={{0,4},{4,12},{12,8},{8,0},{1,5},{5,13},{13,9},{9,1},{2,6},{6,14},{... | collective-permute-start | bytes 786440 | tf_op jit(solution)/shard_map/ppermute | solution.py:202
  9.5 2.4 %collective-permute-start = (f32[2,128,256]{2,1,0:T(8,128)S(1)}, f32[2,128,256]{2,1,0:T(8,128)S(1)}, u32[]{:S(2)}, u32[]{:S(2)}) collective-permute-start(f32[2,128,256]{2,1,0:T(8,128)S(1)} %get-tuple-element.18), channel_id=1, source_target_pairs={{0,1},{1,0},{2,3},{3,2},{4,5},{5,4},{6,7},{7,6},{8,9},{9,8},{10,11... | collective-permute-start | bytes 786440 | tf_op jit(solution)/shard_map/ppermute | solution.py:19
  9.5 10.7 %collective-permute-start.3 = (bf16[128,1024]{1,0:T(8,128)(2,1)S(1)}, bf16[128,1024]{1,0:T(8,128)(2,1)S(1)}, u32[]{:S(2)}, u32[]{:S(2)}) collective-permute-start(bf16[128,1024]{1,0:T(8,128)(2,1)S(1)} %get-tuple-element.16.refs_0_.refs_4_), channel_id=1, source_target_pairs={{0,8},{4,0},{12,4},{8,12},{1,9},{5,1},{13,5},{9,13},{2,10},{6,2},{... | collective-permute-start | bytes 786440 | tf_op jit(solution)/shard_map/ppermute | solution.py:202
  11.8 3.4 %collective-permute-start.2 = (bf16[16,128]{1,0:T(8,128)(2,1)S(1)}, bf16[16,128]{1,0:T(8,128)(2,1)S(1)}, u32[]{:S(2)}, u32[]{:S(2)}) collective-permute-start(bf16[16,128]{1,0:T(8,128)(2,1)S(1)} %slice.16), channel_id=1, source_target_pairs={{0,1},{1,0},{2,3},{3,2},{4,5},{5,4},{6,7},{7,6},{8,9},{9,8},{10,11... | collective-permute-start | bytes 12296 | tf_op jit(solution)/shard_map/ppermute | solution.py:19
  11.9 10.0 %collective-permute-start.6 = (f32[2,128,256]{2,1,0:T(8,128)S(1)}, f32[2,128,256]{2,1,0:T(8,128)S(1)}, u32[]{:S(2)}, u32[]{:S(2)}) collective-permute-start(f32[2,128,256]{2,1,0:T(8,128)S(1)} %add.15.refs_0_), channel_id=1, source_target_pairs={{0,2},{1,3},{2,0},{3,1},{4,6},{5,7},{6,4},{7,5},{8,10},{9,11},{10,... | collective-permute-start | bytes 786440 | tf_op jit(solution)/shard_map/ppermute | solution.py:19
  13.5 13.3 %collective-permute-start.10 = (bf16[128,1024]{1,0:T(8,128)(2,1)S(1)}, bf16[128,1024]{1,0:T(8,128)(2,1)S(1)}, u32[]{:S(2)}, u32[]{:S(2)}) collective-permute-start(bf16[128,1024]{1,0:T(8,128)(2,1)S(1)} %collective-permute-done.1.refs_5_), channel_id=1, source_target_pairs={{0,4},{4,12},{12,8},{8,0},{1,5},{5,13},{13,9},{9,1},{2,6},{6,14},{... | collective-permute-start | bytes 786440 | tf_op jit(solution)/shard_map/ppermute | solution.py:202
  20.3 1.4 %collective-permute-start.4 = (f32[1,128,256]{2,1,0:T(8,128)S(1)}, f32[1,128,256]{2,1,0:T(8,128)S(1)}, u32[]{:S(2)}, u32[]{:S(2)}) collective-permute-start(f32[1,128,256]{2,1,0:T(8,128)S(1)} %get-tuple-element.25), channel_id=1, source_target_pairs={{0,1},{1,0},{2,3},{3,2},{4,5},{5,4},{6,7},{7,6},{8,9},{9,8},{10,11... | collective-permute-start | bytes 393224 | tf_op jit(solution)/shard_map/ppermute | solution.py:19
  20.4 1.5 %collective-permute-start.5 = (f32[1,128,256]{2,1,0:T(8,128)S(1)}, f32[1,128,256]{2,1,0:T(8,128)S(1)}, u32[]{:S(2)}, u32[]{:S(2)}) collective-permute-start(f32[1,128,256]{2,1,0:T(8,128)S(1)} %get-tuple-element.26), channel_id=1, source_target_pairs={{0,1},{1,0},{2,3},{3,2},{4,5},{5,4},{6,7},{7,6},{8,9},{9,8},{10,11... | collective-permute-start | bytes 393224 | tf_op jit(solution)/shard_map/ppermute | solution.py:19
  22.4 4.4 %collective-permute-start.7 = (f32[2,8,128]{2,1,0:T(8,128)S(1)}, f32[2,8,128]{2,1,0:T(8,128)S(1)}, u32[]{:S(2)}, u32[]{:S(2)}) collective-permute-start(f32[2,8,128]{2,1,0:T(8,128)S(1)} %get-tuple-element.22), channel_id=1, source_target_pairs={{0,1},{1,0},{2,3},{3,2},{4,5},{5,4},{6,7},{7,6},{8,9},{9,8},{10,11... | collective-permute-start | bytes 24584 | tf_op jit(solution)/shard_map/ppermute | solution.py:19
  22.8 4.0 %collective-permute-start.8 = (f32[2,8,128]{2,1,0:T(8,128)S(1)}, f32[2,8,128]{2,1,0:T(8,128)S(1)}, u32[]{:S(2)}, u32[]{:S(2)}) collective-permute-start(f32[2,8,128]{2,1,0:T(8,128)S(1)} %get-tuple-element.23), channel_id=1, source_target_pairs={{0,2},{1,3},{2,0},{3,1},{4,6},{5,7},{6,4},{7,5},{8,10},{9,11},{10,... | collective-permute-start | bytes 24584 | tf_op jit(solution)/shard_map/ppermute | solution.py:19
  23.3 3.5 %collective-permute-start.9 = (f32[2,8,128]{2,1,0:T(8,128)S(1)}, f32[2,8,128]{2,1,0:T(8,128)S(1)}, u32[]{:S(2)}, u32[]{:S(2)}) collective-permute-start(f32[2,8,128]{2,1,0:T(8,128)S(1)} %get-tuple-element.24), channel_id=1, source_target_pairs={{0,3},{1,2},{2,1},{3,0},{4,7},{5,6},{6,5},{7,4},{8,11},{9,10},{10,... | collective-permute-start | bytes 24584 | tf_op jit(solution)/shard_map/ppermute | solution.py:19
  27.2 1.9 %collective-permute-start.11 = (f32[8,512]{1,0:T(8,128)S(1)}, f32[8,512]{1,0:T(8,128)S(1)}, u32[]{:S(2)}, u32[]{:S(2)}) collective-permute-start(f32[8,512]{1,0:T(8,128)S(1)} %shard_map.68), channel_id=1, source_target_pairs={{0,1},{1,0},{2,3},{3,2},{4,5},{5,4},{6,7},{7,6},{8,9},{9,8},{10,11... | collective-permute-start | bytes 49160 | tf_op jit(solution)/shard_map/ppermute | solution.py:19
  27.2 3.7 %collective-permute-start.12 = (f32[8,512]{1,0:T(8,128)S(1)}, f32[8,512]{1,0:T(8,128)S(1)}, u32[]{:S(2)}, u32[]{:S(2)}) collective-permute-start(f32[8,512]{1,0:T(8,128)S(1)} %shard_map.68), channel_id=1, source_target_pairs={{0,2},{1,3},{2,0},{3,1},{4,6},{5,7},{6,4},{7,5},{8,10},{9,11},{10,... | collective-permute-start | bytes 49160 | tf_op jit(solution)/shard_map/ppermute | solution.py:19
  28.7 3.2 %collective-permute-start.13 = (f32[8,512]{1,0:T(8,128)S(1)}, f32[8,512]{1,0:T(8,128)S(1)}, u32[]{:S(2)}, u32[]{:S(2)}) collective-permute-start(f32[8,512]{1,0:T(8,128)S(1)} %shard_map.68), channel_id=1, source_target_pairs={{0,3},{1,2},{2,1},{3,0},{4,7},{5,6},{6,5},{7,4},{8,11},{9,10},{10,... | collective-permute-start | bytes 49160 | tf_op jit(solution)/shard_map/ppermute | solution.py:19

commit v18 on v15

--- a/solution.py
+++ b/solution.py
@@ -193,14 +193,14 @@
 
 
 def gather_tests(own, groups):
-    ring = [0, 1, 3, 2] if groups == 4 else list(range(groups))
+    ring = [0, 2, 3, 1] if groups == 4 else list(range(groups))
 
     def shift(value, step):
         return lax.ppermute(value, "dp", [(ring[i], ring[(i + step) % groups]) for i in range(groups)])
 
     if groups == 4:
         first = shift(own, 1)
-        return [(own, 1, 0, 4), (first, -2, 12, 5), (shift(own, -1), 2, 1, 5), (shift(first, 1), -1, 3, 4)]
+        return [(own, 1, 0, 4), (first, 2, 1, 5), (shift(own, -1), -2, 12, 5), (shift(first, 1), -1, 3, 4)]
     return [(own, 1, 0, groups)] + [(shift(own, step), 1, groups - step, groups) for step in range(1, groups)]
 
 

time: 32.7 us -> 34.7 us (1.061)
  the two profiles are of different devices: /device:TPU:0 before, /device:TPU:25 now
where the time goes in v18:
time: 34.7 us; the launch traced here: 34.5 us
  starting transfers between devices  15.6 us (45%)
  Pallas kernels  12.5 us (36%)
  waiting for transfers between devices  5.72 us (16%)
  other arithmetic  0.69 us (2%)
    ppermute x11, starting transfers between devices, xor_permute(): return lax.ppermute(value, axis, [(i, i ^ step) for i in range(size)])  13.1 us
    pallas_call x2, Pallas kernels, project(): pl.pallas_call(functools.partial(project_kernel, steps, share, ahead, pie...  10.6 us
    ppermute x11, waiting for transfers between devices, xor_permute(): return lax.ppermute(value, axis, [(i, i ^ step) for i in range(size)])  5.71 us
    ppermute x3, starting transfers between devices, shift(): lax.ppermute(value, 'dp', [(ring[i], ring[(i + step) % groups]) for i in...  2.47 us
    pallas_call x1, Pallas kernels, cut_tests(): pl.pallas_call(cut_kernel, out_shape=jax.ShapeDtypeStruct((rows, width //...  0.96 us
  transfers between devices with their start and end apart: 14, of which 6 were waited for; matrix products, arithmetic and copies ran while one was open for 0% of the time, Pallas kernels for 32%

profile of v18, /device:TPU:25, one launch (start us, length us, event | category | flops | bytes accessed | tf_op | source)
XLA Modules:
  0.0 34.5 jit_solution(9646840328786809173)
XLA Ops:
  0.0 1.0 %shard_map.64.refs_0_.refs_4_ = bf16[128,1024]{1,0:T(8,128)(2,1)S(1)} custom-call(bf16[128,4096]{1,0:T(8,128)(2,1)} %tests.1), custom_call_target="tpu_custom_call" | custom-call | tf_op jit(solution)/shard_map/pallas_call | solution.py:32
  1.0 0.1 collective-permute-start.1
  1.1 5.3 %shard_map.65 = (f32[2,128,256]{2,1,0:T(8,128)S(1)}, f32[2,128,256]{2,1,0:T(8,128)S(1)}) custom-call(bf16[8,256,1024]{2,1,0:T(8,128)(2,1)} %act.3, bf16[8,256,3584]{2,1,0:T(8,128)(2,1)} %og.3, bf16[64,1024]{1,0:T(8,128)(2,1)} %bitcast.6, bf16[64,3584]{1,0:T(8,128)(2,1)} %bitcast.4, s32[8]{0:T(128)} %lens.3, bf16[128,1024]{1,0:T(8,128)(2,1)S(1)} %shard_map.64.refs_0_.refs_4_), custom_call_target="tpu_custom_call" | custom-call | flops 4294967296 | bytes 16777216 | tf_op jit(solution)/shard_map/pallas_call | solution.py:110
  6.4 1.0 %collective-permute-start = (f32[2,128,256]{2,1,0:T(8,128)S(1)}, f32[2,128,256]{2,1,0:T(8,128)S(1)}, u32[]{:S(2)}, u32[]{:S(2)}) collective-permute-start(f32[2,128,256]{2,1,0:T(8,128)S(1)} %get-tuple-element.14), channel_id=1, source_target_pairs={{0,1},{1,0},{2,3},{3,2},{4,5},{5,4},{6,7},{7,6},{8,9},{9,8},{10,11... | collective-permute-start | bytes 786440 | tf_op jit(solution)/shard_map/ppermute | solution.py:19
  7.4 1.4 %collective-permute-start.3 = (bf16[128,1024]{1,0:T(8,128)(2,1)S(1)}, bf16[128,1024]{1,0:T(8,128)(2,1)S(1)}, u32[]{:S(2)}, u32[]{:S(2)}) collective-permute-start(bf16[128,1024]{1,0:T(8,128)(2,1)S(1)} %shard_map.64.refs_0_.refs_4_), channel_id=1, source_target_pairs={{0,4},{8,0},{12,8},{4,12},{1,5},{9,1},{13,9},{5,13},{2,6},{10,2},{... | collective-permute-start | bytes 786440 | tf_op jit(solution)/shard_map/ppermute | solution.py:199
  8.8 0.0 collective-permute-done.1.refs_5_
  8.8 0.9 %collective-permute-start.2 = (bf16[16,128]{1,0:T(8,128)(2,1)S(1)}, bf16[16,128]{1,0:T(8,128)(2,1)S(1)}, u32[]{:S(2)}, u32[]{:S(2)}) collective-permute-start(bf16[16,128]{1,0:T(8,128)(2,1)S(1)} %slice.16), channel_id=1, source_target_pairs={{0,1},{1,0},{2,3},{3,2},{4,5},{5,4},{6,7},{7,6},{8,9},{9,8},{10,11... | collective-permute-start | bytes 12296 | tf_op jit(solution)/shard_map/ppermute | solution.py:19
  9.7 0.0 collective-permute-done
  9.8 1.3 %collective-permute-start.6 = (f32[2,128,256]{2,1,0:T(8,128)S(1)}, f32[2,128,256]{2,1,0:T(8,128)S(1)}, u32[]{:S(2)}, u32[]{:S(2)}) collective-permute-start(f32[2,128,256]{2,1,0:T(8,128)S(1)} %add.15.refs_0_), channel_id=1, source_target_pairs={{0,2},{1,3},{2,0},{3,1},{4,6},{5,7},{6,4},{7,5},{8,10},{9,11},{10,... | collective-permute-start | bytes 786440 | tf_op jit(solution)/shard_map/ppermute | solution.py:19
  11.1 1.0 %collective-permute-start.10 = (bf16[128,1024]{1,0:T(8,128)(2,1)S(1)}, bf16[128,1024]{1,0:T(8,128)(2,1)S(1)}, u32[]{:S(2)}, u32[]{:S(2)}) collective-permute-start(bf16[128,1024]{1,0:T(8,128)(2,1)S(1)} %collective-permute-done.1.refs_5_), channel_id=1, source_target_pairs={{0,8},{8,12},{12,4},{4,0},{1,9},{9,13},{13,5},{5,1},{2,10},{10,14}... | collective-permute-start | bytes 786440 | tf_op jit(solution)/shard_map/ppermute | solution.py:199
  12.0 0.0 collective-permute-done.2.refs_1_
  12.0 5.3 %shard_map.66 = (f32[2,128,256]{2,1,0:T(8,128)S(1)}, f32[2,128,256]{2,1,0:T(8,128)S(1)}) custom-call(bf16[8,256,1024]{2,1,0:T(8,128)(2,1)} %act.3, bf16[8,256,3584]{2,1,0:T(8,128)(2,1)} %og.3, bf16[64,1024]{1,0:T(8,128)(2,1)} %bitcast.7, bf16[64,3584]{1,0:T(8,128)(2,1)} %bitcast.5, s32[8]{0:T(128)} %lens.3, f32[2,128,256]{2,1,0:T(8,128)S(1)} %add.15.refs_0_, ...), custom_call_target="tpu_custom_call" | custom-call | flops 1024 | bytes 4 | tf_op jit(solution)/shard_map/pallas_call | solution.py:110
  17.3 0.0 collective-permute-done.3.refs_6_
  17.4 5.4 %collective-permute-start.4 = (f32[1,128,256]{2,1,0:T(8,128)S(1)}, f32[1,128,256]{2,1,0:T(8,128)S(1)}, u32[]{:S(2)}, u32[]{:S(2)}) collective-permute-start(f32[1,128,256]{2,1,0:T(8,128)S(1)} %get-tuple-element.21), channel_id=1, source_target_pairs={{0,1},{1,0},{2,3},{3,2},{4,5},{5,4},{6,7},{7,6},{8,9},{9,8},{10,11... | collective-permute-start | bytes 393224 | tf_op jit(solution)/shard_map/ppermute | solution.py:19
  22.8 0.1 collective-permute-start.5
  22.9 0.9 %collective-permute-done.4 = f32[1,128,256]{2,1,0:T(8,128)S(1)} collective-permute-done((f32[1,128,256]{2,1,0:T(8,128)S(1)}, f32[1,128,256]{2,1,0:T(8,128)S(1)}, u32[]{:S(2)}, u32[]{:S(2)}) %collective-permute-start.4) | collective-permute-done | bytes 131104 | tf_op jit(solution)/shard_map/ppermute | solution.py:19
  23.8 0.4 %collective-permute-done.5 = f32[1,128,256]{2,1,0:T(8,128)S(1)} collective-permute-done((f32[1,128,256]{2,1,0:T(8,128)S(1)}, f32[1,128,256]{2,1,0:T(8,128)S(1)}, u32[]{:S(2)}, u32[]{:S(2)}) %collective-permute-start.5) | collective-permute-done | bytes 131104 | tf_op jit(solution)/shard_map/ppermute | solution.py:19
  24.2 0.0 collective-permute-done.6.refs_2_
  24.2 0.5 %shard_map.67 = (f32[2,8,128]{2,1,0:T(8,128)S(1)}, f32[2,8,128]{2,1,0:T(8,128)S(1)}, f32[2,8,128]{2,1,0:T(8,128)S(1)}, f32[2,8,128]{2,1,0:T(8,128)S(1)}) custom-call(f32[2,128,256]{2,1,0:T(8,128)S(1)} %get-tuple-element.15.refs_0_, f32[2,128,256]{2,1,0:T(8,128)S(1)} %pad_maximum_fusion.refs_1_, f32[2,128,256]{2,1,0:T(8,128)S(1)} %collective-permute-done.6.refs_2_), custom_call_target="tpu_custom_call" | custom-call | tf_op jit(solution)/shard_map/pallas_call | solution.py:157
  24.7 0.3 collective-permute-start.7
  24.9 1.2 %collective-permute-start.8 = (f32[2,8,128]{2,1,0:T(8,128)S(1)}, f32[2,8,128]{2,1,0:T(8,128)S(1)}, u32[]{:S(2)}, u32[]{:S(2)}) collective-permute-start(f32[2,8,128]{2,1,0:T(8,128)S(1)} %get-tuple-element.19), channel_id=1, source_target_pairs={{0,2},{1,3},{2,0},{3,1},{4,6},{5,7},{6,4},{7,5},{8,10},{9,11},{10,... | collective-permute-start | bytes 24584 | tf_op jit(solution)/shard_map/ppermute | solution.py:19
  26.2 0.7 %collective-permute-start.9 = (f32[2,8,128]{2,1,0:T(8,128)S(1)}, f32[2,8,128]{2,1,0:T(8,128)S(1)}, u32[]{:S(2)}, u32[]{:S(2)}) collective-permute-start(f32[2,8,128]{2,1,0:T(8,128)S(1)} %get-tuple-element.20), channel_id=1, source_target_pairs={{0,3},{1,2},{2,1},{3,0},{4,7},{5,6},{6,5},{7,4},{8,11},{9,10},{10,... | collective-permute-start | bytes 24584 | tf_op jit(solution)/shard_map/ppermute | solution.py:19
  26.9 0.0 collective-permute-done.10.refs_7_
  26.9 0.5 %collective-permute-done.8.refs_2_ = f32[2,8,128]{2,1,0:T(8,128)S(1)} collective-permute-done((f32[2,8,128]{2,1,0:T(8,128)S(1)}, f32[2,8,128]{2,1,0:T(8,128)S(1)}, u32[]{:S(2)}, u32[]{:S(2)}) %collective-permute-start.8) | collective-permute-done | bytes 8224 | tf_op jit(solution)/shard_map/ppermute | solution.py:19
  27.4 2.0 %collective-permute-done.9.refs_3_ = f32[2,8,128]{2,1,0:T(8,128)S(1)} collective-permute-done((f32[2,8,128]{2,1,0:T(8,128)S(1)}, f32[2,8,128]{2,1,0:T(8,128)S(1)}, u32[]{:S(2)}, u32[]{:S(2)}) %collective-permute-start.9) | collective-permute-done | bytes 8224 | tf_op jit(solution)/shard_map/ppermute | solution.py:19
  29.4 0.4 %shard_map.68 = f32[8,512]{1,0:T(8,128)S(1)} custom-call(f32[2,8,128]{2,1,0:T(8,128)S(1)} %get-tuple-element.17.refs_0_, f32[2,8,128]{2,1,0:T(8,128)S(1)} %collective-permute-done.7.refs_1_, f32[2,8,128]{2,1,0:T(8,128)S(1)} %collective-permute-done.8.refs_2_, f32[2,8,128]{2,1,0:T(8,128)S(1)} %collective-permute-done.9.refs_3_, ...), custom_call_target="tpu_custom_call" | custom-call | tf_op jit(solution)/shard_map/pallas_call | solution.py:185
  29.8 0.4 %collective-permute-start.11 = (f32[8,512]{1,0:T(8,128)S(1)}, f32[8,512]{1,0:T(8,128)S(1)}, u32[]{:S(2)}, u32[]{:S(2)}) collective-permute-start(f32[8,512]{1,0:T(8,128)S(1)} %shard_map.68), channel_id=1, source_target_pairs={{0,1},{1,0},{2,3},{3,2},{4,5},{5,4},{6,7},{7,6},{8,9},{9,8},{10,11... | collective-permute-start | bytes 49160 | tf_op jit(solution)/shard_map/ppermute | solution.py:19
  30.2 0.4 %collective-permute-start.12 = (f32[8,512]{1,0:T(8,128)S(1)}, f32[8,512]{1,0:T(8,128)S(1)}, u32[]{:S(2)}, u32[]{:S(2)}) collective-permute-start(f32[8,512]{1,0:T(8,128)S(1)} %shard_map.68), channel_id=1, source_target_pairs={{0,2},{1,3},{2,0},{3,1},{4,6},{5,7},{6,4},{7,5},{8,10},{9,11},{10,... | collective-permute-start | bytes 49160 | tf_op jit(solution)/shard_map/ppermute | solution.py:19
  30.6 1.4 %collective-permute-start.13 = (f32[8,512]{1,0:T(8,128)S(1)}, f32[8,512]{1,0:T(8,128)S(1)}, u32[]{:S(2)}, u32[]{:S(2)}) collective-permute-start(f32[8,512]{1,0:T(8,128)S(1)} %shard_map.68), channel_id=1, source_target_pairs={{0,3},{1,2},{2,1},{3,0},{4,7},{5,6},{6,5},{7,4},{8,11},{9,10},{10,... | collective-permute-start | bytes 49160 | tf_op jit(solution)/shard_map/ppermute | solution.py:19
  32.0 0.8 %collective-permute-done.12 = f32[8,512]{1,0:T(8,128)S(1)} collective-permute-done((f32[8,512]{1,0:T(8,128)S(1)}, f32[8,512]{1,0:T(8,128)S(1)}, u32[]{:S(2)}, u32[]{:S(2)}) %collective-permute-start.12) | collective-permute-done | bytes 16416 | tf_op jit(solution)/shard_map/ppermute | solution.py:19
  32.8 1.1 %collective-permute-done.13 = f32[8,512]{1,0:T(8,128)S(1)} collective-permute-done((f32[8,512]{1,0:T(8,128)S(1)}, f32[8,512]{1,0:T(8,128)S(1)}, u32[]{:S(2)}, u32[]{:S(2)}) %collective-permute-start.13) | collective-permute-done | bytes 16416 | tf_op jit(solution)/shard_map/ppermute | solution.py:19
  33.9 0.6 %add_add_fusion = f32[8,512]{1,0:T(8,128)} fusion(f32[8,512]{1,0:T(8,128)S(1)} %collective-permute-done.12, f32[8,512]{1,0:T(8,128)S(1)} %collective-permute-done.13, f32[8,512]{1,0:T(8,128)S(1)} %shard_map.68, f32[8,512]{1,0:T(8,128)S(1)} %collective-permute-done.11), kind=kLoop, calls=%fused_computation.2 | loop fusion | flops 12288 | bytes 81920 | tf_op jit(solution)/shard_map/add | solution.py:230
  (6 shorter events, 0.1 us)
Async XLA Ops:
  1.0 7.9 %collective-permute-start.1 = (bf16[128,1024]{1,0:T(8,128)(2,1)S(1)}, bf16[128,1024]{1,0:T(8,128)(2,1)S(1)}, u32[]{:S(2)}, u32[]{:S(2)}) collective-permute-start(bf16[128,1024]{1,0:T(8,128)(2,1)S(1)} %shard_map.64.refs_0_.refs_4_), channel_id=1, source_target_pairs={{0,8},{8,12},{12,4},{4,0},{1,9},{9,13},{13,5},{5,1},{2,10},{10,14}... | collective-permute-start | bytes 786440 | tf_op jit(solution)/shard_map/ppermute | solution.py:199
  6.4 3.4 %collective-permute-start = (f32[2,128,256]{2,1,0:T(8,128)S(1)}, f32[2,128,256]{2,1,0:T(8,128)S(1)}, u32[]{:S(2)}, u32[]{:S(2)}) collective-permute-start(f32[2,128,256]{2,1,0:T(8,128)S(1)} %get-tuple-element.14), channel_id=1, source_target_pairs={{0,1},{1,0},{2,3},{3,2},{4,5},{5,4},{6,7},{7,6},{8,9},{9,8},{10,11... | collective-permute-start | bytes 786440 | tf_op jit(solution)/shard_map/ppermute | solution.py:19
  7.4 9.9 %collective-permute-start.3 = (bf16[128,1024]{1,0:T(8,128)(2,1)S(1)}, bf16[128,1024]{1,0:T(8,128)(2,1)S(1)}, u32[]{:S(2)}, u32[]{:S(2)}) collective-permute-start(bf16[128,1024]{1,0:T(8,128)(2,1)S(1)} %shard_map.64.refs_0_.refs_4_), channel_id=1, source_target_pairs={{0,4},{8,0},{12,8},{4,12},{1,5},{9,1},{13,9},{5,13},{2,6},{10,2},{... | collective-permute-start | bytes 786440 | tf_op jit(solution)/shard_map/ppermute | solution.py:199
  8.8 3.2 %collective-permute-start.2 = (bf16[16,128]{1,0:T(8,128)(2,1)S(1)}, bf16[16,128]{1,0:T(8,128)(2,1)S(1)}, u32[]{:S(2)}, u32[]{:S(2)}) collective-permute-start(bf16[16,128]{1,0:T(8,128)(2,1)S(1)} %slice.16), channel_id=1, source_target_pairs={{0,1},{1,0},{2,3},{3,2},{4,5},{5,4},{6,7},{7,6},{8,9},{9,8},{10,11... | collective-permute-start | bytes 12296 | tf_op jit(solution)/shard_map/ppermute | solution.py:19
  9.8 14.4 %collective-permute-start.6 = (f32[2,128,256]{2,1,0:T(8,128)S(1)}, f32[2,128,256]{2,1,0:T(8,128)S(1)}, u32[]{:S(2)}, u32[]{:S(2)}) collective-permute-start(f32[2,128,256]{2,1,0:T(8,128)S(1)} %add.15.refs_0_), channel_id=1, source_target_pairs={{0,2},{1,3},{2,0},{3,1},{4,6},{5,7},{6,4},{7,5},{8,10},{9,11},{10,... | collective-permute-start | bytes 786440 | tf_op jit(solution)/shard_map/ppermute | solution.py:19
  11.1 15.8 %collective-permute-start.10 = (bf16[128,1024]{1,0:T(8,128)(2,1)S(1)}, bf16[128,1024]{1,0:T(8,128)(2,1)S(1)}, u32[]{:S(2)}, u32[]{:S(2)}) collective-permute-start(bf16[128,1024]{1,0:T(8,128)(2,1)S(1)} %collective-permute-done.1.refs_5_), channel_id=1, source_target_pairs={{0,8},{8,12},{12,4},{4,0},{1,9},{9,13},{13,5},{5,1},{2,10},{10,14}... | collective-permute-start | bytes 786440 | tf_op jit(solution)/shard_map/ppermute | solution.py:199
  17.4 6.4 %collective-permute-start.4 = (f32[1,128,256]{2,1,0:T(8,128)S(1)}, f32[1,128,256]{2,1,0:T(8,128)S(1)}, u32[]{:S(2)}, u32[]{:S(2)}) collective-permute-start(f32[1,128,256]{2,1,0:T(8,128)S(1)} %get-tuple-element.21), channel_id=1, source_target_pairs={{0,1},{1,0},{2,3},{3,2},{4,5},{5,4},{6,7},{7,6},{8,9},{9,8},{10,11... | collective-permute-start | bytes 393224 | tf_op jit(solution)/shard_map/ppermute | solution.py:19
  22.8 1.3 %collective-permute-start.5 = (f32[1,128,256]{2,1,0:T(8,128)S(1)}, f32[1,128,256]{2,1,0:T(8,128)S(1)}, u32[]{:S(2)}, u32[]{:S(2)}) collective-permute-start(f32[1,128,256]{2,1,0:T(8,128)S(1)} %get-tuple-element.22), channel_id=1, source_target_pairs={{0,1},{1,0},{2,3},{3,2},{4,5},{5,4},{6,7},{7,6},{8,9},{9,8},{10,11... | collective-permute-start | bytes 393224 | tf_op jit(solution)/shard_map/ppermute | solution.py:19
  24.7 2.2 %collective-permute-start.7 = (f32[2,8,128]{2,1,0:T(8,128)S(1)}, f32[2,8,128]{2,1,0:T(8,128)S(1)}, u32[]{:S(2)}, u32[]{:S(2)}) collective-permute-start(f32[2,8,128]{2,1,0:T(8,128)S(1)} %get-tuple-element.18), channel_id=1, source_target_pairs={{0,1},{1,0},{2,3},{3,2},{4,5},{5,4},{6,7},{7,6},{8,9},{9,8},{10,11... | collective-permute-start | bytes 24584 | tf_op jit(solution)/shard_map/ppermute | solution.py:19
  24.9 2.5 %collective-permute-start.8 = (f32[2,8,128]{2,1,0:T(8,128)S(1)}, f32[2,8,128]{2,1,0:T(8,128)S(1)}, u32[]{:S(2)}, u32[]{:S(2)}) collective-permute-start(f32[2,8,128]{2,1,0:T(8,128)S(1)} %get-tuple-element.19), channel_id=1, source_target_pairs={{0,2},{1,3},{2,0},{3,1},{4,6},{5,7},{6,4},{7,5},{8,10},{9,11},{10,... | collective-permute-start | bytes 24584 | tf_op jit(solution)/shard_map/ppermute | solution.py:19
  26.2 3.3 %collective-permute-start.9 = (f32[2,8,128]{2,1,0:T(8,128)S(1)}, f32[2,8,128]{2,1,0:T(8,128)S(1)}, u32[]{:S(2)}, u32[]{:S(2)}) collective-permute-start(f32[2,8,128]{2,1,0:T(8,128)S(1)} %get-tuple-element.20), channel_id=1, source_target_pairs={{0,3},{1,2},{2,1},{3,0},{4,7},{5,6},{6,5},{7,4},{8,11},{9,10},{10,... | collective-permute-start | bytes 24584 | tf_op jit(solution)/shard_map/ppermute | solution.py:19
  29.8 2.2 %collective-permute-start.11 = (f32[8,512]{1,0:T(8,128)S(1)}, f32[8,512]{1,0:T(8,128)S(1)}, u32[]{:S(2)}, u32[]{:S(2)}) collective-permute-start(f32[8,512]{1,0:T(8,128)S(1)} %shard_map.68), channel_id=1, source_target_pairs={{0,1},{1,0},{2,3},{3,2},{4,5},{5,4},{6,7},{7,6},{8,9},{9,8},{10,11... | collective-permute-start | bytes 49160 | tf_op jit(solution)/shard_map/ppermute | solution.py:19
  30.2 2.6 %collective-permute-start.12 = (f32[8,512]{1,0:T(8,128)S(1)}, f32[8,512]{1,0:T(8,128)S(1)}, u32[]{:S(2)}, u32[]{:S(2)}) collective-permute-start(f32[8,512]{1,0:T(8,128)S(1)} %shard_map.68), channel_id=1, source_target_pairs={{0,2},{1,3},{2,0},{3,1},{4,6},{5,7},{6,4},{7,5},{8,10},{9,11},{10,... | collective-permute-start | bytes 49160 | tf_op jit(solution)/shard_map/ppermute | solution.py:19
  30.6 3.3 %collective-permute-start.13 = (f32[8,512]{1,0:T(8,128)S(1)}, f32[8,512]{1,0:T(8,128)S(1)}, u32[]{:S(2)}, u32[]{:S(2)}) collective-permute-start(f32[8,512]{1,0:T(8,128)S(1)} %shard_map.68), channel_id=1, source_target_pairs={{0,3},{1,2},{2,1},{3,0},{4,7},{5,6},{6,5},{7,4},{8,11},{9,10},{10,... | collective-permute-start | bytes 49160 | tf_op jit(solution)/shard_map/ppermute | solution.py:19

commit v19 on v18

--- a/solution.py
+++ b/solution.py
@@ -193,14 +193,12 @@
 
 
 def gather_tests(own, groups):
-    ring = [0, 2, 3, 1] if groups == 4 else list(range(groups))
-
     def shift(value, step):
-        return lax.ppermute(value, "dp", [(ring[i], ring[(i + step) % groups]) for i in range(groups)])
+        return lax.ppermute(value, "dp", [(i, (i + step) % groups) for i in range(groups)])
 
     if groups == 4:
         first = shift(own, 1)
-        return [(own, 1, 0, 4), (first, 2, 1, 5), (shift(own, -1), -2, 12, 5), (shift(first, 1), -1, 3, 4)]
+        return [(own, 1, 0, 4), (first, 1, 3, 4), (shift(own, -1), 1, 1, 4), (shift(first, 1), 1, 2, 4)]
     return [(own, 1, 0, groups)] + [(shift(own, step), 1, groups - step, groups) for step in range(1, groups)]
 
 

time: 34.7 us -> 31.8 us (0.916)
  the two profiles are of different devices: /device:TPU:25 before, /device:TPU:0 now
where the time goes in v19:
time: 31.8 us; the launch traced here: 31.6 us
  Pallas kernels  12.5 us (39%)
  starting transfers between devices  11.3 us (36%)
  waiting for transfers between devices  6.99 us (22%)
  other arithmetic  0.7 us (2%)
    pallas_call x2, Pallas kernels, project(): pl.pallas_call(functools.partial(project_kernel, steps, share, ahead, pie...  10.6 us
    ppermute x11, starting transfers between devices, xor_permute(): return lax.ppermute(value, axis, [(i, i ^ step) for i in range(size)])  6.01 us
    ppermute x3, starting transfers between devices, shift(): lax.ppermute(value, 'dp', [(i, (i + step) % groups) for i in range(groups)])  5.33 us
    ppermute x11, waiting for transfers between devices, xor_permute(): return lax.ppermute(value, axis, [(i, i ^ step) for i in range(size)])  4.02 us
    ppermute x3, waiting for transfers between devices, shift(): lax.ppermute(value, 'dp', [(i, (i + step) % groups) for i in range(groups)])  2.97 us
    pallas_call x1, Pallas kernels, cut_tests(): pl.pallas_call(cut_kernel, out_shape=jax.ShapeDtypeStruct((rows, width //...  0.96 us
  transfers between devices with their start and end apart: 14, of which 8 were waited for; matrix products, arithmetic and copies ran while one was open for 0% of the time, Pallas kernels for 35%

profile of v19, /device:TPU:0, one launch (start us, length us, event | category | flops | bytes accessed | tf_op | source)
XLA Modules:
  0.0 31.6 jit_solution(4469703099017441361)
XLA Ops:
  0.0 1.0 %shard_map.64.refs_0_.refs_4_ = bf16[128,1024]{1,0:T(8,128)(2,1)S(1)} custom-call(bf16[128,4096]{1,0:T(8,128)(2,1)} %tests.1), custom_call_target="tpu_custom_call" | custom-call | tf_op jit(solution)/shard_map/pallas_call | solution.py:32
  1.0 3.1 %collective-permute-start.1 = (bf16[128,1024]{1,0:T(8,128)(2,1)S(1)}, bf16[128,1024]{1,0:T(8,128)(2,1)S(1)}, u32[]{:S(2)}, u32[]{:S(2)}) collective-permute-start(bf16[128,1024]{1,0:T(8,128)(2,1)S(1)} %shard_map.64.refs_0_.refs_4_), channel_id=1, source_target_pairs={{0,4},{4,8},{8,12},{12,0},{1,5},{5,9},{9,13},{13,1},{2,6},{6,10},{... | collective-permute-start | bytes 786440 | tf_op jit(solution)/shard_map/ppermute | solution.py:197
  4.0 5.3 %shard_map.65 = (f32[2,128,256]{2,1,0:T(8,128)S(1)}, f32[2,128,256]{2,1,0:T(8,128)S(1)}) custom-call(bf16[8,256,1024]{2,1,0:T(8,128)(2,1)} %act.3, bf16[8,256,3584]{2,1,0:T(8,128)(2,1)} %og.3, bf16[64,1024]{1,0:T(8,128)(2,1)} %bitcast.6, bf16[64,3584]{1,0:T(8,128)(2,1)} %bitcast.4, s32[8]{0:T(128)} %lens.3, bf16[128,1024]{1,0:T(8,128)(2,1)S(1)} %shard_map.64.refs_0_.refs_4_), custom_call_target="tpu_custom_call" | custom-call | flops 4294967296 | bytes 16777216 | tf_op jit(solution)/shard_map/pallas_call | solution.py:110
  9.4 0.1 collective-permute-start
  9.4 2.1 %collective-permute-start.3 = (bf16[128,1024]{1,0:T(8,128)(2,1)S(1)}, bf16[128,1024]{1,0:T(8,128)(2,1)S(1)}, u32[]{:S(2)}, u32[]{:S(2)}) collective-permute-start(bf16[128,1024]{1,0:T(8,128)(2,1)S(1)} %shard_map.64.refs_0_.refs_4_), channel_id=1, source_target_pairs={{0,12},{4,0},{8,4},{12,8},{1,13},{5,1},{9,5},{13,9},{2,14},{6,2},{... | collective-permute-start | bytes 786440 | tf_op jit(solution)/shard_map/ppermute | solution.py:197
  11.5 0.8 %collective-permute-done.1.refs_5_ = bf16[128,1024]{1,0:T(8,128)(2,1)S(1)} collective-permute-done((bf16[128,1024]{1,0:T(8,128)(2,1)S(1)}, bf16[128,1024]{1,0:T(8,128)(2,1)S(1)}, u32[]{:S(2)}, u32[]{:S(2)}) %collective-permute-start.1) | collective-permute-done | bytes 262176 | tf_op jit(solution)/shard_map/ppermute | solution.py:197
  12.4 0.0 collective-permute-start.2
  12.4 0.0 collective-permute-done
  12.4 1.6 %collective-permute-start.6 = (f32[2,128,256]{2,1,0:T(8,128)S(1)}, f32[2,128,256]{2,1,0:T(8,128)S(1)}, u32[]{:S(2)}, u32[]{:S(2)}) collective-permute-start(f32[2,128,256]{2,1,0:T(8,128)S(1)} %add.15.refs_0_), channel_id=1, source_target_pairs={{0,2},{1,3},{2,0},{3,1},{4,6},{5,7},{6,4},{7,5},{8,10},{9,11},{10,... | collective-permute-start | bytes 786440 | tf_op jit(solution)/shard_map/ppermute | solution.py:19
  14.0 0.2 collective-permute-start.10
  14.1 0.0 collective-permute-done.2.refs_1_
  14.1 5.3 %shard_map.66 = (f32[2,128,256]{2,1,0:T(8,128)S(1)}, f32[2,128,256]{2,1,0:T(8,128)S(1)}) custom-call(bf16[8,256,1024]{2,1,0:T(8,128)(2,1)} %act.3, bf16[8,256,3584]{2,1,0:T(8,128)(2,1)} %og.3, bf16[64,1024]{1,0:T(8,128)(2,1)} %bitcast.7, bf16[64,3584]{1,0:T(8,128)(2,1)} %bitcast.5, s32[8]{0:T(128)} %lens.3, f32[2,128,256]{2,1,0:T(8,128)S(1)} %add.15.refs_0_, ...), custom_call_target="tpu_custom_call" | custom-call | flops 1024 | bytes 4 | tf_op jit(solution)/shard_map/pallas_call | solution.py:110
  19.5 0.0 collective-permute-done.3.refs_6_
  19.5 0.1 collective-permute-start.4
  19.6 0.4 %collective-permute-start.5 = (f32[1,128,256]{2,1,0:T(8,128)S(1)}, f32[1,128,256]{2,1,0:T(8,128)S(1)}, u32[]{:S(2)}, u32[]{:S(2)}) collective-permute-start(f32[1,128,256]{2,1,0:T(8,128)S(1)} %get-tuple-element.22), channel_id=1, source_target_pairs={{0,1},{1,0},{2,3},{3,2},{4,5},{5,4},{6,7},{7,6},{8,9},{9,8},{10,11... | collective-permute-start | bytes 393224 | tf_op jit(solution)/shard_map/ppermute | solution.py:19
  20.1 0.8 %collective-permute-done.4 = f32[1,128,256]{2,1,0:T(8,128)S(1)} collective-permute-done((f32[1,128,256]{2,1,0:T(8,128)S(1)}, f32[1,128,256]{2,1,0:T(8,128)S(1)}, u32[]{:S(2)}, u32[]{:S(2)}) %collective-permute-start.4) | collective-permute-done | bytes 131104 | tf_op jit(solution)/shard_map/ppermute | solution.py:19
  20.9 0.2 collective-permute-done.5
  21.1 0.1 collective-permute-done.6.refs_2_
  21.2 0.5 %shard_map.67 = (f32[2,8,128]{2,1,0:T(8,128)S(1)}, f32[2,8,128]{2,1,0:T(8,128)S(1)}, f32[2,8,128]{2,1,0:T(8,128)S(1)}, f32[2,8,128]{2,1,0:T(8,128)S(1)}) custom-call(f32[2,128,256]{2,1,0:T(8,128)S(1)} %get-tuple-element.15.refs_0_, f32[2,128,256]{2,1,0:T(8,128)S(1)} %pad_maximum_fusion.refs_1_, f32[2,128,256]{2,1,0:T(8,128)S(1)} %collective-permute-done.6.refs_2_), custom_call_target="tpu_custom_call" | custom-call | tf_op jit(solution)/shard_map/pallas_call | solution.py:157
  21.7 0.3 %collective-permute-start.7 = (f32[2,8,128]{2,1,0:T(8,128)S(1)}, f32[2,8,128]{2,1,0:T(8,128)S(1)}, u32[]{:S(2)}, u32[]{:S(2)}) collective-permute-start(f32[2,8,128]{2,1,0:T(8,128)S(1)} %get-tuple-element.18), channel_id=1, source_target_pairs={{0,1},{1,0},{2,3},{3,2},{4,5},{5,4},{6,7},{7,6},{8,9},{9,8},{10,11... | collective-permute-start | bytes 24584 | tf_op jit(solution)/shard_map/ppermute | solution.py:19
  22.0 1.3 %collective-permute-start.8 = (f32[2,8,128]{2,1,0:T(8,128)S(1)}, f32[2,8,128]{2,1,0:T(8,128)S(1)}, u32[]{:S(2)}, u32[]{:S(2)}) collective-permute-start(f32[2,8,128]{2,1,0:T(8,128)S(1)} %get-tuple-element.19), channel_id=1, source_target_pairs={{0,2},{1,3},{2,0},{3,1},{4,6},{5,7},{6,4},{7,5},{8,10},{9,11},{10,... | collective-permute-start | bytes 24584 | tf_op jit(solution)/shard_map/ppermute | solution.py:19
  23.4 0.3 collective-permute-start.9
  23.6 2.1 %collective-permute-done.10.refs_7_ = bf16[128,1024]{1,0:T(8,128)(2,1)S(1)} collective-permute-done((bf16[128,1024]{1,0:T(8,128)(2,1)S(1)}, bf16[128,1024]{1,0:T(8,128)(2,1)S(1)}, u32[]{:S(2)}, u32[]{:S(2)}) %collective-permute-start.10) | collective-permute-done | bytes 262176 | tf_op jit(solution)/shard_map/ppermute | solution.py:197
  25.8 0.6 %collective-permute-done.9.refs_3_ = f32[2,8,128]{2,1,0:T(8,128)S(1)} collective-permute-done((f32[2,8,128]{2,1,0:T(8,128)S(1)}, f32[2,8,128]{2,1,0:T(8,128)S(1)}, u32[]{:S(2)}, u32[]{:S(2)}) %collective-permute-start.9) | collective-permute-done | bytes 8224 | tf_op jit(solution)/shard_map/ppermute | solution.py:19
  26.4 0.4 %shard_map.68 = f32[8,512]{1,0:T(8,128)S(1)} custom-call(f32[2,8,128]{2,1,0:T(8,128)S(1)} %get-tuple-element.17.refs_0_, f32[2,8,128]{2,1,0:T(8,128)S(1)} %collective-permute-done.7.refs_1_, f32[2,8,128]{2,1,0:T(8,128)S(1)} %collective-permute-done.8.refs_2_, f32[2,8,128]{2,1,0:T(8,128)S(1)} %collective-permute-done.9.refs_3_, ...), custom_call_target="tpu_custom_call" | custom-call | tf_op jit(solution)/shard_map/pallas_call | solution.py:185
  26.8 0.2 collective-permute-start.11
  27.0 0.8 %collective-permute-start.12 = (f32[8,512]{1,0:T(8,128)S(1)}, f32[8,512]{1,0:T(8,128)S(1)}, u32[]{:S(2)}, u32[]{:S(2)}) collective-permute-start(f32[8,512]{1,0:T(8,128)S(1)} %shard_map.68), channel_id=1, source_target_pairs={{0,2},{1,3},{2,0},{3,1},{4,6},{5,7},{6,4},{7,5},{8,10},{9,11},{10,... | collective-permute-start | bytes 49160 | tf_op jit(solution)/shard_map/ppermute | solution.py:19
  27.8 0.9 %collective-permute-start.13 = (f32[8,512]{1,0:T(8,128)S(1)}, f32[8,512]{1,0:T(8,128)S(1)}, u32[]{:S(2)}, u32[]{:S(2)}) collective-permute-start(f32[8,512]{1,0:T(8,128)S(1)} %shard_map.68), channel_id=1, source_target_pairs={{0,3},{1,2},{2,1},{3,0},{4,7},{5,6},{6,5},{7,4},{8,11},{9,10},{10,... | collective-permute-start | bytes 49160 | tf_op jit(solution)/shard_map/ppermute | solution.py:19
  28.7 0.0 collective-permute-done.11
  28.7 2.0 %collective-permute-done.12 = f32[8,512]{1,0:T(8,128)S(1)} collective-permute-done((f32[8,512]{1,0:T(8,128)S(1)}, f32[8,512]{1,0:T(8,128)S(1)}, u32[]{:S(2)}, u32[]{:S(2)}) %collective-permute-start.12) | collective-permute-done | bytes 16416 | tf_op jit(solution)/shard_map/ppermute | solution.py:19
  30.7 0.2 collective-permute-done.13
  31.0 0.6 %add_add_fusion = f32[8,512]{1,0:T(8,128)} fusion(f32[8,512]{1,0:T(8,128)S(1)} %collective-permute-done.12, f32[8,512]{1,0:T(8,128)S(1)} %collective-permute-done.13, f32[8,512]{1,0:T(8,128)S(1)} %shard_map.68, f32[8,512]{1,0:T(8,128)S(1)} %collective-permute-done.11), kind=kLoop, calls=%fused_computation.2 | loop fusion | flops 12288 | bytes 81920 | tf_op jit(solution)/shard_map/add | solution.py:228
  (6 shorter events, 0.1 us)
Async XLA Ops:
  1.0 11.4 %collective-permute-start.1 = (bf16[128,1024]{1,0:T(8,128)(2,1)S(1)}, bf16[128,1024]{1,0:T(8,128)(2,1)S(1)}, u32[]{:S(2)}, u32[]{:S(2)}) collective-permute-start(bf16[128,1024]{1,0:T(8,128)(2,1)S(1)} %shard_map.64.refs_0_.refs_4_), channel_id=1, source_target_pairs={{0,4},{4,8},{8,12},{12,0},{1,5},{5,9},{9,13},{13,1},{2,6},{6,10},{... | collective-permute-start | bytes 786440 | tf_op jit(solution)/shard_map/ppermute | solution.py:197
  9.4 3.0 %collective-permute-start = (f32[2,128,256]{2,1,0:T(8,128)S(1)}, f32[2,128,256]{2,1,0:T(8,128)S(1)}, u32[]{:S(2)}, u32[]{:S(2)}) collective-permute-start(f32[2,128,256]{2,1,0:T(8,128)S(1)} %get-tuple-element.14), channel_id=1, source_target_pairs={{0,1},{1,0},{2,3},{3,2},{4,5},{5,4},{6,7},{7,6},{8,9},{9,8},{10,11... | collective-permute-start | bytes 786440 | tf_op jit(solution)/shard_map/ppermute | solution.py:19
  9.4 10.0 %collective-permute-start.3 = (bf16[128,1024]{1,0:T(8,128)(2,1)S(1)}, bf16[128,1024]{1,0:T(8,128)(2,1)S(1)}, u32[]{:S(2)}, u32[]{:S(2)}) collective-permute-start(bf16[128,1024]{1,0:T(8,128)(2,1)S(1)} %shard_map.64.refs_0_.refs_4_), channel_id=1, source_target_pairs={{0,12},{4,0},{8,4},{12,8},{1,13},{5,1},{9,5},{13,9},{2,14},{6,2},{... | collective-permute-start | bytes 786440 | tf_op jit(solution)/shard_map/ppermute | solution.py:197
  12.4 1.8 %collective-permute-start.2 = (bf16[16,128]{1,0:T(8,128)(2,1)S(1)}, bf16[16,128]{1,0:T(8,128)(2,1)S(1)}, u32[]{:S(2)}, u32[]{:S(2)}) collective-permute-start(bf16[16,128]{1,0:T(8,128)(2,1)S(1)} %slice.16), channel_id=1, source_target_pairs={{0,1},{1,0},{2,3},{3,2},{4,5},{5,4},{6,7},{7,6},{8,9},{9,8},{10,11... | collective-permute-start | bytes 12296 | tf_op jit(solution)/shard_map/ppermute | solution.py:19
  12.4 8.8 %collective-permute-start.6 = (f32[2,128,256]{2,1,0:T(8,128)S(1)}, f32[2,128,256]{2,1,0:T(8,128)S(1)}, u32[]{:S(2)}, u32[]{:S(2)}) collective-permute-start(f32[2,128,256]{2,1,0:T(8,128)S(1)} %add.15.refs_0_), channel_id=1, source_target_pairs={{0,2},{1,3},{2,0},{3,1},{4,6},{5,7},{6,4},{7,5},{8,10},{9,11},{10,... | collective-permute-start | bytes 786440 | tf_op jit(solution)/shard_map/ppermute | solution.py:19
  14.0 11.8 %collective-permute-start.10 = (bf16[128,1024]{1,0:T(8,128)(2,1)S(1)}, bf16[128,1024]{1,0:T(8,128)(2,1)S(1)}, u32[]{:S(2)}, u32[]{:S(2)}) collective-permute-start(bf16[128,1024]{1,0:T(8,128)(2,1)S(1)} %collective-permute-done.1.refs_5_), channel_id=1, source_target_pairs={{0,4},{4,8},{8,12},{12,0},{1,5},{5,9},{9,13},{13,1},{2,6},{6,10},{... | collective-permute-start | bytes 786440 | tf_op jit(solution)/shard_map/ppermute | solution.py:197
  19.5 1.4 %collective-permute-start.4 = (f32[1,128,256]{2,1,0:T(8,128)S(1)}, f32[1,128,256]{2,1,0:T(8,128)S(1)}, u32[]{:S(2)}, u32[]{:S(2)}) collective-permute-start(f32[1,128,256]{2,1,0:T(8,128)S(1)} %get-tuple-element.21), channel_id=1, source_target_pairs={{0,1},{1,0},{2,3},{3,2},{4,5},{5,4},{6,7},{7,6},{8,9},{9,8},{10,11... | collective-permute-start | bytes 393224 | tf_op jit(solution)/shard_map/ppermute | solution.py:19
  19.6 1.5 %collective-permute-start.5 = (f32[1,128,256]{2,1,0:T(8,128)S(1)}, f32[1,128,256]{2,1,0:T(8,128)S(1)}, u32[]{:S(2)}, u32[]{:S(2)}) collective-permute-start(f32[1,128,256]{2,1,0:T(8,128)S(1)} %get-tuple-element.22), channel_id=1, source_target_pairs={{0,1},{1,0},{2,3},{3,2},{4,5},{5,4},{6,7},{7,6},{8,9},{9,8},{10,11... | collective-permute-start | bytes 393224 | tf_op jit(solution)/shard_map/ppermute | solution.py:19
  21.7 4.1 %collective-permute-start.7 = (f32[2,8,128]{2,1,0:T(8,128)S(1)}, f32[2,8,128]{2,1,0:T(8,128)S(1)}, u32[]{:S(2)}, u32[]{:S(2)}) collective-permute-start(f32[2,8,128]{2,1,0:T(8,128)S(1)} %get-tuple-element.18), channel_id=1, source_target_pairs={{0,1},{1,0},{2,3},{3,2},{4,5},{5,4},{6,7},{7,6},{8,9},{9,8},{10,11... | collective-permute-start | bytes 24584 | tf_op jit(solution)/shard_map/ppermute | solution.py:19
  22.0 3.8 %collective-permute-start.8 = (f32[2,8,128]{2,1,0:T(8,128)S(1)}, f32[2,8,128]{2,1,0:T(8,128)S(1)}, u32[]{:S(2)}, u32[]{:S(2)}) collective-permute-start(f32[2,8,128]{2,1,0:T(8,128)S(1)} %get-tuple-element.19), channel_id=1, source_target_pairs={{0,2},{1,3},{2,0},{3,1},{4,6},{5,7},{6,4},{7,5},{8,10},{9,11},{10,... | collective-permute-start | bytes 24584 | tf_op jit(solution)/shard_map/ppermute | solution.py:19
  23.4 3.1 %collective-permute-start.9 = (f32[2,8,128]{2,1,0:T(8,128)S(1)}, f32[2,8,128]{2,1,0:T(8,128)S(1)}, u32[]{:S(2)}, u32[]{:S(2)}) collective-permute-start(f32[2,8,128]{2,1,0:T(8,128)S(1)} %get-tuple-element.20), channel_id=1, source_target_pairs={{0,3},{1,2},{2,1},{3,0},{4,7},{5,6},{6,5},{7,4},{8,11},{9,10},{10,... | collective-permute-start | bytes 24584 | tf_op jit(solution)/shard_map/ppermute | solution.py:19
  26.8 1.9 %collective-permute-start.11 = (f32[8,512]{1,0:T(8,128)S(1)}, f32[8,512]{1,0:T(8,128)S(1)}, u32[]{:S(2)}, u32[]{:S(2)}) collective-permute-start(f32[8,512]{1,0:T(8,128)S(1)} %shard_map.68), channel_id=1, source_target_pairs={{0,1},{1,0},{2,3},{3,2},{4,5},{5,4},{6,7},{7,6},{8,9},{9,8},{10,11... | collective-permute-start | bytes 49160 | tf_op jit(solution)/shard_map/ppermute | solution.py:19
  27.0 3.7 %collective-permute-start.12 = (f32[8,512]{1,0:T(8,128)S(1)}, f32[8,512]{1,0:T(8,128)S(1)}, u32[]{:S(2)}, u32[]{:S(2)}) collective-permute-start(f32[8,512]{1,0:T(8,128)S(1)} %shard_map.68), channel_id=1, source_target_pairs={{0,2},{1,3},{2,0},{3,1},{4,6},{5,7},{6,4},{7,5},{8,10},{9,11},{10,... | collective-permute-start | bytes 49160 | tf_op jit(solution)/shard_map/ppermute | solution.py:19
  27.8 3.2 %collective-permute-start.13 = (f32[8,512]{1,0:T(8,128)S(1)}, f32[8,512]{1,0:T(8,128)S(1)}, u32[]{:S(2)}, u32[]{:S(2)}) collective-permute-start(f32[8,512]{1,0:T(8,128)S(1)} %shard_map.68), channel_id=1, source_target_pairs={{0,3},{1,2},{2,1},{3,0},{4,7},{5,6},{6,5},{7,4},{8,11},{9,10},{10,... | collective-permute-start | bytes 49160 | tf_op jit(solution)/shard_map/ppermute | solution.py:19

commit v20 on v19

--- a/solution.py
+++ b/solution.py
@@ -197,8 +197,8 @@
         return lax.ppermute(value, "dp", [(i, (i + step) % groups) for i in range(groups)])
 
     if groups == 4:
-        first = shift(own, 1)
-        return [(own, 1, 0, 4), (first, 1, 3, 4), (shift(own, -1), 1, 1, 4), (shift(first, 1), 1, 2, 4)]
+        first = shift(own, -1)
+        return [(own, 1, 0, 4), (first, 1, 1, 4), (shift(own, 1), 1, 3, 4), (shift(first, -1), 1, 2, 4)]
     return [(own, 1, 0, groups)] + [(shift(own, step), 1, groups - step, groups) for step in range(1, groups)]
 
 

time: 31.8 us -> 35.2 us (1.11)
  starting transfers between devices: 11.3 us -> 14.7 us
    ppermute x3, starting transfers between devices: 5.33 us -> 8.25 us  [shift(): lax.ppermute(value, 'dp', [(i, (i + step) % groups) for i in range(groups)])]
    ppermute x11, waiting for transfers between devices: 4.02 us -> 6.42 us  [xor_permute(): return lax.ppermute(value, axis, [(i, i ^ step) for i in range(size)])]
    ppermute x3, waiting for transfers between devices: 2.97 us -> 0.67 us  [shift(): lax.ppermute(value, 'dp', [(i, (i + step) % groups) for i in range(groups)])]
    ppermute x11, starting transfers between devices: 6.01 us -> 6.4 us  [xor_permute(): return lax.ppermute(value, axis, [(i, i ^ step) for i in range(size)])]
  transfers between devices with their start and end apart: 14 -> 14, of which waited for: 8 -> 9; matrix products, arithmetic and copies ran while one was open for 0% -> 0% of each run, Pallas kernels for 35% -> 32%
where the time goes in v20:
time: 35.2 us; the launch traced here: 35 us
  starting transfers between devices  14.7 us (42%)
  Pallas kernels  12.5 us (36%)
  waiting for transfers between devices  7.09 us (20%)
  other arithmetic  0.69 us (2%)
    pallas_call x2, Pallas kernels, project(): pl.pallas_call(functools.partial(project_kernel, steps, share, ahead, pie...  10.6 us
    ppermute x3, starting transfers between devices, shift(): lax.ppermute(value, 'dp', [(i, (i + step) % groups) for i in range(groups)])  8.25 us
    ppermute x11, waiting for transfers between devices, xor_permute(): return lax.ppermute(value, axis, [(i, i ^ step) for i in range(size)])  6.42 us
    ppermute x11, starting transfers between devices, xor_permute(): return lax.ppermute(value, axis, [(i, i ^ step) for i in range(size)])  6.4 us
    pallas_call x1, Pallas kernels, cut_tests(): pl.pallas_call(cut_kernel, out_shape=jax.ShapeDtypeStruct((rows, width //...  0.96 us
  transfers between devices with their start and end apart: 14, of which 9 were waited for; matrix products, arithmetic and copies ran while one was open for 0% of the time, Pallas kernels for 32%

profile of v20, /device:TPU:0, one launch (start us, length us, event | category | flops | bytes accessed | tf_op | source)
XLA Modules:
  0.0 35.0 jit_solution(16838853497617278520)
XLA Ops:
  0.0 1.0 %shard_map.64.refs_0_.refs_4_ = bf16[128,1024]{1,0:T(8,128)(2,1)S(1)} custom-call(bf16[128,4096]{1,0:T(8,128)(2,1)} %tests.1), custom_call_target="tpu_custom_call" | custom-call | tf_op jit(solution)/shard_map/pallas_call | solution.py:32
  1.0 5.1 %collective-permute-start.1 = (bf16[128,1024]{1,0:T(8,128)(2,1)S(1)}, bf16[128,1024]{1,0:T(8,128)(2,1)S(1)}, u32[]{:S(2)}, u32[]{:S(2)}) collective-permute-start(bf16[128,1024]{1,0:T(8,128)(2,1)S(1)} %shard_map.64.refs_0_.refs_4_), channel_id=1, source_target_pairs={{0,12},{4,0},{8,4},{12,8},{1,13},{5,1},{9,5},{13,9},{2,14},{6,2},{... | collective-permute-start | bytes 786440 | tf_op jit(solution)/shard_map/ppermute | solution.py:197
  6.1 5.3 %shard_map.65 = (f32[2,128,256]{2,1,0:T(8,128)S(1)}, f32[2,128,256]{2,1,0:T(8,128)S(1)}) custom-call(bf16[8,256,1024]{2,1,0:T(8,128)(2,1)} %act.3, bf16[8,256,3584]{2,1,0:T(8,128)(2,1)} %og.3, bf16[64,1024]{1,0:T(8,128)(2,1)} %bitcast.6, bf16[64,3584]{1,0:T(8,128)(2,1)} %bitcast.4, s32[8]{0:T(128)} %lens.3, bf16[128,1024]{1,0:T(8,128)(2,1)S(1)} %shard_map.64.refs_0_.refs_4_), custom_call_target="tpu_custom_call" | custom-call | flops 4294967296 | bytes 16777216 | tf_op jit(solution)/shard_map/pallas_call | solution.py:110
  11.4 0.1 collective-permute-start
  11.5 0.1 collective-permute-start.3
  11.5 0.1 collective-permute-done.1.refs_5_
  11.6 0.4 %collective-permute-start.2 = (bf16[16,128]{1,0:T(8,128)(2,1)S(1)}, bf16[16,128]{1,0:T(8,128)(2,1)S(1)}, u32[]{:S(2)}, u32[]{:S(2)}) collective-permute-start(bf16[16,128]{1,0:T(8,128)(2,1)S(1)} %slice.16), channel_id=1, source_target_pairs={{0,1},{1,0},{2,3},{3,2},{4,5},{5,4},{6,7},{7,6},{8,9},{9,8},{10,11... | collective-permute-start | bytes 12296 | tf_op jit(solution)/shard_map/ppermute | solution.py:19
  12.0 0.9 %collective-permute-done = f32[2,128,256]{2,1,0:T(8,128)S(1)} collective-permute-done((f32[2,128,256]{2,1,0:T(8,128)S(1)}, f32[2,128,256]{2,1,0:T(8,128)S(1)}, u32[]{:S(2)}, u32[]{:S(2)}) %collective-permute-start) | collective-permute-done | bytes 262176 | tf_op jit(solution)/shard_map/ppermute | solution.py:19
  13.0 1.6 %collective-permute-start.6 = (f32[2,128,256]{2,1,0:T(8,128)S(1)}, f32[2,128,256]{2,1,0:T(8,128)S(1)}, u32[]{:S(2)}, u32[]{:S(2)}) collective-permute-start(f32[2,128,256]{2,1,0:T(8,128)S(1)} %add.15.refs_0_), channel_id=1, source_target_pairs={{0,2},{1,3},{2,0},{3,1},{4,6},{5,7},{6,4},{7,5},{8,10},{9,11},{10,... | collective-permute-start | bytes 786440 | tf_op jit(solution)/shard_map/ppermute | solution.py:19
  14.6 3.1 %collective-permute-start.10 = (bf16[128,1024]{1,0:T(8,128)(2,1)S(1)}, bf16[128,1024]{1,0:T(8,128)(2,1)S(1)}, u32[]{:S(2)}, u32[]{:S(2)}) collective-permute-start(bf16[128,1024]{1,0:T(8,128)(2,1)S(1)} %collective-permute-done.1.refs_5_), channel_id=1, source_target_pairs={{0,12},{4,0},{8,4},{12,8},{1,13},{5,1},{9,5},{13,9},{2,14},{6,2},{... | collective-permute-start | bytes 786440 | tf_op jit(solution)/shard_map/ppermute | solution.py:197
  17.7 0.0 collective-permute-done.2.refs_1_
  17.7 5.3 %shard_map.66 = (f32[2,128,256]{2,1,0:T(8,128)S(1)}, f32[2,128,256]{2,1,0:T(8,128)S(1)}) custom-call(bf16[8,256,1024]{2,1,0:T(8,128)(2,1)} %act.3, bf16[8,256,3584]{2,1,0:T(8,128)(2,1)} %og.3, bf16[64,1024]{1,0:T(8,128)(2,1)} %bitcast.7, bf16[64,3584]{1,0:T(8,128)(2,1)} %bitcast.5, s32[8]{0:T(128)} %lens.3, f32[2,128,256]{2,1,0:T(8,128)S(1)} %add.15.refs_0_, ...), custom_call_target="tpu_custom_call" | custom-call | flops 1024 | bytes 4 | tf_op jit(solution)/shard_map/pallas_call | solution.py:110
  23.1 0.1 collective-permute-start.4
  23.1 0.5 %collective-permute-start.5 = (f32[1,128,256]{2,1,0:T(8,128)S(1)}, f32[1,128,256]{2,1,0:T(8,128)S(1)}, u32[]{:S(2)}, u32[]{:S(2)}) collective-permute-start(f32[1,128,256]{2,1,0:T(8,128)S(1)} %get-tuple-element.22), channel_id=1, source_target_pairs={{0,1},{1,0},{2,3},{3,2},{4,5},{5,4},{6,7},{7,6},{8,9},{9,8},{10,11... | collective-permute-start | bytes 393224 | tf_op jit(solution)/shard_map/ppermute | solution.py:19
  23.6 0.8 %collective-permute-done.4 = f32[1,128,256]{2,1,0:T(8,128)S(1)} collective-permute-done((f32[1,128,256]{2,1,0:T(8,128)S(1)}, f32[1,128,256]{2,1,0:T(8,128)S(1)}, u32[]{:S(2)}, u32[]{:S(2)}) %collective-permute-start.4) | collective-permute-done | bytes 131104 | tf_op jit(solution)/shard_map/ppermute | solution.py:19
  24.5 0.2 collective-permute-done.5
  24.7 0.0 collective-permute-done.6.refs_2_
  24.7 0.5 %shard_map.67 = (f32[2,8,128]{2,1,0:T(8,128)S(1)}, f32[2,8,128]{2,1,0:T(8,128)S(1)}, f32[2,8,128]{2,1,0:T(8,128)S(1)}, f32[2,8,128]{2,1,0:T(8,128)S(1)}) custom-call(f32[2,128,256]{2,1,0:T(8,128)S(1)} %get-tuple-element.15.refs_0_, f32[2,128,256]{2,1,0:T(8,128)S(1)} %pad_maximum_fusion.refs_1_, f32[2,128,256]{2,1,0:T(8,128)S(1)} %collective-permute-done.6.refs_2_), custom_call_target="tpu_custom_call" | custom-call | tf_op jit(solution)/shard_map/pallas_call | solution.py:157
  25.2 0.4 %collective-permute-start.7 = (f32[2,8,128]{2,1,0:T(8,128)S(1)}, f32[2,8,128]{2,1,0:T(8,128)S(1)}, u32[]{:S(2)}, u32[]{:S(2)}) collective-permute-start(f32[2,8,128]{2,1,0:T(8,128)S(1)} %get-tuple-element.18), channel_id=1, source_target_pairs={{0,1},{1,0},{2,3},{3,2},{4,5},{5,4},{6,7},{7,6},{8,9},{9,8},{10,11... | collective-permute-start | bytes 24584 | tf_op jit(solution)/shard_map/ppermute | solution.py:19
  25.6 0.9 %collective-permute-start.8 = (f32[2,8,128]{2,1,0:T(8,128)S(1)}, f32[2,8,128]{2,1,0:T(8,128)S(1)}, u32[]{:S(2)}, u32[]{:S(2)}) collective-permute-start(f32[2,8,128]{2,1,0:T(8,128)S(1)} %get-tuple-element.19), channel_id=1, source_target_pairs={{0,2},{1,3},{2,0},{3,1},{4,6},{5,7},{6,4},{7,5},{8,10},{9,11},{10,... | collective-permute-start | bytes 24584 | tf_op jit(solution)/shard_map/ppermute | solution.py:19
  26.5 0.6 %collective-permute-start.9 = (f32[2,8,128]{2,1,0:T(8,128)S(1)}, f32[2,8,128]{2,1,0:T(8,128)S(1)}, u32[]{:S(2)}, u32[]{:S(2)}) collective-permute-start(f32[2,8,128]{2,1,0:T(8,128)S(1)} %get-tuple-element.20), channel_id=1, source_target_pairs={{0,3},{1,2},{2,1},{3,0},{4,7},{5,6},{6,5},{7,4},{8,11},{9,10},{10,... | collective-permute-start | bytes 24584 | tf_op jit(solution)/shard_map/ppermute | solution.py:19
  27.1 0.6 %collective-permute-done.10.refs_7_ = bf16[128,1024]{1,0:T(8,128)(2,1)S(1)} collective-permute-done((bf16[128,1024]{1,0:T(8,128)(2,1)S(1)}, bf16[128,1024]{1,0:T(8,128)(2,1)S(1)}, u32[]{:S(2)}, u32[]{:S(2)}) %collective-permute-start.10) | collective-permute-done | bytes 262176 | tf_op jit(solution)/shard_map/ppermute | solution.py:197
  27.7 0.0 collective-permute-done.7.refs_1_
  27.7 1.5 %collective-permute-done.8.refs_2_ = f32[2,8,128]{2,1,0:T(8,128)S(1)} collective-permute-done((f32[2,8,128]{2,1,0:T(8,128)S(1)}, f32[2,8,128]{2,1,0:T(8,128)S(1)}, u32[]{:S(2)}, u32[]{:S(2)}) %collective-permute-start.8) | collective-permute-done | bytes 8224 | tf_op jit(solution)/shard_map/ppermute | solution.py:19
  29.2 0.4 %collective-permute-done.9.refs_3_ = f32[2,8,128]{2,1,0:T(8,128)S(1)} collective-permute-done((f32[2,8,128]{2,1,0:T(8,128)S(1)}, f32[2,8,128]{2,1,0:T(8,128)S(1)}, u32[]{:S(2)}, u32[]{:S(2)}) %collective-permute-start.9) | collective-permute-done | bytes 8224 | tf_op jit(solution)/shard_map/ppermute | solution.py:19
  29.6 0.4 %shard_map.68 = f32[8,512]{1,0:T(8,128)S(1)} custom-call(f32[2,8,128]{2,1,0:T(8,128)S(1)} %get-tuple-element.17.refs_0_, f32[2,8,128]{2,1,0:T(8,128)S(1)} %collective-permute-done.7.refs_1_, f32[2,8,128]{2,1,0:T(8,128)S(1)} %collective-permute-done.8.refs_2_, f32[2,8,128]{2,1,0:T(8,128)S(1)} %collective-permute-done.9.refs_3_, ...), custom_call_target="tpu_custom_call" | custom-call | tf_op jit(solution)/shard_map/pallas_call | solution.py:185
  30.0 0.1 collective-permute-start.11
  30.1 1.1 %collective-permute-start.12 = (f32[8,512]{1,0:T(8,128)S(1)}, f32[8,512]{1,0:T(8,128)S(1)}, u32[]{:S(2)}, u32[]{:S(2)}) collective-permute-start(f32[8,512]{1,0:T(8,128)S(1)} %shard_map.68), channel_id=1, source_target_pairs={{0,2},{1,3},{2,0},{3,1},{4,6},{5,7},{6,4},{7,5},{8,10},{9,11},{10,... | collective-permute-start | bytes 49160 | tf_op jit(solution)/shard_map/ppermute | solution.py:19
  31.2 0.6 %collective-permute-start.13 = (f32[8,512]{1,0:T(8,128)S(1)}, f32[8,512]{1,0:T(8,128)S(1)}, u32[]{:S(2)}, u32[]{:S(2)}) collective-permute-start(f32[8,512]{1,0:T(8,128)S(1)} %shard_map.68), channel_id=1, source_target_pairs={{0,3},{1,2},{2,1},{3,0},{4,7},{5,6},{6,5},{7,4},{8,11},{9,10},{10,... | collective-permute-start | bytes 49160 | tf_op jit(solution)/shard_map/ppermute | solution.py:19
  31.9 2.0 %collective-permute-done.12 = f32[8,512]{1,0:T(8,128)S(1)} collective-permute-done((f32[8,512]{1,0:T(8,128)S(1)}, f32[8,512]{1,0:T(8,128)S(1)}, u32[]{:S(2)}, u32[]{:S(2)}) %collective-permute-start.12) | collective-permute-done | bytes 16416 | tf_op jit(solution)/shard_map/ppermute | solution.py:19
  33.9 0.5 %collective-permute-done.13 = f32[8,512]{1,0:T(8,128)S(1)} collective-permute-done((f32[8,512]{1,0:T(8,128)S(1)}, f32[8,512]{1,0:T(8,128)S(1)}, u32[]{:S(2)}, u32[]{:S(2)}) %collective-permute-start.13) | collective-permute-done | bytes 16416 | tf_op jit(solution)/shard_map/ppermute | solution.py:19
  34.4 0.6 %add_add_fusion = f32[8,512]{1,0:T(8,128)} fusion(f32[8,512]{1,0:T(8,128)S(1)} %collective-permute-done.12, f32[8,512]{1,0:T(8,128)S(1)} %collective-permute-done.13, f32[8,512]{1,0:T(8,128)S(1)} %shard_map.68, f32[8,512]{1,0:T(8,128)S(1)} %collective-permute-done.11), kind=kLoop, calls=%fused_computation.2 | loop fusion | flops 12288 | bytes 81920 | tf_op jit(solution)/shard_map/add | solution.py:228
  (6 shorter events, 0.1 us)
Async XLA Ops:
  1.0 10.7 %collective-permute-start.1 = (bf16[128,1024]{1,0:T(8,128)(2,1)S(1)}, bf16[128,1024]{1,0:T(8,128)(2,1)S(1)}, u32[]{:S(2)}, u32[]{:S(2)}) collective-permute-start(bf16[128,1024]{1,0:T(8,128)(2,1)S(1)} %shard_map.64.refs_0_.refs_4_), channel_id=1, source_target_pairs={{0,12},{4,0},{8,4},{12,8},{1,13},{5,1},{9,5},{13,9},{2,14},{6,2},{... | collective-permute-start | bytes 786440 | tf_op jit(solution)/shard_map/ppermute | solution.py:197
  11.4 1.6 %collective-permute-start = (f32[2,128,256]{2,1,0:T(8,128)S(1)}, f32[2,128,256]{2,1,0:T(8,128)S(1)}, u32[]{:S(2)}, u32[]{:S(2)}) collective-permute-start(f32[2,128,256]{2,1,0:T(8,128)S(1)} %get-tuple-element.14), channel_id=1, source_target_pairs={{0,1},{1,0},{2,3},{3,2},{4,5},{5,4},{6,7},{7,6},{8,9},{9,8},{10,11... | collective-permute-start | bytes 786440 | tf_op jit(solution)/shard_map/ppermute | solution.py:19
  11.5 11.5 %collective-permute-start.3 = (bf16[128,1024]{1,0:T(8,128)(2,1)S(1)}, bf16[128,1024]{1,0:T(8,128)(2,1)S(1)}, u32[]{:S(2)}, u32[]{:S(2)}) collective-permute-start(bf16[128,1024]{1,0:T(8,128)(2,1)S(1)} %shard_map.64.refs_0_.refs_4_), channel_id=1, source_target_pairs={{0,4},{4,8},{8,12},{12,0},{1,5},{5,9},{9,13},{13,1},{2,6},{6,10},{... | collective-permute-start | bytes 786440 | tf_op jit(solution)/shard_map/ppermute | solution.py:197
  11.6 6.0 %collective-permute-start.2 = (bf16[16,128]{1,0:T(8,128)(2,1)S(1)}, bf16[16,128]{1,0:T(8,128)(2,1)S(1)}, u32[]{:S(2)}, u32[]{:S(2)}) collective-permute-start(bf16[16,128]{1,0:T(8,128)(2,1)S(1)} %slice.16), channel_id=1, source_target_pairs={{0,1},{1,0},{2,3},{3,2},{4,5},{5,4},{6,7},{7,6},{8,9},{9,8},{10,11... | collective-permute-start | bytes 12296 | tf_op jit(solution)/shard_map/ppermute | solution.py:19
  13.0 11.6 %collective-permute-start.6 = (f32[2,128,256]{2,1,0:T(8,128)S(1)}, f32[2,128,256]{2,1,0:T(8,128)S(1)}, u32[]{:S(2)}, u32[]{:S(2)}) collective-permute-start(f32[2,128,256]{2,1,0:T(8,128)S(1)} %add.15.refs_0_), channel_id=1, source_target_pairs={{0,2},{1,3},{2,0},{3,1},{4,6},{5,7},{6,4},{7,5},{8,10},{9,11},{10,... | collective-permute-start | bytes 786440 | tf_op jit(solution)/shard_map/ppermute | solution.py:19
  14.6 13.1 %collective-permute-start.10 = (bf16[128,1024]{1,0:T(8,128)(2,1)S(1)}, bf16[128,1024]{1,0:T(8,128)(2,1)S(1)}, u32[]{:S(2)}, u32[]{:S(2)}) collective-permute-start(bf16[128,1024]{1,0:T(8,128)(2,1)S(1)} %collective-permute-done.1.refs_5_), channel_id=1, source_target_pairs={{0,12},{4,0},{8,4},{12,8},{1,13},{5,1},{9,5},{13,9},{2,14},{6,2},{... | collective-permute-start | bytes 786440 | tf_op jit(solution)/shard_map/ppermute | solution.py:197
  23.1 1.4 %collective-permute-start.4 = (f32[1,128,256]{2,1,0:T(8,128)S(1)}, f32[1,128,256]{2,1,0:T(8,128)S(1)}, u32[]{:S(2)}, u32[]{:S(2)}) collective-permute-start(f32[1,128,256]{2,1,0:T(8,128)S(1)} %get-tuple-element.21), channel_id=1, source_target_pairs={{0,1},{1,0},{2,3},{3,2},{4,5},{5,4},{6,7},{7,6},{8,9},{9,8},{10,11... | collective-permute-start | bytes 393224 | tf_op jit(solution)/shard_map/ppermute | solution.py:19
  23.1 1.5 %collective-permute-start.5 = (f32[1,128,256]{2,1,0:T(8,128)S(1)}, f32[1,128,256]{2,1,0:T(8,128)S(1)}, u32[]{:S(2)}, u32[]{:S(2)}) collective-permute-start(f32[1,128,256]{2,1,0:T(8,128)S(1)} %get-tuple-element.22), channel_id=1, source_target_pairs={{0,1},{1,0},{2,3},{3,2},{4,5},{5,4},{6,7},{7,6},{8,9},{9,8},{10,11... | collective-permute-start | bytes 393224 | tf_op jit(solution)/shard_map/ppermute | solution.py:19
  25.2 2.5 %collective-permute-start.7 = (f32[2,8,128]{2,1,0:T(8,128)S(1)}, f32[2,8,128]{2,1,0:T(8,128)S(1)}, u32[]{:S(2)}, u32[]{:S(2)}) collective-permute-start(f32[2,8,128]{2,1,0:T(8,128)S(1)} %get-tuple-element.18), channel_id=1, source_target_pairs={{0,1},{1,0},{2,3},{3,2},{4,5},{5,4},{6,7},{7,6},{8,9},{9,8},{10,11... | collective-permute-start | bytes 24584 | tf_op jit(solution)/shard_map/ppermute | solution.py:19
  25.6 3.7 %collective-permute-start.8 = (f32[2,8,128]{2,1,0:T(8,128)S(1)}, f32[2,8,128]{2,1,0:T(8,128)S(1)}, u32[]{:S(2)}, u32[]{:S(2)}) collective-permute-start(f32[2,8,128]{2,1,0:T(8,128)S(1)} %get-tuple-element.19), channel_id=1, source_target_pairs={{0,2},{1,3},{2,0},{3,1},{4,6},{5,7},{6,4},{7,5},{8,10},{9,11},{10,... | collective-permute-start | bytes 24584 | tf_op jit(solution)/shard_map/ppermute | solution.py:19
  26.5 3.1 %collective-permute-start.9 = (f32[2,8,128]{2,1,0:T(8,128)S(1)}, f32[2,8,128]{2,1,0:T(8,128)S(1)}, u32[]{:S(2)}, u32[]{:S(2)}) collective-permute-start(f32[2,8,128]{2,1,0:T(8,128)S(1)} %get-tuple-element.20), channel_id=1, source_target_pairs={{0,3},{1,2},{2,1},{3,0},{4,7},{5,6},{6,5},{7,4},{8,11},{9,10},{10,... | collective-permute-start | bytes 24584 | tf_op jit(solution)/shard_map/ppermute | solution.py:19
  30.0 1.9 %collective-permute-start.11 = (f32[8,512]{1,0:T(8,128)S(1)}, f32[8,512]{1,0:T(8,128)S(1)}, u32[]{:S(2)}, u32[]{:S(2)}) collective-permute-start(f32[8,512]{1,0:T(8,128)S(1)} %shard_map.68), channel_id=1, source_target_pairs={{0,1},{1,0},{2,3},{3,2},{4,5},{5,4},{6,7},{7,6},{8,9},{9,8},{10,11... | collective-permute-start | bytes 49160 | tf_op jit(solution)/shard_map/ppermute | solution.py:19
  30.1 3.8 %collective-permute-start.12 = (f32[8,512]{1,0:T(8,128)S(1)}, f32[8,512]{1,0:T(8,128)S(1)}, u32[]{:S(2)}, u32[]{:S(2)}) collective-permute-start(f32[8,512]{1,0:T(8,128)S(1)} %shard_map.68), channel_id=1, source_target_pairs={{0,2},{1,3},{2,0},{3,1},{4,6},{5,7},{6,4},{7,5},{8,10},{9,11},{10,... | collective-permute-start | bytes 49160 | tf_op jit(solution)/shard_map/ppermute | solution.py:19
  31.2 3.2 %collective-permute-start.13 = (f32[8,512]{1,0:T(8,128)S(1)}, f32[8,512]{1,0:T(8,128)S(1)}, u32[]{:S(2)}, u32[]{:S(2)}) collective-permute-start(f32[8,512]{1,0:T(8,128)S(1)} %shard_map.68), channel_id=1, source_target_pairs={{0,3},{1,2},{2,1},{3,0},{4,7},{5,6},{6,5},{7,4},{8,11},{9,10},{10,... | collective-permute-start | bytes 49160 | tf_op jit(solution)/shard_map/ppermute | solution.py:19

commit v21 on v17

--- a/solution.py
+++ b/solution.py
@@ -60,7 +60,7 @@
 LATER = 1<<10
 
 
-def project_kernel(steps, share, ahead, piece, after, act, og, lens, wide, *refs):
+def project_kernel(steps, share, ahead, piece, height, after, act, og, lens, wide, *refs):
     refs = refs[after:]
     outs, (buf, lenbuf, sem, lensem) = refs[:-4], refs[-4:]
     me = lax.axis_index("tensor")
@@ -85,35 +85,36 @@
         for copy in group:
             copy.start()
     lencopy.start()
-    sums = [None] * len(steps)
+    count = len(steps) * share
+    sums = [None] * (count // height)
     for slot, (side, at, width) in enumerate(pieces):
         for copy in copies[slot]:
             copy.wait()
         for copy in copies[slot + ahead] if slot + ahead < len(copies) else ():
             copy.start()
         weight = wide[side * feat + at : side * feat + at + width]
-        for i in range(len(steps)):
-            token = buf[slot, i * share : (i + 1) * share].reshape(share * slots, piece)[:, :width]
+        for i in range(len(sums)):
+            token = buf[slot, i * height : (i + 1) * height].reshape(height * slots, piece)[:, :width]
             part = jnp.dot(token, weight, preferred_element_type=jnp.float32)
             sums[i] = part if sums[i] is None else sums[i] + part
     lencopy.wait()
     col = lax.broadcasted_iota(jnp.int32, (rank, slots), 1)
     places = [out.at[i] for out in outs for i in range(out.shape[0])]
     for slot, out in enumerate(places):
-        i, k = divmod(slot, share)
-        length = lenbuf[(me ^ steps[i]) * share + k]
+        length = lenbuf[(me ^ steps[slot // share]) * share + slot % share]
+        i, k = divmod(slot, height)
         both = sums[i][k * slots : (k + 1) * slots].T
         out[:rank] = jnp.where(col < length, both[:rank] * (1.0 / length.astype(jnp.float32)), 0.0)
         out[rank:] = both[rank:]
 
 
-def project(act, og, lens, wide, groups, share, ahead, piece, cost, after=()):
+def project(act, og, lens, wide, groups, share, ahead, piece, height, cost, after=()):
     steps = [step for group in groups for step in group]
     count = len(steps) * share
     slots, feat, hidden = act.shape[1], act.shape[2], og.shape[2]
     pieces = -(-feat // piece) - (-hidden // piece)
     return pl.pallas_call(
-        functools.partial(project_kernel, steps, share, ahead, piece, len(after)),
+        functools.partial(project_kernel, steps, share, ahead, piece, height, len(after)),
         out_shape=[jax.ShapeDtypeStruct((len(group) * share, wide.shape[1], slots), jnp.float32) for group in groups],
         in_specs=[HBM] * 3 + [VMEM] * (1 + len(after)),
         out_specs=[VMEM] * len(groups),
@@ -196,14 +197,12 @@
 
 
 def gather_tests(own, groups):
-    ring = [0, 1, 3, 2] if groups == 4 else list(range(groups))
-
     def shift(value, step):
-        return lax.ppermute(value, "dp", [(ring[i], ring[(i + step) % groups]) for i in range(groups)])
+        return lax.ppermute(value, "dp", [(i, (i + step) % groups) for i in range(groups)])
 
     if groups == 4:
         first = shift(own, 1)
-        return [(own, 1, 0, 4), (first, -2, 12, 5), (shift(own, -1), 2, 1, 5), (shift(first, 1), -1, 3, 4)]
+        return [(own, 1, 0, 4), (first, 1, 3, 4), (shift(own, -1), 1, 1, 4), (shift(first, 1), 1, 2, 4)]
     return [(own, 1, 0, groups)] + [(shift(own, step), 1, groups - step, groups) for step in range(1, groups)]
 
 
@@ -215,11 +214,11 @@
 
     far = [CORES * x for x in range(1, size // CORES)]
     arrays = (activations, out_grads, lengths, wide)
-    far_other, far_own = project(*arrays, [[step ^ 1 for step in far], far], share, 4, 512, COST, [own_tests])
+    far_other, far_own = project(*arrays, [[step ^ 1 for step in far], far], share, 4, 512, 1, COST, [own_tests])
     far_sum = far_own + xor_permute(far_other, "tensor", size, 1)
     sums = [xor_permute(far_sum[i * share : (i + 1) * share], "tensor", size, step) for i, step in enumerate(far)]
     here = xor_permute(tests[1][0][:16, :128], "tensor", size, 1)
-    near_other, near_own = project(*arrays, [[1], [0]], share, 4, 512, LATER, [far_sum, here])
+    near_other, near_own = project(*arrays, [[1], [0]], share, 4, 512, 2 * share, LATER, [far_sum, here])
     late = tests[2][0][: near_other.shape[1], : near_other.shape[2]].astype(jnp.float32)
     pieces = [near_other[k : k + 1] for k in range(share)]
     pieces[0] = pieces[0] + 0.0 * late[None]

time: 32.7 us -> 34 us (1.040)
  Pallas kernels: 12.2 us -> 14.9 us
  waiting for transfers between devices: 7.5 us -> 6.6 us
  starting transfers between devices: 12 us -> 11.6 us
    pallas_call x2, Pallas kernels: 9.93 us -> 12.6 us  [project(): pl.pallas_call(functools.partial(project_kernel, steps, share, ahead, pie...]
    ppermute x3, waiting for transfers between devices: 3.62 us -> 1.06 us  [shift(): lax.ppermute(value, 'dp', [(i, (i + step) % groups) for i in range(groups)])]
    ppermute x11, waiting for transfers between devices: 3.88 us -> 5.54 us  [xor_permute(): return lax.ppermute(value, axis, [(i, i ^ step) for i in range(size)])]
  transfers between devices with their start and end apart: 14 -> 14, of which waited for: 6 -> 8; matrix products, arithmetic and copies ran while one was open for 0% -> 0% of each run, Pallas kernels for 32% -> 39%
where the time goes in v21:
time: 34 us; the launch traced here: 33.9 us
  Pallas kernels  14.9 us (44%)
  starting transfers between devices  11.6 us (34%)
  waiting for transfers between devices  6.6 us (19%)
  other arithmetic  0.69 us (2%)
    pallas_call x2, Pallas kernels, project(): pl.pallas_call(functools.partial(project_kernel, steps, share, ahead, pie...  12.6 us
    ppermute x11, starting transfers between devices, xor_permute(): return lax.ppermute(value, axis, [(i, i ^ step) for i in range(size)])  6 us
    ppermute x3, starting transfers between devices, shift(): lax.ppermute(value, 'dp', [(i, (i + step) % groups) for i in range(groups)])  5.61 us
    ppermute x11, waiting for transfers between devices, xor_permute(): return lax.ppermute(value, axis, [(i, i ^ step) for i in range(size)])  5.54 us
    pallas_call x1, Pallas kernels, first(): pl.pallas_call(first_kernel, out_shape=[jax.ShapeDtypeStruct((rows, width...  1.4 us
    ppermute x3, waiting for transfers between devices, shift(): lax.ppermute(value, 'dp', [(i, (i + step) % groups) for i in range(groups)])  1.06 us
  transfers between devices with their start and end apart: 14, of which 8 were waited for; matrix products, arithmetic and copies ran while one was open for 0% of the time, Pallas kernels for 39%

profile of v21, /device:TPU:0, one launch (start us, length us, event | category | flops | bytes accessed | tf_op | source)
XLA Modules:
  0.0 33.9 jit_solution(3586185383060386977)
XLA Ops:
  0.0 1.4 %shard_map.64 = (bf16[128,1024]{1,0:T(8,128)(2,1)S(1)}, bf16[4608,128]{1,0:T(8,128)(2,1)S(1)}) custom-call(bf16[128,4096]{1,0:T(8,128)(2,1)} %tests.1, bf16[64,1024]{1,0:T(8,128)(2,1)} %bitcast.5, bf16[64,3584]{1,0:T(8,128)(2,1)} %bitcast.4), custom_call_target="tpu_custom_call" | custom-call | tf_op jit(solution)/shard_map/pallas_call | solution.py:46
  1.4 3.1 %collective-permute-start.1 = (bf16[128,1024]{1,0:T(8,128)(2,1)S(1)}, bf16[128,1024]{1,0:T(8,128)(2,1)S(1)}, u32[]{:S(2)}, u32[]{:S(2)}) collective-permute-start(bf16[128,1024]{1,0:T(8,128)(2,1)S(1)} %get-tuple-element.16.refs_0_.refs_4_), channel_id=1, source_target_pairs={{0,4},{4,8},{8,12},{12,0},{1,5},{5,9},{9,13},{13,1},{2,6},{6,10},{... | collective-permute-start | bytes 786440 | tf_op jit(solution)/shard_map/ppermute | solution.py:201
  4.5 5.6 %shard_map.65 = (f32[2,128,256]{2,1,0:T(8,128)S(1)}, f32[2,128,256]{2,1,0:T(8,128)S(1)}) custom-call(bf16[8,256,1024]{2,1,0:T(8,128)(2,1)} %act.3, bf16[8,256,3584]{2,1,0:T(8,128)(2,1)} %og.3, s32[8]{0:T(128)} %lens.3, bf16[4608,128]{1,0:T(8,128)(2,1)S(1)} %get-tuple-element.15.wide, bf16[128,1024]{1,0:T(8,128)(2,1)S(1)} %get-tuple-element.16.refs_0_.refs_4_), custom_call_target="tpu_custom_call" | custom-call | flops 4294967296 | bytes 16777216 | tf_op jit(solution)/shard_map/pallas_call | solution.py:116
  10.1 0.1 collective-permute-start
  10.2 2.1 %collective-permute-start.3 = (bf16[128,1024]{1,0:T(8,128)(2,1)S(1)}, bf16[128,1024]{1,0:T(8,128)(2,1)S(1)}, u32[]{:S(2)}, u32[]{:S(2)}) collective-permute-start(bf16[128,1024]{1,0:T(8,128)(2,1)S(1)} %get-tuple-element.16.refs_0_.refs_4_), channel_id=1, source_target_pairs={{0,12},{4,0},{8,4},{12,8},{1,13},{5,1},{9,5},{13,9},{2,14},{6,2},{... | collective-permute-start | bytes 786440 | tf_op jit(solution)/shard_map/ppermute | solution.py:201
  12.3 0.5 %collective-permute-done.1.refs_5_ = bf16[128,1024]{1,0:T(8,128)(2,1)S(1)} collective-permute-done((bf16[128,1024]{1,0:T(8,128)(2,1)S(1)}, bf16[128,1024]{1,0:T(8,128)(2,1)S(1)}, u32[]{:S(2)}, u32[]{:S(2)}) %collective-permute-start.1) | collective-permute-done | bytes 262176 | tf_op jit(solution)/shard_map/ppermute | solution.py:201
  12.8 0.0 collective-permute-start.2
  12.8 0.0 collective-permute-done
  12.9 1.6 %collective-permute-start.6 = (f32[2,128,256]{2,1,0:T(8,128)S(1)}, f32[2,128,256]{2,1,0:T(8,128)S(1)}, u32[]{:S(2)}, u32[]{:S(2)}) collective-permute-start(f32[2,128,256]{2,1,0:T(8,128)S(1)} %add.15.refs_0_), channel_id=1, source_target_pairs={{0,2},{1,3},{2,0},{3,1},{4,6},{5,7},{6,4},{7,5},{8,10},{9,11},{10,... | collective-permute-start | bytes 786440 | tf_op jit(solution)/shard_map/ppermute | solution.py:19
  14.4 0.4 %collective-permute-start.10 = (bf16[128,1024]{1,0:T(8,128)(2,1)S(1)}, bf16[128,1024]{1,0:T(8,128)(2,1)S(1)}, u32[]{:S(2)}, u32[]{:S(2)}) collective-permute-start(bf16[128,1024]{1,0:T(8,128)(2,1)S(1)} %collective-permute-done.1.refs_5_), channel_id=1, source_target_pairs={{0,4},{4,8},{8,12},{12,0},{1,5},{5,9},{9,13},{13,1},{2,6},{6,10},{... | collective-permute-start | bytes 786440 | tf_op jit(solution)/shard_map/ppermute | solution.py:201
  14.9 0.0 collective-permute-done.2.refs_1_
  14.9 7.0 %shard_map.66 = (f32[2,128,256]{2,1,0:T(8,128)S(1)}, f32[2,128,256]{2,1,0:T(8,128)S(1)}) custom-call(bf16[8,256,1024]{2,1,0:T(8,128)(2,1)} %act.3, bf16[8,256,3584]{2,1,0:T(8,128)(2,1)} %og.3, s32[8]{0:T(128)} %lens.3, bf16[4608,128]{1,0:T(8,128)(2,1)S(1)} %get-tuple-element.15.wide, f32[2,128,256]{2,1,0:T(8,128)S(1)} %add.15.refs_0_, ...), custom_call_target="tpu_custom_call" | custom-call | flops 1024 | bytes 4 | tf_op jit(solution)/shard_map/pallas_call | solution.py:116
  21.9 0.1 collective-permute-start.4
  22.0 0.5 %collective-permute-start.5 = (f32[1,128,256]{2,1,0:T(8,128)S(1)}, f32[1,128,256]{2,1,0:T(8,128)S(1)}, u32[]{:S(2)}, u32[]{:S(2)}) collective-permute-start(f32[1,128,256]{2,1,0:T(8,128)S(1)} %get-tuple-element.26), channel_id=1, source_target_pairs={{0,1},{1,0},{2,3},{3,2},{4,5},{5,4},{6,7},{7,6},{8,9},{9,8},{10,11... | collective-permute-start | bytes 393224 | tf_op jit(solution)/shard_map/ppermute | solution.py:19
  22.5 0.8 %collective-permute-done.4 = f32[1,128,256]{2,1,0:T(8,128)S(1)} collective-permute-done((f32[1,128,256]{2,1,0:T(8,128)S(1)}, f32[1,128,256]{2,1,0:T(8,128)S(1)}, u32[]{:S(2)}, u32[]{:S(2)}) %collective-permute-start.4) | collective-permute-done | bytes 131104 | tf_op jit(solution)/shard_map/ppermute | solution.py:19
  23.4 0.2 collective-permute-done.5
  23.6 0.0 collective-permute-done.6.refs_2_
  23.6 0.5 %shard_map.67 = (f32[2,8,128]{2,1,0:T(8,128)S(1)}, f32[2,8,128]{2,1,0:T(8,128)S(1)}, f32[2,8,128]{2,1,0:T(8,128)S(1)}, f32[2,8,128]{2,1,0:T(8,128)S(1)}) custom-call(f32[2,128,256]{2,1,0:T(8,128)S(1)} %get-tuple-element.19.refs_0_, f32[2,128,256]{2,1,0:T(8,128)S(1)} %pad_maximum_fusion.refs_1_, f32[2,128,256]{2,1,0:T(8,128)S(1)} %collective-permute-done.6.refs_2_), custom_call_target="tpu_custom_call" | custom-call | tf_op jit(solution)/shard_map/pallas_call | solution.py:161
  24.1 0.4 %collective-permute-start.7 = (f32[2,8,128]{2,1,0:T(8,128)S(1)}, f32[2,8,128]{2,1,0:T(8,128)S(1)}, u32[]{:S(2)}, u32[]{:S(2)}) collective-permute-start(f32[2,8,128]{2,1,0:T(8,128)S(1)} %get-tuple-element.22), channel_id=1, source_target_pairs={{0,1},{1,0},{2,3},{3,2},{4,5},{5,4},{6,7},{7,6},{8,9},{9,8},{10,11... | collective-permute-start | bytes 24584 | tf_op jit(solution)/shard_map/ppermute | solution.py:19
  24.5 0.6 %collective-permute-start.8 = (f32[2,8,128]{2,1,0:T(8,128)S(1)}, f32[2,8,128]{2,1,0:T(8,128)S(1)}, u32[]{:S(2)}, u32[]{:S(2)}) collective-permute-start(f32[2,8,128]{2,1,0:T(8,128)S(1)} %get-tuple-element.23), channel_id=1, source_target_pairs={{0,2},{1,3},{2,0},{3,1},{4,6},{5,7},{6,4},{7,5},{8,10},{9,11},{10,... | collective-permute-start | bytes 24584 | tf_op jit(solution)/shard_map/ppermute | solution.py:19
  25.1 0.9 %collective-permute-start.9 = (f32[2,8,128]{2,1,0:T(8,128)S(1)}, f32[2,8,128]{2,1,0:T(8,128)S(1)}, u32[]{:S(2)}, u32[]{:S(2)}) collective-permute-start(f32[2,8,128]{2,1,0:T(8,128)S(1)} %get-tuple-element.24), channel_id=1, source_target_pairs={{0,3},{1,2},{2,1},{3,0},{4,7},{5,6},{6,5},{7,4},{8,11},{9,10},{10,... | collective-permute-start | bytes 24584 | tf_op jit(solution)/shard_map/ppermute | solution.py:19
  26.0 0.5 %collective-permute-done.10.refs_7_ = bf16[128,1024]{1,0:T(8,128)(2,1)S(1)} collective-permute-done((bf16[128,1024]{1,0:T(8,128)(2,1)S(1)}, bf16[128,1024]{1,0:T(8,128)(2,1)S(1)}, u32[]{:S(2)}, u32[]{:S(2)}) %collective-permute-start.10) | collective-permute-done | bytes 262176 | tf_op jit(solution)/shard_map/ppermute | solution.py:201
  26.5 0.0 collective-permute-done.7.refs_1_
  26.5 1.6 %collective-permute-done.8.refs_2_ = f32[2,8,128]{2,1,0:T(8,128)S(1)} collective-permute-done((f32[2,8,128]{2,1,0:T(8,128)S(1)}, f32[2,8,128]{2,1,0:T(8,128)S(1)}, u32[]{:S(2)}, u32[]{:S(2)}) %collective-permute-start.8) | collective-permute-done | bytes 8224 | tf_op jit(solution)/shard_map/ppermute | solution.py:19
  28.2 0.1 collective-permute-done.9.refs_3_
  28.3 0.4 %shard_map.68 = f32[8,512]{1,0:T(8,128)S(1)} custom-call(f32[2,8,128]{2,1,0:T(8,128)S(1)} %get-tuple-element.21.refs_0_, f32[2,8,128]{2,1,0:T(8,128)S(1)} %collective-permute-done.7.refs_1_, f32[2,8,128]{2,1,0:T(8,128)S(1)} %collective-permute-done.8.refs_2_, f32[2,8,128]{2,1,0:T(8,128)S(1)} %collective-permute-done.9.refs_3_, ...), custom_call_target="tpu_custom_call" | custom-call | tf_op jit(solution)/shard_map/pallas_call | solution.py:189
  28.6 0.1 collective-permute-start.11
  28.8 1.4 %collective-permute-start.12 = (f32[8,512]{1,0:T(8,128)S(1)}, f32[8,512]{1,0:T(8,128)S(1)}, u32[]{:S(2)}, u32[]{:S(2)}) collective-permute-start(f32[8,512]{1,0:T(8,128)S(1)} %shard_map.68), channel_id=1, source_target_pairs={{0,2},{1,3},{2,0},{3,1},{4,6},{5,7},{6,4},{7,5},{8,10},{9,11},{10,... | collective-permute-start | bytes 49160 | tf_op jit(solution)/shard_map/ppermute | solution.py:19
  30.1 0.4 %collective-permute-start.13 = (f32[8,512]{1,0:T(8,128)S(1)}, f32[8,512]{1,0:T(8,128)S(1)}, u32[]{:S(2)}, u32[]{:S(2)}) collective-permute-start(f32[8,512]{1,0:T(8,128)S(1)} %shard_map.68), channel_id=1, source_target_pairs={{0,3},{1,2},{2,1},{3,0},{4,7},{5,6},{6,5},{7,4},{8,11},{9,10},{10,... | collective-permute-start | bytes 49160 | tf_op jit(solution)/shard_map/ppermute | solution.py:19
  30.5 2.0 %collective-permute-done.12 = f32[8,512]{1,0:T(8,128)S(1)} collective-permute-done((f32[8,512]{1,0:T(8,128)S(1)}, f32[8,512]{1,0:T(8,128)S(1)}, u32[]{:S(2)}, u32[]{:S(2)}) %collective-permute-start.12) | collective-permute-done | bytes 16416 | tf_op jit(solution)/shard_map/ppermute | solution.py:19
  32.5 0.8 %collective-permute-done.13 = f32[8,512]{1,0:T(8,128)S(1)} collective-permute-done((f32[8,512]{1,0:T(8,128)S(1)}, f32[8,512]{1,0:T(8,128)S(1)}, u32[]{:S(2)}, u32[]{:S(2)}) %collective-permute-start.13) | collective-permute-done | bytes 16416 | tf_op jit(solution)/shard_map/ppermute | solution.py:19
  33.3 0.6 %add_add_fusion = f32[8,512]{1,0:T(8,128)} fusion(f32[8,512]{1,0:T(8,128)S(1)} %collective-permute-done.12, f32[8,512]{1,0:T(8,128)S(1)} %collective-permute-done.13, f32[8,512]{1,0:T(8,128)S(1)} %shard_map.68, f32[8,512]{1,0:T(8,128)S(1)} %collective-permute-done.11), kind=kLoop, calls=%fused_computation.2 | loop fusion | flops 12288 | bytes 81920 | tf_op jit(solution)/shard_map/add | solution.py:232
  (6 shorter events, 0.1 us)
Async XLA Ops:
  1.4 11.4 %collective-permute-start.1 = (bf16[128,1024]{1,0:T(8,128)(2,1)S(1)}, bf16[128,1024]{1,0:T(8,128)(2,1)S(1)}, u32[]{:S(2)}, u32[]{:S(2)}) collective-permute-start(bf16[128,1024]{1,0:T(8,128)(2,1)S(1)} %get-tuple-element.16.refs_0_.refs_4_), channel_id=1, source_target_pairs={{0,4},{4,8},{8,12},{12,0},{1,5},{5,9},{9,13},{13,1},{2,6},{6,10},{... | collective-permute-start | bytes 786440 | tf_op jit(solution)/shard_map/ppermute | solution.py:201
  10.1 2.7 %collective-permute-start = (f32[2,128,256]{2,1,0:T(8,128)S(1)}, f32[2,128,256]{2,1,0:T(8,128)S(1)}, u32[]{:S(2)}, u32[]{:S(2)}) collective-permute-start(f32[2,128,256]{2,1,0:T(8,128)S(1)} %get-tuple-element.18), channel_id=1, source_target_pairs={{0,1},{1,0},{2,3},{3,2},{4,5},{5,4},{6,7},{7,6},{8,9},{9,8},{10,11... | collective-permute-start | bytes 786440 | tf_op jit(solution)/shard_map/ppermute | solution.py:19
  10.2 11.7 %collective-permute-start.3 = (bf16[128,1024]{1,0:T(8,128)(2,1)S(1)}, bf16[128,1024]{1,0:T(8,128)(2,1)S(1)}, u32[]{:S(2)}, u32[]{:S(2)}) collective-permute-start(bf16[128,1024]{1,0:T(8,128)(2,1)S(1)} %get-tuple-element.16.refs_0_.refs_4_), channel_id=1, source_target_pairs={{0,12},{4,0},{8,4},{12,8},{1,13},{5,1},{9,5},{13,9},{2,14},{6,2},{... | collective-permute-start | bytes 786440 | tf_op jit(solution)/shard_map/ppermute | solution.py:201
  12.8 2.0 %collective-permute-start.2 = (bf16[16,128]{1,0:T(8,128)(2,1)S(1)}, bf16[16,128]{1,0:T(8,128)(2,1)S(1)}, u32[]{:S(2)}, u32[]{:S(2)}) collective-permute-start(bf16[16,128]{1,0:T(8,128)(2,1)S(1)} %slice.16), channel_id=1, source_target_pairs={{0,1},{1,0},{2,3},{3,2},{4,5},{5,4},{6,7},{7,6},{8,9},{9,8},{10,11... | collective-permute-start | bytes 12296 | tf_op jit(solution)/shard_map/ppermute | solution.py:19
  12.9 10.7 %collective-permute-start.6 = (f32[2,128,256]{2,1,0:T(8,128)S(1)}, f32[2,128,256]{2,1,0:T(8,128)S(1)}, u32[]{:S(2)}, u32[]{:S(2)}) collective-permute-start(f32[2,128,256]{2,1,0:T(8,128)S(1)} %add.15.refs_0_), channel_id=1, source_target_pairs={{0,2},{1,3},{2,0},{3,1},{4,6},{5,7},{6,4},{7,5},{8,10},{9,11},{10,... | collective-permute-start | bytes 786440 | tf_op jit(solution)/shard_map/ppermute | solution.py:19
  14.4 12.1 %collective-permute-start.10 = (bf16[128,1024]{1,0:T(8,128)(2,1)S(1)}, bf16[128,1024]{1,0:T(8,128)(2,1)S(1)}, u32[]{:S(2)}, u32[]{:S(2)}) collective-permute-start(bf16[128,1024]{1,0:T(8,128)(2,1)S(1)} %collective-permute-done.1.refs_5_), channel_id=1, source_target_pairs={{0,4},{4,8},{8,12},{12,0},{1,5},{5,9},{9,13},{13,1},{2,6},{6,10},{... | collective-permute-start | bytes 786440 | tf_op jit(solution)/shard_map/ppermute | solution.py:201
  21.9 1.4 %collective-permute-start.4 = (f32[1,128,256]{2,1,0:T(8,128)S(1)}, f32[1,128,256]{2,1,0:T(8,128)S(1)}, u32[]{:S(2)}, u32[]{:S(2)}) collective-permute-start(f32[1,128,256]{2,1,0:T(8,128)S(1)} %get-tuple-element.25), channel_id=1, source_target_pairs={{0,1},{1,0},{2,3},{3,2},{4,5},{5,4},{6,7},{7,6},{8,9},{9,8},{10,11... | collective-permute-start | bytes 393224 | tf_op jit(solution)/shard_map/ppermute | solution.py:19
  22.0 1.5 %collective-permute-start.5 = (f32[1,128,256]{2,1,0:T(8,128)S(1)}, f32[1,128,256]{2,1,0:T(8,128)S(1)}, u32[]{:S(2)}, u32[]{:S(2)}) collective-permute-start(f32[1,128,256]{2,1,0:T(8,128)S(1)} %get-tuple-element.26), channel_id=1, source_target_pairs={{0,1},{1,0},{2,3},{3,2},{4,5},{5,4},{6,7},{7,6},{8,9},{9,8},{10,11... | collective-permute-start | bytes 393224 | tf_op jit(solution)/shard_map/ppermute | solution.py:19
  24.1 2.4 %collective-permute-start.7 = (f32[2,8,128]{2,1,0:T(8,128)S(1)}, f32[2,8,128]{2,1,0:T(8,128)S(1)}, u32[]{:S(2)}, u32[]{:S(2)}) collective-permute-start(f32[2,8,128]{2,1,0:T(8,128)S(1)} %get-tuple-element.22), channel_id=1, source_target_pairs={{0,1},{1,0},{2,3},{3,2},{4,5},{5,4},{6,7},{7,6},{8,9},{9,8},{10,11... | collective-permute-start | bytes 24584 | tf_op jit(solution)/shard_map/ppermute | solution.py:19
  24.5 3.7 %collective-permute-start.8 = (f32[2,8,128]{2,1,0:T(8,128)S(1)}, f32[2,8,128]{2,1,0:T(8,128)S(1)}, u32[]{:S(2)}, u32[]{:S(2)}) collective-permute-start(f32[2,8,128]{2,1,0:T(8,128)S(1)} %get-tuple-element.23), channel_id=1, source_target_pairs={{0,2},{1,3},{2,0},{3,1},{4,6},{5,7},{6,4},{7,5},{8,10},{9,11},{10,... | collective-permute-start | bytes 24584 | tf_op jit(solution)/shard_map/ppermute | solution.py:19
  25.1 3.2 %collective-permute-start.9 = (f32[2,8,128]{2,1,0:T(8,128)S(1)}, f32[2,8,128]{2,1,0:T(8,128)S(1)}, u32[]{:S(2)}, u32[]{:S(2)}) collective-permute-start(f32[2,8,128]{2,1,0:T(8,128)S(1)} %get-tuple-element.24), channel_id=1, source_target_pairs={{0,3},{1,2},{2,1},{3,0},{4,7},{5,6},{6,5},{7,4},{8,11},{9,10},{10,... | collective-permute-start | bytes 24584 | tf_op jit(solution)/shard_map/ppermute | solution.py:19
  28.6 1.9 %collective-permute-start.11 = (f32[8,512]{1,0:T(8,128)S(1)}, f32[8,512]{1,0:T(8,128)S(1)}, u32[]{:S(2)}, u32[]{:S(2)}) collective-permute-start(f32[8,512]{1,0:T(8,128)S(1)} %shard_map.68), channel_id=1, source_target_pairs={{0,1},{1,0},{2,3},{3,2},{4,5},{5,4},{6,7},{7,6},{8,9},{9,8},{10,11... | collective-permute-start | bytes 49160 | tf_op jit(solution)/shard_map/ppermute | solution.py:19
  28.8 3.8 %collective-permute-start.12 = (f32[8,512]{1,0:T(8,128)S(1)}, f32[8,512]{1,0:T(8,128)S(1)}, u32[]{:S(2)}, u32[]{:S(2)}) collective-permute-start(f32[8,512]{1,0:T(8,128)S(1)} %shard_map.68), channel_id=1, source_target_pairs={{0,2},{1,3},{2,0},{3,1},{4,6},{5,7},{6,4},{7,5},{8,10},{9,11},{10,... | collective-permute-start | bytes 49160 | tf_op jit(solution)/shard_map/ppermute | solution.py:19
  30.1 3.2 %collective-permute-start.13 = (f32[8,512]{1,0:T(8,128)S(1)}, f32[8,512]{1,0:T(8,128)S(1)}, u32[]{:S(2)}, u32[]{:S(2)}) collective-permute-start(f32[8,512]{1,0:T(8,128)S(1)} %shard_map.68), channel_id=1, source_target_pairs={{0,3},{1,2},{2,1},{3,0},{4,7},{5,6},{6,5},{7,4},{8,11},{9,10},{10,... | collective-permute-start | bytes 49160 | tf_op jit(solution)/shard_map/ppermute | solution.py:19

commit v22 on v21

--- a/solution.py
+++ b/solution.py
@@ -19,54 +19,42 @@
     return lax.ppermute(value, axis, [(i, i ^ step) for i in range(size)])
 
 
-def first_kernel(tests, wi, wo, own, wide, wibuf, wobuf, sem):
-    width = own.shape[1]
+def cut_kernel(tests, out, sem):
+    width = out.shape[1]
     start = pl.multiple_of(lax.axis_index("tensor") * width, 128)
-    copies = [
-        pltpu.make_async_copy(wi, wibuf, sem.at[0]),
-        pltpu.make_async_copy(wo, wobuf, sem.at[1]),
-        pltpu.make_async_copy(tests.at[:, pl.ds(start, width)], own, sem.at[2]),
-    ]
-    for copy in copies:
-        copy.start()
-    feat = wibuf.shape[1]
-    for side, buf in enumerate((wibuf, wobuf)):
-        copies[side].wait()
-        for at in range(0, buf.shape[1], 256):
-            weight = buf[:, at : at + 256]
-            none = jnp.zeros_like(weight)
-            both = jnp.concatenate([none, weight] if side else [weight, none], axis=0)
-            wide[side * feat + at : side * feat + at + weight.shape[1]] = both.T
-    copies[2].wait()
-
-
-def first(tests, wi, wo, size):
+    copy = pltpu.make_async_copy(tests.at[:, pl.ds(start, width)], out, sem)
+    copy.start()
+    copy.wait()
+
+
+def cut_tests(tests, size):
     rows, width = tests.shape
-    rank, feat = wi.shape
-    return pl.pallas_call(
-        first_kernel,
-        out_shape=[
-            jax.ShapeDtypeStruct((rows, width // size), tests.dtype),
-            jax.ShapeDtypeStruct((feat + wo.shape[1], 2 * rank), wi.dtype),
-        ],
-        in_specs=[HBM] * 3,
-        out_specs=[VMEM] * 2,
-        scratch_shapes=[pltpu.VMEM(wi.shape, wi.dtype), pltpu.VMEM(wo.shape, wo.dtype), pltpu.SemaphoreType.DMA((3,))],
+    return pl.pallas_call(
+        cut_kernel,
+        out_shape=jax.ShapeDtypeStruct((rows, width // size), tests.dtype),
+        in_specs=[HBM],
+        out_specs=VMEM,
+        scratch_shapes=[pltpu.SemaphoreType.DMA],
         compiler_params=SMALL,
-    )(in_hbm(tests), in_hbm(wi), in_hbm(wo))
-
-
+    )(in_hbm(tests))
+
+
+AHEAD = 4
 COST = 1 << 32
 LATER = 1<<10
 
 
-def project_kernel(steps, share, ahead, piece, height, after, act, og, lens, wide, *refs):
-    refs = refs[after:]
-    outs, (buf, lenbuf, sem, lensem) = refs[:-4], refs[-4:]
+def project_kernel(steps, share, piece, fresh, after, act, og, lens, *refs):
+    if fresh:
+        (wi, wo), refs = refs[:2], refs[2 + after :]
+        outs, (wide, buf, lenbuf, sem, lensem, wibuf, wobuf, wsem) = refs[:-8], refs[-8:]
+    else:
+        wide, refs = refs[0], refs[1 + after :]
+        outs, (buf, lenbuf, sem, lensem) = refs[:-4], refs[-4:]
     me = lax.axis_index("tensor")
     rank = wide.shape[1] // 2
     slots, feat = act.shape[1:]
-    lencopy = pltpu.make_async_copy(lens, lenbuf, lensem)
+    count = len(steps) * share
     pieces = [
         (side, at, min(piece, ref.shape[2] - at)) for side, ref in enumerate((act, og)) for at in range(0, ref.shape[2], piece)
     ]
@@ -81,52 +69,71 @@
         ]
         for slot, (side, at, width) in enumerate(pieces)
     ]
-    for group in copies[:ahead]:
+    lencopy = pltpu.make_async_copy(lens, lenbuf, lensem)
+    if fresh:
+        weights = [pltpu.make_async_copy(wi, wibuf, wsem.at[0]), pltpu.make_async_copy(wo, wobuf, wsem.at[1])]
+        weights[0].start()
+        weights[1].start()
+    for group in copies[:AHEAD]:
         for copy in group:
             copy.start()
     lencopy.start()
-    count = len(steps) * share
-    sums = [None] * (count // height)
+    sums = [None, None]
     for slot, (side, at, width) in enumerate(pieces):
+        rows = slice(side * feat + at, side * feat + at + width)
+        if fresh:
+            if at == 0:
+                weights[side].wait()
+            weight = (wibuf, wobuf)[side][:, at : at + width]
+            none = jnp.zeros_like(weight)
+            wide[rows] = jnp.concatenate([none, weight] if side else [weight, none], axis=0).T
         for copy in copies[slot]:
             copy.wait()
-        for copy in copies[slot + ahead] if slot + ahead < len(copies) else ():
+        for copy in copies[slot + AHEAD] if slot + AHEAD < len(copies) else ():
             copy.start()
-        weight = wide[side * feat + at : side * feat + at + width]
-        for i in range(len(sums)):
-            token = buf[slot, i * height : (i + 1) * height].reshape(height * slots, piece)[:, :width]
-            part = jnp.dot(token, weight, preferred_element_type=jnp.float32)
-            sums[i] = part if sums[i] is None else sums[i] + part
+        weight = wide[rows]
+        token = buf[slot].reshape(count * slots, piece)
+        for half, start in enumerate(range(0, width, piece // 2)):
+            stop = min(start + piece // 2, width)
+            part = jnp.dot(token[:, start:stop], weight[start:stop], preferred_element_type=jnp.float32)
+            sums[half] = part if sums[half] is None else sums[half] + part
+    total = sums[0] + sums[1]
     lencopy.wait()
     col = lax.broadcasted_iota(jnp.int32, (rank, slots), 1)
     places = [out.at[i] for out in outs for i in range(out.shape[0])]
     for slot, out in enumerate(places):
         length = lenbuf[(me ^ steps[slot // share]) * share + slot % share]
-        i, k = divmod(slot, height)
-        both = sums[i][k * slots : (k + 1) * slots].T
+        both = total[slot * slots : (slot + 1) * slots].T
         out[:rank] = jnp.where(col < length, both[:rank] * (1.0 / length.astype(jnp.float32)), 0.0)
         out[rank:] = both[rank:]
 
 
-def project(act, og, lens, wide, groups, share, ahead, piece, height, cost, after=()):
+def project(act, og, lens, weights, groups, share, piece, cost, after=()):
     steps = [step for group in groups for step in group]
     count = len(steps) * share
     slots, feat, hidden = act.shape[1], act.shape[2], og.shape[2]
     pieces = -(-feat // piece) - (-hidden // piece)
-    return pl.pallas_call(
-        functools.partial(project_kernel, steps, share, ahead, piece, height, len(after)),
-        out_shape=[jax.ShapeDtypeStruct((len(group) * share, wide.shape[1], slots), jnp.float32) for group in groups],
-        in_specs=[HBM] * 3 + [VMEM] * (1 + len(after)),
-        out_specs=[VMEM] * len(groups),
-        scratch_shapes=[
-            pltpu.VMEM((pieces, count, slots, piece), act.dtype),
-            pltpu.SMEM(lens.shape, lens.dtype),
-            pltpu.SemaphoreType.DMA((pieces, len(steps))),
-            pltpu.SemaphoreType.DMA,
-        ],
+    fresh = len(weights) == 2
+    columns = 2 * weights[0].shape[0] if fresh else weights[0].shape[1]
+    shapes = [jax.ShapeDtypeStruct((len(group) * share, columns, slots), jnp.float32) for group in groups]
+    scratch = [
+        pltpu.VMEM((pieces, count, slots, piece), act.dtype),
+        pltpu.SMEM(lens.shape, lens.dtype),
+        pltpu.SemaphoreType.DMA((pieces, len(steps))),
+        pltpu.SemaphoreType.DMA,
+    ]
+    if fresh:
+        shapes += [jax.ShapeDtypeStruct((feat + hidden, columns), act.dtype)]
+        scratch += [pltpu.VMEM(one.shape, one.dtype) for one in weights] + [pltpu.SemaphoreType.DMA((2,))]
+    return pl.pallas_call(
+        functools.partial(project_kernel, steps, share, piece, fresh, len(after)),
+        out_shape=shapes,
+        in_specs=[HBM] * 3 + [HBM if fresh else VMEM] * len(weights) + [VMEM] * len(after),
+        out_specs=[VMEM] * len(shapes),
+        scratch_shapes=scratch,
         compiler_params=pltpu.CompilerParams(vmem_limit_bytes=32 << 20),
         cost_estimate=pl.CostEstimate(flops=cost, bytes_accessed=cost // 256, transcendentals=0),
-    )(*map(in_hbm, (act, og, lens)), wide, *after)
+    )(*map(in_hbm, (act, og, lens)), *(map(in_hbm, weights) if fresh else weights), *after)
 
 
 def unit_kernel(share, rank, size, *refs):
@@ -209,16 +216,17 @@
 def shards(size, groups, activations, out_grads, proj_in, proj_out, lengths, test_grads):
     rank = proj_in.shape[1]
     share = activations.shape[0] // size
-    own_tests, wide = first(test_grads, proj_in.T, proj_out.T, size)
+    own_tests = cut_tests(test_grads, size)
     tests = gather_tests(own_tests, groups)
 
     far = [CORES * x for x in range(1, size // CORES)]
-    arrays = (activations, out_grads, lengths, wide)
-    far_other, far_own = project(*arrays, [[step ^ 1 for step in far], far], share, 4, 512, 1, COST, [own_tests])
+    arrays = (activations, out_grads, lengths)
+    sends = [[step ^ 1 for step in far], far]
+    far_other, far_own, wide = project(*arrays, [proj_in.T, proj_out.T], sends, share, 512, COST, [own_tests])
     far_sum = far_own + xor_permute(far_other, "tensor", size, 1)
     sums = [xor_permute(far_sum[i * share : (i + 1) * share], "tensor", size, step) for i, step in enumerate(far)]
     here = xor_permute(tests[1][0][:16, :128], "tensor", size, 1)
-    near_other, near_own = project(*arrays, [[1], [0]], share, 4, 512, 2 * share, LATER, [far_sum, here])
+    near_other, near_own = project(*arrays, [wide], [[1], [0]], share, 512, LATER, [far_sum, here])
     late = tests[2][0][: near_other.shape[1], : near_other.shape[2]].astype(jnp.float32)
     pieces = [near_other[k : k + 1] for k in range(share)]
     pieces[0] = pieces[0] + 0.0 * late[None]

time: 34 us -> 35.7 us (1.050)
  Pallas kernels: 14.9 us -> 16.5 us
  starting transfers between devices: 11.6 us -> 12.2 us
  waiting for transfers between devices: 6.6 us -> 6.02 us
    pallas_call x3, Pallas kernels: 14 us -> 15.7 us  [the longest x2 14.7 us: project(): pl.pallas_call(functools.partial(project_kernel, steps, share, piece, fre...]
    ppermute x3, waiting for transfers between devices: 1.06 us -> 0.5 us  [shift(): lax.ppermute(value, 'dp', [(i, (i + step) % groups) for i in range(groups)])]
    ppermute x11, starting transfers between devices: 6 us -> 6.4 us  [xor_permute(): return lax.ppermute(value, axis, [(i, i ^ step) for i in range(size)])]
  transfers between devices with their start and end apart: 14 -> 14, of which waited for: 8 -> 6; matrix products, arithmetic and copies ran while one was open for 0% -> 0% of each run, Pallas kernels for 39% -> 43%
where the time goes in v22:
time: 35.7 us; the launch traced here: 35.6 us
  Pallas kernels  16.5 us (46%)
  starting transfers between devices  12.2 us (34%)
  waiting for transfers between devices  6.02 us (17%)
  other arithmetic  0.69 us (2%)
    pallas_call x2, Pallas kernels, project(): pl.pallas_call(functools.partial(project_kernel, steps, share, piece, fre...  14.7 us
    ppermute x11, starting transfers between devices, xor_permute(): return lax.ppermute(value, axis, [(i, i ^ step) for i in range(size)])  6.4 us
    ppermute x3, starting transfers between devices, shift(): lax.ppermute(value, 'dp', [(i, (i + step) % groups) for i in range(groups)])  5.81 us
    ppermute x11, waiting for transfers between devices, xor_permute(): return lax.ppermute(value, axis, [(i, i ^ step) for i in range(size)])  5.52 us
    pallas_call x1, Pallas kernels, cut_tests(): pl.pallas_call(cut_kernel, out_shape=jax.ShapeDtypeStruct((rows, width //...  0.96 us
  transfers between devices with their start and end apart: 14, of which 6 were waited for; matrix products, arithmetic and copies ran while one was open for 0% of the time, Pallas kernels for 43%

profile of v22, /device:TPU:0, one launch (start us, length us, event | category | flops | bytes accessed | tf_op | source)
XLA Modules:
  0.0 35.6 jit_solution(3596983441006618558)
XLA Ops:
  0.0 1.0 %shard_map.64.refs_2_.refs_4_ = bf16[128,1024]{1,0:T(8,128)(2,1)S(1)} custom-call(bf16[128,4096]{1,0:T(8,128)(2,1)} %tests.1), custom_call_target="tpu_custom_call" | custom-call | tf_op jit(solution)/shard_map/pallas_call | solution.py:32
  1.0 3.1 %collective-permute-start.1 = (bf16[128,1024]{1,0:T(8,128)(2,1)S(1)}, bf16[128,1024]{1,0:T(8,128)(2,1)S(1)}, u32[]{:S(2)}, u32[]{:S(2)}) collective-permute-start(bf16[128,1024]{1,0:T(8,128)(2,1)S(1)} %shard_map.64.refs_2_.refs_4_), channel_id=1, source_target_pairs={{0,4},{4,8},{8,12},{12,0},{1,5},{5,9},{9,13},{13,1},{2,6},{6,10},{... | collective-permute-start | bytes 786440 | tf_op jit(solution)/shard_map/ppermute | solution.py:208
  4.0 7.7 %shard_map.65 = (f32[2,128,256]{2,1,0:T(8,128)S(1)}, f32[2,128,256]{2,1,0:T(8,128)S(1)}, bf16[4608,128]{1,0:T(8,128)(2,1)S(1)}) custom-call(bf16[8,256,1024]{2,1,0:T(8,128)(2,1)} %act.3, bf16[8,256,3584]{2,1,0:T(8,128)(2,1)} %og.3, s32[8]{0:T(128)} %lens.3, bf16[64,1024]{1,0:T(8,128)(2,1)} %bitcast.5, bf16[64,3584]{1,0:T(8,128)(2,1)} %bitcast.4, ...), custom_call_target="tpu_custom_call" | custom-call | flops 4294967296 | bytes 16777216 | tf_op jit(solution)/shard_map/pallas_call | solution.py:128
  11.7 0.1 collective-permute-start
  11.8 2.1 %collective-permute-start.3 = (bf16[128,1024]{1,0:T(8,128)(2,1)S(1)}, bf16[128,1024]{1,0:T(8,128)(2,1)S(1)}, u32[]{:S(2)}, u32[]{:S(2)}) collective-permute-start(bf16[128,1024]{1,0:T(8,128)(2,1)S(1)} %shard_map.64.refs_2_.refs_4_), channel_id=1, source_target_pairs={{0,12},{4,0},{8,4},{12,8},{1,13},{5,1},{9,5},{13,9},{2,14},{6,2},{... | collective-permute-start | bytes 786440 | tf_op jit(solution)/shard_map/ppermute | solution.py:208
  13.9 0.2 collective-permute-start.2
  14.1 0.0 collective-permute-done
  14.1 1.8 %collective-permute-start.6 = (f32[2,128,256]{2,1,0:T(8,128)S(1)}, f32[2,128,256]{2,1,0:T(8,128)S(1)}, u32[]{:S(2)}, u32[]{:S(2)}) collective-permute-start(f32[2,128,256]{2,1,0:T(8,128)S(1)} %add.15.refs_1_), channel_id=1, source_target_pairs={{0,2},{1,3},{2,0},{3,1},{4,6},{5,7},{6,4},{7,5},{8,10},{9,11},{10,... | collective-permute-start | bytes 786440 | tf_op jit(solution)/shard_map/ppermute | solution.py:19
  15.9 0.6 %collective-permute-start.10 = (bf16[128,1024]{1,0:T(8,128)(2,1)S(1)}, bf16[128,1024]{1,0:T(8,128)(2,1)S(1)}, u32[]{:S(2)}, u32[]{:S(2)}) collective-permute-start(bf16[128,1024]{1,0:T(8,128)(2,1)S(1)} %collective-permute-done.1.refs_5_), channel_id=1, source_target_pairs={{0,4},{4,8},{8,12},{12,0},{1,5},{5,9},{9,13},{13,1},{2,6},{6,10},{... | collective-permute-start | bytes 786440 | tf_op jit(solution)/shard_map/ppermute | solution.py:208
  16.5 0.0 collective-permute-done.2.refs_2_
  16.5 7.0 %shard_map.66 = (f32[2,128,256]{2,1,0:T(8,128)S(1)}, f32[2,128,256]{2,1,0:T(8,128)S(1)}) custom-call(bf16[8,256,1024]{2,1,0:T(8,128)(2,1)} %act.3, bf16[8,256,3584]{2,1,0:T(8,128)(2,1)} %og.3, s32[8]{0:T(128)} %lens.3, bf16[4608,128]{1,0:T(8,128)(2,1)S(1)} %get-tuple-element.14.refs_0_, f32[2,128,256]{2,1,0:T(8,128)S(1)} %add.15.refs_1_, ...), custom_call_target="tpu_custom_call" | custom-call | flops 1024 | bytes 4 | tf_op jit(solution)/shard_map/pallas_call | solution.py:128
  23.5 0.0 collective-permute-done.3.refs_6_
  23.6 0.1 collective-permute-start.4
  23.7 0.5 %collective-permute-start.5 = (f32[1,128,256]{2,1,0:T(8,128)S(1)}, f32[1,128,256]{2,1,0:T(8,128)S(1)}, u32[]{:S(2)}, u32[]{:S(2)}) collective-permute-start(f32[1,128,256]{2,1,0:T(8,128)S(1)} %get-tuple-element.24), channel_id=1, source_target_pairs={{0,1},{1,0},{2,3},{3,2},{4,5},{5,4},{6,7},{7,6},{8,9},{9,8},{10,11... | collective-permute-start | bytes 393224 | tf_op jit(solution)/shard_map/ppermute | solution.py:19
  24.2 0.8 %collective-permute-done.4 = f32[1,128,256]{2,1,0:T(8,128)S(1)} collective-permute-done((f32[1,128,256]{2,1,0:T(8,128)S(1)}, f32[1,128,256]{2,1,0:T(8,128)S(1)}, u32[]{:S(2)}, u32[]{:S(2)}) %collective-permute-start.4) | collective-permute-done | bytes 131104 | tf_op jit(solution)/shard_map/ppermute | solution.py:19
  25.0 0.2 collective-permute-done.5
  25.2 0.0 collective-permute-done.6.refs_2_
  25.2 0.5 %shard_map.67 = (f32[2,8,128]{2,1,0:T(8,128)S(1)}, f32[2,8,128]{2,1,0:T(8,128)S(1)}, f32[2,8,128]{2,1,0:T(8,128)S(1)}, f32[2,8,128]{2,1,0:T(8,128)S(1)}) custom-call(f32[2,128,256]{2,1,0:T(8,128)S(1)} %get-tuple-element.17.refs_0_, f32[2,128,256]{2,1,0:T(8,128)S(1)} %pad_maximum_fusion.refs_1_, f32[2,128,256]{2,1,0:T(8,128)S(1)} %collective-permute-done.6.refs_2_), custom_call_target="tpu_custom_call" | custom-call | tf_op jit(solution)/shard_map/pallas_call | solution.py:168
  25.7 0.4 %collective-permute-start.7 = (f32[2,8,128]{2,1,0:T(8,128)S(1)}, f32[2,8,128]{2,1,0:T(8,128)S(1)}, u32[]{:S(2)}, u32[]{:S(2)}) collective-permute-start(f32[2,8,128]{2,1,0:T(8,128)S(1)} %get-tuple-element.20), channel_id=1, source_target_pairs={{0,1},{1,0},{2,3},{3,2},{4,5},{5,4},{6,7},{7,6},{8,9},{9,8},{10,11... | collective-permute-start | bytes 24584 | tf_op jit(solution)/shard_map/ppermute | solution.py:19
  26.1 0.5 %collective-permute-start.8 = (f32[2,8,128]{2,1,0:T(8,128)S(1)}, f32[2,8,128]{2,1,0:T(8,128)S(1)}, u32[]{:S(2)}, u32[]{:S(2)}) collective-permute-start(f32[2,8,128]{2,1,0:T(8,128)S(1)} %get-tuple-element.21), channel_id=1, source_target_pairs={{0,2},{1,3},{2,0},{3,1},{4,6},{5,7},{6,4},{7,5},{8,10},{9,11},{10,... | collective-permute-start | bytes 24584 | tf_op jit(solution)/shard_map/ppermute | solution.py:19
  26.6 1.0 %collective-permute-start.9 = (f32[2,8,128]{2,1,0:T(8,128)S(1)}, f32[2,8,128]{2,1,0:T(8,128)S(1)}, u32[]{:S(2)}, u32[]{:S(2)}) collective-permute-start(f32[2,8,128]{2,1,0:T(8,128)S(1)} %get-tuple-element.22), channel_id=1, source_target_pairs={{0,3},{1,2},{2,1},{3,0},{4,7},{5,6},{6,5},{7,4},{8,11},{9,10},{10,... | collective-permute-start | bytes 24584 | tf_op jit(solution)/shard_map/ppermute | solution.py:19
  27.7 0.5 %collective-permute-done.10.refs_7_ = bf16[128,1024]{1,0:T(8,128)(2,1)S(1)} collective-permute-done((bf16[128,1024]{1,0:T(8,128)(2,1)S(1)}, bf16[128,1024]{1,0:T(8,128)(2,1)S(1)}, u32[]{:S(2)}, u32[]{:S(2)}) %collective-permute-start.10) | collective-permute-done | bytes 262176 | tf_op jit(solution)/shard_map/ppermute | solution.py:208
  28.2 0.0 collective-permute-done.7.refs_1_
  28.2 1.7 %collective-permute-done.8.refs_2_ = f32[2,8,128]{2,1,0:T(8,128)S(1)} collective-permute-done((f32[2,8,128]{2,1,0:T(8,128)S(1)}, f32[2,8,128]{2,1,0:T(8,128)S(1)}, u32[]{:S(2)}, u32[]{:S(2)}) %collective-permute-start.8) | collective-permute-done | bytes 8224 | tf_op jit(solution)/shard_map/ppermute | solution.py:19
  29.8 0.0 collective-permute-done.9.refs_3_
  29.8 0.4 %shard_map.68 = f32[8,512]{1,0:T(8,128)S(1)} custom-call(f32[2,8,128]{2,1,0:T(8,128)S(1)} %get-tuple-element.19.refs_0_, f32[2,8,128]{2,1,0:T(8,128)S(1)} %collective-permute-done.7.refs_1_, f32[2,8,128]{2,1,0:T(8,128)S(1)} %collective-permute-done.8.refs_2_, f32[2,8,128]{2,1,0:T(8,128)S(1)} %collective-permute-done.9.refs_3_, ...), custom_call_target="tpu_custom_call" | custom-call | tf_op jit(solution)/shard_map/pallas_call | solution.py:196
  30.2 0.1 collective-permute-start.11
  30.3 1.5 %collective-permute-start.12 = (f32[8,512]{1,0:T(8,128)S(1)}, f32[8,512]{1,0:T(8,128)S(1)}, u32[]{:S(2)}, u32[]{:S(2)}) collective-permute-start(f32[8,512]{1,0:T(8,128)S(1)} %shard_map.68), channel_id=1, source_target_pairs={{0,2},{1,3},{2,0},{3,1},{4,6},{5,7},{6,4},{7,5},{8,10},{9,11},{10,... | collective-permute-start | bytes 49160 | tf_op jit(solution)/shard_map/ppermute | solution.py:19
  31.8 0.3 collective-permute-start.13
  32.1 2.0 %collective-permute-done.12 = f32[8,512]{1,0:T(8,128)S(1)} collective-permute-done((f32[8,512]{1,0:T(8,128)S(1)}, f32[8,512]{1,0:T(8,128)S(1)}, u32[]{:S(2)}, u32[]{:S(2)}) %collective-permute-start.12) | collective-permute-done | bytes 16416 | tf_op jit(solution)/shard_map/ppermute | solution.py:19
  34.1 0.9 %collective-permute-done.13 = f32[8,512]{1,0:T(8,128)S(1)} collective-permute-done((f32[8,512]{1,0:T(8,128)S(1)}, f32[8,512]{1,0:T(8,128)S(1)}, u32[]{:S(2)}, u32[]{:S(2)}) %collective-permute-start.13) | collective-permute-done | bytes 16416 | tf_op jit(solution)/shard_map/ppermute | solution.py:19
  34.9 0.6 %add_add_fusion = f32[8,512]{1,0:T(8,128)} fusion(f32[8,512]{1,0:T(8,128)S(1)} %collective-permute-done.12, f32[8,512]{1,0:T(8,128)S(1)} %collective-permute-done.13, f32[8,512]{1,0:T(8,128)S(1)} %shard_map.68, f32[8,512]{1,0:T(8,128)S(1)} %collective-permute-done.11), kind=kLoop, calls=%fused_computation.2 | loop fusion | flops 12288 | bytes 81920 | tf_op jit(solution)/shard_map/add | solution.py:240
  (6 shorter events, 0.1 us)
Async XLA Ops:
  1.0 12.9 %collective-permute-start.1 = (bf16[128,1024]{1,0:T(8,128)(2,1)S(1)}, bf16[128,1024]{1,0:T(8,128)(2,1)S(1)}, u32[]{:S(2)}, u32[]{:S(2)}) collective-permute-start(bf16[128,1024]{1,0:T(8,128)(2,1)S(1)} %shard_map.64.refs_2_.refs_4_), channel_id=1, source_target_pairs={{0,4},{4,8},{8,12},{12,0},{1,5},{5,9},{9,13},{13,1},{2,6},{6,10},{... | collective-permute-start | bytes 786440 | tf_op jit(solution)/shard_map/ppermute | solution.py:208
  11.7 2.4 %collective-permute-start = (f32[2,128,256]{2,1,0:T(8,128)S(1)}, f32[2,128,256]{2,1,0:T(8,128)S(1)}, u32[]{:S(2)}, u32[]{:S(2)}) collective-permute-start(f32[2,128,256]{2,1,0:T(8,128)S(1)} %get-tuple-element.16), channel_id=1, source_target_pairs={{0,1},{1,0},{2,3},{3,2},{4,5},{5,4},{6,7},{7,6},{8,9},{9,8},{10,11... | collective-permute-start | bytes 786440 | tf_op jit(solution)/shard_map/ppermute | solution.py:19
  11.8 11.7 %collective-permute-start.3 = (bf16[128,1024]{1,0:T(8,128)(2,1)S(1)}, bf16[128,1024]{1,0:T(8,128)(2,1)S(1)}, u32[]{:S(2)}, u32[]{:S(2)}) collective-permute-start(bf16[128,1024]{1,0:T(8,128)(2,1)S(1)} %shard_map.64.refs_2_.refs_4_), channel_id=1, source_target_pairs={{0,12},{4,0},{8,4},{12,8},{1,13},{5,1},{9,5},{13,9},{2,14},{6,2},{... | collective-permute-start | bytes 786440 | tf_op jit(solution)/shard_map/ppermute | solution.py:208
  13.9 2.6 %collective-permute-start.2 = (bf16[16,128]{1,0:T(8,128)(2,1)S(1)}, bf16[16,128]{1,0:T(8,128)(2,1)S(1)}, u32[]{:S(2)}, u32[]{:S(2)}) collective-permute-start(bf16[16,128]{1,0:T(8,128)(2,1)S(1)} %slice.16), channel_id=1, source_target_pairs={{0,1},{1,0},{2,3},{3,2},{4,5},{5,4},{6,7},{7,6},{8,9},{9,8},{10,11... | collective-permute-start | bytes 12296 | tf_op jit(solution)/shard_map/ppermute | solution.py:19
  14.1 11.1 %collective-permute-start.6 = (f32[2,128,256]{2,1,0:T(8,128)S(1)}, f32[2,128,256]{2,1,0:T(8,128)S(1)}, u32[]{:S(2)}, u32[]{:S(2)}) collective-permute-start(f32[2,128,256]{2,1,0:T(8,128)S(1)} %add.15.refs_1_), channel_id=1, source_target_pairs={{0,2},{1,3},{2,0},{3,1},{4,6},{5,7},{6,4},{7,5},{8,10},{9,11},{10,... | collective-permute-start | bytes 786440 | tf_op jit(solution)/shard_map/ppermute | solution.py:19
  15.9 12.3 %collective-permute-start.10 = (bf16[128,1024]{1,0:T(8,128)(2,1)S(1)}, bf16[128,1024]{1,0:T(8,128)(2,1)S(1)}, u32[]{:S(2)}, u32[]{:S(2)}) collective-permute-start(bf16[128,1024]{1,0:T(8,128)(2,1)S(1)} %collective-permute-done.1.refs_5_), channel_id=1, source_target_pairs={{0,4},{4,8},{8,12},{12,0},{1,5},{5,9},{9,13},{13,1},{2,6},{6,10},{... | collective-permute-start | bytes 786440 | tf_op jit(solution)/shard_map/ppermute | solution.py:208
  23.6 1.4 %collective-permute-start.4 = (f32[1,128,256]{2,1,0:T(8,128)S(1)}, f32[1,128,256]{2,1,0:T(8,128)S(1)}, u32[]{:S(2)}, u32[]{:S(2)}) collective-permute-start(f32[1,128,256]{2,1,0:T(8,128)S(1)} %get-tuple-element.23), channel_id=1, source_target_pairs={{0,1},{1,0},{2,3},{3,2},{4,5},{5,4},{6,7},{7,6},{8,9},{9,8},{10,11... | collective-permute-start | bytes 393224 | tf_op jit(solution)/shard_map/ppermute | solution.py:19
  23.7 1.5 %collective-permute-start.5 = (f32[1,128,256]{2,1,0:T(8,128)S(1)}, f32[1,128,256]{2,1,0:T(8,128)S(1)}, u32[]{:S(2)}, u32[]{:S(2)}) collective-permute-start(f32[1,128,256]{2,1,0:T(8,128)S(1)} %get-tuple-element.24), channel_id=1, source_target_pairs={{0,1},{1,0},{2,3},{3,2},{4,5},{5,4},{6,7},{7,6},{8,9},{9,8},{10,11... | collective-permute-start | bytes 393224 | tf_op jit(solution)/shard_map/ppermute | solution.py:19
  25.7 2.4 %collective-permute-start.7 = (f32[2,8,128]{2,1,0:T(8,128)S(1)}, f32[2,8,128]{2,1,0:T(8,128)S(1)}, u32[]{:S(2)}, u32[]{:S(2)}) collective-permute-start(f32[2,8,128]{2,1,0:T(8,128)S(1)} %get-tuple-element.20), channel_id=1, source_target_pairs={{0,1},{1,0},{2,3},{3,2},{4,5},{5,4},{6,7},{7,6},{8,9},{9,8},{10,11... | collective-permute-start | bytes 24584 | tf_op jit(solution)/shard_map/ppermute | solution.py:19
  26.1 3.7 %collective-permute-start.8 = (f32[2,8,128]{2,1,0:T(8,128)S(1)}, f32[2,8,128]{2,1,0:T(8,128)S(1)}, u32[]{:S(2)}, u32[]{:S(2)}) collective-permute-start(f32[2,8,128]{2,1,0:T(8,128)S(1)} %get-tuple-element.21), channel_id=1, source_target_pairs={{0,2},{1,3},{2,0},{3,1},{4,6},{5,7},{6,4},{7,5},{8,10},{9,11},{10,... | collective-permute-start | bytes 24584 | tf_op jit(solution)/shard_map/ppermute | solution.py:19
  26.6 3.2 %collective-permute-start.9 = (f32[2,8,128]{2,1,0:T(8,128)S(1)}, f32[2,8,128]{2,1,0:T(8,128)S(1)}, u32[]{:S(2)}, u32[]{:S(2)}) collective-permute-start(f32[2,8,128]{2,1,0:T(8,128)S(1)} %get-tuple-element.22), channel_id=1, source_target_pairs={{0,3},{1,2},{2,1},{3,0},{4,7},{5,6},{6,5},{7,4},{8,11},{9,10},{10,... | collective-permute-start | bytes 24584 | tf_op jit(solution)/shard_map/ppermute | solution.py:19
  30.2 1.9 %collective-permute-start.11 = (f32[8,512]{1,0:T(8,128)S(1)}, f32[8,512]{1,0:T(8,128)S(1)}, u32[]{:S(2)}, u32[]{:S(2)}) collective-permute-start(f32[8,512]{1,0:T(8,128)S(1)} %shard_map.68), channel_id=1, source_target_pairs={{0,1},{1,0},{2,3},{3,2},{4,5},{5,4},{6,7},{7,6},{8,9},{9,8},{10,11... | collective-permute-start | bytes 49160 | tf_op jit(solution)/shard_map/ppermute | solution.py:19
  30.3 3.7 %collective-permute-start.12 = (f32[8,512]{1,0:T(8,128)S(1)}, f32[8,512]{1,0:T(8,128)S(1)}, u32[]{:S(2)}, u32[]{:S(2)}) collective-permute-start(f32[8,512]{1,0:T(8,128)S(1)} %shard_map.68), channel_id=1, source_target_pairs={{0,2},{1,3},{2,0},{3,1},{4,6},{5,7},{6,4},{7,5},{8,10},{9,11},{10,... | collective-permute-start | bytes 49160 | tf_op jit(solution)/shard_map/ppermute | solution.py:19
  31.8 3.2 %collective-permute-start.13 = (f32[8,512]{1,0:T(8,128)S(1)}, f32[8,512]{1,0:T(8,128)S(1)}, u32[]{:S(2)}, u32[]{:S(2)}) collective-permute-start(f32[8,512]{1,0:T(8,128)S(1)} %shard_map.68), channel_id=1, source_target_pairs={{0,3},{1,2},{2,1},{3,0},{4,7},{5,6},{6,5},{7,4},{8,11},{9,10},{10,... | collective-permute-start | bytes 49160 | tf_op jit(solution)/shard_map/ppermute | solution.py:19

commit v23 on v19

--- a/solution.py
+++ b/solution.py
@@ -43,7 +43,7 @@
 LATER = 1<<10
 
 
-def project_kernel(steps, share, ahead, piece, after, act, og, wi, wo, lens, *refs):
+def project_kernel(steps, share, ahead, pieces, after, act, og, wi, wo, lens, *refs):
     refs = refs[after:]
     outs, (buf, wibuf, wobuf, lenbuf, sem, wsem) = refs[:-6], refs[-6:]
     me = lax.axis_index("tensor")
@@ -56,10 +56,8 @@
         pltpu.make_async_copy(wo, wobuf, wsem.at[1]),
         pltpu.make_async_copy(lens, lenbuf, wsem.at[2]),
     ]
-    pieces = [(side, at) for side, ref in enumerate((act, og)) for at in range(0, ref.shape[2], piece)]
     copies = []
-    for slot, (side, at) in enumerate(pieces):
-        width = min(piece, (act, og)[side].shape[2] - at)
+    for slot, (side, at, width) in enumerate(pieces):
         copies.append(
             [
                 pltpu.make_async_copy(
@@ -79,7 +77,7 @@
             for copy in group:
                 copy.start()
     sums = [None, None]
-    for slot, (side, at) in enumerate(pieces):
+    for slot, (side, at, width) in enumerate(pieces):
         if at == 0:
             small[side].wait()
         for copy in copies[slot]:
@@ -87,8 +85,8 @@
         if slot + ahead < len(pieces):
             for copy in copies[slot + ahead]:
                 copy.start()
-        weight = (wibuf, wobuf)[side][:, at : at + piece]
-        token = buf[slot].reshape(tokens, piece)[:, : weight.shape[1]]
+        weight = (wibuf, wobuf)[side][:, at : at + width]
+        token = buf[slot].reshape(tokens, buf.shape[3])[:, :width]
         part = lax.dot_general(weight, token, NT, preferred_element_type=jnp.float32)
         sums[side] = part if sums[side] is None else sums[side] + part
     small[2].wait()
@@ -106,18 +104,20 @@
     count = len(steps) * share
     slots, feat, hidden = act.shape[1], act.shape[2], og.shape[2]
     rank = wi.shape[0]
-    pieces = -(-feat // piece) - (-hidden // piece)
-    return pl.pallas_call(
-        functools.partial(project_kernel, steps, share, ahead, piece, len(after)),
+    pieces = [(0, at, 256) for at in range(0, min(512, feat), 256)]
+    pieces += [(0, at, min(piece, feat - at)) for at in range(512, feat, piece)]
+    pieces += [(1, at, min(piece, hidden - at)) for at in range(0, hidden, piece)]
+    return pl.pallas_call(
+        functools.partial(project_kernel, steps, share, ahead, pieces, len(after)),
         out_shape=[jax.ShapeDtypeStruct((len(group) * share, 2 * rank, slots), jnp.float32) for group in groups],
         in_specs=[HBM] * 5 + [VMEM] * len(after),
         out_specs=[VMEM] * len(groups),
         scratch_shapes=[
-            pltpu.VMEM((pieces, count, slots, piece), act.dtype),
+            pltpu.VMEM((len(pieces), count, slots, piece), act.dtype),
             pltpu.VMEM((rank, feat), wi.dtype),
             pltpu.VMEM((rank, hidden), wo.dtype),
             pltpu.SMEM(lens.shape, lens.dtype),
-            pltpu.SemaphoreType.DMA((pieces, len(steps))),
+            pltpu.SemaphoreType.DMA((len(pieces), len(steps))),
             pltpu.SemaphoreType.DMA((3,)),
         ],
         compiler_params=pltpu.CompilerParams(vmem_limit_bytes=32 << 20),

time: 31.8 us -> 32 us (level)
    pallas_call x2, Pallas kernels: 10.6 us -> 11 us  [project(): pl.pallas_call(functools.partial(project_kernel, steps, share, ahead, pie...]
  transfers between devices with their start and end apart: 14 -> 14, of which waited for: 8 -> 8; matrix products, arithmetic and copies ran while one was open for 0% -> 0% of each run, Pallas kernels for 35% -> 36%
where the time goes in v23:
time: 32 us; the launch traced here: 31.8 us
  Pallas kernels  12.8 us (40%)
  starting transfers between devices  11.5 us (36%)
  waiting for transfers between devices  6.71 us (21%)
  other arithmetic  0.7 us (2%)
    pallas_call x2, Pallas kernels, project(): pl.pallas_call(functools.partial(project_kernel, steps, share, ahead, pie...  11 us
    ppermute x11, starting transfers between devices, xor_permute(): return lax.ppermute(value, axis, [(i, i ^ step) for i in range(size)])  6 us
    ppermute x3, starting transfers between devices, shift(): lax.ppermute(value, 'dp', [(i, (i + step) % groups) for i in range(groups)])  5.49 us
    ppermute x11, waiting for transfers between devices, xor_permute(): return lax.ppermute(value, axis, [(i, i ^ step) for i in range(size)])  3.99 us
    ppermute x3, waiting for transfers between devices, shift(): lax.ppermute(value, 'dp', [(i, (i + step) % groups) for i in range(groups)])  2.72 us
    pallas_call x1, Pallas kernels, cut_tests(): pl.pallas_call(cut_kernel, out_shape=jax.ShapeDtypeStruct((rows, width //...  0.96 us
  transfers between devices with their start and end apart: 14, of which 8 were waited for; matrix products, arithmetic and copies ran while one was open for 0% of the time, Pallas kernels for 36%

profile of v23, /device:TPU:0, one launch (start us, length us, event | category | flops | bytes accessed | tf_op | source)
XLA Modules:
  0.0 31.8 jit_solution(3998494223245305128)
XLA Ops:
  0.0 1.0 %shard_map.64.refs_0_.refs_4_ = bf16[128,1024]{1,0:T(8,128)(2,1)S(1)} custom-call(bf16[128,4096]{1,0:T(8,128)(2,1)} %tests.1), custom_call_target="tpu_custom_call" | custom-call | tf_op jit(solution)/shard_map/pallas_call | solution.py:32
  1.0 3.1 %collective-permute-start.1 = (bf16[128,1024]{1,0:T(8,128)(2,1)S(1)}, bf16[128,1024]{1,0:T(8,128)(2,1)S(1)}, u32[]{:S(2)}, u32[]{:S(2)}) collective-permute-start(bf16[128,1024]{1,0:T(8,128)(2,1)S(1)} %shard_map.64.refs_0_.refs_4_), channel_id=1, source_target_pairs={{0,4},{4,8},{8,12},{12,0},{1,5},{5,9},{9,13},{13,1},{2,6},{6,10},{... | collective-permute-start | bytes 786440 | tf_op jit(solution)/shard_map/ppermute | solution.py:197
  4.0 5.5 %shard_map.65 = (f32[2,128,256]{2,1,0:T(8,128)S(1)}, f32[2,128,256]{2,1,0:T(8,128)S(1)}) custom-call(bf16[8,256,1024]{2,1,0:T(8,128)(2,1)} %act.3, bf16[8,256,3584]{2,1,0:T(8,128)(2,1)} %og.3, bf16[64,1024]{1,0:T(8,128)(2,1)} %bitcast.6, bf16[64,3584]{1,0:T(8,128)(2,1)} %bitcast.4, s32[8]{0:T(128)} %lens.3, bf16[128,1024]{1,0:T(8,128)(2,1)S(1)} %shard_map.64.refs_0_.refs_4_), custom_call_target="tpu_custom_call" | custom-call | flops 4294967296 | bytes 16777216 | tf_op jit(solution)/shard_map/pallas_call | solution.py:110
  9.5 0.1 collective-permute-start
  9.6 2.1 %collective-permute-start.3 = (bf16[128,1024]{1,0:T(8,128)(2,1)S(1)}, bf16[128,1024]{1,0:T(8,128)(2,1)S(1)}, u32[]{:S(2)}, u32[]{:S(2)}) collective-permute-start(bf16[128,1024]{1,0:T(8,128)(2,1)S(1)} %shard_map.64.refs_0_.refs_4_), channel_id=1, source_target_pairs={{0,12},{4,0},{8,4},{12,8},{1,13},{5,1},{9,5},{13,9},{2,14},{6,2},{... | collective-permute-start | bytes 786440 | tf_op jit(solution)/shard_map/ppermute | solution.py:197
  11.7 0.7 %collective-permute-done.1.refs_5_ = bf16[128,1024]{1,0:T(8,128)(2,1)S(1)} collective-permute-done((bf16[128,1024]{1,0:T(8,128)(2,1)S(1)}, bf16[128,1024]{1,0:T(8,128)(2,1)S(1)}, u32[]{:S(2)}, u32[]{:S(2)}) %collective-permute-start.1) | collective-permute-done | bytes 262176 | tf_op jit(solution)/shard_map/ppermute | solution.py:197
  12.4 0.0 collective-permute-start.2
  12.4 1.6 %collective-permute-start.6 = (f32[2,128,256]{2,1,0:T(8,128)S(1)}, f32[2,128,256]{2,1,0:T(8,128)S(1)}, u32[]{:S(2)}, u32[]{:S(2)}) collective-permute-start(f32[2,128,256]{2,1,0:T(8,128)S(1)} %add.15.refs_0_), channel_id=1, source_target_pairs={{0,2},{1,3},{2,0},{3,1},{4,6},{5,7},{6,4},{7,5},{8,10},{9,11},{10,... | collective-permute-start | bytes 786440 | tf_op jit(solution)/shard_map/ppermute | solution.py:19
  14.0 0.3 collective-permute-start.10
  14.3 0.0 collective-permute-done.2.refs_1_
  14.3 5.5 %shard_map.66 = (f32[2,128,256]{2,1,0:T(8,128)S(1)}, f32[2,128,256]{2,1,0:T(8,128)S(1)}) custom-call(bf16[8,256,1024]{2,1,0:T(8,128)(2,1)} %act.3, bf16[8,256,3584]{2,1,0:T(8,128)(2,1)} %og.3, bf16[64,1024]{1,0:T(8,128)(2,1)} %bitcast.7, bf16[64,3584]{1,0:T(8,128)(2,1)} %bitcast.5, s32[8]{0:T(128)} %lens.3, f32[2,128,256]{2,1,0:T(8,128)S(1)} %add.15.refs_0_, ...), custom_call_target="tpu_custom_call" | custom-call | flops 1024 | bytes 4 | tf_op jit(solution)/shard_map/pallas_call | solution.py:110
  19.8 0.0 collective-permute-done.3.refs_6_
  19.8 0.1 collective-permute-start.4
  19.9 0.5 %collective-permute-start.5 = (f32[1,128,256]{2,1,0:T(8,128)S(1)}, f32[1,128,256]{2,1,0:T(8,128)S(1)}, u32[]{:S(2)}, u32[]{:S(2)}) collective-permute-start(f32[1,128,256]{2,1,0:T(8,128)S(1)} %get-tuple-element.22), channel_id=1, source_target_pairs={{0,1},{1,0},{2,3},{3,2},{4,5},{5,4},{6,7},{7,6},{8,9},{9,8},{10,11... | collective-permute-start | bytes 393224 | tf_op jit(solution)/shard_map/ppermute | solution.py:19
  20.4 0.8 %collective-permute-done.4 = f32[1,128,256]{2,1,0:T(8,128)S(1)} collective-permute-done((f32[1,128,256]{2,1,0:T(8,128)S(1)}, f32[1,128,256]{2,1,0:T(8,128)S(1)}, u32[]{:S(2)}, u32[]{:S(2)}) %collective-permute-start.4) | collective-permute-done | bytes 131104 | tf_op jit(solution)/shard_map/ppermute | solution.py:19
  21.2 0.2 collective-permute-done.5
  21.5 0.0 collective-permute-done.6.refs_2_
  21.5 0.5 %shard_map.67 = (f32[2,8,128]{2,1,0:T(8,128)S(1)}, f32[2,8,128]{2,1,0:T(8,128)S(1)}, f32[2,8,128]{2,1,0:T(8,128)S(1)}, f32[2,8,128]{2,1,0:T(8,128)S(1)}) custom-call(f32[2,128,256]{2,1,0:T(8,128)S(1)} %get-tuple-element.15.refs_0_, f32[2,128,256]{2,1,0:T(8,128)S(1)} %pad_maximum_fusion.refs_1_, f32[2,128,256]{2,1,0:T(8,128)S(1)} %collective-permute-done.6.refs_2_), custom_call_target="tpu_custom_call" | custom-call | tf_op jit(solution)/shard_map/pallas_call | solution.py:157
  22.0 0.4 %collective-permute-start.7 = (f32[2,8,128]{2,1,0:T(8,128)S(1)}, f32[2,8,128]{2,1,0:T(8,128)S(1)}, u32[]{:S(2)}, u32[]{:S(2)}) collective-permute-start(f32[2,8,128]{2,1,0:T(8,128)S(1)} %get-tuple-element.18), channel_id=1, source_target_pairs={{0,1},{1,0},{2,3},{3,2},{4,5},{5,4},{6,7},{7,6},{8,9},{9,8},{10,11... | collective-permute-start | bytes 24584 | tf_op jit(solution)/shard_map/ppermute | solution.py:19
  22.4 1.0 %collective-permute-start.8 = (f32[2,8,128]{2,1,0:T(8,128)S(1)}, f32[2,8,128]{2,1,0:T(8,128)S(1)}, u32[]{:S(2)}, u32[]{:S(2)}) collective-permute-start(f32[2,8,128]{2,1,0:T(8,128)S(1)} %get-tuple-element.19), channel_id=1, source_target_pairs={{0,2},{1,3},{2,0},{3,1},{4,6},{5,7},{6,4},{7,5},{8,10},{9,11},{10,... | collective-permute-start | bytes 24584 | tf_op jit(solution)/shard_map/ppermute | solution.py:19
  23.4 0.6 %collective-permute-start.9 = (f32[2,8,128]{2,1,0:T(8,128)S(1)}, f32[2,8,128]{2,1,0:T(8,128)S(1)}, u32[]{:S(2)}, u32[]{:S(2)}) collective-permute-start(f32[2,8,128]{2,1,0:T(8,128)S(1)} %get-tuple-element.20), channel_id=1, source_target_pairs={{0,3},{1,2},{2,1},{3,0},{4,7},{5,6},{6,5},{7,4},{8,11},{9,10},{10,... | collective-permute-start | bytes 24584 | tf_op jit(solution)/shard_map/ppermute | solution.py:19
  23.9 2.0 %collective-permute-done.10.refs_7_ = bf16[128,1024]{1,0:T(8,128)(2,1)S(1)} collective-permute-done((bf16[128,1024]{1,0:T(8,128)(2,1)S(1)}, bf16[128,1024]{1,0:T(8,128)(2,1)S(1)}, u32[]{:S(2)}, u32[]{:S(2)}) %collective-permute-start.10) | collective-permute-done | bytes 262176 | tf_op jit(solution)/shard_map/ppermute | solution.py:197
  26.0 0.1 collective-permute-done.8.refs_2_
  26.0 0.4 %collective-permute-done.9.refs_3_ = f32[2,8,128]{2,1,0:T(8,128)S(1)} collective-permute-done((f32[2,8,128]{2,1,0:T(8,128)S(1)}, f32[2,8,128]{2,1,0:T(8,128)S(1)}, u32[]{:S(2)}, u32[]{:S(2)}) %collective-permute-start.9) | collective-permute-done | bytes 8224 | tf_op jit(solution)/shard_map/ppermute | solution.py:19
  26.4 0.4 %shard_map.68 = f32[8,512]{1,0:T(8,128)S(1)} custom-call(f32[2,8,128]{2,1,0:T(8,128)S(1)} %get-tuple-element.17.refs_0_, f32[2,8,128]{2,1,0:T(8,128)S(1)} %collective-permute-done.7.refs_1_, f32[2,8,128]{2,1,0:T(8,128)S(1)} %collective-permute-done.8.refs_2_, f32[2,8,128]{2,1,0:T(8,128)S(1)} %collective-permute-done.9.refs_3_, ...), custom_call_target="tpu_custom_call" | custom-call | tf_op jit(solution)/shard_map/pallas_call | solution.py:185
  26.8 0.2 collective-permute-start.11
  27.0 1.0 %collective-permute-start.12 = (f32[8,512]{1,0:T(8,128)S(1)}, f32[8,512]{1,0:T(8,128)S(1)}, u32[]{:S(2)}, u32[]{:S(2)}) collective-permute-start(f32[8,512]{1,0:T(8,128)S(1)} %shard_map.68), channel_id=1, source_target_pairs={{0,2},{1,3},{2,0},{3,1},{4,6},{5,7},{6,4},{7,5},{8,10},{9,11},{10,... | collective-permute-start | bytes 49160 | tf_op jit(solution)/shard_map/ppermute | solution.py:19
  28.0 0.7 %collective-permute-start.13 = (f32[8,512]{1,0:T(8,128)S(1)}, f32[8,512]{1,0:T(8,128)S(1)}, u32[]{:S(2)}, u32[]{:S(2)}) collective-permute-start(f32[8,512]{1,0:T(8,128)S(1)} %shard_map.68), channel_id=1, source_target_pairs={{0,3},{1,2},{2,1},{3,0},{4,7},{5,6},{6,5},{7,4},{8,11},{9,10},{10,... | collective-permute-start | bytes 49160 | tf_op jit(solution)/shard_map/ppermute | solution.py:19
  28.7 0.0 collective-permute-done.11
  28.7 2.0 %collective-permute-done.12 = f32[8,512]{1,0:T(8,128)S(1)} collective-permute-done((f32[8,512]{1,0:T(8,128)S(1)}, f32[8,512]{1,0:T(8,128)S(1)}, u32[]{:S(2)}, u32[]{:S(2)}) %collective-permute-start.12) | collective-permute-done | bytes 16416 | tf_op jit(solution)/shard_map/ppermute | solution.py:19
  30.7 0.4 %collective-permute-done.13 = f32[8,512]{1,0:T(8,128)S(1)} collective-permute-done((f32[8,512]{1,0:T(8,128)S(1)}, f32[8,512]{1,0:T(8,128)S(1)}, u32[]{:S(2)}, u32[]{:S(2)}) %collective-permute-start.13) | collective-permute-done | bytes 16416 | tf_op jit(solution)/shard_map/ppermute | solution.py:19
  31.2 0.6 %add_add_fusion = f32[8,512]{1,0:T(8,128)} fusion(f32[8,512]{1,0:T(8,128)S(1)} %collective-permute-done.12, f32[8,512]{1,0:T(8,128)S(1)} %collective-permute-done.13, f32[8,512]{1,0:T(8,128)S(1)} %shard_map.68, f32[8,512]{1,0:T(8,128)S(1)} %collective-permute-done.11), kind=kLoop, calls=%fused_computation.2 | loop fusion | flops 12288 | bytes 81920 | tf_op jit(solution)/shard_map/add | solution.py:228
  (6 shorter events, 0.1 us)
Async XLA Ops:
  1.0 11.4 %collective-permute-start.1 = (bf16[128,1024]{1,0:T(8,128)(2,1)S(1)}, bf16[128,1024]{1,0:T(8,128)(2,1)S(1)}, u32[]{:S(2)}, u32[]{:S(2)}) collective-permute-start(bf16[128,1024]{1,0:T(8,128)(2,1)S(1)} %shard_map.64.refs_0_.refs_4_), channel_id=1, source_target_pairs={{0,4},{4,8},{8,12},{12,0},{1,5},{5,9},{9,13},{13,1},{2,6},{6,10},{... | collective-permute-start | bytes 786440 | tf_op jit(solution)/shard_map/ppermute | solution.py:197
  9.5 2.9 %collective-permute-start = (f32[2,128,256]{2,1,0:T(8,128)S(1)}, f32[2,128,256]{2,1,0:T(8,128)S(1)}, u32[]{:S(2)}, u32[]{:S(2)}) collective-permute-start(f32[2,128,256]{2,1,0:T(8,128)S(1)} %get-tuple-element.14), channel_id=1, source_target_pairs={{0,1},{1,0},{2,3},{3,2},{4,5},{5,4},{6,7},{7,6},{8,9},{9,8},{10,11... | collective-permute-start | bytes 786440 | tf_op jit(solution)/shard_map/ppermute | solution.py:19
  9.6 10.2 %collective-permute-start.3 = (bf16[128,1024]{1,0:T(8,128)(2,1)S(1)}, bf16[128,1024]{1,0:T(8,128)(2,1)S(1)}, u32[]{:S(2)}, u32[]{:S(2)}) collective-permute-start(bf16[128,1024]{1,0:T(8,128)(2,1)S(1)} %shard_map.64.refs_0_.refs_4_), channel_id=1, source_target_pairs={{0,12},{4,0},{8,4},{12,8},{1,13},{5,1},{9,5},{13,9},{2,14},{6,2},{... | collective-permute-start | bytes 786440 | tf_op jit(solution)/shard_map/ppermute | solution.py:197
  12.4 1.9 %collective-permute-start.2 = (bf16[16,128]{1,0:T(8,128)(2,1)S(1)}, bf16[16,128]{1,0:T(8,128)(2,1)S(1)}, u32[]{:S(2)}, u32[]{:S(2)}) collective-permute-start(bf16[16,128]{1,0:T(8,128)(2,1)S(1)} %slice.16), channel_id=1, source_target_pairs={{0,1},{1,0},{2,3},{3,2},{4,5},{5,4},{6,7},{7,6},{8,9},{9,8},{10,11... | collective-permute-start | bytes 12296 | tf_op jit(solution)/shard_map/ppermute | solution.py:19
  12.4 9.0 %collective-permute-start.6 = (f32[2,128,256]{2,1,0:T(8,128)S(1)}, f32[2,128,256]{2,1,0:T(8,128)S(1)}, u32[]{:S(2)}, u32[]{:S(2)}) collective-permute-start(f32[2,128,256]{2,1,0:T(8,128)S(1)} %add.15.refs_0_), channel_id=1, source_target_pairs={{0,2},{1,3},{2,0},{3,1},{4,6},{5,7},{6,4},{7,5},{8,10},{9,11},{10,... | collective-permute-start | bytes 786440 | tf_op jit(solution)/shard_map/ppermute | solution.py:19
  14.0 12.0 %collective-permute-start.10 = (bf16[128,1024]{1,0:T(8,128)(2,1)S(1)}, bf16[128,1024]{1,0:T(8,128)(2,1)S(1)}, u32[]{:S(2)}, u32[]{:S(2)}) collective-permute-start(bf16[128,1024]{1,0:T(8,128)(2,1)S(1)} %collective-permute-done.1.refs_5_), channel_id=1, source_target_pairs={{0,4},{4,8},{8,12},{12,0},{1,5},{5,9},{9,13},{13,1},{2,6},{6,10},{... | collective-permute-start | bytes 786440 | tf_op jit(solution)/shard_map/ppermute | solution.py:197
  19.8 1.4 %collective-permute-start.4 = (f32[1,128,256]{2,1,0:T(8,128)S(1)}, f32[1,128,256]{2,1,0:T(8,128)S(1)}, u32[]{:S(2)}, u32[]{:S(2)}) collective-permute-start(f32[1,128,256]{2,1,0:T(8,128)S(1)} %get-tuple-element.21), channel_id=1, source_target_pairs={{0,1},{1,0},{2,3},{3,2},{4,5},{5,4},{6,7},{7,6},{8,9},{9,8},{10,11... | collective-permute-start | bytes 393224 | tf_op jit(solution)/shard_map/ppermute | solution.py:19
  19.9 1.5 %collective-permute-start.5 = (f32[1,128,256]{2,1,0:T(8,128)S(1)}, f32[1,128,256]{2,1,0:T(8,128)S(1)}, u32[]{:S(2)}, u32[]{:S(2)}) collective-permute-start(f32[1,128,256]{2,1,0:T(8,128)S(1)} %get-tuple-element.22), channel_id=1, source_target_pairs={{0,1},{1,0},{2,3},{3,2},{4,5},{5,4},{6,7},{7,6},{8,9},{9,8},{10,11... | collective-permute-start | bytes 393224 | tf_op jit(solution)/shard_map/ppermute | solution.py:19
  22.0 4.0 %collective-permute-start.7 = (f32[2,8,128]{2,1,0:T(8,128)S(1)}, f32[2,8,128]{2,1,0:T(8,128)S(1)}, u32[]{:S(2)}, u32[]{:S(2)}) collective-permute-start(f32[2,8,128]{2,1,0:T(8,128)S(1)} %get-tuple-element.18), channel_id=1, source_target_pairs={{0,1},{1,0},{2,3},{3,2},{4,5},{5,4},{6,7},{7,6},{8,9},{9,8},{10,11... | collective-permute-start | bytes 24584 | tf_op jit(solution)/shard_map/ppermute | solution.py:19
  22.4 3.7 %collective-permute-start.8 = (f32[2,8,128]{2,1,0:T(8,128)S(1)}, f32[2,8,128]{2,1,0:T(8,128)S(1)}, u32[]{:S(2)}, u32[]{:S(2)}) collective-permute-start(f32[2,8,128]{2,1,0:T(8,128)S(1)} %get-tuple-element.19), channel_id=1, source_target_pairs={{0,2},{1,3},{2,0},{3,1},{4,6},{5,7},{6,4},{7,5},{8,10},{9,11},{10,... | collective-permute-start | bytes 24584 | tf_op jit(solution)/shard_map/ppermute | solution.py:19
  23.4 3.1 %collective-permute-start.9 = (f32[2,8,128]{2,1,0:T(8,128)S(1)}, f32[2,8,128]{2,1,0:T(8,128)S(1)}, u32[]{:S(2)}, u32[]{:S(2)}) collective-permute-start(f32[2,8,128]{2,1,0:T(8,128)S(1)} %get-tuple-element.20), channel_id=1, source_target_pairs={{0,3},{1,2},{2,1},{3,0},{4,7},{5,6},{6,5},{7,4},{8,11},{9,10},{10,... | collective-permute-start | bytes 24584 | tf_op jit(solution)/shard_map/ppermute | solution.py:19
  26.8 1.9 %collective-permute-start.11 = (f32[8,512]{1,0:T(8,128)S(1)}, f32[8,512]{1,0:T(8,128)S(1)}, u32[]{:S(2)}, u32[]{:S(2)}) collective-permute-start(f32[8,512]{1,0:T(8,128)S(1)} %shard_map.68), channel_id=1, source_target_pairs={{0,1},{1,0},{2,3},{3,2},{4,5},{5,4},{6,7},{7,6},{8,9},{9,8},{10,11... | collective-permute-start | bytes 49160 | tf_op jit(solution)/shard_map/ppermute | solution.py:19
  27.0 3.7 %collective-permute-start.12 = (f32[8,512]{1,0:T(8,128)S(1)}, f32[8,512]{1,0:T(8,128)S(1)}, u32[]{:S(2)}, u32[]{:S(2)}) collective-permute-start(f32[8,512]{1,0:T(8,128)S(1)} %shard_map.68), channel_id=1, source_target_pairs={{0,2},{1,3},{2,0},{3,1},{4,6},{5,7},{6,4},{7,5},{8,10},{9,11},{10,... | collective-permute-start | bytes 49160 | tf_op jit(solution)/shard_map/ppermute | solution.py:19
  28.0 3.2 %collective-permute-start.13 = (f32[8,512]{1,0:T(8,128)S(1)}, f32[8,512]{1,0:T(8,128)S(1)}, u32[]{:S(2)}, u32[]{:S(2)}) collective-permute-start(f32[8,512]{1,0:T(8,128)S(1)} %shard_map.68), channel_id=1, source_target_pairs={{0,3},{1,2},{2,1},{3,0},{4,7},{5,6},{6,5},{7,4},{8,11},{9,10},{10,... | collective-permute-start | bytes 49160 | tf_op jit(solution)/shard_map/ppermute | solution.py:19

commit v24 on v19

--- a/solution.py
+++ b/solution.py
@@ -147,9 +147,9 @@
         scale = jnp.sqrt(jnp.sum(flat * flat) / (rank * rank) + 1e-06)
         unit = flat / scale
         for to in range(size):
-            held[to] = unit[to * span : (to + 1) * span]
+            held[k, to] = unit[to * span : (to + 1) * span]
         for step in range(size):
-            outs[step][k] = held[me ^ step]
+            outs[step][k] = held[k, me ^ step]
 
 
 def units(parts, share, rank, size):
@@ -159,17 +159,17 @@
         out_shape=[jax.ShapeDtypeStruct((share, span, 128), jnp.float32)] * size,
         in_specs=[VMEM] * len(parts),
         out_specs=[VMEM] * size,
-        scratch_shapes=[pltpu.VMEM((share, rank, rank), jnp.float32), pltpu.VMEM((size, span, 128), jnp.float32)],
+        scratch_shapes=[pltpu.VMEM((share, rank, rank), jnp.float32), pltpu.VMEM((share, size, span, 128), jnp.float32)],
         compiler_params=SMALL,
     )(*parts)
 
 
-def score_kernel(share, size, origins, *refs):
-    unit_refs, test_refs, out, held = refs[:size], refs[size:-2], refs[-2], refs[-1]
+def score_kernel(share, steps, origins, *refs):
+    unit_refs, test_refs, out, held = refs[: len(steps)], refs[len(steps) : -2], refs[-2], refs[-1]
     me, dp = lax.axis_index("tensor"), lax.axis_index("dp")
-    for step in range(size):
+    for step, unit_ref in zip(steps, unit_refs):
         for k in range(share):
-            held[(me ^ step) * share + k] = unit_refs[step][k]
+            held[(me ^ step) * share + k] = unit_ref[k]
     unit = jnp.concatenate([held[:, c, :] for c in range(held.shape[1])], axis=1).astype(jnp.bfloat16)
     tests = test_refs[0].shape[0]
     for (factor, offset, modulus), test_ref in zip(origins, test_refs):
@@ -183,13 +183,13 @@
     tests, width = test_parts[0][0].shape
     origins = [origin for _, *origin in test_parts]
     return pl.pallas_call(
-        functools.partial(score_kernel, share, size, origins),
+        functools.partial(score_kernel, share, tuple(unit_parts), origins),
         out_shape=jax.ShapeDtypeStruct((share * size, tests * groups), jnp.float32),
         in_specs=[VMEM] * (size + groups),
         out_specs=VMEM,
         scratch_shapes=[pltpu.VMEM((share * size, width // 128, 128), jnp.float32)],
         compiler_params=SMALL,
-    )(*unit_parts, *(shard for shard, *_ in test_parts))
+    )(*unit_parts.values(), *(shard for shard, *_ in test_parts))
 
 
 def gather_tests(own, groups):
@@ -200,6 +200,10 @@
         first = shift(own, 1)
         return [(own, 1, 0, 4), (first, 1, 3, 4), (shift(own, -1), 1, 1, 4), (shift(first, 1), 1, 2, 4)]
     return [(own, 1, 0, groups)] + [(shift(own, step), 1, groups - step, groups) for step in range(1, groups)]
+
+
+def exchange(outs, size):
+    return {step: xor_permute(outs[step], "tensor", size, step) for step in [*range(2, size), 1]} | {0: outs[0]}
 
 
 def shards(size, groups, activations, out_grads, proj_in, proj_out, lengths, test_grads):
@@ -221,9 +225,10 @@
     arrived = jnp.concatenate([xor_permute(one, "tensor", size, 1) for one in pieces])
 
     unit_outs = units([near_own, arrived] + sums, share, rank, size)
-    unit_parts = [unit_outs[0]] + [xor_permute(unit_outs[step], "tensor", size, step) for step in range(1, size)]
+    unit_parts = exchange(unit_outs, size)
     part = score(unit_parts, tests, share)
-    parts = [part] + [xor_permute(part, "tensor", size, step) for step in range(1, size)]
+    parts = exchange([part] * size, size)
+    parts = [parts[step ^ (size - 2)] for step in range(size)]
     while len(parts) > 1:
         parts = [parts[i] + parts[i + 1] for i in range(0, len(parts), 2)]
     return parts[0]

time: 31.8 us -> 31.7 us (level)
  waiting for transfers between devices: 6.99 us -> 6.34 us
  starting transfers between devices: 11.3 us -> 11.9 us
    ppermute x11, starting transfers between devices: 6.01 us -> 6.57 us  [xor_permute(): return lax.ppermute(value, axis, [(i, i ^ step) for i in range(size)])]
    ppermute x11, waiting for transfers between devices: 4.02 us -> 3.65 us  [xor_permute(): return lax.ppermute(value, axis, [(i, i ^ step) for i in range(size)])]
where the time goes in v24:
time: 31.7 us; the launch traced here: 31.5 us
  Pallas kernels  12.5 us (39%)
  starting transfers between devices  11.9 us (38%)
  waiting for transfers between devices  6.34 us (20%)
  other arithmetic  0.7 us (2%)
    pallas_call x2, Pallas kernels, project(): pl.pallas_call(functools.partial(project_kernel, steps, share, ahead, pie...  10.6 us
    ppermute x11, starting transfers between devices, xor_permute(): return lax.ppermute(value, axis, [(i, i ^ step) for i in range(size)])  6.57 us
    ppermute x3, starting transfers between devices, shift(): lax.ppermute(value, 'dp', [(i, (i + step) % groups) for i in range(groups)])  5.33 us
    ppermute x11, waiting for transfers between devices, xor_permute(): return lax.ppermute(value, axis, [(i, i ^ step) for i in range(size)])  3.65 us
    ppermute x3, waiting for transfers between devices, shift(): lax.ppermute(value, 'dp', [(i, (i + step) % groups) for i in range(groups)])  2.69 us
    pallas_call x1, Pallas kernels, cut_tests(): pl.pallas_call(cut_kernel, out_shape=jax.ShapeDtypeStruct((rows, width //...  0.96 us
  transfers between devices with their start and end apart: 14, of which 8 were waited for; matrix products, arithmetic and copies ran while one was open for 0% of the time, Pallas kernels for 35%

profile of v24, /device:TPU:0, one launch (start us, length us, event | category | flops | bytes accessed | tf_op | source)
XLA Modules:
  0.0 31.5 jit_solution(4024906133115777901)
XLA Ops:
  0.0 1.0 %shard_map.64.refs_0_.refs_4_ = bf16[128,1024]{1,0:T(8,128)(2,1)S(1)} custom-call(bf16[128,4096]{1,0:T(8,128)(2,1)} %tests.1), custom_call_target="tpu_custom_call" | custom-call | tf_op jit(solution)/shard_map/pallas_call | solution.py:32
  1.0 3.1 %collective-permute-start.1 = (bf16[128,1024]{1,0:T(8,128)(2,1)S(1)}, bf16[128,1024]{1,0:T(8,128)(2,1)S(1)}, u32[]{:S(2)}, u32[]{:S(2)}) collective-permute-start(bf16[128,1024]{1,0:T(8,128)(2,1)S(1)} %shard_map.64.refs_0_.refs_4_), channel_id=1, source_target_pairs={{0,4},{4,8},{8,12},{12,0},{1,5},{5,9},{9,13},{13,1},{2,6},{6,10},{... | collective-permute-start | bytes 786440 | tf_op jit(solution)/shard_map/ppermute | solution.py:197
  4.0 5.3 %shard_map.65 = (f32[2,128,256]{2,1,0:T(8,128)S(1)}, f32[2,128,256]{2,1,0:T(8,128)S(1)}) custom-call(bf16[8,256,1024]{2,1,0:T(8,128)(2,1)} %act.3, bf16[8,256,3584]{2,1,0:T(8,128)(2,1)} %og.3, bf16[64,1024]{1,0:T(8,128)(2,1)} %bitcast.6, bf16[64,3584]{1,0:T(8,128)(2,1)} %bitcast.4, s32[8]{0:T(128)} %lens.3, bf16[128,1024]{1,0:T(8,128)(2,1)S(1)} %shard_map.64.refs_0_.refs_4_), custom_call_target="tpu_custom_call" | custom-call | flops 4294967296 | bytes 16777216 | tf_op jit(solution)/shard_map/pallas_call | solution.py:110
  9.4 0.1 collective-permute-start
  9.4 2.1 %collective-permute-start.3 = (bf16[128,1024]{1,0:T(8,128)(2,1)S(1)}, bf16[128,1024]{1,0:T(8,128)(2,1)S(1)}, u32[]{:S(2)}, u32[]{:S(2)}) collective-permute-start(bf16[128,1024]{1,0:T(8,128)(2,1)S(1)} %shard_map.64.refs_0_.refs_4_), channel_id=1, source_target_pairs={{0,12},{4,0},{8,4},{12,8},{1,13},{5,1},{9,5},{13,9},{2,14},{6,2},{... | collective-permute-start | bytes 786440 | tf_op jit(solution)/shard_map/ppermute | solution.py:197
  11.5 0.8 %collective-permute-done.1.refs_5_ = bf16[128,1024]{1,0:T(8,128)(2,1)S(1)} collective-permute-done((bf16[128,1024]{1,0:T(8,128)(2,1)S(1)}, bf16[128,1024]{1,0:T(8,128)(2,1)S(1)}, u32[]{:S(2)}, u32[]{:S(2)}) %collective-permute-start.1) | collective-permute-done | bytes 262176 | tf_op jit(solution)/shard_map/ppermute | solution.py:197
  12.4 0.0 collective-permute-start.2
  12.4 0.0 collective-permute-done
  12.4 1.6 %collective-permute-start.6 = (f32[2,128,256]{2,1,0:T(8,128)S(1)}, f32[2,128,256]{2,1,0:T(8,128)S(1)}, u32[]{:S(2)}, u32[]{:S(2)}) collective-permute-start(f32[2,128,256]{2,1,0:T(8,128)S(1)} %add.15.refs_0_), channel_id=1, source_target_pairs={{0,2},{1,3},{2,0},{3,1},{4,6},{5,7},{6,4},{7,5},{8,10},{9,11},{10,... | collective-permute-start | bytes 786440 | tf_op jit(solution)/shard_map/ppermute | solution.py:19
  14.0 0.2 collective-permute-start.10
  14.1 0.0 collective-permute-done.2.refs_1_
  14.1 5.3 %shard_map.66 = (f32[2,128,256]{2,1,0:T(8,128)S(1)}, f32[2,128,256]{2,1,0:T(8,128)S(1)}) custom-call(bf16[8,256,1024]{2,1,0:T(8,128)(2,1)} %act.3, bf16[8,256,3584]{2,1,0:T(8,128)(2,1)} %og.3, bf16[64,1024]{1,0:T(8,128)(2,1)} %bitcast.7, bf16[64,3584]{1,0:T(8,128)(2,1)} %bitcast.5, s32[8]{0:T(128)} %lens.3, f32[2,128,256]{2,1,0:T(8,128)S(1)} %add.15.refs_0_, ...), custom_call_target="tpu_custom_call" | custom-call | flops 1024 | bytes 4 | tf_op jit(solution)/shard_map/pallas_call | solution.py:110
  19.5 0.0 collective-permute-done.3.refs_6_
  19.5 0.1 collective-permute-start.4
  19.6 0.4 %collective-permute-start.5 = (f32[1,128,256]{2,1,0:T(8,128)S(1)}, f32[1,128,256]{2,1,0:T(8,128)S(1)}, u32[]{:S(2)}, u32[]{:S(2)}) collective-permute-start(f32[1,128,256]{2,1,0:T(8,128)S(1)} %get-tuple-element.22), channel_id=1, source_target_pairs={{0,1},{1,0},{2,3},{3,2},{4,5},{5,4},{6,7},{7,6},{8,9},{9,8},{10,11... | collective-permute-start | bytes 393224 | tf_op jit(solution)/shard_map/ppermute | solution.py:19
  20.1 0.8 %collective-permute-done.4 = f32[1,128,256]{2,1,0:T(8,128)S(1)} collective-permute-done((f32[1,128,256]{2,1,0:T(8,128)S(1)}, f32[1,128,256]{2,1,0:T(8,128)S(1)}, u32[]{:S(2)}, u32[]{:S(2)}) %collective-permute-start.4) | collective-permute-done | bytes 131104 | tf_op jit(solution)/shard_map/ppermute | solution.py:19
  20.9 0.2 collective-permute-done.5
  21.1 0.1 collective-permute-done.6.refs_2_
  21.2 0.5 %shard_map.67 = (f32[2,8,128]{2,1,0:T(8,128)S(1)}, f32[2,8,128]{2,1,0:T(8,128)S(1)}, f32[2,8,128]{2,1,0:T(8,128)S(1)}, f32[2,8,128]{2,1,0:T(8,128)S(1)}) custom-call(f32[2,128,256]{2,1,0:T(8,128)S(1)} %get-tuple-element.15.refs_0_, f32[2,128,256]{2,1,0:T(8,128)S(1)} %pad_maximum_fusion.refs_1_, f32[2,128,256]{2,1,0:T(8,128)S(1)} %collective-permute-done.6.refs_2_), custom_call_target="tpu_custom_call" | custom-call | tf_op jit(solution)/shard_map/pallas_call | solution.py:157
  21.7 1.6 %collective-permute-start.7 = (f32[2,8,128]{2,1,0:T(8,128)S(1)}, f32[2,8,128]{2,1,0:T(8,128)S(1)}, u32[]{:S(2)}, u32[]{:S(2)}) collective-permute-start(f32[2,8,128]{2,1,0:T(8,128)S(1)} %get-tuple-element.17), channel_id=1, source_target_pairs={{0,2},{1,3},{2,0},{3,1},{4,6},{5,7},{6,4},{7,5},{8,10},{9,11},{10,... | collective-permute-start | bytes 24584 | tf_op jit(solution)/shard_map/ppermute | solution.py:19
  23.3 0.1 collective-permute-start.8
  23.4 0.5 %collective-permute-start.9 = (f32[2,8,128]{2,1,0:T(8,128)S(1)}, f32[2,8,128]{2,1,0:T(8,128)S(1)}, u32[]{:S(2)}, u32[]{:S(2)}) collective-permute-start(f32[2,8,128]{2,1,0:T(8,128)S(1)} %get-tuple-element.19), channel_id=1, source_target_pairs={{0,1},{1,0},{2,3},{3,2},{4,5},{5,4},{6,7},{7,6},{8,9},{9,8},{10,11... | collective-permute-start | bytes 24584 | tf_op jit(solution)/shard_map/ppermute | solution.py:19
  23.9 1.9 %collective-permute-done.10.refs_7_ = bf16[128,1024]{1,0:T(8,128)(2,1)S(1)} collective-permute-done((bf16[128,1024]{1,0:T(8,128)(2,1)S(1)}, bf16[128,1024]{1,0:T(8,128)(2,1)S(1)}, u32[]{:S(2)}, u32[]{:S(2)}) %collective-permute-start.10) | collective-permute-done | bytes 262176 | tf_op jit(solution)/shard_map/ppermute | solution.py:197
  25.8 0.0 collective-permute-done.7.refs_0_
  25.8 0.6 %collective-permute-done.8.refs_1_ = f32[2,8,128]{2,1,0:T(8,128)S(1)} collective-permute-done((f32[2,8,128]{2,1,0:T(8,128)S(1)}, f32[2,8,128]{2,1,0:T(8,128)S(1)}, u32[]{:S(2)}, u32[]{:S(2)}) %collective-permute-start.8) | collective-permute-done | bytes 8224 | tf_op jit(solution)/shard_map/ppermute | solution.py:19
  26.4 0.0 collective-permute-done.9.refs_2_
  26.4 0.4 %shard_map.68 = f32[8,512]{1,0:T(8,128)S(1)} custom-call(f32[2,8,128]{2,1,0:T(8,128)S(1)} %collective-permute-done.7.refs_0_, f32[2,8,128]{2,1,0:T(8,128)S(1)} %collective-permute-done.8.refs_1_, f32[2,8,128]{2,1,0:T(8,128)S(1)} %collective-permute-done.9.refs_2_, f32[2,8,128]{2,1,0:T(8,128)S(1)} %get-tuple-element.20.refs_3_, ...), custom_call_target="tpu_custom_call" | custom-call | tf_op jit(solution)/shard_map/pallas_call | solution.py:185
  26.7 1.0 %collective-permute-start.11 = (f32[8,512]{1,0:T(8,128)S(1)}, f32[8,512]{1,0:T(8,128)S(1)}, u32[]{:S(2)}, u32[]{:S(2)}) collective-permute-start(f32[8,512]{1,0:T(8,128)S(1)} %shard_map.68), channel_id=1, source_target_pairs={{0,2},{1,3},{2,0},{3,1},{4,6},{5,7},{6,4},{7,5},{8,10},{9,11},{10,... | collective-permute-start | bytes 49160 | tf_op jit(solution)/shard_map/ppermute | solution.py:19
  27.7 1.2 %collective-permute-start.13 = (f32[8,512]{1,0:T(8,128)S(1)}, f32[8,512]{1,0:T(8,128)S(1)}, u32[]{:S(2)}, u32[]{:S(2)}) collective-permute-start(f32[8,512]{1,0:T(8,128)S(1)} %shard_map.68), channel_id=1, source_target_pairs={{0,1},{1,0},{2,3},{3,2},{4,5},{5,4},{6,7},{7,6},{8,9},{9,8},{10,11... | collective-permute-start | bytes 49160 | tf_op jit(solution)/shard_map/ppermute | solution.py:19
  28.9 1.6 %collective-permute-done.11 = f32[8,512]{1,0:T(8,128)S(1)} collective-permute-done((f32[8,512]{1,0:T(8,128)S(1)}, f32[8,512]{1,0:T(8,128)S(1)}, u32[]{:S(2)}, u32[]{:S(2)}) %collective-permute-start.11) | collective-permute-done | bytes 16416 | tf_op jit(solution)/shard_map/ppermute | solution.py:19
  30.5 0.4 %collective-permute-done.12 = f32[8,512]{1,0:T(8,128)S(1)} collective-permute-done((f32[8,512]{1,0:T(8,128)S(1)}, f32[8,512]{1,0:T(8,128)S(1)}, u32[]{:S(2)}, u32[]{:S(2)}) %collective-permute-start.12) | collective-permute-done | bytes 16416 | tf_op jit(solution)/shard_map/ppermute | solution.py:19
  30.9 0.6 %add_add_fusion = f32[8,512]{1,0:T(8,128)} fusion(f32[8,512]{1,0:T(8,128)S(1)} %shard_map.68, f32[8,512]{1,0:T(8,128)S(1)} %collective-permute-done.13, f32[8,512]{1,0:T(8,128)S(1)} %collective-permute-done.11, f32[8,512]{1,0:T(8,128)S(1)} %collective-permute-done.12), kind=kLoop, calls=%fused_computation.2 | loop fusion | flops 12288 | bytes 81920 | tf_op jit(solution)/shard_map/add | solution.py:233
  (6 shorter events, 0.1 us)
Async XLA Ops:
  1.0 11.4 %collective-permute-start.1 = (bf16[128,1024]{1,0:T(8,128)(2,1)S(1)}, bf16[128,1024]{1,0:T(8,128)(2,1)S(1)}, u32[]{:S(2)}, u32[]{:S(2)}) collective-permute-start(bf16[128,1024]{1,0:T(8,128)(2,1)S(1)} %shard_map.64.refs_0_.refs_4_), channel_id=1, source_target_pairs={{0,4},{4,8},{8,12},{12,0},{1,5},{5,9},{9,13},{13,1},{2,6},{6,10},{... | collective-permute-start | bytes 786440 | tf_op jit(solution)/shard_map/ppermute | solution.py:197
  9.4 3.0 %collective-permute-start = (f32[2,128,256]{2,1,0:T(8,128)S(1)}, f32[2,128,256]{2,1,0:T(8,128)S(1)}, u32[]{:S(2)}, u32[]{:S(2)}) collective-permute-start(f32[2,128,256]{2,1,0:T(8,128)S(1)} %get-tuple-element.14), channel_id=1, source_target_pairs={{0,1},{1,0},{2,3},{3,2},{4,5},{5,4},{6,7},{7,6},{8,9},{9,8},{10,11... | collective-permute-start | bytes 786440 | tf_op jit(solution)/shard_map/ppermute | solution.py:19
  9.4 10.0 %collective-permute-start.3 = (bf16[128,1024]{1,0:T(8,128)(2,1)S(1)}, bf16[128,1024]{1,0:T(8,128)(2,1)S(1)}, u32[]{:S(2)}, u32[]{:S(2)}) collective-permute-start(bf16[128,1024]{1,0:T(8,128)(2,1)S(1)} %shard_map.64.refs_0_.refs_4_), channel_id=1, source_target_pairs={{0,12},{4,0},{8,4},{12,8},{1,13},{5,1},{9,5},{13,9},{2,14},{6,2},{... | collective-permute-start | bytes 786440 | tf_op jit(solution)/shard_map/ppermute | solution.py:197
  12.4 1.8 %collective-permute-start.2 = (bf16[16,128]{1,0:T(8,128)(2,1)S(1)}, bf16[16,128]{1,0:T(8,128)(2,1)S(1)}, u32[]{:S(2)}, u32[]{:S(2)}) collective-permute-start(bf16[16,128]{1,0:T(8,128)(2,1)S(1)} %slice.16), channel_id=1, source_target_pairs={{0,1},{1,0},{2,3},{3,2},{4,5},{5,4},{6,7},{7,6},{8,9},{9,8},{10,11... | collective-permute-start | bytes 12296 | tf_op jit(solution)/shard_map/ppermute | solution.py:19
  12.4 8.8 %collective-permute-start.6 = (f32[2,128,256]{2,1,0:T(8,128)S(1)}, f32[2,128,256]{2,1,0:T(8,128)S(1)}, u32[]{:S(2)}, u32[]{:S(2)}) collective-permute-start(f32[2,128,256]{2,1,0:T(8,128)S(1)} %add.15.refs_0_), channel_id=1, source_target_pairs={{0,2},{1,3},{2,0},{3,1},{4,6},{5,7},{6,4},{7,5},{8,10},{9,11},{10,... | collective-permute-start | bytes 786440 | tf_op jit(solution)/shard_map/ppermute | solution.py:19
  14.0 11.8 %collective-permute-start.10 = (bf16[128,1024]{1,0:T(8,128)(2,1)S(1)}, bf16[128,1024]{1,0:T(8,128)(2,1)S(1)}, u32[]{:S(2)}, u32[]{:S(2)}) collective-permute-start(bf16[128,1024]{1,0:T(8,128)(2,1)S(1)} %collective-permute-done.1.refs_5_), channel_id=1, source_target_pairs={{0,4},{4,8},{8,12},{12,0},{1,5},{5,9},{9,13},{13,1},{2,6},{6,10},{... | collective-permute-start | bytes 786440 | tf_op jit(solution)/shard_map/ppermute | solution.py:197
  19.5 1.4 %collective-permute-start.4 = (f32[1,128,256]{2,1,0:T(8,128)S(1)}, f32[1,128,256]{2,1,0:T(8,128)S(1)}, u32[]{:S(2)}, u32[]{:S(2)}) collective-permute-start(f32[1,128,256]{2,1,0:T(8,128)S(1)} %get-tuple-element.21), channel_id=1, source_target_pairs={{0,1},{1,0},{2,3},{3,2},{4,5},{5,4},{6,7},{7,6},{8,9},{9,8},{10,11... | collective-permute-start | bytes 393224 | tf_op jit(solution)/shard_map/ppermute | solution.py:19
  19.6 1.5 %collective-permute-start.5 = (f32[1,128,256]{2,1,0:T(8,128)S(1)}, f32[1,128,256]{2,1,0:T(8,128)S(1)}, u32[]{:S(2)}, u32[]{:S(2)}) collective-permute-start(f32[1,128,256]{2,1,0:T(8,128)S(1)} %get-tuple-element.22), channel_id=1, source_target_pairs={{0,1},{1,0},{2,3},{3,2},{4,5},{5,4},{6,7},{7,6},{8,9},{9,8},{10,11... | collective-permute-start | bytes 393224 | tf_op jit(solution)/shard_map/ppermute | solution.py:19
  21.7 4.1 %collective-permute-start.7 = (f32[2,8,128]{2,1,0:T(8,128)S(1)}, f32[2,8,128]{2,1,0:T(8,128)S(1)}, u32[]{:S(2)}, u32[]{:S(2)}) collective-permute-start(f32[2,8,128]{2,1,0:T(8,128)S(1)} %get-tuple-element.17), channel_id=1, source_target_pairs={{0,2},{1,3},{2,0},{3,1},{4,6},{5,7},{6,4},{7,5},{8,10},{9,11},{10,... | collective-permute-start | bytes 24584 | tf_op jit(solution)/shard_map/ppermute | solution.py:19
  23.3 3.1 %collective-permute-start.8 = (f32[2,8,128]{2,1,0:T(8,128)S(1)}, f32[2,8,128]{2,1,0:T(8,128)S(1)}, u32[]{:S(2)}, u32[]{:S(2)}) collective-permute-start(f32[2,8,128]{2,1,0:T(8,128)S(1)} %get-tuple-element.18), channel_id=1, source_target_pairs={{0,3},{1,2},{2,1},{3,0},{4,7},{5,6},{6,5},{7,4},{8,11},{9,10},{10,... | collective-permute-start | bytes 24584 | tf_op jit(solution)/shard_map/ppermute | solution.py:19
  23.4 3.0 %collective-permute-start.9 = (f32[2,8,128]{2,1,0:T(8,128)S(1)}, f32[2,8,128]{2,1,0:T(8,128)S(1)}, u32[]{:S(2)}, u32[]{:S(2)}) collective-permute-start(f32[2,8,128]{2,1,0:T(8,128)S(1)} %get-tuple-element.19), channel_id=1, source_target_pairs={{0,1},{1,0},{2,3},{3,2},{4,5},{5,4},{6,7},{7,6},{8,9},{9,8},{10,11... | collective-permute-start | bytes 24584 | tf_op jit(solution)/shard_map/ppermute | solution.py:19
  26.7 3.8 %collective-permute-start.11 = (f32[8,512]{1,0:T(8,128)S(1)}, f32[8,512]{1,0:T(8,128)S(1)}, u32[]{:S(2)}, u32[]{:S(2)}) collective-permute-start(f32[8,512]{1,0:T(8,128)S(1)} %shard_map.68), channel_id=1, source_target_pairs={{0,2},{1,3},{2,0},{3,1},{4,6},{5,7},{6,4},{7,5},{8,10},{9,11},{10,... | collective-permute-start | bytes 49160 | tf_op jit(solution)/shard_map/ppermute | solution.py:19
  27.7 3.2 %collective-permute-start.12 = (f32[8,512]{1,0:T(8,128)S(1)}, f32[8,512]{1,0:T(8,128)S(1)}, u32[]{:S(2)}, u32[]{:S(2)}) collective-permute-start(f32[8,512]{1,0:T(8,128)S(1)} %shard_map.68), channel_id=1, source_target_pairs={{0,3},{1,2},{2,1},{3,0},{4,7},{5,6},{6,5},{7,4},{8,11},{9,10},{10,... | collective-permute-start | bytes 49160 | tf_op jit(solution)/shard_map/ppermute | solution.py:19
  27.7 3.2 %collective-permute-start.13 = (f32[8,512]{1,0:T(8,128)S(1)}, f32[8,512]{1,0:T(8,128)S(1)}, u32[]{:S(2)}, u32[]{:S(2)}) collective-permute-start(f32[8,512]{1,0:T(8,128)S(1)} %shard_map.68), channel_id=1, source_target_pairs={{0,1},{1,0},{2,3},{3,2},{4,5},{5,4},{6,7},{7,6},{8,9},{9,8},{10,11... | collective-permute-start | bytes 49160 | tf_op jit(solution)/shard_map/ppermute | solution.py:19

commit v25 on v24

--- a/solution.py
+++ b/solution.py
@@ -43,23 +43,28 @@
 LATER = 1<<10
 
 
-def project_kernel(steps, share, ahead, piece, after, act, og, wi, wo, lens, *refs):
-    refs = refs[after:]
+def project_kernel(steps, later, share, ahead, piece, after, act, og, wi, wo, lens, *refs):
+    if later:
+        refs = refs[after:]
+    else:
+        given, refs = refs[0], refs[1 + after :]
     outs, (buf, wibuf, wobuf, lenbuf, sem, wsem) = refs[:-6], refs[-6:]
     me = lax.axis_index("tensor")
     rank = wibuf.shape[0]
     slots = buf.shape[2]
-    count = len(steps) * share
-    tokens = count * slots
     small = [
         pltpu.make_async_copy(wi, wibuf, wsem.at[0]),
         pltpu.make_async_copy(wo, wobuf, wsem.at[1]),
         pltpu.make_async_copy(lens, lenbuf, wsem.at[2]),
     ]
-    pieces = [(side, at) for side, ref in enumerate((act, og)) for at in range(0, ref.shape[2], piece)]
+    widths = (act.shape[2], og.shape[2])
+    pieces = [(1, steps, at) for at in range(0, widths[1], piece)]
+    if later:
+        pieces = [(0, steps, at) for at in range(0, widths[0], piece)] + pieces
+        pieces += [(0, later, at) for at in range(0, widths[0], piece)]
     copies = []
-    for slot, (side, at) in enumerate(pieces):
-        width = min(piece, (act, og)[side].shape[2] - at)
+    for slot, (side, owners, at) in enumerate(pieces):
+        width = min(piece, widths[side] - at)
         copies.append(
             [
                 pltpu.make_async_copy(
@@ -67,51 +72,60 @@
                     buf.at[slot, pl.ds(i * share, share), :, pl.ds(0, width)],
                     sem.at[slot, i],
                 )
-                for i, step in enumerate(steps)
+                for i, step in enumerate(owners)
             ]
         )
-    small[0].start()
-    for slot, group in enumerate(copies):
+    needed = small if later else small[1:]
+    needed[0].start()
+    for slot, group in enumerate(copies[:ahead]):
         if slot == 1:
-            small[1].start()
-            small[2].start()
-        if slot < ahead:
-            for copy in group:
+            for copy in needed[1:]:
                 copy.start()
-    sums = [None, None]
-    for slot, (side, at) in enumerate(pieces):
-        if at == 0:
-            small[side].wait()
+        for copy in group:
+            copy.start()
+    for copy in needed if later else needed[:1]:
+        copy.wait()
+    sums = [None, None, None]
+    for slot, (side, owners, at) in enumerate(pieces):
         for copy in copies[slot]:
             copy.wait()
-        if slot + ahead < len(pieces):
-            for copy in copies[slot + ahead]:
-                copy.start()
+        for copy in copies[slot + ahead] if slot + ahead < len(pieces) else ():
+            copy.start()
         weight = (wibuf, wobuf)[side][:, at : at + piece]
-        token = buf[slot].reshape(tokens, piece)[:, : weight.shape[1]]
+        here = len(owners) * share
+        token = buf[slot, :here].reshape(here * slots, piece)[:, : weight.shape[1]]
         part = lax.dot_general(weight, token, NT, preferred_element_type=jnp.float32)
-        sums[side] = part if sums[side] is None else sums[side] + part
-    small[2].wait()
+        to = 2 if owners is later else side
+        sums[to] = part if sums[to] is None else sums[to] + part
+    if not later:
+        for copy in needed[1:]:
+            copy.wait()
     col = lax.broadcasted_iota(jnp.int32, (rank, slots), 1)
-    places = [out.at[i] for out in outs for i in range(out.shape[0])]
+    places = [out.at[i] for out in (outs[:-1] if later else outs) for i in range(out.shape[0])]
     for slot, out in enumerate(places):
+        cols = slice(slot * slots, (slot + 1) * slots)
         length = lenbuf[(me ^ steps[slot // share]) * share + slot % share]
-        one = sums[0][:, slot * slots : (slot + 1) * slots] * (1.0 / length.astype(jnp.float32))
+        one = (sums[0][:, cols] if later else given[slot]) * (1.0 / length.astype(jnp.float32))
         out[:rank] = jnp.where(col < length, one, 0.0)
-        out[rank:] = sums[1][:, slot * slots : (slot + 1) * slots]
-
-
-def project(act, og, wi, wo, lens, groups, share, ahead, piece, cost, after=()):
+        out[rank:] = sums[1][:, cols]
+    for slot in range(len(later) * share):
+        outs[-1][slot] = sums[2][:, slot * slots : (slot + 1) * slots]
+
+
+def project(act, og, wi, wo, lens, groups, later, share, ahead, piece, cost, after=(), given=()):
     steps = [step for group in groups for step in group]
     count = len(steps) * share
     slots, feat, hidden = act.shape[1], act.shape[2], og.shape[2]
     rank = wi.shape[0]
-    pieces = -(-feat // piece) - (-hidden // piece)
-    return pl.pallas_call(
-        functools.partial(project_kernel, steps, share, ahead, piece, len(after)),
-        out_shape=[jax.ShapeDtypeStruct((len(group) * share, 2 * rank, slots), jnp.float32) for group in groups],
-        in_specs=[HBM] * 5 + [VMEM] * len(after),
-        out_specs=[VMEM] * len(groups),
+    pieces = -(-feat // piece) * (2 if later else 0) - (-hidden // piece)
+    shapes = [jax.ShapeDtypeStruct((len(group) * share, 2 * rank, slots), jnp.float32) for group in groups]
+    if later:
+        shapes += [jax.ShapeDtypeStruct((len(later) * share, rank, slots), jnp.float32)]
+    return pl.pallas_call(
+        functools.partial(project_kernel, steps, later, share, ahead, piece, len(after)),
+        out_shape=shapes,
+        in_specs=[HBM] * 5 + [VMEM] * (len(given) + len(after)),
+        out_specs=[VMEM] * len(shapes),
         scratch_shapes=[
             pltpu.VMEM((pieces, count, slots, piece), act.dtype),
             pltpu.VMEM((rank, feat), wi.dtype),
@@ -122,7 +136,7 @@
         ],
         compiler_params=pltpu.CompilerParams(vmem_limit_bytes=32 << 20),
         cost_estimate=pl.CostEstimate(flops=cost, bytes_accessed=cost // 256, transcendentals=0),
-    )(*map(in_hbm, (act, og, wi, wo, lens)), *after)
+    )(*map(in_hbm, (act, og, wi, wo, lens)), *given, *after)
 
 
 def unit_kernel(share, rank, size, *refs):
@@ -214,11 +228,12 @@
 
     far = [CORES * x for x in range(1, size // CORES)]
     arrays = (activations, out_grads, proj_in.T, proj_out.T, lengths)
-    far_other, far_own = project(*arrays, [[step ^ 1 for step in far], far], share, 4, 512, COST, [own_tests])
+    sends, near = [[step ^ 1 for step in far], far], [1, 0]
+    far_other, far_own, in_rows = project(*arrays, sends, near, share, 4, 512, COST, [own_tests])
     far_sum = far_own + xor_permute(far_other, "tensor", size, 1)
     sums = [xor_permute(far_sum[i * share : (i + 1) * share], "tensor", size, step) for i, step in enumerate(far)]
     here = xor_permute(tests[1][0][:16, :128], "tensor", size, 1)
-    near_other, near_own = project(*arrays, [[1], [0]], share, 4, 512, LATER, [far_sum, here])
+    near_other, near_own = project(*arrays, [[1], [0]], [], share, 4, 512, LATER, [far_sum, here], [in_rows])
     late = tests[2][0][: near_other.shape[1], : near_other.shape[2]].astype(jnp.float32)
     pieces = [near_other[k : k + 1] for k in range(share)]
     pieces[0] = pieces[0] + 0.0 * late[None]

time: 31.7 us -> 33 us (1.041)
  starting transfers between devices: 11.9 us -> 12.7 us
  Pallas kernels: 12.5 us -> 13.2 us
    pallas_call x2, Pallas kernels: 10.6 us -> 11.3 us  [project(): pl.pallas_call(functools.partial(project_kernel, steps, later, share, ahe...]
    ppermute x3, starting transfers between devices: 5.33 us -> 5.8 us  [shift(): lax.ppermute(value, 'dp', [(i, (i + step) % groups) for i in range(groups)])]
    ppermute x11, starting transfers between devices: 6.57 us -> 6.93 us  [xor_permute(): return lax.ppermute(value, axis, [(i, i ^ step) for i in range(size)])]
  transfers between devices with their start and end apart: 14 -> 14, of which waited for: 8 -> 5; matrix products, arithmetic and copies ran while one was open for 0% -> 0% of each run, Pallas kernels for 35% -> 36%
where the time goes in v25:
time: 33 us; the launch traced here: 32.8 us
  Pallas kernels  13.2 us (40%)
  starting transfers between devices  12.7 us (38%)
  waiting for transfers between devices  6.08 us (18%)
  other arithmetic  0.69 us (2%)
    pallas_call x2, Pallas kernels, project(): pl.pallas_call(functools.partial(project_kernel, steps, later, share, ahe...  11.3 us
    ppermute x11, starting transfers between devices, xor_permute(): return lax.ppermute(value, axis, [(i, i ^ step) for i in range(size)])  6.93 us
    ppermute x3, starting transfers between devices, shift(): lax.ppermute(value, 'dp', [(i, (i + step) % groups) for i in range(groups)])  5.8 us
    ppermute x11, waiting for transfers between devices, xor_permute(): return lax.ppermute(value, axis, [(i, i ^ step) for i in range(size)])  3.57 us
    ppermute x3, waiting for transfers between devices, shift(): lax.ppermute(value, 'dp', [(i, (i + step) % groups) for i in range(groups)])  2.51 us
    pallas_call x1, Pallas kernels, cut_tests(): pl.pallas_call(cut_kernel, out_shape=jax.ShapeDtypeStruct((rows, width //...  0.96 us
  transfers between devices with their start and end apart: 14, of which 5 were waited for; matrix products, arithmetic and copies ran while one was open for 0% of the time, Pallas kernels for 36%

profile of v25, /device:TPU:0, one launch (start us, length us, event | category | flops | bytes accessed | tf_op | source)
XLA Modules:
  0.0 32.8 jit_solution(5467076614314970149)
XLA Ops:
  0.0 1.0 %shard_map.64.refs_0_.refs_4_ = bf16[128,1024]{1,0:T(8,128)(2,1)S(1)} custom-call(bf16[128,4096]{1,0:T(8,128)(2,1)} %tests.1), custom_call_target="tpu_custom_call" | custom-call | tf_op jit(solution)/shard_map/pallas_call | solution.py:32
  1.0 3.1 %collective-permute-start.1 = (bf16[128,1024]{1,0:T(8,128)(2,1)S(1)}, bf16[128,1024]{1,0:T(8,128)(2,1)S(1)}, u32[]{:S(2)}, u32[]{:S(2)}) collective-permute-start(bf16[128,1024]{1,0:T(8,128)(2,1)S(1)} %shard_map.64.refs_0_.refs_4_), channel_id=1, source_target_pairs={{0,4},{4,8},{8,12},{12,0},{1,5},{5,9},{9,13},{13,1},{2,6},{6,10},{... | collective-permute-start | bytes 786440 | tf_op jit(solution)/shard_map/ppermute | solution.py:211
  4.0 6.6 %shard_map.65 = (f32[2,128,256]{2,1,0:T(8,128)S(1)}, f32[2,128,256]{2,1,0:T(8,128)S(1)}, f32[4,64,256]{2,1,0:T(8,128)S(1)}) custom-call(bf16[8,256,1024]{2,1,0:T(8,128)(2,1)} %act.3, bf16[8,256,3584]{2,1,0:T(8,128)(2,1)} %og.3, bf16[64,1024]{1,0:T(8,128)(2,1)} %bitcast.6, bf16[64,3584]{1,0:T(8,128)(2,1)} %bitcast.4, s32[8]{0:T(128)} %lens.3, ...), custom_call_target="tpu_custom_call" | custom-call | flops 4294967296 | bytes 16777216 | tf_op jit(solution)/shard_map/pallas_call | solution.py:124
  10.6 0.1 collective-permute-start
  10.7 2.1 %collective-permute-start.3 = (bf16[128,1024]{1,0:T(8,128)(2,1)S(1)}, bf16[128,1024]{1,0:T(8,128)(2,1)S(1)}, u32[]{:S(2)}, u32[]{:S(2)}) collective-permute-start(bf16[128,1024]{1,0:T(8,128)(2,1)S(1)} %shard_map.64.refs_0_.refs_4_), channel_id=1, source_target_pairs={{0,12},{4,0},{8,4},{12,8},{1,13},{5,1},{9,5},{13,9},{2,14},{6,2},{... | collective-permute-start | bytes 786440 | tf_op jit(solution)/shard_map/ppermute | solution.py:211
  12.8 0.0 collective-permute-done.1.refs_5_
  12.8 0.2 collective-permute-start.2
  13.0 1.8 %collective-permute-start.6 = (f32[2,128,256]{2,1,0:T(8,128)S(1)}, f32[2,128,256]{2,1,0:T(8,128)S(1)}, u32[]{:S(2)}, u32[]{:S(2)}) collective-permute-start(f32[2,128,256]{2,1,0:T(8,128)S(1)} %add.15.refs_1_), channel_id=1, source_target_pairs={{0,2},{1,3},{2,0},{3,1},{4,6},{5,7},{6,4},{7,5},{8,10},{9,11},{10,... | collective-permute-start | bytes 786440 | tf_op jit(solution)/shard_map/ppermute | solution.py:19
  14.8 0.6 %collective-permute-start.10 = (bf16[128,1024]{1,0:T(8,128)(2,1)S(1)}, bf16[128,1024]{1,0:T(8,128)(2,1)S(1)}, u32[]{:S(2)}, u32[]{:S(2)}) collective-permute-start(bf16[128,1024]{1,0:T(8,128)(2,1)S(1)} %collective-permute-done.1.refs_5_), channel_id=1, source_target_pairs={{0,4},{4,8},{8,12},{12,0},{1,5},{5,9},{9,13},{13,1},{2,6},{6,10},{... | collective-permute-start | bytes 786440 | tf_op jit(solution)/shard_map/ppermute | solution.py:211
  15.4 0.0 collective-permute-done.2.refs_2_
  15.4 4.7 %shard_map.66 = (f32[2,128,256]{2,1,0:T(8,128)S(1)}, f32[2,128,256]{2,1,0:T(8,128)S(1)}) custom-call(bf16[8,256,1024]{2,1,0:T(8,128)(2,1)} %act.3, bf16[8,256,3584]{2,1,0:T(8,128)(2,1)} %og.3, bf16[64,1024]{1,0:T(8,128)(2,1)} %bitcast.7, bf16[64,3584]{1,0:T(8,128)(2,1)} %bitcast.5, s32[8]{0:T(128)} %lens.3, f32[4,64,256]{2,1,0:T(8,128)S(1)} %get-tuple-element.14.refs_0_, ...), custom_call_target="tpu_custom_call" | custom-call | flops 1024 | bytes 4 | tf_op jit(solution)/shard_map/pallas_call | solution.py:124
  20.2 0.0 collective-permute-done.3.refs_6_
  20.2 0.1 collective-permute-start.4
  20.3 0.5 %collective-permute-start.5 = (f32[1,128,256]{2,1,0:T(8,128)S(1)}, f32[1,128,256]{2,1,0:T(8,128)S(1)}, u32[]{:S(2)}, u32[]{:S(2)}) collective-permute-start(f32[1,128,256]{2,1,0:T(8,128)S(1)} %get-tuple-element.24), channel_id=1, source_target_pairs={{0,1},{1,0},{2,3},{3,2},{4,5},{5,4},{6,7},{7,6},{8,9},{9,8},{10,11... | collective-permute-start | bytes 393224 | tf_op jit(solution)/shard_map/ppermute | solution.py:19
  20.8 0.8 %collective-permute-done.4 = f32[1,128,256]{2,1,0:T(8,128)S(1)} collective-permute-done((f32[1,128,256]{2,1,0:T(8,128)S(1)}, f32[1,128,256]{2,1,0:T(8,128)S(1)}, u32[]{:S(2)}, u32[]{:S(2)}) %collective-permute-start.4) | collective-permute-done | bytes 131104 | tf_op jit(solution)/shard_map/ppermute | solution.py:19
  21.6 0.2 collective-permute-done.5
  21.8 0.5 %shard_map.67 = (f32[2,8,128]{2,1,0:T(8,128)S(1)}, f32[2,8,128]{2,1,0:T(8,128)S(1)}, f32[2,8,128]{2,1,0:T(8,128)S(1)}, f32[2,8,128]{2,1,0:T(8,128)S(1)}) custom-call(f32[2,128,256]{2,1,0:T(8,128)S(1)} %get-tuple-element.17.refs_0_, f32[2,128,256]{2,1,0:T(8,128)S(1)} %pad_maximum_fusion.refs_1_, f32[2,128,256]{2,1,0:T(8,128)S(1)} %collective-permute-done.6.refs_2_), custom_call_target="tpu_custom_call" | custom-call | tf_op jit(solution)/shard_map/pallas_call | solution.py:171
  22.4 1.6 %collective-permute-start.7 = (f32[2,8,128]{2,1,0:T(8,128)S(1)}, f32[2,8,128]{2,1,0:T(8,128)S(1)}, u32[]{:S(2)}, u32[]{:S(2)}) collective-permute-start(f32[2,8,128]{2,1,0:T(8,128)S(1)} %get-tuple-element.19), channel_id=1, source_target_pairs={{0,2},{1,3},{2,0},{3,1},{4,6},{5,7},{6,4},{7,5},{8,10},{9,11},{10,... | collective-permute-start | bytes 24584 | tf_op jit(solution)/shard_map/ppermute | solution.py:19
  23.9 0.2 collective-permute-start.8
  24.1 0.5 %collective-permute-start.9 = (f32[2,8,128]{2,1,0:T(8,128)S(1)}, f32[2,8,128]{2,1,0:T(8,128)S(1)}, u32[]{:S(2)}, u32[]{:S(2)}) collective-permute-start(f32[2,8,128]{2,1,0:T(8,128)S(1)} %get-tuple-element.21), channel_id=1, source_target_pairs={{0,1},{1,0},{2,3},{3,2},{4,5},{5,4},{6,7},{7,6},{8,9},{9,8},{10,11... | collective-permute-start | bytes 24584 | tf_op jit(solution)/shard_map/ppermute | solution.py:19
  24.6 2.5 %collective-permute-done.10.refs_7_ = bf16[128,1024]{1,0:T(8,128)(2,1)S(1)} collective-permute-done((bf16[128,1024]{1,0:T(8,128)(2,1)S(1)}, bf16[128,1024]{1,0:T(8,128)(2,1)S(1)}, u32[]{:S(2)}, u32[]{:S(2)}) %collective-permute-start.10) | collective-permute-done | bytes 262176 | tf_op jit(solution)/shard_map/ppermute | solution.py:211
  27.1 0.0 collective-permute-done.7.refs_0_
  27.1 0.0 collective-permute-done.8.refs_1_
  27.1 0.0 collective-permute-done.9.refs_2_
  27.1 0.4 %shard_map.68 = f32[8,512]{1,0:T(8,128)S(1)} custom-call(f32[2,8,128]{2,1,0:T(8,128)S(1)} %collective-permute-done.7.refs_0_, f32[2,8,128]{2,1,0:T(8,128)S(1)} %collective-permute-done.8.refs_1_, f32[2,8,128]{2,1,0:T(8,128)S(1)} %collective-permute-done.9.refs_2_, f32[2,8,128]{2,1,0:T(8,128)S(1)} %get-tuple-element.22.refs_3_, ...), custom_call_target="tpu_custom_call" | custom-call | tf_op jit(solution)/shard_map/pallas_call | solution.py:199
  27.5 1.5 %collective-permute-start.11 = (f32[8,512]{1,0:T(8,128)S(1)}, f32[8,512]{1,0:T(8,128)S(1)}, u32[]{:S(2)}, u32[]{:S(2)}) collective-permute-start(f32[8,512]{1,0:T(8,128)S(1)} %shard_map.68), channel_id=1, source_target_pairs={{0,2},{1,3},{2,0},{3,1},{4,6},{5,7},{6,4},{7,5},{8,10},{9,11},{10,... | collective-permute-start | bytes 49160 | tf_op jit(solution)/shard_map/ppermute | solution.py:19
  29.0 0.0 collective-permute-start.12
  29.0 0.6 %collective-permute-start.13 = (f32[8,512]{1,0:T(8,128)S(1)}, f32[8,512]{1,0:T(8,128)S(1)}, u32[]{:S(2)}, u32[]{:S(2)}) collective-permute-start(f32[8,512]{1,0:T(8,128)S(1)} %shard_map.68), channel_id=1, source_target_pairs={{0,1},{1,0},{2,3},{3,2},{4,5},{5,4},{6,7},{7,6},{8,9},{9,8},{10,11... | collective-permute-start | bytes 49160 | tf_op jit(solution)/shard_map/ppermute | solution.py:19
  29.6 1.6 %collective-permute-done.11 = f32[8,512]{1,0:T(8,128)S(1)} collective-permute-done((f32[8,512]{1,0:T(8,128)S(1)}, f32[8,512]{1,0:T(8,128)S(1)}, u32[]{:S(2)}, u32[]{:S(2)}) %collective-permute-start.11) | collective-permute-done | bytes 16416 | tf_op jit(solution)/shard_map/ppermute | solution.py:19
  31.2 0.9 %collective-permute-done.12 = f32[8,512]{1,0:T(8,128)S(1)} collective-permute-done((f32[8,512]{1,0:T(8,128)S(1)}, f32[8,512]{1,0:T(8,128)S(1)}, u32[]{:S(2)}, u32[]{:S(2)}) %collective-permute-start.12) | collective-permute-done | bytes 16416 | tf_op jit(solution)/shard_map/ppermute | solution.py:19
  32.1 0.0 collective-permute-done.13
  32.2 0.6 %add_add_fusion = f32[8,512]{1,0:T(8,128)} fusion(f32[8,512]{1,0:T(8,128)S(1)} %shard_map.68, f32[8,512]{1,0:T(8,128)S(1)} %collective-permute-done.13, f32[8,512]{1,0:T(8,128)S(1)} %collective-permute-done.11, f32[8,512]{1,0:T(8,128)S(1)} %collective-permute-done.12), kind=kLoop, calls=%fused_computation.2 | loop fusion | flops 12288 | bytes 81920 | tf_op jit(solution)/shard_map/add | solution.py:248
  (6 shorter events, 0.1 us)
Async XLA Ops:
  1.0 11.9 %collective-permute-start.1 = (bf16[128,1024]{1,0:T(8,128)(2,1)S(1)}, bf16[128,1024]{1,0:T(8,128)(2,1)S(1)}, u32[]{:S(2)}, u32[]{:S(2)}) collective-permute-start(bf16[128,1024]{1,0:T(8,128)(2,1)S(1)} %shard_map.64.refs_0_.refs_4_), channel_id=1, source_target_pairs={{0,4},{4,8},{8,12},{12,0},{1,5},{5,9},{9,13},{13,1},{2,6},{6,10},{... | collective-permute-start | bytes 786440 | tf_op jit(solution)/shard_map/ppermute | solution.py:211
  10.6 2.4 %collective-permute-start = (f32[2,128,256]{2,1,0:T(8,128)S(1)}, f32[2,128,256]{2,1,0:T(8,128)S(1)}, u32[]{:S(2)}, u32[]{:S(2)}) collective-permute-start(f32[2,128,256]{2,1,0:T(8,128)S(1)} %get-tuple-element.16), channel_id=1, source_target_pairs={{0,1},{1,0},{2,3},{3,2},{4,5},{5,4},{6,7},{7,6},{8,9},{9,8},{10,11... | collective-permute-start | bytes 786440 | tf_op jit(solution)/shard_map/ppermute | solution.py:19
  10.7 9.4 %collective-permute-start.3 = (bf16[128,1024]{1,0:T(8,128)(2,1)S(1)}, bf16[128,1024]{1,0:T(8,128)(2,1)S(1)}, u32[]{:S(2)}, u32[]{:S(2)}) collective-permute-start(bf16[128,1024]{1,0:T(8,128)(2,1)S(1)} %shard_map.64.refs_0_.refs_4_), channel_id=1, source_target_pairs={{0,12},{4,0},{8,4},{12,8},{1,13},{5,1},{9,5},{13,9},{2,14},{6,2},{... | collective-permute-start | bytes 786440 | tf_op jit(solution)/shard_map/ppermute | solution.py:211
  12.8 2.6 %collective-permute-start.2 = (bf16[16,128]{1,0:T(8,128)(2,1)S(1)}, bf16[16,128]{1,0:T(8,128)(2,1)S(1)}, u32[]{:S(2)}, u32[]{:S(2)}) collective-permute-start(bf16[16,128]{1,0:T(8,128)(2,1)S(1)} %slice.16), channel_id=1, source_target_pairs={{0,1},{1,0},{2,3},{3,2},{4,5},{5,4},{6,7},{7,6},{8,9},{9,8},{10,11... | collective-permute-start | bytes 12296 | tf_op jit(solution)/shard_map/ppermute | solution.py:19
  13.0 8.8 %collective-permute-start.6 = (f32[2,128,256]{2,1,0:T(8,128)S(1)}, f32[2,128,256]{2,1,0:T(8,128)S(1)}, u32[]{:S(2)}, u32[]{:S(2)}) collective-permute-start(f32[2,128,256]{2,1,0:T(8,128)S(1)} %add.15.refs_1_), channel_id=1, source_target_pairs={{0,2},{1,3},{2,0},{3,1},{4,6},{5,7},{6,4},{7,5},{8,10},{9,11},{10,... | collective-permute-start | bytes 786440 | tf_op jit(solution)/shard_map/ppermute | solution.py:19
  14.8 12.3 %collective-permute-start.10 = (bf16[128,1024]{1,0:T(8,128)(2,1)S(1)}, bf16[128,1024]{1,0:T(8,128)(2,1)S(1)}, u32[]{:S(2)}, u32[]{:S(2)}) collective-permute-start(bf16[128,1024]{1,0:T(8,128)(2,1)S(1)} %collective-permute-done.1.refs_5_), channel_id=1, source_target_pairs={{0,4},{4,8},{8,12},{12,0},{1,5},{5,9},{9,13},{13,1},{2,6},{6,10},{... | collective-permute-start | bytes 786440 | tf_op jit(solution)/shard_map/ppermute | solution.py:211
  20.2 1.4 %collective-permute-start.4 = (f32[1,128,256]{2,1,0:T(8,128)S(1)}, f32[1,128,256]{2,1,0:T(8,128)S(1)}, u32[]{:S(2)}, u32[]{:S(2)}) collective-permute-start(f32[1,128,256]{2,1,0:T(8,128)S(1)} %get-tuple-element.23), channel_id=1, source_target_pairs={{0,1},{1,0},{2,3},{3,2},{4,5},{5,4},{6,7},{7,6},{8,9},{9,8},{10,11... | collective-permute-start | bytes 393224 | tf_op jit(solution)/shard_map/ppermute | solution.py:19
  20.3 1.5 %collective-permute-start.5 = (f32[1,128,256]{2,1,0:T(8,128)S(1)}, f32[1,128,256]{2,1,0:T(8,128)S(1)}, u32[]{:S(2)}, u32[]{:S(2)}) collective-permute-start(f32[1,128,256]{2,1,0:T(8,128)S(1)} %get-tuple-element.24), channel_id=1, source_target_pairs={{0,1},{1,0},{2,3},{3,2},{4,5},{5,4},{6,7},{7,6},{8,9},{9,8},{10,11... | collective-permute-start | bytes 393224 | tf_op jit(solution)/shard_map/ppermute | solution.py:19
  22.4 4.7 %collective-permute-start.7 = (f32[2,8,128]{2,1,0:T(8,128)S(1)}, f32[2,8,128]{2,1,0:T(8,128)S(1)}, u32[]{:S(2)}, u32[]{:S(2)}) collective-permute-start(f32[2,8,128]{2,1,0:T(8,128)S(1)} %get-tuple-element.19), channel_id=1, source_target_pairs={{0,2},{1,3},{2,0},{3,1},{4,6},{5,7},{6,4},{7,5},{8,10},{9,11},{10,... | collective-permute-start | bytes 24584 | tf_op jit(solution)/shard_map/ppermute | solution.py:19
  23.9 3.1 %collective-permute-start.8 = (f32[2,8,128]{2,1,0:T(8,128)S(1)}, f32[2,8,128]{2,1,0:T(8,128)S(1)}, u32[]{:S(2)}, u32[]{:S(2)}) collective-permute-start(f32[2,8,128]{2,1,0:T(8,128)S(1)} %get-tuple-element.20), channel_id=1, source_target_pairs={{0,3},{1,2},{2,1},{3,0},{4,7},{5,6},{6,5},{7,4},{8,11},{9,10},{10,... | collective-permute-start | bytes 24584 | tf_op jit(solution)/shard_map/ppermute | solution.py:19
  24.1 3.0 %collective-permute-start.9 = (f32[2,8,128]{2,1,0:T(8,128)S(1)}, f32[2,8,128]{2,1,0:T(8,128)S(1)}, u32[]{:S(2)}, u32[]{:S(2)}) collective-permute-start(f32[2,8,128]{2,1,0:T(8,128)S(1)} %get-tuple-element.21), channel_id=1, source_target_pairs={{0,1},{1,0},{2,3},{3,2},{4,5},{5,4},{6,7},{7,6},{8,9},{9,8},{10,11... | collective-permute-start | bytes 24584 | tf_op jit(solution)/shard_map/ppermute | solution.py:19
  27.5 3.8 %collective-permute-start.11 = (f32[8,512]{1,0:T(8,128)S(1)}, f32[8,512]{1,0:T(8,128)S(1)}, u32[]{:S(2)}, u32[]{:S(2)}) collective-permute-start(f32[8,512]{1,0:T(8,128)S(1)} %shard_map.68), channel_id=1, source_target_pairs={{0,2},{1,3},{2,0},{3,1},{4,6},{5,7},{6,4},{7,5},{8,10},{9,11},{10,... | collective-permute-start | bytes 49160 | tf_op jit(solution)/shard_map/ppermute | solution.py:19
  29.0 3.2 %collective-permute-start.12 = (f32[8,512]{1,0:T(8,128)S(1)}, f32[8,512]{1,0:T(8,128)S(1)}, u32[]{:S(2)}, u32[]{:S(2)}) collective-permute-start(f32[8,512]{1,0:T(8,128)S(1)} %shard_map.68), channel_id=1, source_target_pairs={{0,3},{1,2},{2,1},{3,0},{4,7},{5,6},{6,5},{7,4},{8,11},{9,10},{10,... | collective-permute-start | bytes 49160 | tf_op jit(solution)/shard_map/ppermute | solution.py:19
  29.0 3.2 %collective-permute-start.13 = (f32[8,512]{1,0:T(8,128)S(1)}, f32[8,512]{1,0:T(8,128)S(1)}, u32[]{:S(2)}, u32[]{:S(2)}) collective-permute-start(f32[8,512]{1,0:T(8,128)S(1)} %shard_map.68), channel_id=1, source_target_pairs={{0,1},{1,0},{2,3},{3,2},{4,5},{5,4},{6,7},{7,6},{8,9},{9,8},{10,11... | collective-permute-start | bytes 49160 | tf_op jit(solution)/shard_map/ppermute | solution.py:19

commit v26 on v24

--- a/solution.py
+++ b/solution.py
@@ -43,7 +43,7 @@
 LATER = 1<<10
 
 
-def project_kernel(steps, share, ahead, piece, after, act, og, wi, wo, lens, *refs):
+def project_kernel(steps, share, ahead, pieces, after, act, og, wi, wo, lens, *refs):
     refs = refs[after:]
     outs, (buf, wibuf, wobuf, lenbuf, sem, wsem) = refs[:-6], refs[-6:]
     me = lax.axis_index("tensor")
@@ -56,10 +56,8 @@
         pltpu.make_async_copy(wo, wobuf, wsem.at[1]),
         pltpu.make_async_copy(lens, lenbuf, wsem.at[2]),
     ]
-    pieces = [(side, at) for side, ref in enumerate((act, og)) for at in range(0, ref.shape[2], piece)]
     copies = []
-    for slot, (side, at) in enumerate(pieces):
-        width = min(piece, (act, og)[side].shape[2] - at)
+    for slot, (side, at, width) in enumerate(pieces):
         copies.append(
             [
                 pltpu.make_async_copy(
@@ -79,7 +77,7 @@
             for copy in group:
                 copy.start()
     sums = [None, None]
-    for slot, (side, at) in enumerate(pieces):
+    for slot, (side, at, width) in enumerate(pieces):
         if at == 0:
             small[side].wait()
         for copy in copies[slot]:
@@ -87,8 +85,8 @@
         if slot + ahead < len(pieces):
             for copy in copies[slot + ahead]:
                 copy.start()
-        weight = (wibuf, wobuf)[side][:, at : at + piece]
-        token = buf[slot].reshape(tokens, piece)[:, : weight.shape[1]]
+        weight = (wibuf, wobuf)[side][:, at : at + width]
+        token = buf[slot].reshape(tokens, buf.shape[3])[:, :width]
         part = lax.dot_general(weight, token, NT, preferred_element_type=jnp.float32)
         sums[side] = part if sums[side] is None else sums[side] + part
     small[2].wait()
@@ -106,18 +104,19 @@
     count = len(steps) * share
     slots, feat, hidden = act.shape[1], act.shape[2], og.shape[2]
     rank = wi.shape[0]
-    pieces = -(-feat // piece) - (-hidden // piece)
-    return pl.pallas_call(
-        functools.partial(project_kernel, steps, share, ahead, piece, len(after)),
+    pieces = [(0, at, min(512, feat - at)) for at in range(0, feat, 512)]
+    pieces += [(1, at, min(piece, hidden - at)) for at in range(0, hidden, piece)]
+    return pl.pallas_call(
+        functools.partial(project_kernel, steps, share, ahead, pieces, len(after)),
         out_shape=[jax.ShapeDtypeStruct((len(group) * share, 2 * rank, slots), jnp.float32) for group in groups],
         in_specs=[HBM] * 5 + [VMEM] * len(after),
         out_specs=[VMEM] * len(groups),
         scratch_shapes=[
-            pltpu.VMEM((pieces, count, slots, piece), act.dtype),
+            pltpu.VMEM((len(pieces), count, slots, piece), act.dtype),
             pltpu.VMEM((rank, feat), wi.dtype),
             pltpu.VMEM((rank, hidden), wo.dtype),
             pltpu.SMEM(lens.shape, lens.dtype),
-            pltpu.SemaphoreType.DMA((pieces, len(steps))),
+            pltpu.SemaphoreType.DMA((len(pieces), len(steps))),
             pltpu.SemaphoreType.DMA((3,)),
         ],
         compiler_params=pltpu.CompilerParams(vmem_limit_bytes=32 << 20),
@@ -214,11 +213,11 @@
 
     far = [CORES * x for x in range(1, size // CORES)]
     arrays = (activations, out_grads, proj_in.T, proj_out.T, lengths)
-    far_other, far_own = project(*arrays, [[step ^ 1 for step in far], far], share, 4, 512, COST, [own_tests])
+    far_other, far_own = project(*arrays, [[step ^ 1 for step in far], far], share, 3, 896, COST, [own_tests])
     far_sum = far_own + xor_permute(far_other, "tensor", size, 1)
     sums = [xor_permute(far_sum[i * share : (i + 1) * share], "tensor", size, step) for i, step in enumerate(far)]
     here = xor_permute(tests[1][0][:16, :128], "tensor", size, 1)
-    near_other, near_own = project(*arrays, [[1], [0]], share, 4, 512, LATER, [far_sum, here])
+    near_other, near_own = project(*arrays, [[1], [0]], share, 3, 896, LATER, [far_sum, here])
     late = tests[2][0][: near_other.shape[1], : near_other.shape[2]].astype(jnp.float32)
     pieces = [near_other[k : k + 1] for k in range(share)]
     pieces[0] = pieces[0] + 0.0 * late[None]

time: 31.7 us -> 32.2 us (1.016)
  Pallas kernels: 12.5 us -> 13.2 us
  waiting for transfers between devices: 6.34 us -> 5.8 us
    pallas_call x2, Pallas kernels: 10.6 us -> 11.3 us  [project(): pl.pallas_call(functools.partial(project_kernel, steps, share, ahead, pie...]
    ppermute x3, waiting for transfers between devices: 2.69 us -> 2.06 us  [shift(): lax.ppermute(value, 'dp', [(i, (i + step) % groups) for i in range(groups)])]
    ppermute x3, starting transfers between devices: 5.33 us -> 5.68 us  [shift(): lax.ppermute(value, 'dp', [(i, (i + step) % groups) for i in range(groups)])]
  transfers between devices with their start and end apart: 14 -> 14, of which waited for: 8 -> 7; matrix products, arithmetic and copies ran while one was open for 0% -> 0% of each run, Pallas kernels for 35% -> 37%
where the time goes in v26:
time: 32.2 us; the launch traced here: 32 us
  Pallas kernels  13.2 us (41%)
  starting transfers between devices  12.2 us (38%)
  waiting for transfers between devices  5.8 us (18%)
  other arithmetic  0.7 us (2%)
    pallas_call x2, Pallas kernels, project(): pl.pallas_call(functools.partial(project_kernel, steps, share, ahead, pie...  11.3 us
    ppermute x11, starting transfers between devices, xor_permute(): return lax.ppermute(value, axis, [(i, i ^ step) for i in range(size)])  6.56 us
    ppermute x3, starting transfers between devices, shift(): lax.ppermute(value, 'dp', [(i, (i + step) % groups) for i in range(groups)])  5.68 us
    ppermute x11, waiting for transfers between devices, xor_permute(): return lax.ppermute(value, axis, [(i, i ^ step) for i in range(size)])  3.74 us
    ppermute x3, waiting for transfers between devices, shift(): lax.ppermute(value, 'dp', [(i, (i + step) % groups) for i in range(groups)])  2.06 us
    pallas_call x1, Pallas kernels, cut_tests(): pl.pallas_call(cut_kernel, out_shape=jax.ShapeDtypeStruct((rows, width //...  0.96 us
  transfers between devices with their start and end apart: 14, of which 7 were waited for; matrix products, arithmetic and copies ran while one was open for 0% of the time, Pallas kernels for 37%

profile of v26, /device:TPU:0, one launch (start us, length us, event | category | flops | bytes accessed | tf_op | source)
XLA Modules:
  0.0 32.0 jit_solution(662043204618397563)
XLA Ops:
  0.0 1.0 %shard_map.64.refs_0_.refs_4_ = bf16[128,1024]{1,0:T(8,128)(2,1)S(1)} custom-call(bf16[128,4096]{1,0:T(8,128)(2,1)} %tests.1), custom_call_target="tpu_custom_call" | custom-call | tf_op jit(solution)/shard_map/pallas_call | solution.py:32
  1.0 3.1 %collective-permute-start.1 = (bf16[128,1024]{1,0:T(8,128)(2,1)S(1)}, bf16[128,1024]{1,0:T(8,128)(2,1)S(1)}, u32[]{:S(2)}, u32[]{:S(2)}) collective-permute-start(bf16[128,1024]{1,0:T(8,128)(2,1)S(1)} %shard_map.64.refs_0_.refs_4_), channel_id=1, source_target_pairs={{0,4},{4,8},{8,12},{12,0},{1,5},{5,9},{9,13},{13,1},{2,6},{6,10},{... | collective-permute-start | bytes 786440 | tf_op jit(solution)/shard_map/ppermute | solution.py:196
  4.0 5.7 %shard_map.65 = (f32[2,128,256]{2,1,0:T(8,128)S(1)}, f32[2,128,256]{2,1,0:T(8,128)S(1)}) custom-call(bf16[8,256,1024]{2,1,0:T(8,128)(2,1)} %act.3, bf16[8,256,3584]{2,1,0:T(8,128)(2,1)} %og.3, bf16[64,1024]{1,0:T(8,128)(2,1)} %bitcast.6, bf16[64,3584]{1,0:T(8,128)(2,1)} %bitcast.4, s32[8]{0:T(128)} %lens.3, bf16[128,1024]{1,0:T(8,128)(2,1)S(1)} %shard_map.64.refs_0_.refs_4_), custom_call_target="tpu_custom_call" | custom-call | flops 4294967296 | bytes 16777216 | tf_op jit(solution)/shard_map/pallas_call | solution.py:109
  9.7 0.1 collective-permute-start
  9.8 2.1 %collective-permute-start.3 = (bf16[128,1024]{1,0:T(8,128)(2,1)S(1)}, bf16[128,1024]{1,0:T(8,128)(2,1)S(1)}, u32[]{:S(2)}, u32[]{:S(2)}) collective-permute-start(bf16[128,1024]{1,0:T(8,128)(2,1)S(1)} %shard_map.64.refs_0_.refs_4_), channel_id=1, source_target_pairs={{0,12},{4,0},{8,4},{12,8},{1,13},{5,1},{9,5},{13,9},{2,14},{6,2},{... | collective-permute-start | bytes 786440 | tf_op jit(solution)/shard_map/ppermute | solution.py:196
  11.9 0.5 %collective-permute-done.1.refs_5_ = bf16[128,1024]{1,0:T(8,128)(2,1)S(1)} collective-permute-done((bf16[128,1024]{1,0:T(8,128)(2,1)S(1)}, bf16[128,1024]{1,0:T(8,128)(2,1)S(1)}, u32[]{:S(2)}, u32[]{:S(2)}) %collective-permute-start.1) | collective-permute-done | bytes 262176 | tf_op jit(solution)/shard_map/ppermute | solution.py:196
  12.4 0.0 collective-permute-start.2
  12.4 0.0 collective-permute-done
  12.4 1.6 %collective-permute-start.6 = (f32[2,128,256]{2,1,0:T(8,128)S(1)}, f32[2,128,256]{2,1,0:T(8,128)S(1)}, u32[]{:S(2)}, u32[]{:S(2)}) collective-permute-start(f32[2,128,256]{2,1,0:T(8,128)S(1)} %add.15.refs_0_), channel_id=1, source_target_pairs={{0,2},{1,3},{2,0},{3,1},{4,6},{5,7},{6,4},{7,5},{8,10},{9,11},{10,... | collective-permute-start | bytes 786440 | tf_op jit(solution)/shard_map/ppermute | solution.py:19
  14.0 0.5 %collective-permute-start.10 = (bf16[128,1024]{1,0:T(8,128)(2,1)S(1)}, bf16[128,1024]{1,0:T(8,128)(2,1)S(1)}, u32[]{:S(2)}, u32[]{:S(2)}) collective-permute-start(bf16[128,1024]{1,0:T(8,128)(2,1)S(1)} %collective-permute-done.1.refs_5_), channel_id=1, source_target_pairs={{0,4},{4,8},{8,12},{12,0},{1,5},{5,9},{9,13},{13,1},{2,6},{6,10},{... | collective-permute-start | bytes 786440 | tf_op jit(solution)/shard_map/ppermute | solution.py:196
  14.5 0.0 collective-permute-done.2.refs_1_
  14.5 5.7 %shard_map.66 = (f32[2,128,256]{2,1,0:T(8,128)S(1)}, f32[2,128,256]{2,1,0:T(8,128)S(1)}) custom-call(bf16[8,256,1024]{2,1,0:T(8,128)(2,1)} %act.3, bf16[8,256,3584]{2,1,0:T(8,128)(2,1)} %og.3, bf16[64,1024]{1,0:T(8,128)(2,1)} %bitcast.7, bf16[64,3584]{1,0:T(8,128)(2,1)} %bitcast.5, s32[8]{0:T(128)} %lens.3, f32[2,128,256]{2,1,0:T(8,128)S(1)} %add.15.refs_0_, ...), custom_call_target="tpu_custom_call" | custom-call | flops 1024 | bytes 4 | tf_op jit(solution)/shard_map/pallas_call | solution.py:109
  20.2 0.0 collective-permute-done.3.refs_6_
  20.2 0.1 collective-permute-start.4
  20.3 0.5 %collective-permute-start.5 = (f32[1,128,256]{2,1,0:T(8,128)S(1)}, f32[1,128,256]{2,1,0:T(8,128)S(1)}, u32[]{:S(2)}, u32[]{:S(2)}) collective-permute-start(f32[1,128,256]{2,1,0:T(8,128)S(1)} %get-tuple-element.22), channel_id=1, source_target_pairs={{0,1},{1,0},{2,3},{3,2},{4,5},{5,4},{6,7},{7,6},{8,9},{9,8},{10,11... | collective-permute-start | bytes 393224 | tf_op jit(solution)/shard_map/ppermute | solution.py:19
  20.8 0.8 %collective-permute-done.4 = f32[1,128,256]{2,1,0:T(8,128)S(1)} collective-permute-done((f32[1,128,256]{2,1,0:T(8,128)S(1)}, f32[1,128,256]{2,1,0:T(8,128)S(1)}, u32[]{:S(2)}, u32[]{:S(2)}) %collective-permute-start.4) | collective-permute-done | bytes 131104 | tf_op jit(solution)/shard_map/ppermute | solution.py:19
  21.6 0.2 collective-permute-done.5
  21.8 0.0 collective-permute-done.6.refs_2_
  21.8 0.5 %shard_map.67 = (f32[2,8,128]{2,1,0:T(8,128)S(1)}, f32[2,8,128]{2,1,0:T(8,128)S(1)}, f32[2,8,128]{2,1,0:T(8,128)S(1)}, f32[2,8,128]{2,1,0:T(8,128)S(1)}) custom-call(f32[2,128,256]{2,1,0:T(8,128)S(1)} %get-tuple-element.15.refs_0_, f32[2,128,256]{2,1,0:T(8,128)S(1)} %pad_maximum_fusion.refs_1_, f32[2,128,256]{2,1,0:T(8,128)S(1)} %collective-permute-done.6.refs_2_), custom_call_target="tpu_custom_call" | custom-call | tf_op jit(solution)/shard_map/pallas_call | solution.py:156
  22.4 0.9 %collective-permute-start.7 = (f32[2,8,128]{2,1,0:T(8,128)S(1)}, f32[2,8,128]{2,1,0:T(8,128)S(1)}, u32[]{:S(2)}, u32[]{:S(2)}) collective-permute-start(f32[2,8,128]{2,1,0:T(8,128)S(1)} %get-tuple-element.17), channel_id=1, source_target_pairs={{0,2},{1,3},{2,0},{3,1},{4,6},{5,7},{6,4},{7,5},{8,10},{9,11},{10,... | collective-permute-start | bytes 24584 | tf_op jit(solution)/shard_map/ppermute | solution.py:19
  23.3 0.8 %collective-permute-start.8 = (f32[2,8,128]{2,1,0:T(8,128)S(1)}, f32[2,8,128]{2,1,0:T(8,128)S(1)}, u32[]{:S(2)}, u32[]{:S(2)}) collective-permute-start(f32[2,8,128]{2,1,0:T(8,128)S(1)} %get-tuple-element.18), channel_id=1, source_target_pairs={{0,3},{1,2},{2,1},{3,0},{4,7},{5,6},{6,5},{7,4},{8,11},{9,10},{10,... | collective-permute-start | bytes 24584 | tf_op jit(solution)/shard_map/ppermute | solution.py:19
  24.1 0.5 %collective-permute-start.9 = (f32[2,8,128]{2,1,0:T(8,128)S(1)}, f32[2,8,128]{2,1,0:T(8,128)S(1)}, u32[]{:S(2)}, u32[]{:S(2)}) collective-permute-start(f32[2,8,128]{2,1,0:T(8,128)S(1)} %get-tuple-element.19), channel_id=1, source_target_pairs={{0,1},{1,0},{2,3},{3,2},{4,5},{5,4},{6,7},{7,6},{8,9},{9,8},{10,11... | collective-permute-start | bytes 24584 | tf_op jit(solution)/shard_map/ppermute | solution.py:19
  24.6 1.6 %collective-permute-done.10.refs_7_ = bf16[128,1024]{1,0:T(8,128)(2,1)S(1)} collective-permute-done((bf16[128,1024]{1,0:T(8,128)(2,1)S(1)}, bf16[128,1024]{1,0:T(8,128)(2,1)S(1)}, u32[]{:S(2)}, u32[]{:S(2)}) %collective-permute-start.10) | collective-permute-done | bytes 262176 | tf_op jit(solution)/shard_map/ppermute | solution.py:196
  26.2 0.2 collective-permute-done.8.refs_1_
  26.4 0.0 collective-permute-done.9.refs_2_
  26.4 0.4 %shard_map.68 = f32[8,512]{1,0:T(8,128)S(1)} custom-call(f32[2,8,128]{2,1,0:T(8,128)S(1)} %collective-permute-done.7.refs_0_, f32[2,8,128]{2,1,0:T(8,128)S(1)} %collective-permute-done.8.refs_1_, f32[2,8,128]{2,1,0:T(8,128)S(1)} %collective-permute-done.9.refs_2_, f32[2,8,128]{2,1,0:T(8,128)S(1)} %get-tuple-element.20.refs_3_, ...), custom_call_target="tpu_custom_call" | custom-call | tf_op jit(solution)/shard_map/pallas_call | solution.py:184
  26.7 1.3 %collective-permute-start.11 = (f32[8,512]{1,0:T(8,128)S(1)}, f32[8,512]{1,0:T(8,128)S(1)}, u32[]{:S(2)}, u32[]{:S(2)}) collective-permute-start(f32[8,512]{1,0:T(8,128)S(1)} %shard_map.68), channel_id=1, source_target_pairs={{0,2},{1,3},{2,0},{3,1},{4,6},{5,7},{6,4},{7,5},{8,10},{9,11},{10,... | collective-permute-start | bytes 49160 | tf_op jit(solution)/shard_map/ppermute | solution.py:19
  28.1 0.0 collective-permute-start.12
  28.1 0.8 %collective-permute-start.13 = (f32[8,512]{1,0:T(8,128)S(1)}, f32[8,512]{1,0:T(8,128)S(1)}, u32[]{:S(2)}, u32[]{:S(2)}) collective-permute-start(f32[8,512]{1,0:T(8,128)S(1)} %shard_map.68), channel_id=1, source_target_pairs={{0,1},{1,0},{2,3},{3,2},{4,5},{5,4},{6,7},{7,6},{8,9},{9,8},{10,11... | collective-permute-start | bytes 49160 | tf_op jit(solution)/shard_map/ppermute | solution.py:19
  28.9 1.6 %collective-permute-done.11 = f32[8,512]{1,0:T(8,128)S(1)} collective-permute-done((f32[8,512]{1,0:T(8,128)S(1)}, f32[8,512]{1,0:T(8,128)S(1)}, u32[]{:S(2)}, u32[]{:S(2)}) %collective-permute-start.11) | collective-permute-done | bytes 16416 | tf_op jit(solution)/shard_map/ppermute | solution.py:19
  30.5 0.9 %collective-permute-done.12 = f32[8,512]{1,0:T(8,128)S(1)} collective-permute-done((f32[8,512]{1,0:T(8,128)S(1)}, f32[8,512]{1,0:T(8,128)S(1)}, u32[]{:S(2)}, u32[]{:S(2)}) %collective-permute-start.12) | collective-permute-done | bytes 16416 | tf_op jit(solution)/shard_map/ppermute | solution.py:19
  31.4 0.6 %add_add_fusion = f32[8,512]{1,0:T(8,128)} fusion(f32[8,512]{1,0:T(8,128)S(1)} %shard_map.68, f32[8,512]{1,0:T(8,128)S(1)} %collective-permute-done.13, f32[8,512]{1,0:T(8,128)S(1)} %collective-permute-done.11, f32[8,512]{1,0:T(8,128)S(1)} %collective-permute-done.12), kind=kLoop, calls=%fused_computation.2 | loop fusion | flops 12288 | bytes 81920 | tf_op jit(solution)/shard_map/add | solution.py:232
  (6 shorter events, 0.1 us)
Async XLA Ops:
  1.0 11.4 %collective-permute-start.1 = (bf16[128,1024]{1,0:T(8,128)(2,1)S(1)}, bf16[128,1024]{1,0:T(8,128)(2,1)S(1)}, u32[]{:S(2)}, u32[]{:S(2)}) collective-permute-start(bf16[128,1024]{1,0:T(8,128)(2,1)S(1)} %shard_map.64.refs_0_.refs_4_), channel_id=1, source_target_pairs={{0,4},{4,8},{8,12},{12,0},{1,5},{5,9},{9,13},{13,1},{2,6},{6,10},{... | collective-permute-start | bytes 786440 | tf_op jit(solution)/shard_map/ppermute | solution.py:196
  9.7 2.7 %collective-permute-start = (f32[2,128,256]{2,1,0:T(8,128)S(1)}, f32[2,128,256]{2,1,0:T(8,128)S(1)}, u32[]{:S(2)}, u32[]{:S(2)}) collective-permute-start(f32[2,128,256]{2,1,0:T(8,128)S(1)} %get-tuple-element.14), channel_id=1, source_target_pairs={{0,1},{1,0},{2,3},{3,2},{4,5},{5,4},{6,7},{7,6},{8,9},{9,8},{10,11... | collective-permute-start | bytes 786440 | tf_op jit(solution)/shard_map/ppermute | solution.py:19
  9.8 10.4 %collective-permute-start.3 = (bf16[128,1024]{1,0:T(8,128)(2,1)S(1)}, bf16[128,1024]{1,0:T(8,128)(2,1)S(1)}, u32[]{:S(2)}, u32[]{:S(2)}) collective-permute-start(bf16[128,1024]{1,0:T(8,128)(2,1)S(1)} %shard_map.64.refs_0_.refs_4_), channel_id=1, source_target_pairs={{0,12},{4,0},{8,4},{12,8},{1,13},{5,1},{9,5},{13,9},{2,14},{6,2},{... | collective-permute-start | bytes 786440 | tf_op jit(solution)/shard_map/ppermute | solution.py:196
  12.4 2.1 %collective-permute-start.2 = (bf16[16,128]{1,0:T(8,128)(2,1)S(1)}, bf16[16,128]{1,0:T(8,128)(2,1)S(1)}, u32[]{:S(2)}, u32[]{:S(2)}) collective-permute-start(bf16[16,128]{1,0:T(8,128)(2,1)S(1)} %slice.16), channel_id=1, source_target_pairs={{0,1},{1,0},{2,3},{3,2},{4,5},{5,4},{6,7},{7,6},{8,9},{9,8},{10,11... | collective-permute-start | bytes 12296 | tf_op jit(solution)/shard_map/ppermute | solution.py:19
  12.4 9.4 %collective-permute-start.6 = (f32[2,128,256]{2,1,0:T(8,128)S(1)}, f32[2,128,256]{2,1,0:T(8,128)S(1)}, u32[]{:S(2)}, u32[]{:S(2)}) collective-permute-start(f32[2,128,256]{2,1,0:T(8,128)S(1)} %add.15.refs_0_), channel_id=1, source_target_pairs={{0,2},{1,3},{2,0},{3,1},{4,6},{5,7},{6,4},{7,5},{8,10},{9,11},{10,... | collective-permute-start | bytes 786440 | tf_op jit(solution)/shard_map/ppermute | solution.py:19
  14.0 12.2 %collective-permute-start.10 = (bf16[128,1024]{1,0:T(8,128)(2,1)S(1)}, bf16[128,1024]{1,0:T(8,128)(2,1)S(1)}, u32[]{:S(2)}, u32[]{:S(2)}) collective-permute-start(bf16[128,1024]{1,0:T(8,128)(2,1)S(1)} %collective-permute-done.1.refs_5_), channel_id=1, source_target_pairs={{0,4},{4,8},{8,12},{12,0},{1,5},{5,9},{9,13},{13,1},{2,6},{6,10},{... | collective-permute-start | bytes 786440 | tf_op jit(solution)/shard_map/ppermute | solution.py:196
  20.2 1.4 %collective-permute-start.4 = (f32[1,128,256]{2,1,0:T(8,128)S(1)}, f32[1,128,256]{2,1,0:T(8,128)S(1)}, u32[]{:S(2)}, u32[]{:S(2)}) collective-permute-start(f32[1,128,256]{2,1,0:T(8,128)S(1)} %get-tuple-element.21), channel_id=1, source_target_pairs={{0,1},{1,0},{2,3},{3,2},{4,5},{5,4},{6,7},{7,6},{8,9},{9,8},{10,11... | collective-permute-start | bytes 393224 | tf_op jit(solution)/shard_map/ppermute | solution.py:19
  20.3 1.5 %collective-permute-start.5 = (f32[1,128,256]{2,1,0:T(8,128)S(1)}, f32[1,128,256]{2,1,0:T(8,128)S(1)}, u32[]{:S(2)}, u32[]{:S(2)}) collective-permute-start(f32[1,128,256]{2,1,0:T(8,128)S(1)} %get-tuple-element.22), channel_id=1, source_target_pairs={{0,1},{1,0},{2,3},{3,2},{4,5},{5,4},{6,7},{7,6},{8,9},{9,8},{10,11... | collective-permute-start | bytes 393224 | tf_op jit(solution)/shard_map/ppermute | solution.py:19
  22.4 3.8 %collective-permute-start.7 = (f32[2,8,128]{2,1,0:T(8,128)S(1)}, f32[2,8,128]{2,1,0:T(8,128)S(1)}, u32[]{:S(2)}, u32[]{:S(2)}) collective-permute-start(f32[2,8,128]{2,1,0:T(8,128)S(1)} %get-tuple-element.17), channel_id=1, source_target_pairs={{0,2},{1,3},{2,0},{3,1},{4,6},{5,7},{6,4},{7,5},{8,10},{9,11},{10,... | collective-permute-start | bytes 24584 | tf_op jit(solution)/shard_map/ppermute | solution.py:19
  23.3 3.1 %collective-permute-start.8 = (f32[2,8,128]{2,1,0:T(8,128)S(1)}, f32[2,8,128]{2,1,0:T(8,128)S(1)}, u32[]{:S(2)}, u32[]{:S(2)}) collective-permute-start(f32[2,8,128]{2,1,0:T(8,128)S(1)} %get-tuple-element.18), channel_id=1, source_target_pairs={{0,3},{1,2},{2,1},{3,0},{4,7},{5,6},{6,5},{7,4},{8,11},{9,10},{10,... | collective-permute-start | bytes 24584 | tf_op jit(solution)/shard_map/ppermute | solution.py:19
  24.1 2.3 %collective-permute-start.9 = (f32[2,8,128]{2,1,0:T(8,128)S(1)}, f32[2,8,128]{2,1,0:T(8,128)S(1)}, u32[]{:S(2)}, u32[]{:S(2)}) collective-permute-start(f32[2,8,128]{2,1,0:T(8,128)S(1)} %get-tuple-element.19), channel_id=1, source_target_pairs={{0,1},{1,0},{2,3},{3,2},{4,5},{5,4},{6,7},{7,6},{8,9},{9,8},{10,11... | collective-permute-start | bytes 24584 | tf_op jit(solution)/shard_map/ppermute | solution.py:19
  26.7 3.8 %collective-permute-start.11 = (f32[8,512]{1,0:T(8,128)S(1)}, f32[8,512]{1,0:T(8,128)S(1)}, u32[]{:S(2)}, u32[]{:S(2)}) collective-permute-start(f32[8,512]{1,0:T(8,128)S(1)} %shard_map.68), channel_id=1, source_target_pairs={{0,2},{1,3},{2,0},{3,1},{4,6},{5,7},{6,4},{7,5},{8,10},{9,11},{10,... | collective-permute-start | bytes 49160 | tf_op jit(solution)/shard_map/ppermute | solution.py:19
  28.1 3.3 %collective-permute-start.12 = (f32[8,512]{1,0:T(8,128)S(1)}, f32[8,512]{1,0:T(8,128)S(1)}, u32[]{:S(2)}, u32[]{:S(2)}) collective-permute-start(f32[8,512]{1,0:T(8,128)S(1)} %shard_map.68), channel_id=1, source_target_pairs={{0,3},{1,2},{2,1},{3,0},{4,7},{5,6},{6,5},{7,4},{8,11},{9,10},{10,... | collective-permute-start | bytes 49160 | tf_op jit(solution)/shard_map/ppermute | solution.py:19
  28.1 3.3 %collective-permute-start.13 = (f32[8,512]{1,0:T(8,128)S(1)}, f32[8,512]{1,0:T(8,128)S(1)}, u32[]{:S(2)}, u32[]{:S(2)}) collective-permute-start(f32[8,512]{1,0:T(8,128)S(1)} %shard_map.68), channel_id=1, source_target_pairs={{0,1},{1,0},{2,3},{3,2},{4,5},{5,4},{6,7},{7,6},{8,9},{9,8},{10,11... | collective-permute-start | bytes 49160 | tf_op jit(solution)/shard_map/ppermute | solution.py:19

commit v27 on v24

--- a/solution.py
+++ b/solution.py
@@ -214,11 +214,11 @@
 
     far = [CORES * x for x in range(1, size // CORES)]
     arrays = (activations, out_grads, proj_in.T, proj_out.T, lengths)
-    far_other, far_own = project(*arrays, [[step ^ 1 for step in far], far], share, 4, 512, COST, [own_tests])
+    far_other, far_own = project(*arrays, [[step ^ 1 for step in far], far], share, 5, 512, COST, [own_tests])
     far_sum = far_own + xor_permute(far_other, "tensor", size, 1)
     sums = [xor_permute(far_sum[i * share : (i + 1) * share], "tensor", size, step) for i, step in enumerate(far)]
     here = xor_permute(tests[1][0][:16, :128], "tensor", size, 1)
-    near_other, near_own = project(*arrays, [[1], [0]], share, 4, 512, LATER, [far_sum, here])
+    near_other, near_own = project(*arrays, [[1], [0]], share, 3, 512, LATER, [far_sum, here])
     late = tests[2][0][: near_other.shape[1], : near_other.shape[2]].astype(jnp.float32)
     pieces = [near_other[k : k + 1] for k in range(share)]
     pieces[0] = pieces[0] + 0.0 * late[None]

time: 31.7 us -> 32.2 us (1.016)
  Pallas kernels: 12.5 us -> 13.2 us
  waiting for transfers between devices: 6.34 us -> 5.79 us
    pallas_call x2, Pallas kernels: 10.6 us -> 11.3 us  [project(): pl.pallas_call(functools.partial(project_kernel, steps, share, ahead, pie...]
    ppermute x3, waiting for transfers between devices: 2.69 us -> 2 us  [shift(): lax.ppermute(value, 'dp', [(i, (i + step) % groups) for i in range(groups)])]
    ppermute x3, starting transfers between devices: 5.33 us -> 5.66 us  [shift(): lax.ppermute(value, 'dp', [(i, (i + step) % groups) for i in range(groups)])]
  transfers between devices with their start and end apart: 14 -> 14, of which waited for: 8 -> 8; matrix products, arithmetic and copies ran while one was open for 0% -> 0% of each run, Pallas kernels for 35% -> 37%
where the time goes in v27:
time: 32.2 us; the launch traced here: 32 us
  Pallas kernels  13.2 us (41%)
  starting transfers between devices  12.2 us (38%)
  waiting for transfers between devices  5.79 us (18%)
  other arithmetic  0.7 us (2%)
    pallas_call x2, Pallas kernels, project(): pl.pallas_call(functools.partial(project_kernel, steps, share, ahead, pie...  11.3 us
    ppermute x11, starting transfers between devices, xor_permute(): return lax.ppermute(value, axis, [(i, i ^ step) for i in range(size)])  6.56 us
    ppermute x3, starting transfers between devices, shift(): lax.ppermute(value, 'dp', [(i, (i + step) % groups) for i in range(groups)])  5.66 us
    ppermute x11, waiting for transfers between devices, xor_permute(): return lax.ppermute(value, axis, [(i, i ^ step) for i in range(size)])  3.79 us
    ppermute x3, waiting for transfers between devices, shift(): lax.ppermute(value, 'dp', [(i, (i + step) % groups) for i in range(groups)])  2 us
    pallas_call x1, Pallas kernels, cut_tests(): pl.pallas_call(cut_kernel, out_shape=jax.ShapeDtypeStruct((rows, width //...  0.96 us
  transfers between devices with their start and end apart: 14, of which 8 were waited for; matrix products, arithmetic and copies ran while one was open for 0% of the time, Pallas kernels for 37%

profile of v27, /device:TPU:0, one launch (start us, length us, event | category | flops | bytes accessed | tf_op | source)
XLA Modules:
  0.0 32.0 jit_solution(12054366111182076947)
XLA Ops:
  0.0 1.0 %shard_map.64.refs_0_.refs_4_ = bf16[128,1024]{1,0:T(8,128)(2,1)S(1)} custom-call(bf16[128,4096]{1,0:T(8,128)(2,1)} %tests.1), custom_call_target="tpu_custom_call" | custom-call | tf_op jit(solution)/shard_map/pallas_call | solution.py:32
  1.0 3.1 %collective-permute-start.1 = (bf16[128,1024]{1,0:T(8,128)(2,1)S(1)}, bf16[128,1024]{1,0:T(8,128)(2,1)S(1)}, u32[]{:S(2)}, u32[]{:S(2)}) collective-permute-start(bf16[128,1024]{1,0:T(8,128)(2,1)S(1)} %shard_map.64.refs_0_.refs_4_), channel_id=1, source_target_pairs={{0,4},{4,8},{8,12},{12,0},{1,5},{5,9},{9,13},{13,1},{2,6},{6,10},{... | collective-permute-start | bytes 786440 | tf_op jit(solution)/shard_map/ppermute | solution.py:197
  4.0 5.6 %shard_map.65 = (f32[2,128,256]{2,1,0:T(8,128)S(1)}, f32[2,128,256]{2,1,0:T(8,128)S(1)}) custom-call(bf16[8,256,1024]{2,1,0:T(8,128)(2,1)} %act.3, bf16[8,256,3584]{2,1,0:T(8,128)(2,1)} %og.3, bf16[64,1024]{1,0:T(8,128)(2,1)} %bitcast.6, bf16[64,3584]{1,0:T(8,128)(2,1)} %bitcast.4, s32[8]{0:T(128)} %lens.3, bf16[128,1024]{1,0:T(8,128)(2,1)S(1)} %shard_map.64.refs_0_.refs_4_), custom_call_target="tpu_custom_call" | custom-call | flops 4294967296 | bytes 16777216 | tf_op jit(solution)/shard_map/pallas_call | solution.py:110
  9.6 0.1 collective-permute-start
  9.7 2.1 %collective-permute-start.3 = (bf16[128,1024]{1,0:T(8,128)(2,1)S(1)}, bf16[128,1024]{1,0:T(8,128)(2,1)S(1)}, u32[]{:S(2)}, u32[]{:S(2)}) collective-permute-start(bf16[128,1024]{1,0:T(8,128)(2,1)S(1)} %shard_map.64.refs_0_.refs_4_), channel_id=1, source_target_pairs={{0,12},{4,0},{8,4},{12,8},{1,13},{5,1},{9,5},{13,9},{2,14},{6,2},{... | collective-permute-start | bytes 786440 | tf_op jit(solution)/shard_map/ppermute | solution.py:197
  11.8 0.6 %collective-permute-done.1.refs_5_ = bf16[128,1024]{1,0:T(8,128)(2,1)S(1)} collective-permute-done((bf16[128,1024]{1,0:T(8,128)(2,1)S(1)}, bf16[128,1024]{1,0:T(8,128)(2,1)S(1)}, u32[]{:S(2)}, u32[]{:S(2)}) %collective-permute-start.1) | collective-permute-done | bytes 262176 | tf_op jit(solution)/shard_map/ppermute | solution.py:197
  12.4 0.0 collective-permute-start.2
  12.4 0.0 collective-permute-done
  12.4 1.6 %collective-permute-start.6 = (f32[2,128,256]{2,1,0:T(8,128)S(1)}, f32[2,128,256]{2,1,0:T(8,128)S(1)}, u32[]{:S(2)}, u32[]{:S(2)}) collective-permute-start(f32[2,128,256]{2,1,0:T(8,128)S(1)} %add.15.refs_0_), channel_id=1, source_target_pairs={{0,2},{1,3},{2,0},{3,1},{4,6},{5,7},{6,4},{7,5},{8,10},{9,11},{10,... | collective-permute-start | bytes 786440 | tf_op jit(solution)/shard_map/ppermute | solution.py:19
  14.0 0.5 %collective-permute-start.10 = (bf16[128,1024]{1,0:T(8,128)(2,1)S(1)}, bf16[128,1024]{1,0:T(8,128)(2,1)S(1)}, u32[]{:S(2)}, u32[]{:S(2)}) collective-permute-start(bf16[128,1024]{1,0:T(8,128)(2,1)S(1)} %collective-permute-done.1.refs_5_), channel_id=1, source_target_pairs={{0,4},{4,8},{8,12},{12,0},{1,5},{5,9},{9,13},{13,1},{2,6},{6,10},{... | collective-permute-start | bytes 786440 | tf_op jit(solution)/shard_map/ppermute | solution.py:197
  14.5 5.7 %shard_map.66 = (f32[2,128,256]{2,1,0:T(8,128)S(1)}, f32[2,128,256]{2,1,0:T(8,128)S(1)}) custom-call(bf16[8,256,1024]{2,1,0:T(8,128)(2,1)} %act.3, bf16[8,256,3584]{2,1,0:T(8,128)(2,1)} %og.3, bf16[64,1024]{1,0:T(8,128)(2,1)} %bitcast.7, bf16[64,3584]{1,0:T(8,128)(2,1)} %bitcast.5, s32[8]{0:T(128)} %lens.3, f32[2,128,256]{2,1,0:T(8,128)S(1)} %add.15.refs_0_, ...), custom_call_target="tpu_custom_call" | custom-call | flops 1024 | bytes 4 | tf_op jit(solution)/shard_map/pallas_call | solution.py:110
  20.2 0.0 collective-permute-done.3.refs_6_
  20.3 0.1 collective-permute-start.4
  20.3 0.5 %collective-permute-start.5 = (f32[1,128,256]{2,1,0:T(8,128)S(1)}, f32[1,128,256]{2,1,0:T(8,128)S(1)}, u32[]{:S(2)}, u32[]{:S(2)}) collective-permute-start(f32[1,128,256]{2,1,0:T(8,128)S(1)} %get-tuple-element.22), channel_id=1, source_target_pairs={{0,1},{1,0},{2,3},{3,2},{4,5},{5,4},{6,7},{7,6},{8,9},{9,8},{10,11... | collective-permute-start | bytes 393224 | tf_op jit(solution)/shard_map/ppermute | solution.py:19
  20.8 0.8 %collective-permute-done.4 = f32[1,128,256]{2,1,0:T(8,128)S(1)} collective-permute-done((f32[1,128,256]{2,1,0:T(8,128)S(1)}, f32[1,128,256]{2,1,0:T(8,128)S(1)}, u32[]{:S(2)}, u32[]{:S(2)}) %collective-permute-start.4) | collective-permute-done | bytes 131104 | tf_op jit(solution)/shard_map/ppermute | solution.py:19
  21.7 0.2 collective-permute-done.5
  21.9 0.0 collective-permute-done.6.refs_2_
  21.9 0.5 %shard_map.67 = (f32[2,8,128]{2,1,0:T(8,128)S(1)}, f32[2,8,128]{2,1,0:T(8,128)S(1)}, f32[2,8,128]{2,1,0:T(8,128)S(1)}, f32[2,8,128]{2,1,0:T(8,128)S(1)}) custom-call(f32[2,128,256]{2,1,0:T(8,128)S(1)} %get-tuple-element.15.refs_0_, f32[2,128,256]{2,1,0:T(8,128)S(1)} %pad_maximum_fusion.refs_1_, f32[2,128,256]{2,1,0:T(8,128)S(1)} %collective-permute-done.6.refs_2_), custom_call_target="tpu_custom_call" | custom-call | tf_op jit(solution)/shard_map/pallas_call | solution.py:157
  22.4 0.9 %collective-permute-start.7 = (f32[2,8,128]{2,1,0:T(8,128)S(1)}, f32[2,8,128]{2,1,0:T(8,128)S(1)}, u32[]{:S(2)}, u32[]{:S(2)}) collective-permute-start(f32[2,8,128]{2,1,0:T(8,128)S(1)} %get-tuple-element.17), channel_id=1, source_target_pairs={{0,2},{1,3},{2,0},{3,1},{4,6},{5,7},{6,4},{7,5},{8,10},{9,11},{10,... | collective-permute-start | bytes 24584 | tf_op jit(solution)/shard_map/ppermute | solution.py:19
  23.3 0.9 %collective-permute-start.8 = (f32[2,8,128]{2,1,0:T(8,128)S(1)}, f32[2,8,128]{2,1,0:T(8,128)S(1)}, u32[]{:S(2)}, u32[]{:S(2)}) collective-permute-start(f32[2,8,128]{2,1,0:T(8,128)S(1)} %get-tuple-element.18), channel_id=1, source_target_pairs={{0,3},{1,2},{2,1},{3,0},{4,7},{5,6},{6,5},{7,4},{8,11},{9,10},{10,... | collective-permute-start | bytes 24584 | tf_op jit(solution)/shard_map/ppermute | solution.py:19
  24.1 0.5 %collective-permute-start.9 = (f32[2,8,128]{2,1,0:T(8,128)S(1)}, f32[2,8,128]{2,1,0:T(8,128)S(1)}, u32[]{:S(2)}, u32[]{:S(2)}) collective-permute-start(f32[2,8,128]{2,1,0:T(8,128)S(1)} %get-tuple-element.19), channel_id=1, source_target_pairs={{0,1},{1,0},{2,3},{3,2},{4,5},{5,4},{6,7},{7,6},{8,9},{9,8},{10,11... | collective-permute-start | bytes 24584 | tf_op jit(solution)/shard_map/ppermute | solution.py:19
  24.6 1.4 %collective-permute-done.10.refs_7_ = bf16[128,1024]{1,0:T(8,128)(2,1)S(1)} collective-permute-done((bf16[128,1024]{1,0:T(8,128)(2,1)S(1)}, bf16[128,1024]{1,0:T(8,128)(2,1)S(1)}, u32[]{:S(2)}, u32[]{:S(2)}) %collective-permute-start.10) | collective-permute-done | bytes 262176 | tf_op jit(solution)/shard_map/ppermute | solution.py:197
  26.1 0.1 collective-permute-done.7.refs_0_
  26.1 0.3 collective-permute-done.8.refs_1_
  26.4 0.0 collective-permute-done.9.refs_2_
  26.4 0.4 %shard_map.68 = f32[8,512]{1,0:T(8,128)S(1)} custom-call(f32[2,8,128]{2,1,0:T(8,128)S(1)} %collective-permute-done.7.refs_0_, f32[2,8,128]{2,1,0:T(8,128)S(1)} %collective-permute-done.8.refs_1_, f32[2,8,128]{2,1,0:T(8,128)S(1)} %collective-permute-done.9.refs_2_, f32[2,8,128]{2,1,0:T(8,128)S(1)} %get-tuple-element.20.refs_3_, ...), custom_call_target="tpu_custom_call" | custom-call | tf_op jit(solution)/shard_map/pallas_call | solution.py:185
  26.8 1.2 %collective-permute-start.11 = (f32[8,512]{1,0:T(8,128)S(1)}, f32[8,512]{1,0:T(8,128)S(1)}, u32[]{:S(2)}, u32[]{:S(2)}) collective-permute-start(f32[8,512]{1,0:T(8,128)S(1)} %shard_map.68), channel_id=1, source_target_pairs={{0,2},{1,3},{2,0},{3,1},{4,6},{5,7},{6,4},{7,5},{8,10},{9,11},{10,... | collective-permute-start | bytes 49160 | tf_op jit(solution)/shard_map/ppermute | solution.py:19
  28.0 0.2 collective-permute-start.12
  28.3 0.7 %collective-permute-start.13 = (f32[8,512]{1,0:T(8,128)S(1)}, f32[8,512]{1,0:T(8,128)S(1)}, u32[]{:S(2)}, u32[]{:S(2)}) collective-permute-start(f32[8,512]{1,0:T(8,128)S(1)} %shard_map.68), channel_id=1, source_target_pairs={{0,1},{1,0},{2,3},{3,2},{4,5},{5,4},{6,7},{7,6},{8,9},{9,8},{10,11... | collective-permute-start | bytes 49160 | tf_op jit(solution)/shard_map/ppermute | solution.py:19
  29.0 1.6 %collective-permute-done.11 = f32[8,512]{1,0:T(8,128)S(1)} collective-permute-done((f32[8,512]{1,0:T(8,128)S(1)}, f32[8,512]{1,0:T(8,128)S(1)}, u32[]{:S(2)}, u32[]{:S(2)}) %collective-permute-start.11) | collective-permute-done | bytes 16416 | tf_op jit(solution)/shard_map/ppermute | solution.py:19
  30.6 0.8 %collective-permute-done.12 = f32[8,512]{1,0:T(8,128)S(1)} collective-permute-done((f32[8,512]{1,0:T(8,128)S(1)}, f32[8,512]{1,0:T(8,128)S(1)}, u32[]{:S(2)}, u32[]{:S(2)}) %collective-permute-start.12) | collective-permute-done | bytes 16416 | tf_op jit(solution)/shard_map/ppermute | solution.py:19
  31.4 0.6 %add_add_fusion = f32[8,512]{1,0:T(8,128)} fusion(f32[8,512]{1,0:T(8,128)S(1)} %shard_map.68, f32[8,512]{1,0:T(8,128)S(1)} %collective-permute-done.13, f32[8,512]{1,0:T(8,128)S(1)} %collective-permute-done.11, f32[8,512]{1,0:T(8,128)S(1)} %collective-permute-done.12), kind=kLoop, calls=%fused_computation.2 | loop fusion | flops 12288 | bytes 81920 | tf_op jit(solution)/shard_map/add | solution.py:233
  (6 shorter events, 0.1 us)
Async XLA Ops:
  1.0 11.4 %collective-permute-start.1 = (bf16[128,1024]{1,0:T(8,128)(2,1)S(1)}, bf16[128,1024]{1,0:T(8,128)(2,1)S(1)}, u32[]{:S(2)}, u32[]{:S(2)}) collective-permute-start(bf16[128,1024]{1,0:T(8,128)(2,1)S(1)} %shard_map.64.refs_0_.refs_4_), channel_id=1, source_target_pairs={{0,4},{4,8},{8,12},{12,0},{1,5},{5,9},{9,13},{13,1},{2,6},{6,10},{... | collective-permute-start | bytes 786440 | tf_op jit(solution)/shard_map/ppermute | solution.py:197
  9.6 2.7 %collective-permute-start = (f32[2,128,256]{2,1,0:T(8,128)S(1)}, f32[2,128,256]{2,1,0:T(8,128)S(1)}, u32[]{:S(2)}, u32[]{:S(2)}) collective-permute-start(f32[2,128,256]{2,1,0:T(8,128)S(1)} %get-tuple-element.14), channel_id=1, source_target_pairs={{0,1},{1,0},{2,3},{3,2},{4,5},{5,4},{6,7},{7,6},{8,9},{9,8},{10,11... | collective-permute-start | bytes 786440 | tf_op jit(solution)/shard_map/ppermute | solution.py:19
  9.7 10.5 %collective-permute-start.3 = (bf16[128,1024]{1,0:T(8,128)(2,1)S(1)}, bf16[128,1024]{1,0:T(8,128)(2,1)S(1)}, u32[]{:S(2)}, u32[]{:S(2)}) collective-permute-start(bf16[128,1024]{1,0:T(8,128)(2,1)S(1)} %shard_map.64.refs_0_.refs_4_), channel_id=1, source_target_pairs={{0,12},{4,0},{8,4},{12,8},{1,13},{5,1},{9,5},{13,9},{2,14},{6,2},{... | collective-permute-start | bytes 786440 | tf_op jit(solution)/shard_map/ppermute | solution.py:197
  12.4 2.1 %collective-permute-start.2 = (bf16[16,128]{1,0:T(8,128)(2,1)S(1)}, bf16[16,128]{1,0:T(8,128)(2,1)S(1)}, u32[]{:S(2)}, u32[]{:S(2)}) collective-permute-start(bf16[16,128]{1,0:T(8,128)(2,1)S(1)} %slice.16), channel_id=1, source_target_pairs={{0,1},{1,0},{2,3},{3,2},{4,5},{5,4},{6,7},{7,6},{8,9},{9,8},{10,11... | collective-permute-start | bytes 12296 | tf_op jit(solution)/shard_map/ppermute | solution.py:19
  12.4 9.5 %collective-permute-start.6 = (f32[2,128,256]{2,1,0:T(8,128)S(1)}, f32[2,128,256]{2,1,0:T(8,128)S(1)}, u32[]{:S(2)}, u32[]{:S(2)}) collective-permute-start(f32[2,128,256]{2,1,0:T(8,128)S(1)} %add.15.refs_0_), channel_id=1, source_target_pairs={{0,2},{1,3},{2,0},{3,1},{4,6},{5,7},{6,4},{7,5},{8,10},{9,11},{10,... | collective-permute-start | bytes 786440 | tf_op jit(solution)/shard_map/ppermute | solution.py:19
  14.0 12.1 %collective-permute-start.10 = (bf16[128,1024]{1,0:T(8,128)(2,1)S(1)}, bf16[128,1024]{1,0:T(8,128)(2,1)S(1)}, u32[]{:S(2)}, u32[]{:S(2)}) collective-permute-start(bf16[128,1024]{1,0:T(8,128)(2,1)S(1)} %collective-permute-done.1.refs_5_), channel_id=1, source_target_pairs={{0,4},{4,8},{8,12},{12,0},{1,5},{5,9},{9,13},{13,1},{2,6},{6,10},{... | collective-permute-start | bytes 786440 | tf_op jit(solution)/shard_map/ppermute | solution.py:197
  20.3 1.4 %collective-permute-start.4 = (f32[1,128,256]{2,1,0:T(8,128)S(1)}, f32[1,128,256]{2,1,0:T(8,128)S(1)}, u32[]{:S(2)}, u32[]{:S(2)}) collective-permute-start(f32[1,128,256]{2,1,0:T(8,128)S(1)} %get-tuple-element.21), channel_id=1, source_target_pairs={{0,1},{1,0},{2,3},{3,2},{4,5},{5,4},{6,7},{7,6},{8,9},{9,8},{10,11... | collective-permute-start | bytes 393224 | tf_op jit(solution)/shard_map/ppermute | solution.py:19
  20.3 1.5 %collective-permute-start.5 = (f32[1,128,256]{2,1,0:T(8,128)S(1)}, f32[1,128,256]{2,1,0:T(8,128)S(1)}, u32[]{:S(2)}, u32[]{:S(2)}) collective-permute-start(f32[1,128,256]{2,1,0:T(8,128)S(1)} %get-tuple-element.22), channel_id=1, source_target_pairs={{0,1},{1,0},{2,3},{3,2},{4,5},{5,4},{6,7},{7,6},{8,9},{9,8},{10,11... | collective-permute-start | bytes 393224 | tf_op jit(solution)/shard_map/ppermute | solution.py:19
  22.4 3.7 %collective-permute-start.7 = (f32[2,8,128]{2,1,0:T(8,128)S(1)}, f32[2,8,128]{2,1,0:T(8,128)S(1)}, u32[]{:S(2)}, u32[]{:S(2)}) collective-permute-start(f32[2,8,128]{2,1,0:T(8,128)S(1)} %get-tuple-element.17), channel_id=1, source_target_pairs={{0,2},{1,3},{2,0},{3,1},{4,6},{5,7},{6,4},{7,5},{8,10},{9,11},{10,... | collective-permute-start | bytes 24584 | tf_op jit(solution)/shard_map/ppermute | solution.py:19
  23.3 3.1 %collective-permute-start.8 = (f32[2,8,128]{2,1,0:T(8,128)S(1)}, f32[2,8,128]{2,1,0:T(8,128)S(1)}, u32[]{:S(2)}, u32[]{:S(2)}) collective-permute-start(f32[2,8,128]{2,1,0:T(8,128)S(1)} %get-tuple-element.18), channel_id=1, source_target_pairs={{0,3},{1,2},{2,1},{3,0},{4,7},{5,6},{6,5},{7,4},{8,11},{9,10},{10,... | collective-permute-start | bytes 24584 | tf_op jit(solution)/shard_map/ppermute | solution.py:19
  24.1 2.3 %collective-permute-start.9 = (f32[2,8,128]{2,1,0:T(8,128)S(1)}, f32[2,8,128]{2,1,0:T(8,128)S(1)}, u32[]{:S(2)}, u32[]{:S(2)}) collective-permute-start(f32[2,8,128]{2,1,0:T(8,128)S(1)} %get-tuple-element.19), channel_id=1, source_target_pairs={{0,1},{1,0},{2,3},{3,2},{4,5},{5,4},{6,7},{7,6},{8,9},{9,8},{10,11... | collective-permute-start | bytes 24584 | tf_op jit(solution)/shard_map/ppermute | solution.py:19
  26.8 3.8 %collective-permute-start.11 = (f32[8,512]{1,0:T(8,128)S(1)}, f32[8,512]{1,0:T(8,128)S(1)}, u32[]{:S(2)}, u32[]{:S(2)}) collective-permute-start(f32[8,512]{1,0:T(8,128)S(1)} %shard_map.68), channel_id=1, source_target_pairs={{0,2},{1,3},{2,0},{3,1},{4,6},{5,7},{6,4},{7,5},{8,10},{9,11},{10,... | collective-permute-start | bytes 49160 | tf_op jit(solution)/shard_map/ppermute | solution.py:19
  28.0 3.3 %collective-permute-start.12 = (f32[8,512]{1,0:T(8,128)S(1)}, f32[8,512]{1,0:T(8,128)S(1)}, u32[]{:S(2)}, u32[]{:S(2)}) collective-permute-start(f32[8,512]{1,0:T(8,128)S(1)} %shard_map.68), channel_id=1, source_target_pairs={{0,3},{1,2},{2,1},{3,0},{4,7},{5,6},{6,5},{7,4},{8,11},{9,10},{10,... | collective-permute-start | bytes 49160 | tf_op jit(solution)/shard_map/ppermute | solution.py:19
  28.3 3.1 %collective-permute-start.13 = (f32[8,512]{1,0:T(8,128)S(1)}, f32[8,512]{1,0:T(8,128)S(1)}, u32[]{:S(2)}, u32[]{:S(2)}) collective-permute-start(f32[8,512]{1,0:T(8,128)S(1)} %shard_map.68), channel_id=1, source_target_pairs={{0,1},{1,0},{2,3},{3,2},{4,5},{5,4},{6,7},{7,6},{8,9},{9,8},{10,11... | collective-permute-start | bytes 49160 | tf_op jit(solution)/shard_map/ppermute | solution.py:19

commit v28 on v24

--- a/solution.py
+++ b/solution.py
@@ -126,15 +126,15 @@
 
 
 def unit_kernel(share, rank, size, *refs):
-    parts, outs = refs[: -2 - size], refs[-2 - size : -2]
+    singles, parts, outs = refs[:share], refs[share : -2 - size], refs[-2 - size : -2]
     pairs, held = refs[-2:]
     me = lax.axis_index("tensor")
     rows = rank * rank // 128
     span = rows // size
     dot = functools.partial(lax.dot_general, dimension_numbers=NT, preferred_element_type=jnp.float32)
     for k in range(share):
-        full = parts[0][k]
-        for part in parts[1:]:
+        full = singles[k][0]
+        for part in parts:
             full = full + part[k]
         high = full.astype(jnp.bfloat16)
         low = (full - high.astype(jnp.float32)).astype(jnp.bfloat16)
@@ -152,16 +152,16 @@
             outs[step][k] = held[k, me ^ step]
 
 
-def units(parts, share, rank, size):
+def units(parts, singles, share, rank, size):
     span = rank * rank // 128 // size
     return pl.pallas_call(
         functools.partial(unit_kernel, share, rank, size),
         out_shape=[jax.ShapeDtypeStruct((share, span, 128), jnp.float32)] * size,
-        in_specs=[VMEM] * len(parts),
+        in_specs=[VMEM] * (share + len(parts)),
         out_specs=[VMEM] * size,
         scratch_shapes=[pltpu.VMEM((share, rank, rank), jnp.float32), pltpu.VMEM((share, size, span, 128), jnp.float32)],
         compiler_params=SMALL,
-    )(*parts)
+    )(*singles, *parts)
 
 
 def score_kernel(share, steps, origins, *refs):
@@ -222,9 +222,9 @@
     late = tests[2][0][: near_other.shape[1], : near_other.shape[2]].astype(jnp.float32)
     pieces = [near_other[k : k + 1] for k in range(share)]
     pieces[0] = pieces[0] + 0.0 * late[None]
-    arrived = jnp.concatenate([xor_permute(one, "tensor", size, 1) for one in pieces])
-
-    unit_outs = units([near_own, arrived] + sums, share, rank, size)
+    arrived = [xor_permute(one, "tensor", size, 1) for one in pieces]
+
+    unit_outs = units([near_own] + sums, arrived, share, rank, size)
     unit_parts = exchange(unit_outs, size)
     part = score(unit_parts, tests, share)
     parts = exchange([part] * size, size)

time: 31.7 us -> 31.7 us (level)
  no operation moved by 1% of the time
where the time goes in v28:
time: 31.7 us; the launch traced here: 31.5 us
  Pallas kernels  12.5 us (39%)
  starting transfers between devices  11.9 us (38%)
  waiting for transfers between devices  6.36 us (20%)
  other arithmetic  0.68 us (2%)
    pallas_call x2, Pallas kernels, project(): pl.pallas_call(functools.partial(project_kernel, steps, share, ahead, pie...  10.6 us
    ppermute x11, starting transfers between devices, xor_permute(): return lax.ppermute(value, axis, [(i, i ^ step) for i in range(size)])  6.57 us
    ppermute x3, starting transfers between devices, shift(): lax.ppermute(value, 'dp', [(i, (i + step) % groups) for i in range(groups)])  5.33 us
    ppermute x11, waiting for transfers between devices, xor_permute(): return lax.ppermute(value, axis, [(i, i ^ step) for i in range(size)])  3.67 us
    ppermute x3, waiting for transfers between devices, shift(): lax.ppermute(value, 'dp', [(i, (i + step) % groups) for i in range(groups)])  2.69 us
    pallas_call x1, Pallas kernels, cut_tests(): pl.pallas_call(cut_kernel, out_shape=jax.ShapeDtypeStruct((rows, width //...  0.96 us
  transfers between devices with their start and end apart: 14, of which 8 were waited for; matrix products, arithmetic and copies ran while one was open for 0% of the time, Pallas kernels for 35%

profile of v28, /device:TPU:0, one launch (start us, length us, event | category | flops | bytes accessed | tf_op | source)
XLA Modules:
  0.0 31.5 jit_solution(8971264163920650917)
XLA Ops:
  0.0 1.0 %shard_map.64.refs_0_.refs_4_ = bf16[128,1024]{1,0:T(8,128)(2,1)S(1)} custom-call(bf16[128,4096]{1,0:T(8,128)(2,1)} %tests.1), custom_call_target="tpu_custom_call" | custom-call | tf_op jit(solution)/shard_map/pallas_call | solution.py:32
  1.0 3.1 %collective-permute-start.1 = (bf16[128,1024]{1,0:T(8,128)(2,1)S(1)}, bf16[128,1024]{1,0:T(8,128)(2,1)S(1)}, u32[]{:S(2)}, u32[]{:S(2)}) collective-permute-start(bf16[128,1024]{1,0:T(8,128)(2,1)S(1)} %shard_map.64.refs_0_.refs_4_), channel_id=1, source_target_pairs={{0,4},{4,8},{8,12},{12,0},{1,5},{5,9},{9,13},{13,1},{2,6},{6,10},{... | collective-permute-start | bytes 786440 | tf_op jit(solution)/shard_map/ppermute | solution.py:197
  4.0 5.3 %shard_map.65 = (f32[2,128,256]{2,1,0:T(8,128)S(1)}, f32[2,128,256]{2,1,0:T(8,128)S(1)}) custom-call(bf16[8,256,1024]{2,1,0:T(8,128)(2,1)} %act.3, bf16[8,256,3584]{2,1,0:T(8,128)(2,1)} %og.3, bf16[64,1024]{1,0:T(8,128)(2,1)} %bitcast.6, bf16[64,3584]{1,0:T(8,128)(2,1)} %bitcast.4, s32[8]{0:T(128)} %lens.3, bf16[128,1024]{1,0:T(8,128)(2,1)S(1)} %shard_map.64.refs_0_.refs_4_), custom_call_target="tpu_custom_call" | custom-call | flops 4294967296 | bytes 16777216 | tf_op jit(solution)/shard_map/pallas_call | solution.py:110
  9.4 0.1 collective-permute-start
  9.4 2.1 %collective-permute-start.3 = (bf16[128,1024]{1,0:T(8,128)(2,1)S(1)}, bf16[128,1024]{1,0:T(8,128)(2,1)S(1)}, u32[]{:S(2)}, u32[]{:S(2)}) collective-permute-start(bf16[128,1024]{1,0:T(8,128)(2,1)S(1)} %shard_map.64.refs_0_.refs_4_), channel_id=1, source_target_pairs={{0,12},{4,0},{8,4},{12,8},{1,13},{5,1},{9,5},{13,9},{2,14},{6,2},{... | collective-permute-start | bytes 786440 | tf_op jit(solution)/shard_map/ppermute | solution.py:197
  11.5 0.8 %collective-permute-done.1.refs_5_ = bf16[128,1024]{1,0:T(8,128)(2,1)S(1)} collective-permute-done((bf16[128,1024]{1,0:T(8,128)(2,1)S(1)}, bf16[128,1024]{1,0:T(8,128)(2,1)S(1)}, u32[]{:S(2)}, u32[]{:S(2)}) %collective-permute-start.1) | collective-permute-done | bytes 262176 | tf_op jit(solution)/shard_map/ppermute | solution.py:197
  12.4 0.0 collective-permute-start.2
  12.4 0.0 collective-permute-done
  12.4 1.6 %collective-permute-start.6 = (f32[2,128,256]{2,1,0:T(8,128)S(1)}, f32[2,128,256]{2,1,0:T(8,128)S(1)}, u32[]{:S(2)}, u32[]{:S(2)}) collective-permute-start(f32[2,128,256]{2,1,0:T(8,128)S(1)} %add.15.refs_0_), channel_id=1, source_target_pairs={{0,2},{1,3},{2,0},{3,1},{4,6},{5,7},{6,4},{7,5},{8,10},{9,11},{10,... | collective-permute-start | bytes 786440 | tf_op jit(solution)/shard_map/ppermute | solution.py:19
  14.0 0.2 collective-permute-start.10
  14.1 5.3 %shard_map.66 = (f32[2,128,256]{2,1,0:T(8,128)S(1)}, f32[2,128,256]{2,1,0:T(8,128)S(1)}) custom-call(bf16[8,256,1024]{2,1,0:T(8,128)(2,1)} %act.3, bf16[8,256,3584]{2,1,0:T(8,128)(2,1)} %og.3, bf16[64,1024]{1,0:T(8,128)(2,1)} %bitcast.7, bf16[64,3584]{1,0:T(8,128)(2,1)} %bitcast.5, s32[8]{0:T(128)} %lens.3, f32[2,128,256]{2,1,0:T(8,128)S(1)} %add.15.refs_0_, ...), custom_call_target="tpu_custom_call" | custom-call | flops 1024 | bytes 4 | tf_op jit(solution)/shard_map/pallas_call | solution.py:110
  19.5 0.1 collective-permute-start.4
  19.6 0.4 %collective-permute-start.5 = (f32[1,128,256]{2,1,0:T(8,128)S(1)}, f32[1,128,256]{2,1,0:T(8,128)S(1)}, u32[]{:S(2)}, u32[]{:S(2)}) collective-permute-start(f32[1,128,256]{2,1,0:T(8,128)S(1)} %get-tuple-element.21), channel_id=1, source_target_pairs={{0,1},{1,0},{2,3},{3,2},{4,5},{5,4},{6,7},{7,6},{8,9},{9,8},{10,11... | collective-permute-start | bytes 393224 | tf_op jit(solution)/shard_map/ppermute | solution.py:19
  20.1 0.8 %collective-permute-done.4.refs_0_ = f32[1,128,256]{2,1,0:T(8,128)S(1)} collective-permute-done((f32[1,128,256]{2,1,0:T(8,128)S(1)}, f32[1,128,256]{2,1,0:T(8,128)S(1)}, u32[]{:S(2)}, u32[]{:S(2)}) %collective-permute-start.4) | collective-permute-done | bytes 131104 | tf_op jit(solution)/shard_map/ppermute | solution.py:19
  20.9 0.2 collective-permute-done.5.refs_1_
  21.1 0.1 collective-permute-done.6.refs_3_
  21.2 0.5 %shard_map.67 = (f32[2,8,128]{2,1,0:T(8,128)S(1)}, f32[2,8,128]{2,1,0:T(8,128)S(1)}, f32[2,8,128]{2,1,0:T(8,128)S(1)}, f32[2,8,128]{2,1,0:T(8,128)S(1)}) custom-call(f32[1,128,256]{2,1,0:T(8,128)S(1)} %collective-permute-done.4.refs_0_, f32[1,128,256]{2,1,0:T(8,128)S(1)} %collective-permute-done.5.refs_1_, f32[2,128,256]{2,1,0:T(8,128)S(1)} %get-tuple-element.16.refs_2_, ...), custom_call_target="tpu_custom_call" | custom-call | tf_op jit(solution)/shard_map/pallas_call | solution.py:157
  21.7 1.6 %collective-permute-start.7 = (f32[2,8,128]{2,1,0:T(8,128)S(1)}, f32[2,8,128]{2,1,0:T(8,128)S(1)}, u32[]{:S(2)}, u32[]{:S(2)}) collective-permute-start(f32[2,8,128]{2,1,0:T(8,128)S(1)} %get-tuple-element.17), channel_id=1, source_target_pairs={{0,2},{1,3},{2,0},{3,1},{4,6},{5,7},{6,4},{7,5},{8,10},{9,11},{10,... | collective-permute-start | bytes 24584 | tf_op jit(solution)/shard_map/ppermute | solution.py:19
  23.3 0.1 collective-permute-start.8
  23.4 0.6 %collective-permute-start.9 = (f32[2,8,128]{2,1,0:T(8,128)S(1)}, f32[2,8,128]{2,1,0:T(8,128)S(1)}, u32[]{:S(2)}, u32[]{:S(2)}) collective-permute-start(f32[2,8,128]{2,1,0:T(8,128)S(1)} %get-tuple-element.19), channel_id=1, source_target_pairs={{0,1},{1,0},{2,3},{3,2},{4,5},{5,4},{6,7},{7,6},{8,9},{9,8},{10,11... | collective-permute-start | bytes 24584 | tf_op jit(solution)/shard_map/ppermute | solution.py:19
  23.9 1.9 %collective-permute-done.10.refs_7_ = bf16[128,1024]{1,0:T(8,128)(2,1)S(1)} collective-permute-done((bf16[128,1024]{1,0:T(8,128)(2,1)S(1)}, bf16[128,1024]{1,0:T(8,128)(2,1)S(1)}, u32[]{:S(2)}, u32[]{:S(2)}) %collective-permute-start.10) | collective-permute-done | bytes 262176 | tf_op jit(solution)/shard_map/ppermute | solution.py:197
  25.8 0.0 collective-permute-done.7.refs_0_
  25.8 0.6 %collective-permute-done.8.refs_1_ = f32[2,8,128]{2,1,0:T(8,128)S(1)} collective-permute-done((f32[2,8,128]{2,1,0:T(8,128)S(1)}, f32[2,8,128]{2,1,0:T(8,128)S(1)}, u32[]{:S(2)}, u32[]{:S(2)}) %collective-permute-start.8) | collective-permute-done | bytes 8224 | tf_op jit(solution)/shard_map/ppermute | solution.py:19
  26.4 0.0 collective-permute-done.9.refs_2_
  26.4 0.4 %shard_map.68 = f32[8,512]{1,0:T(8,128)S(1)} custom-call(f32[2,8,128]{2,1,0:T(8,128)S(1)} %collective-permute-done.7.refs_0_, f32[2,8,128]{2,1,0:T(8,128)S(1)} %collective-permute-done.8.refs_1_, f32[2,8,128]{2,1,0:T(8,128)S(1)} %collective-permute-done.9.refs_2_, f32[2,8,128]{2,1,0:T(8,128)S(1)} %get-tuple-element.20.refs_3_, ...), custom_call_target="tpu_custom_call" | custom-call | tf_op jit(solution)/shard_map/pallas_call | solution.py:185
  26.7 1.0 %collective-permute-start.11 = (f32[8,512]{1,0:T(8,128)S(1)}, f32[8,512]{1,0:T(8,128)S(1)}, u32[]{:S(2)}, u32[]{:S(2)}) collective-permute-start(f32[8,512]{1,0:T(8,128)S(1)} %shard_map.68), channel_id=1, source_target_pairs={{0,2},{1,3},{2,0},{3,1},{4,6},{5,7},{6,4},{7,5},{8,10},{9,11},{10,... | collective-permute-start | bytes 49160 | tf_op jit(solution)/shard_map/ppermute | solution.py:19
  27.7 0.0 collective-permute-start.12
  27.7 1.2 %collective-permute-start.13 = (f32[8,512]{1,0:T(8,128)S(1)}, f32[8,512]{1,0:T(8,128)S(1)}, u32[]{:S(2)}, u32[]{:S(2)}) collective-permute-start(f32[8,512]{1,0:T(8,128)S(1)} %shard_map.68), channel_id=1, source_target_pairs={{0,1},{1,0},{2,3},{3,2},{4,5},{5,4},{6,7},{7,6},{8,9},{9,8},{10,11... | collective-permute-start | bytes 49160 | tf_op jit(solution)/shard_map/ppermute | solution.py:19
  28.9 1.6 %collective-permute-done.11 = f32[8,512]{1,0:T(8,128)S(1)} collective-permute-done((f32[8,512]{1,0:T(8,128)S(1)}, f32[8,512]{1,0:T(8,128)S(1)}, u32[]{:S(2)}, u32[]{:S(2)}) %collective-permute-start.11) | collective-permute-done | bytes 16416 | tf_op jit(solution)/shard_map/ppermute | solution.py:19
  30.5 0.4 %collective-permute-done.12 = f32[8,512]{1,0:T(8,128)S(1)} collective-permute-done((f32[8,512]{1,0:T(8,128)S(1)}, f32[8,512]{1,0:T(8,128)S(1)}, u32[]{:S(2)}, u32[]{:S(2)}) %collective-permute-start.12) | collective-permute-done | bytes 16416 | tf_op jit(solution)/shard_map/ppermute | solution.py:19
  30.9 0.0 collective-permute-done.13
  30.9 0.6 %add_add_fusion = f32[8,512]{1,0:T(8,128)} fusion(f32[8,512]{1,0:T(8,128)S(1)} %shard_map.68, f32[8,512]{1,0:T(8,128)S(1)} %collective-permute-done.13, f32[8,512]{1,0:T(8,128)S(1)} %collective-permute-done.11, f32[8,512]{1,0:T(8,128)S(1)} %collective-permute-done.12), kind=kLoop, calls=%fused_computation.1 | loop fusion | flops 12288 | bytes 81920 | tf_op jit(solution)/shard_map/add | solution.py:233
  (5 shorter events, 0.1 us)
Async XLA Ops:
  1.0 11.4 %collective-permute-start.1 = (bf16[128,1024]{1,0:T(8,128)(2,1)S(1)}, bf16[128,1024]{1,0:T(8,128)(2,1)S(1)}, u32[]{:S(2)}, u32[]{:S(2)}) collective-permute-start(bf16[128,1024]{1,0:T(8,128)(2,1)S(1)} %shard_map.64.refs_0_.refs_4_), channel_id=1, source_target_pairs={{0,4},{4,8},{8,12},{12,0},{1,5},{5,9},{9,13},{13,1},{2,6},{6,10},{... | collective-permute-start | bytes 786440 | tf_op jit(solution)/shard_map/ppermute | solution.py:197
  9.4 3.0 %collective-permute-start = (f32[2,128,256]{2,1,0:T(8,128)S(1)}, f32[2,128,256]{2,1,0:T(8,128)S(1)}, u32[]{:S(2)}, u32[]{:S(2)}) collective-permute-start(f32[2,128,256]{2,1,0:T(8,128)S(1)} %get-tuple-element.14), channel_id=1, source_target_pairs={{0,1},{1,0},{2,3},{3,2},{4,5},{5,4},{6,7},{7,6},{8,9},{9,8},{10,11... | collective-permute-start | bytes 786440 | tf_op jit(solution)/shard_map/ppermute | solution.py:19
  9.4 10.0 %collective-permute-start.3 = (bf16[128,1024]{1,0:T(8,128)(2,1)S(1)}, bf16[128,1024]{1,0:T(8,128)(2,1)S(1)}, u32[]{:S(2)}, u32[]{:S(2)}) collective-permute-start(bf16[128,1024]{1,0:T(8,128)(2,1)S(1)} %shard_map.64.refs_0_.refs_4_), channel_id=1, source_target_pairs={{0,12},{4,0},{8,4},{12,8},{1,13},{5,1},{9,5},{13,9},{2,14},{6,2},{... | collective-permute-start | bytes 786440 | tf_op jit(solution)/shard_map/ppermute | solution.py:197
  12.4 1.8 %collective-permute-start.2 = (bf16[16,128]{1,0:T(8,128)(2,1)S(1)}, bf16[16,128]{1,0:T(8,128)(2,1)S(1)}, u32[]{:S(2)}, u32[]{:S(2)}) collective-permute-start(bf16[16,128]{1,0:T(8,128)(2,1)S(1)} %slice.16), channel_id=1, source_target_pairs={{0,1},{1,0},{2,3},{3,2},{4,5},{5,4},{6,7},{7,6},{8,9},{9,8},{10,11... | collective-permute-start | bytes 12296 | tf_op jit(solution)/shard_map/ppermute | solution.py:19
  12.4 8.8 %collective-permute-start.6 = (f32[2,128,256]{2,1,0:T(8,128)S(1)}, f32[2,128,256]{2,1,0:T(8,128)S(1)}, u32[]{:S(2)}, u32[]{:S(2)}) collective-permute-start(f32[2,128,256]{2,1,0:T(8,128)S(1)} %add.15.refs_0_), channel_id=1, source_target_pairs={{0,2},{1,3},{2,0},{3,1},{4,6},{5,7},{6,4},{7,5},{8,10},{9,11},{10,... | collective-permute-start | bytes 786440 | tf_op jit(solution)/shard_map/ppermute | solution.py:19
  14.0 11.8 %collective-permute-start.10 = (bf16[128,1024]{1,0:T(8,128)(2,1)S(1)}, bf16[128,1024]{1,0:T(8,128)(2,1)S(1)}, u32[]{:S(2)}, u32[]{:S(2)}) collective-permute-start(bf16[128,1024]{1,0:T(8,128)(2,1)S(1)} %collective-permute-done.1.refs_5_), channel_id=1, source_target_pairs={{0,4},{4,8},{8,12},{12,0},{1,5},{5,9},{9,13},{13,1},{2,6},{6,10},{... | collective-permute-start | bytes 786440 | tf_op jit(solution)/shard_map/ppermute | solution.py:197
  19.5 1.4 %collective-permute-start.4 = (f32[1,128,256]{2,1,0:T(8,128)S(1)}, f32[1,128,256]{2,1,0:T(8,128)S(1)}, u32[]{:S(2)}, u32[]{:S(2)}) collective-permute-start(f32[1,128,256]{2,1,0:T(8,128)S(1)} %get-tuple-element.22), channel_id=1, source_target_pairs={{0,1},{1,0},{2,3},{3,2},{4,5},{5,4},{6,7},{7,6},{8,9},{9,8},{10,11... | collective-permute-start | bytes 393224 | tf_op jit(solution)/shard_map/ppermute | solution.py:19
  19.6 1.5 %collective-permute-start.5 = (f32[1,128,256]{2,1,0:T(8,128)S(1)}, f32[1,128,256]{2,1,0:T(8,128)S(1)}, u32[]{:S(2)}, u32[]{:S(2)}) collective-permute-start(f32[1,128,256]{2,1,0:T(8,128)S(1)} %get-tuple-element.21), channel_id=1, source_target_pairs={{0,1},{1,0},{2,3},{3,2},{4,5},{5,4},{6,7},{7,6},{8,9},{9,8},{10,11... | collective-permute-start | bytes 393224 | tf_op jit(solution)/shard_map/ppermute | solution.py:19
  21.7 4.1 %collective-permute-start.7 = (f32[2,8,128]{2,1,0:T(8,128)S(1)}, f32[2,8,128]{2,1,0:T(8,128)S(1)}, u32[]{:S(2)}, u32[]{:S(2)}) collective-permute-start(f32[2,8,128]{2,1,0:T(8,128)S(1)} %get-tuple-element.17), channel_id=1, source_target_pairs={{0,2},{1,3},{2,0},{3,1},{4,6},{5,7},{6,4},{7,5},{8,10},{9,11},{10,... | collective-permute-start | bytes 24584 | tf_op jit(solution)/shard_map/ppermute | solution.py:19
  23.3 3.1 %collective-permute-start.8 = (f32[2,8,128]{2,1,0:T(8,128)S(1)}, f32[2,8,128]{2,1,0:T(8,128)S(1)}, u32[]{:S(2)}, u32[]{:S(2)}) collective-permute-start(f32[2,8,128]{2,1,0:T(8,128)S(1)} %get-tuple-element.18), channel_id=1, source_target_pairs={{0,3},{1,2},{2,1},{3,0},{4,7},{5,6},{6,5},{7,4},{8,11},{9,10},{10,... | collective-permute-start | bytes 24584 | tf_op jit(solution)/shard_map/ppermute | solution.py:19
  23.4 3.0 %collective-permute-start.9 = (f32[2,8,128]{2,1,0:T(8,128)S(1)}, f32[2,8,128]{2,1,0:T(8,128)S(1)}, u32[]{:S(2)}, u32[]{:S(2)}) collective-permute-start(f32[2,8,128]{2,1,0:T(8,128)S(1)} %get-tuple-element.19), channel_id=1, source_target_pairs={{0,1},{1,0},{2,3},{3,2},{4,5},{5,4},{6,7},{7,6},{8,9},{9,8},{10,11... | collective-permute-start | bytes 24584 | tf_op jit(solution)/shard_map/ppermute | solution.py:19
  26.7 3.8 %collective-permute-start.11 = (f32[8,512]{1,0:T(8,128)S(1)}, f32[8,512]{1,0:T(8,128)S(1)}, u32[]{:S(2)}, u32[]{:S(2)}) collective-permute-start(f32[8,512]{1,0:T(8,128)S(1)} %shard_map.68), channel_id=1, source_target_pairs={{0,2},{1,3},{2,0},{3,1},{4,6},{5,7},{6,4},{7,5},{8,10},{9,11},{10,... | collective-permute-start | bytes 49160 | tf_op jit(solution)/shard_map/ppermute | solution.py:19
  27.7 3.2 %collective-permute-start.12 = (f32[8,512]{1,0:T(8,128)S(1)}, f32[8,512]{1,0:T(8,128)S(1)}, u32[]{:S(2)}, u32[]{:S(2)}) collective-permute-start(f32[8,512]{1,0:T(8,128)S(1)} %shard_map.68), channel_id=1, source_target_pairs={{0,3},{1,2},{2,1},{3,0},{4,7},{5,6},{6,5},{7,4},{8,11},{9,10},{10,... | collective-permute-start | bytes 49160 | tf_op jit(solution)/shard_map/ppermute | solution.py:19
  27.7 3.2 %collective-permute-start.13 = (f32[8,512]{1,0:T(8,128)S(1)}, f32[8,512]{1,0:T(8,128)S(1)}, u32[]{:S(2)}, u32[]{:S(2)}) collective-permute-start(f32[8,512]{1,0:T(8,128)S(1)} %shard_map.68), channel_id=1, source_target_pairs={{0,1},{1,0},{2,3},{3,2},{4,5},{5,4},{6,7},{7,6},{8,9},{9,8},{10,11... | collective-permute-start | bytes 49160 | tf_op jit(solution)/shard_map/ppermute | solution.py:19

commit v29 on v28

--- a/solution.py
+++ b/solution.py
@@ -139,7 +139,8 @@
         high = full.astype(jnp.bfloat16)
         low = (full - high.astype(jnp.float32)).astype(jnp.bfloat16)
         left, right = slice(None, rank), slice(rank, None)
-        pairs[k] = dot(high[left], high[right]) + (dot(high[left], low[right]) + dot(low[left], high[right]))
+        both = dot(high[left], jnp.concatenate([high[right], low[right]], axis=0))
+        pairs[k] = both[:, :rank] + (both[:, rank:] + dot(low[left], high[right]))
     for k in range(share):
         even = pairs[k, pl.ds(0, rows, stride=2), :]
         odd = pairs[k, pl.ds(1, rows, stride=2), :]

time: 31.7 us -> 31.8 us (level)
  transfers between devices with their start and end apart: 14 -> 14, of which waited for: 8 -> 8; matrix products, arithmetic and copies ran while one was open for 0% -> 0% of each run, Pallas kernels for 35% -> 36%
where the time goes in v29:
time: 31.8 us; the launch traced here: 31.6 us
  Pallas kernels  12.6 us (40%)
  starting transfers between devices  11.9 us (37%)
  waiting for transfers between devices  6.33 us (20%)
  other arithmetic  0.68 us (2%)
    pallas_call x2, Pallas kernels, project(): pl.pallas_call(functools.partial(project_kernel, steps, share, ahead, pie...  10.6 us
    ppermute x11, starting transfers between devices, xor_permute(): return lax.ppermute(value, axis, [(i, i ^ step) for i in range(size)])  6.57 us
    ppermute x3, starting transfers between devices, shift(): lax.ppermute(value, 'dp', [(i, (i + step) % groups) for i in range(groups)])  5.33 us
    ppermute x11, waiting for transfers between devices, xor_permute(): return lax.ppermute(value, axis, [(i, i ^ step) for i in range(size)])  3.77 us
    ppermute x3, waiting for transfers between devices, shift(): lax.ppermute(value, 'dp', [(i, (i + step) % groups) for i in range(groups)])  2.57 us
    pallas_call x1, Pallas kernels, cut_tests(): pl.pallas_call(cut_kernel, out_shape=jax.ShapeDtypeStruct((rows, width //...  0.96 us
    pallas_call x1, Pallas kernels, units(): pl.pallas_call(functools.partial(unit_kernel, share, rank, size), out_sha...  0.64 us
  transfers between devices with their start and end apart: 14, of which 8 were waited for; matrix products, arithmetic and copies ran while one was open for 0% of the time, Pallas kernels for 36%

profile of v29, /device:TPU:0, one launch (start us, length us, event | category | flops | bytes accessed | tf_op | source)
XLA Modules:
  0.0 31.6 jit_solution(8897787194026701988)
XLA Ops:
  0.0 1.0 %shard_map.64.refs_0_.refs_4_ = bf16[128,1024]{1,0:T(8,128)(2,1)S(1)} custom-call(bf16[128,4096]{1,0:T(8,128)(2,1)} %tests.1), custom_call_target="tpu_custom_call" | custom-call | tf_op jit(solution)/shard_map/pallas_call | solution.py:32
  1.0 3.1 %collective-permute-start.1 = (bf16[128,1024]{1,0:T(8,128)(2,1)S(1)}, bf16[128,1024]{1,0:T(8,128)(2,1)S(1)}, u32[]{:S(2)}, u32[]{:S(2)}) collective-permute-start(bf16[128,1024]{1,0:T(8,128)(2,1)S(1)} %shard_map.64.refs_0_.refs_4_), channel_id=1, source_target_pairs={{0,4},{4,8},{8,12},{12,0},{1,5},{5,9},{9,13},{13,1},{2,6},{6,10},{... | collective-permute-start | bytes 786440 | tf_op jit(solution)/shard_map/ppermute | solution.py:198
  4.0 5.3 %shard_map.65 = (f32[2,128,256]{2,1,0:T(8,128)S(1)}, f32[2,128,256]{2,1,0:T(8,128)S(1)}) custom-call(bf16[8,256,1024]{2,1,0:T(8,128)(2,1)} %act.3, bf16[8,256,3584]{2,1,0:T(8,128)(2,1)} %og.3, bf16[64,1024]{1,0:T(8,128)(2,1)} %bitcast.6, bf16[64,3584]{1,0:T(8,128)(2,1)} %bitcast.4, s32[8]{0:T(128)} %lens.3, bf16[128,1024]{1,0:T(8,128)(2,1)S(1)} %shard_map.64.refs_0_.refs_4_), custom_call_target="tpu_custom_call" | custom-call | flops 4294967296 | bytes 16777216 | tf_op jit(solution)/shard_map/pallas_call | solution.py:110
  9.4 0.1 collective-permute-start
  9.4 2.1 %collective-permute-start.3 = (bf16[128,1024]{1,0:T(8,128)(2,1)S(1)}, bf16[128,1024]{1,0:T(8,128)(2,1)S(1)}, u32[]{:S(2)}, u32[]{:S(2)}) collective-permute-start(bf16[128,1024]{1,0:T(8,128)(2,1)S(1)} %shard_map.64.refs_0_.refs_4_), channel_id=1, source_target_pairs={{0,12},{4,0},{8,4},{12,8},{1,13},{5,1},{9,5},{13,9},{2,14},{6,2},{... | collective-permute-start | bytes 786440 | tf_op jit(solution)/shard_map/ppermute | solution.py:198
  11.5 0.8 %collective-permute-done.1.refs_5_ = bf16[128,1024]{1,0:T(8,128)(2,1)S(1)} collective-permute-done((bf16[128,1024]{1,0:T(8,128)(2,1)S(1)}, bf16[128,1024]{1,0:T(8,128)(2,1)S(1)}, u32[]{:S(2)}, u32[]{:S(2)}) %collective-permute-start.1) | collective-permute-done | bytes 262176 | tf_op jit(solution)/shard_map/ppermute | solution.py:198
  12.4 0.0 collective-permute-start.2
  12.4 0.0 collective-permute-done
  12.4 1.6 %collective-permute-start.6 = (f32[2,128,256]{2,1,0:T(8,128)S(1)}, f32[2,128,256]{2,1,0:T(8,128)S(1)}, u32[]{:S(2)}, u32[]{:S(2)}) collective-permute-start(f32[2,128,256]{2,1,0:T(8,128)S(1)} %add.15.refs_0_), channel_id=1, source_target_pairs={{0,2},{1,3},{2,0},{3,1},{4,6},{5,7},{6,4},{7,5},{8,10},{9,11},{10,... | collective-permute-start | bytes 786440 | tf_op jit(solution)/shard_map/ppermute | solution.py:19
  14.0 0.2 collective-permute-start.10
  14.1 0.0 collective-permute-done.2.refs_1_
  14.1 5.3 %shard_map.66 = (f32[2,128,256]{2,1,0:T(8,128)S(1)}, f32[2,128,256]{2,1,0:T(8,128)S(1)}) custom-call(bf16[8,256,1024]{2,1,0:T(8,128)(2,1)} %act.3, bf16[8,256,3584]{2,1,0:T(8,128)(2,1)} %og.3, bf16[64,1024]{1,0:T(8,128)(2,1)} %bitcast.7, bf16[64,3584]{1,0:T(8,128)(2,1)} %bitcast.5, s32[8]{0:T(128)} %lens.3, f32[2,128,256]{2,1,0:T(8,128)S(1)} %add.15.refs_0_, ...), custom_call_target="tpu_custom_call" | custom-call | flops 1024 | bytes 4 | tf_op jit(solution)/shard_map/pallas_call | solution.py:110
  19.5 0.0 collective-permute-done.3.refs_6_
  19.5 0.1 collective-permute-start.4
  19.6 0.4 %collective-permute-start.5 = (f32[1,128,256]{2,1,0:T(8,128)S(1)}, f32[1,128,256]{2,1,0:T(8,128)S(1)}, u32[]{:S(2)}, u32[]{:S(2)}) collective-permute-start(f32[1,128,256]{2,1,0:T(8,128)S(1)} %get-tuple-element.21), channel_id=1, source_target_pairs={{0,1},{1,0},{2,3},{3,2},{4,5},{5,4},{6,7},{7,6},{8,9},{9,8},{10,11... | collective-permute-start | bytes 393224 | tf_op jit(solution)/shard_map/ppermute | solution.py:19
  20.1 0.8 %collective-permute-done.4.refs_0_ = f32[1,128,256]{2,1,0:T(8,128)S(1)} collective-permute-done((f32[1,128,256]{2,1,0:T(8,128)S(1)}, f32[1,128,256]{2,1,0:T(8,128)S(1)}, u32[]{:S(2)}, u32[]{:S(2)}) %collective-permute-start.4) | collective-permute-done | bytes 131104 | tf_op jit(solution)/shard_map/ppermute | solution.py:19
  20.9 0.2 collective-permute-done.5.refs_1_
  21.1 0.1 collective-permute-done.6.refs_3_
  21.2 0.6 %shard_map.67 = (f32[2,8,128]{2,1,0:T(8,128)S(1)}, f32[2,8,128]{2,1,0:T(8,128)S(1)}, f32[2,8,128]{2,1,0:T(8,128)S(1)}, f32[2,8,128]{2,1,0:T(8,128)S(1)}) custom-call(f32[1,128,256]{2,1,0:T(8,128)S(1)} %collective-permute-done.4.refs_0_, f32[1,128,256]{2,1,0:T(8,128)S(1)} %collective-permute-done.5.refs_1_, f32[2,128,256]{2,1,0:T(8,128)S(1)} %get-tuple-element.16.refs_2_, ...), custom_call_target="tpu_custom_call" | custom-call | tf_op jit(solution)/shard_map/pallas_call | solution.py:158
  21.8 1.6 %collective-permute-start.7 = (f32[2,8,128]{2,1,0:T(8,128)S(1)}, f32[2,8,128]{2,1,0:T(8,128)S(1)}, u32[]{:S(2)}, u32[]{:S(2)}) collective-permute-start(f32[2,8,128]{2,1,0:T(8,128)S(1)} %get-tuple-element.17), channel_id=1, source_target_pairs={{0,2},{1,3},{2,0},{3,1},{4,6},{5,7},{6,4},{7,5},{8,10},{9,11},{10,... | collective-permute-start | bytes 24584 | tf_op jit(solution)/shard_map/ppermute | solution.py:19
  23.4 0.1 collective-permute-start.8
  23.5 0.6 %collective-permute-start.9 = (f32[2,8,128]{2,1,0:T(8,128)S(1)}, f32[2,8,128]{2,1,0:T(8,128)S(1)}, u32[]{:S(2)}, u32[]{:S(2)}) collective-permute-start(f32[2,8,128]{2,1,0:T(8,128)S(1)} %get-tuple-element.19), channel_id=1, source_target_pairs={{0,1},{1,0},{2,3},{3,2},{4,5},{5,4},{6,7},{7,6},{8,9},{9,8},{10,11... | collective-permute-start | bytes 24584 | tf_op jit(solution)/shard_map/ppermute | solution.py:19
  24.1 1.7 %collective-permute-done.10.refs_7_ = bf16[128,1024]{1,0:T(8,128)(2,1)S(1)} collective-permute-done((bf16[128,1024]{1,0:T(8,128)(2,1)S(1)}, bf16[128,1024]{1,0:T(8,128)(2,1)S(1)}, u32[]{:S(2)}, u32[]{:S(2)}) %collective-permute-start.10) | collective-permute-done | bytes 262176 | tf_op jit(solution)/shard_map/ppermute | solution.py:198
  25.8 0.7 %collective-permute-done.8.refs_1_ = f32[2,8,128]{2,1,0:T(8,128)S(1)} collective-permute-done((f32[2,8,128]{2,1,0:T(8,128)S(1)}, f32[2,8,128]{2,1,0:T(8,128)S(1)}, u32[]{:S(2)}, u32[]{:S(2)}) %collective-permute-start.8) | collective-permute-done | bytes 8224 | tf_op jit(solution)/shard_map/ppermute | solution.py:19
  26.5 0.4 %shard_map.68 = f32[8,512]{1,0:T(8,128)S(1)} custom-call(f32[2,8,128]{2,1,0:T(8,128)S(1)} %collective-permute-done.7.refs_0_, f32[2,8,128]{2,1,0:T(8,128)S(1)} %collective-permute-done.8.refs_1_, f32[2,8,128]{2,1,0:T(8,128)S(1)} %collective-permute-done.9.refs_2_, f32[2,8,128]{2,1,0:T(8,128)S(1)} %get-tuple-element.20.refs_3_, ...), custom_call_target="tpu_custom_call" | custom-call | tf_op jit(solution)/shard_map/pallas_call | solution.py:186
  26.9 0.8 %collective-permute-start.11 = (f32[8,512]{1,0:T(8,128)S(1)}, f32[8,512]{1,0:T(8,128)S(1)}, u32[]{:S(2)}, u32[]{:S(2)}) collective-permute-start(f32[8,512]{1,0:T(8,128)S(1)} %shard_map.68), channel_id=1, source_target_pairs={{0,2},{1,3},{2,0},{3,1},{4,6},{5,7},{6,4},{7,5},{8,10},{9,11},{10,... | collective-permute-start | bytes 49160 | tf_op jit(solution)/shard_map/ppermute | solution.py:19
  27.7 0.0 collective-permute-start.12
  27.7 1.3 %collective-permute-start.13 = (f32[8,512]{1,0:T(8,128)S(1)}, f32[8,512]{1,0:T(8,128)S(1)}, u32[]{:S(2)}, u32[]{:S(2)}) collective-permute-start(f32[8,512]{1,0:T(8,128)S(1)} %shard_map.68), channel_id=1, source_target_pairs={{0,1},{1,0},{2,3},{3,2},{4,5},{5,4},{6,7},{7,6},{8,9},{9,8},{10,11... | collective-permute-start | bytes 49160 | tf_op jit(solution)/shard_map/ppermute | solution.py:19
  29.0 1.6 %collective-permute-done.11 = f32[8,512]{1,0:T(8,128)S(1)} collective-permute-done((f32[8,512]{1,0:T(8,128)S(1)}, f32[8,512]{1,0:T(8,128)S(1)}, u32[]{:S(2)}, u32[]{:S(2)}) %collective-permute-start.11) | collective-permute-done | bytes 16416 | tf_op jit(solution)/shard_map/ppermute | solution.py:19
  30.6 0.4 %collective-permute-done.12 = f32[8,512]{1,0:T(8,128)S(1)} collective-permute-done((f32[8,512]{1,0:T(8,128)S(1)}, f32[8,512]{1,0:T(8,128)S(1)}, u32[]{:S(2)}, u32[]{:S(2)}) %collective-permute-start.12) | collective-permute-done | bytes 16416 | tf_op jit(solution)/shard_map/ppermute | solution.py:19
  31.0 0.0 collective-permute-done.13
  31.0 0.6 %add_add_fusion = f32[8,512]{1,0:T(8,128)} fusion(f32[8,512]{1,0:T(8,128)S(1)} %shard_map.68, f32[8,512]{1,0:T(8,128)S(1)} %collective-permute-done.13, f32[8,512]{1,0:T(8,128)S(1)} %collective-permute-done.11, f32[8,512]{1,0:T(8,128)S(1)} %collective-permute-done.12), kind=kLoop, calls=%fused_computation.1 | loop fusion | flops 12288 | bytes 81920 | tf_op jit(solution)/shard_map/add | solution.py:234
  (5 shorter events, 0.1 us)
Async XLA Ops:
  1.0 11.4 %collective-permute-start.1 = (bf16[128,1024]{1,0:T(8,128)(2,1)S(1)}, bf16[128,1024]{1,0:T(8,128)(2,1)S(1)}, u32[]{:S(2)}, u32[]{:S(2)}) collective-permute-start(bf16[128,1024]{1,0:T(8,128)(2,1)S(1)} %shard_map.64.refs_0_.refs_4_), channel_id=1, source_target_pairs={{0,4},{4,8},{8,12},{12,0},{1,5},{5,9},{9,13},{13,1},{2,6},{6,10},{... | collective-permute-start | bytes 786440 | tf_op jit(solution)/shard_map/ppermute | solution.py:198
  9.4 3.0 %collective-permute-start = (f32[2,128,256]{2,1,0:T(8,128)S(1)}, f32[2,128,256]{2,1,0:T(8,128)S(1)}, u32[]{:S(2)}, u32[]{:S(2)}) collective-permute-start(f32[2,128,256]{2,1,0:T(8,128)S(1)} %get-tuple-element.14), channel_id=1, source_target_pairs={{0,1},{1,0},{2,3},{3,2},{4,5},{5,4},{6,7},{7,6},{8,9},{9,8},{10,11... | collective-permute-start | bytes 786440 | tf_op jit(solution)/shard_map/ppermute | solution.py:19
  9.4 10.0 %collective-permute-start.3 = (bf16[128,1024]{1,0:T(8,128)(2,1)S(1)}, bf16[128,1024]{1,0:T(8,128)(2,1)S(1)}, u32[]{:S(2)}, u32[]{:S(2)}) collective-permute-start(bf16[128,1024]{1,0:T(8,128)(2,1)S(1)} %shard_map.64.refs_0_.refs_4_), channel_id=1, source_target_pairs={{0,12},{4,0},{8,4},{12,8},{1,13},{5,1},{9,5},{13,9},{2,14},{6,2},{... | collective-permute-start | bytes 786440 | tf_op jit(solution)/shard_map/ppermute | solution.py:198
  12.4 1.8 %collective-permute-start.2 = (bf16[16,128]{1,0:T(8,128)(2,1)S(1)}, bf16[16,128]{1,0:T(8,128)(2,1)S(1)}, u32[]{:S(2)}, u32[]{:S(2)}) collective-permute-start(bf16[16,128]{1,0:T(8,128)(2,1)S(1)} %slice.16), channel_id=1, source_target_pairs={{0,1},{1,0},{2,3},{3,2},{4,5},{5,4},{6,7},{7,6},{8,9},{9,8},{10,11... | collective-permute-start | bytes 12296 | tf_op jit(solution)/shard_map/ppermute | solution.py:19
  12.4 8.8 %collective-permute-start.6 = (f32[2,128,256]{2,1,0:T(8,128)S(1)}, f32[2,128,256]{2,1,0:T(8,128)S(1)}, u32[]{:S(2)}, u32[]{:S(2)}) collective-permute-start(f32[2,128,256]{2,1,0:T(8,128)S(1)} %add.15.refs_0_), channel_id=1, source_target_pairs={{0,2},{1,3},{2,0},{3,1},{4,6},{5,7},{6,4},{7,5},{8,10},{9,11},{10,... | collective-permute-start | bytes 786440 | tf_op jit(solution)/shard_map/ppermute | solution.py:19
  14.0 11.8 %collective-permute-start.10 = (bf16[128,1024]{1,0:T(8,128)(2,1)S(1)}, bf16[128,1024]{1,0:T(8,128)(2,1)S(1)}, u32[]{:S(2)}, u32[]{:S(2)}) collective-permute-start(bf16[128,1024]{1,0:T(8,128)(2,1)S(1)} %collective-permute-done.1.refs_5_), channel_id=1, source_target_pairs={{0,4},{4,8},{8,12},{12,0},{1,5},{5,9},{9,13},{13,1},{2,6},{6,10},{... | collective-permute-start | bytes 786440 | tf_op jit(solution)/shard_map/ppermute | solution.py:198
  19.5 1.4 %collective-permute-start.4 = (f32[1,128,256]{2,1,0:T(8,128)S(1)}, f32[1,128,256]{2,1,0:T(8,128)S(1)}, u32[]{:S(2)}, u32[]{:S(2)}) collective-permute-start(f32[1,128,256]{2,1,0:T(8,128)S(1)} %get-tuple-element.22), channel_id=1, source_target_pairs={{0,1},{1,0},{2,3},{3,2},{4,5},{5,4},{6,7},{7,6},{8,9},{9,8},{10,11... | collective-permute-start | bytes 393224 | tf_op jit(solution)/shard_map/ppermute | solution.py:19
  19.6 1.5 %collective-permute-start.5 = (f32[1,128,256]{2,1,0:T(8,128)S(1)}, f32[1,128,256]{2,1,0:T(8,128)S(1)}, u32[]{:S(2)}, u32[]{:S(2)}) collective-permute-start(f32[1,128,256]{2,1,0:T(8,128)S(1)} %get-tuple-element.21), channel_id=1, source_target_pairs={{0,1},{1,0},{2,3},{3,2},{4,5},{5,4},{6,7},{7,6},{8,9},{9,8},{10,11... | collective-permute-start | bytes 393224 | tf_op jit(solution)/shard_map/ppermute | solution.py:19
  21.8 3.9 %collective-permute-start.7 = (f32[2,8,128]{2,1,0:T(8,128)S(1)}, f32[2,8,128]{2,1,0:T(8,128)S(1)}, u32[]{:S(2)}, u32[]{:S(2)}) collective-permute-start(f32[2,8,128]{2,1,0:T(8,128)S(1)} %get-tuple-element.17), channel_id=1, source_target_pairs={{0,2},{1,3},{2,0},{3,1},{4,6},{5,7},{6,4},{7,5},{8,10},{9,11},{10,... | collective-permute-start | bytes 24584 | tf_op jit(solution)/shard_map/ppermute | solution.py:19
  23.4 3.1 %collective-permute-start.8 = (f32[2,8,128]{2,1,0:T(8,128)S(1)}, f32[2,8,128]{2,1,0:T(8,128)S(1)}, u32[]{:S(2)}, u32[]{:S(2)}) collective-permute-start(f32[2,8,128]{2,1,0:T(8,128)S(1)} %get-tuple-element.18), channel_id=1, source_target_pairs={{0,3},{1,2},{2,1},{3,0},{4,7},{5,6},{6,5},{7,4},{8,11},{9,10},{10,... | collective-permute-start | bytes 24584 | tf_op jit(solution)/shard_map/ppermute | solution.py:19
  23.5 3.0 %collective-permute-start.9 = (f32[2,8,128]{2,1,0:T(8,128)S(1)}, f32[2,8,128]{2,1,0:T(8,128)S(1)}, u32[]{:S(2)}, u32[]{:S(2)}) collective-permute-start(f32[2,8,128]{2,1,0:T(8,128)S(1)} %get-tuple-element.19), channel_id=1, source_target_pairs={{0,1},{1,0},{2,3},{3,2},{4,5},{5,4},{6,7},{7,6},{8,9},{9,8},{10,11... | collective-permute-start | bytes 24584 | tf_op jit(solution)/shard_map/ppermute | solution.py:19
  26.9 3.8 %collective-permute-start.11 = (f32[8,512]{1,0:T(8,128)S(1)}, f32[8,512]{1,0:T(8,128)S(1)}, u32[]{:S(2)}, u32[]{:S(2)}) collective-permute-start(f32[8,512]{1,0:T(8,128)S(1)} %shard_map.68), channel_id=1, source_target_pairs={{0,2},{1,3},{2,0},{3,1},{4,6},{5,7},{6,4},{7,5},{8,10},{9,11},{10,... | collective-permute-start | bytes 49160 | tf_op jit(solution)/shard_map/ppermute | solution.py:19
  27.7 3.3 %collective-permute-start.12 = (f32[8,512]{1,0:T(8,128)S(1)}, f32[8,512]{1,0:T(8,128)S(1)}, u32[]{:S(2)}, u32[]{:S(2)}) collective-permute-start(f32[8,512]{1,0:T(8,128)S(1)} %shard_map.68), channel_id=1, source_target_pairs={{0,3},{1,2},{2,1},{3,0},{4,7},{5,6},{6,5},{7,4},{8,11},{9,10},{10,... | collective-permute-start | bytes 49160 | tf_op jit(solution)/shard_map/ppermute | solution.py:19
  27.7 3.3 %collective-permute-start.13 = (f32[8,512]{1,0:T(8,128)S(1)}, f32[8,512]{1,0:T(8,128)S(1)}, u32[]{:S(2)}, u32[]{:S(2)}) collective-permute-start(f32[8,512]{1,0:T(8,128)S(1)} %shard_map.68), channel_id=1, source_target_pairs={{0,1},{1,0},{2,3},{3,2},{4,5},{5,4},{6,7},{7,6},{8,9},{9,8},{10,11... | collective-permute-start | bytes 49160 | tf_op jit(solution)/shard_map/ppermute | solution.py:19
